TPU v7x, 32 devices: a whole 2x2x4 slice. The times are simulated.
32 devices in a mesh: seq: 8 (over y, x, core), head: 4 (over z).
Axes of the slice: x: 2, y: 2, z: 4, core: 2. Of those that a mesh axis runs over, the one named last changes fastest.
Arguments:
- queries: bfloat16 [64, 64, 192], P('seq', 'head'), may hold values from -120 to 120
- new_latent: bfloat16 [64, 576], P('seq'), may hold values from -6 to 6
- cache: bfloat16 [16, 1024, 576], P('head', 'seq'), may hold values from -6 to 6
- lengths: int32 [16], replicated, may hold values from 8 to 1024, as said below
- w_uk: bfloat16 [64, 128, 512], P('head'), may hold values from -0.5 to 0.5
- w_uv: bfloat16 [64, 512, 128], P('head'), may hold values from -0.25 to 0.25
Outputs:
- attended: bfloat16 [64, 64, 128], P('seq', 'head')
Inputs may be any that keep to these rules, and one draw needn't show every extreme that they name: `lengths`: each sequence keeps at least 8 cached slots; some sequence has exactly 1024.
All inputs are finite; a program needn't handle non-finite values.
Results may differ from a plain program's by a relative error of at most 0.039.
Values may be sent and summed in bfloat16 or wider, within the bound.
No kernel may reach another device: no remote copies, remote signals or barrier semaphores. Data moves between devices by JAX's collectives and lax.ppermute only.
A program may use at most 64 MiB of HBM per device.

v0:
```python
import jax
import jax.numpy as jnp
from jax import lax
from jax.sharding import PartitionSpec as P

NOPE = 128
ROPE = 64
LATENT = 512
SPEC = 4


masked_value = -1e30


def local_partial(
    query_tile_block,
    key_tile_block,
    incoming_keys,
    len_block,
    offset,
    own_first,
    score_scale,
    head_count,
):
    scores = (
        jnp.einsum(
            "vfa,vja->vfj", query_tile_block, key_tile_block, preferred_element_type=jnp.float32
        )
        * score_scale
    )
    positions = offset + lax.broadcasted_iota(jnp.int32, (1, 1, key_tile_block.shape[1]), 2)
    visible = positions < len_block[:, None, None]
    fresh_scores = (
        jnp.einsum(
            "vfa,vja->vfj", query_tile_block, incoming_keys, preferred_element_type=jnp.float32
        )
        * score_scale
    )
    spec_count = incoming_keys.shape[1]
    row_spec = (
        lax.broadcasted_iota(jnp.int32, (1, query_tile_block.shape[1], spec_count), 1) // head_count
    )
    key_spec = lax.broadcasted_iota(jnp.int32, (1, query_tile_block.shape[1], spec_count), 2)
    causal = (key_spec <= row_spec) & own_first
    row_top = jnp.maximum(
        jnp.max(jnp.where(visible, scores, masked_value), axis=2),
        jnp.max(jnp.where(causal, fresh_scores, masked_value), axis=2),
    )
    weights = jnp.where(visible, jnp.exp(scores - row_top[..., None]), 0.0)
    fresh_weights = jnp.where(causal, jnp.exp(fresh_scores - row_top[..., None]), 0.0)
    running_totals = jnp.sum(weights, axis=2) + jnp.sum(fresh_weights, axis=2)
    weighted = jnp.einsum(
        "mpu,mui->mpi",
        weights.astype(jnp.bfloat16),
        key_tile_block[:, :, :LATENT],
        preferred_element_type=jnp.float32,
    )
    weighted = weighted + jnp.einsum(
        "mpu,mui->mpi",
        fresh_weights.astype(jnp.bfloat16),
        incoming_keys[:, :, :LATENT],
        preferred_element_type=jnp.float32,
    )
    return (row_top, running_totals, weighted)


def project_values(latent_rows, value_weight):
    return jnp.einsum("rhc,hcv->rhv", latent_rows, value_weight, precision=lax.Precision.HIGHEST)


def shards(queries, new_latent, cache, lengths, w_uk, w_uv):
    own_rows, head_count, _ = queries.shape
    score_scale = (NOPE + ROPE) ** (-0.5)
    gathered, new_all = (
        lax.all_gather(queries, "seq", axis=0, tiled=True),
        lax.all_gather(new_latent, "seq", axis=0, tiled=True),
    )
    absorbed = jnp.einsum(
        "rhn,hnc->rhc", gathered[:, :, :NOPE], w_uk, preferred_element_type=jnp.float32
    ).astype(jnp.bfloat16)
    q_all = jnp.concatenate([absorbed, gathered[:, :, NOPE:]], axis=2)
    total_rows = q_all.shape[0]
    seq_count = total_rows // SPEC
    query_slots = SPEC * head_count
    q_seq = q_all.reshape(seq_count, query_slots, q_all.shape[2])
    new_seq = new_all.reshape(seq_count, SPEC, new_all.shape[1])
    seq_index = lax.axis_index("seq")
    offset = seq_index * cache.shape[1]
    own_first = seq_index == 0
    partial_value = local_partial(
        q_seq,
        lax.all_gather(cache, "head", axis=0, tiled=True),
        new_seq,
        lengths,
        offset,
        own_first,
        score_scale,
        head_count,
    )
    row_top, running_totals, weighted = tuple((value for value in partial_value))
    value_weight = w_uv.astype(jnp.float32)
    global_top = lax.pmax(row_top, "seq")
    factor = jnp.exp(row_top - global_top)
    scaled_totals = (running_totals * factor).reshape(total_rows, head_count)
    scaled_weighted = (weighted * factor[..., None]).reshape(total_rows, head_count, LATENT)
    row_totals, row_weighted = (
        lax.psum_scatter(scaled_totals, "seq", scatter_dimension=0, tiled=True),
        lax.psum_scatter(scaled_weighted, "seq", scatter_dimension=0, tiled=True),
    )
    latent_output = row_weighted / row_totals[..., None]
    result = project_values(latent_output, value_weight)
    return result.astype(jnp.bfloat16)


def solution(mesh):
    return jax.shard_map(
        shards,
        mesh=mesh,
        in_specs=(
            P("seq", "head", None),
            P("seq", None),
            P("head", "seq", None),
            P(),
            P("head", None, None),
            P("head", None, None),
        ),
        out_specs=P("seq", "head", None),
        check_vma=False,
    )
```

profile of v0, /device:TPU:0, one launch (start us, length us, event | category | flops | bytes accessed | tf_op | source)
XLA Modules:
  0.0 135.0 jit_solution(10142985846056384315)
XLA Ops:
  6.5 0.7 all-gather.2.cloned.1.call-update
  7.3 0.9 copy.18
  8.2 12.4 %all_gather.9 = bf16[64,16,192]{2,0,1:T(8,128)(2,1)S(1)} all-gather(bf16[8,16,192]{2,0,1:T(8,128)(2,1)S(1)} %copy.18), channel_id=1, replica_groups=mesh['seq'=8,'head'=4] {'seq'}, dimensions={0}, use_global_device_ids=true | all-gather | bytes 442368 | tf_op jit(solution)/shard_map/all_gather | solution.py:75
  20.6 0.4 fusion.2
  21.1 0.1 pad_maximum_fusion
  21.2 0.7 copy.19
  22.0 10.2 %all_gather.11 = bf16[64,576]{1,0:T(8,128)(2,1)} all-gather(bf16[8,576]{1,0:T(8,128)(2,1)S(1)} %copy-done.1), channel_id=1, replica_groups=mesh['seq'=8,'head'=4] {'seq'}, dimensions={0}, use_global_device_ids=true | all-gather | bytes 82944 | tf_op jit(solution)/shard_map/all_gather | solution.py:76
  32.1 0.9 reshape.96
  33.1 0.1 broadcast_compare_fusion
  33.2 0.5 select_reduce_fusion.1
  33.7 28.4 %all-gather.2.cloned.1.call-done = bf16[16,128,576]{1,2,0:T(8,128)(2,1)} async-done(((bf16[4,128,576]{1,2,0:T(8,128)(2,1)}), bf16[16,128,576]{1,2,0:T(8,128)(2,1)}) %all-gather.2.cloned.1.call-update) | async-done | bytes 2359312 | tf_op jit(solution)/shard_map/all_gather | solution.py:92
  62.1 3.1 %select_reduce_fusion = (f32[16,64]{1,0:T(8,128)S(1)}, f32[16,64,128]{2,1,0:T(8,128)}) fusion(pred[16,128]{1,0:T(8,128)(4,1)S(1)} %broadcast_compare_fusion, bf16[16,64,576]{2,1,0:T(8,128)(2,1)S(1)} %bitcast.14, bf16[16,128,576]{1,2,0:T(8,128)(2,1)} %all-gather.2.cloned.1.call-done), kind=kOutput, calls=%fused_computation.11 | convolution fusion | flops 151387136 | bytes 4069376 | tf_op jit(solution)/shard_map/vfa,vja->vfj/dot_general | solution.py:26
  65.2 13.8 %pmax.7 = f32[16,64]{1,0:T(8,128)S(1)} all-reduce(f32[16,64]{1,0:T(8,128)S(1)} %max.9), channel_id=1, replica_groups=mesh['seq'=8,'head'=4] {'seq'}, use_global_device_ids=true, to_apply=%region_2.3 | all-reduce | flops 1024 | bytes 8192 | tf_op jit(solution)/shard_map/pmax | solution.py:102
  79.1 1.4 %fusion.4 = f32[16,64]{1,0:T(8,128)S(1)} fusion(f32[16,64,128]{2,1,0:T(8,128)} %get-tuple-element.8, f32[16,64]{1,0:T(8,128)S(1)} %max.9, pred[16,128]{1,0:T(8,128)(4,1)S(1)} %broadcast_compare_fusion), kind=kLoop, calls=%fused_computation.12 | loop fusion | flops 392192 | bytes 534528 | tf_op jit(solution)/shard_map/reduce_sum | solution.py:51
  80.6 2.7 %fusion = f32[16,64,512]{2,1,0:T(8,128)S(1)} fusion(bf16[16,128,576]{1,2,0:T(8,128)(2,1)} %all-gather.2.cloned.1.call-done, f32[16,64,128]{2,1,0:T(8,128)} %get-tuple-element.8, f32[16,64]{1,0:T(8,128)S(1)} %max.9, pred[16,128]{1,0:T(8,128)(4,1)S(1)} %broadcast_compare_fusion), kind=kOutput, calls=%fused_computation | convolution fusion | flops 134610944 | bytes 4724736 | tf_op jit(solution)/shard_map/mpu,mui->mpi/dot_general | solution.py:52
  83.3 0.5 add_multiply_fusion
  83.8 2.6 %copy.21 = f32[64,16,512]{2,0,1:T(8,128)} copy(f32[64,16,512]{2,1,0:T(8,128)S(1)} %bitcast.15) | data formatting | bytes 4194304 | tf_op jit(solution)/shard_map/reshape | solution.py:105
  86.4 0.6 copy-done.3
  87.0 0.6 dynamic-slice
  88.3 22.6 %all-reduce = f32[64,16]{1,0:T(8,128)S(1)} all-reduce(f32[64,16]{1,0:T(8,128)S(1)} %reshape.98), channel_id=3, replica_groups=mesh['seq'=8,'head'=4] {'seq'}, use_global_device_ids=true, to_apply=%region_6.7.clone | all-reduce | flops 1024 | bytes 8192
  110.9 0.1 copy.22
  110.9 13.9 %reduce-scatter.2.cloned.1.call-done = f32[8,16,512]{2,0,1:T(8,128)} async-done(((f32[64,16,512]{2,0,1:T(8,128)}), f32[8,16,512]{2,0,1:T(8,128)}) %reduce-scatter.2.cloned.1.call-update) | async-done | bytes 262160 | tf_op jit(solution)/shard_map/reduce_scatter | solution.py:108
  124.9 2.7 %fusion.3 = bf16[8,16,128]{2,0,1:T(8,128)(2,1)S(1)} fusion(bf16[16,512,128]{2,1,0:T(8,128)(2,1)} %param.11, f32[8,16,512]{2,0,1:T(8,128)} %reduce-scatter.2.cloned.1.call-done, f32[8,16]{0,1:T(8,128)S(1)} %copy.22), kind=kOutput, calls=%fused_computation.9 | convolution fusion | flops 100745216 | bytes 2392576 | tf_op jit(solution)/shard_map/rhc,hcv->rhv/dot_general | solution.py:68
  127.5 0.6 copy.23
  (20 shorter events, 0.3 us)
Async XLA Ops:
  6.5 14.1 %copy-start = (bf16[16,128,512]{2,1,0:T(8,128)(2,1)S(1)}, bf16[16,128,512]{2,1,0:T(8,128)(2,1)}, u32[]{:S(2)}) copy-start(bf16[16,128,512]{2,1,0:T(8,128)(2,1)} %param.10) | copy-start | bytes 6291460
  6.5 55.6 %all-gather.2.cloned.1.call-start = ((), (), s32[]{:S(2)}) async-start(), calls=%async_computation.1 | async-start | bytes 2949120 | tf_op jit(solution)/shard_map/all_gather | solution.py:92
  7.3 117.6 %reduce-scatter.2.cloned.1.call-start = ((), (), s32[]{:S(2)}) async-start(), calls=%async_computation.2 | async-start | bytes 2359296 | tf_op jit(solution)/shard_map/reduce_scatter | solution.py:108
  21.0 0.9 copy-start.1
  21.2 11.9 %copy-start.2 = (s32[16]{0:T(128)S(1)}, s32[16]{0:T(128)}, u32[]{:S(2)}) copy-start(s32[16]{0:T(128)} %param.9) | copy-start | bytes 196
  86.4 0.7 copy-start.3
Sparse Core Ops, SparseCore 0:
  8.9 53.1 all-gather.1
  86.5 38.3 reduce-scatter.1
where the time goes:
time: 135 us
  blocking collectives  58.9 us (44%)
  waiting for transfers between devices  43.1 us (32%)
  between operations  14.2 us (11%)
  matrix products  9.89 us (7%)
  local copies, waits for them, and re-layouts  7.15 us (5%)
  other arithmetic  1.72 us (1%)
    all_gather x1, waiting for transfers between devices, shards(): lax.all_gather(cache, 'head', axis=0, tiled=True)  28.4 us
    unnamed x1, blocking collectives  22.6 us
    reduce_scatter x1, waiting for transfers between devices, shards(): lax.psum_scatter(scaled_weighted, 'seq', scatter_dimension=0, tiled=True)  13.9 us
    pmax x1, blocking collectives, shards(): global_top = lax.pmax(row_top, 'seq')  13.8 us
    all_gather x1, blocking collectives, shards(): lax.all_gather(queries, 'seq', axis=0, tiled=True)  12.4 us
    all_gather x1, blocking collectives, shards(): lax.all_gather(new_latent, 'seq', axis=0, tiled=True)  10.2 us
    dot_general x1, matrix products, local_partial(): jnp.einsum('vfa,vja->vfj', query_tile_block, key_tile_block, preferred_el...  3.08 us
  transfers between devices with their start and end apart: 2, of which 2 were waited for; matrix products, arithmetic and copies ran while one was open for 3% of the time, Pallas kernels for 0%

commit v1 on v0

--- a/solution.py
+++ b/solution.py
@@ -1,15 +1,209 @@
+import functools
+
 import jax
 import jax.numpy as jnp
 from jax import lax
+from jax.experimental import pallas as pl
+from jax.experimental.pallas import tpu as pltpu
 from jax.sharding import PartitionSpec as P
 
 NOPE = 128
 ROPE = 64
 LATENT = 512
 SPEC = 4
-
+SCORE_SCALE = (NOPE + ROPE) ** (-0.5)
+VMEM_LIMIT = 16 * 1024 * 1024
 
 masked_value = -1e30
+
+
+def pick_kernel(owners, copies, cache_ref, *rest):
+    outs, sem = rest[:-1], rest[-1]
+    group = lax.axis_index("seq") // copies
+    moves = [
+        pltpu.make_async_copy(cache_ref.at[group ^ k], outs[k], sem.at[k])
+        for k in range(owners)
+    ]
+    for move in moves:
+        move.start()
+    for move in moves:
+        move.wait()
+
+
+def absorb_kernel(per_device, fresh_pad, q_ref, new_ref, w_ref, *outs):
+    rows, heads, width = q_ref.shape
+    q = q_ref[...].reshape(rows * heads, width)
+    nope = q[:, :NOPE]
+    own_head = lax.broadcasted_iota(jnp.int32, (rows * heads, NOPE), 0) % heads
+    spread = jnp.concatenate(
+        [jnp.where(own_head == h, nope, jnp.zeros_like(nope)) for h in range(heads)], axis=1
+    )
+    absorbed = jnp.dot(
+        spread, w_ref[...].reshape(heads * NOPE, LATENT), preferred_element_type=jnp.float32
+    ).astype(jnp.bfloat16)
+    piece = SPEC * heads
+    fresh = new_ref[...].astype(jnp.float32)
+    fresh = jnp.concatenate(
+        [fresh, jnp.zeros((fresh_pad - rows, fresh.shape[1]), jnp.float32)], axis=0
+    ).astype(jnp.bfloat16)
+    head_shard = lax.axis_index("head")
+    for k in range(per_device):
+        which = (head_shard + k) % per_device
+        for a in range(per_device):
+
+            @pl.when(which == a)
+            def _():
+                outs[k][:piece, :LATENT] = absorbed[a * piece : (a + 1) * piece]
+                outs[k][:piece, LATENT:] = q[a * piece : (a + 1) * piece, NOPE:]
+
+        if k == 0:
+            outs[k][piece:, :] = fresh
+
+
+def attend_kernel(owners, copies, per_device, heads, len_ref, *refs):
+    block_count = owners * copies
+    q_refs = refs[:per_device]
+    key_refs = refs[per_device : per_device + block_count]
+    outs = refs[per_device + block_count :]
+    seq_index = lax.axis_index("seq")
+    group, core = seq_index // copies, seq_index % copies
+    sequence = lax.axis_index("head") * owners + group
+    length = len_ref[sequence]
+    piece = SPEC * heads
+    q = jnp.concatenate([ref[:piece, :] for ref in q_refs], axis=0)
+    fresh = q_refs[0][piece:, :]
+    slots = key_refs[0].shape[1]
+    lane = lax.broadcasted_iota(jnp.int32, (1, slots), 1)
+    scores = []
+    for k in range(owners):
+        for e in range(copies):
+            start = ((group ^ k) * copies + (core + copies - e) % copies) * slots
+            s = jnp.dot(q, key_refs[k * copies + e][...], preferred_element_type=jnp.float32)
+            scores.append(jnp.where(lane + start < length, s * SCORE_SCALE, masked_value))
+    s = lax.dot_general(
+        q, fresh, (((1,), (1,)), ((), ())), preferred_element_type=jnp.float32
+    )
+    row = lax.broadcasted_iota(jnp.int32, s.shape, 0)
+    key = lax.broadcasted_iota(jnp.int32, s.shape, 1)
+    causal = (key // SPEC == sequence % per_device) & (key % SPEC <= (row % piece) // heads)
+    scores.append(jnp.where(causal, s * SCORE_SCALE, masked_value))
+    top = functools.reduce(jnp.maximum, [jnp.max(s, axis=1, keepdims=True) for s in scores])
+    total = jnp.zeros_like(top)
+    out = jnp.zeros((q.shape[0], LATENT), jnp.float32)
+    for s, ref in zip(scores, list(key_refs) + [None]):
+        w = jnp.exp(s - top)
+        total += jnp.sum(w, axis=1, keepdims=True)
+        w = w.astype(jnp.bfloat16)
+        if ref is None:
+            out += jnp.dot(w, fresh[:, :LATENT], preferred_element_type=jnp.float32)
+        else:
+            out += lax.dot_general(
+                w, ref[:LATENT, :], (((1,), (1,)), ((), ())), preferred_element_type=jnp.float32
+            )
+    out = (out / total).astype(jnp.bfloat16)
+    for k in range(per_device):
+        outs[k][...] = out[k * piece : (k + 1) * piece]
+
+
+def project_kernel(per_device, w_ref, *refs):
+    lat_refs, out_ref = refs[:-1], refs[-1]
+    rows, heads, width = out_ref.shape
+    piece = SPEC * heads
+    head_shard = lax.axis_index("head")
+    parts = []
+    for a in range(per_device):
+        part = lat_refs[0][...]
+        for k in range(1, per_device):
+            part = jnp.where((head_shard + k) % per_device == a, lat_refs[k][...], part)
+        parts.append(part)
+    latent = jnp.concatenate(parts, axis=0)
+    own_head = lax.broadcasted_iota(jnp.int32, latent.shape, 0) % heads
+    out = jnp.zeros((rows * heads, width), jnp.float32)
+    for h in range(heads):
+        out += jnp.dot(
+            jnp.where(own_head == h, latent, jnp.zeros_like(latent)),
+            w_ref[h],
+            preferred_element_type=jnp.float32,
+        )
+    out_ref[...] = out.astype(out_ref.dtype).reshape(out_ref.shape)
+
+
+def whole_sequences(seq_size, head_size, queries, new_latent, cache, lengths, w_uk, w_uv):
+    rows, heads, _ = queries.shape
+    owners, slots, width = cache.shape
+    copies = seq_size // owners
+    per_device = rows // SPEC
+    piece = SPEC * heads
+    fresh_pad = -(-rows // 16) * 16
+    params = pltpu.CompilerParams(vmem_limit_bytes=VMEM_LIMIT)
+    vmem = pl.BlockSpec(memory_space=pltpu.VMEM)
+    anywhere = pl.BlockSpec(memory_space=pl.ANY)
+    both = ("seq", "head")
+
+    def flat(seq_index, head_index):
+        return seq_index * head_size + head_index
+
+    turned = jnp.swapaxes(cache, 1, 2)
+    picked = pl.pallas_call(
+        functools.partial(pick_kernel, owners, copies),
+        out_shape=[jax.ShapeDtypeStruct((width, slots), cache.dtype)] * owners,
+        in_specs=[anywhere],
+        out_specs=[anywhere] * owners,
+        scratch_shapes=[pltpu.SemaphoreType.DMA((owners,))],
+        compiler_params=params,
+    )(turned)
+    keys = []
+    for k in range(owners):
+        for e in range(copies):
+            if k == 0 and e == 0:
+                keys.append(picked[0])
+                continue
+            perm = [
+                (g * copies + t, (g ^ k) * copies + (t + e) % copies)
+                for g in range(owners)
+                for t in range(copies)
+            ]
+            keys.append(lax.ppermute(picked[k], "seq", perm))
+
+    pieces = pl.pallas_call(
+        functools.partial(absorb_kernel, per_device, fresh_pad),
+        out_shape=[
+            jax.ShapeDtypeStruct((piece + (fresh_pad if k == 0 else 0), width), cache.dtype)
+            for k in range(per_device)
+        ],
+        in_specs=[vmem] * 3,
+        out_specs=[vmem] * per_device,
+        compiler_params=params,
+    )(queries, new_latent, w_uk)
+    there = []
+    for k in range(per_device):
+        perm = []
+        for i in range(seq_size):
+            for j in range(head_size):
+                sequence = i * per_device + (j + k) % per_device
+                target = (sequence % owners) * copies + j // per_device
+                perm.append((flat(i, j), flat(target, sequence // owners)))
+        there.append(perm)
+    arrived = [lax.ppermute(pieces[k], both, there[k]) for k in range(per_device)]
+
+    latent = pl.pallas_call(
+        functools.partial(attend_kernel, owners, copies, per_device, heads),
+        out_shape=[jax.ShapeDtypeStruct((piece, LATENT), jnp.bfloat16)] * per_device,
+        in_specs=[pl.BlockSpec(memory_space=pltpu.SMEM)] + [vmem] * (per_device + len(keys)),
+        out_specs=[vmem] * per_device,
+        compiler_params=params,
+    )(lengths, *arrived, *keys)
+
+    back = [
+        lax.ppermute(latent[k], both, [(b, a) for a, b in there[k]]) for k in range(per_device)
+    ]
+    return pl.pallas_call(
+        functools.partial(project_kernel, per_device),
+        out_shape=jax.ShapeDtypeStruct((rows, heads, w_uv.shape[2]), jnp.bfloat16),
+        in_specs=[vmem] * (1 + per_device),
+        out_specs=vmem,
+        compiler_params=params,
+    )(w_uv, *back)
 
 
 def local_partial(
@@ -68,7 +262,7 @@
     return jnp.einsum("rhc,hcv->rhv", latent_rows, value_weight, precision=lax.Precision.HIGHEST)
 
 
-def shards(queries, new_latent, cache, lengths, w_uk, w_uv):
+def split_positions(queries, new_latent, cache, lengths, w_uk, w_uv):
     own_rows, head_count, _ = queries.shape
     score_scale = (NOPE + ROPE) ** (-0.5)
     gathered, new_all = (
@@ -87,7 +281,7 @@
     seq_index = lax.axis_index("seq")
     offset = seq_index * cache.shape[1]
     own_first = seq_index == 0
-    partial_value = local_partial(
+    row_top, running_totals, weighted = local_partial(
         q_seq,
         lax.all_gather(cache, "head", axis=0, tiled=True),
         new_seq,
@@ -97,7 +291,6 @@
         score_scale,
         head_count,
     )
-    row_top, running_totals, weighted = tuple((value for value in partial_value))
     value_weight = w_uv.astype(jnp.float32)
     global_top = lax.pmax(row_top, "seq")
     factor = jnp.exp(row_top - global_top)
@@ -112,9 +305,24 @@
     return result.astype(jnp.bfloat16)
 
 
+def shards(seq_size, head_size, queries, new_latent, cache, lengths, w_uk, w_uv):
+    rows, owners = queries.shape[0], cache.shape[0]
+    per_device = rows // SPEC
+    if (
+        rows % SPEC == 0
+        and owners & (owners - 1) == 0
+        and seq_size % owners == 0
+        and head_size == per_device * (seq_size // owners)
+    ):
+        return whole_sequences(
+            seq_size, head_size, queries, new_latent, cache, lengths, w_uk, w_uv
+        )
+    return split_positions(queries, new_latent, cache, lengths, w_uk, w_uv)
+
+
 def solution(mesh):
     return jax.shard_map(
-        shards,
+        functools.partial(shards, mesh.shape["seq"], mesh.shape["head"]),
         mesh=mesh,
         in_specs=(
             P("seq", "head", None),

time: 135 us -> 52.8 us (0.39)
  the two profiles are of different devices: /device:TPU:0 before, /device:TPU:9 now
where the time goes in v1:
time: 52.8 us; the launch traced here: 52.5 us
  waiting for transfers between devices  25.3 us (48%)
  starting transfers between devices  18.7 us (35%)
  local copies, waits for them, and re-layouts  4.22 us (8%)
  Pallas kernels  4.17 us (8%)
    ppermute x7, waiting for transfers between devices, whole_sequences(): keys.append(lax.ppermute(picked[k], 'seq', perm))  10.9 us
    ppermute x2, waiting for transfers between devices, whole_sequences(): lax.ppermute(pieces[k], both, there[k])  8.97 us
    ppermute x2, starting transfers between devices, whole_sequences(): lax.ppermute(latent[k], both, [(b, a) for a, b in there[k]])  6.4 us
    ppermute x7, starting transfers between devices, whole_sequences(): keys.append(lax.ppermute(picked[k], 'seq', perm))  6.36 us
    ppermute x2, starting transfers between devices, whole_sequences(): lax.ppermute(pieces[k], both, there[k])  5.99 us
    ppermute x2, waiting for transfers between devices, whole_sequences(): lax.ppermute(latent[k], both, [(b, a) for a, b in there[k]])  5.45 us
    unnamed x12, local copies, waits for them, and re-layouts  4.22 us
    pallas_call x1, Pallas kernels, whole_sequences(): pl.pallas_call(functools.partial(attend_kernel, owners, copies, per_devic...  1.62 us
  transfers between devices with their start and end apart: 11, of which 4 were waited for; matrix products, arithmetic and copies ran while one was open for 0% of the time, Pallas kernels for 1%

profile of v1, /device:TPU:9, one launch (start us, length us, event | category | flops | bytes accessed | tf_op | source)
XLA Modules:
  0.0 52.5 jit_solution(17717617029327556508)
XLA Ops:
  0.0 1.1 %copy-done.2 = bf16[4,128,576]{1,2,0:T(8,128)(2,1)S(1)} copy-done((bf16[4,128,576]{1,2,0:T(8,128)(2,1)S(1)}, bf16[4,128,576]{1,2,0:T(8,128)(2,1)}, u32[]{:S(2)}) %copy-start.2) | copy-done | bytes 589848
  1.1 0.8 %shard_map.65 = (bf16[576,128]{1,0:T(8,128)(2,1)S(1)}, bf16[576,128]{1,0:T(8,128)(2,1)S(1)}, bf16[576,128]{1,0:T(8,128)(2,1)S(1)}, bf16[576,128]{1,0:T(8,128)(2,1)S(1)}) custom-call(bf16[4,576,128]{2,1,0:T(8,128)(2,1)S(1)} %bitcast.1), custom_call_target="tpu_custom_call" | custom-call | tf_op jit(solution)/shard_map/pallas_call | solution.py:147
  1.9 0.7 %collective-permute-start.2 = (bf16[576,128]{1,0:T(8,128)(2,1)S(1)}, bf16[576,128]{1,0:T(8,128)(2,1)S(1)}, u32[]{:S(2)}, u32[]{:S(2)}) collective-permute-start(bf16[576,128]{1,0:T(8,128)(2,1)S(1)} %get-tuple-element.15.refs_2_), channel_id=1, source_target_pairs={{0,4},{4,0},{8,12},{12,8},{16,20},{20,16},{24,28},{28,24},{1,5},{5... | collective-permute-start | bytes 442376 | tf_op jit(solution)/shard_map/ppermute | solution.py:166
  2.6 1.2 %collective-permute-start.3 = (bf16[576,128]{1,0:T(8,128)(2,1)S(1)}, bf16[576,128]{1,0:T(8,128)(2,1)S(1)}, u32[]{:S(2)}, u32[]{:S(2)}) collective-permute-start(bf16[576,128]{1,0:T(8,128)(2,1)S(1)} %get-tuple-element.16), channel_id=1, source_target_pairs={{0,8},{4,12},{8,0},{12,4},{16,24},{20,28},{24,16},{28,20},{1,9},{5... | collective-permute-start | bytes 442376 | tf_op jit(solution)/shard_map/ppermute | solution.py:166
  3.8 1.6 %copy-done = bf16[16,128,512]{2,1,0:T(8,128)(2,1)S(1)} copy-done((bf16[16,128,512]{2,1,0:T(8,128)(2,1)S(1)}, bf16[16,128,512]{2,1,0:T(8,128)(2,1)}, u32[]{:S(2)}) %copy-start) | copy-done | bytes 2097176
  5.4 0.8 %copy-done.3 = bf16[8,16,192]{2,1,0:T(8,128)(2,1)S(1)} copy-done((bf16[8,16,192]{2,1,0:T(8,128)(2,1)S(1)}, bf16[8,16,192]{2,1,0:T(8,128)(2,1)}, u32[]{:S(2)}) %copy-start.3) | copy-done | bytes 49176
  6.3 0.7 %copy-done.4 = bf16[8,576]{1,0:T(8,128)(2,1)S(1)} copy-done((bf16[8,576]{1,0:T(8,128)(2,1)S(1)}, bf16[8,576]{1,0:T(8,128)(2,1)}, u32[]{:S(2)}) %copy-start.4) | copy-done | bytes 9240
  7.0 0.5 shard_map.64
  7.4 3.4 %collective-permute-start = (bf16[80,576]{1,0:T(8,128)(2,1)S(1)}, bf16[80,576]{1,0:T(8,128)(2,1)S(1)}, u32[]{:S(2)}, u32[]{:S(2)}) collective-permute-start(bf16[80,576]{1,0:T(8,128)(2,1)S(1)} %get-tuple-element.13), channel_id=1, source_target_pairs={{0,0},{1,8},{2,4},{3,12},{4,16},{5,24},{6,20},{7,28},{8,1},{9,9},{... | collective-permute-start | bytes 276488 | tf_op jit(solution)/shard_map/ppermute | solution.py:187
  10.8 2.6 %collective-permute-start.1 = (bf16[64,576]{1,0:T(8,128)(2,1)S(1)}, bf16[64,576]{1,0:T(8,128)(2,1)S(1)}, u32[]{:S(2)}, u32[]{:S(2)}) collective-permute-start(bf16[64,576]{1,0:T(8,128)(2,1)S(1)} %get-tuple-element.14), channel_id=1, source_target_pairs={{0,8},{1,0},{2,12},{3,4},{4,24},{5,16},{6,28},{7,20},{8,9},{9,1},{... | collective-permute-start | bytes 221192 | tf_op jit(solution)/shard_map/ppermute | solution.py:187
  13.4 9.0 %collective-permute-done.1.refs_1_ = bf16[64,576]{1,0:T(8,128)(2,1)S(1)} collective-permute-done((bf16[64,576]{1,0:T(8,128)(2,1)S(1)}, bf16[64,576]{1,0:T(8,128)(2,1)S(1)}, u32[]{:S(2)}, u32[]{:S(2)}) %collective-permute-start.1) | collective-permute-done | bytes 73760 | tf_op jit(solution)/shard_map/ppermute | solution.py:187
  22.4 0.0 collective-permute-start.5
  22.4 0.0 collective-permute-done.refs_0_
  22.4 1.3 %collective-permute-start.6 = (bf16[576,128]{1,0:T(8,128)(2,1)S(1)}, bf16[576,128]{1,0:T(8,128)(2,1)S(1)}, u32[]{:S(2)}, u32[]{:S(2)}) collective-permute-start(bf16[576,128]{1,0:T(8,128)(2,1)S(1)} %get-tuple-element.17), channel_id=1, source_target_pairs={{0,20},{4,16},{8,28},{12,24},{16,4},{20,0},{24,12},{28,8},{1,21},{... | collective-permute-start | bytes 442376 | tf_op jit(solution)/shard_map/ppermute | solution.py:166
  23.7 0.0 collective-permute-done.2.refs_3_
  23.7 0.0 collective-permute-start.7
  23.7 3.1 %collective-permute-start.8 = (bf16[576,128]{1,0:T(8,128)(2,1)S(1)}, bf16[576,128]{1,0:T(8,128)(2,1)S(1)}, u32[]{:S(2)}, u32[]{:S(2)}) collective-permute-start(bf16[576,128]{1,0:T(8,128)(2,1)S(1)} %get-tuple-element.18), channel_id=1, source_target_pairs={{0,28},{4,24},{8,20},{12,16},{16,12},{20,8},{24,4},{28,0},{1,29},{... | collective-permute-start | bytes 442376 | tf_op jit(solution)/shard_map/ppermute | solution.py:166
  26.8 7.7 %collective-permute-done.5.refs_6_ = bf16[576,128]{1,0:T(8,128)(2,1)S(1)} collective-permute-done((bf16[576,128]{1,0:T(8,128)(2,1)S(1)}, bf16[576,128]{1,0:T(8,128)(2,1)S(1)}, u32[]{:S(2)}, u32[]{:S(2)}) %collective-permute-start.5) | collective-permute-done | bytes 147488 | tf_op jit(solution)/shard_map/ppermute | solution.py:166
  34.5 3.2 %collective-permute-done.6.refs_7_ = bf16[576,128]{1,0:T(8,128)(2,1)S(1)} collective-permute-done((bf16[576,128]{1,0:T(8,128)(2,1)S(1)}, bf16[576,128]{1,0:T(8,128)(2,1)S(1)}, u32[]{:S(2)}, u32[]{:S(2)}) %collective-permute-start.6) | collective-permute-done | bytes 147488 | tf_op jit(solution)/shard_map/ppermute | solution.py:166
  37.7 1.6 %shard_map.66 = (bf16[64,512]{1,0:T(8,128)(2,1)S(1)}, bf16[64,512]{1,0:T(8,128)(2,1)S(1)}) custom-call(s32[16]{0:T(128)S(1)} %copy-done.5, bf16[80,576]{1,0:T(8,128)(2,1)S(1)} %collective-permute-done.refs_0_, bf16[64,576]{1,0:T(8,128)(2,1)S(1)} %collective-permute-done.1.refs_1_, bf16[576,128]{1,0:T(8,128)(2,1)S(1)} %get-tuple-element.15.refs_2_, ...), custom_call_target="tpu_custom_call" | custom-call | tf_op jit(solution)/shard_map/pallas_call | solution.py:189
  39.3 4.5 %collective-permute-start.10 = (bf16[64,512]{1,0:T(8,128)(2,1)S(1)}, bf16[64,512]{1,0:T(8,128)(2,1)S(1)}, u32[]{:S(2)}, u32[]{:S(2)}) collective-permute-start(bf16[64,512]{1,0:T(8,128)(2,1)S(1)} %get-tuple-element.20), channel_id=1, source_target_pairs={{8,0},{0,1},{12,2},{4,3},{24,4},{16,5},{28,6},{20,7},{9,8},{1,9},{... | collective-permute-start | bytes 196616 | tf_op jit(solution)/shard_map/ppermute | solution.py:198
  43.8 1.9 %collective-permute-start.9 = (bf16[64,512]{1,0:T(8,128)(2,1)S(1)}, bf16[64,512]{1,0:T(8,128)(2,1)S(1)}, u32[]{:S(2)}, u32[]{:S(2)}) collective-permute-start(bf16[64,512]{1,0:T(8,128)(2,1)S(1)} %get-tuple-element.19), channel_id=1, source_target_pairs={{0,0},{8,1},{4,2},{12,3},{16,4},{24,5},{20,6},{28,7},{1,8},{9,9},{... | collective-permute-start | bytes 196616 | tf_op jit(solution)/shard_map/ppermute | solution.py:198
  45.7 5.4 %collective-permute-done.9.refs_0_ = bf16[64,512]{1,0:T(8,128)(2,1)S(1)} collective-permute-done((bf16[64,512]{1,0:T(8,128)(2,1)S(1)}, bf16[64,512]{1,0:T(8,128)(2,1)S(1)}, u32[]{:S(2)}, u32[]{:S(2)}) %collective-permute-start.9) | collective-permute-done | bytes 65568 | tf_op jit(solution)/shard_map/ppermute | solution.py:198
  51.2 1.3 %shard_map.67 = bf16[8,16,128]{2,1,0:T(8,128)(2,1)} custom-call(bf16[16,512,128]{2,1,0:T(8,128)(2,1)S(1)} %copy-done.1, bf16[64,512]{1,0:T(8,128)(2,1)S(1)} %collective-permute-done.9.refs_0_, bf16[64,512]{1,0:T(8,128)(2,1)S(1)} %collective-permute-done.10.refs_1_), custom_call_target="tpu_custom_call" | custom-call | tf_op jit(solution)/shard_map/pallas_call | solution.py:200
  (14 shorter events, 0.0 us)
Async XLA Ops:
  0.0 37.7 %copy-start.5 = (s32[16]{0:T(128)S(1)}, s32[16]{0:T(128)}, u32[]{:S(2)}) copy-start(s32[16]{0:T(128)} %len_ref.1) | copy-start | bytes 196
  0.0 1.1 %copy-start.2 = (bf16[4,128,576]{1,2,0:T(8,128)(2,1)S(1)}, bf16[4,128,576]{1,2,0:T(8,128)(2,1)}, u32[]{:S(2)}) copy-start(bf16[4,128,576]{1,2,0:T(8,128)(2,1)} %param.8) | copy-start | bytes 1769476
  1.9 21.8 %collective-permute-start.2 = (bf16[576,128]{1,0:T(8,128)(2,1)S(1)}, bf16[576,128]{1,0:T(8,128)(2,1)S(1)}, u32[]{:S(2)}, u32[]{:S(2)}) collective-permute-start(bf16[576,128]{1,0:T(8,128)(2,1)S(1)} %get-tuple-element.15.refs_2_), channel_id=1, source_target_pairs={{0,4},{4,0},{8,12},{12,8},{16,20},{20,16},{24,28},{28,24},{1,5},{5... | collective-permute-start | bytes 442376 | tf_op jit(solution)/shard_map/ppermute | solution.py:166
  2.6 21.1 %collective-permute-start.3 = (bf16[576,128]{1,0:T(8,128)(2,1)S(1)}, bf16[576,128]{1,0:T(8,128)(2,1)S(1)}, u32[]{:S(2)}, u32[]{:S(2)}) collective-permute-start(bf16[576,128]{1,0:T(8,128)(2,1)S(1)} %get-tuple-element.16), channel_id=1, source_target_pairs={{0,8},{4,12},{8,0},{12,4},{16,24},{20,28},{24,16},{28,20},{1,9},{5... | collective-permute-start | bytes 442376 | tf_op jit(solution)/shard_map/ppermute | solution.py:166
  3.8 1.6 %copy-start = (bf16[16,128,512]{2,1,0:T(8,128)(2,1)S(1)}, bf16[16,128,512]{2,1,0:T(8,128)(2,1)}, u32[]{:S(2)}) copy-start(bf16[16,128,512]{2,1,0:T(8,128)(2,1)} %w_ref.2) | copy-start | bytes 6291460
  5.4 0.8 %copy-start.3 = (bf16[8,16,192]{2,1,0:T(8,128)(2,1)S(1)}, bf16[8,16,192]{2,1,0:T(8,128)(2,1)}, u32[]{:S(2)}) copy-start(bf16[8,16,192]{2,1,0:T(8,128)(2,1)} %q_ref.1) | copy-start | bytes 147460
  6.3 0.7 %copy-start.4 = (bf16[8,576]{1,0:T(8,128)(2,1)S(1)}, bf16[8,576]{1,0:T(8,128)(2,1)}, u32[]{:S(2)}) copy-start(bf16[8,576]{1,0:T(8,128)(2,1)} %new_ref.1) | copy-start | bytes 27652
  7.0 44.2 %copy-start.1 = (bf16[16,512,128]{2,1,0:T(8,128)(2,1)S(1)}, bf16[16,512,128]{2,1,0:T(8,128)(2,1)}, u32[]{:S(2)}) copy-start(bf16[16,512,128]{2,1,0:T(8,128)(2,1)} %w_ref.3) | copy-start | bytes 6291460
  7.4 15.0 %collective-permute-start = (bf16[80,576]{1,0:T(8,128)(2,1)S(1)}, bf16[80,576]{1,0:T(8,128)(2,1)S(1)}, u32[]{:S(2)}, u32[]{:S(2)}) collective-permute-start(bf16[80,576]{1,0:T(8,128)(2,1)S(1)} %get-tuple-element.13), channel_id=1, source_target_pairs={{0,0},{1,8},{2,4},{3,12},{4,16},{5,24},{6,20},{7,28},{8,1},{9,9},{... | collective-permute-start | bytes 276488 | tf_op jit(solution)/shard_map/ppermute | solution.py:187
  10.8 11.6 %collective-permute-start.1 = (bf16[64,576]{1,0:T(8,128)(2,1)S(1)}, bf16[64,576]{1,0:T(8,128)(2,1)S(1)}, u32[]{:S(2)}, u32[]{:S(2)}) collective-permute-start(bf16[64,576]{1,0:T(8,128)(2,1)S(1)} %get-tuple-element.14), channel_id=1, source_target_pairs={{0,8},{1,0},{2,12},{3,4},{4,24},{5,16},{6,28},{7,20},{8,9},{9,1},{... | collective-permute-start | bytes 221192 | tf_op jit(solution)/shard_map/ppermute | solution.py:187
  13.4 13.4 %collective-permute-start.4 = (bf16[576,128]{1,0:T(8,128)(2,1)S(1)}, bf16[576,128]{1,0:T(8,128)(2,1)S(1)}, u32[]{:S(2)}, u32[]{:S(2)}) collective-permute-start(bf16[576,128]{1,0:T(8,128)(2,1)S(1)} %get-tuple-element.16), channel_id=1, source_target_pairs={{0,12},{4,8},{8,4},{12,0},{16,28},{20,24},{24,20},{28,16},{1,13},{... | collective-permute-start | bytes 442376 | tf_op jit(solution)/shard_map/ppermute | solution.py:166
  22.4 12.1 %collective-permute-start.5 = (bf16[576,128]{1,0:T(8,128)(2,1)S(1)}, bf16[576,128]{1,0:T(8,128)(2,1)S(1)}, u32[]{:S(2)}, u32[]{:S(2)}) collective-permute-start(bf16[576,128]{1,0:T(8,128)(2,1)S(1)} %get-tuple-element.17), channel_id=1, source_target_pairs={{0,16},{4,20},{8,24},{12,28},{16,0},{20,4},{24,8},{28,12},{1,17},{... | collective-permute-start | bytes 442376 | tf_op jit(solution)/shard_map/ppermute | solution.py:166
  22.4 15.2 %collective-permute-start.6 = (bf16[576,128]{1,0:T(8,128)(2,1)S(1)}, bf16[576,128]{1,0:T(8,128)(2,1)S(1)}, u32[]{:S(2)}, u32[]{:S(2)}) collective-permute-start(bf16[576,128]{1,0:T(8,128)(2,1)S(1)} %get-tuple-element.17), channel_id=1, source_target_pairs={{0,20},{4,16},{8,28},{12,24},{16,4},{20,0},{24,12},{28,8},{1,21},{... | collective-permute-start | bytes 442376 | tf_op jit(solution)/shard_map/ppermute | solution.py:166
  23.7 14.0 %collective-permute-start.7 = (bf16[576,128]{1,0:T(8,128)(2,1)S(1)}, bf16[576,128]{1,0:T(8,128)(2,1)S(1)}, u32[]{:S(2)}, u32[]{:S(2)}) collective-permute-start(bf16[576,128]{1,0:T(8,128)(2,1)S(1)} %get-tuple-element.18), channel_id=1, source_target_pairs={{0,24},{4,28},{8,16},{12,20},{16,8},{20,12},{24,0},{28,4},{1,25},{... | collective-permute-start | bytes 442376 | tf_op jit(solution)/shard_map/ppermute | solution.py:166
  23.7 14.0 %collective-permute-start.8 = (bf16[576,128]{1,0:T(8,128)(2,1)S(1)}, bf16[576,128]{1,0:T(8,128)(2,1)S(1)}, u32[]{:S(2)}, u32[]{:S(2)}) collective-permute-start(bf16[576,128]{1,0:T(8,128)(2,1)S(1)} %get-tuple-element.18), channel_id=1, source_target_pairs={{0,28},{4,24},{8,20},{12,16},{16,12},{20,8},{24,4},{28,0},{1,29},{... | collective-permute-start | bytes 442376 | tf_op jit(solution)/shard_map/ppermute | solution.py:166
  39.3 6.4 %collective-permute-start.10 = (bf16[64,512]{1,0:T(8,128)(2,1)S(1)}, bf16[64,512]{1,0:T(8,128)(2,1)S(1)}, u32[]{:S(2)}, u32[]{:S(2)}) collective-permute-start(bf16[64,512]{1,0:T(8,128)(2,1)S(1)} %get-tuple-element.20), channel_id=1, source_target_pairs={{8,0},{0,1},{12,2},{4,3},{24,4},{16,5},{28,6},{20,7},{9,8},{1,9},{... | collective-permute-start | bytes 196616 | tf_op jit(solution)/shard_map/ppermute | solution.py:198
  43.8 7.4 %collective-permute-start.9 = (bf16[64,512]{1,0:T(8,128)(2,1)S(1)}, bf16[64,512]{1,0:T(8,128)(2,1)S(1)}, u32[]{:S(2)}, u32[]{:S(2)}) collective-permute-start(bf16[64,512]{1,0:T(8,128)(2,1)S(1)} %get-tuple-element.19), channel_id=1, source_target_pairs={{0,0},{8,1},{4,2},{12,3},{16,4},{24,5},{20,6},{28,7},{1,8},{9,9},{... | collective-permute-start | bytes 196616 | tf_op jit(solution)/shard_map/ppermute | solution.py:198

commit v2 on v1

--- a/solution.py
+++ b/solution.py
@@ -17,30 +17,43 @@
 masked_value = -1e30
 
 
-def pick_kernel(owners, copies, cache_ref, *rest):
-    outs, sem = rest[:-1], rest[-1]
-    group = lax.axis_index("seq") // copies
-    moves = [
-        pltpu.make_async_copy(cache_ref.at[group ^ k], outs[k], sem.at[k])
-        for k in range(owners)
+def absorb_kernel(per_device, fresh_pad, parts, q_hbm, new_hbm, w_hbm, *rest):
+    outs, (q_ref, new_ref, w_ref, sem) = rest[:per_device], rest[per_device:]
+    rows, heads, width = q_ref.shape
+    share = heads // parts
+    small = [
+        pltpu.make_async_copy(q_hbm, q_ref, sem.at[parts]),
+        pltpu.make_async_copy(new_hbm, new_ref, sem.at[parts + 1]),
     ]
-    for move in moves:
+    weights = [
+        pltpu.make_async_copy(
+            w_hbm.at[pl.ds(n * share, share)], w_ref.at[pl.ds(n * share, share)], sem.at[n]
+        )
+        for n in range(parts)
+    ]
+    for move in small + weights:
         move.start()
-    for move in moves:
+    for move in small:
         move.wait()
-
-
-def absorb_kernel(per_device, fresh_pad, q_ref, new_ref, w_ref, *outs):
-    rows, heads, width = q_ref.shape
     q = q_ref[...].reshape(rows * heads, width)
     nope = q[:, :NOPE]
-    own_head = lax.broadcasted_iota(jnp.int32, (rows * heads, NOPE), 0) % heads
-    spread = jnp.concatenate(
-        [jnp.where(own_head == h, nope, jnp.zeros_like(nope)) for h in range(heads)], axis=1
-    )
-    absorbed = jnp.dot(
-        spread, w_ref[...].reshape(heads * NOPE, LATENT), preferred_element_type=jnp.float32
-    ).astype(jnp.bfloat16)
+    own_head = lax.broadcasted_iota(jnp.int32, nope.shape, 0) % heads
+    absorbed = jnp.zeros((rows * heads, LATENT), jnp.float32)
+    for n in range(parts):
+        spread = jnp.concatenate(
+            [
+                jnp.where(own_head == h, nope, jnp.zeros_like(nope))
+                for h in range(n * share, (n + 1) * share)
+            ],
+            axis=1,
+        )
+        weights[n].wait()
+        absorbed += jnp.dot(
+            spread,
+            w_ref[n * share : (n + 1) * share].reshape(share * NOPE, LATENT),
+            preferred_element_type=jnp.float32,
+        )
+    absorbed = absorbed.astype(jnp.bfloat16)
     piece = SPEC * heads
     fresh = new_ref[...].astype(jnp.float32)
     fresh = jnp.concatenate(
@@ -61,10 +74,9 @@
 
 
 def attend_kernel(owners, copies, per_device, heads, len_ref, *refs):
-    block_count = owners * copies
     q_refs = refs[:per_device]
-    key_refs = refs[per_device : per_device + block_count]
-    outs = refs[per_device + block_count :]
+    key_refs = refs[per_device : per_device + copies]
+    outs = refs[per_device + copies :]
     seq_index = lax.axis_index("seq")
     group, core = seq_index // copies, seq_index % copies
     sequence = lax.axis_index("head") * owners + group
@@ -72,13 +84,13 @@
     piece = SPEC * heads
     q = jnp.concatenate([ref[:piece, :] for ref in q_refs], axis=0)
     fresh = q_refs[0][piece:, :]
-    slots = key_refs[0].shape[1]
+    slots = key_refs[0].shape[2]
     lane = lax.broadcasted_iota(jnp.int32, (1, slots), 1)
     scores = []
-    for k in range(owners):
-        for e in range(copies):
-            start = ((group ^ k) * copies + (core + copies - e) % copies) * slots
-            s = jnp.dot(q, key_refs[k * copies + e][...], preferred_element_type=jnp.float32)
+    for e in range(copies):
+        for g in range(owners):
+            start = (g * copies + (core + copies - e) % copies) * slots
+            s = jnp.dot(q, key_refs[e][g], preferred_element_type=jnp.float32)
             scores.append(jnp.where(lane + start < length, s * SCORE_SCALE, masked_value))
     s = lax.dot_general(
         q, fresh, (((1,), (1,)), ((), ())), preferred_element_type=jnp.float32
@@ -90,15 +102,18 @@
     top = functools.reduce(jnp.maximum, [jnp.max(s, axis=1, keepdims=True) for s in scores])
     total = jnp.zeros_like(top)
     out = jnp.zeros((q.shape[0], LATENT), jnp.float32)
-    for s, ref in zip(scores, list(key_refs) + [None]):
+    for n, s in enumerate(scores):
         w = jnp.exp(s - top)
         total += jnp.sum(w, axis=1, keepdims=True)
         w = w.astype(jnp.bfloat16)
-        if ref is None:
+        if n == owners * copies:
             out += jnp.dot(w, fresh[:, :LATENT], preferred_element_type=jnp.float32)
         else:
             out += lax.dot_general(
-                w, ref[:LATENT, :], (((1,), (1,)), ((), ())), preferred_element_type=jnp.float32
+                w,
+                key_refs[n // owners][n % owners, :LATENT, :],
+                (((1,), (1,)), ((), ())),
+                preferred_element_type=jnp.float32,
             )
     out = (out / total).astype(jnp.bfloat16)
     for k in range(per_device):
@@ -137,42 +152,45 @@
     fresh_pad = -(-rows // 16) * 16
     params = pltpu.CompilerParams(vmem_limit_bytes=VMEM_LIMIT)
     vmem = pl.BlockSpec(memory_space=pltpu.VMEM)
-    anywhere = pl.BlockSpec(memory_space=pl.ANY)
     both = ("seq", "head")
 
     def flat(seq_index, head_index):
         return seq_index * head_size + head_index
 
-    turned = jnp.swapaxes(cache, 1, 2)
-    picked = pl.pallas_call(
-        functools.partial(pick_kernel, owners, copies),
-        out_shape=[jax.ShapeDtypeStruct((width, slots), cache.dtype)] * owners,
-        in_specs=[anywhere],
-        out_specs=[anywhere] * owners,
-        scratch_shapes=[pltpu.SemaphoreType.DMA((owners,))],
-        compiler_params=params,
-    )(turned)
-    keys = []
-    for k in range(owners):
-        for e in range(copies):
-            if k == 0 and e == 0:
-                keys.append(picked[0])
-                continue
-            perm = [
-                (g * copies + t, (g ^ k) * copies + (t + e) % copies)
-                for g in range(owners)
-                for t in range(copies)
-            ]
-            keys.append(lax.ppermute(picked[k], "seq", perm))
-
+    same_core = [[g * copies + t for g in range(owners)] for t in range(copies)]
+    keys = [
+        lax.all_to_all(
+            jnp.swapaxes(cache, 1, 2),
+            "seq",
+            split_axis=0,
+            concat_axis=0,
+            axis_index_groups=same_core,
+            tiled=True,
+        )
+    ]
+    for e in range(1, copies):
+        perm = [
+            (g * copies + t, g * copies + (t + e) % copies)
+            for g in range(owners)
+            for t in range(copies)
+        ]
+        keys.append(lax.ppermute(keys[0], "seq", perm))
+
+    parts = 4 if heads % 4 == 0 else 1
     pieces = pl.pallas_call(
-        functools.partial(absorb_kernel, per_device, fresh_pad),
+        functools.partial(absorb_kernel, per_device, fresh_pad, parts),
         out_shape=[
             jax.ShapeDtypeStruct((piece + (fresh_pad if k == 0 else 0), width), cache.dtype)
             for k in range(per_device)
         ],
-        in_specs=[vmem] * 3,
+        in_specs=[pl.BlockSpec(memory_space=pltpu.HBM)] * 3,
         out_specs=[vmem] * per_device,
+        scratch_shapes=[
+            pltpu.VMEM(queries.shape, queries.dtype),
+            pltpu.VMEM(new_latent.shape, new_latent.dtype),
+            pltpu.VMEM(w_uk.shape, w_uk.dtype),
+            pltpu.SemaphoreType.DMA((parts + 2,)),
+        ],
         compiler_params=params,
     )(queries, new_latent, w_uk)
     there = []

time: 52.8 us -> 47.6 us (0.902)
  the two profiles are of different devices: /device:TPU:9 before, /device:TPU:7 now
where the time goes in v2:
time: 47.6 us; the launch traced here: 47.3 us
  starting transfers between devices  16.4 us (34%)
  waiting for transfers between devices  13.4 us (28%)
  blocking collectives  10.4 us (22%)
  Pallas kernels  3.84 us (8%)
  local copies, waits for them, and re-layouts  3.14 us (7%)
    all_to_all x1, blocking collectives, whole_sequences(): lax.all_to_all(jnp.swapaxes(cache, 1, 2), 'seq', split_axis=0, concat_axi...  10.4 us
    ppermute x2, waiting for transfers between devices, whole_sequences(): lax.ppermute(pieces[k], both, there[k])  7.97 us
    ppermute x2, starting transfers between devices, whole_sequences(): lax.ppermute(latent[k], both, [(b, a) for a, b in there[k]])  7.86 us
    ppermute x2, starting transfers between devices, whole_sequences(): lax.ppermute(pieces[k], both, there[k])  6.76 us
    ppermute x2, waiting for transfers between devices, whole_sequences(): lax.ppermute(latent[k], both, [(b, a) for a, b in there[k]])  5.47 us
    unnamed x10, local copies, waits for them, and re-layouts  3.14 us
    ppermute x1, starting transfers between devices, whole_sequences(): keys.append(lax.ppermute(keys[0], 'seq', perm))  1.79 us
    pallas_call x1, Pallas kernels, whole_sequences(): pl.pallas_call(functools.partial(attend_kernel, owners, copies, per_devic...  1.61 us
  transfers between devices with their start and end apart: 5, of which 3 were waited for; matrix products, arithmetic and copies ran while one was open for 0% of the time, Pallas kernels for 2%

profile of v2, /device:TPU:7, one launch (start us, length us, event | category | flops | bytes accessed | tf_op | source)
XLA Modules:
  0.0 47.3 jit_solution(7646994627407042740)
XLA Ops:
  0.0 0.0 copy-start.4
  0.0 10.4 %all_to_all.5.refs_2_ = bf16[4,576,128]{2,1,0:T(8,128)(2,1)S(1)} all-to-all(bf16[4,576,128]{2,1,0:T(8,128)(2,1)} %bitcast.1), channel_id=1, replica_groups={{0,8,16,24},{4,12,20,28},{1,9,17,25},{5,13,21,29},{2,10,18,26},{6,14,22..., dimensions={0} | all-to-all | bytes 1179648 | tf_op jit(solution)/shard_map/all_to_all | solution.py:162
  10.4 1.8 %collective-permute-start.2 = (bf16[4,576,128]{2,1,0:T(8,128)(2,1)S(1)}, bf16[4,576,128]{2,1,0:T(8,128)(2,1)S(1)}, u32[]{:S(2)}, u32[]{:S(2)}) collective-permute-start(bf16[4,576,128]{2,1,0:T(8,128)(2,1)S(1)} %all_to_all.5.refs_2_), channel_id=1, source_target_pairs={{0,4},{4,0},{8,12},{12,8},{16,20},{20,16},{24,28},{28,24},{1,5},{5... | collective-permute-start | bytes 1769480 | tf_op jit(solution)/shard_map/ppermute | solution.py:177
  12.2 0.0 copy-start
  12.2 1.6 %copy-done = bf16[16,128,512]{2,1,0:T(8,128)(2,1)S(1)} copy-done((bf16[16,128,512]{2,1,0:T(8,128)(2,1)S(1)}, bf16[16,128,512]{2,1,0:T(8,128)(2,1)}, u32[]{:S(2)}) %copy-start) | copy-done | bytes 2097176
  13.8 0.0 copy-start.2
  13.8 0.8 %copy-done.2 = bf16[8,16,192]{2,1,0:T(8,128)(2,1)S(1)} copy-done((bf16[8,16,192]{2,1,0:T(8,128)(2,1)S(1)}, bf16[8,16,192]{2,1,0:T(8,128)(2,1)}, u32[]{:S(2)}) %copy-start.2) | copy-done | bytes 49176
  14.6 0.0 copy-start.3
  14.6 0.7 %copy-done.3 = bf16[8,576]{1,0:T(8,128)(2,1)S(1)} copy-done((bf16[8,576]{1,0:T(8,128)(2,1)S(1)}, bf16[8,576]{1,0:T(8,128)(2,1)}, u32[]{:S(2)}) %copy-start.3) | copy-done | bytes 9240
  15.3 0.0 copy-start.1
  15.4 0.9 %shard_map.64 = (bf16[80,576]{1,0:T(8,128)(2,1)S(1)}, bf16[64,576]{1,0:T(8,128)(2,1)S(1)}) custom-call(bf16[8,16,192]{2,1,0:T(8,128)(2,1)S(1)} %copy-done.2, bf16[8,576]{1,0:T(8,128)(2,1)S(1)} %copy-done.3, bf16[16,128,512]{2,1,0:T(8,128)(2,1)S(1)} %copy-done), custom_call_target="tpu_custom_call" | custom-call | tf_op jit(solution)/shard_map/pallas_call | solution.py:180
  16.3 6.0 %collective-permute-start = (bf16[80,576]{1,0:T(8,128)(2,1)S(1)}, bf16[80,576]{1,0:T(8,128)(2,1)S(1)}, u32[]{:S(2)}, u32[]{:S(2)}) collective-permute-start(bf16[80,576]{1,0:T(8,128)(2,1)S(1)} %get-tuple-element.9), channel_id=1, source_target_pairs={{0,0},{1,8},{2,4},{3,12},{4,16},{5,24},{6,20},{7,28},{8,1},{9,9},{... | collective-permute-start | bytes 276488 | tf_op jit(solution)/shard_map/ppermute | solution.py:205
  22.3 0.7 %collective-permute-start.1 = (bf16[64,576]{1,0:T(8,128)(2,1)S(1)}, bf16[64,576]{1,0:T(8,128)(2,1)S(1)}, u32[]{:S(2)}, u32[]{:S(2)}) collective-permute-start(bf16[64,576]{1,0:T(8,128)(2,1)S(1)} %get-tuple-element.10), channel_id=1, source_target_pairs={{0,8},{1,0},{2,12},{3,4},{4,24},{5,16},{6,28},{7,20},{8,9},{9,1},{... | collective-permute-start | bytes 221192 | tf_op jit(solution)/shard_map/ppermute | solution.py:205
  23.0 8.0 %collective-permute-done.1.refs_1_ = bf16[64,576]{1,0:T(8,128)(2,1)S(1)} collective-permute-done((bf16[64,576]{1,0:T(8,128)(2,1)S(1)}, bf16[64,576]{1,0:T(8,128)(2,1)S(1)}, u32[]{:S(2)}, u32[]{:S(2)}) %collective-permute-start.1) | collective-permute-done | bytes 73760 | tf_op jit(solution)/shard_map/ppermute | solution.py:205
  31.0 0.0 collective-permute-done.refs_0_
  31.0 0.0 collective-permute-done.2.refs_3_
  31.0 0.0 copy-done.4
  31.0 1.6 %shard_map.65 = (bf16[64,512]{1,0:T(8,128)(2,1)S(1)}, bf16[64,512]{1,0:T(8,128)(2,1)S(1)}) custom-call(s32[16]{0:T(128)S(1)} %copy-done.4, bf16[80,576]{1,0:T(8,128)(2,1)S(1)} %collective-permute-done.refs_0_, bf16[64,576]{1,0:T(8,128)(2,1)S(1)} %collective-permute-done.1.refs_1_, bf16[4,576,128]{2,1,0:T(8,128)(2,1)S(1)} %all_to_all.5.refs_2_, ...), custom_call_target="tpu_custom_call" | custom-call | tf_op jit(solution)/shard_map/pallas_call | solution.py:207
  32.6 7.8 %collective-permute-start.3 = (bf16[64,512]{1,0:T(8,128)(2,1)S(1)}, bf16[64,512]{1,0:T(8,128)(2,1)S(1)}, u32[]{:S(2)}, u32[]{:S(2)}) collective-permute-start(bf16[64,512]{1,0:T(8,128)(2,1)S(1)} %get-tuple-element.11), channel_id=1, source_target_pairs={{0,0},{8,1},{4,2},{12,3},{16,4},{24,5},{20,6},{28,7},{1,8},{9,9},{... | collective-permute-start | bytes 196616 | tf_op jit(solution)/shard_map/ppermute | solution.py:216
  40.4 0.1 collective-permute-start.4
  40.5 1.2 %collective-permute-done.3.refs_0_ = bf16[64,512]{1,0:T(8,128)(2,1)S(1)} collective-permute-done((bf16[64,512]{1,0:T(8,128)(2,1)S(1)}, bf16[64,512]{1,0:T(8,128)(2,1)S(1)}, u32[]{:S(2)}, u32[]{:S(2)}) %collective-permute-start.3) | collective-permute-done | bytes 65568 | tf_op jit(solution)/shard_map/ppermute | solution.py:216
  41.8 4.2 %collective-permute-done.4.refs_1_ = bf16[64,512]{1,0:T(8,128)(2,1)S(1)} collective-permute-done((bf16[64,512]{1,0:T(8,128)(2,1)S(1)}, bf16[64,512]{1,0:T(8,128)(2,1)S(1)}, u32[]{:S(2)}, u32[]{:S(2)}) %collective-permute-start.4) | collective-permute-done | bytes 65568 | tf_op jit(solution)/shard_map/ppermute | solution.py:216
  46.0 0.0 copy-done.1
  46.0 1.3 %shard_map.66 = bf16[8,16,128]{2,1,0:T(8,128)(2,1)} custom-call(bf16[16,512,128]{2,1,0:T(8,128)(2,1)S(1)} %copy-done.1, bf16[64,512]{1,0:T(8,128)(2,1)S(1)} %collective-permute-done.3.refs_0_, bf16[64,512]{1,0:T(8,128)(2,1)S(1)} %collective-permute-done.4.refs_1_), custom_call_target="tpu_custom_call" | custom-call | tf_op jit(solution)/shard_map/pallas_call | solution.py:218
Async XLA Ops:
  0.0 31.0 %copy-start.4 = (s32[16]{0:T(128)S(1)}, s32[16]{0:T(128)}, u32[]{:S(2)}) copy-start(s32[16]{0:T(128)} %len_ref.1) | copy-start | bytes 196
  10.4 20.6 %collective-permute-start.2 = (bf16[4,576,128]{2,1,0:T(8,128)(2,1)S(1)}, bf16[4,576,128]{2,1,0:T(8,128)(2,1)S(1)}, u32[]{:S(2)}, u32[]{:S(2)}) collective-permute-start(bf16[4,576,128]{2,1,0:T(8,128)(2,1)S(1)} %all_to_all.5.refs_2_), channel_id=1, source_target_pairs={{0,4},{4,0},{8,12},{12,8},{16,20},{20,16},{24,28},{28,24},{1,5},{5... | collective-permute-start | bytes 1769480 | tf_op jit(solution)/shard_map/ppermute | solution.py:177
  12.2 1.6 %copy-start = (bf16[16,128,512]{2,1,0:T(8,128)(2,1)S(1)}, bf16[16,128,512]{2,1,0:T(8,128)(2,1)}, u32[]{:S(2)}) copy-start(bf16[16,128,512]{2,1,0:T(8,128)(2,1)} %w_hbm.1) | copy-start | bytes 6291460
  13.8 0.8 %copy-start.2 = (bf16[8,16,192]{2,1,0:T(8,128)(2,1)S(1)}, bf16[8,16,192]{2,1,0:T(8,128)(2,1)}, u32[]{:S(2)}) copy-start(bf16[8,16,192]{2,1,0:T(8,128)(2,1)} %q_hbm.1) | copy-start | bytes 147460
  14.6 0.7 %copy-start.3 = (bf16[8,576]{1,0:T(8,128)(2,1)S(1)}, bf16[8,576]{1,0:T(8,128)(2,1)}, u32[]{:S(2)}) copy-start(bf16[8,576]{1,0:T(8,128)(2,1)} %new_hbm.1) | copy-start | bytes 27652
  15.3 30.6 %copy-start.1 = (bf16[16,512,128]{2,1,0:T(8,128)(2,1)S(1)}, bf16[16,512,128]{2,1,0:T(8,128)(2,1)}, u32[]{:S(2)}) copy-start(bf16[16,512,128]{2,1,0:T(8,128)(2,1)} %w_ref.1) | copy-start | bytes 6291460
  16.3 14.7 %collective-permute-start = (bf16[80,576]{1,0:T(8,128)(2,1)S(1)}, bf16[80,576]{1,0:T(8,128)(2,1)S(1)}, u32[]{:S(2)}, u32[]{:S(2)}) collective-permute-start(bf16[80,576]{1,0:T(8,128)(2,1)S(1)} %get-tuple-element.9), channel_id=1, source_target_pairs={{0,0},{1,8},{2,4},{3,12},{4,16},{5,24},{6,20},{7,28},{8,1},{9,9},{... | collective-permute-start | bytes 276488 | tf_op jit(solution)/shard_map/ppermute | solution.py:205
  22.3 8.7 %collective-permute-start.1 = (bf16[64,576]{1,0:T(8,128)(2,1)S(1)}, bf16[64,576]{1,0:T(8,128)(2,1)S(1)}, u32[]{:S(2)}, u32[]{:S(2)}) collective-permute-start(bf16[64,576]{1,0:T(8,128)(2,1)S(1)} %get-tuple-element.10), channel_id=1, source_target_pairs={{0,8},{1,0},{2,12},{3,4},{4,24},{5,16},{6,28},{7,20},{8,9},{9,1},{... | collective-permute-start | bytes 221192 | tf_op jit(solution)/shard_map/ppermute | solution.py:205
  32.6 9.1 %collective-permute-start.3 = (bf16[64,512]{1,0:T(8,128)(2,1)S(1)}, bf16[64,512]{1,0:T(8,128)(2,1)S(1)}, u32[]{:S(2)}, u32[]{:S(2)}) collective-permute-start(bf16[64,512]{1,0:T(8,128)(2,1)S(1)} %get-tuple-element.11), channel_id=1, source_target_pairs={{0,0},{8,1},{4,2},{12,3},{16,4},{24,5},{20,6},{28,7},{1,8},{9,9},{... | collective-permute-start | bytes 196616 | tf_op jit(solution)/shard_map/ppermute | solution.py:216
  40.4 5.5 %collective-permute-start.4 = (bf16[64,512]{1,0:T(8,128)(2,1)S(1)}, bf16[64,512]{1,0:T(8,128)(2,1)S(1)}, u32[]{:S(2)}, u32[]{:S(2)}) collective-permute-start(bf16[64,512]{1,0:T(8,128)(2,1)S(1)} %get-tuple-element.12), channel_id=1, source_target_pairs={{8,0},{0,1},{12,2},{4,3},{24,4},{16,5},{28,6},{20,7},{9,8},{1,9},{... | collective-permute-start | bytes 196616 | tf_op jit(solution)/shard_map/ppermute | solution.py:216

commit v3 on v2

--- a/solution.py
+++ b/solution.py
@@ -13,12 +13,15 @@
 SPEC = 4
 SCORE_SCALE = (NOPE + ROPE) ** (-0.5)
 VMEM_LIMIT = 16 * 1024 * 1024
+ABSORB_VMEM_LIMIT = 63 * 1024 * 1024
 
 masked_value = -1e30
 
 
-def absorb_kernel(per_device, fresh_pad, parts, q_hbm, new_hbm, w_hbm, *rest):
-    outs, (q_ref, new_ref, w_ref, sem) = rest[:per_device], rest[per_device:]
+def absorb_kernel(per_device, owners, copies, fresh_pad, parts, *refs):
+    q_hbm, new_hbm, w_hbm, cache_hbm = refs[:4]
+    outs, picked = refs[4 : 4 + per_device], refs[4 + per_device : 4 + per_device + owners]
+    q_ref, new_ref, w_ref, sem = refs[4 + per_device + owners :]
     rows, heads, width = q_ref.shape
     share = heads // parts
     small = [
@@ -31,7 +34,12 @@
         )
         for n in range(parts)
     ]
-    for move in small + weights:
+    group = lax.axis_index("seq") // copies
+    picks = [
+        pltpu.make_async_copy(cache_hbm.at[group ^ k], picked[k], sem.at[parts + 2 + k])
+        for k in range(owners)
+    ]
+    for move in small + weights + picks:
         move.start()
     for move in small:
         move.wait()
@@ -71,12 +79,14 @@
 
         if k == 0:
             outs[k][piece:, :] = fresh
+    for move in picks:
+        move.wait()
 
 
 def attend_kernel(owners, copies, per_device, heads, len_ref, *refs):
     q_refs = refs[:per_device]
-    key_refs = refs[per_device : per_device + copies]
-    outs = refs[per_device + copies :]
+    key_refs = refs[per_device : per_device + copies * owners]
+    outs = refs[per_device + copies * owners :]
     seq_index = lax.axis_index("seq")
     group, core = seq_index // copies, seq_index % copies
     sequence = lax.axis_index("head") * owners + group
@@ -84,13 +94,13 @@
     piece = SPEC * heads
     q = jnp.concatenate([ref[:piece, :] for ref in q_refs], axis=0)
     fresh = q_refs[0][piece:, :]
-    slots = key_refs[0].shape[2]
+    slots = key_refs[0].shape[1]
     lane = lax.broadcasted_iota(jnp.int32, (1, slots), 1)
     scores = []
     for e in range(copies):
-        for g in range(owners):
-            start = (g * copies + (core + copies - e) % copies) * slots
-            s = jnp.dot(q, key_refs[e][g], preferred_element_type=jnp.float32)
+        for k in range(owners):
+            start = ((group ^ k) * copies + (core + copies - e) % copies) * slots
+            s = jnp.dot(q, key_refs[e * owners + k][...], preferred_element_type=jnp.float32)
             scores.append(jnp.where(lane + start < length, s * SCORE_SCALE, masked_value))
     s = lax.dot_general(
         q, fresh, (((1,), (1,)), ((), ())), preferred_element_type=jnp.float32
@@ -111,7 +121,7 @@
         else:
             out += lax.dot_general(
                 w,
-                key_refs[n // owners][n % owners, :LATENT, :],
+                key_refs[n][:LATENT, :],
                 (((1,), (1,)), ((), ())),
                 preferred_element_type=jnp.float32,
             )
@@ -152,47 +162,31 @@
     fresh_pad = -(-rows // 16) * 16
     params = pltpu.CompilerParams(vmem_limit_bytes=VMEM_LIMIT)
     vmem = pl.BlockSpec(memory_space=pltpu.VMEM)
+    anywhere = pl.BlockSpec(memory_space=pl.ANY)
     both = ("seq", "head")
 
     def flat(seq_index, head_index):
         return seq_index * head_size + head_index
 
-    same_core = [[g * copies + t for g in range(owners)] for t in range(copies)]
-    keys = [
-        lax.all_to_all(
-            jnp.swapaxes(cache, 1, 2),
-            "seq",
-            split_axis=0,
-            concat_axis=0,
-            axis_index_groups=same_core,
-            tiled=True,
-        )
-    ]
-    for e in range(1, copies):
-        perm = [
-            (g * copies + t, g * copies + (t + e) % copies)
-            for g in range(owners)
-            for t in range(copies)
-        ]
-        keys.append(lax.ppermute(keys[0], "seq", perm))
-
     parts = 4 if heads % 4 == 0 else 1
-    pieces = pl.pallas_call(
-        functools.partial(absorb_kernel, per_device, fresh_pad, parts),
+    made = pl.pallas_call(
+        functools.partial(absorb_kernel, per_device, owners, copies, fresh_pad, parts),
         out_shape=[
             jax.ShapeDtypeStruct((piece + (fresh_pad if k == 0 else 0), width), cache.dtype)
             for k in range(per_device)
-        ],
-        in_specs=[pl.BlockSpec(memory_space=pltpu.HBM)] * 3,
-        out_specs=[vmem] * per_device,
+        ]
+        + [jax.ShapeDtypeStruct((width, slots), cache.dtype)] * owners,
+        in_specs=[anywhere] * 4,
+        out_specs=[vmem] * per_device + [anywhere] * owners,
         scratch_shapes=[
             pltpu.VMEM(queries.shape, queries.dtype),
             pltpu.VMEM(new_latent.shape, new_latent.dtype),
             pltpu.VMEM(w_uk.shape, w_uk.dtype),
-            pltpu.SemaphoreType.DMA((parts + 2,)),
+            pltpu.SemaphoreType.DMA((parts + 2 + owners,)),
         ],
-        compiler_params=params,
-    )(queries, new_latent, w_uk)
+        compiler_params=pltpu.CompilerParams(vmem_limit_bytes=ABSORB_VMEM_LIMIT),
+    )(queries, new_latent, w_uk, jnp.swapaxes(cache, 1, 2))
+    pieces, picked = made[:per_device], made[per_device:]
     there = []
     for k in range(per_device):
         perm = []
@@ -203,6 +197,20 @@
                 perm.append((flat(i, j), flat(target, sequence // owners)))
         there.append(perm)
     arrived = [lax.ppermute(pieces[k], both, there[k]) for k in range(per_device)]
+
+    keys = [picked[0]]
+    for k in range(1, owners):
+        perm = [
+            (g * copies + t, (g ^ k) * copies + t) for g in range(owners) for t in range(copies)
+        ]
+        keys.append(lax.ppermute(picked[k], "seq", perm))
+    for e in range(1, copies):
+        perm = [
+            (g * copies + t, g * copies + (t + e) % copies)
+            for g in range(owners)
+            for t in range(copies)
+        ]
+        keys += [lax.ppermute(keys[k], "seq", perm) for k in range(owners)]
 
     latent = pl.pallas_call(
         functools.partial(attend_kernel, owners, copies, per_device, heads),

time: 47.6 us -> 60.5 us (1.27)
  the two profiles are of different devices: /device:TPU:7 before, /device:TPU:6 now
where the time goes in v3:
time: 60.5 us; the launch traced here: 59.9 us
  Pallas kernels  22.7 us (38%)
  waiting for transfers between devices  18.1 us (30%)
  starting transfers between devices  16.6 us (27%)
  local copies, waits for them, and re-layouts  2.5 us (4%)
    pallas_call x1, Pallas kernels, whole_sequences(): pl.pallas_call(functools.partial(absorb_kernel, per_device, owners, copie...  19.8 us
    ppermute x2, starting transfers between devices, whole_sequences(): lax.ppermute(pieces[k], both, there[k])  10.5 us
    ppermute x2, waiting for transfers between devices, whole_sequences(): lax.ppermute(latent[k], both, [(b, a) for a, b in there[k]])  7.76 us
    ppermute x2, waiting for transfers between devices, whole_sequences(): lax.ppermute(pieces[k], both, there[k])  6.35 us
    ppermute x3, waiting for transfers between devices, whole_sequences(): keys.append(lax.ppermute(picked[k], 'seq', perm))  3.98 us
    ppermute x3, starting transfers between devices, whole_sequences(): keys.append(lax.ppermute(picked[k], 'seq', perm))  3.55 us
    unnamed x6, local copies, waits for them, and re-layouts  2.5 us
    ppermute x2, starting transfers between devices, whole_sequences(): lax.ppermute(latent[k], both, [(b, a) for a, b in there[k]])  1.98 us
  transfers between devices with their start and end apart: 11, of which 4 were waited for; matrix products, arithmetic and copies ran while one was open for 0% of the time, Pallas kernels for 0%

profile of v3, /device:TPU:6, one launch (start us, length us, event | category | flops | bytes accessed | tf_op | source)
XLA Modules:
  0.0 59.9 jit_solution(10771994433815888940)
XLA Ops:
  0.0 19.8 %shard_map.64 = (bf16[80,576]{1,0:T(8,128)(2,1)}, bf16[64,576]{1,0:T(8,128)(2,1)}, bf16[576,128]{1,0:T(8,128)(2,1)}, bf16[576,128]{1,0:T(8,128)(2,1)}, bf16[576,...) custom-call(bf16[8,16,192]{2,1,0:T(8,128)(2,1)} %refs_0_.1, bf16[8,576]{1,0:T(8,128)(2,1)} %refs_1_.1, ...), custom_call_target="tpu_custom_call" | custom-call | tf_op jit(solution)/shard_map/pallas_call | solution.py:172
  19.8 0.6 %collective-permute-start.2 = (bf16[576,128]{1,0:T(8,128)(2,1)}, bf16[576,128]{1,0:T(8,128)(2,1)S(1)}, u32[]{:S(2)}, u32[]{:S(2)}) collective-permute-start(bf16[576,128]{1,0:T(8,128)(2,1)} %get-tuple-element.16), channel_id=1, source_target_pairs={{0,8},{4,12},{8,0},{12,4},{16,24},{20,28},{24,16},{28,20},{1,9},{5... | collective-permute-start | bytes 442376 | tf_op jit(solution)/shard_map/ppermute | solution.py:206
  20.4 0.0 collective-permute-start.3
  20.4 2.9 %collective-permute-start.4 = (bf16[576,128]{1,0:T(8,128)(2,1)}, bf16[576,128]{1,0:T(8,128)(2,1)S(1)}, u32[]{:S(2)}, u32[]{:S(2)}) collective-permute-start(bf16[576,128]{1,0:T(8,128)(2,1)} %get-tuple-element.18), channel_id=1, source_target_pairs={{0,24},{4,28},{8,16},{12,20},{16,8},{20,12},{24,0},{28,4},{1,25},{... | collective-permute-start | bytes 442376 | tf_op jit(solution)/shard_map/ppermute | solution.py:206
  23.3 3.5 %collective-permute-start.1 = (bf16[64,576]{1,0:T(8,128)(2,1)}, bf16[64,576]{1,0:T(8,128)(2,1)S(1)}, u32[]{:S(2)}, u32[]{:S(2)}) collective-permute-start(bf16[64,576]{1,0:T(8,128)(2,1)} %get-tuple-element.14), channel_id=1, source_target_pairs={{0,8},{1,0},{2,12},{3,4},{4,24},{5,16},{6,28},{7,20},{8,9},{9,1},{... | collective-permute-start | bytes 221192 | tf_op jit(solution)/shard_map/ppermute | solution.py:199
  26.9 0.2 collective-permute-start.5
  27.0 0.0 collective-permute-done.2.refs_3_
  27.0 0.3 collective-permute-start.6
  27.4 1.0 %collective-permute-done.3.refs_4_ = bf16[576,128]{1,0:T(8,128)(2,1)S(1)} collective-permute-done((bf16[576,128]{1,0:T(8,128)(2,1)}, bf16[576,128]{1,0:T(8,128)(2,1)S(1)}, u32[]{:S(2)}, u32[]{:S(2)}) %collective-permute-start.3) | collective-permute-done | bytes 147488 | tf_op jit(solution)/shard_map/ppermute | solution.py:206
  28.3 0.0 collective-permute-start.7
  28.3 3.0 %collective-permute-done.4.refs_5_ = bf16[576,128]{1,0:T(8,128)(2,1)S(1)} collective-permute-done((bf16[576,128]{1,0:T(8,128)(2,1)}, bf16[576,128]{1,0:T(8,128)(2,1)S(1)}, u32[]{:S(2)}, u32[]{:S(2)}) %collective-permute-start.4) | collective-permute-done | bytes 147488 | tf_op jit(solution)/shard_map/ppermute | solution.py:206
  31.4 0.0 collective-permute-start.8
  31.4 0.0 collective-permute-done.1.refs_1_
  31.4 7.0 %collective-permute-start = (bf16[80,576]{1,0:T(8,128)(2,1)}, bf16[80,576]{1,0:T(8,128)(2,1)S(1)}, u32[]{:S(2)}, u32[]{:S(2)}) collective-permute-start(bf16[80,576]{1,0:T(8,128)(2,1)} %get-tuple-element.13), channel_id=1, source_target_pairs={{0,0},{1,8},{2,4},{3,12},{4,16},{5,24},{6,20},{7,28},{8,1},{9,9},{... | collective-permute-start | bytes 276488 | tf_op jit(solution)/shard_map/ppermute | solution.py:199
  38.3 6.3 %collective-permute-done.refs_0_ = bf16[80,576]{1,0:T(8,128)(2,1)S(1)} collective-permute-done((bf16[80,576]{1,0:T(8,128)(2,1)}, bf16[80,576]{1,0:T(8,128)(2,1)S(1)}, u32[]{:S(2)}, u32[]{:S(2)}) %collective-permute-start) | collective-permute-done | bytes 92192 | tf_op jit(solution)/shard_map/ppermute | solution.py:199
  44.7 0.0 collective-permute-done.8.refs_9_
  44.7 0.9 %copy-done.1 = bf16[576,128]{1,0:T(8,128)(2,1)S(1)} copy-done((bf16[576,128]{1,0:T(8,128)(2,1)S(1)}, bf16[576,128]{1,0:T(8,128)(2,1)}, u32[]{:S(2)}) %copy-start.1) | copy-done | bytes 147480
  45.6 1.6 %shard_map.65 = (bf16[64,512]{1,0:T(8,128)(2,1)S(1)}, bf16[64,512]{1,0:T(8,128)(2,1)S(1)}) custom-call(s32[16]{0:T(128)S(1)} %copy-done.2, bf16[80,576]{1,0:T(8,128)(2,1)S(1)} %collective-permute-done.refs_0_, bf16[64,576]{1,0:T(8,128)(2,1)S(1)} %collective-permute-done.1.refs_1_, bf16[576,128]{1,0:T(8,128)(2,1)S(1)} %copy-done.1, ...), custom_call_target="tpu_custom_call" | custom-call | tf_op jit(solution)/shard_map/pallas_call | solution.py:215
  47.2 1.9 %collective-permute-start.9 = (bf16[64,512]{1,0:T(8,128)(2,1)S(1)}, bf16[64,512]{1,0:T(8,128)(2,1)S(1)}, u32[]{:S(2)}, u32[]{:S(2)}) collective-permute-start(bf16[64,512]{1,0:T(8,128)(2,1)S(1)} %get-tuple-element.19), channel_id=1, source_target_pairs={{0,0},{8,1},{4,2},{12,3},{16,4},{24,5},{20,6},{28,7},{1,8},{9,9},{... | collective-permute-start | bytes 196616 | tf_op jit(solution)/shard_map/ppermute | solution.py:224
  49.2 0.1 collective-permute-start.10
  49.2 7.8 %collective-permute-done.9.refs_0_ = bf16[64,512]{1,0:T(8,128)(2,1)S(1)} collective-permute-done((bf16[64,512]{1,0:T(8,128)(2,1)S(1)}, bf16[64,512]{1,0:T(8,128)(2,1)S(1)}, u32[]{:S(2)}, u32[]{:S(2)}) %collective-permute-start.9) | collective-permute-done | bytes 65568 | tf_op jit(solution)/shard_map/ppermute | solution.py:224
  57.0 0.0 collective-permute-done.10.refs_1_
  57.0 1.6 %copy-done = bf16[16,512,128]{2,1,0:T(8,128)(2,1)S(1)} copy-done((bf16[16,512,128]{2,1,0:T(8,128)(2,1)S(1)}, bf16[16,512,128]{2,1,0:T(8,128)(2,1)}, u32[]{:S(2)}) %copy-start) | copy-done | bytes 2097176
  58.6 1.3 %shard_map.66 = bf16[8,16,128]{2,1,0:T(8,128)(2,1)} custom-call(bf16[16,512,128]{2,1,0:T(8,128)(2,1)S(1)} %copy-done, bf16[64,512]{1,0:T(8,128)(2,1)S(1)} %collective-permute-done.9.refs_0_, bf16[64,512]{1,0:T(8,128)(2,1)S(1)} %collective-permute-done.10.refs_1_), custom_call_target="tpu_custom_call" | custom-call | tf_op jit(solution)/shard_map/pallas_call | solution.py:226
  (7 shorter events, 0.0 us)
Async XLA Ops:
  0.0 44.7 %copy-start.2 = (s32[16]{0:T(128)S(1)}, s32[16]{0:T(128)}, u32[]{:S(2)}) copy-start(s32[16]{0:T(128)} %len_ref.1) | copy-start | bytes 196
  19.8 7.3 %collective-permute-start.2 = (bf16[576,128]{1,0:T(8,128)(2,1)}, bf16[576,128]{1,0:T(8,128)(2,1)S(1)}, u32[]{:S(2)}, u32[]{:S(2)}) collective-permute-start(bf16[576,128]{1,0:T(8,128)(2,1)} %get-tuple-element.16), channel_id=1, source_target_pairs={{0,8},{4,12},{8,0},{12,4},{16,24},{20,28},{24,16},{28,20},{1,9},{5... | collective-permute-start | bytes 442376 | tf_op jit(solution)/shard_map/ppermute | solution.py:206
  20.4 8.0 %collective-permute-start.3 = (bf16[576,128]{1,0:T(8,128)(2,1)}, bf16[576,128]{1,0:T(8,128)(2,1)S(1)}, u32[]{:S(2)}, u32[]{:S(2)}) collective-permute-start(bf16[576,128]{1,0:T(8,128)(2,1)} %get-tuple-element.17), channel_id=1, source_target_pairs={{0,16},{4,20},{8,24},{12,28},{16,0},{20,4},{24,8},{28,12},{1,17},{... | collective-permute-start | bytes 442376 | tf_op jit(solution)/shard_map/ppermute | solution.py:206
  20.4 10.9 %collective-permute-start.4 = (bf16[576,128]{1,0:T(8,128)(2,1)}, bf16[576,128]{1,0:T(8,128)(2,1)S(1)}, u32[]{:S(2)}, u32[]{:S(2)}) collective-permute-start(bf16[576,128]{1,0:T(8,128)(2,1)} %get-tuple-element.18), channel_id=1, source_target_pairs={{0,24},{4,28},{8,16},{12,20},{16,8},{20,12},{24,0},{28,4},{1,25},{... | collective-permute-start | bytes 442376 | tf_op jit(solution)/shard_map/ppermute | solution.py:206
  23.3 8.1 %collective-permute-start.1 = (bf16[64,576]{1,0:T(8,128)(2,1)}, bf16[64,576]{1,0:T(8,128)(2,1)S(1)}, u32[]{:S(2)}, u32[]{:S(2)}) collective-permute-start(bf16[64,576]{1,0:T(8,128)(2,1)} %get-tuple-element.14), channel_id=1, source_target_pairs={{0,8},{1,0},{2,12},{3,4},{4,24},{5,16},{6,28},{7,20},{8,9},{9,1},{... | collective-permute-start | bytes 221192 | tf_op jit(solution)/shard_map/ppermute | solution.py:199
  26.9 17.8 %collective-permute-start.5 = (bf16[576,128]{1,0:T(8,128)(2,1)}, bf16[576,128]{1,0:T(8,128)(2,1)S(1)}, u32[]{:S(2)}, u32[]{:S(2)}) collective-permute-start(bf16[576,128]{1,0:T(8,128)(2,1)} %get-tuple-element.15.refs_2_), channel_id=1, source_target_pairs={{0,4},{4,0},{8,12},{12,8},{16,20},{20,16},{24,28},{28,24},{1,5},{5... | collective-permute-start | bytes 442376 | tf_op jit(solution)/shard_map/ppermute | solution.py:213
  27.0 17.7 %collective-permute-start.6 = (bf16[576,128]{1,0:T(8,128)(2,1)S(1)}, bf16[576,128]{1,0:T(8,128)(2,1)S(1)}, u32[]{:S(2)}, u32[]{:S(2)}) collective-permute-start(bf16[576,128]{1,0:T(8,128)(2,1)S(1)} %collective-permute-done.2.refs_3_), channel_id=1, source_target_pairs={{0,4},{4,0},{8,12},{12,8},{16,20},{20,16},{24,28},{28,24},{1,5},{5... | collective-permute-start | bytes 442376 | tf_op jit(solution)/shard_map/ppermute | solution.py:213
  28.3 16.4 %collective-permute-start.7 = (bf16[576,128]{1,0:T(8,128)(2,1)S(1)}, bf16[576,128]{1,0:T(8,128)(2,1)S(1)}, u32[]{:S(2)}, u32[]{:S(2)}) collective-permute-start(bf16[576,128]{1,0:T(8,128)(2,1)S(1)} %collective-permute-done.3.refs_4_), channel_id=1, source_target_pairs={{0,4},{4,0},{8,12},{12,8},{16,20},{20,16},{24,28},{28,24},{1,5},{5... | collective-permute-start | bytes 442376 | tf_op jit(solution)/shard_map/ppermute | solution.py:213
  31.4 13.3 %collective-permute-start.8 = (bf16[576,128]{1,0:T(8,128)(2,1)S(1)}, bf16[576,128]{1,0:T(8,128)(2,1)S(1)}, u32[]{:S(2)}, u32[]{:S(2)}) collective-permute-start(bf16[576,128]{1,0:T(8,128)(2,1)S(1)} %collective-permute-done.4.refs_5_), channel_id=1, source_target_pairs={{0,4},{4,0},{8,12},{12,8},{16,20},{20,16},{24,28},{28,24},{1,5},{5... | collective-permute-start | bytes 442376 | tf_op jit(solution)/shard_map/ppermute | solution.py:213
  31.4 13.3 %collective-permute-start = (bf16[80,576]{1,0:T(8,128)(2,1)}, bf16[80,576]{1,0:T(8,128)(2,1)S(1)}, u32[]{:S(2)}, u32[]{:S(2)}) collective-permute-start(bf16[80,576]{1,0:T(8,128)(2,1)} %get-tuple-element.13), channel_id=1, source_target_pairs={{0,0},{1,8},{2,4},{3,12},{4,16},{5,24},{6,20},{7,28},{8,1},{9,9},{... | collective-permute-start | bytes 276488 | tf_op jit(solution)/shard_map/ppermute | solution.py:199
  44.7 0.9 %copy-start.1 = (bf16[576,128]{1,0:T(8,128)(2,1)S(1)}, bf16[576,128]{1,0:T(8,128)(2,1)}, u32[]{:S(2)}) copy-start(bf16[576,128]{1,0:T(8,128)(2,1)} %get-tuple-element.15.refs_2_) | copy-start | bytes 442372
  47.2 9.8 %collective-permute-start.9 = (bf16[64,512]{1,0:T(8,128)(2,1)S(1)}, bf16[64,512]{1,0:T(8,128)(2,1)S(1)}, u32[]{:S(2)}, u32[]{:S(2)}) collective-permute-start(bf16[64,512]{1,0:T(8,128)(2,1)S(1)} %get-tuple-element.19), channel_id=1, source_target_pairs={{0,0},{8,1},{4,2},{12,3},{16,4},{24,5},{20,6},{28,7},{1,8},{9,9},{... | collective-permute-start | bytes 196616 | tf_op jit(solution)/shard_map/ppermute | solution.py:224
  49.2 7.8 %collective-permute-start.10 = (bf16[64,512]{1,0:T(8,128)(2,1)S(1)}, bf16[64,512]{1,0:T(8,128)(2,1)S(1)}, u32[]{:S(2)}, u32[]{:S(2)}) collective-permute-start(bf16[64,512]{1,0:T(8,128)(2,1)S(1)} %get-tuple-element.20), channel_id=1, source_target_pairs={{8,0},{0,1},{12,2},{4,3},{24,4},{16,5},{28,6},{20,7},{9,8},{1,9},{... | collective-permute-start | bytes 196616 | tf_op jit(solution)/shard_map/ppermute | solution.py:224
  57.0 1.6 %copy-start = (bf16[16,512,128]{2,1,0:T(8,128)(2,1)S(1)}, bf16[16,512,128]{2,1,0:T(8,128)(2,1)}, u32[]{:S(2)}) copy-start(bf16[16,512,128]{2,1,0:T(8,128)(2,1)} %w_ref.1) | copy-start | bytes 6291460

commit v4 on v1

--- a/solution.py
+++ b/solution.py
@@ -13,39 +13,74 @@
 SPEC = 4
 SCORE_SCALE = (NOPE + ROPE) ** (-0.5)
 VMEM_LIMIT = 16 * 1024 * 1024
+LONG = pl.CostEstimate(flops=2 * 10**10, bytes_accessed=0, transcendentals=0)
 
 masked_value = -1e30
 
 
-def pick_kernel(owners, copies, cache_ref, *rest):
-    outs, sem = rest[:-1], rest[-1]
-    group = lax.axis_index("seq") // copies
+def copy_all(sources, targets, sem):
     moves = [
-        pltpu.make_async_copy(cache_ref.at[group ^ k], outs[k], sem.at[k])
-        for k in range(owners)
+        pltpu.make_async_copy(source, target, sem.at[n])
+        for n, (source, target) in enumerate(zip(sources, targets))
     ]
     for move in moves:
         move.start()
-    for move in moves:
+    return moves
+
+
+def pack_kernel(owners, copies, cache_hbm, q_hbm, new_hbm, *refs):
+    picked, (pack_ref, q_ref, new_ref, sem) = refs[:owners], refs[owners:]
+    group = lax.axis_index("seq") // copies
+    moves = copy_all(
+        [q_hbm, new_hbm] + [cache_hbm.at[group ^ k] for k in range(owners)],
+        [q_ref, new_ref] + list(picked),
+        sem,
+    )
+    moves[0].wait()
+    moves[1].wait()
+    rows, heads, width = q_ref.shape
+    pack_ref[: rows * heads, :] = q_ref[...].reshape(rows * heads, width)
+    fresh = new_ref[...].astype(jnp.float32)
+    parts = [fresh[:, n : n + width] for n in range(0, fresh.shape[1], width)]
+    spare = pack_ref.shape[0] - rows * heads - rows * len(parts)
+    if spare:
+        parts.append(jnp.zeros((spare, width), jnp.float32))
+    pack_ref[rows * heads :, :] = jnp.concatenate(parts, axis=0).astype(pack_ref.dtype)
+    for move in moves[2:]:
         move.wait()
 
 
-def absorb_kernel(per_device, fresh_pad, q_ref, new_ref, w_ref, *outs):
-    rows, heads, width = q_ref.shape
-    q = q_ref[...].reshape(rows * heads, width)
+def place_kernel(owners, copies, *refs):
+    blocks, out_ref, sem = refs[:-2], refs[-2], refs[-1]
+    group = lax.axis_index("seq") // copies
+    for move in copy_all(blocks, [out_ref.at[group ^ k] for k in range(owners)], sem):
+        move.wait()
+
+
+def absorb_kernel(per_device, rows, pack_ref, w_ref, *outs):
+    heads = w_ref.shape[0]
+    piece, all_rows = SPEC * heads, rows * heads
+    q = pack_ref[:all_rows, :]
     nope = q[:, :NOPE]
-    own_head = lax.broadcasted_iota(jnp.int32, (rows * heads, NOPE), 0) % heads
+    own_head = lax.broadcasted_iota(jnp.int32, nope.shape, 0) % heads
     spread = jnp.concatenate(
         [jnp.where(own_head == h, nope, jnp.zeros_like(nope)) for h in range(heads)], axis=1
     )
     absorbed = jnp.dot(
         spread, w_ref[...].reshape(heads * NOPE, LATENT), preferred_element_type=jnp.float32
     ).astype(jnp.bfloat16)
-    piece = SPEC * heads
-    fresh = new_ref[...].astype(jnp.float32)
+    fresh = pack_ref[all_rows:, :].astype(jnp.float32)
     fresh = jnp.concatenate(
-        [fresh, jnp.zeros((fresh_pad - rows, fresh.shape[1]), jnp.float32)], axis=0
-    ).astype(jnp.bfloat16)
+        [
+            fresh[n * rows : (n + 1) * rows]
+            for n in range((LATENT + ROPE) // (NOPE + ROPE))
+        ],
+        axis=1,
+    )
+    spare = outs[0].shape[0] - piece - rows
+    if spare:
+        fresh = jnp.concatenate([fresh, jnp.zeros((spare, fresh.shape[1]), jnp.float32)], axis=0)
+    outs[0][piece:, :] = fresh.astype(jnp.bfloat16)
     head_shard = lax.axis_index("head")
     for k in range(per_device):
         which = (head_shard + k) % per_device
@@ -56,51 +91,86 @@
                 outs[k][:piece, :LATENT] = absorbed[a * piece : (a + 1) * piece]
                 outs[k][:piece, LATENT:] = q[a * piece : (a + 1) * piece, NOPE:]
 
-        if k == 0:
-            outs[k][piece:, :] = fresh
-
-
-def attend_kernel(owners, copies, per_device, heads, len_ref, *refs):
-    block_count = owners * copies
-    q_refs = refs[:per_device]
-    key_refs = refs[per_device : per_device + block_count]
-    outs = refs[per_device + block_count :]
+
+def block_scores(q, keys_ref, n, start, length):
+    s = jnp.dot(q, keys_ref[n], preferred_element_type=jnp.float32) * SCORE_SCALE
+    lane = lax.broadcasted_iota(jnp.int32, (1, s.shape[1]), 1)
+    return jnp.where(lane + start < length, s, masked_value)
+
+
+def weigh(scores, values, top):
+    total, out = 0.0, 0.0
+    for s, value in zip(scores, values):
+        w = jnp.exp(s - top)
+        total += jnp.sum(w, axis=1, keepdims=True)
+        out += lax.dot_general(
+            w.astype(jnp.bfloat16),
+            value(),
+            (((1,), (1,)), ((), ())),
+            preferred_element_type=jnp.float32,
+        )
+    return total, out
+
+
+def begin_kernel(owners, copies, per_device, heads, len_ref, *refs):
+    q_refs, (keys_ref, q_out, top_ref, total_ref, out_ref) = refs[:per_device], refs[per_device:]
     seq_index = lax.axis_index("seq")
-    group, core = seq_index // copies, seq_index % copies
-    sequence = lax.axis_index("head") * owners + group
+    sequence = lax.axis_index("head") * owners + seq_index // copies
     length = len_ref[sequence]
     piece = SPEC * heads
+    slots = keys_ref.shape[2]
     q = jnp.concatenate([ref[:piece, :] for ref in q_refs], axis=0)
     fresh = q_refs[0][piece:, :]
-    slots = key_refs[0].shape[1]
-    lane = lax.broadcasted_iota(jnp.int32, (1, slots), 1)
-    scores = []
-    for k in range(owners):
-        for e in range(copies):
-            start = ((group ^ k) * copies + (core + copies - e) % copies) * slots
-            s = jnp.dot(q, key_refs[k * copies + e][...], preferred_element_type=jnp.float32)
-            scores.append(jnp.where(lane + start < length, s * SCORE_SCALE, masked_value))
+    scores = [
+        block_scores(q, keys_ref, g, (g * copies + seq_index % copies) * slots, length)
+        for g in range(owners)
+    ]
     s = lax.dot_general(
         q, fresh, (((1,), (1,)), ((), ())), preferred_element_type=jnp.float32
     )
     row = lax.broadcasted_iota(jnp.int32, s.shape, 0)
     key = lax.broadcasted_iota(jnp.int32, s.shape, 1)
     causal = (key // SPEC == sequence % per_device) & (key % SPEC <= (row % piece) // heads)
-    scores.append(jnp.where(causal, s * SCORE_SCALE, masked_value))
-    top = functools.reduce(jnp.maximum, [jnp.max(s, axis=1, keepdims=True) for s in scores])
-    total = jnp.zeros_like(top)
-    out = jnp.zeros((q.shape[0], LATENT), jnp.float32)
-    for s, ref in zip(scores, list(key_refs) + [None]):
-        w = jnp.exp(s - top)
-        total += jnp.sum(w, axis=1, keepdims=True)
-        w = w.astype(jnp.bfloat16)
-        if ref is None:
-            out += jnp.dot(w, fresh[:, :LATENT], preferred_element_type=jnp.float32)
-        else:
-            out += lax.dot_general(
-                w, ref[:LATENT, :], (((1,), (1,)), ((), ())), preferred_element_type=jnp.float32
-            )
-    out = (out / total).astype(jnp.bfloat16)
+    s = jnp.where(causal, s * SCORE_SCALE, masked_value)
+    top = functools.reduce(
+        jnp.maximum, [jnp.max(s, axis=1, keepdims=True) for s in scores + [s]]
+    )
+    total, out = weigh(
+        scores, [functools.partial(lambda g: keys_ref[g, :LATENT, :], g) for g in range(owners)], top
+    )
+    w = jnp.exp(s - top)
+    total += jnp.sum(w, axis=1, keepdims=True)
+    out += jnp.dot(
+        w.astype(jnp.bfloat16), fresh[:, :LATENT], preferred_element_type=jnp.float32
+    )
+    q_out[...] = q
+    top_ref[...] = jnp.broadcast_to(top, top_ref.shape)
+    total_ref[...] = jnp.broadcast_to(total, total_ref.shape)
+    out_ref[...] = out
+
+
+def finish_kernel(owners, copies, per_device, len_ref, q_ref, top_ref, total_ref, part_ref, *refs):
+    key_refs, outs = refs[: copies - 1], refs[copies - 1 :]
+    seq_index = lax.axis_index("seq")
+    length = len_ref[lax.axis_index("head") * owners + seq_index // copies]
+    q = q_ref[...]
+    scores, values = [], []
+    for e in range(1, copies):
+        core = (seq_index + copies - e) % copies
+        for g in range(owners):
+            keys_ref = key_refs[e - 1]
+            start = (g * copies + core) * keys_ref.shape[2]
+            scores.append(block_scores(q, keys_ref, g, start, length))
+            values.append(functools.partial(lambda r, g: r[g, :LATENT, :], keys_ref, g))
+    first = top_ref[:, :1]
+    top = functools.reduce(
+        jnp.maximum, [first] + [jnp.max(s, axis=1, keepdims=True) for s in scores]
+    )
+    total, out = weigh(scores, values, top)
+    scale = jnp.exp(first - top)
+    out = (out + part_ref[...] * scale) / (total + total_ref[:, :1] * scale)
+    out = out.astype(jnp.bfloat16)
+    piece = out.shape[0] // per_device
     for k in range(per_device):
         outs[k][...] = out[k * piece : (k + 1) * piece]
 
@@ -129,12 +199,13 @@
 
 
 def whole_sequences(seq_size, head_size, queries, new_latent, cache, lengths, w_uk, w_uv):
-    rows, heads, _ = queries.shape
+    rows, heads, q_width = queries.shape
     owners, slots, width = cache.shape
     copies = seq_size // owners
     per_device = rows // SPEC
     piece = SPEC * heads
     fresh_pad = -(-rows // 16) * 16
+    packed_rows = rows * heads + -(-rows * (width // q_width) // 16) * 16
     params = pltpu.CompilerParams(vmem_limit_bytes=VMEM_LIMIT)
     vmem = pl.BlockSpec(memory_space=pltpu.VMEM)
     anywhere = pl.BlockSpec(memory_space=pl.ANY)
@@ -143,59 +214,107 @@
     def flat(seq_index, head_index):
         return seq_index * head_size + head_index
 
-    turned = jnp.swapaxes(cache, 1, 2)
-    picked = pl.pallas_call(
-        functools.partial(pick_kernel, owners, copies),
-        out_shape=[jax.ShapeDtypeStruct((width, slots), cache.dtype)] * owners,
-        in_specs=[anywhere],
-        out_specs=[anywhere] * owners,
-        scratch_shapes=[pltpu.SemaphoreType.DMA((owners,))],
+    def in_hbm(x):
+        return pltpu.with_memory_space_constraint(x, pltpu.HBM)
+
+    *picked, packed = pl.pallas_call(
+        functools.partial(pack_kernel, owners, copies),
+        out_shape=[jax.ShapeDtypeStruct((width, slots), cache.dtype)] * owners
+        + [jax.ShapeDtypeStruct((packed_rows, q_width), queries.dtype)],
+        in_specs=[anywhere] * 3,
+        out_specs=[vmem] * (owners + 1),
+        scratch_shapes=[
+            pltpu.VMEM(queries.shape, queries.dtype),
+            pltpu.VMEM(new_latent.shape, new_latent.dtype),
+            pltpu.SemaphoreType.DMA((owners + 2,)),
+        ],
         compiler_params=params,
-    )(turned)
-    keys = []
-    for k in range(owners):
-        for e in range(copies):
-            if k == 0 and e == 0:
-                keys.append(picked[0])
-                continue
-            perm = [
-                (g * copies + t, (g ^ k) * copies + (t + e) % copies)
-                for g in range(owners)
-                for t in range(copies)
-            ]
-            keys.append(lax.ppermute(picked[k], "seq", perm))
-
+        cost_estimate=LONG,
+    )(in_hbm(jnp.swapaxes(cache, 1, 2)), in_hbm(queries), in_hbm(new_latent))
+
+    block = seq_size // head_size
+    turn = (0, 2, 3, 1) if head_size == 4 else range(head_size)
+
+    def host(i, j):
+        return ((i // block) ^ turn[j]) * block + i % block
+
+    devices = [(i, j) for i in range(seq_size) for j in range(head_size)]
+    packed = lax.ppermute(packed, both, [(flat(i, j), flat(host(i, j), j)) for i, j in devices])
     pieces = pl.pallas_call(
-        functools.partial(absorb_kernel, per_device, fresh_pad),
+        functools.partial(absorb_kernel, per_device, rows),
         out_shape=[
             jax.ShapeDtypeStruct((piece + (fresh_pad if k == 0 else 0), width), cache.dtype)
             for k in range(per_device)
         ],
-        in_specs=[vmem] * 3,
+        in_specs=[vmem] * 2,
         out_specs=[vmem] * per_device,
         compiler_params=params,
-    )(queries, new_latent, w_uk)
-    there = []
-    for k in range(per_device):
-        perm = []
-        for i in range(seq_size):
-            for j in range(head_size):
-                sequence = i * per_device + (j + k) % per_device
-                target = (sequence % owners) * copies + j // per_device
-                perm.append((flat(i, j), flat(target, sequence // owners)))
-        there.append(perm)
-    arrived = [lax.ppermute(pieces[k], both, there[k]) for k in range(per_device)]
-
+        cost_estimate=LONG,
+    )(packed, w_uk)
+
+    def owner(i, j, k):
+        sequence = i * per_device + (j + k) % per_device
+        return flat((sequence % owners) * copies + j // per_device, sequence // owners)
+
+    arrived = [
+        lax.ppermute(
+            pieces[k], both, [(flat(host(i, j), j), owner(i, j, k)) for i, j in devices]
+        )
+        for k in range(per_device)
+    ]
+
+    def in_plane(move):
+        return [
+            (g * copies + t, move(g, t)) for g in range(owners) for t in range(copies)
+        ]
+
+    blocks = [picked[0]] + [
+        lax.ppermute(picked[k], "seq", in_plane(lambda g, t: (g ^ k) * copies + t))
+        for k in range(1, owners)
+    ]
+    keys = [
+        pl.pallas_call(
+            functools.partial(place_kernel, owners, copies),
+            out_shape=jax.ShapeDtypeStruct((owners, width, slots), cache.dtype),
+            in_specs=[anywhere] * owners,
+            out_specs=vmem,
+            scratch_shapes=[pltpu.SemaphoreType.DMA((owners,))],
+            compiler_params=params,
+        )(*blocks)
+    ]
+    for e in range(1, copies):
+        keys.append(
+            lax.ppermute(
+                keys[0], "seq", in_plane(lambda g, t: g * copies + (t + e) % copies)
+            )
+        )
+
+    all_rows = per_device * piece
+    smem = pl.BlockSpec(memory_space=pltpu.SMEM)
+    state = pl.pallas_call(
+        functools.partial(begin_kernel, owners, copies, per_device, heads),
+        out_shape=[
+            jax.ShapeDtypeStruct((all_rows, width), jnp.bfloat16),
+            jax.ShapeDtypeStruct((all_rows, 128), jnp.float32),
+            jax.ShapeDtypeStruct((all_rows, 128), jnp.float32),
+            jax.ShapeDtypeStruct((all_rows, LATENT), jnp.float32),
+        ],
+        in_specs=[smem] + [vmem] * (per_device + 1),
+        out_specs=[vmem] * 4,
+        compiler_params=params,
+        cost_estimate=LONG,
+    )(lengths, *arrived, keys[0])
     latent = pl.pallas_call(
-        functools.partial(attend_kernel, owners, copies, per_device, heads),
+        functools.partial(finish_kernel, owners, copies, per_device),
         out_shape=[jax.ShapeDtypeStruct((piece, LATENT), jnp.bfloat16)] * per_device,
-        in_specs=[pl.BlockSpec(memory_space=pltpu.SMEM)] + [vmem] * (per_device + len(keys)),
+        in_specs=[smem] + [vmem] * (len(state) + copies - 1),
         out_specs=[vmem] * per_device,
         compiler_params=params,
-    )(lengths, *arrived, *keys)
+    )(lengths, *state, *keys[1:])
 
     back = [
-        lax.ppermute(latent[k], both, [(b, a) for a, b in there[k]]) for k in range(per_device)
+        lax.ppermute(latent[k], both, [(owner(i, j, k), flat(i, j)) for i, j in devices])
+        for k in range(per_device)
     ]
     return pl.pallas_call(
         functools.partial(project_kernel, per_device),
@@ -313,6 +432,9 @@
         and owners & (owners - 1) == 0
         and seq_size % owners == 0
         and head_size == per_device * (seq_size // owners)
+        and head_size & (head_size - 1) == 0
+        and seq_size % head_size == 0
+        and cache.shape[2] % queries.shape[2] == 0
     ):
         return whole_sequences(
             seq_size, head_size, queries, new_latent, cache, lengths, w_uk, w_uv

time: 52.8 us -> 36.4 us (0.69)
  the two profiles are of different devices: /device:TPU:9 before, /device:TPU:6 now
where the time goes in v4:
time: 36.4 us; the launch traced here: 36.2 us
  starting transfers between devices  19 us (52%)
  waiting for transfers between devices  10.4 us (29%)
  Pallas kernels  6.63 us (18%)
    ppermute x2, starting transfers between devices, whole_sequences(): lax.ppermute(pieces[k], both, [(flat(host(i, j), j), owner(i, j, k)) for...  10.4 us
    ppermute x2, waiting for transfers between devices, whole_sequences(): lax.ppermute(latent[k], both, [(owner(i, j, k), flat(i, j)) for i, j in d...  6.95 us
    ppermute x2, starting transfers between devices, whole_sequences(): lax.ppermute(latent[k], both, [(owner(i, j, k), flat(i, j)) for i, j in d...  4.2 us
    ppermute x3, starting transfers between devices, whole_sequences(): lax.ppermute(picked[k], 'seq', in_plane(lambda g, t: (g ^ k) * copies + t))  3.55 us
    ppermute x2, waiting for transfers between devices, whole_sequences(): lax.ppermute(pieces[k], both, [(flat(host(i, j), j), owner(i, j, k)) for...  3.43 us
    pallas_call x1, Pallas kernels, whole_sequences(): pl.pallas_call(functools.partial(pack_kernel, owners, copies), out_shape=...  1.37 us
    pallas_call x1, Pallas kernels, whole_sequences(): pl.pallas_call(functools.partial(finish_kernel, owners, copies, per_devic...  1.33 us
    pallas_call x1, Pallas kernels, whole_sequences(): pl.pallas_call(functools.partial(project_kernel, per_device), out_shape=j...  1.32 us
  transfers between devices with their start and end apart: 9, of which 3 were waited for; matrix products, arithmetic and copies ran while one was open for 0% of the time, Pallas kernels for 7%

profile of v4, /device:TPU:6, one launch (start us, length us, event | category | flops | bytes accessed | tf_op | source)
XLA Modules:
  0.0 36.2 jit_solution(5886300237676785342)
XLA Ops:
  0.0 1.4 %shard_map.64 = (bf16[576,128]{1,0:T(8,128)(2,1)S(1)}, bf16[576,128]{1,0:T(8,128)(2,1)S(1)}, bf16[576,128]{1,0:T(8,128)(2,1)S(1)}, bf16[576,128]{1,0:T(8,128)(2,1)S(1)}, bf16[160,192]{1,0:T(8,128)(2,1)S(1)}) custom-call(bf16[4,576,128]{2,1,0:T(8,128)(2,1)} %bitcast.1, bf16[8,16,192]{2,1,0:T(8,128)(2,1)} %q_hbm.1, bf16[8,576]{1,0:T(8,128)(2,1)} %new_hbm.1), custom_call_target="tpu_custom_call" | custom-call | flops 20000000000 | tf_op jit(solution)/shard_map/pallas_call | solution.py:220
  1.4 0.7 %collective-permute-start = (bf16[160,192]{1,0:T(8,128)(2,1)S(1)}, bf16[160,192]{1,0:T(8,128)(2,1)S(1)}, u32[]{:S(2)}, u32[]{:S(2)}) collective-permute-start(bf16[160,192]{1,0:T(8,128)(2,1)S(1)} %get-tuple-element.18), channel_id=1, source_target_pairs={{0,0},{1,17},{2,26},{3,11},{4,4},{5,21},{6,30},{7,15},{8,8},{9,25}... | collective-permute-start | bytes 184328 | tf_op jit(solution)/shard_map/ppermute | solution.py:242
  2.1 0.6 %collective-permute-start.3 = (bf16[576,128]{1,0:T(8,128)(2,1)S(1)}, bf16[576,128]{1,0:T(8,128)(2,1)S(1)}, u32[]{:S(2)}, u32[]{:S(2)}) collective-permute-start(bf16[576,128]{1,0:T(8,128)(2,1)S(1)} %get-tuple-element.22), channel_id=1, source_target_pairs={{0,8},{4,12},{8,0},{12,4},{16,24},{20,28},{24,16},{28,20},{1,9},{5... | collective-permute-start | bytes 442376 | tf_op jit(solution)/shard_map/ppermute | solution.py:272
  2.7 0.1 collective-permute-start.4
  2.7 2.9 %collective-permute-start.5 = (bf16[576,128]{1,0:T(8,128)(2,1)S(1)}, bf16[576,128]{1,0:T(8,128)(2,1)S(1)}, u32[]{:S(2)}, u32[]{:S(2)}) collective-permute-start(bf16[576,128]{1,0:T(8,128)(2,1)S(1)} %get-tuple-element.24), channel_id=1, source_target_pairs={{0,24},{4,28},{8,16},{12,20},{16,8},{20,12},{24,0},{28,4},{1,25},{... | collective-permute-start | bytes 442376 | tf_op jit(solution)/shard_map/ppermute | solution.py:272
  5.6 0.0 collective-permute-done.pack_ref
  5.6 0.5 %shard_map.65 = (bf16[80,576]{1,0:T(8,128)(2,1)S(1)}, bf16[64,576]{1,0:T(8,128)(2,1)S(1)}) custom-call(bf16[160,192]{1,0:T(8,128)(2,1)S(1)} %collective-permute-done.pack_ref, bf16[16,128,512]{2,1,0:T(8,128)(2,1)S(1)} %copy-done.2), custom_call_target="tpu_custom_call" | custom-call | flops 20000000000 | tf_op jit(solution)/shard_map/pallas_call | solution.py:243
  6.1 8.2 %collective-permute-start.1 = (bf16[80,576]{1,0:T(8,128)(2,1)S(1)}, bf16[80,576]{1,0:T(8,128)(2,1)S(1)}, u32[]{:S(2)}, u32[]{:S(2)}) collective-permute-start(bf16[80,576]{1,0:T(8,128)(2,1)S(1)} %get-tuple-element.19), channel_id=1, source_target_pairs={{0,0},{17,8},{26,4},{11,12},{4,16},{21,24},{30,20},{15,28},{8,1},{... | collective-permute-start | bytes 276488 | tf_op jit(solution)/shard_map/ppermute | solution.py:260
  14.3 2.1 %collective-permute-start.2 = (bf16[64,576]{1,0:T(8,128)(2,1)S(1)}, bf16[64,576]{1,0:T(8,128)(2,1)S(1)}, u32[]{:S(2)}, u32[]{:S(2)}) collective-permute-start(bf16[64,576]{1,0:T(8,128)(2,1)S(1)} %get-tuple-element.20), channel_id=1, source_target_pairs={{0,8},{17,0},{26,12},{11,4},{4,24},{21,16},{30,28},{15,20},{8,9},{... | collective-permute-start | bytes 221192 | tf_op jit(solution)/shard_map/ppermute | solution.py:260
  16.5 0.0 collective-permute-done.3.refs_1_
  16.5 0.0 collective-permute-done.4.refs_2_
  16.5 0.0 collective-permute-done.5.refs_3_
  16.5 0.8 %shard_map.66.refs_2_ = bf16[4,576,128]{2,1,0:T(8,128)(2,1)S(1)} custom-call(bf16[576,128]{1,0:T(8,128)(2,1)S(1)} %get-tuple-element.21.refs_0_, bf16[576,128]{1,0:T(8,128)(2,1)S(1)} %collective-permute-done.3.refs_1_, bf16[576,128]{1,0:T(8,128)(2,1)S(1)} %collective-permute-done.4.refs_2_, bf16[576,128]{1,0:T(8,128)(2,1)S(1)} %collective-permute-done.5.refs_3_), custom_call_target="tpu_custom_call" | custom-call | tf_op jit(solution)/shard_map/pallas_call | solution.py:276
  17.3 0.2 collective-permute-start.6
  17.6 3.4 %collective-permute-done.2.refs_1_ = bf16[64,576]{1,0:T(8,128)(2,1)S(1)} collective-permute-done((bf16[64,576]{1,0:T(8,128)(2,1)S(1)}, bf16[64,576]{1,0:T(8,128)(2,1)S(1)}, u32[]{:S(2)}, u32[]{:S(2)}) %collective-permute-start.2) | collective-permute-done | bytes 73760 | tf_op jit(solution)/shard_map/ppermute | solution.py:260
  21.0 0.0 collective-permute-done.1.refs_0_
  21.0 1.3 %shard_map.67 = (bf16[128,576]{1,0:T(8,128)(2,1)S(1)}, f32[128,128]{1,0:T(8,128)S(1)}, f32[128,128]{1,0:T(8,128)S(1)}, f32[128,512]{1,0:T(8,128)S(1)}) custom-call(s32[16]{0:T(128)S(1)} %copy-done.1, bf16[80,576]{1,0:T(8,128)(2,1)S(1)} %collective-permute-done.1.refs_0_, bf16[64,576]{1,0:T(8,128)(2,1)S(1)} %collective-permute-done.2.refs_1_, ...), custom_call_target="tpu_custom_call" | custom-call | flops 20000000000 | tf_op jit(solution)/shard_map/pallas_call | solution.py:294
  22.3 0.0 collective-permute-done.6.refs_0_
  22.3 1.3 %shard_map.68 = (bf16[64,512]{1,0:T(8,128)(2,1)S(1)}, bf16[64,512]{1,0:T(8,128)(2,1)S(1)}) custom-call(s32[16]{0:T(128)S(1)} %copy-done.1, bf16[128,576]{1,0:T(8,128)(2,1)S(1)} %get-tuple-element.25.q_ref, f32[128,128]{1,0:T(8,128)S(1)} %get-tuple-element.26.top_ref, f32[128,128]{1,0:T(8,128)S(1)} %get-tuple-element.27.total_ref, ...), custom_call_target="tpu_custom_call" | custom-call | tf_op jit(solution)/shard_map/pallas_call | solution.py:307
  23.7 4.1 %collective-permute-start.7 = (bf16[64,512]{1,0:T(8,128)(2,1)S(1)}, bf16[64,512]{1,0:T(8,128)(2,1)S(1)}, u32[]{:S(2)}, u32[]{:S(2)}) collective-permute-start(bf16[64,512]{1,0:T(8,128)(2,1)S(1)} %get-tuple-element.29), channel_id=1, source_target_pairs={{0,0},{8,1},{4,2},{12,3},{16,4},{24,5},{20,6},{28,7},{1,8},{9,9},{... | collective-permute-start | bytes 196616 | tf_op jit(solution)/shard_map/ppermute | solution.py:316
  27.8 0.1 collective-permute-start.8
  27.9 5.6 %collective-permute-done.7.refs_0_ = bf16[64,512]{1,0:T(8,128)(2,1)S(1)} collective-permute-done((bf16[64,512]{1,0:T(8,128)(2,1)S(1)}, bf16[64,512]{1,0:T(8,128)(2,1)S(1)}, u32[]{:S(2)}, u32[]{:S(2)}) %collective-permute-start.7) | collective-permute-done | bytes 65568 | tf_op jit(solution)/shard_map/ppermute | solution.py:316
  33.5 1.3 %collective-permute-done.8.refs_1_ = bf16[64,512]{1,0:T(8,128)(2,1)S(1)} collective-permute-done((bf16[64,512]{1,0:T(8,128)(2,1)S(1)}, bf16[64,512]{1,0:T(8,128)(2,1)S(1)}, u32[]{:S(2)}, u32[]{:S(2)}) %collective-permute-start.8) | collective-permute-done | bytes 65568 | tf_op jit(solution)/shard_map/ppermute | solution.py:316
  34.9 1.3 %shard_map.69 = bf16[8,16,128]{2,1,0:T(8,128)(2,1)} custom-call(bf16[16,512,128]{2,1,0:T(8,128)(2,1)S(1)} %copy-done, bf16[64,512]{1,0:T(8,128)(2,1)S(1)} %collective-permute-done.7.refs_0_, bf16[64,512]{1,0:T(8,128)(2,1)S(1)} %collective-permute-done.8.refs_1_), custom_call_target="tpu_custom_call" | custom-call | tf_op jit(solution)/shard_map/pallas_call | solution.py:319
  (6 shorter events, 0.0 us)
Async XLA Ops:
  0.0 5.6 %copy-start.2 = (bf16[16,128,512]{2,1,0:T(8,128)(2,1)S(1)}, bf16[16,128,512]{2,1,0:T(8,128)(2,1)}, u32[]{:S(2)}) copy-start(bf16[16,128,512]{2,1,0:T(8,128)(2,1)} %w_ref.2) | copy-start | bytes 6291460
  1.4 4.2 %collective-permute-start = (bf16[160,192]{1,0:T(8,128)(2,1)S(1)}, bf16[160,192]{1,0:T(8,128)(2,1)S(1)}, u32[]{:S(2)}, u32[]{:S(2)}) collective-permute-start(bf16[160,192]{1,0:T(8,128)(2,1)S(1)} %get-tuple-element.18), channel_id=1, source_target_pairs={{0,0},{1,17},{2,26},{3,11},{4,4},{5,21},{6,30},{7,15},{8,8},{9,25}... | collective-permute-start | bytes 184328 | tf_op jit(solution)/shard_map/ppermute | solution.py:242
  2.1 14.4 %collective-permute-start.3 = (bf16[576,128]{1,0:T(8,128)(2,1)S(1)}, bf16[576,128]{1,0:T(8,128)(2,1)S(1)}, u32[]{:S(2)}, u32[]{:S(2)}) collective-permute-start(bf16[576,128]{1,0:T(8,128)(2,1)S(1)} %get-tuple-element.22), channel_id=1, source_target_pairs={{0,8},{4,12},{8,0},{12,4},{16,24},{20,28},{24,16},{28,20},{1,9},{5... | collective-permute-start | bytes 442376 | tf_op jit(solution)/shard_map/ppermute | solution.py:272
  2.7 13.8 %collective-permute-start.4 = (bf16[576,128]{1,0:T(8,128)(2,1)S(1)}, bf16[576,128]{1,0:T(8,128)(2,1)S(1)}, u32[]{:S(2)}, u32[]{:S(2)}) collective-permute-start(bf16[576,128]{1,0:T(8,128)(2,1)S(1)} %get-tuple-element.23), channel_id=1, source_target_pairs={{0,16},{4,20},{8,24},{12,28},{16,0},{20,4},{24,8},{28,12},{1,17},{... | collective-permute-start | bytes 442376 | tf_op jit(solution)/shard_map/ppermute | solution.py:272
  2.7 18.3 %copy-start.1 = (s32[16]{0:T(128)S(1)}, s32[16]{0:T(128)}, u32[]{:S(2)}) copy-start(s32[16]{0:T(128)} %len_ref.3) | copy-start | bytes 196
  2.7 13.8 %collective-permute-start.5 = (bf16[576,128]{1,0:T(8,128)(2,1)S(1)}, bf16[576,128]{1,0:T(8,128)(2,1)S(1)}, u32[]{:S(2)}, u32[]{:S(2)}) collective-permute-start(bf16[576,128]{1,0:T(8,128)(2,1)S(1)} %get-tuple-element.24), channel_id=1, source_target_pairs={{0,24},{4,28},{8,16},{12,20},{16,8},{20,12},{24,0},{28,4},{1,25},{... | collective-permute-start | bytes 442376 | tf_op jit(solution)/shard_map/ppermute | solution.py:272
  6.1 14.9 %collective-permute-start.1 = (bf16[80,576]{1,0:T(8,128)(2,1)S(1)}, bf16[80,576]{1,0:T(8,128)(2,1)S(1)}, u32[]{:S(2)}, u32[]{:S(2)}) collective-permute-start(bf16[80,576]{1,0:T(8,128)(2,1)S(1)} %get-tuple-element.19), channel_id=1, source_target_pairs={{0,0},{17,8},{26,4},{11,12},{4,16},{21,24},{30,20},{15,28},{8,1},{... | collective-permute-start | bytes 276488 | tf_op jit(solution)/shard_map/ppermute | solution.py:260
  14.3 6.7 %collective-permute-start.2 = (bf16[64,576]{1,0:T(8,128)(2,1)S(1)}, bf16[64,576]{1,0:T(8,128)(2,1)S(1)}, u32[]{:S(2)}, u32[]{:S(2)}) collective-permute-start(bf16[64,576]{1,0:T(8,128)(2,1)S(1)} %get-tuple-element.20), channel_id=1, source_target_pairs={{0,8},{17,0},{26,12},{11,4},{4,24},{21,16},{30,28},{15,20},{8,9},{... | collective-permute-start | bytes 221192 | tf_op jit(solution)/shard_map/ppermute | solution.py:260
  17.3 5.0 %collective-permute-start.6 = (bf16[4,576,128]{2,1,0:T(8,128)(2,1)S(1)}, bf16[4,576,128]{2,1,0:T(8,128)(2,1)S(1)}, u32[]{:S(2)}, u32[]{:S(2)}) collective-permute-start(bf16[4,576,128]{2,1,0:T(8,128)(2,1)S(1)} %shard_map.66.refs_2_), channel_id=1, source_target_pairs={{0,4},{4,0},{8,12},{12,8},{16,20},{20,16},{24,28},{28,24},{1,5},{5... | collective-permute-start | bytes 1769480 | tf_op jit(solution)/shard_map/ppermute | solution.py:287
  21.0 13.8 %copy-start = (bf16[16,512,128]{2,1,0:T(8,128)(2,1)S(1)}, bf16[16,512,128]{2,1,0:T(8,128)(2,1)}, u32[]{:S(2)}) copy-start(bf16[16,512,128]{2,1,0:T(8,128)(2,1)} %w_ref.3) | copy-start | bytes 6291460
  23.7 9.8 %collective-permute-start.7 = (bf16[64,512]{1,0:T(8,128)(2,1)S(1)}, bf16[64,512]{1,0:T(8,128)(2,1)S(1)}, u32[]{:S(2)}, u32[]{:S(2)}) collective-permute-start(bf16[64,512]{1,0:T(8,128)(2,1)S(1)} %get-tuple-element.29), channel_id=1, source_target_pairs={{0,0},{8,1},{4,2},{12,3},{16,4},{24,5},{20,6},{28,7},{1,8},{9,9},{... | collective-permute-start | bytes 196616 | tf_op jit(solution)/shard_map/ppermute | solution.py:316
  27.8 7.0 %collective-permute-start.8 = (bf16[64,512]{1,0:T(8,128)(2,1)S(1)}, bf16[64,512]{1,0:T(8,128)(2,1)S(1)}, u32[]{:S(2)}, u32[]{:S(2)}) collective-permute-start(bf16[64,512]{1,0:T(8,128)(2,1)S(1)} %get-tuple-element.30), channel_id=1, source_target_pairs={{8,0},{0,1},{12,2},{4,3},{24,4},{16,5},{28,6},{20,7},{9,8},{1,9},{... | collective-permute-start | bytes 196616 | tf_op jit(solution)/shard_map/ppermute | solution.py:316

commit v5 on v4

--- a/solution.py
+++ b/solution.py
@@ -30,9 +30,9 @@
 
 def pack_kernel(owners, copies, cache_hbm, q_hbm, new_hbm, *refs):
     picked, (pack_ref, q_ref, new_ref, sem) = refs[:owners], refs[owners:]
-    group = lax.axis_index("seq") // copies
+    own = (lax.axis_index("seq") // copies) ^ (owners // 2)
     moves = copy_all(
-        [q_hbm, new_hbm] + [cache_hbm.at[group ^ k] for k in range(owners)],
+        [q_hbm, new_hbm] + [cache_hbm.at[own ^ k] for k in range(owners)],
         [q_ref, new_ref] + list(picked),
         sem,
     )
@@ -115,7 +115,7 @@
 def begin_kernel(owners, copies, per_device, heads, len_ref, *refs):
     q_refs, (keys_ref, q_out, top_ref, total_ref, out_ref) = refs[:per_device], refs[per_device:]
     seq_index = lax.axis_index("seq")
-    sequence = lax.axis_index("head") * owners + seq_index // copies
+    sequence = lax.axis_index("head") * owners + (seq_index // copies ^ (owners // 2))
     length = len_ref[sequence]
     piece = SPEC * heads
     slots = keys_ref.shape[2]
@@ -152,7 +152,7 @@
 def finish_kernel(owners, copies, per_device, len_ref, q_ref, top_ref, total_ref, part_ref, *refs):
     key_refs, outs = refs[: copies - 1], refs[copies - 1 :]
     seq_index = lax.axis_index("seq")
-    length = len_ref[lax.axis_index("head") * owners + seq_index // copies]
+    length = len_ref[lax.axis_index("head") * owners + (seq_index // copies ^ (owners // 2))]
     q = q_ref[...]
     scores, values = [], []
     for e in range(1, copies):
@@ -232,11 +232,10 @@
         cost_estimate=LONG,
     )(in_hbm(jnp.swapaxes(cache, 1, 2)), in_hbm(queries), in_hbm(new_latent))
 
-    block = seq_size // head_size
-    turn = (0, 2, 3, 1) if head_size == 4 else range(head_size)
-
     def host(i, j):
-        return ((i // block) ^ turn[j]) * block + i % block
+        chip, core = i // copies, i % copies
+        half = head_size // 2
+        return (chip ^ j ^ (core * half)) * copies + (core ^ (j % half == 0))
 
     devices = [(i, j) for i in range(seq_size) for j in range(head_size)]
     packed = lax.ppermute(packed, both, [(flat(i, j), flat(host(i, j), j)) for i, j in devices])
@@ -254,7 +253,8 @@
 
     def owner(i, j, k):
         sequence = i * per_device + (j + k) % per_device
-        return flat((sequence % owners) * copies + j // per_device, sequence // owners)
+        group = (sequence % owners) ^ (owners // 2)
+        return flat(group * copies + j // per_device, sequence // owners)
 
     arrived = [
         lax.ppermute(
@@ -428,12 +428,12 @@
     rows, owners = queries.shape[0], cache.shape[0]
     per_device = rows // SPEC
     if (
-        rows % SPEC == 0
+        per_device == 2
+        and rows % SPEC == 0
+        and seq_size == 2 * owners
+        and head_size == owners
+        and owners >= 4
         and owners & (owners - 1) == 0
-        and seq_size % owners == 0
-        and head_size == per_device * (seq_size // owners)
-        and head_size & (head_size - 1) == 0
-        and seq_size % head_size == 0
         and cache.shape[2] % queries.shape[2] == 0
     ):
         return whole_sequences(

time: 36.4 us -> 30.8 us (0.85)
  the two profiles are of different devices: /device:TPU:6 before, /device:TPU:15 now
where the time goes in v5:
time: 30.8 us; the launch traced here: 30.6 us
  waiting for transfers between devices  13.7 us (44%)
  starting transfers between devices  10.3 us (33%)
  Pallas kernels  6.57 us (21%)
    ppermute x2, waiting for transfers between devices, whole_sequences(): lax.ppermute(latent[k], both, [(owner(i, j, k), flat(i, j)) for i, j in d...  6.38 us
    ppermute x3, waiting for transfers between devices, whole_sequences(): lax.ppermute(picked[k], 'seq', in_plane(lambda g, t: (g ^ k) * copies + t))  4.94 us
    ppermute x2, starting transfers between devices, whole_sequences(): lax.ppermute(latent[k], both, [(owner(i, j, k), flat(i, j)) for i, j in d...  3.66 us
    ppermute x2, starting transfers between devices, whole_sequences(): lax.ppermute(pieces[k], both, [(flat(host(i, j), j), owner(i, j, k)) for...  2.85 us
    ppermute x3, starting transfers between devices, whole_sequences(): lax.ppermute(picked[k], 'seq', in_plane(lambda g, t: (g ^ k) * copies + t))  2.65 us
    ppermute x1, waiting for transfers between devices, whole_sequences(): lax.ppermute(packed, both, [(flat(i, j), flat(host(i, j), j)) for i, j in...  2.04 us
    pallas_call x1, Pallas kernels, whole_sequences(): pl.pallas_call(functools.partial(pack_kernel, owners, copies), out_shape=...  1.37 us
    pallas_call x1, Pallas kernels, whole_sequences(): pl.pallas_call(functools.partial(finish_kernel, owners, copies, per_devic...  1.32 us
  transfers between devices with their start and end apart: 9, of which 5 were waited for; matrix products, arithmetic and copies ran while one was open for 0% of the time, Pallas kernels for 8%

profile of v5, /device:TPU:15, one launch (start us, length us, event | category | flops | bytes accessed | tf_op | source)
XLA Modules:
  0.0 30.6 jit_solution(2485918055541846373)
XLA Ops:
  0.0 1.4 %shard_map.64 = (bf16[576,128]{1,0:T(8,128)(2,1)S(1)}, bf16[576,128]{1,0:T(8,128)(2,1)S(1)}, bf16[576,128]{1,0:T(8,128)(2,1)S(1)}, bf16[576,128]{1,0:T(8,128)(2,1)S(1)}, bf16[160,192]{1,0:T(8,128)(2,1)S(1)}) custom-call(bf16[4,576,128]{2,1,0:T(8,128)(2,1)} %bitcast.1, bf16[8,16,192]{2,1,0:T(8,128)(2,1)} %q_hbm.1, bf16[8,576]{1,0:T(8,128)(2,1)} %new_hbm.1), custom_call_target="tpu_custom_call" | custom-call | flops 20000000000 | tf_op jit(solution)/shard_map/pallas_call | solution.py:220
  1.4 0.2 collective-permute-start
  1.6 1.2 %collective-permute-start.3 = (bf16[576,128]{1,0:T(8,128)(2,1)S(1)}, bf16[576,128]{1,0:T(8,128)(2,1)S(1)}, u32[]{:S(2)}, u32[]{:S(2)}) collective-permute-start(bf16[576,128]{1,0:T(8,128)(2,1)S(1)} %get-tuple-element.22), channel_id=1, source_target_pairs={{0,8},{4,12},{8,0},{12,4},{16,24},{20,28},{24,16},{28,20},{1,9},{5... | collective-permute-start | bytes 442376 | tf_op jit(solution)/shard_map/ppermute | solution.py:272
  2.8 1.2 %collective-permute-start.4 = (bf16[576,128]{1,0:T(8,128)(2,1)S(1)}, bf16[576,128]{1,0:T(8,128)(2,1)S(1)}, u32[]{:S(2)}, u32[]{:S(2)}) collective-permute-start(bf16[576,128]{1,0:T(8,128)(2,1)S(1)} %get-tuple-element.23), channel_id=1, source_target_pairs={{0,16},{4,20},{8,24},{12,28},{16,0},{20,4},{24,8},{28,12},{1,17},{... | collective-permute-start | bytes 442376 | tf_op jit(solution)/shard_map/ppermute | solution.py:272
  4.1 0.2 collective-permute-start.5
  4.3 2.0 %collective-permute-done.pack_ref = bf16[160,192]{1,0:T(8,128)(2,1)S(1)} collective-permute-done((bf16[160,192]{1,0:T(8,128)(2,1)S(1)}, bf16[160,192]{1,0:T(8,128)(2,1)S(1)}, u32[]{:S(2)}, u32[]{:S(2)}) %collective-permute-start) | collective-permute-done | bytes 61472 | tf_op jit(solution)/shard_map/ppermute | solution.py:241
  6.3 0.5 %shard_map.65 = (bf16[80,576]{1,0:T(8,128)(2,1)S(1)}, bf16[64,576]{1,0:T(8,128)(2,1)S(1)}) custom-call(bf16[160,192]{1,0:T(8,128)(2,1)S(1)} %collective-permute-done.pack_ref, bf16[16,128,512]{2,1,0:T(8,128)(2,1)S(1)} %copy-done.2), custom_call_target="tpu_custom_call" | custom-call | flops 20000000000 | tf_op jit(solution)/shard_map/pallas_call | solution.py:242
  6.8 0.1 collective-permute-start.1
  6.9 2.8 %collective-permute-start.2 = (bf16[64,576]{1,0:T(8,128)(2,1)S(1)}, bf16[64,576]{1,0:T(8,128)(2,1)S(1)}, u32[]{:S(2)}, u32[]{:S(2)}) collective-permute-start(bf16[64,576]{1,0:T(8,128)(2,1)S(1)} %get-tuple-element.20), channel_id=1, source_target_pairs={{4,24},{9,16},{22,28},{27,20},{16,8},{29,0},{2,12},{15,4},{12,25},... | collective-permute-start | bytes 221192 | tf_op jit(solution)/shard_map/ppermute | solution.py:260
  9.7 0.0 collective-permute-done.3.refs_1_
  9.7 0.0 collective-permute-done.4.refs_2_
  9.7 4.9 %collective-permute-done.5.refs_3_ = bf16[576,128]{1,0:T(8,128)(2,1)S(1)} collective-permute-done((bf16[576,128]{1,0:T(8,128)(2,1)S(1)}, bf16[576,128]{1,0:T(8,128)(2,1)S(1)}, u32[]{:S(2)}, u32[]{:S(2)}) %collective-permute-start.5) | collective-permute-done | bytes 147488 | tf_op jit(solution)/shard_map/ppermute | solution.py:272
  14.6 0.8 %shard_map.66.refs_2_ = bf16[4,576,128]{2,1,0:T(8,128)(2,1)S(1)} custom-call(bf16[576,128]{1,0:T(8,128)(2,1)S(1)} %get-tuple-element.21.refs_0_, bf16[576,128]{1,0:T(8,128)(2,1)S(1)} %collective-permute-done.3.refs_1_, bf16[576,128]{1,0:T(8,128)(2,1)S(1)} %collective-permute-done.4.refs_2_, bf16[576,128]{1,0:T(8,128)(2,1)S(1)} %collective-permute-done.5.refs_3_), custom_call_target="tpu_custom_call" | custom-call | tf_op jit(solution)/shard_map/pallas_call | solution.py:276
  15.4 0.9 %collective-permute-start.6 = (bf16[4,576,128]{2,1,0:T(8,128)(2,1)S(1)}, bf16[4,576,128]{2,1,0:T(8,128)(2,1)S(1)}, u32[]{:S(2)}, u32[]{:S(2)}) collective-permute-start(bf16[4,576,128]{2,1,0:T(8,128)(2,1)S(1)} %shard_map.66.refs_2_), channel_id=1, source_target_pairs={{0,4},{4,0},{8,12},{12,8},{16,20},{20,16},{24,28},{28,24},{1,5},{5... | collective-permute-start | bytes 1769480 | tf_op jit(solution)/shard_map/ppermute | solution.py:287
  16.3 0.0 collective-permute-done.2.refs_1_
  16.3 0.0 collective-permute-done.1.refs_0_
  16.3 0.0 copy-start
  16.4 1.3 %shard_map.67 = (bf16[128,576]{1,0:T(8,128)(2,1)S(1)}, f32[128,128]{1,0:T(8,128)S(1)}, f32[128,128]{1,0:T(8,128)S(1)}, f32[128,512]{1,0:T(8,128)S(1)}) custom-call(s32[16]{0:T(128)S(1)} %copy-done.1, bf16[80,576]{1,0:T(8,128)(2,1)S(1)} %collective-permute-done.1.refs_0_, bf16[64,576]{1,0:T(8,128)(2,1)S(1)} %collective-permute-done.2.refs_1_, ...), custom_call_target="tpu_custom_call" | custom-call | flops 20000000000 | tf_op jit(solution)/shard_map/pallas_call | solution.py:294
  17.7 0.3 collective-permute-done.6.refs_0_
  18.0 1.3 %shard_map.68 = (bf16[64,512]{1,0:T(8,128)(2,1)S(1)}, bf16[64,512]{1,0:T(8,128)(2,1)S(1)}) custom-call(s32[16]{0:T(128)S(1)} %copy-done.1, bf16[128,576]{1,0:T(8,128)(2,1)S(1)} %get-tuple-element.25.q_ref, f32[128,128]{1,0:T(8,128)S(1)} %get-tuple-element.26.top_ref, f32[128,128]{1,0:T(8,128)S(1)} %get-tuple-element.27.total_ref, ...), custom_call_target="tpu_custom_call" | custom-call | tf_op jit(solution)/shard_map/pallas_call | solution.py:307
  19.3 3.7 %collective-permute-start.7 = (bf16[64,512]{1,0:T(8,128)(2,1)S(1)}, bf16[64,512]{1,0:T(8,128)(2,1)S(1)}, u32[]{:S(2)}, u32[]{:S(2)}) collective-permute-start(bf16[64,512]{1,0:T(8,128)(2,1)S(1)} %get-tuple-element.29), channel_id=1, source_target_pairs={{16,0},{24,1},{20,2},{28,3},{0,4},{8,5},{4,6},{12,7},{17,8},{25,9}... | collective-permute-start | bytes 196616 | tf_op jit(solution)/shard_map/ppermute | solution.py:316
  22.9 2.6 %collective-permute-done.7.refs_0_ = bf16[64,512]{1,0:T(8,128)(2,1)S(1)} collective-permute-done((bf16[64,512]{1,0:T(8,128)(2,1)S(1)}, bf16[64,512]{1,0:T(8,128)(2,1)S(1)}, u32[]{:S(2)}, u32[]{:S(2)}) %collective-permute-start.7) | collective-permute-done | bytes 65568 | tf_op jit(solution)/shard_map/ppermute | solution.py:316
  25.5 3.8 %collective-permute-done.8.refs_1_ = bf16[64,512]{1,0:T(8,128)(2,1)S(1)} collective-permute-done((bf16[64,512]{1,0:T(8,128)(2,1)S(1)}, bf16[64,512]{1,0:T(8,128)(2,1)S(1)}, u32[]{:S(2)}, u32[]{:S(2)}) %collective-permute-start.8) | collective-permute-done | bytes 65568 | tf_op jit(solution)/shard_map/ppermute | solution.py:316
  29.3 1.3 %shard_map.69 = bf16[8,16,128]{2,1,0:T(8,128)(2,1)} custom-call(bf16[16,512,128]{2,1,0:T(8,128)(2,1)S(1)} %copy-done, bf16[64,512]{1,0:T(8,128)(2,1)S(1)} %collective-permute-done.7.refs_0_, bf16[64,512]{1,0:T(8,128)(2,1)S(1)} %collective-permute-done.8.refs_1_), custom_call_target="tpu_custom_call" | custom-call | tf_op jit(solution)/shard_map/pallas_call | solution.py:319
  (6 shorter events, 0.0 us)
Async XLA Ops:
  0.0 6.3 %copy-start.2 = (bf16[16,128,512]{2,1,0:T(8,128)(2,1)S(1)}, bf16[16,128,512]{2,1,0:T(8,128)(2,1)}, u32[]{:S(2)}) copy-start(bf16[16,128,512]{2,1,0:T(8,128)(2,1)} %w_ref.2) | copy-start | bytes 6291460
  1.4 4.9 %collective-permute-start = (bf16[160,192]{1,0:T(8,128)(2,1)S(1)}, bf16[160,192]{1,0:T(8,128)(2,1)S(1)}, u32[]{:S(2)}, u32[]{:S(2)}) collective-permute-start(bf16[160,192]{1,0:T(8,128)(2,1)S(1)} %get-tuple-element.18), channel_id=1, source_target_pairs={{0,4},{1,9},{2,22},{3,27},{4,16},{5,29},{6,2},{7,15},{8,12},{9,1},... | collective-permute-start | bytes 184328 | tf_op jit(solution)/shard_map/ppermute | solution.py:241
  1.6 8.0 %collective-permute-start.3 = (bf16[576,128]{1,0:T(8,128)(2,1)S(1)}, bf16[576,128]{1,0:T(8,128)(2,1)S(1)}, u32[]{:S(2)}, u32[]{:S(2)}) collective-permute-start(bf16[576,128]{1,0:T(8,128)(2,1)S(1)} %get-tuple-element.22), channel_id=1, source_target_pairs={{0,8},{4,12},{8,0},{12,4},{16,24},{20,28},{24,16},{28,20},{1,9},{5... | collective-permute-start | bytes 442376 | tf_op jit(solution)/shard_map/ppermute | solution.py:272
  2.8 6.8 %collective-permute-start.4 = (bf16[576,128]{1,0:T(8,128)(2,1)S(1)}, bf16[576,128]{1,0:T(8,128)(2,1)S(1)}, u32[]{:S(2)}, u32[]{:S(2)}) collective-permute-start(bf16[576,128]{1,0:T(8,128)(2,1)S(1)} %get-tuple-element.23), channel_id=1, source_target_pairs={{0,16},{4,20},{8,24},{12,28},{16,0},{20,4},{24,8},{28,12},{1,17},{... | collective-permute-start | bytes 442376 | tf_op jit(solution)/shard_map/ppermute | solution.py:272
  4.1 12.3 %copy-start.1 = (s32[16]{0:T(128)S(1)}, s32[16]{0:T(128)}, u32[]{:S(2)}) copy-start(s32[16]{0:T(128)} %len_ref.3) | copy-start | bytes 196
  4.1 10.5 %collective-permute-start.5 = (bf16[576,128]{1,0:T(8,128)(2,1)S(1)}, bf16[576,128]{1,0:T(8,128)(2,1)S(1)}, u32[]{:S(2)}, u32[]{:S(2)}) collective-permute-start(bf16[576,128]{1,0:T(8,128)(2,1)S(1)} %get-tuple-element.24), channel_id=1, source_target_pairs={{0,24},{4,28},{8,16},{12,20},{16,8},{20,12},{24,0},{28,4},{1,25},{... | collective-permute-start | bytes 442376 | tf_op jit(solution)/shard_map/ppermute | solution.py:272
  6.8 9.5 %collective-permute-start.1 = (bf16[80,576]{1,0:T(8,128)(2,1)S(1)}, bf16[80,576]{1,0:T(8,128)(2,1)S(1)}, u32[]{:S(2)}, u32[]{:S(2)}) collective-permute-start(bf16[80,576]{1,0:T(8,128)(2,1)S(1)} %get-tuple-element.19), channel_id=1, source_target_pairs={{4,16},{9,24},{22,20},{27,28},{16,0},{29,8},{2,4},{15,12},{12,17},... | collective-permute-start | bytes 276488 | tf_op jit(solution)/shard_map/ppermute | solution.py:260
  6.9 9.4 %collective-permute-start.2 = (bf16[64,576]{1,0:T(8,128)(2,1)S(1)}, bf16[64,576]{1,0:T(8,128)(2,1)S(1)}, u32[]{:S(2)}, u32[]{:S(2)}) collective-permute-start(bf16[64,576]{1,0:T(8,128)(2,1)S(1)} %get-tuple-element.20), channel_id=1, source_target_pairs={{4,24},{9,16},{22,28},{27,20},{16,8},{29,0},{2,12},{15,4},{12,25},... | collective-permute-start | bytes 221192 | tf_op jit(solution)/shard_map/ppermute | solution.py:260
  15.4 2.6 %collective-permute-start.6 = (bf16[4,576,128]{2,1,0:T(8,128)(2,1)S(1)}, bf16[4,576,128]{2,1,0:T(8,128)(2,1)S(1)}, u32[]{:S(2)}, u32[]{:S(2)}) collective-permute-start(bf16[4,576,128]{2,1,0:T(8,128)(2,1)S(1)} %shard_map.66.refs_2_), channel_id=1, source_target_pairs={{0,4},{4,0},{8,12},{12,8},{16,20},{20,16},{24,28},{28,24},{1,5},{5... | collective-permute-start | bytes 1769480 | tf_op jit(solution)/shard_map/ppermute | solution.py:287
  16.3 13.0 %copy-start = (bf16[16,512,128]{2,1,0:T(8,128)(2,1)S(1)}, bf16[16,512,128]{2,1,0:T(8,128)(2,1)}, u32[]{:S(2)}) copy-start(bf16[16,512,128]{2,1,0:T(8,128)(2,1)} %w_ref.3) | copy-start | bytes 6291460
  19.3 6.2 %collective-permute-start.7 = (bf16[64,512]{1,0:T(8,128)(2,1)S(1)}, bf16[64,512]{1,0:T(8,128)(2,1)S(1)}, u32[]{:S(2)}, u32[]{:S(2)}) collective-permute-start(bf16[64,512]{1,0:T(8,128)(2,1)S(1)} %get-tuple-element.29), channel_id=1, source_target_pairs={{16,0},{24,1},{20,2},{28,3},{0,4},{8,5},{4,6},{12,7},{17,8},{25,9}... | collective-permute-start | bytes 196616 | tf_op jit(solution)/shard_map/ppermute | solution.py:316
  22.9 6.4 %collective-permute-start.8 = (bf16[64,512]{1,0:T(8,128)(2,1)S(1)}, bf16[64,512]{1,0:T(8,128)(2,1)S(1)}, u32[]{:S(2)}, u32[]{:S(2)}) collective-permute-start(bf16[64,512]{1,0:T(8,128)(2,1)S(1)} %get-tuple-element.30), channel_id=1, source_target_pairs={{24,0},{16,1},{28,2},{20,3},{8,4},{0,5},{12,6},{4,7},{25,8},{17,9}... | collective-permute-start | bytes 196616 | tf_op jit(solution)/shard_map/ppermute | solution.py:316

commit v6 on v0

--- a/solution.py
+++ b/solution.py
@@ -1,15 +1,305 @@
+import functools
+
 import jax
 import jax.numpy as jnp
 from jax import lax
+from jax.experimental import pallas as pl
+from jax.experimental.pallas import tpu as pltpu
 from jax.sharding import PartitionSpec as P
 
 NOPE = 128
 ROPE = 64
 LATENT = 512
 SPEC = 4
-
+SCORE_SCALE = (NOPE + ROPE) ** (-0.5)
+VMEM_LIMIT = 16 * 1024 * 1024
+LONG = pl.CostEstimate(flops=2 * 10**10, bytes_accessed=0, transcendentals=0)
 
 masked_value = -1e30
+
+
+def pick_kernel(owners, copies, cache_hbm, new_hbm, *refs):
+    outs, (new_ref, sem) = refs[:owners], refs[owners:]
+    group = lax.axis_index("seq") // copies
+    width = cache_hbm.shape[1]
+    moves = [
+        pltpu.make_async_copy(
+            cache_hbm.at[group ^ k], outs[k].at[pl.ds(0, width)], sem.at[k]
+        )
+        for k in range(owners)
+    ]
+    fresh_move = pltpu.make_async_copy(new_hbm, new_ref, sem.at[owners])
+    fresh_move.start()
+    for move in moves:
+        move.start()
+    fresh_move.wait()
+    fresh = new_ref[...].astype(jnp.float32)
+    rows, slots = outs[0].shape
+    spare = -width % slots
+    if spare:
+        fresh = jnp.concatenate([fresh, jnp.zeros((fresh.shape[0], spare), jnp.float32)], axis=1)
+    parts = [fresh[:, n : n + slots] for n in range(0, width, slots)]
+    spare = rows - width - len(parts) * fresh.shape[0]
+    if spare:
+        parts.append(jnp.zeros((spare, slots), jnp.float32))
+    fresh = jnp.concatenate(parts, axis=0).astype(outs[0].dtype)
+    for out in outs:
+        out[width:, :] = fresh
+    for move in moves:
+        move.wait()
+
+
+def absorb_kernel(per_device, q_ref, w_ref, *outs):
+    rows, heads, width = q_ref.shape
+    piece = SPEC * heads
+    q = q_ref[...].reshape(rows * heads, width)
+    nope = q[:, :NOPE]
+    own_head = lax.broadcasted_iota(jnp.int32, nope.shape, 0) % heads
+    spread = jnp.concatenate(
+        [jnp.where(own_head == h, nope, jnp.zeros_like(nope)) for h in range(heads)], axis=1
+    )
+    absorbed = jnp.dot(
+        spread, w_ref[...].reshape(heads * NOPE, LATENT), preferred_element_type=jnp.float32
+    ).astype(jnp.bfloat16)
+    head_shard = lax.axis_index("head")
+    for k in range(per_device):
+        which = (head_shard + k) % per_device
+        for a in range(per_device):
+
+            @pl.when(which == a)
+            def _():
+                outs[k][:, :LATENT] = absorbed[a * piece : (a + 1) * piece]
+                outs[k][:, LATENT:] = q[a * piece : (a + 1) * piece, NOPE:]
+
+
+def block_scores(q, refs, starts, length):
+    width = q.shape[1]
+    keys = jnp.concatenate([ref[:width, :] for ref in refs], axis=1)
+    lane = lax.broadcasted_iota(jnp.int32, (1, refs[0].shape[1]), 1)
+    position = jnp.concatenate([lane + start for start in starts], axis=1)
+    s = jnp.dot(q, keys, preferred_element_type=jnp.float32) * SCORE_SCALE
+    return jnp.where(position < length, s, masked_value)
+
+
+def weigh(s, refs, top):
+    w = jnp.exp(s - top)
+    values = jnp.concatenate([ref[:LATENT, :] for ref in refs], axis=1)
+    out = lax.dot_general(
+        w.astype(jnp.bfloat16),
+        values,
+        (((1,), (1,)), ((), ())),
+        preferred_element_type=jnp.float32,
+    )
+    return jnp.sum(w, axis=1, keepdims=True), out
+
+
+def begin_kernel(owners, copies, per_device, len_ref, *refs):
+    q_refs, key_refs = refs[:per_device], refs[per_device : per_device + owners]
+    q_out, top_ref, total_ref, out_ref = refs[per_device + owners :]
+    seq_index = lax.axis_index("seq")
+    group, core = seq_index // copies, seq_index % copies
+    length = len_ref[lax.axis_index("head") * owners + group]
+    slots = key_refs[0].shape[1]
+    q = jnp.concatenate([ref[...] for ref in q_refs], axis=0)
+    starts = [((group ^ k) * copies + core) * slots for k in range(owners)]
+    s = block_scores(q, key_refs, starts, length)
+    top = jnp.max(s, axis=1, keepdims=True)
+    total, out = weigh(s, key_refs, top)
+    q_out[...] = q
+    top_ref[...] = jnp.broadcast_to(top, top_ref.shape)
+    total_ref[...] = jnp.broadcast_to(total, total_ref.shape)
+    out_ref[...] = out
+
+
+def finish_kernel(
+    owners, copies, per_device, heads, len_ref, q_ref, top_ref, total_ref, part_ref, *refs
+):
+    own_refs, far_refs = refs[:owners], refs[owners : owners * copies]
+    outs, fresh_ref = refs[owners * copies : -1], refs[-1]
+    seq_index = lax.axis_index("seq")
+    group, core = seq_index // copies, seq_index % copies
+    sequence = lax.axis_index("head") * owners + group
+    length = len_ref[sequence]
+    q = q_ref[...]
+    slots, width = own_refs[0].shape[1], q.shape[1]
+
+    home = sequence // per_device
+    for e in range(copies):
+        for k in range(owners):
+            source = (group ^ k) * copies + (core + copies - e) % copies
+
+            @pl.when(source == home)
+            def _():
+                fresh_ref[...] = (own_refs + far_refs)[e * owners + k][width:, :]
+
+    parts = -(-width // slots)
+    rows = per_device * SPEC
+    fresh = fresh_ref[...].astype(jnp.float32)
+    fresh = jnp.concatenate([fresh[n * rows : (n + 1) * rows] for n in range(parts)], axis=1)
+    fresh = fresh[:, :width]
+    spare = -rows % 16
+    if spare:
+        fresh = jnp.concatenate([fresh, jnp.zeros((spare, width), jnp.float32)], axis=0)
+    fresh = fresh.astype(jnp.bfloat16)
+    f = lax.dot_general(
+        q, fresh, (((1,), (1,)), ((), ())), preferred_element_type=jnp.float32
+    )
+    row = lax.broadcasted_iota(jnp.int32, f.shape, 0) % (SPEC * heads)
+    key = lax.broadcasted_iota(jnp.int32, f.shape, 1)
+    causal = (key // SPEC == sequence % per_device) & (key % SPEC <= row // heads)
+    f = jnp.where(causal, f * SCORE_SCALE, masked_value)
+
+    starts = [
+        ((group ^ k) * copies + (core + copies - e) % copies) * slots
+        for e in range(1, copies)
+        for k in range(owners)
+    ]
+    s = block_scores(q, far_refs, starts, length)
+    first = top_ref[:, :1]
+    top = jnp.maximum(
+        jnp.maximum(first, jnp.max(s, axis=1, keepdims=True)), jnp.max(f, axis=1, keepdims=True)
+    )
+    total, out = weigh(s, far_refs, top)
+    w = jnp.exp(f - top)
+    scale = jnp.exp(first - top)
+    total += jnp.sum(w, axis=1, keepdims=True) + total_ref[:, :1] * scale
+    out += part_ref[...] * scale
+    out += jnp.dot(
+        w.astype(jnp.bfloat16), fresh[:, :LATENT], preferred_element_type=jnp.float32
+    )
+    out = (out / total).astype(jnp.bfloat16)
+    piece = SPEC * heads
+    for k in range(per_device):
+        outs[k][...] = out[k * piece : (k + 1) * piece]
+
+
+def project_kernel(per_device, w_ref, *refs):
+    lat_refs, out_ref = refs[:-1], refs[-1]
+    rows, heads, width = out_ref.shape
+    head_shard = lax.axis_index("head")
+    parts = []
+    for a in range(per_device):
+        part = lat_refs[0][...]
+        for k in range(1, per_device):
+            part = jnp.where((head_shard + k) % per_device == a, lat_refs[k][...], part)
+        parts.append(part)
+    latent = jnp.concatenate(parts, axis=0)
+    out = jnp.zeros((rows * heads, width), jnp.float32)
+    own_head = lax.broadcasted_iota(jnp.int32, out.shape, 0) % heads
+    step = 2 if heads % 2 == 0 else 1
+    for h in range(0, heads, step):
+        group = jnp.concatenate([w_ref[h + n] for n in range(step)], axis=1)
+        product = jnp.dot(latent, group, preferred_element_type=jnp.float32)
+        for n in range(step):
+            out = jnp.where(own_head == h + n, product[:, n * width : (n + 1) * width], out)
+    out_ref[...] = out.astype(out_ref.dtype).reshape(out_ref.shape)
+
+
+def whole_sequences(seq_size, head_size, queries, new_latent, cache, lengths, w_uk, w_uv):
+    rows, heads, _ = queries.shape
+    owners, slots, width = cache.shape
+    copies = seq_size // owners
+    per_device = rows // SPEC
+    piece = SPEC * heads
+    all_rows = per_device * piece
+    fresh_rows = -(-rows * -(-width // slots) // 16) * 16
+    params = pltpu.CompilerParams(vmem_limit_bytes=VMEM_LIMIT)
+    vmem = pl.BlockSpec(memory_space=pltpu.VMEM)
+    smem = pl.BlockSpec(memory_space=pltpu.SMEM)
+    anywhere = pl.BlockSpec(memory_space=pl.ANY)
+    both = ("seq", "head")
+    devices = [(i, j) for i in range(seq_size) for j in range(head_size)]
+
+    def flat(seq_index, head_index):
+        return seq_index * head_size + head_index
+
+    def in_hbm(x):
+        return pltpu.with_memory_space_constraint(x, pltpu.HBM)
+
+    def host(i, j):
+        other = (i // copies) ^ (2 - ((j ^ (j >> 1)) & 1))
+        return ((i % copies) * 2 + other // 2) * copies + other % 2
+
+    def owner(i, j, k):
+        sequence = i * per_device + (j + k) % per_device
+        core = (j // per_device) ^ 1
+        return flat((sequence % owners) * copies + core, sequence // owners)
+
+    moved = lax.ppermute(queries, both, [(flat(i, j), flat(host(i, j), j)) for i, j in devices])
+
+    def in_plane(move):
+        return [(g * copies + t, move(g, t)) for g in range(owners) for t in range(copies)]
+
+    picked = pl.pallas_call(
+        functools.partial(pick_kernel, owners, copies),
+        out_shape=[jax.ShapeDtypeStruct((width + fresh_rows, slots), cache.dtype)] * owners,
+        in_specs=[anywhere] * 2,
+        out_specs=[vmem] * owners,
+        scratch_shapes=[
+            pltpu.VMEM(new_latent.shape, new_latent.dtype),
+            pltpu.SemaphoreType.DMA((owners + 1,)),
+        ],
+        compiler_params=params,
+        cost_estimate=LONG,
+    )(in_hbm(jnp.swapaxes(cache, 1, 2)), in_hbm(new_latent))
+    own_keys = [picked[0]] + [
+        lax.ppermute(picked[k], "seq", in_plane(lambda g, t: (g ^ k) * copies + t))
+        for k in range(1, owners)
+    ]
+    far_keys = [
+        lax.ppermute(keys, "seq", in_plane(lambda g, t: g * copies + (t + e) % copies))
+        for e in range(1, copies)
+        for keys in own_keys
+    ]
+
+    pieces = pl.pallas_call(
+        functools.partial(absorb_kernel, per_device),
+        out_shape=[jax.ShapeDtypeStruct((piece, width), cache.dtype)] * per_device,
+        in_specs=[vmem] * 2,
+        out_specs=[vmem] * per_device,
+        compiler_params=params,
+        cost_estimate=LONG,
+    )(moved, w_uk)
+    arrived = [
+        lax.ppermute(
+            pieces[k], both, [(flat(host(i, j), j), owner(i, j, k)) for i, j in devices]
+        )
+        for k in range(per_device)
+    ]
+
+    state = pl.pallas_call(
+        functools.partial(begin_kernel, owners, copies, per_device),
+        out_shape=[
+            jax.ShapeDtypeStruct((all_rows, width), jnp.bfloat16),
+            jax.ShapeDtypeStruct((all_rows, 128), jnp.float32),
+            jax.ShapeDtypeStruct((all_rows, 128), jnp.float32),
+            jax.ShapeDtypeStruct((all_rows, LATENT), jnp.float32),
+        ],
+        in_specs=[smem] + [vmem] * (per_device + owners),
+        out_specs=[vmem] * 4,
+        compiler_params=params,
+        cost_estimate=LONG,
+    )(lengths, *arrived, *own_keys)
+    latent = pl.pallas_call(
+        functools.partial(finish_kernel, owners, copies, per_device, heads),
+        out_shape=[jax.ShapeDtypeStruct((piece, LATENT), jnp.bfloat16)] * per_device,
+        in_specs=[smem] + [vmem] * (len(state) + owners * copies),
+        out_specs=[vmem] * per_device,
+        scratch_shapes=[pltpu.VMEM((fresh_rows, slots), jnp.bfloat16)],
+        compiler_params=params,
+    )(lengths, *state, *own_keys, *far_keys)
+
+    back = [
+        lax.ppermute(latent[k], both, [(owner(i, j, k), flat(i, j)) for i, j in devices])
+        for k in range(per_device)
+    ]
+    return pl.pallas_call(
+        functools.partial(project_kernel, per_device),
+        out_shape=jax.ShapeDtypeStruct((rows, heads, w_uv.shape[2]), jnp.bfloat16),
+        in_specs=[vmem] * (1 + per_device),
+        out_specs=vmem,
+        compiler_params=params,
+    )(w_uv, *back)
 
 
 def local_partial(
@@ -68,7 +358,7 @@
     return jnp.einsum("rhc,hcv->rhv", latent_rows, value_weight, precision=lax.Precision.HIGHEST)
 
 
-def shards(queries, new_latent, cache, lengths, w_uk, w_uv):
+def split_positions(queries, new_latent, cache, lengths, w_uk, w_uv):
     own_rows, head_count, _ = queries.shape
     score_scale = (NOPE + ROPE) ** (-0.5)
     gathered, new_all = (
@@ -87,7 +377,7 @@
     seq_index = lax.axis_index("seq")
     offset = seq_index * cache.shape[1]
     own_first = seq_index == 0
-    partial_value = local_partial(
+    row_top, running_totals, weighted = local_partial(
         q_seq,
         lax.all_gather(cache, "head", axis=0, tiled=True),
         new_seq,
@@ -97,7 +387,6 @@
         score_scale,
         head_count,
     )
-    row_top, running_totals, weighted = tuple((value for value in partial_value))
     value_weight = w_uv.astype(jnp.float32)
     global_top = lax.pmax(row_top, "seq")
     factor = jnp.exp(row_top - global_top)
@@ -112,9 +401,24 @@
     return result.astype(jnp.bfloat16)
 
 
+def shards(seq_size, head_size, queries, new_latent, cache, lengths, w_uk, w_uv):
+    rows, owners = queries.shape[0], cache.shape[0]
+    per_device = rows // SPEC
+    if (
+        per_device == 2
+        and rows % SPEC == 0
+        and seq_size == 2 * owners
+        and head_size == owners == 4
+    ):
+        return whole_sequences(
+            seq_size, head_size, queries, new_latent, cache, lengths, w_uk, w_uv
+        )
+    return split_positions(queries, new_latent, cache, lengths, w_uk, w_uv)
+
+
 def solution(mesh):
     return jax.shard_map(
-        shards,
+        functools.partial(shards, mesh.shape["seq"], mesh.shape["head"]),
         mesh=mesh,
         in_specs=(
             P("seq", "head", None),

time: 135 us -> 28.4 us (0.21)
  the two profiles are of different devices: /device:TPU:0 before, /device:TPU:6 now
where the time goes in v6:
time: 28.4 us; the launch traced here: 28.3 us
  waiting for transfers between devices  12.4 us (44%)
  starting transfers between devices  10.4 us (37%)
  Pallas kernels  5.35 us (19%)
    ppermute x2, waiting for transfers between devices, whole_sequences(): lax.ppermute(pieces[k], both, [(flat(host(i, j), j), owner(i, j, k)) for...  6.01 us
    ppermute x2, waiting for transfers between devices, whole_sequences(): lax.ppermute(latent[k], both, [(owner(i, j, k), flat(i, j)) for i, j in d...  5.8 us
    ppermute x2, starting transfers between devices, whole_sequences(): lax.ppermute(latent[k], both, [(owner(i, j, k), flat(i, j)) for i, j in d...  4.9 us
    ppermute x3, starting transfers between devices, whole_sequences(): lax.ppermute(picked[k], 'seq', in_plane(lambda g, t: (g ^ k) * copies + t))  3.55 us
    pallas_call x1, Pallas kernels, whole_sequences(): pl.pallas_call(functools.partial(finish_kernel, owners, copies, per_devic...  1.36 us
    pallas_call x1, Pallas kernels, whole_sequences(): pl.pallas_call(functools.partial(pick_kernel, owners, copies), out_shape=...  1.33 us
    pallas_call x1, Pallas kernels, whole_sequences(): pl.pallas_call(functools.partial(begin_kernel, owners, copies, per_device...  1.12 us
    ppermute x2, starting transfers between devices, whole_sequences(): lax.ppermute(pieces[k], both, [(flat(host(i, j), j), owner(i, j, k)) for...  1.08 us
  transfers between devices with their start and end apart: 12, of which 5 were waited for; matrix products, arithmetic and copies ran while one was open for 0% of the time, Pallas kernels for 10%

profile of v6, /device:TPU:6, one launch (start us, length us, event | category | flops | bytes accessed | tf_op | source)
XLA Modules:
  0.0 28.3 jit_solution(13478133387202066425)
XLA Ops:
  0.0 0.0 collective-permute-start
  0.0 1.3 %shard_map.65 = (bf16[624,128]{1,0:T(8,128)(2,1)S(1)}, bf16[624,128]{1,0:T(8,128)(2,1)S(1)}, bf16[624,128]{1,0:T(8,128)(2,1)S(1)}, bf16[624,128]{1,0:T(8,128)(2,1)S(1)}) custom-call(bf16[4,576,128]{2,1,0:T(8,128)(2,1)} %bitcast.1, bf16[8,576]{1,0:T(8,128)(2,1)} %new_hbm.1), custom_call_target="tpu_custom_call" | custom-call | flops 20000000000 | tf_op jit(solution)/shard_map/pallas_call | solution.py:233
  1.3 0.6 %collective-permute-start.3 = (bf16[624,128]{1,0:T(8,128)(2,1)S(1)}, bf16[624,128]{1,0:T(8,128)(2,1)S(1)}, u32[]{:S(2)}, u32[]{:S(2)}) collective-permute-start(bf16[624,128]{1,0:T(8,128)(2,1)S(1)} %get-tuple-element.20), channel_id=1, source_target_pairs={{0,8},{4,12},{8,0},{12,4},{16,24},{20,28},{24,16},{28,20},{1,9},{5... | collective-permute-start | bytes 479240 | tf_op jit(solution)/shard_map/ppermute | solution.py:246
  1.9 2.0 %collective-permute-start.4 = (bf16[624,128]{1,0:T(8,128)(2,1)S(1)}, bf16[624,128]{1,0:T(8,128)(2,1)S(1)}, u32[]{:S(2)}, u32[]{:S(2)}) collective-permute-start(bf16[624,128]{1,0:T(8,128)(2,1)S(1)} %get-tuple-element.21), channel_id=1, source_target_pairs={{0,16},{4,20},{8,24},{12,28},{16,0},{20,4},{24,8},{28,12},{1,17},{... | collective-permute-start | bytes 479240 | tf_op jit(solution)/shard_map/ppermute | solution.py:246
  3.9 1.0 %collective-permute-start.5 = (bf16[624,128]{1,0:T(8,128)(2,1)S(1)}, bf16[624,128]{1,0:T(8,128)(2,1)S(1)}, u32[]{:S(2)}, u32[]{:S(2)}) collective-permute-start(bf16[624,128]{1,0:T(8,128)(2,1)S(1)} %get-tuple-element.22), channel_id=1, source_target_pairs={{0,24},{4,28},{8,16},{12,20},{16,8},{20,12},{24,0},{28,4},{1,25},{... | collective-permute-start | bytes 479240 | tf_op jit(solution)/shard_map/ppermute | solution.py:246
  4.9 0.5 %collective-permute-done.q_ref = bf16[8,16,192]{2,1,0:T(8,128)(2,1)S(1)} collective-permute-done((bf16[8,16,192]{2,1,0:T(8,128)(2,1)}, bf16[8,16,192]{2,1,0:T(8,128)(2,1)S(1)}, u32[]{:S(2)}, u32[]{:S(2)}) %collective-permute-start) | collective-permute-done | bytes 49184 | tf_op jit(solution)/shard_map/ppermute | solution.py:228
  5.4 0.5 %shard_map.64 = (bf16[64,576]{1,0:T(8,128)(2,1)S(1)}, bf16[64,576]{1,0:T(8,128)(2,1)S(1)}) custom-call(bf16[8,16,192]{2,1,0:T(8,128)(2,1)S(1)} %collective-permute-done.q_ref, bf16[16,128,512]{2,1,0:T(8,128)(2,1)S(1)} %copy-done.2), custom_call_target="tpu_custom_call" | custom-call | flops 20000000000 | tf_op jit(solution)/shard_map/pallas_call | solution.py:255
  5.8 0.2 collective-permute-start.1
  6.1 0.8 %collective-permute-start.2 = (bf16[64,576]{1,0:T(8,128)(2,1)S(1)}, bf16[64,576]{1,0:T(8,128)(2,1)S(1)}, u32[]{:S(2)}, u32[]{:S(2)}) collective-permute-start(bf16[64,576]{1,0:T(8,128)(2,1)S(1)} %get-tuple-element.18), channel_id=1, source_target_pairs={{8,12},{5,4},{6,8},{11,0},{24,28},{21,20},{22,24},{27,16},{12,13},... | collective-permute-start | bytes 221192 | tf_op jit(solution)/shard_map/ppermute | solution.py:264
  6.9 6.0 %collective-permute-done.1.refs_0_ = bf16[64,576]{1,0:T(8,128)(2,1)S(1)} collective-permute-done((bf16[64,576]{1,0:T(8,128)(2,1)S(1)}, bf16[64,576]{1,0:T(8,128)(2,1)S(1)}, u32[]{:S(2)}, u32[]{:S(2)}) %collective-permute-start.1) | collective-permute-done | bytes 73760 | tf_op jit(solution)/shard_map/ppermute | solution.py:264
  12.9 0.5 %collective-permute-start.7 = (bf16[624,128]{1,0:T(8,128)(2,1)S(1)}, bf16[624,128]{1,0:T(8,128)(2,1)S(1)}, u32[]{:S(2)}, u32[]{:S(2)}) collective-permute-start(bf16[624,128]{1,0:T(8,128)(2,1)S(1)} %collective-permute-done.3.refs_3_.refs_1_), channel_id=1, source_target_pairs={{0,4},{4,0},{8,12},{12,8},{16,20},{20,16},{24,28},{28,24},{1,5},{5... | collective-permute-start | bytes 479240 | tf_op jit(solution)/shard_map/ppermute | solution.py:250
  13.5 0.1 collective-permute-start.8
  13.5 0.1 collective-permute-done.5.refs_5_.refs_3_
  13.6 0.3 %collective-permute-start.9 = (bf16[624,128]{1,0:T(8,128)(2,1)S(1)}, bf16[624,128]{1,0:T(8,128)(2,1)S(1)}, u32[]{:S(2)}, u32[]{:S(2)}) collective-permute-start(bf16[624,128]{1,0:T(8,128)(2,1)S(1)} %collective-permute-done.5.refs_5_.refs_3_), channel_id=1, source_target_pairs={{0,4},{4,0},{8,12},{12,8},{16,20},{20,16},{24,28},{28,24},{1,5},{5... | collective-permute-start | bytes 479240 | tf_op jit(solution)/shard_map/ppermute | solution.py:250
  14.0 1.1 %shard_map.66 = (bf16[128,576]{1,0:T(8,128)(2,1)S(1)}, f32[128,128]{1,0:T(8,128)S(1)}, f32[128,128]{1,0:T(8,128)S(1)}, f32[128,512]{1,0:T(8,128)S(1)}) custom-call(s32[16]{0:T(128)S(1)} %copy-done.1, bf16[64,576]{1,0:T(8,128)(2,1)S(1)} %collective-permute-done.1.refs_0_, bf16[64,576]{1,0:T(8,128)(2,1)S(1)} %collective-permute-done.2.refs_1_, ...), custom_call_target="tpu_custom_call" | custom-call | flops 20000000000 | tf_op jit(solution)/shard_map/pallas_call | solution.py:270
  15.1 0.0 collective-permute-done.6.refs_4_
  15.1 0.0 collective-permute-done.7.refs_5_
  15.1 0.0 collective-permute-done.9.refs_7_
  15.1 1.4 %shard_map.67 = (bf16[64,512]{1,0:T(8,128)(2,1)S(1)}, bf16[64,512]{1,0:T(8,128)(2,1)S(1)}) custom-call(s32[16]{0:T(128)S(1)} %copy-done.1, bf16[128,576]{1,0:T(8,128)(2,1)S(1)} %get-tuple-element.23.q_ref, f32[128,128]{1,0:T(8,128)S(1)} %get-tuple-element.24.top_ref, f32[128,128]{1,0:T(8,128)S(1)} %get-tuple-element.25.total_ref, ...), custom_call_target="tpu_custom_call" | custom-call | tf_op jit(solution)/shard_map/pallas_call | solution.py:283
  16.5 4.3 %collective-permute-start.10 = (bf16[64,512]{1,0:T(8,128)(2,1)S(1)}, bf16[64,512]{1,0:T(8,128)(2,1)S(1)}, u32[]{:S(2)}, u32[]{:S(2)}) collective-permute-start(bf16[64,512]{1,0:T(8,128)(2,1)S(1)} %get-tuple-element.27), channel_id=1, source_target_pairs={{4,0},{12,1},{0,2},{8,3},{20,4},{28,5},{16,6},{24,7},{5,8},{13,9},... | collective-permute-start | bytes 196616 | tf_op jit(solution)/shard_map/ppermute | solution.py:293
  20.8 0.6 %collective-permute-start.11 = (bf16[64,512]{1,0:T(8,128)(2,1)S(1)}, bf16[64,512]{1,0:T(8,128)(2,1)S(1)}, u32[]{:S(2)}, u32[]{:S(2)}) collective-permute-start(bf16[64,512]{1,0:T(8,128)(2,1)S(1)} %get-tuple-element.28), channel_id=1, source_target_pairs={{12,0},{4,1},{8,2},{0,3},{28,4},{20,5},{24,6},{16,7},{13,8},{5,9},... | collective-permute-start | bytes 196616 | tf_op jit(solution)/shard_map/ppermute | solution.py:293
  21.4 2.5 %collective-permute-done.10.refs_0_ = bf16[64,512]{1,0:T(8,128)(2,1)S(1)} collective-permute-done((bf16[64,512]{1,0:T(8,128)(2,1)S(1)}, bf16[64,512]{1,0:T(8,128)(2,1)S(1)}, u32[]{:S(2)}, u32[]{:S(2)}) %collective-permute-start.10) | collective-permute-done | bytes 65568 | tf_op jit(solution)/shard_map/ppermute | solution.py:293
  24.0 3.3 %collective-permute-done.11.refs_1_ = bf16[64,512]{1,0:T(8,128)(2,1)S(1)} collective-permute-done((bf16[64,512]{1,0:T(8,128)(2,1)S(1)}, bf16[64,512]{1,0:T(8,128)(2,1)S(1)}, u32[]{:S(2)}, u32[]{:S(2)}) %collective-permute-start.11) | collective-permute-done | bytes 65568 | tf_op jit(solution)/shard_map/ppermute | solution.py:293
  27.2 1.1 %shard_map.68 = bf16[8,16,128]{2,1,0:T(8,128)(2,1)} custom-call(bf16[16,512,128]{2,1,0:T(8,128)(2,1)S(1)} %copy-done, bf16[64,512]{1,0:T(8,128)(2,1)S(1)} %collective-permute-done.10.refs_0_, bf16[64,512]{1,0:T(8,128)(2,1)S(1)} %collective-permute-done.11.refs_1_), custom_call_target="tpu_custom_call" | custom-call | tf_op jit(solution)/shard_map/pallas_call | solution.py:296
  (11 shorter events, 0.0 us)
Async XLA Ops:
  0.0 5.4 %collective-permute-start = (bf16[8,16,192]{2,1,0:T(8,128)(2,1)}, bf16[8,16,192]{2,1,0:T(8,128)(2,1)S(1)}, u32[]{:S(2)}, u32[]{:S(2)}) collective-permute-start(bf16[8,16,192]{2,1,0:T(8,128)(2,1)} %param.6), channel_id=1, source_target_pairs={{0,8},{1,5},{2,6},{3,11},{4,24},{5,21},{6,22},{7,27},{8,12},{9,1},... | collective-permute-start | bytes 147464 | tf_op jit(solution)/shard_map/ppermute | solution.py:228
  0.0 5.4 %copy-start.2 = (bf16[16,128,512]{2,1,0:T(8,128)(2,1)S(1)}, bf16[16,128,512]{2,1,0:T(8,128)(2,1)}, u32[]{:S(2)}) copy-start(bf16[16,128,512]{2,1,0:T(8,128)(2,1)} %w_ref.2) | copy-start | bytes 6291460
  1.3 11.6 %collective-permute-start.3 = (bf16[624,128]{1,0:T(8,128)(2,1)S(1)}, bf16[624,128]{1,0:T(8,128)(2,1)S(1)}, u32[]{:S(2)}, u32[]{:S(2)}) collective-permute-start(bf16[624,128]{1,0:T(8,128)(2,1)S(1)} %get-tuple-element.20), channel_id=1, source_target_pairs={{0,8},{4,12},{8,0},{12,4},{16,24},{20,28},{24,16},{28,20},{1,9},{5... | collective-permute-start | bytes 479240 | tf_op jit(solution)/shard_map/ppermute | solution.py:246
  1.9 11.5 %collective-permute-start.4 = (bf16[624,128]{1,0:T(8,128)(2,1)S(1)}, bf16[624,128]{1,0:T(8,128)(2,1)S(1)}, u32[]{:S(2)}, u32[]{:S(2)}) collective-permute-start(bf16[624,128]{1,0:T(8,128)(2,1)S(1)} %get-tuple-element.21), channel_id=1, source_target_pairs={{0,16},{4,20},{8,24},{12,28},{16,0},{20,4},{24,8},{28,12},{1,17},{... | collective-permute-start | bytes 479240 | tf_op jit(solution)/shard_map/ppermute | solution.py:246
  3.9 10.0 %copy-start.1 = (s32[16]{0:T(128)S(1)}, s32[16]{0:T(128)}, u32[]{:S(2)}) copy-start(s32[16]{0:T(128)} %len_ref.3) | copy-start | bytes 196
  3.9 9.7 %collective-permute-start.5 = (bf16[624,128]{1,0:T(8,128)(2,1)S(1)}, bf16[624,128]{1,0:T(8,128)(2,1)S(1)}, u32[]{:S(2)}, u32[]{:S(2)}) collective-permute-start(bf16[624,128]{1,0:T(8,128)(2,1)S(1)} %get-tuple-element.22), channel_id=1, source_target_pairs={{0,24},{4,28},{8,16},{12,20},{16,8},{20,12},{24,0},{28,4},{1,25},{... | collective-permute-start | bytes 479240 | tf_op jit(solution)/shard_map/ppermute | solution.py:246
  5.8 7.1 %collective-permute-start.1 = (bf16[64,576]{1,0:T(8,128)(2,1)S(1)}, bf16[64,576]{1,0:T(8,128)(2,1)S(1)}, u32[]{:S(2)}, u32[]{:S(2)}) collective-permute-start(bf16[64,576]{1,0:T(8,128)(2,1)S(1)} %get-tuple-element.17), channel_id=1, source_target_pairs={{8,4},{5,12},{6,0},{11,8},{24,20},{21,28},{22,16},{27,24},{12,5},{... | collective-permute-start | bytes 221192 | tf_op jit(solution)/shard_map/ppermute | solution.py:264
  6.1 7.9 %collective-permute-start.2 = (bf16[64,576]{1,0:T(8,128)(2,1)S(1)}, bf16[64,576]{1,0:T(8,128)(2,1)S(1)}, u32[]{:S(2)}, u32[]{:S(2)}) collective-permute-start(bf16[64,576]{1,0:T(8,128)(2,1)S(1)} %get-tuple-element.18), channel_id=1, source_target_pairs={{8,12},{5,4},{6,8},{11,0},{24,28},{21,20},{22,24},{27,16},{12,13},... | collective-permute-start | bytes 221192 | tf_op jit(solution)/shard_map/ppermute | solution.py:264
  12.9 2.2 %collective-permute-start.6 = (bf16[624,128]{1,0:T(8,128)(2,1)S(1)}, bf16[624,128]{1,0:T(8,128)(2,1)S(1)}, u32[]{:S(2)}, u32[]{:S(2)}) collective-permute-start(bf16[624,128]{1,0:T(8,128)(2,1)S(1)} %get-tuple-element.19.refs_2_.refs_0_), channel_id=1, source_target_pairs={{0,4},{4,0},{8,12},{12,8},{16,20},{20,16},{24,28},{28,24},{1,5},{5... | collective-permute-start | bytes 479240 | tf_op jit(solution)/shard_map/ppermute | solution.py:250
  12.9 2.2 %collective-permute-start.7 = (bf16[624,128]{1,0:T(8,128)(2,1)S(1)}, bf16[624,128]{1,0:T(8,128)(2,1)S(1)}, u32[]{:S(2)}, u32[]{:S(2)}) collective-permute-start(bf16[624,128]{1,0:T(8,128)(2,1)S(1)} %collective-permute-done.3.refs_3_.refs_1_), channel_id=1, source_target_pairs={{0,4},{4,0},{8,12},{12,8},{16,20},{20,16},{24,28},{28,24},{1,5},{5... | collective-permute-start | bytes 479240 | tf_op jit(solution)/shard_map/ppermute | solution.py:250
  13.5 1.7 %collective-permute-start.8 = (bf16[624,128]{1,0:T(8,128)(2,1)S(1)}, bf16[624,128]{1,0:T(8,128)(2,1)S(1)}, u32[]{:S(2)}, u32[]{:S(2)}) collective-permute-start(bf16[624,128]{1,0:T(8,128)(2,1)S(1)} %collective-permute-done.4.refs_4_.refs_2_), channel_id=1, source_target_pairs={{0,4},{4,0},{8,12},{12,8},{16,20},{20,16},{24,28},{28,24},{1,5},{5... | collective-permute-start | bytes 479240 | tf_op jit(solution)/shard_map/ppermute | solution.py:250
  13.6 1.5 %collective-permute-start.9 = (bf16[624,128]{1,0:T(8,128)(2,1)S(1)}, bf16[624,128]{1,0:T(8,128)(2,1)S(1)}, u32[]{:S(2)}, u32[]{:S(2)}) collective-permute-start(bf16[624,128]{1,0:T(8,128)(2,1)S(1)} %collective-permute-done.5.refs_5_.refs_3_), channel_id=1, source_target_pairs={{0,4},{4,0},{8,12},{12,8},{16,20},{20,16},{24,28},{28,24},{1,5},{5... | collective-permute-start | bytes 479240 | tf_op jit(solution)/shard_map/ppermute | solution.py:250
  14.0 13.2 %copy-start = (bf16[16,512,128]{2,1,0:T(8,128)(2,1)S(1)}, bf16[16,512,128]{2,1,0:T(8,128)(2,1)}, u32[]{:S(2)}) copy-start(bf16[16,512,128]{2,1,0:T(8,128)(2,1)} %w_ref.3) | copy-start | bytes 6291460
  16.5 7.4 %collective-permute-start.10 = (bf16[64,512]{1,0:T(8,128)(2,1)S(1)}, bf16[64,512]{1,0:T(8,128)(2,1)S(1)}, u32[]{:S(2)}, u32[]{:S(2)}) collective-permute-start(bf16[64,512]{1,0:T(8,128)(2,1)S(1)} %get-tuple-element.27), channel_id=1, source_target_pairs={{4,0},{12,1},{0,2},{8,3},{20,4},{28,5},{16,6},{24,7},{5,8},{13,9},... | collective-permute-start | bytes 196616 | tf_op jit(solution)/shard_map/ppermute | solution.py:293
  20.8 6.4 %collective-permute-start.11 = (bf16[64,512]{1,0:T(8,128)(2,1)S(1)}, bf16[64,512]{1,0:T(8,128)(2,1)S(1)}, u32[]{:S(2)}, u32[]{:S(2)}) collective-permute-start(bf16[64,512]{1,0:T(8,128)(2,1)S(1)} %get-tuple-element.28), channel_id=1, source_target_pairs={{12,0},{4,1},{8,2},{0,3},{28,4},{20,5},{24,6},{16,7},{13,8},{5,9},... | collective-permute-start | bytes 196616 | tf_op jit(solution)/shard_map/ppermute | solution.py:293

commit v7 on v6

--- a/solution.py
+++ b/solution.py
@@ -49,6 +49,18 @@
         move.wait()
 
 
+def place_kernel(owners, copies, *refs):
+    blocks, out_ref, sem = refs[:owners], refs[owners], refs[owners + 1]
+    group = lax.axis_index("seq") // copies
+    moves = [
+        pltpu.make_async_copy(blocks[k], out_ref.at[group ^ k], sem.at[k]) for k in range(owners)
+    ]
+    for move in moves:
+        move.start()
+    for move in moves:
+        move.wait()
+
+
 def absorb_kernel(per_device, q_ref, w_ref, *outs):
     rows, heads, width = q_ref.shape
     piece = SPEC * heads
@@ -72,72 +84,43 @@
                 outs[k][:, LATENT:] = q[a * piece : (a + 1) * piece, NOPE:]
 
 
-def block_scores(q, refs, starts, length):
+def merge_kernel(*refs):
+    q_refs, out_ref = refs[:-1], refs[-1]
+    piece = q_refs[0].shape[0]
+    for k, ref in enumerate(q_refs):
+        out_ref[k * piece : (k + 1) * piece] = ref[...]
+
+
+def attend_kernel(copies, per_device, heads, len_ref, q_ref, *refs):
+    key_refs, outs = refs[:copies], refs[copies:]
+    owners, rows, slots = key_refs[0].shape
+    q = q_ref[...]
     width = q.shape[1]
-    keys = jnp.concatenate([ref[:width, :] for ref in refs], axis=1)
-    lane = lax.broadcasted_iota(jnp.int32, (1, refs[0].shape[1]), 1)
-    position = jnp.concatenate([lane + start for start in starts], axis=1)
-    s = jnp.dot(q, keys, preferred_element_type=jnp.float32) * SCORE_SCALE
-    return jnp.where(position < length, s, masked_value)
-
-
-def weigh(s, refs, top):
-    w = jnp.exp(s - top)
-    values = jnp.concatenate([ref[:LATENT, :] for ref in refs], axis=1)
-    out = lax.dot_general(
-        w.astype(jnp.bfloat16),
-        values,
-        (((1,), (1,)), ((), ())),
-        preferred_element_type=jnp.float32,
-    )
-    return jnp.sum(w, axis=1, keepdims=True), out
-
-
-def begin_kernel(owners, copies, per_device, len_ref, *refs):
-    q_refs, key_refs = refs[:per_device], refs[per_device : per_device + owners]
-    q_out, top_ref, total_ref, out_ref = refs[per_device + owners :]
-    seq_index = lax.axis_index("seq")
-    group, core = seq_index // copies, seq_index % copies
-    length = len_ref[lax.axis_index("head") * owners + group]
-    slots = key_refs[0].shape[1]
-    q = jnp.concatenate([ref[...] for ref in q_refs], axis=0)
-    starts = [((group ^ k) * copies + core) * slots for k in range(owners)]
-    s = block_scores(q, key_refs, starts, length)
-    top = jnp.max(s, axis=1, keepdims=True)
-    total, out = weigh(s, key_refs, top)
-    q_out[...] = q
-    top_ref[...] = jnp.broadcast_to(top, top_ref.shape)
-    total_ref[...] = jnp.broadcast_to(total, total_ref.shape)
-    out_ref[...] = out
-
-
-def finish_kernel(
-    owners, copies, per_device, heads, len_ref, q_ref, top_ref, total_ref, part_ref, *refs
-):
-    own_refs, far_refs = refs[:owners], refs[owners : owners * copies]
-    outs, fresh_ref = refs[owners * copies : -1], refs[-1]
     seq_index = lax.axis_index("seq")
     group, core = seq_index // copies, seq_index % copies
     sequence = lax.axis_index("head") * owners + group
     length = len_ref[sequence]
-    q = q_ref[...]
-    slots, width = own_refs[0].shape[1], q.shape[1]
+    lane = lax.broadcasted_iota(jnp.int32, (1, slots), 1)
+    scores = []
+    for e in range(copies):
+        keys = jnp.concatenate([key_refs[e][g, :width] for g in range(owners)], axis=1)
+        first = (core + copies - e) % copies
+        position = jnp.concatenate(
+            [lane + (g * copies + first) * slots for g in range(owners)], axis=1
+        )
+        s = jnp.dot(q, keys, preferred_element_type=jnp.float32) * SCORE_SCALE
+        scores.append(jnp.where(position < length, s, masked_value))
 
     home = sequence // per_device
-    for e in range(copies):
-        for k in range(owners):
-            source = (group ^ k) * copies + (core + copies - e) % copies
-
-            @pl.when(source == home)
-            def _():
-                fresh_ref[...] = (own_refs + far_refs)[e * owners + k][width:, :]
-
-    parts = -(-width // slots)
-    rows = per_device * SPEC
-    fresh = fresh_ref[...].astype(jnp.float32)
-    fresh = jnp.concatenate([fresh[n * rows : (n + 1) * rows] for n in range(parts)], axis=1)
-    fresh = fresh[:, :width]
-    spare = -rows % 16
+    fresh_all = key_refs[0][home // copies, width:]
+    for e in range(1, copies):
+        mine = (core + copies - e) % copies == home % copies
+        fresh_all = jnp.where(mine, key_refs[e][home // copies, width:], fresh_all)
+    fresh_all = fresh_all.astype(jnp.float32)
+    count = per_device * SPEC
+    parts = [fresh_all[n * count : (n + 1) * count] for n in range(-(-width // slots))]
+    fresh = jnp.concatenate(parts, axis=1)[:, :width]
+    spare = -count % 16
     if spare:
         fresh = jnp.concatenate([fresh, jnp.zeros((spare, width), jnp.float32)], axis=0)
     fresh = fresh.astype(jnp.bfloat16)
@@ -149,24 +132,22 @@
     causal = (key // SPEC == sequence % per_device) & (key % SPEC <= row // heads)
     f = jnp.where(causal, f * SCORE_SCALE, masked_value)
 
-    starts = [
-        ((group ^ k) * copies + (core + copies - e) % copies) * slots
-        for e in range(1, copies)
-        for k in range(owners)
-    ]
-    s = block_scores(q, far_refs, starts, length)
-    first = top_ref[:, :1]
-    top = jnp.maximum(
-        jnp.maximum(first, jnp.max(s, axis=1, keepdims=True)), jnp.max(f, axis=1, keepdims=True)
-    )
-    total, out = weigh(s, far_refs, top)
+    top = functools.reduce(
+        jnp.maximum, [jnp.max(s, axis=1, keepdims=True) for s in scores + [f]]
+    )
     w = jnp.exp(f - top)
-    scale = jnp.exp(first - top)
-    total += jnp.sum(w, axis=1, keepdims=True) + total_ref[:, :1] * scale
-    out += part_ref[...] * scale
-    out += jnp.dot(
-        w.astype(jnp.bfloat16), fresh[:, :LATENT], preferred_element_type=jnp.float32
-    )
+    total = jnp.sum(w, axis=1, keepdims=True)
+    out = jnp.dot(w.astype(jnp.bfloat16), fresh[:, :LATENT], preferred_element_type=jnp.float32)
+    for s, ref in zip(scores, key_refs):
+        w = jnp.exp(s - top)
+        total += jnp.sum(w, axis=1, keepdims=True)
+        values = jnp.concatenate([ref[g, :LATENT] for g in range(owners)], axis=1)
+        out += lax.dot_general(
+            w.astype(jnp.bfloat16),
+            values,
+            (((1,), (1,)), ((), ())),
+            preferred_element_type=jnp.float32,
+        )
     out = (out / total).astype(jnp.bfloat16)
     piece = SPEC * heads
     for k in range(per_device):
@@ -242,15 +223,26 @@
         compiler_params=params,
         cost_estimate=LONG,
     )(in_hbm(jnp.swapaxes(cache, 1, 2)), in_hbm(new_latent))
-    own_keys = [picked[0]] + [
+    blocks = [picked[0]] + [
         lax.ppermute(picked[k], "seq", in_plane(lambda g, t: (g ^ k) * copies + t))
         for k in range(1, owners)
     ]
-    far_keys = [
-        lax.ppermute(keys, "seq", in_plane(lambda g, t: g * copies + (t + e) % copies))
-        for e in range(1, copies)
-        for keys in own_keys
-    ]
+    keys = [
+        pl.pallas_call(
+            functools.partial(place_kernel, owners, copies),
+            out_shape=jax.ShapeDtypeStruct((owners, *blocks[0].shape), cache.dtype),
+            in_specs=[vmem] * owners,
+            out_specs=vmem,
+            scratch_shapes=[pltpu.SemaphoreType.DMA((owners,))],
+            compiler_params=params,
+        )(*blocks)
+    ]
+    for e in range(1, copies):
+        keys.append(
+            lax.ppermute(
+                keys[0], "seq", in_plane(lambda g, t: g * copies + (t + e) % copies)
+            )
+        )
 
     pieces = pl.pallas_call(
         functools.partial(absorb_kernel, per_device),
@@ -267,27 +259,21 @@
         for k in range(per_device)
     ]
 
-    state = pl.pallas_call(
-        functools.partial(begin_kernel, owners, copies, per_device),
-        out_shape=[
-            jax.ShapeDtypeStruct((all_rows, width), jnp.bfloat16),
-            jax.ShapeDtypeStruct((all_rows, 128), jnp.float32),
-            jax.ShapeDtypeStruct((all_rows, 128), jnp.float32),
-            jax.ShapeDtypeStruct((all_rows, LATENT), jnp.float32),
-        ],
-        in_specs=[smem] + [vmem] * (per_device + owners),
-        out_specs=[vmem] * 4,
+    q_all = pl.pallas_call(
+        merge_kernel,
+        out_shape=jax.ShapeDtypeStruct((all_rows, width), jnp.bfloat16),
+        in_specs=[vmem] * per_device,
+        out_specs=vmem,
         compiler_params=params,
         cost_estimate=LONG,
-    )(lengths, *arrived, *own_keys)
+    )(*arrived)
     latent = pl.pallas_call(
-        functools.partial(finish_kernel, owners, copies, per_device, heads),
+        functools.partial(attend_kernel, copies, per_device, heads),
         out_shape=[jax.ShapeDtypeStruct((piece, LATENT), jnp.bfloat16)] * per_device,
-        in_specs=[smem] + [vmem] * (len(state) + owners * copies),
+        in_specs=[smem] + [vmem] * (1 + copies),
         out_specs=[vmem] * per_device,
-        scratch_shapes=[pltpu.VMEM((fresh_rows, slots), jnp.bfloat16)],
         compiler_params=params,
-    )(lengths, *state, *own_keys, *far_keys)
+    )(lengths, q_all, *keys)
 
     back = [
         lax.ppermute(latent[k], both, [(owner(i, j, k), flat(i, j)) for i, j in devices])

time: 28.4 us -> 29.2 us (1.028)
  waiting for transfers between devices: 12.4 us -> 15.8 us
  starting transfers between devices: 10.4 us -> 8.04 us
    ppermute x3, waiting for transfers between devices: 0.13 us -> 6.72 us  [whole_sequences(): lax.ppermute(picked[k], 'seq', in_plane(lambda g, t: (g ^ k) * copies + t))]
    ppermute x2, waiting for transfers between devices: 6.01 us -> 0.01 us  [whole_sequences(): lax.ppermute(pieces[k], both, [(flat(host(i, j), j), owner(i, j, k)) for...]
    ppermute x4 -> x1, waiting for transfers between devices: 0.01 us -> 1.92 us  [whole_sequences(): lax.ppermute(keys[0], 'seq', in_plane(lambda g, t: g * copies + (t + e) %...]
    ppermute x2, starting transfers between devices: 4.9 us -> 3.22 us  [whole_sequences(): lax.ppermute(latent[k], both, [(owner(i, j, k), flat(i, j)) for i, j in d...]
    ppermute x2, waiting for transfers between devices: 5.8 us -> 6.65 us  [whole_sequences(): lax.ppermute(latent[k], both, [(owner(i, j, k), flat(i, j)) for i, j in d...]
    ppermute x4 -> x1, starting transfers between devices: 0.9 us -> 0.18 us  [whole_sequences(): lax.ppermute(keys[0], 'seq', in_plane(lambda g, t: g * copies + (t + e) %...]
    pallas_call x2 -> x3, Pallas kernels: 2.48 us -> 2.27 us  [the longest x1 1.43 us: whole_sequences(): pl.pallas_call(functools.partial(attend_kernel, copies, per_device, heads...]
  transfers between devices with their start and end apart: 12 -> 9, of which waited for: 5 -> 7; matrix products, arithmetic and copies ran while one was open for 0% -> 0% of each run, Pallas kernels for 10% -> 9%
where the time goes in v7:
time: 29.2 us; the launch traced here: 29 us
  waiting for transfers between devices  15.8 us (54%)
  starting transfers between devices  8.04 us (28%)
  Pallas kernels  5.14 us (18%)
    ppermute x3, waiting for transfers between devices, whole_sequences(): lax.ppermute(picked[k], 'seq', in_plane(lambda g, t: (g ^ k) * copies + t))  6.72 us
    ppermute x2, waiting for transfers between devices, whole_sequences(): lax.ppermute(latent[k], both, [(owner(i, j, k), flat(i, j)) for i, j in d...  6.65 us
    ppermute x3, starting transfers between devices, whole_sequences(): lax.ppermute(picked[k], 'seq', in_plane(lambda g, t: (g ^ k) * copies + t))  3.55 us
    ppermute x2, starting transfers between devices, whole_sequences(): lax.ppermute(latent[k], both, [(owner(i, j, k), flat(i, j)) for i, j in d...  3.22 us
    ppermute x1, waiting for transfers between devices, whole_sequences(): lax.ppermute(keys[0], 'seq', in_plane(lambda g, t: g * copies + (t + e) %...  1.92 us
    pallas_call x1, Pallas kernels, whole_sequences(): pl.pallas_call(functools.partial(attend_kernel, copies, per_device, heads...  1.43 us
    pallas_call x1, Pallas kernels, whole_sequences(): pl.pallas_call(functools.partial(pick_kernel, owners, copies), out_shape=...  1.33 us
    ppermute x2, starting transfers between devices, whole_sequences(): lax.ppermute(pieces[k], both, [(flat(host(i, j), j), owner(i, j, k)) for...  1.08 us
  transfers between devices with their start and end apart: 9, of which 7 were waited for; matrix products, arithmetic and copies ran while one was open for 0% of the time, Pallas kernels for 9%

profile of v7, /device:TPU:6, one launch (start us, length us, event | category | flops | bytes accessed | tf_op | source)
XLA Modules:
  0.0 29.0 jit_solution(17196449176269775935)
XLA Ops:
  0.0 0.0 collective-permute-start
  0.0 1.3 %shard_map.66 = (bf16[624,128]{1,0:T(8,128)(2,1)S(1)}, bf16[624,128]{1,0:T(8,128)(2,1)S(1)}, bf16[624,128]{1,0:T(8,128)(2,1)S(1)}, bf16[624,128]{1,0:T(8,128)(2,1)S(1)}) custom-call(bf16[4,576,128]{2,1,0:T(8,128)(2,1)} %bitcast.1, bf16[8,576]{1,0:T(8,128)(2,1)} %new_hbm.1), custom_call_target="tpu_custom_call" | custom-call | flops 20000000000 | tf_op jit(solution)/shard_map/pallas_call | solution.py:214
  1.3 0.6 %collective-permute-start.3 = (bf16[624,128]{1,0:T(8,128)(2,1)S(1)}, bf16[624,128]{1,0:T(8,128)(2,1)S(1)}, u32[]{:S(2)}, u32[]{:S(2)}) collective-permute-start(bf16[624,128]{1,0:T(8,128)(2,1)S(1)} %get-tuple-element.16), channel_id=1, source_target_pairs={{0,8},{4,12},{8,0},{12,4},{16,24},{20,28},{24,16},{28,20},{1,9},{5... | collective-permute-start | bytes 479240 | tf_op jit(solution)/shard_map/ppermute | solution.py:227
  1.9 2.0 %collective-permute-start.4 = (bf16[624,128]{1,0:T(8,128)(2,1)S(1)}, bf16[624,128]{1,0:T(8,128)(2,1)S(1)}, u32[]{:S(2)}, u32[]{:S(2)}) collective-permute-start(bf16[624,128]{1,0:T(8,128)(2,1)S(1)} %get-tuple-element.17), channel_id=1, source_target_pairs={{0,16},{4,20},{8,24},{12,28},{16,0},{20,4},{24,8},{28,12},{1,17},{... | collective-permute-start | bytes 479240 | tf_op jit(solution)/shard_map/ppermute | solution.py:227
  3.9 1.0 %collective-permute-start.5 = (bf16[624,128]{1,0:T(8,128)(2,1)S(1)}, bf16[624,128]{1,0:T(8,128)(2,1)S(1)}, u32[]{:S(2)}, u32[]{:S(2)}) collective-permute-start(bf16[624,128]{1,0:T(8,128)(2,1)S(1)} %get-tuple-element.18), channel_id=1, source_target_pairs={{0,24},{4,28},{8,16},{12,20},{16,8},{20,12},{24,0},{28,4},{1,25},{... | collective-permute-start | bytes 479240 | tf_op jit(solution)/shard_map/ppermute | solution.py:227
  4.9 0.5 %collective-permute-done.q_ref = bf16[8,16,192]{2,1,0:T(8,128)(2,1)S(1)} collective-permute-done((bf16[8,16,192]{2,1,0:T(8,128)(2,1)}, bf16[8,16,192]{2,1,0:T(8,128)(2,1)S(1)}, u32[]{:S(2)}, u32[]{:S(2)}) %collective-permute-start) | collective-permute-done | bytes 49184 | tf_op jit(solution)/shard_map/ppermute | solution.py:209
  5.4 0.5 %shard_map.64 = (bf16[64,576]{1,0:T(8,128)(2,1)S(1)}, bf16[64,576]{1,0:T(8,128)(2,1)S(1)}) custom-call(bf16[8,16,192]{2,1,0:T(8,128)(2,1)S(1)} %collective-permute-done.q_ref, bf16[16,128,512]{2,1,0:T(8,128)(2,1)S(1)} %copy-done.2), custom_call_target="tpu_custom_call" | custom-call | flops 20000000000 | tf_op jit(solution)/shard_map/pallas_call | solution.py:247
  5.8 0.2 collective-permute-start.1
  6.1 0.8 %collective-permute-start.2 = (bf16[64,576]{1,0:T(8,128)(2,1)S(1)}, bf16[64,576]{1,0:T(8,128)(2,1)S(1)}, u32[]{:S(2)}, u32[]{:S(2)}) collective-permute-start(bf16[64,576]{1,0:T(8,128)(2,1)S(1)} %get-tuple-element.14), channel_id=1, source_target_pairs={{8,12},{5,4},{6,8},{11,0},{24,28},{21,20},{22,24},{27,16},{12,13},... | collective-permute-start | bytes 221192 | tf_op jit(solution)/shard_map/ppermute | solution.py:256
  6.9 1.3 %collective-permute-done.3.refs_1_ = bf16[624,128]{1,0:T(8,128)(2,1)S(1)} collective-permute-done((bf16[624,128]{1,0:T(8,128)(2,1)S(1)}, bf16[624,128]{1,0:T(8,128)(2,1)S(1)}, u32[]{:S(2)}, u32[]{:S(2)}) %collective-permute-start.3) | collective-permute-done | bytes 159776 | tf_op jit(solution)/shard_map/ppermute | solution.py:227
  8.2 3.2 %collective-permute-done.4.refs_2_ = bf16[624,128]{1,0:T(8,128)(2,1)S(1)} collective-permute-done((bf16[624,128]{1,0:T(8,128)(2,1)S(1)}, bf16[624,128]{1,0:T(8,128)(2,1)S(1)}, u32[]{:S(2)}, u32[]{:S(2)}) %collective-permute-start.4) | collective-permute-done | bytes 159776 | tf_op jit(solution)/shard_map/ppermute | solution.py:227
  11.4 2.3 %collective-permute-done.5.refs_3_ = bf16[624,128]{1,0:T(8,128)(2,1)S(1)} collective-permute-done((bf16[624,128]{1,0:T(8,128)(2,1)S(1)}, bf16[624,128]{1,0:T(8,128)(2,1)S(1)}, u32[]{:S(2)}, u32[]{:S(2)}) %collective-permute-start.5) | collective-permute-done | bytes 159776 | tf_op jit(solution)/shard_map/ppermute | solution.py:227
  13.6 0.8 %shard_map.67.refs_0_ = bf16[4,624,128]{2,1,0:T(8,128)(2,1)S(1)} custom-call(bf16[624,128]{1,0:T(8,128)(2,1)S(1)} %get-tuple-element.15.refs_0_, bf16[624,128]{1,0:T(8,128)(2,1)S(1)} %collective-permute-done.3.refs_1_, bf16[624,128]{1,0:T(8,128)(2,1)S(1)} %collective-permute-done.4.refs_2_, bf16[624,128]{1,0:T(8,128)(2,1)S(1)} %collective-permute-done.5.refs_3_), custom_call_target="tpu_custom_call" | custom-call | tf_op jit(solution)/shard_map/pallas_call | solution.py:231
  14.5 0.0 copy-start.1
  14.5 0.2 collective-permute-start.6
  14.7 0.0 collective-permute-done.1.refs_0_
  14.7 0.0 collective-permute-done.2.refs_1_
  14.7 1.9 %collective-permute-done.6.refs_1_ = bf16[4,624,128]{2,1,0:T(8,128)(2,1)S(1)} collective-permute-done((bf16[4,624,128]{2,1,0:T(8,128)(2,1)S(1)}, bf16[4,624,128]{2,1,0:T(8,128)(2,1)S(1)}, u32[]{:S(2)}, u32[]{:S(2)}) %collective-permute-start.6) | collective-permute-done | bytes 639008 | tf_op jit(solution)/shard_map/ppermute | solution.py:242
  16.6 1.4 %shard_map.68 = (bf16[64,512]{1,0:T(8,128)(2,1)S(1)}, bf16[64,512]{1,0:T(8,128)(2,1)S(1)}) custom-call(s32[16]{0:T(128)S(1)} %copy-done.1, bf16[128,576]{1,0:T(8,128)(2,1)S(1)} %shard_map.65.q_ref, bf16[4,624,128]{2,1,0:T(8,128)(2,1)S(1)} %shard_map.67.refs_0_, bf16[4,624,128]{2,1,0:T(8,128)(2,1)S(1)} %collective-permute-done.6.refs_1_), custom_call_target="tpu_custom_call" | custom-call | tf_op jit(solution)/shard_map/pallas_call | solution.py:270
  18.1 3.0 %collective-permute-start.7 = (bf16[64,512]{1,0:T(8,128)(2,1)S(1)}, bf16[64,512]{1,0:T(8,128)(2,1)S(1)}, u32[]{:S(2)}, u32[]{:S(2)}) collective-permute-start(bf16[64,512]{1,0:T(8,128)(2,1)S(1)} %get-tuple-element.19), channel_id=1, source_target_pairs={{4,0},{12,1},{0,2},{8,3},{20,4},{28,5},{16,6},{24,7},{5,8},{13,9},... | collective-permute-start | bytes 196616 | tf_op jit(solution)/shard_map/ppermute | solution.py:279
  21.1 0.2 collective-permute-start.8
  21.3 4.2 %collective-permute-done.7.refs_0_ = bf16[64,512]{1,0:T(8,128)(2,1)S(1)} collective-permute-done((bf16[64,512]{1,0:T(8,128)(2,1)S(1)}, bf16[64,512]{1,0:T(8,128)(2,1)S(1)}, u32[]{:S(2)}, u32[]{:S(2)}) %collective-permute-start.7) | collective-permute-done | bytes 65568 | tf_op jit(solution)/shard_map/ppermute | solution.py:279
  25.4 2.5 %collective-permute-done.8.refs_1_ = bf16[64,512]{1,0:T(8,128)(2,1)S(1)} collective-permute-done((bf16[64,512]{1,0:T(8,128)(2,1)S(1)}, bf16[64,512]{1,0:T(8,128)(2,1)S(1)}, u32[]{:S(2)}, u32[]{:S(2)}) %collective-permute-start.8) | collective-permute-done | bytes 65568 | tf_op jit(solution)/shard_map/ppermute | solution.py:279
  27.9 1.1 %shard_map.69 = bf16[8,16,128]{2,1,0:T(8,128)(2,1)} custom-call(bf16[16,512,128]{2,1,0:T(8,128)(2,1)S(1)} %copy-done, bf16[64,512]{1,0:T(8,128)(2,1)S(1)} %collective-permute-done.7.refs_0_, bf16[64,512]{1,0:T(8,128)(2,1)S(1)} %collective-permute-done.8.refs_1_), custom_call_target="tpu_custom_call" | custom-call | tf_op jit(solution)/shard_map/pallas_call | solution.py:282
  (6 shorter events, 0.0 us)
Async XLA Ops:
  0.0 5.4 %collective-permute-start = (bf16[8,16,192]{2,1,0:T(8,128)(2,1)}, bf16[8,16,192]{2,1,0:T(8,128)(2,1)S(1)}, u32[]{:S(2)}, u32[]{:S(2)}) collective-permute-start(bf16[8,16,192]{2,1,0:T(8,128)(2,1)} %param.6), channel_id=1, source_target_pairs={{0,8},{1,5},{2,6},{3,11},{4,24},{5,21},{6,22},{7,27},{8,12},{9,1},... | collective-permute-start | bytes 147464 | tf_op jit(solution)/shard_map/ppermute | solution.py:209
  0.0 5.4 %copy-start.2 = (bf16[16,128,512]{2,1,0:T(8,128)(2,1)S(1)}, bf16[16,128,512]{2,1,0:T(8,128)(2,1)}, u32[]{:S(2)}) copy-start(bf16[16,128,512]{2,1,0:T(8,128)(2,1)} %w_ref.2) | copy-start | bytes 6291460
  1.3 6.8 %collective-permute-start.3 = (bf16[624,128]{1,0:T(8,128)(2,1)S(1)}, bf16[624,128]{1,0:T(8,128)(2,1)S(1)}, u32[]{:S(2)}, u32[]{:S(2)}) collective-permute-start(bf16[624,128]{1,0:T(8,128)(2,1)S(1)} %get-tuple-element.16), channel_id=1, source_target_pairs={{0,8},{4,12},{8,0},{12,4},{16,24},{20,28},{24,16},{28,20},{1,9},{5... | collective-permute-start | bytes 479240 | tf_op jit(solution)/shard_map/ppermute | solution.py:227
  1.9 9.4 %collective-permute-start.4 = (bf16[624,128]{1,0:T(8,128)(2,1)S(1)}, bf16[624,128]{1,0:T(8,128)(2,1)S(1)}, u32[]{:S(2)}, u32[]{:S(2)}) collective-permute-start(bf16[624,128]{1,0:T(8,128)(2,1)S(1)} %get-tuple-element.17), channel_id=1, source_target_pairs={{0,16},{4,20},{8,24},{12,28},{16,0},{20,4},{24,8},{28,12},{1,17},{... | collective-permute-start | bytes 479240 | tf_op jit(solution)/shard_map/ppermute | solution.py:227
  3.9 9.7 %collective-permute-start.5 = (bf16[624,128]{1,0:T(8,128)(2,1)S(1)}, bf16[624,128]{1,0:T(8,128)(2,1)S(1)}, u32[]{:S(2)}, u32[]{:S(2)}) collective-permute-start(bf16[624,128]{1,0:T(8,128)(2,1)S(1)} %get-tuple-element.18), channel_id=1, source_target_pairs={{0,24},{4,28},{8,16},{12,20},{16,8},{20,12},{24,0},{28,4},{1,25},{... | collective-permute-start | bytes 479240 | tf_op jit(solution)/shard_map/ppermute | solution.py:227
  5.8 8.8 %collective-permute-start.1 = (bf16[64,576]{1,0:T(8,128)(2,1)S(1)}, bf16[64,576]{1,0:T(8,128)(2,1)S(1)}, u32[]{:S(2)}, u32[]{:S(2)}) collective-permute-start(bf16[64,576]{1,0:T(8,128)(2,1)S(1)} %get-tuple-element.13), channel_id=1, source_target_pairs={{8,4},{5,12},{6,0},{11,8},{24,20},{21,28},{22,16},{27,24},{12,5},{... | collective-permute-start | bytes 221192 | tf_op jit(solution)/shard_map/ppermute | solution.py:256
  6.1 8.6 %collective-permute-start.2 = (bf16[64,576]{1,0:T(8,128)(2,1)S(1)}, bf16[64,576]{1,0:T(8,128)(2,1)S(1)}, u32[]{:S(2)}, u32[]{:S(2)}) collective-permute-start(bf16[64,576]{1,0:T(8,128)(2,1)S(1)} %get-tuple-element.14), channel_id=1, source_target_pairs={{8,12},{5,4},{6,8},{11,0},{24,28},{21,20},{22,24},{27,16},{12,13},... | collective-permute-start | bytes 221192 | tf_op jit(solution)/shard_map/ppermute | solution.py:256
  14.5 2.2 %copy-start.1 = (s32[16]{0:T(128)S(1)}, s32[16]{0:T(128)}, u32[]{:S(2)}) copy-start(s32[16]{0:T(128)} %len_ref.1) | copy-start | bytes 196
  14.5 2.1 %collective-permute-start.6 = (bf16[4,624,128]{2,1,0:T(8,128)(2,1)S(1)}, bf16[4,624,128]{2,1,0:T(8,128)(2,1)S(1)}, u32[]{:S(2)}, u32[]{:S(2)}) collective-permute-start(bf16[4,624,128]{2,1,0:T(8,128)(2,1)S(1)} %shard_map.67.refs_0_), channel_id=1, source_target_pairs={{0,4},{4,0},{8,12},{12,8},{16,20},{20,16},{24,28},{28,24},{1,5},{5... | collective-permute-start | bytes 1916936 | tf_op jit(solution)/shard_map/ppermute | solution.py:242
  14.7 13.3 %copy-start = (bf16[16,512,128]{2,1,0:T(8,128)(2,1)S(1)}, bf16[16,512,128]{2,1,0:T(8,128)(2,1)}, u32[]{:S(2)}) copy-start(bf16[16,512,128]{2,1,0:T(8,128)(2,1)} %w_ref.3) | copy-start | bytes 6291460
  18.1 7.4 %collective-permute-start.7 = (bf16[64,512]{1,0:T(8,128)(2,1)S(1)}, bf16[64,512]{1,0:T(8,128)(2,1)S(1)}, u32[]{:S(2)}, u32[]{:S(2)}) collective-permute-start(bf16[64,512]{1,0:T(8,128)(2,1)S(1)} %get-tuple-element.19), channel_id=1, source_target_pairs={{4,0},{12,1},{0,2},{8,3},{20,4},{28,5},{16,6},{24,7},{5,8},{13,9},... | collective-permute-start | bytes 196616 | tf_op jit(solution)/shard_map/ppermute | solution.py:279
  21.1 6.8 %collective-permute-start.8 = (bf16[64,512]{1,0:T(8,128)(2,1)S(1)}, bf16[64,512]{1,0:T(8,128)(2,1)S(1)}, u32[]{:S(2)}, u32[]{:S(2)}) collective-permute-start(bf16[64,512]{1,0:T(8,128)(2,1)S(1)} %get-tuple-element.20), channel_id=1, source_target_pairs={{12,0},{4,1},{8,2},{0,3},{28,4},{20,5},{24,6},{16,7},{13,8},{5,9},... | collective-permute-start | bytes 196616 | tf_op jit(solution)/shard_map/ppermute | solution.py:279

commit v8 on v6

--- a/solution.py
+++ b/solution.py
@@ -18,13 +18,14 @@
 masked_value = -1e30
 
 
-def pick_kernel(owners, copies, cache_hbm, new_hbm, *refs):
+def pick_kernel(turn, copies, cache_hbm, new_hbm, *refs):
+    owners = len(turn)
     outs, (new_ref, sem) = refs[:owners], refs[owners:]
     group = lax.axis_index("seq") // copies
     width = cache_hbm.shape[1]
     moves = [
         pltpu.make_async_copy(
-            cache_hbm.at[group ^ k], outs[k].at[pl.ds(0, width)], sem.at[k]
+            cache_hbm.at[group ^ turn[k]], outs[k].at[pl.ds(0, width)], sem.at[k]
         )
         for k in range(owners)
     ]
@@ -49,6 +50,17 @@
         move.wait()
 
 
+def pair_kernel(first_ref, second_ref, out_ref, sem):
+    moves = [
+        pltpu.make_async_copy(ref, out_ref.at[n], sem.at[n])
+        for n, ref in enumerate((first_ref, second_ref))
+    ]
+    for move in moves:
+        move.start()
+    for move in moves:
+        move.wait()
+
+
 def absorb_kernel(per_device, q_ref, w_ref, *outs):
     rows, heads, width = q_ref.shape
     piece = SPEC * heads
@@ -93,7 +105,8 @@
     return jnp.sum(w, axis=1, keepdims=True), out
 
 
-def begin_kernel(owners, copies, per_device, len_ref, *refs):
+def begin_kernel(turn, copies, per_device, len_ref, *refs):
+    owners = len(turn)
     q_refs, key_refs = refs[:per_device], refs[per_device : per_device + owners]
     q_out, top_ref, total_ref, out_ref = refs[per_device + owners :]
     seq_index = lax.axis_index("seq")
@@ -101,7 +114,7 @@
     length = len_ref[lax.axis_index("head") * owners + group]
     slots = key_refs[0].shape[1]
     q = jnp.concatenate([ref[...] for ref in q_refs], axis=0)
-    starts = [((group ^ k) * copies + core) * slots for k in range(owners)]
+    starts = [((group ^ k) * copies + core) * slots for k in turn]
     s = block_scores(q, key_refs, starts, length)
     top = jnp.max(s, axis=1, keepdims=True)
     total, out = weigh(s, key_refs, top)
@@ -112,10 +125,12 @@
 
 
 def finish_kernel(
-    owners, copies, per_device, heads, len_ref, q_ref, top_ref, total_ref, part_ref, *refs
+    turn, copies, per_device, heads, len_ref, q_ref, top_ref, total_ref, part_ref, *refs
 ):
-    own_refs, far_refs = refs[:owners], refs[owners : owners * copies]
-    outs, fresh_ref = refs[owners * copies : -1], refs[-1]
+    owners = len(turn)
+    own_refs, (pair_ref, *far_refs) = refs[:owners], refs[owners : 2 * owners - 1]
+    far_refs = [pair_ref.at[0], pair_ref.at[1]] + far_refs
+    outs, fresh_ref = refs[2 * owners - 1 : -1], refs[-1]
     seq_index = lax.axis_index("seq")
     group, core = seq_index // copies, seq_index % copies
     sequence = lax.axis_index("head") * owners + group
@@ -126,11 +141,11 @@
     home = sequence // per_device
     for e in range(copies):
         for k in range(owners):
-            source = (group ^ k) * copies + (core + copies - e) % copies
+            source = (group ^ turn[k]) * copies + (core + copies - e) % copies
 
             @pl.when(source == home)
             def _():
-                fresh_ref[...] = (own_refs + far_refs)[e * owners + k][width:, :]
+                fresh_ref[...] = (far_refs if e else own_refs)[k][width:, :]
 
     parts = -(-width // slots)
     rows = per_device * SPEC
@@ -152,7 +167,7 @@
     starts = [
         ((group ^ k) * copies + (core + copies - e) % copies) * slots
         for e in range(1, copies)
-        for k in range(owners)
+        for k in turn
     ]
     s = block_scores(q, far_refs, starts, length)
     first = top_ref[:, :1]
@@ -227,11 +242,13 @@
 
     moved = lax.ppermute(queries, both, [(flat(i, j), flat(host(i, j), j)) for i, j in devices])
 
+    turn = [0] + list(range(owners - 1, 0, -1))
+
     def in_plane(move):
         return [(g * copies + t, move(g, t)) for g in range(owners) for t in range(copies)]
 
     picked = pl.pallas_call(
-        functools.partial(pick_kernel, owners, copies),
+        functools.partial(pick_kernel, turn, copies),
         out_shape=[jax.ShapeDtypeStruct((width + fresh_rows, slots), cache.dtype)] * owners,
         in_specs=[anywhere] * 2,
         out_specs=[vmem] * owners,
@@ -243,14 +260,19 @@
         cost_estimate=LONG,
     )(in_hbm(jnp.swapaxes(cache, 1, 2)), in_hbm(new_latent))
     own_keys = [picked[0]] + [
-        lax.ppermute(picked[k], "seq", in_plane(lambda g, t: (g ^ k) * copies + t))
+        lax.ppermute(picked[k], "seq", in_plane(lambda g, t: (g ^ turn[k]) * copies + t))
         for k in range(1, owners)
     ]
-    far_keys = [
-        lax.ppermute(keys, "seq", in_plane(lambda g, t: g * copies + (t + e) % copies))
-        for e in range(1, copies)
-        for keys in own_keys
-    ]
+    pair = pl.pallas_call(
+        pair_kernel,
+        out_shape=jax.ShapeDtypeStruct((2, *picked[0].shape), cache.dtype),
+        in_specs=[vmem] * 2,
+        out_specs=vmem,
+        scratch_shapes=[pltpu.SemaphoreType.DMA((2,))],
+        compiler_params=params,
+    )(*own_keys[:2])
+    other_core = in_plane(lambda g, t: g * copies + (t + 1) % copies)
+    far_keys = [lax.ppermute(keys, "seq", other_core) for keys in [pair] + own_keys[2:]]
 
     pieces = pl.pallas_call(
         functools.partial(absorb_kernel, per_device),
@@ -268,7 +290,7 @@
     ]
 
     state = pl.pallas_call(
-        functools.partial(begin_kernel, owners, copies, per_device),
+        functools.partial(begin_kernel, turn, copies, per_device),
         out_shape=[
             jax.ShapeDtypeStruct((all_rows, width), jnp.bfloat16),
             jax.ShapeDtypeStruct((all_rows, 128), jnp.float32),
@@ -281,9 +303,9 @@
         cost_estimate=LONG,
     )(lengths, *arrived, *own_keys)
     latent = pl.pallas_call(
-        functools.partial(finish_kernel, owners, copies, per_device, heads),
+        functools.partial(finish_kernel, turn, copies, per_device, heads),
         out_shape=[jax.ShapeDtypeStruct((piece, LATENT), jnp.bfloat16)] * per_device,
-        in_specs=[smem] + [vmem] * (len(state) + owners * copies),
+        in_specs=[smem] + [vmem] * (len(state) + len(own_keys) + len(far_keys)),
         out_specs=[vmem] * per_device,
         scratch_shapes=[pltpu.VMEM((fresh_rows, slots), jnp.bfloat16)],
         compiler_params=params,

time: 28.4 us -> 28.2 us (level)
  waiting for transfers between devices: 12.4 us -> 11.9 us
  Pallas kernels: 5.35 us -> 5.76 us
    ppermute x2, waiting for transfers between devices: 6.01 us -> 0.01 us  [whole_sequences(): lax.ppermute(pieces[k], both, [(flat(host(i, j), j), owner(i, j, k)) for...]
    ppermute x7 -> x6, waiting for transfers between devices: 0.14 us -> 6.06 us  [the longest x3 5.94 us: whole_sequences(): lax.ppermute(picked[k], 'seq', in_plane(lambda g, t: (g ^ turn[k]) * copi...]
    ppermute x7 -> x6, starting transfers between devices: 4.45 us -> 3.84 us  [the longest x3 3.55 us: whole_sequences(): lax.ppermute(picked[k], 'seq', in_plane(lambda g, t: (g ^ turn[k]) * copi...]
    pallas_call x3 -> x4, Pallas kernels: 3.81 us -> 4.21 us  [the longest x1 1.36 us: whole_sequences(): pl.pallas_call(functools.partial(finish_kernel, turn, copies, per_device,...]
  transfers between devices with their start and end apart: 12 -> 11, of which waited for: 5 -> 7; matrix products, arithmetic and copies ran while one was open for 0% -> 0% of each run, Pallas kernels for 10% -> 12%
where the time goes in v8:
time: 28.2 us; the launch traced here: 28.1 us
  waiting for transfers between devices  11.9 us (42%)
  starting transfers between devices  10.3 us (37%)
  Pallas kernels  5.76 us (20%)
    ppermute x3, waiting for transfers between devices, whole_sequences(): lax.ppermute(picked[k], 'seq', in_plane(lambda g, t: (g ^ turn[k]) * copi...  5.94 us
    ppermute x2, waiting for transfers between devices, whole_sequences(): lax.ppermute(latent[k], both, [(owner(i, j, k), flat(i, j)) for i, j in d...  5.64 us
    ppermute x2, starting transfers between devices, whole_sequences(): lax.ppermute(latent[k], both, [(owner(i, j, k), flat(i, j)) for i, j in d...  5.17 us
    ppermute x3, starting transfers between devices, whole_sequences(): lax.ppermute(picked[k], 'seq', in_plane(lambda g, t: (g ^ turn[k]) * copi...  3.55 us
    pallas_call x1, Pallas kernels, whole_sequences(): pl.pallas_call(functools.partial(finish_kernel, turn, copies, per_device,...  1.36 us
    pallas_call x1, Pallas kernels, whole_sequences(): pl.pallas_call(functools.partial(pick_kernel, turn, copies), out_shape=[j...  1.33 us
    ppermute x2, starting transfers between devices, whole_sequences(): lax.ppermute(pieces[k], both, [(flat(host(i, j), j), owner(i, j, k)) for...  1.31 us
    pallas_call x1, Pallas kernels, whole_sequences(): pl.pallas_call(functools.partial(begin_kernel, turn, copies, per_device),...  1.12 us
  transfers between devices with their start and end apart: 11, of which 7 were waited for; matrix products, arithmetic and copies ran while one was open for 0% of the time, Pallas kernels for 12%

profile of v8, /device:TPU:6, one launch (start us, length us, event | category | flops | bytes accessed | tf_op | source)
XLA Modules:
  0.0 28.1 jit_solution(4406131182361703366)
XLA Ops:
  0.0 1.3 %shard_map.65 = (bf16[624,128]{1,0:T(8,128)(2,1)S(1)}, bf16[624,128]{1,0:T(8,128)(2,1)S(1)}, bf16[624,128]{1,0:T(8,128)(2,1)S(1)}, bf16[624,128]{1,0:T(8,128)(2,1)S(1)}) custom-call(bf16[4,576,128]{2,1,0:T(8,128)(2,1)} %bitcast.1, bf16[8,576]{1,0:T(8,128)(2,1)} %new_hbm.1), custom_call_target="tpu_custom_call" | custom-call | flops 20000000000 | tf_op jit(solution)/shard_map/pallas_call | solution.py:250
  1.3 2.0 %collective-permute-start.3 = (bf16[624,128]{1,0:T(8,128)(2,1)S(1)}, bf16[624,128]{1,0:T(8,128)(2,1)S(1)}, u32[]{:S(2)}, u32[]{:S(2)}) collective-permute-start(bf16[624,128]{1,0:T(8,128)(2,1)S(1)} %get-tuple-element.20), channel_id=1, source_target_pairs={{0,24},{4,28},{8,16},{12,20},{16,8},{20,12},{24,0},{28,4},{1,25},{... | collective-permute-start | bytes 479240 | tf_op jit(solution)/shard_map/ppermute | solution.py:263
  3.4 0.0 collective-permute-start.4
  3.4 1.5 %collective-permute-start.5 = (bf16[624,128]{1,0:T(8,128)(2,1)S(1)}, bf16[624,128]{1,0:T(8,128)(2,1)S(1)}, u32[]{:S(2)}, u32[]{:S(2)}) collective-permute-start(bf16[624,128]{1,0:T(8,128)(2,1)S(1)} %get-tuple-element.22), channel_id=1, source_target_pairs={{0,8},{4,12},{8,0},{12,4},{16,24},{20,28},{24,16},{28,20},{1,9},{5... | collective-permute-start | bytes 479240 | tf_op jit(solution)/shard_map/ppermute | solution.py:263
  4.9 0.2 collective-permute-done.q_ref
  5.1 0.5 %shard_map.64 = (bf16[64,576]{1,0:T(8,128)(2,1)S(1)}, bf16[64,576]{1,0:T(8,128)(2,1)S(1)}) custom-call(bf16[8,16,192]{2,1,0:T(8,128)(2,1)S(1)} %collective-permute-done.q_ref, bf16[16,128,512]{2,1,0:T(8,128)(2,1)S(1)} %copy-done.2), custom_call_target="tpu_custom_call" | custom-call | flops 20000000000 | tf_op jit(solution)/shard_map/pallas_call | solution.py:277
  5.6 0.5 %collective-permute-start.1 = (bf16[64,576]{1,0:T(8,128)(2,1)S(1)}, bf16[64,576]{1,0:T(8,128)(2,1)S(1)}, u32[]{:S(2)}, u32[]{:S(2)}) collective-permute-start(bf16[64,576]{1,0:T(8,128)(2,1)S(1)} %get-tuple-element.17), channel_id=1, source_target_pairs={{8,4},{5,12},{6,0},{11,8},{24,20},{21,28},{22,16},{27,24},{12,5},{... | collective-permute-start | bytes 221192 | tf_op jit(solution)/shard_map/ppermute | solution.py:286
  6.1 0.8 %collective-permute-start.2 = (bf16[64,576]{1,0:T(8,128)(2,1)S(1)}, bf16[64,576]{1,0:T(8,128)(2,1)S(1)}, u32[]{:S(2)}, u32[]{:S(2)}) collective-permute-start(bf16[64,576]{1,0:T(8,128)(2,1)S(1)} %get-tuple-element.18), channel_id=1, source_target_pairs={{8,12},{5,4},{6,8},{11,0},{24,28},{21,20},{22,24},{27,16},{12,13},... | collective-permute-start | bytes 221192 | tf_op jit(solution)/shard_map/ppermute | solution.py:286
  6.9 2.3 %collective-permute-done.3.refs_3_.second_ref.refs_1_ = bf16[624,128]{1,0:T(8,128)(2,1)S(1)} collective-permute-done((bf16[624,128]{1,0:T(8,128)(2,1)S(1)}, bf16[624,128]{1,0:T(8,128)(2,1)S(1)}, u32[]{:S(2)}, u32[]{:S(2)}) %collective-permute-start.3) | collective-permute-done | bytes 159776 | tf_op jit(solution)/shard_map/ppermute | solution.py:263
  9.2 0.4 %shard_map.67 = bf16[2,624,128]{2,1,0:T(8,128)(2,1)S(1)} custom-call(bf16[624,128]{1,0:T(8,128)(2,1)S(1)} %get-tuple-element.19.refs_2_.first_ref.refs_0_, bf16[624,128]{1,0:T(8,128)(2,1)S(1)} %collective-permute-done.3.refs_3_.second_ref.refs_1_), custom_call_target="tpu_custom_call" | custom-call | tf_op jit(solution)/shard_map/pallas_call | solution.py:266
  9.6 0.1 collective-permute-start.6
  9.7 2.4 %collective-permute-done.4.refs_4_.refs_2_ = bf16[624,128]{1,0:T(8,128)(2,1)S(1)} collective-permute-done((bf16[624,128]{1,0:T(8,128)(2,1)S(1)}, bf16[624,128]{1,0:T(8,128)(2,1)S(1)}, u32[]{:S(2)}, u32[]{:S(2)}) %collective-permute-start.4) | collective-permute-done | bytes 159776 | tf_op jit(solution)/shard_map/ppermute | solution.py:263
  12.1 0.1 collective-permute-start.7
  12.2 1.2 %collective-permute-done.5.refs_5_.refs_3_ = bf16[624,128]{1,0:T(8,128)(2,1)S(1)} collective-permute-done((bf16[624,128]{1,0:T(8,128)(2,1)S(1)}, bf16[624,128]{1,0:T(8,128)(2,1)S(1)}, u32[]{:S(2)}, u32[]{:S(2)}) %collective-permute-start.5) | collective-permute-done | bytes 159776 | tf_op jit(solution)/shard_map/ppermute | solution.py:263
  13.5 0.1 collective-permute-start.8
  13.6 0.0 copy-start
  13.6 1.1 %shard_map.66 = (bf16[128,576]{1,0:T(8,128)(2,1)S(1)}, f32[128,128]{1,0:T(8,128)S(1)}, f32[128,128]{1,0:T(8,128)S(1)}, f32[128,512]{1,0:T(8,128)S(1)}) custom-call(s32[16]{0:T(128)S(1)} %copy-done.1, bf16[64,576]{1,0:T(8,128)(2,1)S(1)} %collective-permute-done.1.refs_0_, bf16[64,576]{1,0:T(8,128)(2,1)S(1)} %collective-permute-done.2.refs_1_, ...), custom_call_target="tpu_custom_call" | custom-call | flops 20000000000 | tf_op jit(solution)/shard_map/pallas_call | solution.py:292
  14.7 0.1 collective-permute-done.8.refs_6_
  14.9 1.4 %shard_map.68 = (bf16[64,512]{1,0:T(8,128)(2,1)S(1)}, bf16[64,512]{1,0:T(8,128)(2,1)S(1)}) custom-call(s32[16]{0:T(128)S(1)} %copy-done.1, bf16[128,576]{1,0:T(8,128)(2,1)S(1)} %get-tuple-element.23.q_ref, f32[128,128]{1,0:T(8,128)S(1)} %get-tuple-element.24.top_ref, f32[128,128]{1,0:T(8,128)S(1)} %get-tuple-element.25.total_ref, ...), custom_call_target="tpu_custom_call" | custom-call | tf_op jit(solution)/shard_map/pallas_call | solution.py:305
  16.2 3.5 %collective-permute-start.10 = (bf16[64,512]{1,0:T(8,128)(2,1)S(1)}, bf16[64,512]{1,0:T(8,128)(2,1)S(1)}, u32[]{:S(2)}, u32[]{:S(2)}) collective-permute-start(bf16[64,512]{1,0:T(8,128)(2,1)S(1)} %get-tuple-element.28), channel_id=1, source_target_pairs={{12,0},{4,1},{8,2},{0,3},{28,4},{20,5},{24,6},{16,7},{13,8},{5,9},... | collective-permute-start | bytes 196616 | tf_op jit(solution)/shard_map/ppermute | solution.py:315
  19.7 1.6 %collective-permute-start.9 = (bf16[64,512]{1,0:T(8,128)(2,1)S(1)}, bf16[64,512]{1,0:T(8,128)(2,1)S(1)}, u32[]{:S(2)}, u32[]{:S(2)}) collective-permute-start(bf16[64,512]{1,0:T(8,128)(2,1)S(1)} %get-tuple-element.27), channel_id=1, source_target_pairs={{4,0},{12,1},{0,2},{8,3},{20,4},{28,5},{16,6},{24,7},{5,8},{13,9},... | collective-permute-start | bytes 196616 | tf_op jit(solution)/shard_map/ppermute | solution.py:315
  21.4 1.3 %collective-permute-done.10.refs_1_ = bf16[64,512]{1,0:T(8,128)(2,1)S(1)} collective-permute-done((bf16[64,512]{1,0:T(8,128)(2,1)S(1)}, bf16[64,512]{1,0:T(8,128)(2,1)S(1)}, u32[]{:S(2)}, u32[]{:S(2)}) %collective-permute-start.10) | collective-permute-done | bytes 65568 | tf_op jit(solution)/shard_map/ppermute | solution.py:315
  22.7 4.4 %collective-permute-done.9.refs_0_ = bf16[64,512]{1,0:T(8,128)(2,1)S(1)} collective-permute-done((bf16[64,512]{1,0:T(8,128)(2,1)S(1)}, bf16[64,512]{1,0:T(8,128)(2,1)S(1)}, u32[]{:S(2)}, u32[]{:S(2)}) %collective-permute-start.9) | collective-permute-done | bytes 65568 | tf_op jit(solution)/shard_map/ppermute | solution.py:315
  27.0 1.1 %shard_map.69 = bf16[8,16,128]{2,1,0:T(8,128)(2,1)} custom-call(bf16[16,512,128]{2,1,0:T(8,128)(2,1)S(1)} %copy-done, bf16[64,512]{1,0:T(8,128)(2,1)S(1)} %collective-permute-done.9.refs_0_, bf16[64,512]{1,0:T(8,128)(2,1)S(1)} %collective-permute-done.10.refs_1_), custom_call_target="tpu_custom_call" | custom-call | tf_op jit(solution)/shard_map/pallas_call | solution.py:318
  (10 shorter events, 0.0 us)
Async XLA Ops:
  0.0 5.1 %collective-permute-start = (bf16[8,16,192]{2,1,0:T(8,128)(2,1)}, bf16[8,16,192]{2,1,0:T(8,128)(2,1)S(1)}, u32[]{:S(2)}, u32[]{:S(2)}) collective-permute-start(bf16[8,16,192]{2,1,0:T(8,128)(2,1)} %param.6), channel_id=1, source_target_pairs={{0,8},{1,5},{2,6},{3,11},{4,24},{5,21},{6,22},{7,27},{8,12},{9,1},... | collective-permute-start | bytes 147464 | tf_op jit(solution)/shard_map/ppermute | solution.py:243
  0.0 5.1 %copy-start.2 = (bf16[16,128,512]{2,1,0:T(8,128)(2,1)S(1)}, bf16[16,128,512]{2,1,0:T(8,128)(2,1)}, u32[]{:S(2)}) copy-start(bf16[16,128,512]{2,1,0:T(8,128)(2,1)} %w_ref.2) | copy-start | bytes 6291460
  1.3 7.9 %collective-permute-start.3 = (bf16[624,128]{1,0:T(8,128)(2,1)S(1)}, bf16[624,128]{1,0:T(8,128)(2,1)S(1)}, u32[]{:S(2)}, u32[]{:S(2)}) collective-permute-start(bf16[624,128]{1,0:T(8,128)(2,1)S(1)} %get-tuple-element.20), channel_id=1, source_target_pairs={{0,24},{4,28},{8,16},{12,20},{16,8},{20,12},{24,0},{28,4},{1,25},{... | collective-permute-start | bytes 479240 | tf_op jit(solution)/shard_map/ppermute | solution.py:263
  3.4 8.8 %collective-permute-start.4 = (bf16[624,128]{1,0:T(8,128)(2,1)S(1)}, bf16[624,128]{1,0:T(8,128)(2,1)S(1)}, u32[]{:S(2)}, u32[]{:S(2)}) collective-permute-start(bf16[624,128]{1,0:T(8,128)(2,1)S(1)} %get-tuple-element.21), channel_id=1, source_target_pairs={{0,16},{4,20},{8,24},{12,28},{16,0},{20,4},{24,8},{28,12},{1,17},{... | collective-permute-start | bytes 479240 | tf_op jit(solution)/shard_map/ppermute | solution.py:263
  3.4 10.2 %copy-start.1 = (s32[16]{0:T(128)S(1)}, s32[16]{0:T(128)}, u32[]{:S(2)}) copy-start(s32[16]{0:T(128)} %len_ref.3) | copy-start | bytes 196
  3.4 10.0 %collective-permute-start.5 = (bf16[624,128]{1,0:T(8,128)(2,1)S(1)}, bf16[624,128]{1,0:T(8,128)(2,1)S(1)}, u32[]{:S(2)}, u32[]{:S(2)}) collective-permute-start(bf16[624,128]{1,0:T(8,128)(2,1)S(1)} %get-tuple-element.22), channel_id=1, source_target_pairs={{0,8},{4,12},{8,0},{12,4},{16,24},{20,28},{24,16},{28,20},{1,9},{5... | collective-permute-start | bytes 479240 | tf_op jit(solution)/shard_map/ppermute | solution.py:263
  5.6 8.0 %collective-permute-start.1 = (bf16[64,576]{1,0:T(8,128)(2,1)S(1)}, bf16[64,576]{1,0:T(8,128)(2,1)S(1)}, u32[]{:S(2)}, u32[]{:S(2)}) collective-permute-start(bf16[64,576]{1,0:T(8,128)(2,1)S(1)} %get-tuple-element.17), channel_id=1, source_target_pairs={{8,4},{5,12},{6,0},{11,8},{24,20},{21,28},{22,16},{27,24},{12,5},{... | collective-permute-start | bytes 221192 | tf_op jit(solution)/shard_map/ppermute | solution.py:286
  6.1 7.5 %collective-permute-start.2 = (bf16[64,576]{1,0:T(8,128)(2,1)S(1)}, bf16[64,576]{1,0:T(8,128)(2,1)S(1)}, u32[]{:S(2)}, u32[]{:S(2)}) collective-permute-start(bf16[64,576]{1,0:T(8,128)(2,1)S(1)} %get-tuple-element.18), channel_id=1, source_target_pairs={{8,12},{5,4},{6,8},{11,0},{24,28},{21,20},{22,24},{27,16},{12,13},... | collective-permute-start | bytes 221192 | tf_op jit(solution)/shard_map/ppermute | solution.py:286
  9.6 5.2 %collective-permute-start.6 = (bf16[2,624,128]{2,1,0:T(8,128)(2,1)S(1)}, bf16[2,624,128]{2,1,0:T(8,128)(2,1)S(1)}, u32[]{:S(2)}, u32[]{:S(2)}) collective-permute-start(bf16[2,624,128]{2,1,0:T(8,128)(2,1)S(1)} %shard_map.67), channel_id=1, source_target_pairs={{0,4},{4,0},{8,12},{12,8},{16,20},{20,16},{24,28},{28,24},{1,5},{5... | collective-permute-start | bytes 958472 | tf_op jit(solution)/shard_map/ppermute | solution.py:275
  12.1 2.6 %collective-permute-start.7 = (bf16[624,128]{1,0:T(8,128)(2,1)S(1)}, bf16[624,128]{1,0:T(8,128)(2,1)S(1)}, u32[]{:S(2)}, u32[]{:S(2)}) collective-permute-start(bf16[624,128]{1,0:T(8,128)(2,1)S(1)} %collective-permute-done.4.refs_4_.refs_2_), channel_id=1, source_target_pairs={{0,4},{4,0},{8,12},{12,8},{16,20},{20,16},{24,28},{28,24},{1,5},{5... | collective-permute-start | bytes 479240 | tf_op jit(solution)/shard_map/ppermute | solution.py:275
  13.5 1.4 %collective-permute-start.8 = (bf16[624,128]{1,0:T(8,128)(2,1)S(1)}, bf16[624,128]{1,0:T(8,128)(2,1)S(1)}, u32[]{:S(2)}, u32[]{:S(2)}) collective-permute-start(bf16[624,128]{1,0:T(8,128)(2,1)S(1)} %collective-permute-done.5.refs_5_.refs_3_), channel_id=1, source_target_pairs={{0,4},{4,0},{8,12},{12,8},{16,20},{20,16},{24,28},{28,24},{1,5},{5... | collective-permute-start | bytes 479240 | tf_op jit(solution)/shard_map/ppermute | solution.py:275
  13.6 13.4 %copy-start = (bf16[16,512,128]{2,1,0:T(8,128)(2,1)S(1)}, bf16[16,512,128]{2,1,0:T(8,128)(2,1)}, u32[]{:S(2)}) copy-start(bf16[16,512,128]{2,1,0:T(8,128)(2,1)} %w_ref.3) | copy-start | bytes 6291460
  16.2 6.4 %collective-permute-start.10 = (bf16[64,512]{1,0:T(8,128)(2,1)S(1)}, bf16[64,512]{1,0:T(8,128)(2,1)S(1)}, u32[]{:S(2)}, u32[]{:S(2)}) collective-permute-start(bf16[64,512]{1,0:T(8,128)(2,1)S(1)} %get-tuple-element.28), channel_id=1, source_target_pairs={{12,0},{4,1},{8,2},{0,3},{28,4},{20,5},{24,6},{16,7},{13,8},{5,9},... | collective-permute-start | bytes 196616 | tf_op jit(solution)/shard_map/ppermute | solution.py:315
  19.7 7.3 %collective-permute-start.9 = (bf16[64,512]{1,0:T(8,128)(2,1)S(1)}, bf16[64,512]{1,0:T(8,128)(2,1)S(1)}, u32[]{:S(2)}, u32[]{:S(2)}) collective-permute-start(bf16[64,512]{1,0:T(8,128)(2,1)S(1)} %get-tuple-element.27), channel_id=1, source_target_pairs={{4,0},{12,1},{0,2},{8,3},{20,4},{28,5},{16,6},{24,7},{5,8},{13,9},... | collective-permute-start | bytes 196616 | tf_op jit(solution)/shard_map/ppermute | solution.py:315

commit v9 on v8

--- a/solution.py
+++ b/solution.py
@@ -12,10 +12,30 @@
 LATENT = 512
 SPEC = 4
 SCORE_SCALE = (NOPE + ROPE) ** (-0.5)
+COPIES = 2
 VMEM_LIMIT = 16 * 1024 * 1024
 LONG = pl.CostEstimate(flops=2 * 10**10, bytes_accessed=0, transcendentals=0)
 
 masked_value = -1e30
+
+
+def far_half(plane, pair):
+    return 1 * (plane <= 2 * pair)
+
+
+def first_out(host_chip, k):
+    return (host_chip + 1 + k) % 2
+
+
+def first_back(home_chip, head_shard):
+    far = 1 * (far_half(home_chip, head_shard // 2) == head_shard % 2)
+    return home_chip % 2 ^ far
+
+
+def first_block(plane, chip, core):
+    arrived = 1 - chip % 2 ^ plane // 2 ^ core
+    back = far_half(plane, 1 - core) ^ (1 * (chip % 2 == plane % 2))
+    return arrived ^ back
 
 
 def pick_kernel(turn, copies, cache_hbm, new_hbm, *refs):
@@ -73,9 +93,9 @@
     absorbed = jnp.dot(
         spread, w_ref[...].reshape(heads * NOPE, LATENT), preferred_element_type=jnp.float32
     ).astype(jnp.bfloat16)
-    head_shard = lax.axis_index("head")
+    group = lax.axis_index("seq") // COPIES
     for k in range(per_device):
-        which = (head_shard + k) % per_device
+        which = first_out(group, k)
         for a in range(per_device):
 
             @pl.when(which == a)
@@ -184,20 +204,20 @@
     )
     out = (out / total).astype(jnp.bfloat16)
     piece = SPEC * heads
+    swapped = first_block(lax.axis_index("head"), group, core)
     for k in range(per_device):
-        outs[k][...] = out[k * piece : (k + 1) * piece]
+        for n in range(per_device):
+
+            @pl.when(swapped ^ k != n)
+            def _():
+                outs[k][...] = out[n * piece : (n + 1) * piece]
 
 
 def project_kernel(per_device, w_ref, *refs):
     lat_refs, out_ref = refs[:-1], refs[-1]
     rows, heads, width = out_ref.shape
-    head_shard = lax.axis_index("head")
-    parts = []
-    for a in range(per_device):
-        part = lat_refs[0][...]
-        for k in range(1, per_device):
-            part = jnp.where((head_shard + k) % per_device == a, lat_refs[k][...], part)
-        parts.append(part)
+    first = first_back(lax.axis_index("seq") // COPIES, lax.axis_index("head"))
+    parts = [jnp.where(first == a, lat_refs[0][...], lat_refs[1][...]) for a in range(per_device)]
     latent = jnp.concatenate(parts, axis=0)
     out = jnp.zeros((rows * heads, width), jnp.float32)
     own_head = lax.broadcasted_iota(jnp.int32, out.shape, 0) % heads
@@ -235,14 +255,14 @@
         other = (i // copies) ^ (2 - ((j ^ (j >> 1)) & 1))
         return ((i % copies) * 2 + other // 2) * copies + other % 2
 
-    def owner(i, j, k):
-        sequence = i * per_device + (j + k) % per_device
+    def owner(i, j, a):
+        sequence = i * per_device + a
         core = (j // per_device) ^ 1
         return flat((sequence % owners) * copies + core, sequence // owners)
 
     moved = lax.ppermute(queries, both, [(flat(i, j), flat(host(i, j), j)) for i, j in devices])
 
-    turn = [0] + list(range(owners - 1, 0, -1))
+    turn = [0, 1, 3, 2]
 
     def in_plane(move):
         return [(g * copies + t, move(g, t)) for g in range(owners) for t in range(copies)]
@@ -284,7 +304,12 @@
     )(moved, w_uk)
     arrived = [
         lax.ppermute(
-            pieces[k], both, [(flat(host(i, j), j), owner(i, j, k)) for i, j in devices]
+            pieces[k],
+            both,
+            [
+                (flat(host(i, j), j), owner(i, j, first_out(host(i, j) // copies, k)))
+                for i, j in devices
+            ],
         )
         for k in range(per_device)
     ]
@@ -312,7 +337,11 @@
     )(lengths, *state, *own_keys, *far_keys)
 
     back = [
-        lax.ppermute(latent[k], both, [(owner(i, j, k), flat(i, j)) for i, j in devices])
+        lax.ppermute(
+            latent[k],
+            both,
+            [(owner(i, j, first_back(i // copies, j) ^ k ^ 1), flat(i, j)) for i, j in devices],
+        )
         for k in range(per_device)
     ]
     return pl.pallas_call(
@@ -321,7 +350,7 @@
         in_specs=[vmem] * (1 + per_device),
         out_specs=vmem,
         compiler_params=params,
-    )(w_uv, *back)
+    )(w_uv, *back[::-1])
 
 
 def local_partial(
@@ -429,7 +458,7 @@
     if (
         per_device == 2
         and rows % SPEC == 0
-        and seq_size == 2 * owners
+        and seq_size == COPIES * owners
         and head_size == owners == 4
     ):
         return whole_sequences(

time: 28.2 us -> 28.5 us (1.011)
  starting transfers between devices: 10.3 us -> 10.6 us
    ppermute x3, starting transfers between devices: 0.29 us -> 0.61 us  [whole_sequences(): lax.ppermute(keys, 'seq', other_core)]
  transfers between devices with their start and end apart: 11 -> 11, of which waited for: 7 -> 6; matrix products, arithmetic and copies ran while one was open for 0% -> 0% of each run, Pallas kernels for 12% -> 12%
where the time goes in v9:
time: 28.5 us; the launch traced here: 28.3 us
  waiting for transfers between devices  11.9 us (42%)
  starting transfers between devices  10.6 us (37%)
  Pallas kernels  5.77 us (20%)
    ppermute x3, waiting for transfers between devices, whole_sequences(): lax.ppermute(picked[k], 'seq', in_plane(lambda g, t: (g ^ turn[k]) * copi...  6.06 us
    ppermute x2, starting transfers between devices, whole_sequences(): lax.ppermute(latent[k], both, [(owner(i, j, first_back(i // copies, j) ^...  5.35 us
    ppermute x2, waiting for transfers between devices, whole_sequences(): lax.ppermute(latent[k], both, [(owner(i, j, first_back(i // copies, j) ^...  5.1 us
    ppermute x3, starting transfers between devices, whole_sequences(): lax.ppermute(picked[k], 'seq', in_plane(lambda g, t: (g ^ turn[k]) * copi...  3.55 us
    pallas_call x1, Pallas kernels, whole_sequences(): pl.pallas_call(functools.partial(finish_kernel, turn, copies, per_device,...  1.37 us
    pallas_call x1, Pallas kernels, whole_sequences(): pl.pallas_call(functools.partial(pick_kernel, turn, copies), out_shape=[j...  1.33 us
    pallas_call x1, Pallas kernels, whole_sequences(): pl.pallas_call(functools.partial(begin_kernel, turn, copies, per_device),...  1.12 us
    ppermute x2, starting transfers between devices, whole_sequences(): lax.ppermute(pieces[k], both, [(flat(host(i, j), j), owner(i, j, first_ou...  1.08 us
  transfers between devices with their start and end apart: 11, of which 6 were waited for; matrix products, arithmetic and copies ran while one was open for 0% of the time, Pallas kernels for 12%

profile of v9, /device:TPU:6, one launch (start us, length us, event | category | flops | bytes accessed | tf_op | source)
XLA Modules:
  0.0 28.3 jit_solution(10006587663726561261)
XLA Ops:
  0.0 0.0 collective-permute-start
  0.0 1.3 %shard_map.65 = (bf16[624,128]{1,0:T(8,128)(2,1)S(1)}, bf16[624,128]{1,0:T(8,128)(2,1)S(1)}, bf16[624,128]{1,0:T(8,128)(2,1)S(1)}, bf16[624,128]{1,0:T(8,128)(2,1)S(1)}) custom-call(bf16[4,576,128]{2,1,0:T(8,128)(2,1)} %bitcast.1, bf16[8,576]{1,0:T(8,128)(2,1)} %new_hbm.1), custom_call_target="tpu_custom_call" | custom-call | flops 20000000000 | tf_op jit(solution)/shard_map/pallas_call | solution.py:270
  1.3 0.6 %collective-permute-start.3 = (bf16[624,128]{1,0:T(8,128)(2,1)S(1)}, bf16[624,128]{1,0:T(8,128)(2,1)S(1)}, u32[]{:S(2)}, u32[]{:S(2)}) collective-permute-start(bf16[624,128]{1,0:T(8,128)(2,1)S(1)} %get-tuple-element.20), channel_id=1, source_target_pairs={{0,8},{4,12},{8,0},{12,4},{16,24},{20,28},{24,16},{28,20},{1,9},{5... | collective-permute-start | bytes 479240 | tf_op jit(solution)/shard_map/ppermute | solution.py:283
  1.9 1.5 %collective-permute-start.4 = (bf16[624,128]{1,0:T(8,128)(2,1)S(1)}, bf16[624,128]{1,0:T(8,128)(2,1)S(1)}, u32[]{:S(2)}, u32[]{:S(2)}) collective-permute-start(bf16[624,128]{1,0:T(8,128)(2,1)S(1)} %get-tuple-element.21), channel_id=1, source_target_pairs={{0,24},{4,28},{8,16},{12,20},{16,8},{20,12},{24,0},{28,4},{1,25},{... | collective-permute-start | bytes 479240 | tf_op jit(solution)/shard_map/ppermute | solution.py:283
  3.5 1.4 %collective-permute-start.5 = (bf16[624,128]{1,0:T(8,128)(2,1)S(1)}, bf16[624,128]{1,0:T(8,128)(2,1)S(1)}, u32[]{:S(2)}, u32[]{:S(2)}) collective-permute-start(bf16[624,128]{1,0:T(8,128)(2,1)S(1)} %get-tuple-element.22), channel_id=1, source_target_pairs={{0,16},{4,20},{8,24},{12,28},{16,0},{20,4},{24,8},{28,12},{1,17},{... | collective-permute-start | bytes 479240 | tf_op jit(solution)/shard_map/ppermute | solution.py:283
  4.9 0.5 %collective-permute-done.q_ref = bf16[8,16,192]{2,1,0:T(8,128)(2,1)S(1)} collective-permute-done((bf16[8,16,192]{2,1,0:T(8,128)(2,1)}, bf16[8,16,192]{2,1,0:T(8,128)(2,1)S(1)}, u32[]{:S(2)}, u32[]{:S(2)}) %collective-permute-start) | collective-permute-done | bytes 49184 | tf_op jit(solution)/shard_map/ppermute | solution.py:263
  5.4 0.5 %shard_map.64 = (bf16[64,576]{1,0:T(8,128)(2,1)S(1)}, bf16[64,576]{1,0:T(8,128)(2,1)S(1)}) custom-call(bf16[8,16,192]{2,1,0:T(8,128)(2,1)S(1)} %collective-permute-done.q_ref, bf16[16,128,512]{2,1,0:T(8,128)(2,1)S(1)} %copy-done.2), custom_call_target="tpu_custom_call" | custom-call | flops 20000000000 | tf_op jit(solution)/shard_map/pallas_call | solution.py:297
  5.8 0.2 collective-permute-start.1
  6.1 0.8 %collective-permute-start.2 = (bf16[64,576]{1,0:T(8,128)(2,1)S(1)}, bf16[64,576]{1,0:T(8,128)(2,1)S(1)}, u32[]{:S(2)}, u32[]{:S(2)}) collective-permute-start(bf16[64,576]{1,0:T(8,128)(2,1)S(1)} %get-tuple-element.18), channel_id=1, source_target_pairs={{8,12},{5,4},{6,0},{11,8},{24,28},{21,20},{22,16},{27,24},{12,13},... | collective-permute-start | bytes 221192 | tf_op jit(solution)/shard_map/ppermute | solution.py:306
  6.9 1.3 %collective-permute-done.3.refs_3_.second_ref.refs_1_ = bf16[624,128]{1,0:T(8,128)(2,1)S(1)} collective-permute-done((bf16[624,128]{1,0:T(8,128)(2,1)S(1)}, bf16[624,128]{1,0:T(8,128)(2,1)S(1)}, u32[]{:S(2)}, u32[]{:S(2)}) %collective-permute-start.3) | collective-permute-done | bytes 159776 | tf_op jit(solution)/shard_map/ppermute | solution.py:283
  8.2 0.4 %shard_map.67 = bf16[2,624,128]{2,1,0:T(8,128)(2,1)S(1)} custom-call(bf16[624,128]{1,0:T(8,128)(2,1)S(1)} %get-tuple-element.19.refs_2_.first_ref.refs_0_, bf16[624,128]{1,0:T(8,128)(2,1)S(1)} %collective-permute-done.3.refs_3_.second_ref.refs_1_), custom_call_target="tpu_custom_call" | custom-call | tf_op jit(solution)/shard_map/pallas_call | solution.py:286
  8.6 0.1 collective-permute-start.6
  8.7 4.8 %collective-permute-done.4.refs_4_.refs_2_ = bf16[624,128]{1,0:T(8,128)(2,1)S(1)} collective-permute-done((bf16[624,128]{1,0:T(8,128)(2,1)S(1)}, bf16[624,128]{1,0:T(8,128)(2,1)S(1)}, u32[]{:S(2)}, u32[]{:S(2)}) %collective-permute-start.4) | collective-permute-done | bytes 159776 | tf_op jit(solution)/shard_map/ppermute | solution.py:283
  13.5 0.4 %collective-permute-start.7 = (bf16[624,128]{1,0:T(8,128)(2,1)S(1)}, bf16[624,128]{1,0:T(8,128)(2,1)S(1)}, u32[]{:S(2)}, u32[]{:S(2)}) collective-permute-start(bf16[624,128]{1,0:T(8,128)(2,1)S(1)} %collective-permute-done.4.refs_4_.refs_2_), channel_id=1, source_target_pairs={{0,4},{4,0},{8,12},{12,8},{16,20},{20,16},{24,28},{28,24},{1,5},{5... | collective-permute-start | bytes 479240 | tf_op jit(solution)/shard_map/ppermute | solution.py:295
  13.8 0.0 collective-permute-done.5.refs_5_.refs_3_
  13.8 0.2 collective-permute-start.8
  14.0 0.3 collective-permute-done.2.refs_1_
  14.3 1.1 %shard_map.66 = (bf16[128,576]{1,0:T(8,128)(2,1)S(1)}, f32[128,128]{1,0:T(8,128)S(1)}, f32[128,128]{1,0:T(8,128)S(1)}, f32[128,512]{1,0:T(8,128)S(1)}) custom-call(s32[16]{0:T(128)S(1)} %copy-done.1, bf16[64,576]{1,0:T(8,128)(2,1)S(1)} %collective-permute-done.1.refs_0_, bf16[64,576]{1,0:T(8,128)(2,1)S(1)} %collective-permute-done.2.refs_1_, ...), custom_call_target="tpu_custom_call" | custom-call | flops 20000000000 | tf_op jit(solution)/shard_map/pallas_call | solution.py:317
  15.4 1.4 %shard_map.68 = (bf16[64,512]{1,0:T(8,128)(2,1)S(1)}, bf16[64,512]{1,0:T(8,128)(2,1)S(1)}) custom-call(s32[16]{0:T(128)S(1)} %copy-done.1, bf16[128,576]{1,0:T(8,128)(2,1)S(1)} %get-tuple-element.23.q_ref, f32[128,128]{1,0:T(8,128)S(1)} %get-tuple-element.24.top_ref, f32[128,128]{1,0:T(8,128)S(1)} %get-tuple-element.25.total_ref, ...), custom_call_target="tpu_custom_call" | custom-call | tf_op jit(solution)/shard_map/pallas_call | solution.py:330
  16.8 3.2 %collective-permute-start.10 = (bf16[64,512]{1,0:T(8,128)(2,1)S(1)}, bf16[64,512]{1,0:T(8,128)(2,1)S(1)}, u32[]{:S(2)}, u32[]{:S(2)}) collective-permute-start(bf16[64,512]{1,0:T(8,128)(2,1)S(1)} %get-tuple-element.28), channel_id=1, source_target_pairs={{12,0},{4,1},{8,2},{0,3},{28,4},{20,5},{24,6},{16,7},{13,8},{5,9},... | collective-permute-start | bytes 196616 | tf_op jit(solution)/shard_map/ppermute | solution.py:340
  20.0 2.2 %collective-permute-start.9 = (bf16[64,512]{1,0:T(8,128)(2,1)S(1)}, bf16[64,512]{1,0:T(8,128)(2,1)S(1)}, u32[]{:S(2)}, u32[]{:S(2)}) collective-permute-start(bf16[64,512]{1,0:T(8,128)(2,1)S(1)} %get-tuple-element.27), channel_id=1, source_target_pairs={{4,0},{12,1},{0,2},{8,3},{20,4},{28,5},{16,6},{24,7},{5,8},{13,9},... | collective-permute-start | bytes 196616 | tf_op jit(solution)/shard_map/ppermute | solution.py:340
  22.2 1.1 %collective-permute-done.10.refs_1_ = bf16[64,512]{1,0:T(8,128)(2,1)S(1)} collective-permute-done((bf16[64,512]{1,0:T(8,128)(2,1)S(1)}, bf16[64,512]{1,0:T(8,128)(2,1)S(1)}, u32[]{:S(2)}, u32[]{:S(2)}) %collective-permute-start.10) | collective-permute-done | bytes 65568 | tf_op jit(solution)/shard_map/ppermute | solution.py:340
  23.3 4.0 %collective-permute-done.9.refs_0_ = bf16[64,512]{1,0:T(8,128)(2,1)S(1)} collective-permute-done((bf16[64,512]{1,0:T(8,128)(2,1)S(1)}, bf16[64,512]{1,0:T(8,128)(2,1)S(1)}, u32[]{:S(2)}, u32[]{:S(2)}) %collective-permute-start.9) | collective-permute-done | bytes 65568 | tf_op jit(solution)/shard_map/ppermute | solution.py:340
  27.3 1.1 %shard_map.69 = bf16[8,16,128]{2,1,0:T(8,128)(2,1)} custom-call(bf16[16,512,128]{2,1,0:T(8,128)(2,1)S(1)} %copy-done, bf16[64,512]{1,0:T(8,128)(2,1)S(1)} %collective-permute-done.9.refs_0_, bf16[64,512]{1,0:T(8,128)(2,1)S(1)} %collective-permute-done.10.refs_1_), custom_call_target="tpu_custom_call" | custom-call | tf_op jit(solution)/shard_map/pallas_call | solution.py:347
  (10 shorter events, 0.0 us)
Async XLA Ops:
  0.0 5.4 %collective-permute-start = (bf16[8,16,192]{2,1,0:T(8,128)(2,1)}, bf16[8,16,192]{2,1,0:T(8,128)(2,1)S(1)}, u32[]{:S(2)}, u32[]{:S(2)}) collective-permute-start(bf16[8,16,192]{2,1,0:T(8,128)(2,1)} %param.6), channel_id=1, source_target_pairs={{0,8},{1,5},{2,6},{3,11},{4,24},{5,21},{6,22},{7,27},{8,12},{9,1},... | collective-permute-start | bytes 147464 | tf_op jit(solution)/shard_map/ppermute | solution.py:263
  0.0 5.4 %copy-start.2 = (bf16[16,128,512]{2,1,0:T(8,128)(2,1)S(1)}, bf16[16,128,512]{2,1,0:T(8,128)(2,1)}, u32[]{:S(2)}) copy-start(bf16[16,128,512]{2,1,0:T(8,128)(2,1)} %w_ref.2) | copy-start | bytes 6291460
  1.3 6.9 %collective-permute-start.3 = (bf16[624,128]{1,0:T(8,128)(2,1)S(1)}, bf16[624,128]{1,0:T(8,128)(2,1)S(1)}, u32[]{:S(2)}, u32[]{:S(2)}) collective-permute-start(bf16[624,128]{1,0:T(8,128)(2,1)S(1)} %get-tuple-element.20), channel_id=1, source_target_pairs={{0,8},{4,12},{8,0},{12,4},{16,24},{20,28},{24,16},{28,20},{1,9},{5... | collective-permute-start | bytes 479240 | tf_op jit(solution)/shard_map/ppermute | solution.py:283
  1.9 11.5 %collective-permute-start.4 = (bf16[624,128]{1,0:T(8,128)(2,1)S(1)}, bf16[624,128]{1,0:T(8,128)(2,1)S(1)}, u32[]{:S(2)}, u32[]{:S(2)}) collective-permute-start(bf16[624,128]{1,0:T(8,128)(2,1)S(1)} %get-tuple-element.21), channel_id=1, source_target_pairs={{0,24},{4,28},{8,16},{12,20},{16,8},{20,12},{24,0},{28,4},{1,25},{... | collective-permute-start | bytes 479240 | tf_op jit(solution)/shard_map/ppermute | solution.py:283
  3.5 10.8 %copy-start.1 = (s32[16]{0:T(128)S(1)}, s32[16]{0:T(128)}, u32[]{:S(2)}) copy-start(s32[16]{0:T(128)} %len_ref.3) | copy-start | bytes 196
  3.5 10.4 %collective-permute-start.5 = (bf16[624,128]{1,0:T(8,128)(2,1)S(1)}, bf16[624,128]{1,0:T(8,128)(2,1)S(1)}, u32[]{:S(2)}, u32[]{:S(2)}) collective-permute-start(bf16[624,128]{1,0:T(8,128)(2,1)S(1)} %get-tuple-element.22), channel_id=1, source_target_pairs={{0,16},{4,20},{8,24},{12,28},{16,0},{20,4},{24,8},{28,12},{1,17},{... | collective-permute-start | bytes 479240 | tf_op jit(solution)/shard_map/ppermute | solution.py:283
  5.8 8.2 %collective-permute-start.1 = (bf16[64,576]{1,0:T(8,128)(2,1)S(1)}, bf16[64,576]{1,0:T(8,128)(2,1)S(1)}, u32[]{:S(2)}, u32[]{:S(2)}) collective-permute-start(bf16[64,576]{1,0:T(8,128)(2,1)S(1)} %get-tuple-element.17), channel_id=1, source_target_pairs={{8,4},{5,12},{6,8},{11,0},{24,20},{21,28},{22,24},{27,16},{12,5},{... | collective-permute-start | bytes 221192 | tf_op jit(solution)/shard_map/ppermute | solution.py:306
  6.1 8.2 %collective-permute-start.2 = (bf16[64,576]{1,0:T(8,128)(2,1)S(1)}, bf16[64,576]{1,0:T(8,128)(2,1)S(1)}, u32[]{:S(2)}, u32[]{:S(2)}) collective-permute-start(bf16[64,576]{1,0:T(8,128)(2,1)S(1)} %get-tuple-element.18), channel_id=1, source_target_pairs={{8,12},{5,4},{6,0},{11,8},{24,28},{21,20},{22,16},{27,24},{12,13},... | collective-permute-start | bytes 221192 | tf_op jit(solution)/shard_map/ppermute | solution.py:306
  8.6 6.8 %collective-permute-start.6 = (bf16[2,624,128]{2,1,0:T(8,128)(2,1)S(1)}, bf16[2,624,128]{2,1,0:T(8,128)(2,1)S(1)}, u32[]{:S(2)}, u32[]{:S(2)}) collective-permute-start(bf16[2,624,128]{2,1,0:T(8,128)(2,1)S(1)} %shard_map.67), channel_id=1, source_target_pairs={{0,4},{4,0},{8,12},{12,8},{16,20},{20,16},{24,28},{28,24},{1,5},{5... | collective-permute-start | bytes 958472 | tf_op jit(solution)/shard_map/ppermute | solution.py:295
  13.5 1.9 %collective-permute-start.7 = (bf16[624,128]{1,0:T(8,128)(2,1)S(1)}, bf16[624,128]{1,0:T(8,128)(2,1)S(1)}, u32[]{:S(2)}, u32[]{:S(2)}) collective-permute-start(bf16[624,128]{1,0:T(8,128)(2,1)S(1)} %collective-permute-done.4.refs_4_.refs_2_), channel_id=1, source_target_pairs={{0,4},{4,0},{8,12},{12,8},{16,20},{20,16},{24,28},{28,24},{1,5},{5... | collective-permute-start | bytes 479240 | tf_op jit(solution)/shard_map/ppermute | solution.py:295
  13.8 1.6 %collective-permute-start.8 = (bf16[624,128]{1,0:T(8,128)(2,1)S(1)}, bf16[624,128]{1,0:T(8,128)(2,1)S(1)}, u32[]{:S(2)}, u32[]{:S(2)}) collective-permute-start(bf16[624,128]{1,0:T(8,128)(2,1)S(1)} %collective-permute-done.5.refs_5_.refs_3_), channel_id=1, source_target_pairs={{0,4},{4,0},{8,12},{12,8},{16,20},{20,16},{24,28},{28,24},{1,5},{5... | collective-permute-start | bytes 479240 | tf_op jit(solution)/shard_map/ppermute | solution.py:295
  14.3 13.0 %copy-start = (bf16[16,512,128]{2,1,0:T(8,128)(2,1)S(1)}, bf16[16,512,128]{2,1,0:T(8,128)(2,1)}, u32[]{:S(2)}) copy-start(bf16[16,512,128]{2,1,0:T(8,128)(2,1)} %w_ref.3) | copy-start | bytes 6291460
  16.8 6.4 %collective-permute-start.10 = (bf16[64,512]{1,0:T(8,128)(2,1)S(1)}, bf16[64,512]{1,0:T(8,128)(2,1)S(1)}, u32[]{:S(2)}, u32[]{:S(2)}) collective-permute-start(bf16[64,512]{1,0:T(8,128)(2,1)S(1)} %get-tuple-element.28), channel_id=1, source_target_pairs={{12,0},{4,1},{8,2},{0,3},{28,4},{20,5},{24,6},{16,7},{13,8},{5,9},... | collective-permute-start | bytes 196616 | tf_op jit(solution)/shard_map/ppermute | solution.py:340
  20.0 7.3 %collective-permute-start.9 = (bf16[64,512]{1,0:T(8,128)(2,1)S(1)}, bf16[64,512]{1,0:T(8,128)(2,1)S(1)}, u32[]{:S(2)}, u32[]{:S(2)}) collective-permute-start(bf16[64,512]{1,0:T(8,128)(2,1)S(1)} %get-tuple-element.27), channel_id=1, source_target_pairs={{4,0},{12,1},{0,2},{8,3},{20,4},{28,5},{16,6},{24,7},{5,8},{13,9},... | collective-permute-start | bytes 196616 | tf_op jit(solution)/shard_map/ppermute | solution.py:340

commit v10 on v9

--- a/solution.py
+++ b/solution.py
@@ -19,12 +19,16 @@
 masked_value = -1e30
 
 
+def leaves_as(k, chip, head_shard):
+    return (k + chip + head_shard) % 2
+
+
+def owner_core(plane, chip, head_shard):
+    return 1 ^ head_shard // 2 ^ chip // 2 ^ plane // 2
+
+
 def far_half(plane, pair):
     return 1 * (plane <= 2 * pair)
-
-
-def first_out(host_chip, k):
-    return (host_chip + 1 + k) % 2
 
 
 def first_back(home_chip, head_shard):
@@ -33,40 +37,43 @@
 
 
 def first_block(plane, chip, core):
-    arrived = 1 - chip % 2 ^ plane // 2 ^ core
-    back = far_half(plane, 1 - core) ^ (1 * (chip % 2 == plane % 2))
-    return arrived ^ back
-
-
-def pick_kernel(turn, copies, cache_hbm, new_hbm, *refs):
+    return far_half(plane, 1 ^ core ^ chip // 2 ^ plane // 2) ^ 1
+
+
+def pick_kernel(turn, per_device, cache_hbm, q_hbm, new_hbm, *refs):
     owners = len(turn)
-    outs, (new_ref, sem) = refs[:owners], refs[owners:]
-    group = lax.axis_index("seq") // copies
-    width = cache_hbm.shape[1]
+    blocks, outs = refs[:owners], refs[owners : owners + per_device]
+    q_ref, new_ref, sem = refs[owners + per_device :]
+    chip = lax.axis_index("seq") // COPIES
     moves = [
-        pltpu.make_async_copy(
-            cache_hbm.at[group ^ turn[k]], outs[k].at[pl.ds(0, width)], sem.at[k]
-        )
+        pltpu.make_async_copy(q_hbm, q_ref, sem.at[owners]),
+        pltpu.make_async_copy(new_hbm, new_ref, sem.at[owners + 1]),
+    ] + [
+        pltpu.make_async_copy(cache_hbm.at[chip ^ turn[k]], blocks[k], sem.at[k])
         for k in range(owners)
     ]
-    fresh_move = pltpu.make_async_copy(new_hbm, new_ref, sem.at[owners])
-    fresh_move.start()
     for move in moves:
         move.start()
-    fresh_move.wait()
+    moves[0].wait()
+    moves[1].wait()
+    heads, width = q_ref.shape[1:]
     fresh = new_ref[...].astype(jnp.float32)
-    rows, slots = outs[0].shape
-    spare = -width % slots
-    if spare:
-        fresh = jnp.concatenate([fresh, jnp.zeros((fresh.shape[0], spare), jnp.float32)], axis=1)
-    parts = [fresh[:, n : n + slots] for n in range(0, width, slots)]
-    spare = rows - width - len(parts) * fresh.shape[0]
-    if spare:
-        parts.append(jnp.zeros((spare, slots), jnp.float32))
-    fresh = jnp.concatenate(parts, axis=0).astype(outs[0].dtype)
-    for out in outs:
-        out[width:, :] = fresh
-    for move in moves:
+    for a in range(per_device):
+        rows = q_ref[a * SPEC : (a + 1) * SPEC].reshape(SPEC * heads, width)
+        own = fresh[a * SPEC : (a + 1) * SPEC]
+        parts = [own[:, n : n + ROPE] for n in range(0, own.shape[1], ROPE)]
+        spare = SPEC * heads - SPEC * len(parts)
+        if spare:
+            parts.append(jnp.zeros((spare, ROPE), jnp.float32))
+        own = jnp.concatenate(parts, axis=0).astype(rows.dtype)
+        packed = jnp.concatenate([rows, own], axis=1)
+        for k in range(per_device):
+
+            @pl.when(leaves_as(k, chip, lax.axis_index("head")) == a)
+            def _():
+                outs[k][...] = packed
+
+    for move in moves[2:]:
         move.wait()
 
 
@@ -81,11 +88,10 @@
         move.wait()
 
 
-def absorb_kernel(per_device, q_ref, w_ref, *outs):
-    rows, heads, width = q_ref.shape
-    piece = SPEC * heads
-    q = q_ref[...].reshape(rows * heads, width)
-    nope = q[:, :NOPE]
+def absorb_kernel(per_device, w_ref, *refs):
+    packed, outs = refs[:per_device], refs[per_device:]
+    heads = w_ref.shape[0]
+    nope = jnp.concatenate([ref[:, :NOPE] for ref in packed], axis=0)
     own_head = lax.broadcasted_iota(jnp.int32, nope.shape, 0) % heads
     spread = jnp.concatenate(
         [jnp.where(own_head == h, nope, jnp.zeros_like(nope)) for h in range(heads)], axis=1
@@ -93,15 +99,10 @@
     absorbed = jnp.dot(
         spread, w_ref[...].reshape(heads * NOPE, LATENT), preferred_element_type=jnp.float32
     ).astype(jnp.bfloat16)
-    group = lax.axis_index("seq") // COPIES
+    piece = SPEC * heads
     for k in range(per_device):
-        which = first_out(group, k)
-        for a in range(per_device):
-
-            @pl.when(which == a)
-            def _():
-                outs[k][:, :LATENT] = absorbed[a * piece : (a + 1) * piece]
-                outs[k][:, LATENT:] = q[a * piece : (a + 1) * piece, NOPE:]
+        outs[k][:, :LATENT] = absorbed[k * piece : (k + 1) * piece]
+        outs[k][:, LATENT:] = packed[k][:, NOPE:]
 
 
 def block_scores(q, refs, starts, length):
@@ -125,19 +126,39 @@
     return jnp.sum(w, axis=1, keepdims=True), out
 
 
-def begin_kernel(turn, copies, per_device, len_ref, *refs):
+def begin_kernel(turn, per_device, heads, len_ref, *refs):
     owners = len(turn)
     q_refs, key_refs = refs[:per_device], refs[per_device : per_device + owners]
     q_out, top_ref, total_ref, out_ref = refs[per_device + owners :]
     seq_index = lax.axis_index("seq")
-    group, core = seq_index // copies, seq_index % copies
-    length = len_ref[lax.axis_index("head") * owners + group]
+    chip, core = seq_index // COPIES, seq_index % COPIES
+    length = len_ref[lax.axis_index("head") * owners + chip]
     slots = key_refs[0].shape[1]
-    q = jnp.concatenate([ref[...] for ref in q_refs], axis=0)
-    starts = [((group ^ k) * copies + core) * slots for k in turn]
+    width = LATENT + ROPE
+    q = jnp.concatenate([ref[:, :width] for ref in q_refs], axis=0)
+
+    fresh = q_refs[0][:, width:].astype(jnp.float32)
+    fresh = jnp.concatenate(
+        [fresh[n * SPEC : (n + 1) * SPEC] for n in range(width // ROPE)], axis=1
+    )
+    fresh = jnp.concatenate([fresh, jnp.zeros((16 - SPEC, width), jnp.float32)], axis=0)
+    fresh = fresh.astype(jnp.bfloat16)
+    f = lax.dot_general(
+        q, fresh, (((1,), (1,)), ((), ())), preferred_element_type=jnp.float32
+    )
+    row = lax.broadcasted_iota(jnp.int32, f.shape, 0) % (SPEC * heads)
+    key = lax.broadcasted_iota(jnp.int32, f.shape, 1)
+    f = jnp.where(key <= row // heads, f * SCORE_SCALE, masked_value)
+
+    starts = [((chip ^ k) * COPIES + core) * slots for k in turn]
     s = block_scores(q, key_refs, starts, length)
-    top = jnp.max(s, axis=1, keepdims=True)
+    top = jnp.maximum(jnp.max(s, axis=1, keepdims=True), jnp.max(f, axis=1, keepdims=True))
     total, out = weigh(s, key_refs, top)
+    w = jnp.exp(f - top)
+    total += jnp.sum(w, axis=1, keepdims=True)
+    out += jnp.dot(
+        w.astype(jnp.bfloat16), fresh[:, :LATENT], preferred_element_type=jnp.float32
+    )
     q_out[...] = q
     top_ref[...] = jnp.broadcast_to(top, top_ref.shape)
     total_ref[...] = jnp.broadcast_to(total, total_ref.shape)
@@ -145,70 +166,31 @@
 
 
 def finish_kernel(
-    turn, copies, per_device, heads, len_ref, q_ref, top_ref, total_ref, part_ref, *refs
+    turn, per_device, len_ref, q_ref, top_ref, total_ref, part_ref, pair_ref, *refs
 ):
     owners = len(turn)
-    own_refs, (pair_ref, *far_refs) = refs[:owners], refs[owners : 2 * owners - 1]
-    far_refs = [pair_ref.at[0], pair_ref.at[1]] + far_refs
-    outs, fresh_ref = refs[2 * owners - 1 : -1], refs[-1]
+    key_refs = [pair_ref.at[0], pair_ref.at[1], *refs[: owners - 2]]
+    outs = refs[owners - 2 :]
     seq_index = lax.axis_index("seq")
-    group, core = seq_index // copies, seq_index % copies
-    sequence = lax.axis_index("head") * owners + group
-    length = len_ref[sequence]
-    q = q_ref[...]
-    slots, width = own_refs[0].shape[1], q.shape[1]
-
-    home = sequence // per_device
-    for e in range(copies):
-        for k in range(owners):
-            source = (group ^ turn[k]) * copies + (core + copies - e) % copies
-
-            @pl.when(source == home)
-            def _():
-                fresh_ref[...] = (far_refs if e else own_refs)[k][width:, :]
-
-    parts = -(-width // slots)
-    rows = per_device * SPEC
-    fresh = fresh_ref[...].astype(jnp.float32)
-    fresh = jnp.concatenate([fresh[n * rows : (n + 1) * rows] for n in range(parts)], axis=1)
-    fresh = fresh[:, :width]
-    spare = -rows % 16
-    if spare:
-        fresh = jnp.concatenate([fresh, jnp.zeros((spare, width), jnp.float32)], axis=0)
-    fresh = fresh.astype(jnp.bfloat16)
-    f = lax.dot_general(
-        q, fresh, (((1,), (1,)), ((), ())), preferred_element_type=jnp.float32
-    )
-    row = lax.broadcasted_iota(jnp.int32, f.shape, 0) % (SPEC * heads)
-    key = lax.broadcasted_iota(jnp.int32, f.shape, 1)
-    causal = (key // SPEC == sequence % per_device) & (key % SPEC <= row // heads)
-    f = jnp.where(causal, f * SCORE_SCALE, masked_value)
-
-    starts = [
-        ((group ^ k) * copies + (core + copies - e) % copies) * slots
-        for e in range(1, copies)
-        for k in turn
-    ]
-    s = block_scores(q, far_refs, starts, length)
+    chip, core = seq_index // COPIES, seq_index % COPIES
+    plane = lax.axis_index("head")
+    length = len_ref[plane * owners + chip]
+    slots = key_refs[0].shape[1]
+    starts = [((chip ^ k) * COPIES + 1 - core) * slots for k in turn]
+    s = block_scores(q_ref[...], key_refs, starts, length)
     first = top_ref[:, :1]
-    top = jnp.maximum(
-        jnp.maximum(first, jnp.max(s, axis=1, keepdims=True)), jnp.max(f, axis=1, keepdims=True)
-    )
-    total, out = weigh(s, far_refs, top)
-    w = jnp.exp(f - top)
+    top = jnp.maximum(first, jnp.max(s, axis=1, keepdims=True))
+    total, out = weigh(s, key_refs, top)
     scale = jnp.exp(first - top)
-    total += jnp.sum(w, axis=1, keepdims=True) + total_ref[:, :1] * scale
+    total += total_ref[:, :1] * scale
     out += part_ref[...] * scale
-    out += jnp.dot(
-        w.astype(jnp.bfloat16), fresh[:, :LATENT], preferred_element_type=jnp.float32
-    )
     out = (out / total).astype(jnp.bfloat16)
-    piece = SPEC * heads
-    swapped = first_block(lax.axis_index("head"), group, core)
+    piece = out.shape[0] // per_device
+    sent_first = first_block(plane, chip, core)
     for k in range(per_device):
         for n in range(per_device):
 
-            @pl.when(swapped ^ k != n)
+            @pl.when(sent_first ^ k == n)
             def _():
                 outs[k][...] = out[n * piece : (n + 1) * piece]
 
@@ -217,7 +199,7 @@
     lat_refs, out_ref = refs[:-1], refs[-1]
     rows, heads, width = out_ref.shape
     first = first_back(lax.axis_index("seq") // COPIES, lax.axis_index("head"))
-    parts = [jnp.where(first == a, lat_refs[0][...], lat_refs[1][...]) for a in range(per_device)]
+    parts = [jnp.where(first == a, lat_refs[1][...], lat_refs[0][...]) for a in range(per_device)]
     latent = jnp.concatenate(parts, axis=0)
     out = jnp.zeros((rows * heads, width), jnp.float32)
     own_head = lax.broadcasted_iota(jnp.int32, out.shape, 0) % heads
@@ -231,13 +213,11 @@
 
 
 def whole_sequences(seq_size, head_size, queries, new_latent, cache, lengths, w_uk, w_uv):
-    rows, heads, _ = queries.shape
+    rows, heads, q_width = queries.shape
     owners, slots, width = cache.shape
-    copies = seq_size // owners
     per_device = rows // SPEC
     piece = SPEC * heads
     all_rows = per_device * piece
-    fresh_rows = -(-rows * -(-width // slots) // 16) * 16
     params = pltpu.CompilerParams(vmem_limit_bytes=VMEM_LIMIT)
     vmem = pl.BlockSpec(memory_space=pltpu.VMEM)
     smem = pl.BlockSpec(memory_space=pltpu.SMEM)
@@ -251,36 +231,46 @@
     def in_hbm(x):
         return pltpu.with_memory_space_constraint(x, pltpu.HBM)
 
-    def host(i, j):
-        other = (i // copies) ^ (2 - ((j ^ (j >> 1)) & 1))
-        return ((i % copies) * 2 + other // 2) * copies + other % 2
+    def host(i, j, a):
+        home, chip = i // COPIES, i % COPIES * per_device + a
+        core = home // 2 ^ chip // 2 ^ j // 2
+        exchanged = chip == home and home // 2 == j // 2
+        return flat((chip ^ exchanged) * COPIES + core, j)
 
     def owner(i, j, a):
-        sequence = i * per_device + a
-        core = (j // per_device) ^ 1
-        return flat((sequence % owners) * copies + core, sequence // owners)
-
-    moved = lax.ppermute(queries, both, [(flat(i, j), flat(host(i, j), j)) for i, j in devices])
+        plane, chip = i // COPIES, i % COPIES * per_device + a
+        return flat(chip * COPIES + owner_core(plane, chip, j), plane)
 
     turn = [0, 1, 3, 2]
 
     def in_plane(move):
-        return [(g * copies + t, move(g, t)) for g in range(owners) for t in range(copies)]
-
-    picked = pl.pallas_call(
-        functools.partial(pick_kernel, turn, copies),
-        out_shape=[jax.ShapeDtypeStruct((width + fresh_rows, slots), cache.dtype)] * owners,
-        in_specs=[anywhere] * 2,
-        out_specs=[vmem] * owners,
+        return [(g * COPIES + t, move(g, t)) for g in range(owners) for t in range(COPIES)]
+
+    made = pl.pallas_call(
+        functools.partial(pick_kernel, turn, per_device),
+        out_shape=[jax.ShapeDtypeStruct((width, slots), cache.dtype)] * owners
+        + [jax.ShapeDtypeStruct((piece, q_width + ROPE), queries.dtype)] * per_device,
+        in_specs=[anywhere] * 3,
+        out_specs=[vmem] * (owners + per_device),
         scratch_shapes=[
+            pltpu.VMEM(queries.shape, queries.dtype),
             pltpu.VMEM(new_latent.shape, new_latent.dtype),
-            pltpu.SemaphoreType.DMA((owners + 1,)),
+            pltpu.SemaphoreType.DMA((owners + 2,)),
         ],
         compiler_params=params,
         cost_estimate=LONG,
-    )(in_hbm(jnp.swapaxes(cache, 1, 2)), in_hbm(new_latent))
+    )(in_hbm(jnp.swapaxes(cache, 1, 2)), in_hbm(queries), in_hbm(new_latent))
+    picked, packed = made[:owners], made[owners:]
+    packed = [
+        lax.ppermute(
+            packed[k],
+            both,
+            [(flat(i, j), host(i, j, leaves_as(k, i // COPIES, j))) for i, j in devices],
+        )
+        for k in range(per_device)
+    ]
     own_keys = [picked[0]] + [
-        lax.ppermute(picked[k], "seq", in_plane(lambda g, t: (g ^ turn[k]) * copies + t))
+        lax.ppermute(picked[k], "seq", in_plane(lambda g, t: (g ^ turn[k]) * COPIES + t))
         for k in range(1, owners)
     ]
     pair = pl.pallas_call(
@@ -291,31 +281,32 @@
         scratch_shapes=[pltpu.SemaphoreType.DMA((2,))],
         compiler_params=params,
     )(*own_keys[:2])
-    other_core = in_plane(lambda g, t: g * copies + (t + 1) % copies)
+    other_core = in_plane(lambda g, t: g * COPIES + 1 - t)
     far_keys = [lax.ppermute(keys, "seq", other_core) for keys in [pair] + own_keys[2:]]
 
     pieces = pl.pallas_call(
         functools.partial(absorb_kernel, per_device),
-        out_shape=[jax.ShapeDtypeStruct((piece, width), cache.dtype)] * per_device,
-        in_specs=[vmem] * 2,
+        out_shape=[jax.ShapeDtypeStruct((piece, width + ROPE), cache.dtype)] * per_device,
+        in_specs=[vmem] * (1 + per_device),
         out_specs=[vmem] * per_device,
         compiler_params=params,
         cost_estimate=LONG,
-    )(moved, w_uk)
+    )(w_uk, *packed)
     arrived = [
         lax.ppermute(
             pieces[k],
             both,
             [
-                (flat(host(i, j), j), owner(i, j, first_out(host(i, j) // copies, k)))
+                (host(i, j, a), owner(i, j, a))
                 for i, j in devices
+                for a in [leaves_as(k, i // COPIES, j)]
             ],
         )
         for k in range(per_device)
     ]
 
     state = pl.pallas_call(
-        functools.partial(begin_kernel, turn, copies, per_device),
+        functools.partial(begin_kernel, turn, per_device, heads),
         out_shape=[
             jax.ShapeDtypeStruct((all_rows, width), jnp.bfloat16),
             jax.ShapeDtypeStruct((all_rows, 128), jnp.float32),
@@ -328,19 +319,18 @@
         cost_estimate=LONG,
     )(lengths, *arrived, *own_keys)
     latent = pl.pallas_call(
-        functools.partial(finish_kernel, turn, copies, per_device, heads),
+        functools.partial(finish_kernel, turn, per_device),
         out_shape=[jax.ShapeDtypeStruct((piece, LATENT), jnp.bfloat16)] * per_device,
-        in_specs=[smem] + [vmem] * (len(state) + len(own_keys) + len(far_keys)),
+        in_specs=[smem] + [vmem] * (len(state) + len(far_keys)),
         out_specs=[vmem] * per_device,
-        scratch_shapes=[pltpu.VMEM((fresh_rows, slots), jnp.bfloat16)],
-        compiler_params=params,
-    )(lengths, *state, *own_keys, *far_keys)
+        compiler_params=params,
+    )(lengths, *state, *far_keys)
 
     back = [
         lax.ppermute(
             latent[k],
             both,
-            [(owner(i, j, first_back(i // copies, j) ^ k ^ 1), flat(i, j)) for i, j in devices],
+            [(owner(i, j, first_back(i // COPIES, j) ^ k), flat(i, j)) for i, j in devices],
         )
         for k in range(per_device)
     ]

time: 28.5 us -> 27.8 us (0.975)
  waiting for transfers between devices: 11.9 us -> 10.4 us
  starting transfers between devices: 10.6 us -> 11.2 us
    ppermute x8 -> x9, waiting for transfers between devices: 11.9 us -> 10.4 us  [the longest x2 7.14 us: whole_sequences(): lax.ppermute(latent[k], both, [(owner(i, j, first_back(i // COPIES, j) ^...]
    ppermute x8 -> x9, starting transfers between devices: 9.98 us -> 11.1 us  [the longest x3 3.49 us: whole_sequences(): lax.ppermute(picked[k], 'seq', in_plane(lambda g, t: (g ^ turn[k]) * COPI...]
    ppermute x3, starting transfers between devices: 0.61 us -> 0.08 us  [whole_sequences(): lax.ppermute(keys, 'seq', other_core)]
  transfers between devices with their start and end apart: 11 -> 12, of which waited for: 6 -> 4; matrix products, arithmetic and copies ran while one was open for 0% -> 0% of each run, Pallas kernels for 12% -> 8%
where the time goes in v10:
time: 27.8 us; the launch traced here: 27.5 us
  starting transfers between devices  11.2 us (40%)
  waiting for transfers between devices  10.4 us (37%)
  Pallas kernels  5.81 us (21%)
    ppermute x2, waiting for transfers between devices, whole_sequences(): lax.ppermute(latent[k], both, [(owner(i, j, first_back(i // COPIES, j) ^...  7.14 us
    ppermute x3, starting transfers between devices, whole_sequences(): lax.ppermute(picked[k], 'seq', in_plane(lambda g, t: (g ^ turn[k]) * COPI...  3.49 us
    ppermute x2, starting transfers between devices, whole_sequences(): lax.ppermute(pieces[k], both, [(host(i, j, a), owner(i, j, a)) for i, j i...  3.25 us
    ppermute x3, waiting for transfers between devices, whole_sequences(): lax.ppermute(picked[k], 'seq', in_plane(lambda g, t: (g ^ turn[k]) * COPI...  3.21 us
    ppermute x2, starting transfers between devices, whole_sequences(): lax.ppermute(latent[k], both, [(owner(i, j, first_back(i // COPIES, j) ^...  3.13 us
    pallas_call x1, Pallas kernels, whole_sequences(): pl.pallas_call(functools.partial(pick_kernel, turn, per_device), out_shap...  1.37 us
    pallas_call x1, Pallas kernels, whole_sequences(): pl.pallas_call(functools.partial(begin_kernel, turn, per_device, heads),...  1.3 us
    pallas_call x1, Pallas kernels, whole_sequences(): pl.pallas_call(functools.partial(finish_kernel, turn, per_device), out_sh...  1.25 us
  transfers between devices with their start and end apart: 12, of which 4 were waited for; matrix products, arithmetic and copies ran while one was open for 0% of the time, Pallas kernels for 8%

profile of v10, /device:TPU:6, one launch (start us, length us, event | category | flops | bytes accessed | tf_op | source)
XLA Modules:
  0.0 27.5 jit_solution(10035670240055045726)
XLA Ops:
  0.0 1.4 %shard_map.64 = (bf16[576,128]{1,0:T(8,128)(2,1)S(1)}, bf16[576,128]{1,0:T(8,128)(2,1)S(1)}, bf16[576,128]{1,0:T(8,128)(2,1)S(1)}, bf16[576,128]{1,0:T(8,128)(2,...) custom-call(bf16[4,576,128]{2,1,0:T(8,128)(2,1)} %bitcast.1, bf16[8,16,192]{2,1,0:T(8,128)(2,1)} %q_hbm.1, ...), custom_call_target="tpu_custom_call" | custom-call | flops 20000000000 | tf_op jit(solution)/shard_map/pallas_call | solution.py:249
  1.4 0.1 collective-permute-start
  1.4 1.1 %collective-permute-start.1 = (bf16[64,256]{1,0:T(8,128)(2,1)S(1)}, bf16[64,256]{1,0:T(8,128)(2,1)S(1)}, u32[]{:S(2)}, u32[]{:S(2)}) collective-permute-start(bf16[64,256]{1,0:T(8,128)(2,1)S(1)} %get-tuple-element.20), channel_id=1, source_target_pairs={{0,8},{1,9},{2,14},{3,7},{4,28},{5,21},{6,26},{7,19},{8,0},{9,1},{... | collective-permute-start | bytes 98312 | tf_op jit(solution)/shard_map/ppermute | solution.py:265
  2.6 1.5 %collective-permute-start.4 = (bf16[576,128]{1,0:T(8,128)(2,1)S(1)}, bf16[576,128]{1,0:T(8,128)(2,1)S(1)}, u32[]{:S(2)}, u32[]{:S(2)}) collective-permute-start(bf16[576,128]{1,0:T(8,128)(2,1)S(1)} %get-tuple-element.24), channel_id=1, source_target_pairs={{0,8},{4,12},{8,0},{12,4},{16,24},{20,28},{24,16},{28,20},{1,9},{5... | collective-permute-start | bytes 442376 | tf_op jit(solution)/shard_map/ppermute | solution.py:273
  4.1 1.3 %collective-permute-start.5 = (bf16[576,128]{1,0:T(8,128)(2,1)S(1)}, bf16[576,128]{1,0:T(8,128)(2,1)S(1)}, u32[]{:S(2)}, u32[]{:S(2)}) collective-permute-start(bf16[576,128]{1,0:T(8,128)(2,1)S(1)} %get-tuple-element.25), channel_id=1, source_target_pairs={{0,24},{4,28},{8,16},{12,20},{16,8},{20,12},{24,0},{28,4},{1,25},{... | collective-permute-start | bytes 442376 | tf_op jit(solution)/shard_map/ppermute | solution.py:273
  5.4 0.7 %collective-permute-start.6 = (bf16[576,128]{1,0:T(8,128)(2,1)S(1)}, bf16[576,128]{1,0:T(8,128)(2,1)S(1)}, u32[]{:S(2)}, u32[]{:S(2)}) collective-permute-start(bf16[576,128]{1,0:T(8,128)(2,1)S(1)} %get-tuple-element.26), channel_id=1, source_target_pairs={{0,16},{4,20},{8,24},{12,28},{16,0},{20,4},{24,8},{28,12},{1,17},{... | collective-permute-start | bytes 442376 | tf_op jit(solution)/shard_map/ppermute | solution.py:273
  6.1 0.0 collective-permute-done.refs_0_
  6.1 0.4 %shard_map.65 = (bf16[64,640]{1,0:T(8,128)(2,1)S(1)}, bf16[64,640]{1,0:T(8,128)(2,1)S(1)}) custom-call(bf16[16,128,512]{2,1,0:T(8,128)(2,1)S(1)} %copy-done.2, bf16[64,256]{1,0:T(8,128)(2,1)S(1)} %collective-permute-done.refs_0_, bf16[64,256]{1,0:T(8,128)(2,1)S(1)} %collective-permute-done.1.refs_1_), custom_call_target="tpu_custom_call" | custom-call | flops 20000000000 | tf_op jit(solution)/shard_map/pallas_call | solution.py:287
  6.5 2.6 %collective-permute-start.2 = (bf16[64,640]{1,0:T(8,128)(2,1)S(1)}, bf16[64,640]{1,0:T(8,128)(2,1)S(1)}, u32[]{:S(2)}, u32[]{:S(2)}) collective-permute-start(bf16[64,640]{1,0:T(8,128)(2,1)S(1)} %get-tuple-element.21), channel_id=1, source_target_pairs={{8,4},{9,12},{6,0},{15,8},{20,16},{29,24},{18,20},{27,28},{0,13},{... | collective-permute-start | bytes 245768 | tf_op jit(solution)/shard_map/ppermute | solution.py:296
  9.1 0.7 %collective-permute-start.3 = (bf16[64,640]{1,0:T(8,128)(2,1)S(1)}, bf16[64,640]{1,0:T(8,128)(2,1)S(1)}, u32[]{:S(2)}, u32[]{:S(2)}) collective-permute-start(bf16[64,640]{1,0:T(8,128)(2,1)S(1)} %get-tuple-element.22), channel_id=1, source_target_pairs={{8,12},{9,4},{14,8},{7,0},{28,24},{21,16},{26,28},{19,20},{0,5},{1... | collective-permute-start | bytes 245768 | tf_op jit(solution)/shard_map/ppermute | solution.py:296
  9.8 0.4 %shard_map.67 = bf16[2,576,128]{2,1,0:T(8,128)(2,1)S(1)} custom-call(bf16[576,128]{1,0:T(8,128)(2,1)S(1)} %get-tuple-element.23.refs_2_.first_ref, bf16[576,128]{1,0:T(8,128)(2,1)S(1)} %collective-permute-done.4.refs_3_.second_ref), custom_call_target="tpu_custom_call" | custom-call | tf_op jit(solution)/shard_map/pallas_call | solution.py:276
  10.2 0.1 collective-permute-start.7
  10.3 2.2 %collective-permute-done.5.refs_4_ = bf16[576,128]{1,0:T(8,128)(2,1)S(1)} collective-permute-done((bf16[576,128]{1,0:T(8,128)(2,1)S(1)}, bf16[576,128]{1,0:T(8,128)(2,1)S(1)}, u32[]{:S(2)}, u32[]{:S(2)}) %collective-permute-start.5) | collective-permute-done | bytes 147488 | tf_op jit(solution)/shard_map/ppermute | solution.py:273
  12.4 1.1 %collective-permute-done.6.refs_5_ = bf16[576,128]{1,0:T(8,128)(2,1)S(1)} collective-permute-done((bf16[576,128]{1,0:T(8,128)(2,1)S(1)}, bf16[576,128]{1,0:T(8,128)(2,1)S(1)}, u32[]{:S(2)}, u32[]{:S(2)}) %collective-permute-start.6) | collective-permute-done | bytes 147488 | tf_op jit(solution)/shard_map/ppermute | solution.py:273
  13.5 0.0 collective-permute-done.3.refs_1_
  13.5 0.0 copy-start
  13.5 1.3 %shard_map.66 = (bf16[128,576]{1,0:T(8,128)(2,1)S(1)}, f32[128,128]{1,0:T(8,128)S(1)}, f32[128,128]{1,0:T(8,128)S(1)}, f32[128,512]{1,0:T(8,128)S(1)}) custom-call(s32[16]{0:T(128)S(1)} %copy-done.1, bf16[64,640]{1,0:T(8,128)(2,1)S(1)} %collective-permute-done.2.refs_0_, bf16[64,640]{1,0:T(8,128)(2,1)S(1)} %collective-permute-done.3.refs_1_, ...), custom_call_target="tpu_custom_call" | custom-call | flops 20000000000 | tf_op jit(solution)/shard_map/pallas_call | solution.py:308
  14.8 0.0 collective-permute-done.9.refs_1_
  14.9 1.3 %shard_map.68 = (bf16[64,512]{1,0:T(8,128)(2,1)S(1)}, bf16[64,512]{1,0:T(8,128)(2,1)S(1)}) custom-call(s32[16]{0:T(128)S(1)} %copy-done.1, bf16[128,576]{1,0:T(8,128)(2,1)S(1)} %get-tuple-element.27.q_ref, f32[128,128]{1,0:T(8,128)S(1)} %get-tuple-element.28.top_ref, f32[128,128]{1,0:T(8,128)S(1)} %get-tuple-element.29.total_ref, ...), custom_call_target="tpu_custom_call" | custom-call | tf_op jit(solution)/shard_map/pallas_call | solution.py:321
  16.1 2.4 %collective-permute-start.10 = (bf16[64,512]{1,0:T(8,128)(2,1)S(1)}, bf16[64,512]{1,0:T(8,128)(2,1)S(1)}, u32[]{:S(2)}, u32[]{:S(2)}) collective-permute-start(bf16[64,512]{1,0:T(8,128)(2,1)S(1)} %get-tuple-element.31), channel_id=1, source_target_pairs={{12,0},{4,1},{8,2},{0,3},{24,4},{16,5},{28,6},{20,7},{13,8},{5,9},... | collective-permute-start | bytes 196616 | tf_op jit(solution)/shard_map/ppermute | solution.py:330
  18.5 0.8 %collective-permute-start.11 = (bf16[64,512]{1,0:T(8,128)(2,1)S(1)}, bf16[64,512]{1,0:T(8,128)(2,1)S(1)}, u32[]{:S(2)}, u32[]{:S(2)}) collective-permute-start(bf16[64,512]{1,0:T(8,128)(2,1)S(1)} %get-tuple-element.32), channel_id=1, source_target_pairs={{4,0},{12,1},{0,2},{8,3},{16,4},{24,5},{20,6},{28,7},{5,8},{13,9},... | collective-permute-start | bytes 196616 | tf_op jit(solution)/shard_map/ppermute | solution.py:330
  19.3 4.5 %collective-permute-done.10.refs_0_ = bf16[64,512]{1,0:T(8,128)(2,1)S(1)} collective-permute-done((bf16[64,512]{1,0:T(8,128)(2,1)S(1)}, bf16[64,512]{1,0:T(8,128)(2,1)S(1)}, u32[]{:S(2)}, u32[]{:S(2)}) %collective-permute-start.10) | collective-permute-done | bytes 65568 | tf_op jit(solution)/shard_map/ppermute | solution.py:330
  23.8 2.6 %collective-permute-done.11.refs_1_ = bf16[64,512]{1,0:T(8,128)(2,1)S(1)} collective-permute-done((bf16[64,512]{1,0:T(8,128)(2,1)S(1)}, bf16[64,512]{1,0:T(8,128)(2,1)S(1)}, u32[]{:S(2)}, u32[]{:S(2)}) %collective-permute-start.11) | collective-permute-done | bytes 65568 | tf_op jit(solution)/shard_map/ppermute | solution.py:330
  26.4 1.1 %shard_map.69 = bf16[8,16,128]{2,1,0:T(8,128)(2,1)} custom-call(bf16[16,512,128]{2,1,0:T(8,128)(2,1)S(1)} %copy-done, bf16[64,512]{1,0:T(8,128)(2,1)S(1)} %collective-permute-done.10.refs_0_, bf16[64,512]{1,0:T(8,128)(2,1)S(1)} %collective-permute-done.11.refs_1_), custom_call_target="tpu_custom_call" | custom-call | tf_op jit(solution)/shard_map/pallas_call | solution.py:337
  (12 shorter events, 0.0 us)
Async XLA Ops:
  0.0 6.1 %copy-start.2 = (bf16[16,128,512]{2,1,0:T(8,128)(2,1)S(1)}, bf16[16,128,512]{2,1,0:T(8,128)(2,1)}, u32[]{:S(2)}) copy-start(bf16[16,128,512]{2,1,0:T(8,128)(2,1)} %w_ref.2) | copy-start | bytes 6291460
  1.4 4.7 %collective-permute-start = (bf16[64,256]{1,0:T(8,128)(2,1)S(1)}, bf16[64,256]{1,0:T(8,128)(2,1)S(1)}, u32[]{:S(2)}, u32[]{:S(2)}) collective-permute-start(bf16[64,256]{1,0:T(8,128)(2,1)S(1)} %get-tuple-element.19), channel_id=1, source_target_pairs={{0,8},{1,9},{2,6},{3,15},{4,20},{5,29},{6,18},{7,27},{8,0},{9,1},{... | collective-permute-start | bytes 98312 | tf_op jit(solution)/shard_map/ppermute | solution.py:265
  1.4 4.6 %collective-permute-start.1 = (bf16[64,256]{1,0:T(8,128)(2,1)S(1)}, bf16[64,256]{1,0:T(8,128)(2,1)S(1)}, u32[]{:S(2)}, u32[]{:S(2)}) collective-permute-start(bf16[64,256]{1,0:T(8,128)(2,1)S(1)} %get-tuple-element.20), channel_id=1, source_target_pairs={{0,8},{1,9},{2,14},{3,7},{4,28},{5,21},{6,26},{7,19},{8,0},{9,1},{... | collective-permute-start | bytes 98312 | tf_op jit(solution)/shard_map/ppermute | solution.py:265
  2.6 7.2 %collective-permute-start.4 = (bf16[576,128]{1,0:T(8,128)(2,1)S(1)}, bf16[576,128]{1,0:T(8,128)(2,1)S(1)}, u32[]{:S(2)}, u32[]{:S(2)}) collective-permute-start(bf16[576,128]{1,0:T(8,128)(2,1)S(1)} %get-tuple-element.24), channel_id=1, source_target_pairs={{0,8},{4,12},{8,0},{12,4},{16,24},{20,28},{24,16},{28,20},{1,9},{5... | collective-permute-start | bytes 442376 | tf_op jit(solution)/shard_map/ppermute | solution.py:273
  4.1 8.3 %collective-permute-start.5 = (bf16[576,128]{1,0:T(8,128)(2,1)S(1)}, bf16[576,128]{1,0:T(8,128)(2,1)S(1)}, u32[]{:S(2)}, u32[]{:S(2)}) collective-permute-start(bf16[576,128]{1,0:T(8,128)(2,1)S(1)} %get-tuple-element.25), channel_id=1, source_target_pairs={{0,24},{4,28},{8,16},{12,20},{16,8},{20,12},{24,0},{28,4},{1,25},{... | collective-permute-start | bytes 442376 | tf_op jit(solution)/shard_map/ppermute | solution.py:273
  5.4 8.1 %copy-start.1 = (s32[16]{0:T(128)S(1)}, s32[16]{0:T(128)}, u32[]{:S(2)}) copy-start(s32[16]{0:T(128)} %len_ref.3) | copy-start | bytes 196
  5.4 8.0 %collective-permute-start.6 = (bf16[576,128]{1,0:T(8,128)(2,1)S(1)}, bf16[576,128]{1,0:T(8,128)(2,1)S(1)}, u32[]{:S(2)}, u32[]{:S(2)}) collective-permute-start(bf16[576,128]{1,0:T(8,128)(2,1)S(1)} %get-tuple-element.26), channel_id=1, source_target_pairs={{0,16},{4,20},{8,24},{12,28},{16,0},{20,4},{24,8},{28,12},{1,17},{... | collective-permute-start | bytes 442376 | tf_op jit(solution)/shard_map/ppermute | solution.py:273
  6.5 6.9 %collective-permute-start.2 = (bf16[64,640]{1,0:T(8,128)(2,1)S(1)}, bf16[64,640]{1,0:T(8,128)(2,1)S(1)}, u32[]{:S(2)}, u32[]{:S(2)}) collective-permute-start(bf16[64,640]{1,0:T(8,128)(2,1)S(1)} %get-tuple-element.21), channel_id=1, source_target_pairs={{8,4},{9,12},{6,0},{15,8},{20,16},{29,24},{18,20},{27,28},{0,13},{... | collective-permute-start | bytes 245768 | tf_op jit(solution)/shard_map/ppermute | solution.py:296
  9.1 4.4 %collective-permute-start.3 = (bf16[64,640]{1,0:T(8,128)(2,1)S(1)}, bf16[64,640]{1,0:T(8,128)(2,1)S(1)}, u32[]{:S(2)}, u32[]{:S(2)}) collective-permute-start(bf16[64,640]{1,0:T(8,128)(2,1)S(1)} %get-tuple-element.22), channel_id=1, source_target_pairs={{8,12},{9,4},{14,8},{7,0},{28,24},{21,16},{26,28},{19,20},{0,5},{1... | collective-permute-start | bytes 245768 | tf_op jit(solution)/shard_map/ppermute | solution.py:296
  10.2 4.7 %collective-permute-start.7 = (bf16[2,576,128]{2,1,0:T(8,128)(2,1)S(1)}, bf16[2,576,128]{2,1,0:T(8,128)(2,1)S(1)}, u32[]{:S(2)}, u32[]{:S(2)}) collective-permute-start(bf16[2,576,128]{2,1,0:T(8,128)(2,1)S(1)} %shard_map.67), channel_id=1, source_target_pairs={{0,4},{4,0},{8,12},{12,8},{16,20},{20,16},{24,28},{28,24},{1,5},{5... | collective-permute-start | bytes 884744 | tf_op jit(solution)/shard_map/ppermute | solution.py:285
  12.4 2.4 %collective-permute-start.8 = (bf16[576,128]{1,0:T(8,128)(2,1)S(1)}, bf16[576,128]{1,0:T(8,128)(2,1)S(1)}, u32[]{:S(2)}, u32[]{:S(2)}) collective-permute-start(bf16[576,128]{1,0:T(8,128)(2,1)S(1)} %collective-permute-done.5.refs_4_), channel_id=1, source_target_pairs={{0,4},{4,0},{8,12},{12,8},{16,20},{20,16},{24,28},{28,24},{1,5},{5... | collective-permute-start | bytes 442376 | tf_op jit(solution)/shard_map/ppermute | solution.py:285
  13.5 1.4 %collective-permute-start.9 = (bf16[576,128]{1,0:T(8,128)(2,1)S(1)}, bf16[576,128]{1,0:T(8,128)(2,1)S(1)}, u32[]{:S(2)}, u32[]{:S(2)}) collective-permute-start(bf16[576,128]{1,0:T(8,128)(2,1)S(1)} %collective-permute-done.6.refs_5_), channel_id=1, source_target_pairs={{0,4},{4,0},{8,12},{12,8},{16,20},{20,16},{24,28},{28,24},{1,5},{5... | collective-permute-start | bytes 442376 | tf_op jit(solution)/shard_map/ppermute | solution.py:285
  13.5 12.9 %copy-start = (bf16[16,512,128]{2,1,0:T(8,128)(2,1)S(1)}, bf16[16,512,128]{2,1,0:T(8,128)(2,1)}, u32[]{:S(2)}) copy-start(bf16[16,512,128]{2,1,0:T(8,128)(2,1)} %w_ref.3) | copy-start | bytes 6291460
  16.1 7.7 %collective-permute-start.10 = (bf16[64,512]{1,0:T(8,128)(2,1)S(1)}, bf16[64,512]{1,0:T(8,128)(2,1)S(1)}, u32[]{:S(2)}, u32[]{:S(2)}) collective-permute-start(bf16[64,512]{1,0:T(8,128)(2,1)S(1)} %get-tuple-element.31), channel_id=1, source_target_pairs={{12,0},{4,1},{8,2},{0,3},{24,4},{16,5},{28,6},{20,7},{13,8},{5,9},... | collective-permute-start | bytes 196616 | tf_op jit(solution)/shard_map/ppermute | solution.py:330
  18.5 7.9 %collective-permute-start.11 = (bf16[64,512]{1,0:T(8,128)(2,1)S(1)}, bf16[64,512]{1,0:T(8,128)(2,1)S(1)}, u32[]{:S(2)}, u32[]{:S(2)}) collective-permute-start(bf16[64,512]{1,0:T(8,128)(2,1)S(1)} %get-tuple-element.32), channel_id=1, source_target_pairs={{4,0},{12,1},{0,2},{8,3},{16,4},{24,5},{20,6},{28,7},{5,8},{13,9},... | collective-permute-start | bytes 196616 | tf_op jit(solution)/shard_map/ppermute | solution.py:330

commit v11 on v10

--- a/solution.py
+++ b/solution.py
@@ -241,7 +241,7 @@
         plane, chip = i // COPIES, i % COPIES * per_device + a
         return flat(chip * COPIES + owner_core(plane, chip, j), plane)
 
-    turn = [0, 1, 3, 2]
+    turn = [0, 3, 1, 2]
 
     def in_plane(move):
         return [(g * COPIES + t, move(g, t)) for g in range(owners) for t in range(COPIES)]

time: 27.8 us -> 27.7 us (level)
  starting transfers between devices: 11.2 us -> 12.3 us
  waiting for transfers between devices: 10.4 us -> 9.3 us
    ppermute x3, waiting for transfers between devices: 3.21 us -> 2.08 us  [whole_sequences(): lax.ppermute(picked[k], 'seq', in_plane(lambda g, t: (g ^ turn[k]) * COPI...]
    ppermute x2, starting transfers between devices: 3.13 us -> 3.76 us  [whole_sequences(): lax.ppermute(latent[k], both, [(owner(i, j, first_back(i // COPIES, j) ^...]
    ppermute x3, starting transfers between devices: 0.08 us -> 0.58 us  [whole_sequences(): lax.ppermute(keys, 'seq', other_core)]
where the time goes in v11:
time: 27.7 us; the launch traced here: 27.5 us
  starting transfers between devices  12.3 us (44%)
  waiting for transfers between devices  9.3 us (34%)
  Pallas kernels  5.82 us (21%)
    ppermute x2, waiting for transfers between devices, whole_sequences(): lax.ppermute(latent[k], both, [(owner(i, j, first_back(i // COPIES, j) ^...  7.2 us
    ppermute x2, starting transfers between devices, whole_sequences(): lax.ppermute(latent[k], both, [(owner(i, j, first_back(i // COPIES, j) ^...  3.76 us
    ppermute x3, starting transfers between devices, whole_sequences(): lax.ppermute(picked[k], 'seq', in_plane(lambda g, t: (g ^ turn[k]) * COPI...  3.49 us
    ppermute x2, starting transfers between devices, whole_sequences(): lax.ppermute(pieces[k], both, [(host(i, j, a), owner(i, j, a)) for i, j i...  3.25 us
    ppermute x3, waiting for transfers between devices, whole_sequences(): lax.ppermute(picked[k], 'seq', in_plane(lambda g, t: (g ^ turn[k]) * COPI...  2.08 us
    pallas_call x1, Pallas kernels, whole_sequences(): pl.pallas_call(functools.partial(pick_kernel, turn, per_device), out_shap...  1.37 us
    pallas_call x1, Pallas kernels, whole_sequences(): pl.pallas_call(functools.partial(begin_kernel, turn, per_device, heads),...  1.3 us
    pallas_call x1, Pallas kernels, whole_sequences(): pl.pallas_call(functools.partial(finish_kernel, turn, per_device), out_sh...  1.26 us
  transfers between devices with their start and end apart: 12, of which 4 were waited for; matrix products, arithmetic and copies ran while one was open for 0% of the time, Pallas kernels for 8%

profile of v11, /device:TPU:6, one launch (start us, length us, event | category | flops | bytes accessed | tf_op | source)
XLA Modules:
  0.0 27.5 jit_solution(9246238395148571195)
XLA Ops:
  0.0 1.4 %shard_map.64 = (bf16[576,128]{1,0:T(8,128)(2,1)S(1)}, bf16[576,128]{1,0:T(8,128)(2,1)S(1)}, bf16[576,128]{1,0:T(8,128)(2,1)S(1)}, bf16[576,128]{1,0:T(8,128)(2,...) custom-call(bf16[4,576,128]{2,1,0:T(8,128)(2,1)} %bitcast.1, bf16[8,16,192]{2,1,0:T(8,128)(2,1)} %q_hbm.1, ...), custom_call_target="tpu_custom_call" | custom-call | flops 20000000000 | tf_op jit(solution)/shard_map/pallas_call | solution.py:249
  1.4 0.1 collective-permute-start
  1.4 1.1 %collective-permute-start.1 = (bf16[64,256]{1,0:T(8,128)(2,1)S(1)}, bf16[64,256]{1,0:T(8,128)(2,1)S(1)}, u32[]{:S(2)}, u32[]{:S(2)}) collective-permute-start(bf16[64,256]{1,0:T(8,128)(2,1)S(1)} %get-tuple-element.20), channel_id=1, source_target_pairs={{0,8},{1,9},{2,14},{3,7},{4,28},{5,21},{6,26},{7,19},{8,0},{9,1},{... | collective-permute-start | bytes 98312 | tf_op jit(solution)/shard_map/ppermute | solution.py:265
  2.6 0.9 %collective-permute-start.4 = (bf16[576,128]{1,0:T(8,128)(2,1)S(1)}, bf16[576,128]{1,0:T(8,128)(2,1)S(1)}, u32[]{:S(2)}, u32[]{:S(2)}) collective-permute-start(bf16[576,128]{1,0:T(8,128)(2,1)S(1)} %get-tuple-element.24), channel_id=1, source_target_pairs={{0,24},{4,28},{8,16},{12,20},{16,8},{20,12},{24,0},{28,4},{1,25},{... | collective-permute-start | bytes 442376 | tf_op jit(solution)/shard_map/ppermute | solution.py:273
  3.5 2.0 %collective-permute-start.5 = (bf16[576,128]{1,0:T(8,128)(2,1)S(1)}, bf16[576,128]{1,0:T(8,128)(2,1)S(1)}, u32[]{:S(2)}, u32[]{:S(2)}) collective-permute-start(bf16[576,128]{1,0:T(8,128)(2,1)S(1)} %get-tuple-element.25), channel_id=1, source_target_pairs={{0,8},{4,12},{8,0},{12,4},{16,24},{20,28},{24,16},{28,20},{1,9},{5... | collective-permute-start | bytes 442376 | tf_op jit(solution)/shard_map/ppermute | solution.py:273
  5.4 0.7 %collective-permute-start.6 = (bf16[576,128]{1,0:T(8,128)(2,1)S(1)}, bf16[576,128]{1,0:T(8,128)(2,1)S(1)}, u32[]{:S(2)}, u32[]{:S(2)}) collective-permute-start(bf16[576,128]{1,0:T(8,128)(2,1)S(1)} %get-tuple-element.26), channel_id=1, source_target_pairs={{0,16},{4,20},{8,24},{12,28},{16,0},{20,4},{24,8},{28,12},{1,17},{... | collective-permute-start | bytes 442376 | tf_op jit(solution)/shard_map/ppermute | solution.py:273
  6.1 0.4 %shard_map.65 = (bf16[64,640]{1,0:T(8,128)(2,1)S(1)}, bf16[64,640]{1,0:T(8,128)(2,1)S(1)}) custom-call(bf16[16,128,512]{2,1,0:T(8,128)(2,1)S(1)} %copy-done.2, bf16[64,256]{1,0:T(8,128)(2,1)S(1)} %collective-permute-done.refs_0_, bf16[64,256]{1,0:T(8,128)(2,1)S(1)} %collective-permute-done.1.refs_1_), custom_call_target="tpu_custom_call" | custom-call | flops 20000000000 | tf_op jit(solution)/shard_map/pallas_call | solution.py:287
  6.6 2.6 %collective-permute-start.2 = (bf16[64,640]{1,0:T(8,128)(2,1)S(1)}, bf16[64,640]{1,0:T(8,128)(2,1)S(1)}, u32[]{:S(2)}, u32[]{:S(2)}) collective-permute-start(bf16[64,640]{1,0:T(8,128)(2,1)S(1)} %get-tuple-element.21), channel_id=1, source_target_pairs={{8,4},{9,12},{6,0},{15,8},{20,16},{29,24},{18,20},{27,28},{0,13},{... | collective-permute-start | bytes 245768 | tf_op jit(solution)/shard_map/ppermute | solution.py:296
  9.1 0.7 %collective-permute-start.3 = (bf16[64,640]{1,0:T(8,128)(2,1)S(1)}, bf16[64,640]{1,0:T(8,128)(2,1)S(1)}, u32[]{:S(2)}, u32[]{:S(2)}) collective-permute-start(bf16[64,640]{1,0:T(8,128)(2,1)S(1)} %get-tuple-element.22), channel_id=1, source_target_pairs={{8,12},{9,4},{14,8},{7,0},{28,24},{21,16},{26,28},{19,20},{0,5},{1... | collective-permute-start | bytes 245768 | tf_op jit(solution)/shard_map/ppermute | solution.py:296
  9.8 0.5 %collective-permute-done.4.refs_3_.second_ref = bf16[576,128]{1,0:T(8,128)(2,1)S(1)} collective-permute-done((bf16[576,128]{1,0:T(8,128)(2,1)S(1)}, bf16[576,128]{1,0:T(8,128)(2,1)S(1)}, u32[]{:S(2)}, u32[]{:S(2)}) %collective-permute-start.4) | collective-permute-done | bytes 147488 | tf_op jit(solution)/shard_map/ppermute | solution.py:273
  10.3 0.4 %shard_map.67 = bf16[2,576,128]{2,1,0:T(8,128)(2,1)S(1)} custom-call(bf16[576,128]{1,0:T(8,128)(2,1)S(1)} %get-tuple-element.23.refs_2_.first_ref, bf16[576,128]{1,0:T(8,128)(2,1)S(1)} %collective-permute-done.4.refs_3_.second_ref), custom_call_target="tpu_custom_call" | custom-call | tf_op jit(solution)/shard_map/pallas_call | solution.py:276
  10.7 0.1 collective-permute-start.7
  10.7 1.6 %collective-permute-done.5.refs_4_ = bf16[576,128]{1,0:T(8,128)(2,1)S(1)} collective-permute-done((bf16[576,128]{1,0:T(8,128)(2,1)S(1)}, bf16[576,128]{1,0:T(8,128)(2,1)S(1)}, u32[]{:S(2)}, u32[]{:S(2)}) %collective-permute-start.5) | collective-permute-done | bytes 147488 | tf_op jit(solution)/shard_map/ppermute | solution.py:273
  12.3 0.0 collective-permute-start.8
  12.3 0.0 collective-permute-done.6.refs_5_
  12.3 0.5 %collective-permute-start.9 = (bf16[576,128]{1,0:T(8,128)(2,1)S(1)}, bf16[576,128]{1,0:T(8,128)(2,1)S(1)}, u32[]{:S(2)}, u32[]{:S(2)}) collective-permute-start(bf16[576,128]{1,0:T(8,128)(2,1)S(1)} %collective-permute-done.6.refs_5_), channel_id=1, source_target_pairs={{0,4},{4,0},{8,12},{12,8},{16,20},{20,16},{24,28},{28,24},{1,5},{5... | collective-permute-start | bytes 442376 | tf_op jit(solution)/shard_map/ppermute | solution.py:285
  12.9 0.0 copy-start
  12.9 1.3 %shard_map.66 = (bf16[128,576]{1,0:T(8,128)(2,1)S(1)}, f32[128,128]{1,0:T(8,128)S(1)}, f32[128,128]{1,0:T(8,128)S(1)}, f32[128,512]{1,0:T(8,128)S(1)}) custom-call(s32[16]{0:T(128)S(1)} %copy-done.1, bf16[64,640]{1,0:T(8,128)(2,1)S(1)} %collective-permute-done.2.refs_0_, bf16[64,640]{1,0:T(8,128)(2,1)S(1)} %collective-permute-done.3.refs_1_, ...), custom_call_target="tpu_custom_call" | custom-call | flops 20000000000 | tf_op jit(solution)/shard_map/pallas_call | solution.py:308
  14.2 1.3 %shard_map.68 = (bf16[64,512]{1,0:T(8,128)(2,1)S(1)}, bf16[64,512]{1,0:T(8,128)(2,1)S(1)}) custom-call(s32[16]{0:T(128)S(1)} %copy-done.1, bf16[128,576]{1,0:T(8,128)(2,1)S(1)} %get-tuple-element.27.q_ref, f32[128,128]{1,0:T(8,128)S(1)} %get-tuple-element.28.top_ref, f32[128,128]{1,0:T(8,128)S(1)} %get-tuple-element.29.total_ref, ...), custom_call_target="tpu_custom_call" | custom-call | tf_op jit(solution)/shard_map/pallas_call | solution.py:321
  15.5 3.0 %collective-permute-start.10 = (bf16[64,512]{1,0:T(8,128)(2,1)S(1)}, bf16[64,512]{1,0:T(8,128)(2,1)S(1)}, u32[]{:S(2)}, u32[]{:S(2)}) collective-permute-start(bf16[64,512]{1,0:T(8,128)(2,1)S(1)} %get-tuple-element.31), channel_id=1, source_target_pairs={{12,0},{4,1},{8,2},{0,3},{24,4},{16,5},{28,6},{20,7},{13,8},{5,9},... | collective-permute-start | bytes 196616 | tf_op jit(solution)/shard_map/ppermute | solution.py:330
  18.5 0.7 %collective-permute-start.11 = (bf16[64,512]{1,0:T(8,128)(2,1)S(1)}, bf16[64,512]{1,0:T(8,128)(2,1)S(1)}, u32[]{:S(2)}, u32[]{:S(2)}) collective-permute-start(bf16[64,512]{1,0:T(8,128)(2,1)S(1)} %get-tuple-element.32), channel_id=1, source_target_pairs={{4,0},{12,1},{0,2},{8,3},{16,4},{24,5},{20,6},{28,7},{5,8},{13,9},... | collective-permute-start | bytes 196616 | tf_op jit(solution)/shard_map/ppermute | solution.py:330
  19.2 3.7 %collective-permute-done.10.refs_0_ = bf16[64,512]{1,0:T(8,128)(2,1)S(1)} collective-permute-done((bf16[64,512]{1,0:T(8,128)(2,1)S(1)}, bf16[64,512]{1,0:T(8,128)(2,1)S(1)}, u32[]{:S(2)}, u32[]{:S(2)}) %collective-permute-start.10) | collective-permute-done | bytes 65568 | tf_op jit(solution)/shard_map/ppermute | solution.py:330
  23.0 3.5 %collective-permute-done.11.refs_1_ = bf16[64,512]{1,0:T(8,128)(2,1)S(1)} collective-permute-done((bf16[64,512]{1,0:T(8,128)(2,1)S(1)}, bf16[64,512]{1,0:T(8,128)(2,1)S(1)}, u32[]{:S(2)}, u32[]{:S(2)}) %collective-permute-start.11) | collective-permute-done | bytes 65568 | tf_op jit(solution)/shard_map/ppermute | solution.py:330
  26.4 1.1 %shard_map.69 = bf16[8,16,128]{2,1,0:T(8,128)(2,1)} custom-call(bf16[16,512,128]{2,1,0:T(8,128)(2,1)S(1)} %copy-done, bf16[64,512]{1,0:T(8,128)(2,1)S(1)} %collective-permute-done.10.refs_0_, bf16[64,512]{1,0:T(8,128)(2,1)S(1)} %collective-permute-done.11.refs_1_), custom_call_target="tpu_custom_call" | custom-call | tf_op jit(solution)/shard_map/pallas_call | solution.py:337
  (12 shorter events, 0.0 us)
Async XLA Ops:
  0.0 6.1 %copy-start.2 = (bf16[16,128,512]{2,1,0:T(8,128)(2,1)S(1)}, bf16[16,128,512]{2,1,0:T(8,128)(2,1)}, u32[]{:S(2)}) copy-start(bf16[16,128,512]{2,1,0:T(8,128)(2,1)} %w_ref.2) | copy-start | bytes 6291460
  1.4 4.7 %collective-permute-start = (bf16[64,256]{1,0:T(8,128)(2,1)S(1)}, bf16[64,256]{1,0:T(8,128)(2,1)S(1)}, u32[]{:S(2)}, u32[]{:S(2)}) collective-permute-start(bf16[64,256]{1,0:T(8,128)(2,1)S(1)} %get-tuple-element.19), channel_id=1, source_target_pairs={{0,8},{1,9},{2,6},{3,15},{4,20},{5,29},{6,18},{7,27},{8,0},{9,1},{... | collective-permute-start | bytes 98312 | tf_op jit(solution)/shard_map/ppermute | solution.py:265
  1.4 4.6 %collective-permute-start.1 = (bf16[64,256]{1,0:T(8,128)(2,1)S(1)}, bf16[64,256]{1,0:T(8,128)(2,1)S(1)}, u32[]{:S(2)}, u32[]{:S(2)}) collective-permute-start(bf16[64,256]{1,0:T(8,128)(2,1)S(1)} %get-tuple-element.20), channel_id=1, source_target_pairs={{0,8},{1,9},{2,14},{3,7},{4,28},{5,21},{6,26},{7,19},{8,0},{9,1},{... | collective-permute-start | bytes 98312 | tf_op jit(solution)/shard_map/ppermute | solution.py:265
  2.6 7.7 %collective-permute-start.4 = (bf16[576,128]{1,0:T(8,128)(2,1)S(1)}, bf16[576,128]{1,0:T(8,128)(2,1)S(1)}, u32[]{:S(2)}, u32[]{:S(2)}) collective-permute-start(bf16[576,128]{1,0:T(8,128)(2,1)S(1)} %get-tuple-element.24), channel_id=1, source_target_pairs={{0,24},{4,28},{8,16},{12,20},{16,8},{20,12},{24,0},{28,4},{1,25},{... | collective-permute-start | bytes 442376 | tf_op jit(solution)/shard_map/ppermute | solution.py:273
  3.5 8.9 %collective-permute-start.5 = (bf16[576,128]{1,0:T(8,128)(2,1)S(1)}, bf16[576,128]{1,0:T(8,128)(2,1)S(1)}, u32[]{:S(2)}, u32[]{:S(2)}) collective-permute-start(bf16[576,128]{1,0:T(8,128)(2,1)S(1)} %get-tuple-element.25), channel_id=1, source_target_pairs={{0,8},{4,12},{8,0},{12,4},{16,24},{20,28},{24,16},{28,20},{1,9},{5... | collective-permute-start | bytes 442376 | tf_op jit(solution)/shard_map/ppermute | solution.py:273
  5.4 7.4 %copy-start.1 = (s32[16]{0:T(128)S(1)}, s32[16]{0:T(128)}, u32[]{:S(2)}) copy-start(s32[16]{0:T(128)} %len_ref.3) | copy-start | bytes 196
  5.4 6.9 %collective-permute-start.6 = (bf16[576,128]{1,0:T(8,128)(2,1)S(1)}, bf16[576,128]{1,0:T(8,128)(2,1)S(1)}, u32[]{:S(2)}, u32[]{:S(2)}) collective-permute-start(bf16[576,128]{1,0:T(8,128)(2,1)S(1)} %get-tuple-element.26), channel_id=1, source_target_pairs={{0,16},{4,20},{8,24},{12,28},{16,0},{20,4},{24,8},{28,12},{1,17},{... | collective-permute-start | bytes 442376 | tf_op jit(solution)/shard_map/ppermute | solution.py:273
  6.6 6.3 %collective-permute-start.2 = (bf16[64,640]{1,0:T(8,128)(2,1)S(1)}, bf16[64,640]{1,0:T(8,128)(2,1)S(1)}, u32[]{:S(2)}, u32[]{:S(2)}) collective-permute-start(bf16[64,640]{1,0:T(8,128)(2,1)S(1)} %get-tuple-element.21), channel_id=1, source_target_pairs={{8,4},{9,12},{6,0},{15,8},{20,16},{29,24},{18,20},{27,28},{0,13},{... | collective-permute-start | bytes 245768 | tf_op jit(solution)/shard_map/ppermute | solution.py:296
  9.1 3.7 %collective-permute-start.3 = (bf16[64,640]{1,0:T(8,128)(2,1)S(1)}, bf16[64,640]{1,0:T(8,128)(2,1)S(1)}, u32[]{:S(2)}, u32[]{:S(2)}) collective-permute-start(bf16[64,640]{1,0:T(8,128)(2,1)S(1)} %get-tuple-element.22), channel_id=1, source_target_pairs={{8,12},{9,4},{14,8},{7,0},{28,24},{21,16},{26,28},{19,20},{0,5},{1... | collective-permute-start | bytes 245768 | tf_op jit(solution)/shard_map/ppermute | solution.py:296
  10.7 3.5 %collective-permute-start.7 = (bf16[2,576,128]{2,1,0:T(8,128)(2,1)S(1)}, bf16[2,576,128]{2,1,0:T(8,128)(2,1)S(1)}, u32[]{:S(2)}, u32[]{:S(2)}) collective-permute-start(bf16[2,576,128]{2,1,0:T(8,128)(2,1)S(1)} %shard_map.67), channel_id=1, source_target_pairs={{0,4},{4,0},{8,12},{12,8},{16,20},{20,16},{24,28},{28,24},{1,5},{5... | collective-permute-start | bytes 884744 | tf_op jit(solution)/shard_map/ppermute | solution.py:285
  12.3 1.9 %collective-permute-start.8 = (bf16[576,128]{1,0:T(8,128)(2,1)S(1)}, bf16[576,128]{1,0:T(8,128)(2,1)S(1)}, u32[]{:S(2)}, u32[]{:S(2)}) collective-permute-start(bf16[576,128]{1,0:T(8,128)(2,1)S(1)} %collective-permute-done.5.refs_4_), channel_id=1, source_target_pairs={{0,4},{4,0},{8,12},{12,8},{16,20},{20,16},{24,28},{28,24},{1,5},{5... | collective-permute-start | bytes 442376 | tf_op jit(solution)/shard_map/ppermute | solution.py:285
  12.3 1.9 %collective-permute-start.9 = (bf16[576,128]{1,0:T(8,128)(2,1)S(1)}, bf16[576,128]{1,0:T(8,128)(2,1)S(1)}, u32[]{:S(2)}, u32[]{:S(2)}) collective-permute-start(bf16[576,128]{1,0:T(8,128)(2,1)S(1)} %collective-permute-done.6.refs_5_), channel_id=1, source_target_pairs={{0,4},{4,0},{8,12},{12,8},{16,20},{20,16},{24,28},{28,24},{1,5},{5... | collective-permute-start | bytes 442376 | tf_op jit(solution)/shard_map/ppermute | solution.py:285
  12.9 13.6 %copy-start = (bf16[16,512,128]{2,1,0:T(8,128)(2,1)S(1)}, bf16[16,512,128]{2,1,0:T(8,128)(2,1)}, u32[]{:S(2)}) copy-start(bf16[16,512,128]{2,1,0:T(8,128)(2,1)} %w_ref.3) | copy-start | bytes 6291460
  15.5 7.5 %collective-permute-start.10 = (bf16[64,512]{1,0:T(8,128)(2,1)S(1)}, bf16[64,512]{1,0:T(8,128)(2,1)S(1)}, u32[]{:S(2)}, u32[]{:S(2)}) collective-permute-start(bf16[64,512]{1,0:T(8,128)(2,1)S(1)} %get-tuple-element.31), channel_id=1, source_target_pairs={{12,0},{4,1},{8,2},{0,3},{24,4},{16,5},{28,6},{20,7},{13,8},{5,9},... | collective-permute-start | bytes 196616 | tf_op jit(solution)/shard_map/ppermute | solution.py:330
  18.5 7.9 %collective-permute-start.11 = (bf16[64,512]{1,0:T(8,128)(2,1)S(1)}, bf16[64,512]{1,0:T(8,128)(2,1)S(1)}, u32[]{:S(2)}, u32[]{:S(2)}) collective-permute-start(bf16[64,512]{1,0:T(8,128)(2,1)S(1)} %get-tuple-element.32), channel_id=1, source_target_pairs={{4,0},{12,1},{0,2},{8,3},{16,4},{24,5},{20,6},{28,7},{5,8},{13,9},... | collective-permute-start | bytes 196616 | tf_op jit(solution)/shard_map/ppermute | solution.py:330

commit v12 on v11

--- a/solution.py
+++ b/solution.py
@@ -15,6 +15,7 @@
 COPIES = 2
 VMEM_LIMIT = 16 * 1024 * 1024
 LONG = pl.CostEstimate(flops=2 * 10**10, bytes_accessed=0, transcendentals=0)
+SHORT = pl.CostEstimate(flops=10**8, bytes_accessed=0, transcendentals=0)
 
 masked_value = -1e30
 
@@ -280,6 +281,7 @@
         out_specs=vmem,
         scratch_shapes=[pltpu.SemaphoreType.DMA((2,))],
         compiler_params=params,
+        cost_estimate=LONG,
     )(*own_keys[:2])
     other_core = in_plane(lambda g, t: g * COPIES + 1 - t)
     far_keys = [lax.ppermute(keys, "seq", other_core) for keys in [pair] + own_keys[2:]]
@@ -290,7 +292,7 @@
         in_specs=[vmem] * (1 + per_device),
         out_specs=[vmem] * per_device,
         compiler_params=params,
-        cost_estimate=LONG,
+        cost_estimate=SHORT,
     )(w_uk, *packed)
     arrived = [
         lax.ppermute(

time: 27.7 us -> 30.7 us (1.11)
  starting transfers between devices: 12.3 us -> 16.6 us
  waiting for transfers between devices: 9.3 us -> 8.01 us
    ppermute x3, waiting for transfers between devices: 2.08 us -> 0.01 us  [whole_sequences(): lax.ppermute(picked[k], 'seq', in_plane(lambda g, t: (g ^ turn[k]) * COPI...]
    ppermute x2, starting transfers between devices: 3.25 us -> 4.98 us  [whole_sequences(): lax.ppermute(pieces[k], both, [(host(i, j, a), owner(i, j, a)) for i, j i...]
    ppermute x2, starting transfers between devices: 3.76 us -> 5.38 us  [whole_sequences(): lax.ppermute(latent[k], both, [(owner(i, j, first_back(i // COPIES, j) ^...]
    ppermute x2, starting transfers between devices: 1.21 us -> 2.3 us  [whole_sequences(): lax.ppermute(packed[k], both, [(flat(i, j), host(i, j, leaves_as(k, i //...]
    ppermute x2, waiting for transfers between devices: 0.01 us -> 0.99 us  [whole_sequences(): lax.ppermute(pieces[k], both, [(host(i, j, a), owner(i, j, a)) for i, j i...]
  transfers between devices with their start and end apart: 12 -> 12, of which waited for: 4 -> 3; matrix products, arithmetic and copies ran while one was open for 0% -> 0% of each run, Pallas kernels for 8% -> 7%
where the time goes in v12:
time: 30.7 us; the launch traced here: 30.5 us
  starting transfers between devices  16.6 us (54%)
  waiting for transfers between devices  8.01 us (26%)
  Pallas kernels  5.82 us (19%)
    ppermute x2, waiting for transfers between devices, whole_sequences(): lax.ppermute(latent[k], both, [(owner(i, j, first_back(i // COPIES, j) ^...  7 us
    ppermute x2, starting transfers between devices, whole_sequences(): lax.ppermute(latent[k], both, [(owner(i, j, first_back(i // COPIES, j) ^...  5.38 us
    ppermute x2, starting transfers between devices, whole_sequences(): lax.ppermute(pieces[k], both, [(host(i, j, a), owner(i, j, a)) for i, j i...  4.98 us
    ppermute x3, starting transfers between devices, whole_sequences(): lax.ppermute(picked[k], 'seq', in_plane(lambda g, t: (g ^ turn[k]) * COPI...  3.27 us
    ppermute x2, starting transfers between devices, whole_sequences(): lax.ppermute(packed[k], both, [(flat(i, j), host(i, j, leaves_as(k, i //...  2.3 us
    pallas_call x1, Pallas kernels, whole_sequences(): pl.pallas_call(functools.partial(pick_kernel, turn, per_device), out_shap...  1.37 us
    pallas_call x1, Pallas kernels, whole_sequences(): pl.pallas_call(functools.partial(begin_kernel, turn, per_device, heads),...  1.3 us
    pallas_call x1, Pallas kernels, whole_sequences(): pl.pallas_call(functools.partial(finish_kernel, turn, per_device), out_sh...  1.25 us
  transfers between devices with their start and end apart: 12, of which 3 were waited for; matrix products, arithmetic and copies ran while one was open for 0% of the time, Pallas kernels for 7%

profile of v12, /device:TPU:6, one launch (start us, length us, event | category | flops | bytes accessed | tf_op | source)
XLA Modules:
  0.0 30.5 jit_solution(9347897545688391392)
XLA Ops:
  0.0 1.4 %shard_map.64 = (bf16[576,128]{1,0:T(8,128)(2,1)S(1)}, bf16[576,128]{1,0:T(8,128)(2,1)S(1)}, bf16[576,128]{1,0:T(8,128)(2,1)S(1)}, bf16[576,128]{1,0:T(8,128)(2,...) custom-call(bf16[4,576,128]{2,1,0:T(8,128)(2,1)} %bitcast.1, bf16[8,16,192]{2,1,0:T(8,128)(2,1)} %q_hbm.1, ...), custom_call_target="tpu_custom_call" | custom-call | flops 20000000000 | tf_op jit(solution)/shard_map/pallas_call | solution.py:250
  1.4 0.1 collective-permute-start.4
  1.5 1.1 %collective-permute-start = (bf16[64,256]{1,0:T(8,128)(2,1)S(1)}, bf16[64,256]{1,0:T(8,128)(2,1)S(1)}, u32[]{:S(2)}, u32[]{:S(2)}) collective-permute-start(bf16[64,256]{1,0:T(8,128)(2,1)S(1)} %get-tuple-element.19), channel_id=1, source_target_pairs={{0,8},{1,9},{2,6},{3,15},{4,20},{5,29},{6,18},{7,27},{8,0},{9,1},{... | collective-permute-start | bytes 98312 | tf_op jit(solution)/shard_map/ppermute | solution.py:266
  2.6 1.2 %collective-permute-start.1 = (bf16[64,256]{1,0:T(8,128)(2,1)S(1)}, bf16[64,256]{1,0:T(8,128)(2,1)S(1)}, u32[]{:S(2)}, u32[]{:S(2)}) collective-permute-start(bf16[64,256]{1,0:T(8,128)(2,1)S(1)} %get-tuple-element.20), channel_id=1, source_target_pairs={{0,8},{1,9},{2,14},{3,7},{4,28},{5,21},{6,26},{7,19},{8,0},{9,1},{... | collective-permute-start | bytes 98312 | tf_op jit(solution)/shard_map/ppermute | solution.py:266
  3.8 0.4 %collective-permute-start.5 = (bf16[576,128]{1,0:T(8,128)(2,1)S(1)}, bf16[576,128]{1,0:T(8,128)(2,1)S(1)}, u32[]{:S(2)}, u32[]{:S(2)}) collective-permute-start(bf16[576,128]{1,0:T(8,128)(2,1)S(1)} %get-tuple-element.25), channel_id=1, source_target_pairs={{0,8},{4,12},{8,0},{12,4},{16,24},{20,28},{24,16},{28,20},{1,9},{5... | collective-permute-start | bytes 442376 | tf_op jit(solution)/shard_map/ppermute | solution.py:274
  4.2 2.8 %collective-permute-start.6 = (bf16[576,128]{1,0:T(8,128)(2,1)S(1)}, bf16[576,128]{1,0:T(8,128)(2,1)S(1)}, u32[]{:S(2)}, u32[]{:S(2)}) collective-permute-start(bf16[576,128]{1,0:T(8,128)(2,1)S(1)} %get-tuple-element.26), channel_id=1, source_target_pairs={{0,16},{4,20},{8,24},{12,28},{16,0},{20,4},{24,8},{28,12},{1,17},{... | collective-permute-start | bytes 442376 | tf_op jit(solution)/shard_map/ppermute | solution.py:274
  7.0 0.0 collective-permute-done.refs_0_
  7.0 0.0 collective-permute-done.1.refs_1_
  7.0 0.4 %shard_map.65 = (bf16[64,640]{1,0:T(8,128)(2,1)S(1)}, bf16[64,640]{1,0:T(8,128)(2,1)S(1)}) custom-call(bf16[16,128,512]{2,1,0:T(8,128)(2,1)S(1)} %copy-done, bf16[64,256]{1,0:T(8,128)(2,1)S(1)} %collective-permute-done.refs_0_, bf16[64,256]{1,0:T(8,128)(2,1)S(1)} %collective-permute-done.1.refs_1_), custom_call_target="tpu_custom_call" | custom-call | flops 100000000 | tf_op jit(solution)/shard_map/pallas_call | solution.py:289
  7.4 3.6 %collective-permute-start.2 = (bf16[64,640]{1,0:T(8,128)(2,1)S(1)}, bf16[64,640]{1,0:T(8,128)(2,1)S(1)}, u32[]{:S(2)}, u32[]{:S(2)}) collective-permute-start(bf16[64,640]{1,0:T(8,128)(2,1)S(1)} %get-tuple-element.21), channel_id=1, source_target_pairs={{8,4},{9,12},{6,0},{15,8},{20,16},{29,24},{18,20},{27,28},{0,13},{... | collective-permute-start | bytes 245768 | tf_op jit(solution)/shard_map/ppermute | solution.py:298
  11.1 1.3 %collective-permute-start.3 = (bf16[64,640]{1,0:T(8,128)(2,1)S(1)}, bf16[64,640]{1,0:T(8,128)(2,1)S(1)}, u32[]{:S(2)}, u32[]{:S(2)}) collective-permute-start(bf16[64,640]{1,0:T(8,128)(2,1)S(1)} %get-tuple-element.22), channel_id=1, source_target_pairs={{8,12},{9,4},{14,8},{7,0},{28,24},{21,16},{26,28},{19,20},{0,5},{1... | collective-permute-start | bytes 245768 | tf_op jit(solution)/shard_map/ppermute | solution.py:298
  12.4 0.0 collective-permute-done.4.refs_3_.second_ref
  12.4 0.4 %shard_map.67 = bf16[2,576,128]{2,1,0:T(8,128)(2,1)S(1)} custom-call(bf16[576,128]{1,0:T(8,128)(2,1)S(1)} %get-tuple-element.23.refs_2_.first_ref, bf16[576,128]{1,0:T(8,128)(2,1)S(1)} %collective-permute-done.4.refs_3_.second_ref), custom_call_target="tpu_custom_call" | custom-call | flops 20000000000 | tf_op jit(solution)/shard_map/pallas_call | solution.py:277
  12.8 0.1 collective-permute-start.7
  12.9 0.5 %collective-permute-start.8 = (bf16[576,128]{1,0:T(8,128)(2,1)S(1)}, bf16[576,128]{1,0:T(8,128)(2,1)S(1)}, u32[]{:S(2)}, u32[]{:S(2)}) collective-permute-start(bf16[576,128]{1,0:T(8,128)(2,1)S(1)} %collective-permute-done.5.refs_4_), channel_id=1, source_target_pairs={{0,4},{4,0},{8,12},{12,8},{16,20},{20,16},{24,28},{28,24},{1,5},{5... | collective-permute-start | bytes 442376 | tf_op jit(solution)/shard_map/ppermute | solution.py:287
  13.4 0.1 collective-permute-start.9
  13.5 1.0 %collective-permute-done.3.refs_1_ = bf16[64,640]{1,0:T(8,128)(2,1)S(1)} collective-permute-done((bf16[64,640]{1,0:T(8,128)(2,1)S(1)}, bf16[64,640]{1,0:T(8,128)(2,1)S(1)}, u32[]{:S(2)}, u32[]{:S(2)}) %collective-permute-start.3) | collective-permute-done | bytes 81952 | tf_op jit(solution)/shard_map/ppermute | solution.py:298
  14.5 1.3 %shard_map.66 = (bf16[128,576]{1,0:T(8,128)(2,1)S(1)}, f32[128,128]{1,0:T(8,128)S(1)}, f32[128,128]{1,0:T(8,128)S(1)}, f32[128,512]{1,0:T(8,128)S(1)}) custom-call(s32[16]{0:T(128)S(1)} %copy-done.2, bf16[64,640]{1,0:T(8,128)(2,1)S(1)} %collective-permute-done.2.refs_0_, bf16[64,640]{1,0:T(8,128)(2,1)S(1)} %collective-permute-done.3.refs_1_, ...), custom_call_target="tpu_custom_call" | custom-call | flops 20000000000 | tf_op jit(solution)/shard_map/pallas_call | solution.py:310
  15.8 1.3 %shard_map.68 = (bf16[64,512]{1,0:T(8,128)(2,1)S(1)}, bf16[64,512]{1,0:T(8,128)(2,1)S(1)}) custom-call(s32[16]{0:T(128)S(1)} %copy-done.2, bf16[128,576]{1,0:T(8,128)(2,1)S(1)} %get-tuple-element.27.q_ref, f32[128,128]{1,0:T(8,128)S(1)} %get-tuple-element.28.top_ref, f32[128,128]{1,0:T(8,128)S(1)} %get-tuple-element.29.total_ref, ...), custom_call_target="tpu_custom_call" | custom-call | tf_op jit(solution)/shard_map/pallas_call | solution.py:323
  17.1 4.5 %collective-permute-start.10 = (bf16[64,512]{1,0:T(8,128)(2,1)S(1)}, bf16[64,512]{1,0:T(8,128)(2,1)S(1)}, u32[]{:S(2)}, u32[]{:S(2)}) collective-permute-start(bf16[64,512]{1,0:T(8,128)(2,1)S(1)} %get-tuple-element.31), channel_id=1, source_target_pairs={{12,0},{4,1},{8,2},{0,3},{24,4},{16,5},{28,6},{20,7},{13,8},{5,9},... | collective-permute-start | bytes 196616 | tf_op jit(solution)/shard_map/ppermute | solution.py:332
  21.6 0.9 %collective-permute-start.11 = (bf16[64,512]{1,0:T(8,128)(2,1)S(1)}, bf16[64,512]{1,0:T(8,128)(2,1)S(1)}, u32[]{:S(2)}, u32[]{:S(2)}) collective-permute-start(bf16[64,512]{1,0:T(8,128)(2,1)S(1)} %get-tuple-element.32), channel_id=1, source_target_pairs={{4,0},{12,1},{0,2},{8,3},{16,4},{24,5},{20,6},{28,7},{5,8},{13,9},... | collective-permute-start | bytes 196616 | tf_op jit(solution)/shard_map/ppermute | solution.py:332
  22.4 2.2 %collective-permute-done.10.refs_0_ = bf16[64,512]{1,0:T(8,128)(2,1)S(1)} collective-permute-done((bf16[64,512]{1,0:T(8,128)(2,1)S(1)}, bf16[64,512]{1,0:T(8,128)(2,1)S(1)}, u32[]{:S(2)}, u32[]{:S(2)}) %collective-permute-start.10) | collective-permute-done | bytes 65568 | tf_op jit(solution)/shard_map/ppermute | solution.py:332
  24.6 4.8 %collective-permute-done.11.refs_1_ = bf16[64,512]{1,0:T(8,128)(2,1)S(1)} collective-permute-done((bf16[64,512]{1,0:T(8,128)(2,1)S(1)}, bf16[64,512]{1,0:T(8,128)(2,1)S(1)}, u32[]{:S(2)}, u32[]{:S(2)}) %collective-permute-start.11) | collective-permute-done | bytes 65568 | tf_op jit(solution)/shard_map/ppermute | solution.py:332
  29.4 1.1 %shard_map.69 = bf16[8,16,128]{2,1,0:T(8,128)(2,1)} custom-call(bf16[16,512,128]{2,1,0:T(8,128)(2,1)S(1)} %copy-done.1, bf16[64,512]{1,0:T(8,128)(2,1)S(1)} %collective-permute-done.10.refs_0_, bf16[64,512]{1,0:T(8,128)(2,1)S(1)} %collective-permute-done.11.refs_1_), custom_call_target="tpu_custom_call" | custom-call | tf_op jit(solution)/shard_map/pallas_call | solution.py:339
  (12 shorter events, 0.0 us)
Async XLA Ops:
  0.0 7.0 %copy-start = (bf16[16,128,512]{2,1,0:T(8,128)(2,1)S(1)}, bf16[16,128,512]{2,1,0:T(8,128)(2,1)}, u32[]{:S(2)}) copy-start(bf16[16,128,512]{2,1,0:T(8,128)(2,1)} %w_ref.2) | copy-start | bytes 6291460
  1.4 11.0 %collective-permute-start.4 = (bf16[576,128]{1,0:T(8,128)(2,1)S(1)}, bf16[576,128]{1,0:T(8,128)(2,1)S(1)}, u32[]{:S(2)}, u32[]{:S(2)}) collective-permute-start(bf16[576,128]{1,0:T(8,128)(2,1)S(1)} %get-tuple-element.24), channel_id=1, source_target_pairs={{0,24},{4,28},{8,16},{12,20},{16,8},{20,12},{24,0},{28,4},{1,25},{... | collective-permute-start | bytes 442376 | tf_op jit(solution)/shard_map/ppermute | solution.py:274
  1.5 5.5 %collective-permute-start = (bf16[64,256]{1,0:T(8,128)(2,1)S(1)}, bf16[64,256]{1,0:T(8,128)(2,1)S(1)}, u32[]{:S(2)}, u32[]{:S(2)}) collective-permute-start(bf16[64,256]{1,0:T(8,128)(2,1)S(1)} %get-tuple-element.19), channel_id=1, source_target_pairs={{0,8},{1,9},{2,6},{3,15},{4,20},{5,29},{6,18},{7,27},{8,0},{9,1},{... | collective-permute-start | bytes 98312 | tf_op jit(solution)/shard_map/ppermute | solution.py:266
  2.6 4.4 %collective-permute-start.1 = (bf16[64,256]{1,0:T(8,128)(2,1)S(1)}, bf16[64,256]{1,0:T(8,128)(2,1)S(1)}, u32[]{:S(2)}, u32[]{:S(2)}) collective-permute-start(bf16[64,256]{1,0:T(8,128)(2,1)S(1)} %get-tuple-element.20), channel_id=1, source_target_pairs={{0,8},{1,9},{2,14},{3,7},{4,28},{5,21},{6,26},{7,19},{8,0},{9,1},{... | collective-permute-start | bytes 98312 | tf_op jit(solution)/shard_map/ppermute | solution.py:266
  3.8 9.1 %collective-permute-start.5 = (bf16[576,128]{1,0:T(8,128)(2,1)S(1)}, bf16[576,128]{1,0:T(8,128)(2,1)S(1)}, u32[]{:S(2)}, u32[]{:S(2)}) collective-permute-start(bf16[576,128]{1,0:T(8,128)(2,1)S(1)} %get-tuple-element.25), channel_id=1, source_target_pairs={{0,8},{4,12},{8,0},{12,4},{16,24},{20,28},{24,16},{28,20},{1,9},{5... | collective-permute-start | bytes 442376 | tf_op jit(solution)/shard_map/ppermute | solution.py:274
  4.2 9.2 %collective-permute-start.6 = (bf16[576,128]{1,0:T(8,128)(2,1)S(1)}, bf16[576,128]{1,0:T(8,128)(2,1)S(1)}, u32[]{:S(2)}, u32[]{:S(2)}) collective-permute-start(bf16[576,128]{1,0:T(8,128)(2,1)S(1)} %get-tuple-element.26), channel_id=1, source_target_pairs={{0,16},{4,20},{8,24},{12,28},{16,0},{20,4},{24,8},{28,12},{1,17},{... | collective-permute-start | bytes 442376 | tf_op jit(solution)/shard_map/ppermute | solution.py:274
  7.4 6.0 %collective-permute-start.2 = (bf16[64,640]{1,0:T(8,128)(2,1)S(1)}, bf16[64,640]{1,0:T(8,128)(2,1)S(1)}, u32[]{:S(2)}, u32[]{:S(2)}) collective-permute-start(bf16[64,640]{1,0:T(8,128)(2,1)S(1)} %get-tuple-element.21), channel_id=1, source_target_pairs={{8,4},{9,12},{6,0},{15,8},{20,16},{29,24},{18,20},{27,28},{0,13},{... | collective-permute-start | bytes 245768 | tf_op jit(solution)/shard_map/ppermute | solution.py:298
  11.1 3.4 %collective-permute-start.3 = (bf16[64,640]{1,0:T(8,128)(2,1)S(1)}, bf16[64,640]{1,0:T(8,128)(2,1)S(1)}, u32[]{:S(2)}, u32[]{:S(2)}) collective-permute-start(bf16[64,640]{1,0:T(8,128)(2,1)S(1)} %get-tuple-element.22), channel_id=1, source_target_pairs={{8,12},{9,4},{14,8},{7,0},{28,24},{21,16},{26,28},{19,20},{0,5},{1... | collective-permute-start | bytes 245768 | tf_op jit(solution)/shard_map/ppermute | solution.py:298
  12.4 2.1 %copy-start.2 = (s32[16]{0:T(128)S(1)}, s32[16]{0:T(128)}, u32[]{:S(2)}) copy-start(s32[16]{0:T(128)} %len_ref.3) | copy-start | bytes 196
  12.8 3.0 %collective-permute-start.7 = (bf16[2,576,128]{2,1,0:T(8,128)(2,1)S(1)}, bf16[2,576,128]{2,1,0:T(8,128)(2,1)S(1)}, u32[]{:S(2)}, u32[]{:S(2)}) collective-permute-start(bf16[2,576,128]{2,1,0:T(8,128)(2,1)S(1)} %shard_map.67), channel_id=1, source_target_pairs={{0,4},{4,0},{8,12},{12,8},{16,20},{20,16},{24,28},{28,24},{1,5},{5... | collective-permute-start | bytes 884744 | tf_op jit(solution)/shard_map/ppermute | solution.py:287
  12.9 2.9 %collective-permute-start.8 = (bf16[576,128]{1,0:T(8,128)(2,1)S(1)}, bf16[576,128]{1,0:T(8,128)(2,1)S(1)}, u32[]{:S(2)}, u32[]{:S(2)}) collective-permute-start(bf16[576,128]{1,0:T(8,128)(2,1)S(1)} %collective-permute-done.5.refs_4_), channel_id=1, source_target_pairs={{0,4},{4,0},{8,12},{12,8},{16,20},{20,16},{24,28},{28,24},{1,5},{5... | collective-permute-start | bytes 442376 | tf_op jit(solution)/shard_map/ppermute | solution.py:287
  13.4 2.4 %collective-permute-start.9 = (bf16[576,128]{1,0:T(8,128)(2,1)S(1)}, bf16[576,128]{1,0:T(8,128)(2,1)S(1)}, u32[]{:S(2)}, u32[]{:S(2)}) collective-permute-start(bf16[576,128]{1,0:T(8,128)(2,1)S(1)} %collective-permute-done.6.refs_5_), channel_id=1, source_target_pairs={{0,4},{4,0},{8,12},{12,8},{16,20},{20,16},{24,28},{28,24},{1,5},{5... | collective-permute-start | bytes 442376 | tf_op jit(solution)/shard_map/ppermute | solution.py:287
  14.5 15.0 %copy-start.1 = (bf16[16,512,128]{2,1,0:T(8,128)(2,1)S(1)}, bf16[16,512,128]{2,1,0:T(8,128)(2,1)}, u32[]{:S(2)}) copy-start(bf16[16,512,128]{2,1,0:T(8,128)(2,1)} %w_ref.3) | copy-start | bytes 6291460
  17.1 7.6 %collective-permute-start.10 = (bf16[64,512]{1,0:T(8,128)(2,1)S(1)}, bf16[64,512]{1,0:T(8,128)(2,1)S(1)}, u32[]{:S(2)}, u32[]{:S(2)}) collective-permute-start(bf16[64,512]{1,0:T(8,128)(2,1)S(1)} %get-tuple-element.31), channel_id=1, source_target_pairs={{12,0},{4,1},{8,2},{0,3},{24,4},{16,5},{28,6},{20,7},{13,8},{5,9},... | collective-permute-start | bytes 196616 | tf_op jit(solution)/shard_map/ppermute | solution.py:332
  21.6 7.9 %collective-permute-start.11 = (bf16[64,512]{1,0:T(8,128)(2,1)S(1)}, bf16[64,512]{1,0:T(8,128)(2,1)S(1)}, u32[]{:S(2)}, u32[]{:S(2)}) collective-permute-start(bf16[64,512]{1,0:T(8,128)(2,1)S(1)} %get-tuple-element.32), channel_id=1, source_target_pairs={{4,0},{12,1},{0,2},{8,3},{16,4},{24,5},{20,6},{28,7},{5,8},{13,9},... | collective-permute-start | bytes 196616 | tf_op jit(solution)/shard_map/ppermute | solution.py:332

commit v13 on v11

--- a/solution.py
+++ b/solution.py
@@ -40,16 +40,20 @@
     return far_half(plane, 1 ^ core ^ chip // 2 ^ plane // 2) ^ 1
 
 
-def pick_kernel(turn, per_device, cache_hbm, q_hbm, new_hbm, *refs):
-    owners = len(turn)
+def partner(k, core):
+    return (0, 3, 1 ^ 3 * core, 2 ^ 3 * core)[k]
+
+
+def pick_kernel(per_device, cache_hbm, q_hbm, new_hbm, *refs):
+    owners = cache_hbm.shape[0]
     blocks, outs = refs[:owners], refs[owners : owners + per_device]
     q_ref, new_ref, sem = refs[owners + per_device :]
-    chip = lax.axis_index("seq") // COPIES
+    chip, core = lax.axis_index("seq") // COPIES, lax.axis_index("seq") % COPIES
     moves = [
         pltpu.make_async_copy(q_hbm, q_ref, sem.at[owners]),
         pltpu.make_async_copy(new_hbm, new_ref, sem.at[owners + 1]),
     ] + [
-        pltpu.make_async_copy(cache_hbm.at[chip ^ turn[k]], blocks[k], sem.at[k])
+        pltpu.make_async_copy(cache_hbm.at[chip ^ partner(k, core)], blocks[k], sem.at[k])
         for k in range(owners)
     ]
     for move in moves:
@@ -126,8 +130,7 @@
     return jnp.sum(w, axis=1, keepdims=True), out
 
 
-def begin_kernel(turn, per_device, heads, len_ref, *refs):
-    owners = len(turn)
+def begin_kernel(owners, per_device, heads, len_ref, *refs):
     q_refs, key_refs = refs[:per_device], refs[per_device : per_device + owners]
     q_out, top_ref, total_ref, out_ref = refs[per_device + owners :]
     seq_index = lax.axis_index("seq")
@@ -150,7 +153,7 @@
     key = lax.broadcasted_iota(jnp.int32, f.shape, 1)
     f = jnp.where(key <= row // heads, f * SCORE_SCALE, masked_value)
 
-    starts = [((chip ^ k) * COPIES + core) * slots for k in turn]
+    starts = [((chip ^ partner(k, core)) * COPIES + core) * slots for k in range(owners)]
     s = block_scores(q, key_refs, starts, length)
     top = jnp.maximum(jnp.max(s, axis=1, keepdims=True), jnp.max(f, axis=1, keepdims=True))
     total, out = weigh(s, key_refs, top)
@@ -166,9 +169,8 @@
 
 
 def finish_kernel(
-    turn, per_device, len_ref, q_ref, top_ref, total_ref, part_ref, pair_ref, *refs
+    owners, per_device, len_ref, q_ref, top_ref, total_ref, part_ref, pair_ref, *refs
 ):
-    owners = len(turn)
     key_refs = [pair_ref.at[0], pair_ref.at[1], *refs[: owners - 2]]
     outs = refs[owners - 2 :]
     seq_index = lax.axis_index("seq")
@@ -176,7 +178,7 @@
     plane = lax.axis_index("head")
     length = len_ref[plane * owners + chip]
     slots = key_refs[0].shape[1]
-    starts = [((chip ^ k) * COPIES + 1 - core) * slots for k in turn]
+    starts = [((chip ^ partner(k, 1 - core)) * COPIES + 1 - core) * slots for k in range(owners)]
     s = block_scores(q_ref[...], key_refs, starts, length)
     first = top_ref[:, :1]
     top = jnp.maximum(first, jnp.max(s, axis=1, keepdims=True))
@@ -241,13 +243,11 @@
         plane, chip = i // COPIES, i % COPIES * per_device + a
         return flat(chip * COPIES + owner_core(plane, chip, j), plane)
 
-    turn = [0, 3, 1, 2]
-
     def in_plane(move):
         return [(g * COPIES + t, move(g, t)) for g in range(owners) for t in range(COPIES)]
 
     made = pl.pallas_call(
-        functools.partial(pick_kernel, turn, per_device),
+        functools.partial(pick_kernel, per_device),
         out_shape=[jax.ShapeDtypeStruct((width, slots), cache.dtype)] * owners
         + [jax.ShapeDtypeStruct((piece, q_width + ROPE), queries.dtype)] * per_device,
         in_specs=[anywhere] * 3,
@@ -270,7 +270,7 @@
         for k in range(per_device)
     ]
     own_keys = [picked[0]] + [
-        lax.ppermute(picked[k], "seq", in_plane(lambda g, t: (g ^ turn[k]) * COPIES + t))
+        lax.ppermute(picked[k], "seq", in_plane(lambda g, t: (g ^ partner(k, t)) * COPIES + t))
         for k in range(1, owners)
     ]
     pair = pl.pallas_call(
@@ -306,7 +306,7 @@
     ]
 
     state = pl.pallas_call(
-        functools.partial(begin_kernel, turn, per_device, heads),
+        functools.partial(begin_kernel, owners, per_device, heads),
         out_shape=[
             jax.ShapeDtypeStruct((all_rows, width), jnp.bfloat16),
             jax.ShapeDtypeStruct((all_rows, 128), jnp.float32),
@@ -319,7 +319,7 @@
         cost_estimate=LONG,
     )(lengths, *arrived, *own_keys)
     latent = pl.pallas_call(
-        functools.partial(finish_kernel, turn, per_device),
+        functools.partial(finish_kernel, owners, per_device),
         out_shape=[jax.ShapeDtypeStruct((piece, LATENT), jnp.bfloat16)] * per_device,
         in_specs=[smem] + [vmem] * (len(state) + len(far_keys)),
         out_specs=[vmem] * per_device,

time: 27.7 us -> 27.7 us (level)
  no operation moved by 1% of the time
where the time goes in v13:
time: 27.7 us; the launch traced here: 27.5 us
  starting transfers between devices  12.3 us (44%)
  waiting for transfers between devices  9.31 us (34%)
  Pallas kernels  5.82 us (21%)
    ppermute x2, waiting for transfers between devices, whole_sequences(): lax.ppermute(latent[k], both, [(owner(i, j, first_back(i // COPIES, j) ^...  7.21 us
    ppermute x2, starting transfers between devices, whole_sequences(): lax.ppermute(latent[k], both, [(owner(i, j, first_back(i // COPIES, j) ^...  3.76 us
    ppermute x3, starting transfers between devices, whole_sequences(): lax.ppermute(picked[k], 'seq', in_plane(lambda g, t: (g ^ partner(k, t))...  3.49 us
    ppermute x2, starting transfers between devices, whole_sequences(): lax.ppermute(pieces[k], both, [(host(i, j, a), owner(i, j, a)) for i, j i...  3.25 us
    ppermute x3, waiting for transfers between devices, whole_sequences(): lax.ppermute(picked[k], 'seq', in_plane(lambda g, t: (g ^ partner(k, t))...  2.08 us
    pallas_call x1, Pallas kernels, whole_sequences(): pl.pallas_call(functools.partial(pick_kernel, per_device), out_shape=[jax...  1.37 us
    pallas_call x1, Pallas kernels, whole_sequences(): pl.pallas_call(functools.partial(begin_kernel, owners, per_device, heads)...  1.3 us
    pallas_call x1, Pallas kernels, whole_sequences(): pl.pallas_call(functools.partial(finish_kernel, owners, per_device), out_...  1.26 us
  transfers between devices with their start and end apart: 12, of which 4 were waited for; matrix products, arithmetic and copies ran while one was open for 0% of the time, Pallas kernels for 8%

profile of v13, /device:TPU:6, one launch (start us, length us, event | category | flops | bytes accessed | tf_op | source)
XLA Modules:
  0.0 27.5 jit_solution(143896750677805430)
XLA Ops:
  0.0 1.4 %shard_map.64 = (bf16[576,128]{1,0:T(8,128)(2,1)S(1)}, bf16[576,128]{1,0:T(8,128)(2,1)S(1)}, bf16[576,128]{1,0:T(8,128)(2,1)S(1)}, bf16[576,128]{1,0:T(8,128)(2,...) custom-call(bf16[4,576,128]{2,1,0:T(8,128)(2,1)} %bitcast.1, bf16[8,16,192]{2,1,0:T(8,128)(2,1)} %q_hbm.1, ...), custom_call_target="tpu_custom_call" | custom-call | flops 20000000000 | tf_op jit(solution)/shard_map/pallas_call | solution.py:249
  1.4 0.1 collective-permute-start
  1.4 1.1 %collective-permute-start.1 = (bf16[64,256]{1,0:T(8,128)(2,1)S(1)}, bf16[64,256]{1,0:T(8,128)(2,1)S(1)}, u32[]{:S(2)}, u32[]{:S(2)}) collective-permute-start(bf16[64,256]{1,0:T(8,128)(2,1)S(1)} %get-tuple-element.20), channel_id=1, source_target_pairs={{0,8},{1,9},{2,14},{3,7},{4,28},{5,21},{6,26},{7,19},{8,0},{9,1},{... | collective-permute-start | bytes 98312 | tf_op jit(solution)/shard_map/ppermute | solution.py:265
  2.6 0.9 %collective-permute-start.4 = (bf16[576,128]{1,0:T(8,128)(2,1)S(1)}, bf16[576,128]{1,0:T(8,128)(2,1)S(1)}, u32[]{:S(2)}, u32[]{:S(2)}) collective-permute-start(bf16[576,128]{1,0:T(8,128)(2,1)S(1)} %get-tuple-element.24), channel_id=1, source_target_pairs={{0,24},{4,28},{8,16},{12,20},{16,8},{20,12},{24,0},{28,4},{1,25},{... | collective-permute-start | bytes 442376 | tf_op jit(solution)/shard_map/ppermute | solution.py:273
  3.5 2.0 %collective-permute-start.5 = (bf16[576,128]{1,0:T(8,128)(2,1)S(1)}, bf16[576,128]{1,0:T(8,128)(2,1)S(1)}, u32[]{:S(2)}, u32[]{:S(2)}) collective-permute-start(bf16[576,128]{1,0:T(8,128)(2,1)S(1)} %get-tuple-element.25), channel_id=1, source_target_pairs={{0,8},{4,20},{8,0},{12,28},{16,24},{20,4},{24,16},{28,12},{1,9},{5... | collective-permute-start | bytes 442376 | tf_op jit(solution)/shard_map/ppermute | solution.py:273
  5.4 0.7 %collective-permute-start.6 = (bf16[576,128]{1,0:T(8,128)(2,1)S(1)}, bf16[576,128]{1,0:T(8,128)(2,1)S(1)}, u32[]{:S(2)}, u32[]{:S(2)}) collective-permute-start(bf16[576,128]{1,0:T(8,128)(2,1)S(1)} %get-tuple-element.26), channel_id=1, source_target_pairs={{0,16},{4,12},{8,24},{12,4},{16,0},{20,28},{24,8},{28,20},{1,17},{... | collective-permute-start | bytes 442376 | tf_op jit(solution)/shard_map/ppermute | solution.py:273
  6.1 0.4 %shard_map.65 = (bf16[64,640]{1,0:T(8,128)(2,1)S(1)}, bf16[64,640]{1,0:T(8,128)(2,1)S(1)}) custom-call(bf16[16,128,512]{2,1,0:T(8,128)(2,1)S(1)} %copy-done.2, bf16[64,256]{1,0:T(8,128)(2,1)S(1)} %collective-permute-done.refs_0_, bf16[64,256]{1,0:T(8,128)(2,1)S(1)} %collective-permute-done.1.refs_1_), custom_call_target="tpu_custom_call" | custom-call | flops 20000000000 | tf_op jit(solution)/shard_map/pallas_call | solution.py:287
  6.6 2.6 %collective-permute-start.2 = (bf16[64,640]{1,0:T(8,128)(2,1)S(1)}, bf16[64,640]{1,0:T(8,128)(2,1)S(1)}, u32[]{:S(2)}, u32[]{:S(2)}) collective-permute-start(bf16[64,640]{1,0:T(8,128)(2,1)S(1)} %get-tuple-element.21), channel_id=1, source_target_pairs={{8,4},{9,12},{6,0},{15,8},{20,16},{29,24},{18,20},{27,28},{0,13},{... | collective-permute-start | bytes 245768 | tf_op jit(solution)/shard_map/ppermute | solution.py:296
  9.1 0.7 %collective-permute-start.3 = (bf16[64,640]{1,0:T(8,128)(2,1)S(1)}, bf16[64,640]{1,0:T(8,128)(2,1)S(1)}, u32[]{:S(2)}, u32[]{:S(2)}) collective-permute-start(bf16[64,640]{1,0:T(8,128)(2,1)S(1)} %get-tuple-element.22), channel_id=1, source_target_pairs={{8,12},{9,4},{14,8},{7,0},{28,24},{21,16},{26,28},{19,20},{0,5},{1... | collective-permute-start | bytes 245768 | tf_op jit(solution)/shard_map/ppermute | solution.py:296
  9.8 0.4 %collective-permute-done.4.refs_3_.second_ref = bf16[576,128]{1,0:T(8,128)(2,1)S(1)} collective-permute-done((bf16[576,128]{1,0:T(8,128)(2,1)S(1)}, bf16[576,128]{1,0:T(8,128)(2,1)S(1)}, u32[]{:S(2)}, u32[]{:S(2)}) %collective-permute-start.4) | collective-permute-done | bytes 147488 | tf_op jit(solution)/shard_map/ppermute | solution.py:273
  10.2 0.4 %shard_map.67 = bf16[2,576,128]{2,1,0:T(8,128)(2,1)S(1)} custom-call(bf16[576,128]{1,0:T(8,128)(2,1)S(1)} %get-tuple-element.23.refs_2_.first_ref, bf16[576,128]{1,0:T(8,128)(2,1)S(1)} %collective-permute-done.4.refs_3_.second_ref), custom_call_target="tpu_custom_call" | custom-call | tf_op jit(solution)/shard_map/pallas_call | solution.py:276
  10.6 0.1 collective-permute-start.7
  10.7 1.7 %collective-permute-done.5.refs_4_ = bf16[576,128]{1,0:T(8,128)(2,1)S(1)} collective-permute-done((bf16[576,128]{1,0:T(8,128)(2,1)S(1)}, bf16[576,128]{1,0:T(8,128)(2,1)S(1)}, u32[]{:S(2)}, u32[]{:S(2)}) %collective-permute-start.5) | collective-permute-done | bytes 147488 | tf_op jit(solution)/shard_map/ppermute | solution.py:273
  12.3 0.0 collective-permute-start.8
  12.3 0.5 %collective-permute-start.9 = (bf16[576,128]{1,0:T(8,128)(2,1)S(1)}, bf16[576,128]{1,0:T(8,128)(2,1)S(1)}, u32[]{:S(2)}, u32[]{:S(2)}) collective-permute-start(bf16[576,128]{1,0:T(8,128)(2,1)S(1)} %collective-permute-done.6.refs_5_), channel_id=1, source_target_pairs={{0,4},{4,0},{8,12},{12,8},{16,20},{20,16},{24,28},{28,24},{1,5},{5... | collective-permute-start | bytes 442376 | tf_op jit(solution)/shard_map/ppermute | solution.py:285
  12.9 0.0 copy-start
  12.9 1.3 %shard_map.66 = (bf16[128,576]{1,0:T(8,128)(2,1)S(1)}, f32[128,128]{1,0:T(8,128)S(1)}, f32[128,128]{1,0:T(8,128)S(1)}, f32[128,512]{1,0:T(8,128)S(1)}) custom-call(s32[16]{0:T(128)S(1)} %copy-done.1, bf16[64,640]{1,0:T(8,128)(2,1)S(1)} %collective-permute-done.2.refs_0_, bf16[64,640]{1,0:T(8,128)(2,1)S(1)} %collective-permute-done.3.refs_1_, ...), custom_call_target="tpu_custom_call" | custom-call | flops 20000000000 | tf_op jit(solution)/shard_map/pallas_call | solution.py:308
  14.2 0.0 collective-permute-done.9.refs_1_
  14.2 1.3 %shard_map.68 = (bf16[64,512]{1,0:T(8,128)(2,1)S(1)}, bf16[64,512]{1,0:T(8,128)(2,1)S(1)}) custom-call(s32[16]{0:T(128)S(1)} %copy-done.1, bf16[128,576]{1,0:T(8,128)(2,1)S(1)} %get-tuple-element.27.q_ref, f32[128,128]{1,0:T(8,128)S(1)} %get-tuple-element.28.top_ref, f32[128,128]{1,0:T(8,128)S(1)} %get-tuple-element.29.total_ref, ...), custom_call_target="tpu_custom_call" | custom-call | tf_op jit(solution)/shard_map/pallas_call | solution.py:321
  15.5 3.0 %collective-permute-start.10 = (bf16[64,512]{1,0:T(8,128)(2,1)S(1)}, bf16[64,512]{1,0:T(8,128)(2,1)S(1)}, u32[]{:S(2)}, u32[]{:S(2)}) collective-permute-start(bf16[64,512]{1,0:T(8,128)(2,1)S(1)} %get-tuple-element.31), channel_id=1, source_target_pairs={{12,0},{4,1},{8,2},{0,3},{24,4},{16,5},{28,6},{20,7},{13,8},{5,9},... | collective-permute-start | bytes 196616 | tf_op jit(solution)/shard_map/ppermute | solution.py:330
  18.5 0.7 %collective-permute-start.11 = (bf16[64,512]{1,0:T(8,128)(2,1)S(1)}, bf16[64,512]{1,0:T(8,128)(2,1)S(1)}, u32[]{:S(2)}, u32[]{:S(2)}) collective-permute-start(bf16[64,512]{1,0:T(8,128)(2,1)S(1)} %get-tuple-element.32), channel_id=1, source_target_pairs={{4,0},{12,1},{0,2},{8,3},{16,4},{24,5},{20,6},{28,7},{5,8},{13,9},... | collective-permute-start | bytes 196616 | tf_op jit(solution)/shard_map/ppermute | solution.py:330
  19.2 3.7 %collective-permute-done.10.refs_0_ = bf16[64,512]{1,0:T(8,128)(2,1)S(1)} collective-permute-done((bf16[64,512]{1,0:T(8,128)(2,1)S(1)}, bf16[64,512]{1,0:T(8,128)(2,1)S(1)}, u32[]{:S(2)}, u32[]{:S(2)}) %collective-permute-start.10) | collective-permute-done | bytes 65568 | tf_op jit(solution)/shard_map/ppermute | solution.py:330
  23.0 3.5 %collective-permute-done.11.refs_1_ = bf16[64,512]{1,0:T(8,128)(2,1)S(1)} collective-permute-done((bf16[64,512]{1,0:T(8,128)(2,1)S(1)}, bf16[64,512]{1,0:T(8,128)(2,1)S(1)}, u32[]{:S(2)}, u32[]{:S(2)}) %collective-permute-start.11) | collective-permute-done | bytes 65568 | tf_op jit(solution)/shard_map/ppermute | solution.py:330
  26.5 1.1 %shard_map.69 = bf16[8,16,128]{2,1,0:T(8,128)(2,1)} custom-call(bf16[16,512,128]{2,1,0:T(8,128)(2,1)S(1)} %copy-done, bf16[64,512]{1,0:T(8,128)(2,1)S(1)} %collective-permute-done.10.refs_0_, bf16[64,512]{1,0:T(8,128)(2,1)S(1)} %collective-permute-done.11.refs_1_), custom_call_target="tpu_custom_call" | custom-call | tf_op jit(solution)/shard_map/pallas_call | solution.py:337
  (12 shorter events, 0.0 us)
Async XLA Ops:
  0.0 6.1 %copy-start.2 = (bf16[16,128,512]{2,1,0:T(8,128)(2,1)S(1)}, bf16[16,128,512]{2,1,0:T(8,128)(2,1)}, u32[]{:S(2)}) copy-start(bf16[16,128,512]{2,1,0:T(8,128)(2,1)} %w_ref.2) | copy-start | bytes 6291460
  1.4 4.7 %collective-permute-start = (bf16[64,256]{1,0:T(8,128)(2,1)S(1)}, bf16[64,256]{1,0:T(8,128)(2,1)S(1)}, u32[]{:S(2)}, u32[]{:S(2)}) collective-permute-start(bf16[64,256]{1,0:T(8,128)(2,1)S(1)} %get-tuple-element.19), channel_id=1, source_target_pairs={{0,8},{1,9},{2,6},{3,15},{4,20},{5,29},{6,18},{7,27},{8,0},{9,1},{... | collective-permute-start | bytes 98312 | tf_op jit(solution)/shard_map/ppermute | solution.py:265
  1.4 4.6 %collective-permute-start.1 = (bf16[64,256]{1,0:T(8,128)(2,1)S(1)}, bf16[64,256]{1,0:T(8,128)(2,1)S(1)}, u32[]{:S(2)}, u32[]{:S(2)}) collective-permute-start(bf16[64,256]{1,0:T(8,128)(2,1)S(1)} %get-tuple-element.20), channel_id=1, source_target_pairs={{0,8},{1,9},{2,14},{3,7},{4,28},{5,21},{6,26},{7,19},{8,0},{9,1},{... | collective-permute-start | bytes 98312 | tf_op jit(solution)/shard_map/ppermute | solution.py:265
  2.6 7.6 %collective-permute-start.4 = (bf16[576,128]{1,0:T(8,128)(2,1)S(1)}, bf16[576,128]{1,0:T(8,128)(2,1)S(1)}, u32[]{:S(2)}, u32[]{:S(2)}) collective-permute-start(bf16[576,128]{1,0:T(8,128)(2,1)S(1)} %get-tuple-element.24), channel_id=1, source_target_pairs={{0,24},{4,28},{8,16},{12,20},{16,8},{20,12},{24,0},{28,4},{1,25},{... | collective-permute-start | bytes 442376 | tf_op jit(solution)/shard_map/ppermute | solution.py:273
  3.5 8.9 %collective-permute-start.5 = (bf16[576,128]{1,0:T(8,128)(2,1)S(1)}, bf16[576,128]{1,0:T(8,128)(2,1)S(1)}, u32[]{:S(2)}, u32[]{:S(2)}) collective-permute-start(bf16[576,128]{1,0:T(8,128)(2,1)S(1)} %get-tuple-element.25), channel_id=1, source_target_pairs={{0,8},{4,20},{8,0},{12,28},{16,24},{20,4},{24,16},{28,12},{1,9},{5... | collective-permute-start | bytes 442376 | tf_op jit(solution)/shard_map/ppermute | solution.py:273
  5.4 7.4 %copy-start.1 = (s32[16]{0:T(128)S(1)}, s32[16]{0:T(128)}, u32[]{:S(2)}) copy-start(s32[16]{0:T(128)} %len_ref.3) | copy-start | bytes 196
  5.4 6.9 %collective-permute-start.6 = (bf16[576,128]{1,0:T(8,128)(2,1)S(1)}, bf16[576,128]{1,0:T(8,128)(2,1)S(1)}, u32[]{:S(2)}, u32[]{:S(2)}) collective-permute-start(bf16[576,128]{1,0:T(8,128)(2,1)S(1)} %get-tuple-element.26), channel_id=1, source_target_pairs={{0,16},{4,12},{8,24},{12,4},{16,0},{20,28},{24,8},{28,20},{1,17},{... | collective-permute-start | bytes 442376 | tf_op jit(solution)/shard_map/ppermute | solution.py:273
  6.6 6.3 %collective-permute-start.2 = (bf16[64,640]{1,0:T(8,128)(2,1)S(1)}, bf16[64,640]{1,0:T(8,128)(2,1)S(1)}, u32[]{:S(2)}, u32[]{:S(2)}) collective-permute-start(bf16[64,640]{1,0:T(8,128)(2,1)S(1)} %get-tuple-element.21), channel_id=1, source_target_pairs={{8,4},{9,12},{6,0},{15,8},{20,16},{29,24},{18,20},{27,28},{0,13},{... | collective-permute-start | bytes 245768 | tf_op jit(solution)/shard_map/ppermute | solution.py:296
  9.1 3.7 %collective-permute-start.3 = (bf16[64,640]{1,0:T(8,128)(2,1)S(1)}, bf16[64,640]{1,0:T(8,128)(2,1)S(1)}, u32[]{:S(2)}, u32[]{:S(2)}) collective-permute-start(bf16[64,640]{1,0:T(8,128)(2,1)S(1)} %get-tuple-element.22), channel_id=1, source_target_pairs={{8,12},{9,4},{14,8},{7,0},{28,24},{21,16},{26,28},{19,20},{0,5},{1... | collective-permute-start | bytes 245768 | tf_op jit(solution)/shard_map/ppermute | solution.py:296
  10.6 3.6 %collective-permute-start.7 = (bf16[2,576,128]{2,1,0:T(8,128)(2,1)S(1)}, bf16[2,576,128]{2,1,0:T(8,128)(2,1)S(1)}, u32[]{:S(2)}, u32[]{:S(2)}) collective-permute-start(bf16[2,576,128]{2,1,0:T(8,128)(2,1)S(1)} %shard_map.67), channel_id=1, source_target_pairs={{0,4},{4,0},{8,12},{12,8},{16,20},{20,16},{24,28},{28,24},{1,5},{5... | collective-permute-start | bytes 884744 | tf_op jit(solution)/shard_map/ppermute | solution.py:285
  12.3 1.9 %collective-permute-start.8 = (bf16[576,128]{1,0:T(8,128)(2,1)S(1)}, bf16[576,128]{1,0:T(8,128)(2,1)S(1)}, u32[]{:S(2)}, u32[]{:S(2)}) collective-permute-start(bf16[576,128]{1,0:T(8,128)(2,1)S(1)} %collective-permute-done.5.refs_4_), channel_id=1, source_target_pairs={{0,4},{4,0},{8,12},{12,8},{16,20},{20,16},{24,28},{28,24},{1,5},{5... | collective-permute-start | bytes 442376 | tf_op jit(solution)/shard_map/ppermute | solution.py:285
  12.3 1.9 %collective-permute-start.9 = (bf16[576,128]{1,0:T(8,128)(2,1)S(1)}, bf16[576,128]{1,0:T(8,128)(2,1)S(1)}, u32[]{:S(2)}, u32[]{:S(2)}) collective-permute-start(bf16[576,128]{1,0:T(8,128)(2,1)S(1)} %collective-permute-done.6.refs_5_), channel_id=1, source_target_pairs={{0,4},{4,0},{8,12},{12,8},{16,20},{20,16},{24,28},{28,24},{1,5},{5... | collective-permute-start | bytes 442376 | tf_op jit(solution)/shard_map/ppermute | solution.py:285
  12.9 13.6 %copy-start = (bf16[16,512,128]{2,1,0:T(8,128)(2,1)S(1)}, bf16[16,512,128]{2,1,0:T(8,128)(2,1)}, u32[]{:S(2)}) copy-start(bf16[16,512,128]{2,1,0:T(8,128)(2,1)} %w_ref.3) | copy-start | bytes 6291460
  15.5 7.5 %collective-permute-start.10 = (bf16[64,512]{1,0:T(8,128)(2,1)S(1)}, bf16[64,512]{1,0:T(8,128)(2,1)S(1)}, u32[]{:S(2)}, u32[]{:S(2)}) collective-permute-start(bf16[64,512]{1,0:T(8,128)(2,1)S(1)} %get-tuple-element.31), channel_id=1, source_target_pairs={{12,0},{4,1},{8,2},{0,3},{24,4},{16,5},{28,6},{20,7},{13,8},{5,9},... | collective-permute-start | bytes 196616 | tf_op jit(solution)/shard_map/ppermute | solution.py:330
  18.5 8.0 %collective-permute-start.11 = (bf16[64,512]{1,0:T(8,128)(2,1)S(1)}, bf16[64,512]{1,0:T(8,128)(2,1)S(1)}, u32[]{:S(2)}, u32[]{:S(2)}) collective-permute-start(bf16[64,512]{1,0:T(8,128)(2,1)S(1)} %get-tuple-element.32), channel_id=1, source_target_pairs={{4,0},{12,1},{0,2},{8,3},{16,4},{24,5},{20,6},{28,7},{5,8},{13,9},... | collective-permute-start | bytes 196616 | tf_op jit(solution)/shard_map/ppermute | solution.py:330

commit v14 on v13

--- a/solution.py
+++ b/solution.py
@@ -81,13 +81,15 @@
         move.wait()
 
 
-def pair_kernel(first_ref, second_ref, out_ref, sem):
+def pair_kernel(owners, len_ref, first_ref, second_ref, out_ref, limit_ref, sem):
     moves = [
         pltpu.make_async_copy(ref, out_ref.at[n], sem.at[n])
         for n, ref in enumerate((first_ref, second_ref))
     ]
     for move in moves:
         move.start()
+    length = len_ref[lax.axis_index("head") * owners + lax.axis_index("seq") // COPIES]
+    limit_ref[...] = jnp.full(limit_ref.shape, length, limit_ref.dtype)
     for move in moves:
         move.wait()
 
@@ -109,13 +111,14 @@
         outs[k][:, LATENT:] = packed[k][:, NOPE:]
 
 
-def block_scores(q, refs, starts, length):
+def block_scores(q, refs, starts, limit_ref):
     width = q.shape[1]
     keys = jnp.concatenate([ref[:width, :] for ref in refs], axis=1)
-    lane = lax.broadcasted_iota(jnp.int32, (1, refs[0].shape[1]), 1)
-    position = jnp.concatenate([lane + start for start in starts], axis=1)
+    limit = limit_ref[:1, :]
+    lane = lax.broadcasted_iota(jnp.int32, limit.shape, 1)
+    visible = jnp.concatenate([lane + start < limit for start in starts], axis=1)
     s = jnp.dot(q, keys, preferred_element_type=jnp.float32) * SCORE_SCALE
-    return jnp.where(position < length, s, masked_value)
+    return jnp.where(visible, s, masked_value)
 
 
 def weigh(s, refs, top):
@@ -130,12 +133,11 @@
     return jnp.sum(w, axis=1, keepdims=True), out
 
 
-def begin_kernel(owners, per_device, heads, len_ref, *refs):
+def begin_kernel(owners, per_device, heads, limit_ref, *refs):
     q_refs, key_refs = refs[:per_device], refs[per_device : per_device + owners]
     q_out, top_ref, total_ref, out_ref = refs[per_device + owners :]
     seq_index = lax.axis_index("seq")
     chip, core = seq_index // COPIES, seq_index % COPIES
-    length = len_ref[lax.axis_index("head") * owners + chip]
     slots = key_refs[0].shape[1]
     width = LATENT + ROPE
     q = jnp.concatenate([ref[:, :width] for ref in q_refs], axis=0)
@@ -154,7 +156,7 @@
     f = jnp.where(key <= row // heads, f * SCORE_SCALE, masked_value)
 
     starts = [((chip ^ partner(k, core)) * COPIES + core) * slots for k in range(owners)]
-    s = block_scores(q, key_refs, starts, length)
+    s = block_scores(q, key_refs, starts, limit_ref)
     top = jnp.maximum(jnp.max(s, axis=1, keepdims=True), jnp.max(f, axis=1, keepdims=True))
     total, out = weigh(s, key_refs, top)
     w = jnp.exp(f - top)
@@ -169,24 +171,23 @@
 
 
 def finish_kernel(
-    owners, per_device, len_ref, q_ref, top_ref, total_ref, part_ref, pair_ref, *refs
+    owners, per_device, limit_ref, q_ref, top_ref, total_ref, part_ref, pair_ref, *refs
 ):
     key_refs = [pair_ref.at[0], pair_ref.at[1], *refs[: owners - 2]]
     outs = refs[owners - 2 :]
     seq_index = lax.axis_index("seq")
     chip, core = seq_index // COPIES, seq_index % COPIES
     plane = lax.axis_index("head")
-    length = len_ref[plane * owners + chip]
     slots = key_refs[0].shape[1]
     starts = [((chip ^ partner(k, 1 - core)) * COPIES + 1 - core) * slots for k in range(owners)]
-    s = block_scores(q_ref[...], key_refs, starts, length)
+    s = block_scores(q_ref[...], key_refs, starts, limit_ref)
     first = top_ref[:, :1]
     top = jnp.maximum(first, jnp.max(s, axis=1, keepdims=True))
     total, out = weigh(s, key_refs, top)
     scale = jnp.exp(first - top)
     total += total_ref[:, :1] * scale
     out += part_ref[...] * scale
-    out = (out / total).astype(jnp.bfloat16)
+    out = (out * (1.0 / total)).astype(jnp.bfloat16)
     piece = out.shape[0] // per_device
     sent_first = first_block(plane, chip, core)
     for k in range(per_device):
@@ -273,14 +274,17 @@
         lax.ppermute(picked[k], "seq", in_plane(lambda g, t: (g ^ partner(k, t)) * COPIES + t))
         for k in range(1, owners)
     ]
-    pair = pl.pallas_call(
-        pair_kernel,
-        out_shape=jax.ShapeDtypeStruct((2, *picked[0].shape), cache.dtype),
-        in_specs=[vmem] * 2,
-        out_specs=vmem,
+    pair, limit = pl.pallas_call(
+        functools.partial(pair_kernel, owners),
+        out_shape=[
+            jax.ShapeDtypeStruct((2, *picked[0].shape), cache.dtype),
+            jax.ShapeDtypeStruct((8, slots), jnp.int32),
+        ],
+        in_specs=[smem] + [vmem] * 2,
+        out_specs=[vmem] * 2,
         scratch_shapes=[pltpu.SemaphoreType.DMA((2,))],
         compiler_params=params,
-    )(*own_keys[:2])
+    )(lengths, *own_keys[:2])
     other_core = in_plane(lambda g, t: g * COPIES + 1 - t)
     far_keys = [lax.ppermute(keys, "seq", other_core) for keys in [pair] + own_keys[2:]]
 
@@ -313,18 +317,18 @@
             jax.ShapeDtypeStruct((all_rows, 128), jnp.float32),
             jax.ShapeDtypeStruct((all_rows, LATENT), jnp.float32),
         ],
-        in_specs=[smem] + [vmem] * (per_device + owners),
+        in_specs=[vmem] * (1 + per_device + owners),
         out_specs=[vmem] * 4,
         compiler_params=params,
         cost_estimate=LONG,
-    )(lengths, *arrived, *own_keys)
+    )(limit, *arrived, *own_keys)
     latent = pl.pallas_call(
         functools.partial(finish_kernel, owners, per_device),
         out_shape=[jax.ShapeDtypeStruct((piece, LATENT), jnp.bfloat16)] * per_device,
-        in_specs=[smem] + [vmem] * (len(state) + len(far_keys)),
+        in_specs=[vmem] * (1 + len(state) + len(far_keys)),
         out_specs=[vmem] * per_device,
         compiler_params=params,
-    )(lengths, *state, *far_keys)
+    )(limit, *state, *far_keys)
 
     back = [
         lax.ppermute(

time: 27.7 us -> 27.1 us (0.978)
  Pallas kernels: 5.82 us -> 5.3 us
  starting transfers between devices: 12.3 us -> 12 us
    ppermute x3, waiting for transfers between devices: 2.08 us -> 1.49 us  [whole_sequences(): lax.ppermute(picked[k], 'seq', in_plane(lambda g, t: (g ^ partner(k, t))...]
    pallas_call x1, Pallas kernels: 0.37 us -> 0.96 us  [whole_sequences(): pl.pallas_call(functools.partial(pair_kernel, owners), out_shape=[jax.Sha...]
    pallas_call x1, Pallas kernels: 1.26 us -> 0.7 us  [whole_sequences(): pl.pallas_call(functools.partial(finish_kernel, owners, per_device), out_...]
    pallas_call x1, Pallas kernels: 1.3 us -> 0.76 us  [whole_sequences(): pl.pallas_call(functools.partial(begin_kernel, owners, per_device, heads)...]
    ppermute x2, waiting for transfers between devices: 7.21 us -> 7.73 us  [whole_sequences(): lax.ppermute(latent[k], both, [(owner(i, j, first_back(i // COPIES, j) ^...]
    ppermute x3, waiting for transfers between devices: 0.01 us -> 0.29 us  [whole_sequences(): lax.ppermute(keys, 'seq', other_core)]
  transfers between devices with their start and end apart: 12 -> 12, of which waited for: 4 -> 6; matrix products, arithmetic and copies ran while one was open for 0% -> 0% of each run, Pallas kernels for 8% -> 8%
where the time goes in v14:
time: 27.1 us; the launch traced here: 27 us
  starting transfers between devices  12 us (44%)
  waiting for transfers between devices  9.52 us (35%)
  Pallas kernels  5.3 us (20%)
    ppermute x2, waiting for transfers between devices, whole_sequences(): lax.ppermute(latent[k], both, [(owner(i, j, first_back(i // COPIES, j) ^...  7.73 us
    ppermute x2, starting transfers between devices, whole_sequences(): lax.ppermute(latent[k], both, [(owner(i, j, first_back(i // COPIES, j) ^...  3.52 us
    ppermute x3, starting transfers between devices, whole_sequences(): lax.ppermute(picked[k], 'seq', in_plane(lambda g, t: (g ^ partner(k, t))...  3.49 us
    ppermute x2, starting transfers between devices, whole_sequences(): lax.ppermute(pieces[k], both, [(host(i, j, a), owner(i, j, a)) for i, j i...  3.25 us
    ppermute x3, waiting for transfers between devices, whole_sequences(): lax.ppermute(picked[k], 'seq', in_plane(lambda g, t: (g ^ partner(k, t))...  1.49 us
    pallas_call x1, Pallas kernels, whole_sequences(): pl.pallas_call(functools.partial(pick_kernel, per_device), out_shape=[jax...  1.37 us
    ppermute x2, starting transfers between devices, whole_sequences(): lax.ppermute(packed[k], both, [(flat(i, j), host(i, j, leaves_as(k, i //...  1.21 us
    pallas_call x1, Pallas kernels, whole_sequences(): pl.pallas_call(functools.partial(project_kernel, per_device), out_shape=j...  1.06 us
  transfers between devices with their start and end apart: 12, of which 6 were waited for; matrix products, arithmetic and copies ran while one was open for 0% of the time, Pallas kernels for 8%

profile of v14, /device:TPU:6, one launch (start us, length us, event | category | flops | bytes accessed | tf_op | source)
XLA Modules:
  0.0 27.0 jit_solution(13907156418672211999)
XLA Ops:
  0.0 1.4 %shard_map.64 = (bf16[576,128]{1,0:T(8,128)(2,1)S(1)}, bf16[576,128]{1,0:T(8,128)(2,1)S(1)}, bf16[576,128]{1,0:T(8,128)(2,1)S(1)}, bf16[576,128]{1,0:T(8,128)(2,...) custom-call(bf16[4,576,128]{2,1,0:T(8,128)(2,1)} %bitcast.1, bf16[8,16,192]{2,1,0:T(8,128)(2,1)} %q_hbm.1, ...), custom_call_target="tpu_custom_call" | custom-call | flops 20000000000 | tf_op jit(solution)/shard_map/pallas_call | solution.py:250
  1.4 0.1 collective-permute-start.1
  1.4 1.1 %collective-permute-start.2 = (bf16[64,256]{1,0:T(8,128)(2,1)S(1)}, bf16[64,256]{1,0:T(8,128)(2,1)S(1)}, u32[]{:S(2)}, u32[]{:S(2)}) collective-permute-start(bf16[64,256]{1,0:T(8,128)(2,1)S(1)} %get-tuple-element.25), channel_id=1, source_target_pairs={{0,8},{1,9},{2,14},{3,7},{4,28},{5,21},{6,26},{7,19},{8,0},{9,1},{... | collective-permute-start | bytes 98312 | tf_op jit(solution)/shard_map/ppermute | solution.py:266
  2.6 0.9 %collective-permute-start = (bf16[576,128]{1,0:T(8,128)(2,1)S(1)}, bf16[576,128]{1,0:T(8,128)(2,1)S(1)}, u32[]{:S(2)}, u32[]{:S(2)}) collective-permute-start(bf16[576,128]{1,0:T(8,128)(2,1)S(1)} %get-tuple-element.22), channel_id=1, source_target_pairs={{0,24},{4,28},{8,16},{12,20},{16,8},{20,12},{24,0},{28,4},{1,25},{... | collective-permute-start | bytes 442376 | tf_op jit(solution)/shard_map/ppermute | solution.py:274
  3.5 2.0 %collective-permute-start.5 = (bf16[576,128]{1,0:T(8,128)(2,1)S(1)}, bf16[576,128]{1,0:T(8,128)(2,1)S(1)}, u32[]{:S(2)}, u32[]{:S(2)}) collective-permute-start(bf16[576,128]{1,0:T(8,128)(2,1)S(1)} %get-tuple-element.28), channel_id=1, source_target_pairs={{0,8},{4,20},{8,0},{12,28},{16,24},{20,4},{24,16},{28,12},{1,9},{5... | collective-permute-start | bytes 442376 | tf_op jit(solution)/shard_map/ppermute | solution.py:274
  5.4 0.7 %collective-permute-start.6 = (bf16[576,128]{1,0:T(8,128)(2,1)S(1)}, bf16[576,128]{1,0:T(8,128)(2,1)S(1)}, u32[]{:S(2)}, u32[]{:S(2)}) collective-permute-start(bf16[576,128]{1,0:T(8,128)(2,1)S(1)} %get-tuple-element.29), channel_id=1, source_target_pairs={{0,16},{4,12},{8,24},{12,4},{16,0},{20,28},{24,8},{28,20},{1,17},{... | collective-permute-start | bytes 442376 | tf_op jit(solution)/shard_map/ppermute | solution.py:274
  6.1 0.4 %shard_map.66 = (bf16[64,640]{1,0:T(8,128)(2,1)S(1)}, bf16[64,640]{1,0:T(8,128)(2,1)S(1)}) custom-call(bf16[16,128,512]{2,1,0:T(8,128)(2,1)S(1)} %copy-done.2, bf16[64,256]{1,0:T(8,128)(2,1)S(1)} %collective-permute-done.1.refs_0_, bf16[64,256]{1,0:T(8,128)(2,1)S(1)} %collective-permute-done.2.refs_1_), custom_call_target="tpu_custom_call" | custom-call | flops 20000000000 | tf_op jit(solution)/shard_map/pallas_call | solution.py:291
  6.6 2.6 %collective-permute-start.3 = (bf16[64,640]{1,0:T(8,128)(2,1)S(1)}, bf16[64,640]{1,0:T(8,128)(2,1)S(1)}, u32[]{:S(2)}, u32[]{:S(2)}) collective-permute-start(bf16[64,640]{1,0:T(8,128)(2,1)S(1)} %get-tuple-element.26), channel_id=1, source_target_pairs={{8,4},{9,12},{6,0},{15,8},{20,16},{29,24},{18,20},{27,28},{0,13},{... | collective-permute-start | bytes 245768 | tf_op jit(solution)/shard_map/ppermute | solution.py:300
  9.1 0.7 %collective-permute-start.4 = (bf16[64,640]{1,0:T(8,128)(2,1)S(1)}, bf16[64,640]{1,0:T(8,128)(2,1)S(1)}, u32[]{:S(2)}, u32[]{:S(2)}) collective-permute-start(bf16[64,640]{1,0:T(8,128)(2,1)S(1)} %get-tuple-element.27), channel_id=1, source_target_pairs={{8,12},{9,4},{14,8},{7,0},{28,24},{21,16},{26,28},{19,20},{0,5},{1... | collective-permute-start | bytes 245768 | tf_op jit(solution)/shard_map/ppermute | solution.py:300
  9.8 0.4 %collective-permute-done.second_ref.refs_3_ = bf16[576,128]{1,0:T(8,128)(2,1)S(1)} collective-permute-done((bf16[576,128]{1,0:T(8,128)(2,1)S(1)}, bf16[576,128]{1,0:T(8,128)(2,1)S(1)}, u32[]{:S(2)}, u32[]{:S(2)}) %collective-permute-start) | collective-permute-done | bytes 147488 | tf_op jit(solution)/shard_map/ppermute | solution.py:274
  10.2 1.0 %shard_map.65 = (bf16[2,576,128]{2,1,0:T(8,128)(2,1)S(1)}, s32[8,128]{1,0:T(8,128)S(1)}) custom-call(s32[16]{0:T(128)S(1)} %copy-done.1, bf16[576,128]{1,0:T(8,128)(2,1)S(1)} %get-tuple-element.21.first_ref.refs_2_, bf16[576,128]{1,0:T(8,128)(2,1)S(1)} %collective-permute-done.second_ref.refs_3_), custom_call_target="tpu_custom_call" | custom-call | tf_op jit(solution)/shard_map/pallas_call | solution.py:277
  11.2 0.1 collective-permute-start.7
  11.3 1.1 %collective-permute-done.5.refs_4_ = bf16[576,128]{1,0:T(8,128)(2,1)S(1)} collective-permute-done((bf16[576,128]{1,0:T(8,128)(2,1)S(1)}, bf16[576,128]{1,0:T(8,128)(2,1)S(1)}, u32[]{:S(2)}, u32[]{:S(2)}) %collective-permute-start.5) | collective-permute-done | bytes 147488 | tf_op jit(solution)/shard_map/ppermute | solution.py:274
  12.3 0.0 collective-permute-start.8
  12.3 0.5 %collective-permute-start.9 = (bf16[576,128]{1,0:T(8,128)(2,1)S(1)}, bf16[576,128]{1,0:T(8,128)(2,1)S(1)}, u32[]{:S(2)}, u32[]{:S(2)}) collective-permute-start(bf16[576,128]{1,0:T(8,128)(2,1)S(1)} %collective-permute-done.6.refs_5_), channel_id=1, source_target_pairs={{0,4},{4,0},{8,12},{12,8},{16,20},{20,16},{24,28},{28,24},{1,5},{5... | collective-permute-start | bytes 442376 | tf_op jit(solution)/shard_map/ppermute | solution.py:289
  12.9 0.8 %shard_map.67 = (bf16[128,576]{1,0:T(8,128)(2,1)S(1)}, f32[128,128]{1,0:T(8,128)S(1)}, f32[128,128]{1,0:T(8,128)S(1)}, f32[128,512]{1,0:T(8,128)S(1)}) custom-call(s32[8,128]{1,0:T(8,128)S(1)} %get-tuple-element.23.limit_ref, bf16[64,640]{1,0:T(8,128)(2,1)S(1)} %collective-permute-done.3.refs_0_, bf16[64,640]{1,0:T(8,128)(2,1)S(1)} %collective-permute-done.4.refs_1_, ...), custom_call_target="tpu_custom_call" | custom-call | flops 20000000000 | tf_op jit(solution)/shard_map/pallas_call | solution.py:312
  13.6 0.1 collective-permute-done.8.refs_0_
  13.7 0.2 collective-permute-done.9.refs_1_
  13.9 0.7 %shard_map.68 = (bf16[64,512]{1,0:T(8,128)(2,1)S(1)}, bf16[64,512]{1,0:T(8,128)(2,1)S(1)}) custom-call(s32[8,128]{1,0:T(8,128)S(1)} %get-tuple-element.23.limit_ref, bf16[128,576]{1,0:T(8,128)(2,1)S(1)} %get-tuple-element.30.q_ref, f32[128,128]{1,0:T(8,128)S(1)} %get-tuple-element.31.top_ref, f32[128,128]{1,0:T(8,128)S(1)} %get-tuple-element.32.total_ref, ...), custom_call_target="tpu_custom_call" | custom-call | tf_op jit(solution)/shard_map/pallas_call | solution.py:325
  14.6 2.8 %collective-permute-start.10 = (bf16[64,512]{1,0:T(8,128)(2,1)S(1)}, bf16[64,512]{1,0:T(8,128)(2,1)S(1)}, u32[]{:S(2)}, u32[]{:S(2)}) collective-permute-start(bf16[64,512]{1,0:T(8,128)(2,1)S(1)} %get-tuple-element.35), channel_id=1, source_target_pairs={{12,0},{4,1},{8,2},{0,3},{24,4},{16,5},{28,6},{20,7},{13,8},{5,9},... | collective-permute-start | bytes 196616 | tf_op jit(solution)/shard_map/ppermute | solution.py:334
  17.4 0.8 %collective-permute-start.11 = (bf16[64,512]{1,0:T(8,128)(2,1)S(1)}, bf16[64,512]{1,0:T(8,128)(2,1)S(1)}, u32[]{:S(2)}, u32[]{:S(2)}) collective-permute-start(bf16[64,512]{1,0:T(8,128)(2,1)S(1)} %get-tuple-element.36), channel_id=1, source_target_pairs={{4,0},{12,1},{0,2},{8,3},{16,4},{24,5},{20,6},{28,7},{5,8},{13,9},... | collective-permute-start | bytes 196616 | tf_op jit(solution)/shard_map/ppermute | solution.py:334
  18.2 4.0 %collective-permute-done.10.refs_0_ = bf16[64,512]{1,0:T(8,128)(2,1)S(1)} collective-permute-done((bf16[64,512]{1,0:T(8,128)(2,1)S(1)}, bf16[64,512]{1,0:T(8,128)(2,1)S(1)}, u32[]{:S(2)}, u32[]{:S(2)}) %collective-permute-start.10) | collective-permute-done | bytes 65568 | tf_op jit(solution)/shard_map/ppermute | solution.py:334
  22.1 3.8 %collective-permute-done.11.refs_1_ = bf16[64,512]{1,0:T(8,128)(2,1)S(1)} collective-permute-done((bf16[64,512]{1,0:T(8,128)(2,1)S(1)}, bf16[64,512]{1,0:T(8,128)(2,1)S(1)}, u32[]{:S(2)}, u32[]{:S(2)}) %collective-permute-start.11) | collective-permute-done | bytes 65568 | tf_op jit(solution)/shard_map/ppermute | solution.py:334
  25.9 1.1 %shard_map.69 = bf16[8,16,128]{2,1,0:T(8,128)(2,1)} custom-call(bf16[16,512,128]{2,1,0:T(8,128)(2,1)S(1)} %copy-done, bf16[64,512]{1,0:T(8,128)(2,1)S(1)} %collective-permute-done.10.refs_0_, bf16[64,512]{1,0:T(8,128)(2,1)S(1)} %collective-permute-done.11.refs_1_), custom_call_target="tpu_custom_call" | custom-call | tf_op jit(solution)/shard_map/pallas_call | solution.py:341
  (12 shorter events, 0.0 us)
Async XLA Ops:
  0.0 6.1 %copy-start.2 = (bf16[16,128,512]{2,1,0:T(8,128)(2,1)S(1)}, bf16[16,128,512]{2,1,0:T(8,128)(2,1)}, u32[]{:S(2)}) copy-start(bf16[16,128,512]{2,1,0:T(8,128)(2,1)} %w_ref.2) | copy-start | bytes 6291460
  1.4 4.7 %collective-permute-start.1 = (bf16[64,256]{1,0:T(8,128)(2,1)S(1)}, bf16[64,256]{1,0:T(8,128)(2,1)S(1)}, u32[]{:S(2)}, u32[]{:S(2)}) collective-permute-start(bf16[64,256]{1,0:T(8,128)(2,1)S(1)} %get-tuple-element.24), channel_id=1, source_target_pairs={{0,8},{1,9},{2,6},{3,15},{4,20},{5,29},{6,18},{7,27},{8,0},{9,1},{... | collective-permute-start | bytes 98312 | tf_op jit(solution)/shard_map/ppermute | solution.py:266
  1.4 4.6 %collective-permute-start.2 = (bf16[64,256]{1,0:T(8,128)(2,1)S(1)}, bf16[64,256]{1,0:T(8,128)(2,1)S(1)}, u32[]{:S(2)}, u32[]{:S(2)}) collective-permute-start(bf16[64,256]{1,0:T(8,128)(2,1)S(1)} %get-tuple-element.25), channel_id=1, source_target_pairs={{0,8},{1,9},{2,14},{3,7},{4,28},{5,21},{6,26},{7,19},{8,0},{9,1},{... | collective-permute-start | bytes 98312 | tf_op jit(solution)/shard_map/ppermute | solution.py:266
  2.6 7.6 %collective-permute-start = (bf16[576,128]{1,0:T(8,128)(2,1)S(1)}, bf16[576,128]{1,0:T(8,128)(2,1)S(1)}, u32[]{:S(2)}, u32[]{:S(2)}) collective-permute-start(bf16[576,128]{1,0:T(8,128)(2,1)S(1)} %get-tuple-element.22), channel_id=1, source_target_pairs={{0,24},{4,28},{8,16},{12,20},{16,8},{20,12},{24,0},{28,4},{1,25},{... | collective-permute-start | bytes 442376 | tf_op jit(solution)/shard_map/ppermute | solution.py:274
  3.5 8.9 %collective-permute-start.5 = (bf16[576,128]{1,0:T(8,128)(2,1)S(1)}, bf16[576,128]{1,0:T(8,128)(2,1)S(1)}, u32[]{:S(2)}, u32[]{:S(2)}) collective-permute-start(bf16[576,128]{1,0:T(8,128)(2,1)S(1)} %get-tuple-element.28), channel_id=1, source_target_pairs={{0,8},{4,20},{8,0},{12,28},{16,24},{20,4},{24,16},{28,12},{1,9},{5... | collective-permute-start | bytes 442376 | tf_op jit(solution)/shard_map/ppermute | solution.py:274
  5.4 4.8 %copy-start.1 = (s32[16]{0:T(128)S(1)}, s32[16]{0:T(128)}, u32[]{:S(2)}) copy-start(s32[16]{0:T(128)} %len_ref.1) | copy-start | bytes 196
  5.4 6.9 %collective-permute-start.6 = (bf16[576,128]{1,0:T(8,128)(2,1)S(1)}, bf16[576,128]{1,0:T(8,128)(2,1)S(1)}, u32[]{:S(2)}, u32[]{:S(2)}) collective-permute-start(bf16[576,128]{1,0:T(8,128)(2,1)S(1)} %get-tuple-element.29), channel_id=1, source_target_pairs={{0,16},{4,12},{8,24},{12,4},{16,0},{20,28},{24,8},{28,20},{1,17},{... | collective-permute-start | bytes 442376 | tf_op jit(solution)/shard_map/ppermute | solution.py:274
  6.6 6.3 %collective-permute-start.3 = (bf16[64,640]{1,0:T(8,128)(2,1)S(1)}, bf16[64,640]{1,0:T(8,128)(2,1)S(1)}, u32[]{:S(2)}, u32[]{:S(2)}) collective-permute-start(bf16[64,640]{1,0:T(8,128)(2,1)S(1)} %get-tuple-element.26), channel_id=1, source_target_pairs={{8,4},{9,12},{6,0},{15,8},{20,16},{29,24},{18,20},{27,28},{0,13},{... | collective-permute-start | bytes 245768 | tf_op jit(solution)/shard_map/ppermute | solution.py:300
  9.1 3.7 %collective-permute-start.4 = (bf16[64,640]{1,0:T(8,128)(2,1)S(1)}, bf16[64,640]{1,0:T(8,128)(2,1)S(1)}, u32[]{:S(2)}, u32[]{:S(2)}) collective-permute-start(bf16[64,640]{1,0:T(8,128)(2,1)S(1)} %get-tuple-element.27), channel_id=1, source_target_pairs={{8,12},{9,4},{14,8},{7,0},{28,24},{21,16},{26,28},{19,20},{0,5},{1... | collective-permute-start | bytes 245768 | tf_op jit(solution)/shard_map/ppermute | solution.py:300
  11.2 2.7 %collective-permute-start.7 = (bf16[2,576,128]{2,1,0:T(8,128)(2,1)S(1)}, bf16[2,576,128]{2,1,0:T(8,128)(2,1)S(1)}, u32[]{:S(2)}, u32[]{:S(2)}) collective-permute-start(bf16[2,576,128]{2,1,0:T(8,128)(2,1)S(1)} %get-tuple-element.34), channel_id=1, source_target_pairs={{0,4},{4,0},{8,12},{12,8},{16,20},{20,16},{24,28},{28,24},{1,5},{5... | collective-permute-start | bytes 884744 | tf_op jit(solution)/shard_map/ppermute | solution.py:289
  12.3 1.4 %collective-permute-start.8 = (bf16[576,128]{1,0:T(8,128)(2,1)S(1)}, bf16[576,128]{1,0:T(8,128)(2,1)S(1)}, u32[]{:S(2)}, u32[]{:S(2)}) collective-permute-start(bf16[576,128]{1,0:T(8,128)(2,1)S(1)} %collective-permute-done.5.refs_4_), channel_id=1, source_target_pairs={{0,4},{4,0},{8,12},{12,8},{16,20},{20,16},{24,28},{28,24},{1,5},{5... | collective-permute-start | bytes 442376 | tf_op jit(solution)/shard_map/ppermute | solution.py:289
  12.3 1.6 %collective-permute-start.9 = (bf16[576,128]{1,0:T(8,128)(2,1)S(1)}, bf16[576,128]{1,0:T(8,128)(2,1)S(1)}, u32[]{:S(2)}, u32[]{:S(2)}) collective-permute-start(bf16[576,128]{1,0:T(8,128)(2,1)S(1)} %collective-permute-done.6.refs_5_), channel_id=1, source_target_pairs={{0,4},{4,0},{8,12},{12,8},{16,20},{20,16},{24,28},{28,24},{1,5},{5... | collective-permute-start | bytes 442376 | tf_op jit(solution)/shard_map/ppermute | solution.py:289
  12.9 13.0 %copy-start = (bf16[16,512,128]{2,1,0:T(8,128)(2,1)S(1)}, bf16[16,512,128]{2,1,0:T(8,128)(2,1)}, u32[]{:S(2)}) copy-start(bf16[16,512,128]{2,1,0:T(8,128)(2,1)} %w_ref.3) | copy-start | bytes 6291460
  14.6 7.5 %collective-permute-start.10 = (bf16[64,512]{1,0:T(8,128)(2,1)S(1)}, bf16[64,512]{1,0:T(8,128)(2,1)S(1)}, u32[]{:S(2)}, u32[]{:S(2)}) collective-permute-start(bf16[64,512]{1,0:T(8,128)(2,1)S(1)} %get-tuple-element.35), channel_id=1, source_target_pairs={{12,0},{4,1},{8,2},{0,3},{24,4},{16,5},{28,6},{20,7},{13,8},{5,9},... | collective-permute-start | bytes 196616 | tf_op jit(solution)/shard_map/ppermute | solution.py:334
  17.4 8.5 %collective-permute-start.11 = (bf16[64,512]{1,0:T(8,128)(2,1)S(1)}, bf16[64,512]{1,0:T(8,128)(2,1)S(1)}, u32[]{:S(2)}, u32[]{:S(2)}) collective-permute-start(bf16[64,512]{1,0:T(8,128)(2,1)S(1)} %get-tuple-element.36), channel_id=1, source_target_pairs={{4,0},{12,1},{0,2},{8,3},{16,4},{24,5},{20,6},{28,7},{5,8},{13,9},... | collective-permute-start | bytes 196616 | tf_op jit(solution)/shard_map/ppermute | solution.py:334

commit v15 on v14

--- a/solution.py
+++ b/solution.py
@@ -19,12 +19,8 @@
 masked_value = -1e30
 
 
-def leaves_as(k, chip, head_shard):
-    return (k + chip + head_shard) % 2
-
-
-def owner_core(plane, chip, head_shard):
-    return 1 ^ head_shard // 2 ^ chip // 2 ^ plane // 2
+def leaves_as(k, head_shard):
+    return (k + head_shard) % 2
 
 
 def far_half(plane, pair):
@@ -37,21 +33,22 @@
 
 
 def first_block(plane, chip, core):
-    return far_half(plane, 1 ^ core ^ chip // 2 ^ plane // 2) ^ 1
+    near = 1 * (chip % 2 == plane % 2)
+    return far_half(plane, 1 - core) ^ near ^ chip % 2
 
 
 def partner(k, core):
     return (0, 3, 1 ^ 3 * core, 2 ^ 3 * core)[k]
 
 
-def pick_kernel(per_device, cache_hbm, q_hbm, new_hbm, *refs):
+def pick_kernel(per_device, cache_hbm, q_hbm, new_hbm, len_hbm, *refs):
     owners = cache_hbm.shape[0]
-    blocks, outs = refs[:owners], refs[owners : owners + per_device]
-    q_ref, new_ref, sem = refs[owners + per_device :]
+    blocks, (out_ref, limit_ref, q_ref, new_ref, len_ref, sem) = refs[:owners], refs[owners:]
     chip, core = lax.axis_index("seq") // COPIES, lax.axis_index("seq") % COPIES
     moves = [
         pltpu.make_async_copy(q_hbm, q_ref, sem.at[owners]),
         pltpu.make_async_copy(new_hbm, new_ref, sem.at[owners + 1]),
+        pltpu.make_async_copy(len_hbm, len_ref, sem.at[owners + 2]),
     ] + [
         pltpu.make_async_copy(cache_hbm.at[chip ^ partner(k, core)], blocks[k], sem.at[k])
         for k in range(owners)
@@ -62,42 +59,38 @@
     moves[1].wait()
     heads, width = q_ref.shape[1:]
     fresh = new_ref[...].astype(jnp.float32)
+    piece = SPEC * heads
     for a in range(per_device):
-        rows = q_ref[a * SPEC : (a + 1) * SPEC].reshape(SPEC * heads, width)
+        rows = q_ref[a * SPEC : (a + 1) * SPEC].reshape(piece, width)
         own = fresh[a * SPEC : (a + 1) * SPEC]
         parts = [own[:, n : n + ROPE] for n in range(0, own.shape[1], ROPE)]
-        spare = SPEC * heads - SPEC * len(parts)
+        spare = piece - SPEC * len(parts)
         if spare:
             parts.append(jnp.zeros((spare, ROPE), jnp.float32))
         own = jnp.concatenate(parts, axis=0).astype(rows.dtype)
-        packed = jnp.concatenate([rows, own], axis=1)
-        for k in range(per_device):
-
-            @pl.when(leaves_as(k, chip, lax.axis_index("head")) == a)
-            def _():
-                outs[k][...] = packed
-
-    for move in moves[2:]:
+        out_ref[a * piece : (a + 1) * piece] = jnp.concatenate([rows, own], axis=1)
+    moves[2].wait()
+    length = len_ref[lax.axis_index("head") * owners + chip]
+    limit_ref[...] = jnp.full(limit_ref.shape, length, limit_ref.dtype)
+    for move in moves[3:]:
         move.wait()
 
 
-def pair_kernel(owners, len_ref, first_ref, second_ref, out_ref, limit_ref, sem):
+def pair_kernel(first_ref, second_ref, out_ref, sem):
     moves = [
         pltpu.make_async_copy(ref, out_ref.at[n], sem.at[n])
         for n, ref in enumerate((first_ref, second_ref))
     ]
     for move in moves:
         move.start()
-    length = len_ref[lax.axis_index("head") * owners + lax.axis_index("seq") // COPIES]
-    limit_ref[...] = jnp.full(limit_ref.shape, length, limit_ref.dtype)
     for move in moves:
         move.wait()
 
 
-def absorb_kernel(per_device, w_ref, *refs):
-    packed, outs = refs[:per_device], refs[per_device:]
+def absorb_kernel(per_device, w_ref, packed_ref, *outs):
     heads = w_ref.shape[0]
-    nope = jnp.concatenate([ref[:, :NOPE] for ref in packed], axis=0)
+    piece = SPEC * heads
+    nope = packed_ref[:, :NOPE]
     own_head = lax.broadcasted_iota(jnp.int32, nope.shape, 0) % heads
     spread = jnp.concatenate(
         [jnp.where(own_head == h, nope, jnp.zeros_like(nope)) for h in range(heads)], axis=1
@@ -105,10 +98,15 @@
     absorbed = jnp.dot(
         spread, w_ref[...].reshape(heads * NOPE, LATENT), preferred_element_type=jnp.float32
     ).astype(jnp.bfloat16)
-    piece = SPEC * heads
     for k in range(per_device):
-        outs[k][:, :LATENT] = absorbed[k * piece : (k + 1) * piece]
-        outs[k][:, LATENT:] = packed[k][:, NOPE:]
+        which = leaves_as(k, lax.axis_index("head"))
+        for a in range(per_device):
+
+            @pl.when(which == a)
+            def _():
+                rows = slice(a * piece, (a + 1) * piece)
+                outs[k][:, :LATENT] = absorbed[rows]
+                outs[k][:, LATENT:] = packed_ref[rows, NOPE:]
 
 
 def block_scores(q, refs, starts, limit_ref):
@@ -223,7 +221,6 @@
     all_rows = per_device * piece
     params = pltpu.CompilerParams(vmem_limit_bytes=VMEM_LIMIT)
     vmem = pl.BlockSpec(memory_space=pltpu.VMEM)
-    smem = pl.BlockSpec(memory_space=pltpu.SMEM)
     anywhere = pl.BlockSpec(memory_space=pl.ANY)
     both = ("seq", "head")
     devices = [(i, j) for i in range(seq_size) for j in range(head_size)]
@@ -234,77 +231,64 @@
     def in_hbm(x):
         return pltpu.with_memory_space_constraint(x, pltpu.HBM)
 
-    def host(i, j, a):
-        home, chip = i // COPIES, i % COPIES * per_device + a
-        core = home // 2 ^ chip // 2 ^ j // 2
-        exchanged = chip == home and home // 2 == j // 2
-        return flat((chip ^ exchanged) * COPIES + core, j)
+    def host(i, j):
+        other = (i // COPIES) ^ (2 - ((j ^ (j >> 1)) & 1))
+        return flat(((i % COPIES) * 2 + other // 2) * COPIES + other % 2, j)
 
     def owner(i, j, a):
         plane, chip = i // COPIES, i % COPIES * per_device + a
-        return flat(chip * COPIES + owner_core(plane, chip, j), plane)
+        return flat(chip * COPIES + 1 - j // 2, plane)
 
     def in_plane(move):
         return [(g * COPIES + t, move(g, t)) for g in range(owners) for t in range(COPIES)]
 
-    made = pl.pallas_call(
+    *picked, packed, limit = pl.pallas_call(
         functools.partial(pick_kernel, per_device),
         out_shape=[jax.ShapeDtypeStruct((width, slots), cache.dtype)] * owners
-        + [jax.ShapeDtypeStruct((piece, q_width + ROPE), queries.dtype)] * per_device,
-        in_specs=[anywhere] * 3,
-        out_specs=[vmem] * (owners + per_device),
+        + [
+            jax.ShapeDtypeStruct((all_rows, q_width + ROPE), queries.dtype),
+            jax.ShapeDtypeStruct((8, slots), jnp.int32),
+        ],
+        in_specs=[anywhere] * 4,
+        out_specs=[vmem] * (owners + 2),
         scratch_shapes=[
             pltpu.VMEM(queries.shape, queries.dtype),
             pltpu.VMEM(new_latent.shape, new_latent.dtype),
-            pltpu.SemaphoreType.DMA((owners + 2,)),
+            pltpu.SMEM(lengths.shape, lengths.dtype),
+            pltpu.SemaphoreType.DMA((owners + 3,)),
         ],
         compiler_params=params,
         cost_estimate=LONG,
-    )(in_hbm(jnp.swapaxes(cache, 1, 2)), in_hbm(queries), in_hbm(new_latent))
-    picked, packed = made[:owners], made[owners:]
-    packed = [
-        lax.ppermute(
-            packed[k],
-            both,
-            [(flat(i, j), host(i, j, leaves_as(k, i // COPIES, j))) for i, j in devices],
-        )
-        for k in range(per_device)
-    ]
+    )(*[in_hbm(x) for x in (jnp.swapaxes(cache, 1, 2), queries, new_latent, lengths)])
+    moved = lax.ppermute(packed, both, [(flat(i, j), host(i, j)) for i, j in devices])
     own_keys = [picked[0]] + [
         lax.ppermute(picked[k], "seq", in_plane(lambda g, t: (g ^ partner(k, t)) * COPIES + t))
         for k in range(1, owners)
     ]
-    pair, limit = pl.pallas_call(
-        functools.partial(pair_kernel, owners),
-        out_shape=[
-            jax.ShapeDtypeStruct((2, *picked[0].shape), cache.dtype),
-            jax.ShapeDtypeStruct((8, slots), jnp.int32),
-        ],
-        in_specs=[smem] + [vmem] * 2,
-        out_specs=[vmem] * 2,
+    pair = pl.pallas_call(
+        pair_kernel,
+        out_shape=jax.ShapeDtypeStruct((2, *picked[0].shape), cache.dtype),
+        in_specs=[vmem] * 2,
+        out_specs=vmem,
         scratch_shapes=[pltpu.SemaphoreType.DMA((2,))],
         compiler_params=params,
-    )(lengths, *own_keys[:2])
+    )(*own_keys[:2])
     other_core = in_plane(lambda g, t: g * COPIES + 1 - t)
     far_keys = [lax.ppermute(keys, "seq", other_core) for keys in [pair] + own_keys[2:]]
 
     pieces = pl.pallas_call(
         functools.partial(absorb_kernel, per_device),
         out_shape=[jax.ShapeDtypeStruct((piece, width + ROPE), cache.dtype)] * per_device,
-        in_specs=[vmem] * (1 + per_device),
+        in_specs=[vmem] * 2,
         out_specs=[vmem] * per_device,
         compiler_params=params,
         cost_estimate=LONG,
-    )(w_uk, *packed)
+    )(w_uk, moved)
     arrived = [
         lax.ppermute(
             pieces[k],
             both,
-            [
-                (host(i, j, a), owner(i, j, a))
-                for i, j in devices
-                for a in [leaves_as(k, i // COPIES, j)]
-            ],
+            [(host(i, j), owner(i, j, leaves_as(k, j))) for i, j in devices],
         )
         for k in range(per_device)
     ]

time: 27.1 us -> 26.5 us (0.978)
  starting transfers between devices: 12 us -> 9.4 us
  waiting for transfers between devices: 9.52 us -> 12.1 us
  Pallas kernels: 5.3 us -> 4.75 us
    ppermute x4 -> x3, starting transfers between devices: 4.45 us -> 0.2 us  [the longest x2 0.13 us: whole_sequences(): lax.ppermute(pieces[k], both, [(host(i, j), owner(i, j, leaves_as(k, j)))...]
    ppermute x4 -> x3, waiting for transfers between devices: 0.01 us -> 2.38 us  [the longest x1 1.63 us: whole_sequences(): lax.ppermute(packed, both, [(flat(i, j), host(i, j)) for i, j in devices])]
    ppermute x3, waiting for transfers between devices: 1.49 us -> 3.53 us  [whole_sequences(): lax.ppermute(picked[k], 'seq', in_plane(lambda g, t: (g ^ partner(k, t))...]
    ppermute x2, waiting for transfers between devices: 7.73 us -> 6.18 us  [whole_sequences(): lax.ppermute(latent[k], both, [(owner(i, j, first_back(i // COPIES, j) ^...]
    ppermute x3, starting transfers between devices: 0.58 us -> 1.81 us  [whole_sequences(): lax.ppermute(keys, 'seq', other_core)]
    pallas_call x1, Pallas kernels: 0.96 us -> 0.37 us  [whole_sequences(): pl.pallas_call(pair_kernel, out_shape=jax.ShapeDtypeStruct((2, *picked[0]...]
    ppermute x2, starting transfers between devices: 3.52 us -> 3.85 us  [whole_sequences(): lax.ppermute(latent[k], both, [(owner(i, j, first_back(i // COPIES, j) ^...]
    ppermute x3, waiting for transfers between devices: 0.29 us -> 0.01 us  [whole_sequences(): lax.ppermute(keys, 'seq', other_core)]
  transfers between devices with their start and end apart: 12 -> 11, of which waited for: 6 -> 7; matrix products, arithmetic and copies ran while one was open for 0% -> 0% of each run, Pallas kernels for 8% -> 6%
where the time goes in v15:
time: 26.5 us; the launch traced here: 26.4 us
  waiting for transfers between devices  12.1 us (46%)
  starting transfers between devices  9.4 us (35%)
  Pallas kernels  4.75 us (18%)
    ppermute x2, waiting for transfers between devices, whole_sequences(): lax.ppermute(latent[k], both, [(owner(i, j, first_back(i // COPIES, j) ^...  6.18 us
    ppermute x2, starting transfers between devices, whole_sequences(): lax.ppermute(latent[k], both, [(owner(i, j, first_back(i // COPIES, j) ^...  3.85 us
    ppermute x3, starting transfers between devices, whole_sequences(): lax.ppermute(picked[k], 'seq', in_plane(lambda g, t: (g ^ partner(k, t))...  3.55 us
    ppermute x3, waiting for transfers between devices, whole_sequences(): lax.ppermute(picked[k], 'seq', in_plane(lambda g, t: (g ^ partner(k, t))...  3.53 us
    ppermute x3, starting transfers between devices, whole_sequences(): lax.ppermute(keys, 'seq', other_core)  1.81 us
    ppermute x1, waiting for transfers between devices, whole_sequences(): lax.ppermute(packed, both, [(flat(i, j), host(i, j)) for i, j in devices])  1.63 us
    pallas_call x1, Pallas kernels, whole_sequences(): pl.pallas_call(functools.partial(pick_kernel, per_device), out_shape=[jax...  1.38 us
    pallas_call x1, Pallas kernels, whole_sequences(): pl.pallas_call(functools.partial(project_kernel, per_device), out_shape=j...  1.06 us
  transfers between devices with their start and end apart: 11, of which 7 were waited for; matrix products, arithmetic and copies ran while one was open for 0% of the time, Pallas kernels for 6%

profile of v15, /device:TPU:6, one launch (start us, length us, event | category | flops | bytes accessed | tf_op | source)
XLA Modules:
  0.0 26.4 jit_solution(15085183751377672868)
XLA Ops:
  0.0 1.4 %shard_map.64 = (bf16[576,128]{1,0:T(8,128)(2,1)S(1)}, bf16[576,128]{1,0:T(8,128)(2,1)S(1)}, bf16[576,128]{1,0:T(8,128)(2,1)S(1)}, bf16[576,128]{1,0:T(8,128)(2,...) custom-call(bf16[4,576,128]{2,1,0:T(8,128)(2,1)} %bitcast.1, bf16[8,16,192]{2,1,0:T(8,128)(2,1)} %q_hbm.1, ...), custom_call_target="tpu_custom_call" | custom-call | flops 20000000000 | tf_op jit(solution)/shard_map/pallas_call | solution.py:245
  1.4 0.1 collective-permute-start
  1.5 2.0 %collective-permute-start.3 = (bf16[576,128]{1,0:T(8,128)(2,1)S(1)}, bf16[576,128]{1,0:T(8,128)(2,1)S(1)}, u32[]{:S(2)}, u32[]{:S(2)}) collective-permute-start(bf16[576,128]{1,0:T(8,128)(2,1)S(1)} %get-tuple-element.24), channel_id=1, source_target_pairs={{0,24},{4,28},{8,16},{12,20},{16,8},{20,12},{24,0},{28,4},{1,25},{... | collective-permute-start | bytes 442376 | tf_op jit(solution)/shard_map/ppermute | solution.py:265
  3.4 0.1 collective-permute-start.4
  3.5 1.5 %collective-permute-start.5 = (bf16[576,128]{1,0:T(8,128)(2,1)S(1)}, bf16[576,128]{1,0:T(8,128)(2,1)S(1)}, u32[]{:S(2)}, u32[]{:S(2)}) collective-permute-start(bf16[576,128]{1,0:T(8,128)(2,1)S(1)} %get-tuple-element.26), channel_id=1, source_target_pairs={{0,16},{4,12},{8,24},{12,4},{16,0},{20,28},{24,8},{28,20},{1,17},{... | collective-permute-start | bytes 442376 | tf_op jit(solution)/shard_map/ppermute | solution.py:265
  5.0 1.6 %collective-permute-done.packed_ref = bf16[128,256]{1,0:T(8,128)(2,1)S(1)} collective-permute-done((bf16[128,256]{1,0:T(8,128)(2,1)S(1)}, bf16[128,256]{1,0:T(8,128)(2,1)S(1)}, u32[]{:S(2)}, u32[]{:S(2)}) %collective-permute-start) | collective-permute-done | bytes 65568 | tf_op jit(solution)/shard_map/ppermute | solution.py:263
  6.7 0.5 %shard_map.65 = (bf16[64,640]{1,0:T(8,128)(2,1)S(1)}, bf16[64,640]{1,0:T(8,128)(2,1)S(1)}) custom-call(bf16[16,128,512]{2,1,0:T(8,128)(2,1)S(1)} %copy-done.1, bf16[128,256]{1,0:T(8,128)(2,1)S(1)} %collective-permute-done.packed_ref), custom_call_target="tpu_custom_call" | custom-call | flops 20000000000 | tf_op jit(solution)/shard_map/pallas_call | solution.py:279
  7.1 0.1 collective-permute-start.1
  7.2 0.1 collective-permute-start.2
  7.3 2.0 %collective-permute-done.3.refs_3_.second_ref = bf16[576,128]{1,0:T(8,128)(2,1)S(1)} collective-permute-done((bf16[576,128]{1,0:T(8,128)(2,1)S(1)}, bf16[576,128]{1,0:T(8,128)(2,1)S(1)}, u32[]{:S(2)}, u32[]{:S(2)}) %collective-permute-start.3) | collective-permute-done | bytes 147488 | tf_op jit(solution)/shard_map/ppermute | solution.py:265
  9.3 0.4 %shard_map.67 = bf16[2,576,128]{2,1,0:T(8,128)(2,1)S(1)} custom-call(bf16[576,128]{1,0:T(8,128)(2,1)S(1)} %get-tuple-element.23.refs_2_.first_ref, bf16[576,128]{1,0:T(8,128)(2,1)S(1)} %collective-permute-done.3.refs_3_.second_ref), custom_call_target="tpu_custom_call" | custom-call | tf_op jit(solution)/shard_map/pallas_call | solution.py:268
  9.7 1.3 %collective-permute-start.6 = (bf16[2,576,128]{2,1,0:T(8,128)(2,1)S(1)}, bf16[2,576,128]{2,1,0:T(8,128)(2,1)S(1)}, u32[]{:S(2)}, u32[]{:S(2)}) collective-permute-start(bf16[2,576,128]{2,1,0:T(8,128)(2,1)S(1)} %shard_map.67), channel_id=1, source_target_pairs={{0,4},{4,0},{8,12},{12,8},{16,20},{20,16},{24,28},{28,24},{1,5},{5... | collective-permute-start | bytes 884744 | tf_op jit(solution)/shard_map/ppermute | solution.py:277
  11.0 1.5 %collective-permute-done.4.refs_4_ = bf16[576,128]{1,0:T(8,128)(2,1)S(1)} collective-permute-done((bf16[576,128]{1,0:T(8,128)(2,1)S(1)}, bf16[576,128]{1,0:T(8,128)(2,1)S(1)}, u32[]{:S(2)}, u32[]{:S(2)}) %collective-permute-start.4) | collective-permute-done | bytes 147488 | tf_op jit(solution)/shard_map/ppermute | solution.py:265
  12.5 0.3 %collective-permute-start.7 = (bf16[576,128]{1,0:T(8,128)(2,1)S(1)}, bf16[576,128]{1,0:T(8,128)(2,1)S(1)}, u32[]{:S(2)}, u32[]{:S(2)}) collective-permute-start(bf16[576,128]{1,0:T(8,128)(2,1)S(1)} %collective-permute-done.4.refs_4_), channel_id=1, source_target_pairs={{0,4},{4,0},{8,12},{12,8},{16,20},{20,16},{24,28},{28,24},{1,5},{5... | collective-permute-start | bytes 442376 | tf_op jit(solution)/shard_map/ppermute | solution.py:277
  12.8 0.2 collective-permute-start.8
  13.0 0.6 %collective-permute-done.1.refs_0_ = bf16[64,640]{1,0:T(8,128)(2,1)S(1)} collective-permute-done((bf16[64,640]{1,0:T(8,128)(2,1)S(1)}, bf16[64,640]{1,0:T(8,128)(2,1)S(1)}, u32[]{:S(2)}, u32[]{:S(2)}) %collective-permute-start.1) | collective-permute-done | bytes 81952 | tf_op jit(solution)/shard_map/ppermute | solution.py:288
  13.6 0.1 collective-permute-done.2.refs_1_
  13.7 0.8 %shard_map.66 = (bf16[128,576]{1,0:T(8,128)(2,1)S(1)}, f32[128,128]{1,0:T(8,128)S(1)}, f32[128,128]{1,0:T(8,128)S(1)}, f32[128,512]{1,0:T(8,128)S(1)}) custom-call(s32[8,128]{1,0:T(8,128)S(1)} %get-tuple-element.19.limit_ref, bf16[64,640]{1,0:T(8,128)(2,1)S(1)} %collective-permute-done.1.refs_0_, bf16[64,640]{1,0:T(8,128)(2,1)S(1)} %collective-permute-done.2.refs_1_, ...), custom_call_target="tpu_custom_call" | custom-call | flops 20000000000 | tf_op jit(solution)/shard_map/pallas_call | solution.py:296
  14.5 0.7 %shard_map.68 = (bf16[64,512]{1,0:T(8,128)(2,1)S(1)}, bf16[64,512]{1,0:T(8,128)(2,1)S(1)}) custom-call(s32[8,128]{1,0:T(8,128)S(1)} %get-tuple-element.19.limit_ref, bf16[128,576]{1,0:T(8,128)(2,1)S(1)} %get-tuple-element.27.q_ref, f32[128,128]{1,0:T(8,128)S(1)} %get-tuple-element.28.top_ref, f32[128,128]{1,0:T(8,128)S(1)} %get-tuple-element.29.total_ref, ...), custom_call_target="tpu_custom_call" | custom-call | tf_op jit(solution)/shard_map/pallas_call | solution.py:309
  15.3 3.4 %collective-permute-start.10 = (bf16[64,512]{1,0:T(8,128)(2,1)S(1)}, bf16[64,512]{1,0:T(8,128)(2,1)S(1)}, u32[]{:S(2)}, u32[]{:S(2)}) collective-permute-start(bf16[64,512]{1,0:T(8,128)(2,1)S(1)} %get-tuple-element.32), channel_id=1, source_target_pairs={{4,0},{12,1},{0,2},{8,3},{20,4},{28,5},{16,6},{24,7},{5,8},{13,9},... | collective-permute-start | bytes 196616 | tf_op jit(solution)/shard_map/ppermute | solution.py:318
  18.7 0.4 %collective-permute-start.9 = (bf16[64,512]{1,0:T(8,128)(2,1)S(1)}, bf16[64,512]{1,0:T(8,128)(2,1)S(1)}, u32[]{:S(2)}, u32[]{:S(2)}) collective-permute-start(bf16[64,512]{1,0:T(8,128)(2,1)S(1)} %get-tuple-element.31), channel_id=1, source_target_pairs={{12,0},{4,1},{8,2},{0,3},{28,4},{20,5},{24,6},{16,7},{13,8},{5,9},... | collective-permute-start | bytes 196616 | tf_op jit(solution)/shard_map/ppermute | solution.py:318
  19.1 3.8 %collective-permute-done.10.refs_1_ = bf16[64,512]{1,0:T(8,128)(2,1)S(1)} collective-permute-done((bf16[64,512]{1,0:T(8,128)(2,1)S(1)}, bf16[64,512]{1,0:T(8,128)(2,1)S(1)}, u32[]{:S(2)}, u32[]{:S(2)}) %collective-permute-start.10) | collective-permute-done | bytes 65568 | tf_op jit(solution)/shard_map/ppermute | solution.py:318
  23.0 2.3 %collective-permute-done.9.refs_0_ = bf16[64,512]{1,0:T(8,128)(2,1)S(1)} collective-permute-done((bf16[64,512]{1,0:T(8,128)(2,1)S(1)}, bf16[64,512]{1,0:T(8,128)(2,1)S(1)}, u32[]{:S(2)}, u32[]{:S(2)}) %collective-permute-start.9) | collective-permute-done | bytes 65568 | tf_op jit(solution)/shard_map/ppermute | solution.py:318
  25.3 1.1 %shard_map.69 = bf16[8,16,128]{2,1,0:T(8,128)(2,1)} custom-call(bf16[16,512,128]{2,1,0:T(8,128)(2,1)S(1)} %copy-done, bf16[64,512]{1,0:T(8,128)(2,1)S(1)} %collective-permute-done.9.refs_0_, bf16[64,512]{1,0:T(8,128)(2,1)S(1)} %collective-permute-done.10.refs_1_), custom_call_target="tpu_custom_call" | custom-call | tf_op jit(solution)/shard_map/pallas_call | solution.py:325
  (8 shorter events, 0.0 us)
Async XLA Ops:
  0.0 6.7 %copy-start.1 = (bf16[16,128,512]{2,1,0:T(8,128)(2,1)S(1)}, bf16[16,128,512]{2,1,0:T(8,128)(2,1)}, u32[]{:S(2)}) copy-start(bf16[16,128,512]{2,1,0:T(8,128)(2,1)} %w_ref.2) | copy-start | bytes 6291460
  1.4 5.3 %collective-permute-start = (bf16[128,256]{1,0:T(8,128)(2,1)S(1)}, bf16[128,256]{1,0:T(8,128)(2,1)S(1)}, u32[]{:S(2)}, u32[]{:S(2)}) collective-permute-start(bf16[128,256]{1,0:T(8,128)(2,1)S(1)} %get-tuple-element.20), channel_id=1, source_target_pairs={{0,8},{1,5},{2,6},{3,11},{4,24},{5,21},{6,22},{7,27},{8,12},{9,1},... | collective-permute-start | bytes 196616 | tf_op jit(solution)/shard_map/ppermute | solution.py:263
  1.5 7.9 %collective-permute-start.3 = (bf16[576,128]{1,0:T(8,128)(2,1)S(1)}, bf16[576,128]{1,0:T(8,128)(2,1)S(1)}, u32[]{:S(2)}, u32[]{:S(2)}) collective-permute-start(bf16[576,128]{1,0:T(8,128)(2,1)S(1)} %get-tuple-element.24), channel_id=1, source_target_pairs={{0,24},{4,28},{8,16},{12,20},{16,8},{20,12},{24,0},{28,4},{1,25},{... | collective-permute-start | bytes 442376 | tf_op jit(solution)/shard_map/ppermute | solution.py:265
  3.4 9.1 %collective-permute-start.4 = (bf16[576,128]{1,0:T(8,128)(2,1)S(1)}, bf16[576,128]{1,0:T(8,128)(2,1)S(1)}, u32[]{:S(2)}, u32[]{:S(2)}) collective-permute-start(bf16[576,128]{1,0:T(8,128)(2,1)S(1)} %get-tuple-element.25), channel_id=1, source_target_pairs={{0,8},{4,20},{8,0},{12,28},{16,24},{20,4},{24,16},{28,12},{1,9},{5... | collective-permute-start | bytes 442376 | tf_op jit(solution)/shard_map/ppermute | solution.py:265
  3.5 9.3 %collective-permute-start.5 = (bf16[576,128]{1,0:T(8,128)(2,1)S(1)}, bf16[576,128]{1,0:T(8,128)(2,1)S(1)}, u32[]{:S(2)}, u32[]{:S(2)}) collective-permute-start(bf16[576,128]{1,0:T(8,128)(2,1)S(1)} %get-tuple-element.26), channel_id=1, source_target_pairs={{0,16},{4,12},{8,24},{12,4},{16,0},{20,28},{24,8},{28,20},{1,17},{... | collective-permute-start | bytes 442376 | tf_op jit(solution)/shard_map/ppermute | solution.py:265
  7.1 6.5 %collective-permute-start.1 = (bf16[64,640]{1,0:T(8,128)(2,1)S(1)}, bf16[64,640]{1,0:T(8,128)(2,1)S(1)}, u32[]{:S(2)}, u32[]{:S(2)}) collective-permute-start(bf16[64,640]{1,0:T(8,128)(2,1)S(1)} %get-tuple-element.21), channel_id=1, source_target_pairs={{8,4},{5,12},{6,0},{11,8},{24,20},{21,28},{22,16},{27,24},{12,5},{... | collective-permute-start | bytes 245768 | tf_op jit(solution)/shard_map/ppermute | solution.py:288
  7.2 6.5 %collective-permute-start.2 = (bf16[64,640]{1,0:T(8,128)(2,1)S(1)}, bf16[64,640]{1,0:T(8,128)(2,1)S(1)}, u32[]{:S(2)}, u32[]{:S(2)}) collective-permute-start(bf16[64,640]{1,0:T(8,128)(2,1)S(1)} %get-tuple-element.22), channel_id=1, source_target_pairs={{8,12},{5,4},{6,8},{11,0},{24,28},{21,20},{22,24},{27,16},{12,13},... | collective-permute-start | bytes 245768 | tf_op jit(solution)/shard_map/ppermute | solution.py:288
  9.7 4.8 %collective-permute-start.6 = (bf16[2,576,128]{2,1,0:T(8,128)(2,1)S(1)}, bf16[2,576,128]{2,1,0:T(8,128)(2,1)S(1)}, u32[]{:S(2)}, u32[]{:S(2)}) collective-permute-start(bf16[2,576,128]{2,1,0:T(8,128)(2,1)S(1)} %shard_map.67), channel_id=1, source_target_pairs={{0,4},{4,0},{8,12},{12,8},{16,20},{20,16},{24,28},{28,24},{1,5},{5... | collective-permute-start | bytes 884744 | tf_op jit(solution)/shard_map/ppermute | solution.py:277
  12.5 2.0 %collective-permute-start.7 = (bf16[576,128]{1,0:T(8,128)(2,1)S(1)}, bf16[576,128]{1,0:T(8,128)(2,1)S(1)}, u32[]{:S(2)}, u32[]{:S(2)}) collective-permute-start(bf16[576,128]{1,0:T(8,128)(2,1)S(1)} %collective-permute-done.4.refs_4_), channel_id=1, source_target_pairs={{0,4},{4,0},{8,12},{12,8},{16,20},{20,16},{24,28},{28,24},{1,5},{5... | collective-permute-start | bytes 442376 | tf_op jit(solution)/shard_map/ppermute | solution.py:277
  12.8 1.7 %collective-permute-start.8 = (bf16[576,128]{1,0:T(8,128)(2,1)S(1)}, bf16[576,128]{1,0:T(8,128)(2,1)S(1)}, u32[]{:S(2)}, u32[]{:S(2)}) collective-permute-start(bf16[576,128]{1,0:T(8,128)(2,1)S(1)} %collective-permute-done.5.refs_5_), channel_id=1, source_target_pairs={{0,4},{4,0},{8,12},{12,8},{16,20},{20,16},{24,28},{28,24},{1,5},{5... | collective-permute-start | bytes 442376 | tf_op jit(solution)/shard_map/ppermute | solution.py:277
  13.7 11.6 %copy-start = (bf16[16,512,128]{2,1,0:T(8,128)(2,1)S(1)}, bf16[16,512,128]{2,1,0:T(8,128)(2,1)}, u32[]{:S(2)}) copy-start(bf16[16,512,128]{2,1,0:T(8,128)(2,1)} %w_ref.3) | copy-start | bytes 6291460
  15.3 7.7 %collective-permute-start.10 = (bf16[64,512]{1,0:T(8,128)(2,1)S(1)}, bf16[64,512]{1,0:T(8,128)(2,1)S(1)}, u32[]{:S(2)}, u32[]{:S(2)}) collective-permute-start(bf16[64,512]{1,0:T(8,128)(2,1)S(1)} %get-tuple-element.32), channel_id=1, source_target_pairs={{4,0},{12,1},{0,2},{8,3},{20,4},{28,5},{16,6},{24,7},{5,8},{13,9},... | collective-permute-start | bytes 196616 | tf_op jit(solution)/shard_map/ppermute | solution.py:318
  18.7 6.6 %collective-permute-start.9 = (bf16[64,512]{1,0:T(8,128)(2,1)S(1)}, bf16[64,512]{1,0:T(8,128)(2,1)S(1)}, u32[]{:S(2)}, u32[]{:S(2)}) collective-permute-start(bf16[64,512]{1,0:T(8,128)(2,1)S(1)} %get-tuple-element.31), channel_id=1, source_target_pairs={{12,0},{4,1},{8,2},{0,3},{28,4},{20,5},{24,6},{16,7},{13,8},{5,9},... | collective-permute-start | bytes 196616 | tf_op jit(solution)/shard_map/ppermute | solution.py:318

commit v16 on v15

--- a/solution.py
+++ b/solution.py
@@ -41,38 +41,41 @@
     return (0, 3, 1 ^ 3 * core, 2 ^ 3 * core)[k]
 
 
-def pick_kernel(per_device, cache_hbm, q_hbm, new_hbm, len_hbm, *refs):
-    owners = cache_hbm.shape[0]
-    blocks, (out_ref, limit_ref, q_ref, new_ref, len_ref, sem) = refs[:owners], refs[owners:]
+def pick_kernel(per_device, cache_hbm, new_hbm, len_hbm, *refs):
+    owners, width, slots = cache_hbm.shape
+    blocks, (limit_ref, new_ref, len_ref, sem) = refs[:owners], refs[owners:]
     chip, core = lax.axis_index("seq") // COPIES, lax.axis_index("seq") % COPIES
+    takers = [chip ^ partner(k, core) for k in range(owners)]
     moves = [
-        pltpu.make_async_copy(q_hbm, q_ref, sem.at[owners]),
-        pltpu.make_async_copy(new_hbm, new_ref, sem.at[owners + 1]),
-        pltpu.make_async_copy(len_hbm, len_ref, sem.at[owners + 2]),
+        pltpu.make_async_copy(new_hbm, new_ref, sem.at[owners]),
+        pltpu.make_async_copy(len_hbm, len_ref, sem.at[owners + 1]),
     ] + [
-        pltpu.make_async_copy(cache_hbm.at[chip ^ partner(k, core)], blocks[k], sem.at[k])
+        pltpu.make_async_copy(cache_hbm.at[takers[k]], blocks[k].at[pl.ds(0, width)], sem.at[k])
         for k in range(owners)
     ]
     for move in moves:
         move.start()
     moves[0].wait()
+    fresh = new_ref[...].astype(jnp.float32)
+    spare = -width % slots
+    if spare:
+        fresh = jnp.concatenate([fresh, jnp.zeros((fresh.shape[0], spare), jnp.float32)], axis=1)
+    below = []
+    for a in range(per_device):
+        parts = [
+            fresh[a * SPEC : (a + 1) * SPEC, n : n + slots] for n in range(0, width, slots)
+        ]
+        spare = blocks[0].shape[0] - width - SPEC * len(parts)
+        if spare:
+            parts.append(jnp.zeros((spare, slots), jnp.float32))
+        below.append(jnp.concatenate(parts, axis=0))
+    for k in range(owners):
+        rows = jnp.where(takers[k] % per_device == 0, below[0], below[1])
+        blocks[k][width:, :] = rows.astype(blocks[k].dtype)
     moves[1].wait()
-    heads, width = q_ref.shape[1:]
-    fresh = new_ref[...].astype(jnp.float32)
-    piece = SPEC * heads
-    for a in range(per_device):
-        rows = q_ref[a * SPEC : (a + 1) * SPEC].reshape(piece, width)
-        own = fresh[a * SPEC : (a + 1) * SPEC]
-        parts = [own[:, n : n + ROPE] for n in range(0, own.shape[1], ROPE)]
-        spare = piece - SPEC * len(parts)
-        if spare:
-            parts.append(jnp.zeros((spare, ROPE), jnp.float32))
-        own = jnp.concatenate(parts, axis=0).astype(rows.dtype)
-        out_ref[a * piece : (a + 1) * piece] = jnp.concatenate([rows, own], axis=1)
-    moves[2].wait()
     length = len_ref[lax.axis_index("head") * owners + chip]
     limit_ref[...] = jnp.full(limit_ref.shape, length, limit_ref.dtype)
-    for move in moves[3:]:
+    for move in moves[2:]:
         move.wait()
 
 
@@ -87,10 +90,11 @@
         move.wait()
 
 
-def absorb_kernel(per_device, w_ref, packed_ref, *outs):
-    heads = w_ref.shape[0]
+def absorb_kernel(per_device, w_ref, q_ref, *outs):
+    rows, heads, width = q_ref.shape
     piece = SPEC * heads
-    nope = packed_ref[:, :NOPE]
+    q = q_ref[...].reshape(rows * heads, width)
+    nope = q[:, :NOPE]
     own_head = lax.broadcasted_iota(jnp.int32, nope.shape, 0) % heads
     spread = jnp.concatenate(
         [jnp.where(own_head == h, nope, jnp.zeros_like(nope)) for h in range(heads)], axis=1
@@ -104,9 +108,8 @@
 
             @pl.when(which == a)
             def _():
-                rows = slice(a * piece, (a + 1) * piece)
-                outs[k][:, :LATENT] = absorbed[rows]
-                outs[k][:, LATENT:] = packed_ref[rows, NOPE:]
+                outs[k][:, :LATENT] = absorbed[a * piece : (a + 1) * piece]
+                outs[k][:, LATENT:] = q[a * piece : (a + 1) * piece, NOPE:]
 
 
 def block_scores(q, refs, starts, limit_ref):
@@ -131,19 +134,46 @@
     return jnp.sum(w, axis=1, keepdims=True), out
 
 
-def begin_kernel(owners, per_device, heads, limit_ref, *refs):
+def begin_kernel(owners, per_device, limit_ref, *refs):
     q_refs, key_refs = refs[:per_device], refs[per_device : per_device + owners]
     q_out, top_ref, total_ref, out_ref = refs[per_device + owners :]
     seq_index = lax.axis_index("seq")
     chip, core = seq_index // COPIES, seq_index % COPIES
     slots = key_refs[0].shape[1]
-    width = LATENT + ROPE
-    q = jnp.concatenate([ref[:, :width] for ref in q_refs], axis=0)
-
-    fresh = q_refs[0][:, width:].astype(jnp.float32)
-    fresh = jnp.concatenate(
-        [fresh[n * SPEC : (n + 1) * SPEC] for n in range(width // ROPE)], axis=1
-    )
+    q = jnp.concatenate([ref[...] for ref in q_refs], axis=0)
+    starts = [((chip ^ partner(k, core)) * COPIES + core) * slots for k in range(owners)]
+    s = block_scores(q, key_refs, starts, limit_ref)
+    top = jnp.max(s, axis=1, keepdims=True)
+    total, out = weigh(s, key_refs, top)
+    q_out[...] = q
+    top_ref[...] = jnp.broadcast_to(top, top_ref.shape)
+    total_ref[...] = jnp.broadcast_to(total, total_ref.shape)
+    out_ref[...] = out
+
+
+def finish_kernel(
+    owners, per_device, heads, limit_ref, q_ref, top_ref, total_ref, part_ref, *refs
+):
+    own_refs, (pair_ref, *far_refs) = refs[:owners], refs[owners : 2 * owners - 1]
+    far_refs = [pair_ref.at[0], pair_ref.at[1], *far_refs]
+    outs, fresh_ref = refs[2 * owners - 1 : -1], refs[-1]
+    seq_index = lax.axis_index("seq")
+    chip, core = seq_index // COPIES, seq_index % COPIES
+    plane = lax.axis_index("head")
+    q = q_ref[...]
+    width, slots = q.shape[1], pair_ref.shape[2]
+
+    for key_refs, source_core in ((own_refs, core), (far_refs, 1 - core)):
+        for k in range(owners):
+            source = chip ^ partner(k, source_core)
+
+            @pl.when((source == plane) & (source_core == chip // per_device))
+            def _():
+                fresh_ref[...] = key_refs[k][width:, :]
+
+    fresh = fresh_ref[...].astype(jnp.float32)
+    parts = [fresh[n * SPEC : (n + 1) * SPEC] for n in range(-(-width // slots))]
+    fresh = jnp.concatenate(parts, axis=1)[:, :width]
     fresh = jnp.concatenate([fresh, jnp.zeros((16 - SPEC, width), jnp.float32)], axis=0)
     fresh = fresh.astype(jnp.bfloat16)
     f = lax.dot_general(
@@ -153,38 +183,20 @@
     key = lax.broadcasted_iota(jnp.int32, f.shape, 1)
     f = jnp.where(key <= row // heads, f * SCORE_SCALE, masked_value)
 
-    starts = [((chip ^ partner(k, core)) * COPIES + core) * slots for k in range(owners)]
-    s = block_scores(q, key_refs, starts, limit_ref)
-    top = jnp.maximum(jnp.max(s, axis=1, keepdims=True), jnp.max(f, axis=1, keepdims=True))
-    total, out = weigh(s, key_refs, top)
+    starts = [((chip ^ partner(k, 1 - core)) * COPIES + 1 - core) * slots for k in range(owners)]
+    s = block_scores(q, far_refs, starts, limit_ref)
+    first = top_ref[:, :1]
+    top = jnp.maximum(
+        jnp.maximum(first, jnp.max(f, axis=1, keepdims=True)), jnp.max(s, axis=1, keepdims=True)
+    )
+    total, out = weigh(s, far_refs, top)
     w = jnp.exp(f - top)
-    total += jnp.sum(w, axis=1, keepdims=True)
+    scale = jnp.exp(first - top)
+    total += jnp.sum(w, axis=1, keepdims=True) + total_ref[:, :1] * scale
+    out += part_ref[...] * scale
     out += jnp.dot(
         w.astype(jnp.bfloat16), fresh[:, :LATENT], preferred_element_type=jnp.float32
     )
-    q_out[...] = q
-    top_ref[...] = jnp.broadcast_to(top, top_ref.shape)
-    total_ref[...] = jnp.broadcast_to(total, total_ref.shape)
-    out_ref[...] = out
-
-
-def finish_kernel(
-    owners, per_device, limit_ref, q_ref, top_ref, total_ref, part_ref, pair_ref, *refs
-):
-    key_refs = [pair_ref.at[0], pair_ref.at[1], *refs[: owners - 2]]
-    outs = refs[owners - 2 :]
-    seq_index = lax.axis_index("seq")
-    chip, core = seq_index // COPIES, seq_index % COPIES
-    plane = lax.axis_index("head")
-    slots = key_refs[0].shape[1]
-    starts = [((chip ^ partner(k, 1 - core)) * COPIES + 1 - core) * slots for k in range(owners)]
-    s = block_scores(q_ref[...], key_refs, starts, limit_ref)
-    first = top_ref[:, :1]
-    top = jnp.maximum(first, jnp.max(s, axis=1, keepdims=True))
-    total, out = weigh(s, key_refs, top)
-    scale = jnp.exp(first - top)
-    total += total_ref[:, :1] * scale
-    out += part_ref[...] * scale
     out = (out * (1.0 / total)).astype(jnp.bfloat16)
     piece = out.shape[0] // per_device
     sent_first = first_block(plane, chip, core)
@@ -214,7 +226,7 @@
 
 
 def whole_sequences(seq_size, head_size, queries, new_latent, cache, lengths, w_uk, w_uv):
-    rows, heads, q_width = queries.shape
+    rows, heads, _ = queries.shape
     owners, slots, width = cache.shape
     per_device = rows // SPEC
     piece = SPEC * heads
@@ -242,25 +254,22 @@
     def in_plane(move):
         return [(g * COPIES + t, move(g, t)) for g in range(owners) for t in range(COPIES)]
 
-    *picked, packed, limit = pl.pallas_call(
+    moved = lax.ppermute(queries, both, [(flat(i, j), host(i, j)) for i, j in devices])
+    below = -(-SPEC * -(-width // slots) // 16) * 16
+    *picked, limit = pl.pallas_call(
         functools.partial(pick_kernel, per_device),
-        out_shape=[jax.ShapeDtypeStruct((width, slots), cache.dtype)] * owners
-        + [
-            jax.ShapeDtypeStruct((all_rows, q_width + ROPE), queries.dtype),
-            jax.ShapeDtypeStruct((8, slots), jnp.int32),
-        ],
-        in_specs=[anywhere] * 4,
-        out_specs=[vmem] * (owners + 2),
+        out_shape=[jax.ShapeDtypeStruct((width + below, slots), cache.dtype)] * owners
+        + [jax.ShapeDtypeStruct((8, slots), jnp.int32)],
+        in_specs=[anywhere] * 3,
+        out_specs=[vmem] * (owners + 1),
         scratch_shapes=[
-            pltpu.VMEM(queries.shape, queries.dtype),
             pltpu.VMEM(new_latent.shape, new_latent.dtype),
             pltpu.SMEM(lengths.shape, lengths.dtype),
-            pltpu.SemaphoreType.DMA((owners + 3,)),
+            pltpu.SemaphoreType.DMA((owners + 2,)),
         ],
         compiler_params=params,
         cost_estimate=LONG,
-    )(*[in_hbm(x) for x in (jnp.swapaxes(cache, 1, 2), queries, new_latent, lengths)])
-    moved = lax.ppermute(packed, both, [(flat(i, j), host(i, j)) for i, j in devices])
+    )(*[in_hbm(x) for x in (jnp.swapaxes(cache, 1, 2), new_latent, lengths)])
     own_keys = [picked[0]] + [
         lax.ppermute(picked[k], "seq", in_plane(lambda g, t: (g ^ partner(k, t)) * COPIES + t))
         for k in range(1, owners)
@@ -278,7 +287,7 @@
 
     pieces = pl.pallas_call(
         functools.partial(absorb_kernel, per_device),
-        out_shape=[jax.ShapeDtypeStruct((piece, width + ROPE), cache.dtype)] * per_device,
+        out_shape=[jax.ShapeDtypeStruct((piece, width), cache.dtype)] * per_device,
         in_specs=[vmem] * 2,
         out_specs=[vmem] * per_device,
         compiler_params=params,
@@ -294,7 +303,7 @@
     ]
 
     state = pl.pallas_call(
-        functools.partial(begin_kernel, owners, per_device, heads),
+        functools.partial(begin_kernel, owners, per_device),
         out_shape=[
             jax.ShapeDtypeStruct((all_rows, width), jnp.bfloat16),
             jax.ShapeDtypeStruct((all_rows, 128), jnp.float32),
@@ -307,12 +316,13 @@
         cost_estimate=LONG,
     )(limit, *arrived, *own_keys)
     latent = pl.pallas_call(
-        functools.partial(finish_kernel, owners, per_device),
+        functools.partial(finish_kernel, owners, per_device, heads),
         out_shape=[jax.ShapeDtypeStruct((piece, LATENT), jnp.bfloat16)] * per_device,
-        in_specs=[vmem] * (1 + len(state) + len(far_keys)),
+        in_specs=[vmem] * (1 + len(state) + len(own_keys) + len(far_keys)),
         out_specs=[vmem] * per_device,
-        compiler_params=params,
-    )(limit, *state, *far_keys)
+        scratch_shapes=[pltpu.VMEM((below, slots), cache.dtype)],
+        compiler_params=params,
+    )(limit, *state, *own_keys, *far_keys)
 
     back = [
         lax.ppermute(

time: 26.5 us -> 27.8 us (1.049)
  waiting for transfers between devices: 12.1 us -> 13.4 us
    ppermute x3, waiting for transfers between devices: 3.53 us -> 5.88 us  [whole_sequences(): lax.ppermute(picked[k], 'seq', in_plane(lambda g, t: (g ^ partner(k, t))...]
    ppermute x1, waiting for transfers between devices: 1.63 us -> 0.21 us  [whole_sequences(): lax.ppermute(queries, both, [(flat(i, j), host(i, j)) for i, j in devices])]
    ppermute x3, starting transfers between devices: 1.81 us -> 0.58 us  [whole_sequences(): lax.ppermute(keys, 'seq', other_core)]
    ppermute x2, starting transfers between devices: 0.13 us -> 1.32 us  [whole_sequences(): lax.ppermute(pieces[k], both, [(host(i, j), owner(i, j, leaves_as(k, j)))...]
    ppermute x2, waiting for transfers between devices: 0.74 us -> 0.01 us  [whole_sequences(): lax.ppermute(pieces[k], both, [(host(i, j), owner(i, j, leaves_as(k, j)))...]
    ppermute x2, waiting for transfers between devices: 6.18 us -> 6.79 us  [whole_sequences(): lax.ppermute(latent[k], both, [(owner(i, j, first_back(i // COPIES, j) ^...]
    ppermute x3, waiting for transfers between devices: 0.01 us -> 0.49 us  [whole_sequences(): lax.ppermute(keys, 'seq', other_core)]
  transfers between devices with their start and end apart: 11 -> 11, of which waited for: 7 -> 7; matrix products, arithmetic and copies ran while one was open for 0% -> 0% of each run, Pallas kernels for 6% -> 10%
where the time goes in v16:
time: 27.8 us; the launch traced here: 27.7 us
  waiting for transfers between devices  13.4 us (48%)
  starting transfers between devices  9.55 us (34%)
  Pallas kernels  4.7 us (17%)
    ppermute x2, waiting for transfers between devices, whole_sequences(): lax.ppermute(latent[k], both, [(owner(i, j, first_back(i // COPIES, j) ^...  6.79 us
    ppermute x3, waiting for transfers between devices, whole_sequences(): lax.ppermute(picked[k], 'seq', in_plane(lambda g, t: (g ^ partner(k, t))...  5.88 us
    ppermute x2, starting transfers between devices, whole_sequences(): lax.ppermute(latent[k], both, [(owner(i, j, first_back(i // COPIES, j) ^...  4.1 us
    ppermute x3, starting transfers between devices, whole_sequences(): lax.ppermute(picked[k], 'seq', in_plane(lambda g, t: (g ^ partner(k, t))...  3.55 us
    pallas_call x1, Pallas kernels, whole_sequences(): pl.pallas_call(functools.partial(pick_kernel, per_device), out_shape=[jax...  1.34 us
    ppermute x2, starting transfers between devices, whole_sequences(): lax.ppermute(pieces[k], both, [(host(i, j), owner(i, j, leaves_as(k, j)))...  1.32 us
    pallas_call x1, Pallas kernels, whole_sequences(): pl.pallas_call(functools.partial(project_kernel, per_device), out_shape=j...  1.07 us
    pallas_call x1, Pallas kernels, whole_sequences(): pl.pallas_call(functools.partial(finish_kernel, owners, per_device, heads...  0.84 us
  transfers between devices with their start and end apart: 11, of which 7 were waited for; matrix products, arithmetic and copies ran while one was open for 0% of the time, Pallas kernels for 10%

profile of v16, /device:TPU:6, one launch (start us, length us, event | category | flops | bytes accessed | tf_op | source)
XLA Modules:
  0.0 27.7 jit_solution(10475893618065818912)
XLA Ops:
  0.0 0.0 collective-permute-start
  0.0 1.3 %shard_map.64 = (bf16[608,128]{1,0:T(8,128)(2,1)S(1)}, bf16[608,128]{1,0:T(8,128)(2,1)S(1)}, bf16[608,128]{1,0:T(8,128)(2,1)S(1)}, bf16[608,128]{1,0:T(8,128)(2,1)S(1)}, s32[8,128]{1,0:T(8,128)S(1)}) custom-call(bf16[4,576,128]{2,1,0:T(8,128)(2,1)} %bitcast.1, bf16[8,576]{1,0:T(8,128)(2,1)} %new_hbm.1, s32[16]{0:T(128)} %len_hbm.1), custom_call_target="tpu_custom_call" | custom-call | flops 20000000000 | tf_op jit(solution)/shard_map/pallas_call | solution.py:259
  1.4 2.0 %collective-permute-start.3 = (bf16[608,128]{1,0:T(8,128)(2,1)S(1)}, bf16[608,128]{1,0:T(8,128)(2,1)S(1)}, u32[]{:S(2)}, u32[]{:S(2)}) collective-permute-start(bf16[608,128]{1,0:T(8,128)(2,1)S(1)} %get-tuple-element.22), channel_id=1, source_target_pairs={{0,24},{4,28},{8,16},{12,20},{16,8},{20,12},{24,0},{28,4},{1,25},{... | collective-permute-start | bytes 466952 | tf_op jit(solution)/shard_map/ppermute | solution.py:274
  3.4 0.0 collective-permute-start.4
  3.4 1.5 %collective-permute-start.5 = (bf16[608,128]{1,0:T(8,128)(2,1)S(1)}, bf16[608,128]{1,0:T(8,128)(2,1)S(1)}, u32[]{:S(2)}, u32[]{:S(2)}) collective-permute-start(bf16[608,128]{1,0:T(8,128)(2,1)S(1)} %get-tuple-element.24), channel_id=1, source_target_pairs={{0,16},{4,12},{8,24},{12,4},{16,0},{20,28},{24,8},{28,20},{1,17},{... | collective-permute-start | bytes 466952 | tf_op jit(solution)/shard_map/ppermute | solution.py:274
  4.9 0.2 collective-permute-done.q_ref
  5.1 0.5 %shard_map.65 = (bf16[64,576]{1,0:T(8,128)(2,1)S(1)}, bf16[64,576]{1,0:T(8,128)(2,1)S(1)}) custom-call(bf16[16,128,512]{2,1,0:T(8,128)(2,1)S(1)} %copy-done.1, bf16[8,16,192]{2,1,0:T(8,128)(2,1)S(1)} %collective-permute-done.q_ref), custom_call_target="tpu_custom_call" | custom-call | flops 20000000000 | tf_op jit(solution)/shard_map/pallas_call | solution.py:288
  5.6 0.5 %collective-permute-start.1 = (bf16[64,576]{1,0:T(8,128)(2,1)S(1)}, bf16[64,576]{1,0:T(8,128)(2,1)S(1)}, u32[]{:S(2)}, u32[]{:S(2)}) collective-permute-start(bf16[64,576]{1,0:T(8,128)(2,1)S(1)} %get-tuple-element.19), channel_id=1, source_target_pairs={{8,4},{5,12},{6,0},{11,8},{24,20},{21,28},{22,16},{27,24},{12,5},{... | collective-permute-start | bytes 221192 | tf_op jit(solution)/shard_map/ppermute | solution.py:297
  6.1 0.8 %collective-permute-start.2 = (bf16[64,576]{1,0:T(8,128)(2,1)S(1)}, bf16[64,576]{1,0:T(8,128)(2,1)S(1)}, u32[]{:S(2)}, u32[]{:S(2)}) collective-permute-start(bf16[64,576]{1,0:T(8,128)(2,1)S(1)} %get-tuple-element.20), channel_id=1, source_target_pairs={{8,12},{5,4},{6,8},{11,0},{24,28},{21,20},{22,24},{27,16},{12,13},... | collective-permute-start | bytes 221192 | tf_op jit(solution)/shard_map/ppermute | solution.py:297
  6.9 2.2 %collective-permute-done.3.refs_3_.second_ref.refs_1_ = bf16[608,128]{1,0:T(8,128)(2,1)S(1)} collective-permute-done((bf16[608,128]{1,0:T(8,128)(2,1)S(1)}, bf16[608,128]{1,0:T(8,128)(2,1)S(1)}, u32[]{:S(2)}, u32[]{:S(2)}) %collective-permute-start.3) | collective-permute-done | bytes 155680 | tf_op jit(solution)/shard_map/ppermute | solution.py:274
  9.2 0.4 %shard_map.67 = bf16[2,608,128]{2,1,0:T(8,128)(2,1)S(1)} custom-call(bf16[608,128]{1,0:T(8,128)(2,1)S(1)} %get-tuple-element.21.refs_2_.first_ref.refs_0_, bf16[608,128]{1,0:T(8,128)(2,1)S(1)} %collective-permute-done.3.refs_3_.second_ref.refs_1_), custom_call_target="tpu_custom_call" | custom-call | tf_op jit(solution)/shard_map/pallas_call | solution.py:277
  9.6 0.1 collective-permute-start.6
  9.6 3.7 %collective-permute-done.4.refs_4_.refs_2_ = bf16[608,128]{1,0:T(8,128)(2,1)S(1)} collective-permute-done((bf16[608,128]{1,0:T(8,128)(2,1)S(1)}, bf16[608,128]{1,0:T(8,128)(2,1)S(1)}, u32[]{:S(2)}, u32[]{:S(2)}) %collective-permute-start.4) | collective-permute-done | bytes 155680 | tf_op jit(solution)/shard_map/ppermute | solution.py:274
  13.3 0.0 collective-permute-start.7
  13.3 0.5 %collective-permute-start.8 = (bf16[608,128]{1,0:T(8,128)(2,1)S(1)}, bf16[608,128]{1,0:T(8,128)(2,1)S(1)}, u32[]{:S(2)}, u32[]{:S(2)}) collective-permute-start(bf16[608,128]{1,0:T(8,128)(2,1)S(1)} %collective-permute-done.5.refs_5_.refs_3_), channel_id=1, source_target_pairs={{0,4},{4,0},{8,12},{12,8},{16,20},{20,16},{24,28},{28,24},{1,5},{5... | collective-permute-start | bytes 466952 | tf_op jit(solution)/shard_map/ppermute | solution.py:286
  13.8 0.6 %shard_map.66 = (bf16[128,576]{1,0:T(8,128)(2,1)S(1)}, f32[128,128]{1,0:T(8,128)S(1)}, f32[128,128]{1,0:T(8,128)S(1)}, f32[128,512]{1,0:T(8,128)S(1)}) custom-call(s32[8,128]{1,0:T(8,128)S(1)} %get-tuple-element.18.limit_ref, bf16[64,576]{1,0:T(8,128)(2,1)S(1)} %collective-permute-done.1.refs_0_, bf16[64,576]{1,0:T(8,128)(2,1)S(1)} %collective-permute-done.2.refs_1_, ...), custom_call_target="tpu_custom_call" | custom-call | flops 20000000000 | tf_op jit(solution)/shard_map/pallas_call | solution.py:305
  14.4 0.3 collective-permute-done.7.refs_5_
  14.7 0.2 collective-permute-done.8.refs_6_
  14.9 0.8 %shard_map.68 = (bf16[64,512]{1,0:T(8,128)(2,1)S(1)}, bf16[64,512]{1,0:T(8,128)(2,1)S(1)}) custom-call(s32[8,128]{1,0:T(8,128)S(1)} %get-tuple-element.18.limit_ref, bf16[128,576]{1,0:T(8,128)(2,1)S(1)} %get-tuple-element.25.q_ref, f32[128,128]{1,0:T(8,128)S(1)} %get-tuple-element.26.top_ref, f32[128,128]{1,0:T(8,128)S(1)} %get-tuple-element.27.total_ref, ...), custom_call_target="tpu_custom_call" | custom-call | tf_op jit(solution)/shard_map/pallas_call | solution.py:318
  15.7 4.1 %collective-permute-start.10 = (bf16[64,512]{1,0:T(8,128)(2,1)S(1)}, bf16[64,512]{1,0:T(8,128)(2,1)S(1)}, u32[]{:S(2)}, u32[]{:S(2)}) collective-permute-start(bf16[64,512]{1,0:T(8,128)(2,1)S(1)} %get-tuple-element.30), channel_id=1, source_target_pairs={{4,0},{12,1},{0,2},{8,3},{20,4},{28,5},{16,6},{24,7},{5,8},{13,9},... | collective-permute-start | bytes 196616 | tf_op jit(solution)/shard_map/ppermute | solution.py:328
  19.8 0.0 collective-permute-start.9
  19.8 3.2 %collective-permute-done.10.refs_1_ = bf16[64,512]{1,0:T(8,128)(2,1)S(1)} collective-permute-done((bf16[64,512]{1,0:T(8,128)(2,1)S(1)}, bf16[64,512]{1,0:T(8,128)(2,1)S(1)}, u32[]{:S(2)}, u32[]{:S(2)}) %collective-permute-start.10) | collective-permute-done | bytes 65568 | tf_op jit(solution)/shard_map/ppermute | solution.py:328
  23.1 3.5 %collective-permute-done.9.refs_0_ = bf16[64,512]{1,0:T(8,128)(2,1)S(1)} collective-permute-done((bf16[64,512]{1,0:T(8,128)(2,1)S(1)}, bf16[64,512]{1,0:T(8,128)(2,1)S(1)}, u32[]{:S(2)}, u32[]{:S(2)}) %collective-permute-start.9) | collective-permute-done | bytes 65568 | tf_op jit(solution)/shard_map/ppermute | solution.py:328
  26.6 1.1 %shard_map.69 = bf16[8,16,128]{2,1,0:T(8,128)(2,1)} custom-call(bf16[16,512,128]{2,1,0:T(8,128)(2,1)S(1)} %copy-done, bf16[64,512]{1,0:T(8,128)(2,1)S(1)} %collective-permute-done.9.refs_0_, bf16[64,512]{1,0:T(8,128)(2,1)S(1)} %collective-permute-done.10.refs_1_), custom_call_target="tpu_custom_call" | custom-call | tf_op jit(solution)/shard_map/pallas_call | solution.py:335
  (8 shorter events, 0.0 us)
Async XLA Ops:
  0.0 5.1 %collective-permute-start = (bf16[8,16,192]{2,1,0:T(8,128)(2,1)}, bf16[8,16,192]{2,1,0:T(8,128)(2,1)S(1)}, u32[]{:S(2)}, u32[]{:S(2)}) collective-permute-start(bf16[8,16,192]{2,1,0:T(8,128)(2,1)} %param.6), channel_id=1, source_target_pairs={{0,8},{1,5},{2,6},{3,11},{4,24},{5,21},{6,22},{7,27},{8,12},{9,1},... | collective-permute-start | bytes 147464 | tf_op jit(solution)/shard_map/ppermute | solution.py:257
  0.0 5.1 %copy-start.1 = (bf16[16,128,512]{2,1,0:T(8,128)(2,1)S(1)}, bf16[16,128,512]{2,1,0:T(8,128)(2,1)}, u32[]{:S(2)}) copy-start(bf16[16,128,512]{2,1,0:T(8,128)(2,1)} %w_ref.2) | copy-start | bytes 6291460
  1.4 7.8 %collective-permute-start.3 = (bf16[608,128]{1,0:T(8,128)(2,1)S(1)}, bf16[608,128]{1,0:T(8,128)(2,1)S(1)}, u32[]{:S(2)}, u32[]{:S(2)}) collective-permute-start(bf16[608,128]{1,0:T(8,128)(2,1)S(1)} %get-tuple-element.22), channel_id=1, source_target_pairs={{0,24},{4,28},{8,16},{12,20},{16,8},{20,12},{24,0},{28,4},{1,25},{... | collective-permute-start | bytes 466952 | tf_op jit(solution)/shard_map/ppermute | solution.py:274
  3.4 9.9 %collective-permute-start.4 = (bf16[608,128]{1,0:T(8,128)(2,1)S(1)}, bf16[608,128]{1,0:T(8,128)(2,1)S(1)}, u32[]{:S(2)}, u32[]{:S(2)}) collective-permute-start(bf16[608,128]{1,0:T(8,128)(2,1)S(1)} %get-tuple-element.23), channel_id=1, source_target_pairs={{0,8},{4,20},{8,0},{12,28},{16,24},{20,4},{24,16},{28,12},{1,9},{5... | collective-permute-start | bytes 466952 | tf_op jit(solution)/shard_map/ppermute | solution.py:274
  3.4 9.9 %collective-permute-start.5 = (bf16[608,128]{1,0:T(8,128)(2,1)S(1)}, bf16[608,128]{1,0:T(8,128)(2,1)S(1)}, u32[]{:S(2)}, u32[]{:S(2)}) collective-permute-start(bf16[608,128]{1,0:T(8,128)(2,1)S(1)} %get-tuple-element.24), channel_id=1, source_target_pairs={{0,16},{4,12},{8,24},{12,4},{16,0},{20,28},{24,8},{28,20},{1,17},{... | collective-permute-start | bytes 466952 | tf_op jit(solution)/shard_map/ppermute | solution.py:274
  5.6 8.2 %collective-permute-start.1 = (bf16[64,576]{1,0:T(8,128)(2,1)S(1)}, bf16[64,576]{1,0:T(8,128)(2,1)S(1)}, u32[]{:S(2)}, u32[]{:S(2)}) collective-permute-start(bf16[64,576]{1,0:T(8,128)(2,1)S(1)} %get-tuple-element.19), channel_id=1, source_target_pairs={{8,4},{5,12},{6,0},{11,8},{24,20},{21,28},{22,16},{27,24},{12,5},{... | collective-permute-start | bytes 221192 | tf_op jit(solution)/shard_map/ppermute | solution.py:297
  6.1 7.7 %collective-permute-start.2 = (bf16[64,576]{1,0:T(8,128)(2,1)S(1)}, bf16[64,576]{1,0:T(8,128)(2,1)S(1)}, u32[]{:S(2)}, u32[]{:S(2)}) collective-permute-start(bf16[64,576]{1,0:T(8,128)(2,1)S(1)} %get-tuple-element.20), channel_id=1, source_target_pairs={{8,12},{5,4},{6,8},{11,0},{24,28},{21,20},{22,24},{27,16},{12,13},... | collective-permute-start | bytes 221192 | tf_op jit(solution)/shard_map/ppermute | solution.py:297
  9.6 5.3 %collective-permute-start.6 = (bf16[2,608,128]{2,1,0:T(8,128)(2,1)S(1)}, bf16[2,608,128]{2,1,0:T(8,128)(2,1)S(1)}, u32[]{:S(2)}, u32[]{:S(2)}) collective-permute-start(bf16[2,608,128]{2,1,0:T(8,128)(2,1)S(1)} %shard_map.67), channel_id=1, source_target_pairs={{0,4},{4,0},{8,12},{12,8},{16,20},{20,16},{24,28},{28,24},{1,5},{5... | collective-permute-start | bytes 933896 | tf_op jit(solution)/shard_map/ppermute | solution.py:286
  13.3 1.4 %collective-permute-start.7 = (bf16[608,128]{1,0:T(8,128)(2,1)S(1)}, bf16[608,128]{1,0:T(8,128)(2,1)S(1)}, u32[]{:S(2)}, u32[]{:S(2)}) collective-permute-start(bf16[608,128]{1,0:T(8,128)(2,1)S(1)} %collective-permute-done.4.refs_4_.refs_2_), channel_id=1, source_target_pairs={{0,4},{4,0},{8,12},{12,8},{16,20},{20,16},{24,28},{28,24},{1,5},{5... | collective-permute-start | bytes 466952 | tf_op jit(solution)/shard_map/ppermute | solution.py:286
  13.3 1.6 %collective-permute-start.8 = (bf16[608,128]{1,0:T(8,128)(2,1)S(1)}, bf16[608,128]{1,0:T(8,128)(2,1)S(1)}, u32[]{:S(2)}, u32[]{:S(2)}) collective-permute-start(bf16[608,128]{1,0:T(8,128)(2,1)S(1)} %collective-permute-done.5.refs_5_.refs_3_), channel_id=1, source_target_pairs={{0,4},{4,0},{8,12},{12,8},{16,20},{20,16},{24,28},{28,24},{1,5},{5... | collective-permute-start | bytes 466952 | tf_op jit(solution)/shard_map/ppermute | solution.py:286
  13.8 12.8 %copy-start = (bf16[16,512,128]{2,1,0:T(8,128)(2,1)S(1)}, bf16[16,512,128]{2,1,0:T(8,128)(2,1)}, u32[]{:S(2)}) copy-start(bf16[16,512,128]{2,1,0:T(8,128)(2,1)} %w_ref.3) | copy-start | bytes 6291460
  15.7 7.3 %collective-permute-start.10 = (bf16[64,512]{1,0:T(8,128)(2,1)S(1)}, bf16[64,512]{1,0:T(8,128)(2,1)S(1)}, u32[]{:S(2)}, u32[]{:S(2)}) collective-permute-start(bf16[64,512]{1,0:T(8,128)(2,1)S(1)} %get-tuple-element.30), channel_id=1, source_target_pairs={{4,0},{12,1},{0,2},{8,3},{20,4},{28,5},{16,6},{24,7},{5,8},{13,9},... | collective-permute-start | bytes 196616 | tf_op jit(solution)/shard_map/ppermute | solution.py:328
  19.8 6.8 %collective-permute-start.9 = (bf16[64,512]{1,0:T(8,128)(2,1)S(1)}, bf16[64,512]{1,0:T(8,128)(2,1)S(1)}, u32[]{:S(2)}, u32[]{:S(2)}) collective-permute-start(bf16[64,512]{1,0:T(8,128)(2,1)S(1)} %get-tuple-element.29), channel_id=1, source_target_pairs={{12,0},{4,1},{8,2},{0,3},{28,4},{20,5},{24,6},{16,7},{13,8},{5,9},... | collective-permute-start | bytes 196616 | tf_op jit(solution)/shard_map/ppermute | solution.py:328

commit v17 on v15

--- a/solution.py
+++ b/solution.py
@@ -34,7 +34,7 @@
 
 def first_block(plane, chip, core):
     near = 1 * (chip % 2 == plane % 2)
-    return far_half(plane, 1 - core) ^ near ^ chip % 2
+    return far_half(plane, core ^ 1 * (chip == plane)) ^ near ^ chip % 2
 
 
 def partner(k, core):
@@ -232,12 +232,13 @@
         return pltpu.with_memory_space_constraint(x, pltpu.HBM)
 
     def host(i, j):
-        other = (i // COPIES) ^ (2 - ((j ^ (j >> 1)) & 1))
-        return flat(((i % COPIES) * 2 + other // 2) * COPIES + other % 2, j)
+        home, row = i // COPIES, i % COPIES
+        exchanged = row == home // 2 == j // 2
+        return flat((row * 2 + home % 2 ^ exchanged) * COPIES + 1 - home // 2, j)
 
     def owner(i, j, a):
         plane, chip = i // COPIES, i % COPIES * per_device + a
-        return flat(chip * COPIES + 1 - j // 2, plane)
+        return flat(chip * COPIES + (j // 2 ^ (chip == plane)), plane)
 
     def in_plane(move):
         return [(g * COPIES + t, move(g, t)) for g in range(owners) for t in range(COPIES)]

time: 26.5 us -> 27.3 us (1.030)
  the two profiles are of different devices: /device:TPU:6 before, /device:TPU:7 now
where the time goes in v17:
time: 27.3 us; the launch traced here: 27.1 us
  starting transfers between devices  15.8 us (58%)
  waiting for transfers between devices  6.46 us (24%)
  Pallas kernels  4.76 us (17%)
    ppermute x2, starting transfers between devices, whole_sequences(): lax.ppermute(latent[k], both, [(owner(i, j, first_back(i // COPIES, j) ^...  5.98 us
    ppermute x2, waiting for transfers between devices, whole_sequences(): lax.ppermute(latent[k], both, [(owner(i, j, first_back(i // COPIES, j) ^...  4.91 us
    ppermute x2, starting transfers between devices, whole_sequences(): lax.ppermute(pieces[k], both, [(host(i, j), owner(i, j, leaves_as(k, j)))...  4.09 us
    ppermute x3, starting transfers between devices, whole_sequences(): lax.ppermute(picked[k], 'seq', in_plane(lambda g, t: (g ^ partner(k, t))...  2.65 us
    ppermute x3, starting transfers between devices, whole_sequences(): lax.ppermute(keys, 'seq', other_core)  2.4 us
    pallas_call x1, Pallas kernels, whole_sequences(): pl.pallas_call(functools.partial(pick_kernel, per_device), out_shape=[jax...  1.38 us
    pallas_call x1, Pallas kernels, whole_sequences(): pl.pallas_call(functools.partial(project_kernel, per_device), out_shape=j...  1.06 us
    ppermute x3, waiting for transfers between devices, whole_sequences(): lax.ppermute(picked[k], 'seq', in_plane(lambda g, t: (g ^ partner(k, t))...  0.95 us
  transfers between devices with their start and end apart: 11, of which 5 were waited for; matrix products, arithmetic and copies ran while one was open for 0% of the time, Pallas kernels for 6%

profile of v17, /device:TPU:7, one launch (start us, length us, event | category | flops | bytes accessed | tf_op | source)
XLA Modules:
  0.0 27.1 jit_solution(13696004146147875988)
XLA Ops:
  0.0 1.4 %shard_map.64 = (bf16[576,128]{1,0:T(8,128)(2,1)S(1)}, bf16[576,128]{1,0:T(8,128)(2,1)S(1)}, bf16[576,128]{1,0:T(8,128)(2,1)S(1)}, bf16[576,128]{1,0:T(8,128)(2,...) custom-call(bf16[4,576,128]{2,1,0:T(8,128)(2,1)} %bitcast.1, bf16[8,16,192]{2,1,0:T(8,128)(2,1)} %q_hbm.1, ...), custom_call_target="tpu_custom_call" | custom-call | flops 20000000000 | tf_op jit(solution)/shard_map/pallas_call | solution.py:246
  1.4 0.7 %collective-permute-start = (bf16[128,256]{1,0:T(8,128)(2,1)S(1)}, bf16[128,256]{1,0:T(8,128)(2,1)S(1)}, u32[]{:S(2)}, u32[]{:S(2)}) collective-permute-start(bf16[128,256]{1,0:T(8,128)(2,1)S(1)} %get-tuple-element.20), channel_id=1, source_target_pairs={{0,12},{1,13},{2,6},{3,7},{4,20},{5,21},{6,22},{7,23},{8,4},{9,5},... | collective-permute-start | bytes 196616 | tf_op jit(solution)/shard_map/ppermute | solution.py:264
  2.1 0.8 %collective-permute-start.3 = (bf16[576,128]{1,0:T(8,128)(2,1)S(1)}, bf16[576,128]{1,0:T(8,128)(2,1)S(1)}, u32[]{:S(2)}, u32[]{:S(2)}) collective-permute-start(bf16[576,128]{1,0:T(8,128)(2,1)S(1)} %get-tuple-element.24), channel_id=1, source_target_pairs={{0,24},{4,28},{8,16},{12,20},{16,8},{20,12},{24,0},{28,4},{1,25},{... | collective-permute-start | bytes 442376 | tf_op jit(solution)/shard_map/ppermute | solution.py:266
  2.9 0.7 %collective-permute-start.4 = (bf16[576,128]{1,0:T(8,128)(2,1)S(1)}, bf16[576,128]{1,0:T(8,128)(2,1)S(1)}, u32[]{:S(2)}, u32[]{:S(2)}) collective-permute-start(bf16[576,128]{1,0:T(8,128)(2,1)S(1)} %get-tuple-element.25), channel_id=1, source_target_pairs={{0,8},{4,20},{8,0},{12,28},{16,24},{20,4},{24,16},{28,12},{1,9},{5... | collective-permute-start | bytes 442376 | tf_op jit(solution)/shard_map/ppermute | solution.py:266
  3.6 1.2 %collective-permute-start.5 = (bf16[576,128]{1,0:T(8,128)(2,1)S(1)}, bf16[576,128]{1,0:T(8,128)(2,1)S(1)}, u32[]{:S(2)}, u32[]{:S(2)}) collective-permute-start(bf16[576,128]{1,0:T(8,128)(2,1)S(1)} %get-tuple-element.26), channel_id=1, source_target_pairs={{0,16},{4,12},{8,24},{12,4},{16,0},{20,28},{24,8},{28,20},{1,17},{... | collective-permute-start | bytes 442376 | tf_op jit(solution)/shard_map/ppermute | solution.py:266
  4.8 0.5 %shard_map.65 = (bf16[64,640]{1,0:T(8,128)(2,1)S(1)}, bf16[64,640]{1,0:T(8,128)(2,1)S(1)}) custom-call(bf16[16,128,512]{2,1,0:T(8,128)(2,1)S(1)} %copy-done.1, bf16[128,256]{1,0:T(8,128)(2,1)S(1)} %collective-permute-done.packed_ref), custom_call_target="tpu_custom_call" | custom-call | flops 20000000000 | tf_op jit(solution)/shard_map/pallas_call | solution.py:280
  5.3 2.6 %collective-permute-start.1 = (bf16[64,640]{1,0:T(8,128)(2,1)S(1)}, bf16[64,640]{1,0:T(8,128)(2,1)S(1)}, u32[]{:S(2)}, u32[]{:S(2)}) collective-permute-start(bf16[64,640]{1,0:T(8,128)(2,1)S(1)} %get-tuple-element.21), channel_id=1, source_target_pairs={{12,4},{13,8},{6,0},{7,12},{20,16},{21,24},{22,20},{23,28},{4,1},{... | collective-permute-start | bytes 245768 | tf_op jit(solution)/shard_map/ppermute | solution.py:289
  7.8 1.5 %collective-permute-start.2 = (bf16[64,640]{1,0:T(8,128)(2,1)S(1)}, bf16[64,640]{1,0:T(8,128)(2,1)S(1)}, u32[]{:S(2)}, u32[]{:S(2)}) collective-permute-start(bf16[64,640]{1,0:T(8,128)(2,1)S(1)} %get-tuple-element.22), channel_id=1, source_target_pairs={{12,8},{13,4},{6,12},{7,0},{20,24},{21,16},{22,28},{23,20},{4,13},... | collective-permute-start | bytes 245768 | tf_op jit(solution)/shard_map/ppermute | solution.py:289
  9.3 0.0 collective-permute-done.3.refs_3_.second_ref
  9.4 0.4 %shard_map.67 = bf16[2,576,128]{2,1,0:T(8,128)(2,1)S(1)} custom-call(bf16[576,128]{1,0:T(8,128)(2,1)S(1)} %get-tuple-element.23.refs_2_.first_ref, bf16[576,128]{1,0:T(8,128)(2,1)S(1)} %collective-permute-done.3.refs_3_.second_ref), custom_call_target="tpu_custom_call" | custom-call | tf_op jit(solution)/shard_map/pallas_call | solution.py:269
  9.7 1.0 %collective-permute-start.6 = (bf16[2,576,128]{2,1,0:T(8,128)(2,1)S(1)}, bf16[2,576,128]{2,1,0:T(8,128)(2,1)S(1)}, u32[]{:S(2)}, u32[]{:S(2)}) collective-permute-start(bf16[2,576,128]{2,1,0:T(8,128)(2,1)S(1)} %shard_map.67), channel_id=1, source_target_pairs={{0,4},{4,0},{8,12},{12,8},{16,20},{20,16},{24,28},{28,24},{1,5},{5... | collective-permute-start | bytes 884744 | tf_op jit(solution)/shard_map/ppermute | solution.py:278
  10.7 0.9 %collective-permute-done.4.refs_4_ = bf16[576,128]{1,0:T(8,128)(2,1)S(1)} collective-permute-done((bf16[576,128]{1,0:T(8,128)(2,1)S(1)}, bf16[576,128]{1,0:T(8,128)(2,1)S(1)}, u32[]{:S(2)}, u32[]{:S(2)}) %collective-permute-start.4) | collective-permute-done | bytes 147488 | tf_op jit(solution)/shard_map/ppermute | solution.py:266
  11.7 1.4 %collective-permute-start.7 = (bf16[576,128]{1,0:T(8,128)(2,1)S(1)}, bf16[576,128]{1,0:T(8,128)(2,1)S(1)}, u32[]{:S(2)}, u32[]{:S(2)}) collective-permute-start(bf16[576,128]{1,0:T(8,128)(2,1)S(1)} %collective-permute-done.4.refs_4_), channel_id=1, source_target_pairs={{0,4},{4,0},{8,12},{12,8},{16,20},{20,16},{24,28},{28,24},{1,5},{5... | collective-permute-start | bytes 442376 | tf_op jit(solution)/shard_map/ppermute | solution.py:278
  13.1 0.0 collective-permute-done.5.refs_5_
  13.1 0.0 collective-permute-start.8
  13.1 0.0 collective-permute-done.1.refs_0_
  13.1 0.3 collective-permute-done.2.refs_1_
  13.4 0.8 %shard_map.66 = (bf16[128,576]{1,0:T(8,128)(2,1)S(1)}, f32[128,128]{1,0:T(8,128)S(1)}, f32[128,128]{1,0:T(8,128)S(1)}, f32[128,512]{1,0:T(8,128)S(1)}) custom-call(s32[8,128]{1,0:T(8,128)S(1)} %get-tuple-element.19.limit_ref, bf16[64,640]{1,0:T(8,128)(2,1)S(1)} %collective-permute-done.1.refs_0_, bf16[64,640]{1,0:T(8,128)(2,1)S(1)} %collective-permute-done.2.refs_1_, ...), custom_call_target="tpu_custom_call" | custom-call | flops 20000000000 | tf_op jit(solution)/shard_map/pallas_call | solution.py:297
  14.1 0.3 %collective-permute-done.8.refs_1_ = bf16[576,128]{1,0:T(8,128)(2,1)S(1)} collective-permute-done((bf16[576,128]{1,0:T(8,128)(2,1)S(1)}, bf16[576,128]{1,0:T(8,128)(2,1)S(1)}, u32[]{:S(2)}, u32[]{:S(2)}) %collective-permute-start.8) | collective-permute-done | bytes 147488 | tf_op jit(solution)/shard_map/ppermute | solution.py:278
  14.5 0.7 %shard_map.68 = (bf16[64,512]{1,0:T(8,128)(2,1)S(1)}, bf16[64,512]{1,0:T(8,128)(2,1)S(1)}) custom-call(s32[8,128]{1,0:T(8,128)S(1)} %get-tuple-element.19.limit_ref, bf16[128,576]{1,0:T(8,128)(2,1)S(1)} %get-tuple-element.27.q_ref, f32[128,128]{1,0:T(8,128)S(1)} %get-tuple-element.28.top_ref, f32[128,128]{1,0:T(8,128)S(1)} %get-tuple-element.29.total_ref, ...), custom_call_target="tpu_custom_call" | custom-call | tf_op jit(solution)/shard_map/pallas_call | solution.py:310
  15.2 6.0 %collective-permute-start.10 = (bf16[64,512]{1,0:T(8,128)(2,1)S(1)}, bf16[64,512]{1,0:T(8,128)(2,1)S(1)}, u32[]{:S(2)}, u32[]{:S(2)}) collective-permute-start(bf16[64,512]{1,0:T(8,128)(2,1)S(1)} %get-tuple-element.32), channel_id=1, source_target_pairs={{4,0},{8,1},{0,2},{12,3},{16,4},{24,5},{20,6},{28,7},{1,8},{13,9},... | collective-permute-start | bytes 196616 | tf_op jit(solution)/shard_map/ppermute | solution.py:319
  21.2 1.6 %collective-permute-done.10.refs_1_ = bf16[64,512]{1,0:T(8,128)(2,1)S(1)} collective-permute-done((bf16[64,512]{1,0:T(8,128)(2,1)S(1)}, bf16[64,512]{1,0:T(8,128)(2,1)S(1)}, u32[]{:S(2)}, u32[]{:S(2)}) %collective-permute-start.10) | collective-permute-done | bytes 65568 | tf_op jit(solution)/shard_map/ppermute | solution.py:319
  22.8 3.3 %collective-permute-done.9.refs_0_ = bf16[64,512]{1,0:T(8,128)(2,1)S(1)} collective-permute-done((bf16[64,512]{1,0:T(8,128)(2,1)S(1)}, bf16[64,512]{1,0:T(8,128)(2,1)S(1)}, u32[]{:S(2)}, u32[]{:S(2)}) %collective-permute-start.9) | collective-permute-done | bytes 65568 | tf_op jit(solution)/shard_map/ppermute | solution.py:319
  26.1 1.1 %shard_map.69 = bf16[8,16,128]{2,1,0:T(8,128)(2,1)} custom-call(bf16[16,512,128]{2,1,0:T(8,128)(2,1)S(1)} %copy-done, bf16[64,512]{1,0:T(8,128)(2,1)S(1)} %collective-permute-done.9.refs_0_, bf16[64,512]{1,0:T(8,128)(2,1)S(1)} %collective-permute-done.10.refs_1_), custom_call_target="tpu_custom_call" | custom-call | tf_op jit(solution)/shard_map/pallas_call | solution.py:326
  (8 shorter events, 0.0 us)
Async XLA Ops:
  0.0 4.8 %copy-start.1 = (bf16[16,128,512]{2,1,0:T(8,128)(2,1)S(1)}, bf16[16,128,512]{2,1,0:T(8,128)(2,1)}, u32[]{:S(2)}) copy-start(bf16[16,128,512]{2,1,0:T(8,128)(2,1)} %w_ref.2) | copy-start | bytes 6291460
  1.4 3.4 %collective-permute-start = (bf16[128,256]{1,0:T(8,128)(2,1)S(1)}, bf16[128,256]{1,0:T(8,128)(2,1)S(1)}, u32[]{:S(2)}, u32[]{:S(2)}) collective-permute-start(bf16[128,256]{1,0:T(8,128)(2,1)S(1)} %get-tuple-element.20), channel_id=1, source_target_pairs={{0,12},{1,13},{2,6},{3,7},{4,20},{5,21},{6,22},{7,23},{8,4},{9,5},... | collective-permute-start | bytes 196616 | tf_op jit(solution)/shard_map/ppermute | solution.py:264
  2.1 7.2 %collective-permute-start.3 = (bf16[576,128]{1,0:T(8,128)(2,1)S(1)}, bf16[576,128]{1,0:T(8,128)(2,1)S(1)}, u32[]{:S(2)}, u32[]{:S(2)}) collective-permute-start(bf16[576,128]{1,0:T(8,128)(2,1)S(1)} %get-tuple-element.24), channel_id=1, source_target_pairs={{0,24},{4,28},{8,16},{12,20},{16,8},{20,12},{24,0},{28,4},{1,25},{... | collective-permute-start | bytes 442376 | tf_op jit(solution)/shard_map/ppermute | solution.py:266
  2.9 8.8 %collective-permute-start.4 = (bf16[576,128]{1,0:T(8,128)(2,1)S(1)}, bf16[576,128]{1,0:T(8,128)(2,1)S(1)}, u32[]{:S(2)}, u32[]{:S(2)}) collective-permute-start(bf16[576,128]{1,0:T(8,128)(2,1)S(1)} %get-tuple-element.25), channel_id=1, source_target_pairs={{0,8},{4,20},{8,0},{12,28},{16,24},{20,4},{24,16},{28,12},{1,9},{5... | collective-permute-start | bytes 442376 | tf_op jit(solution)/shard_map/ppermute | solution.py:266
  3.6 9.5 %collective-permute-start.5 = (bf16[576,128]{1,0:T(8,128)(2,1)S(1)}, bf16[576,128]{1,0:T(8,128)(2,1)S(1)}, u32[]{:S(2)}, u32[]{:S(2)}) collective-permute-start(bf16[576,128]{1,0:T(8,128)(2,1)S(1)} %get-tuple-element.26), channel_id=1, source_target_pairs={{0,16},{4,12},{8,24},{12,4},{16,0},{20,28},{24,8},{28,20},{1,17},{... | collective-permute-start | bytes 442376 | tf_op jit(solution)/shard_map/ppermute | solution.py:266
  5.3 7.8 %collective-permute-start.1 = (bf16[64,640]{1,0:T(8,128)(2,1)S(1)}, bf16[64,640]{1,0:T(8,128)(2,1)S(1)}, u32[]{:S(2)}, u32[]{:S(2)}) collective-permute-start(bf16[64,640]{1,0:T(8,128)(2,1)S(1)} %get-tuple-element.21), channel_id=1, source_target_pairs={{12,4},{13,8},{6,0},{7,12},{20,16},{21,24},{22,20},{23,28},{4,1},{... | collective-permute-start | bytes 245768 | tf_op jit(solution)/shard_map/ppermute | solution.py:289
  7.8 5.5 %collective-permute-start.2 = (bf16[64,640]{1,0:T(8,128)(2,1)S(1)}, bf16[64,640]{1,0:T(8,128)(2,1)S(1)}, u32[]{:S(2)}, u32[]{:S(2)}) collective-permute-start(bf16[64,640]{1,0:T(8,128)(2,1)S(1)} %get-tuple-element.22), channel_id=1, source_target_pairs={{12,8},{13,4},{6,12},{7,0},{20,24},{21,16},{22,28},{23,20},{4,13},... | collective-permute-start | bytes 245768 | tf_op jit(solution)/shard_map/ppermute | solution.py:289
  9.7 4.7 %collective-permute-start.6 = (bf16[2,576,128]{2,1,0:T(8,128)(2,1)S(1)}, bf16[2,576,128]{2,1,0:T(8,128)(2,1)S(1)}, u32[]{:S(2)}, u32[]{:S(2)}) collective-permute-start(bf16[2,576,128]{2,1,0:T(8,128)(2,1)S(1)} %shard_map.67), channel_id=1, source_target_pairs={{0,4},{4,0},{8,12},{12,8},{16,20},{20,16},{24,28},{28,24},{1,5},{5... | collective-permute-start | bytes 884744 | tf_op jit(solution)/shard_map/ppermute | solution.py:278
  11.7 2.4 %collective-permute-start.7 = (bf16[576,128]{1,0:T(8,128)(2,1)S(1)}, bf16[576,128]{1,0:T(8,128)(2,1)S(1)}, u32[]{:S(2)}, u32[]{:S(2)}) collective-permute-start(bf16[576,128]{1,0:T(8,128)(2,1)S(1)} %collective-permute-done.4.refs_4_), channel_id=1, source_target_pairs={{0,4},{4,0},{8,12},{12,8},{16,20},{20,16},{24,28},{28,24},{1,5},{5... | collective-permute-start | bytes 442376 | tf_op jit(solution)/shard_map/ppermute | solution.py:278
  13.1 1.4 %collective-permute-start.8 = (bf16[576,128]{1,0:T(8,128)(2,1)S(1)}, bf16[576,128]{1,0:T(8,128)(2,1)S(1)}, u32[]{:S(2)}, u32[]{:S(2)}) collective-permute-start(bf16[576,128]{1,0:T(8,128)(2,1)S(1)} %collective-permute-done.5.refs_5_), channel_id=1, source_target_pairs={{0,4},{4,0},{8,12},{12,8},{16,20},{20,16},{24,28},{28,24},{1,5},{5... | collective-permute-start | bytes 442376 | tf_op jit(solution)/shard_map/ppermute | solution.py:278
  13.4 12.7 %copy-start = (bf16[16,512,128]{2,1,0:T(8,128)(2,1)S(1)}, bf16[16,512,128]{2,1,0:T(8,128)(2,1)}, u32[]{:S(2)}) copy-start(bf16[16,512,128]{2,1,0:T(8,128)(2,1)} %w_ref.3) | copy-start | bytes 6291460
  15.2 7.6 %collective-permute-start.10 = (bf16[64,512]{1,0:T(8,128)(2,1)S(1)}, bf16[64,512]{1,0:T(8,128)(2,1)S(1)}, u32[]{:S(2)}, u32[]{:S(2)}) collective-permute-start(bf16[64,512]{1,0:T(8,128)(2,1)S(1)} %get-tuple-element.32), channel_id=1, source_target_pairs={{4,0},{8,1},{0,2},{12,3},{16,4},{24,5},{20,6},{28,7},{1,8},{13,9},... | collective-permute-start | bytes 196616 | tf_op jit(solution)/shard_map/ppermute | solution.py:319
  21.2 4.9 %collective-permute-start.9 = (bf16[64,512]{1,0:T(8,128)(2,1)S(1)}, bf16[64,512]{1,0:T(8,128)(2,1)S(1)}, u32[]{:S(2)}, u32[]{:S(2)}) collective-permute-start(bf16[64,512]{1,0:T(8,128)(2,1)S(1)} %get-tuple-element.31), channel_id=1, source_target_pairs={{8,0},{4,1},{12,2},{0,3},{24,4},{16,5},{28,6},{20,7},{13,8},{1,9},... | collective-permute-start | bytes 196616 | tf_op jit(solution)/shard_map/ppermute | solution.py:319

commit v18 on v15

--- a/solution.py
+++ b/solution.py
@@ -15,6 +15,7 @@
 COPIES = 2
 VMEM_LIMIT = 16 * 1024 * 1024
 LONG = pl.CostEstimate(flops=2 * 10**10, bytes_accessed=0, transcendentals=0)
+SHORT = pl.CostEstimate(flops=10**8, bytes_accessed=0, transcendentals=0)
 
 masked_value = -1e30
 
@@ -41,22 +42,15 @@
     return (0, 3, 1 ^ 3 * core, 2 ^ 3 * core)[k]
 
 
-def pick_kernel(per_device, cache_hbm, q_hbm, new_hbm, len_hbm, *refs):
-    owners = cache_hbm.shape[0]
-    blocks, (out_ref, limit_ref, q_ref, new_ref, len_ref, sem) = refs[:owners], refs[owners:]
-    chip, core = lax.axis_index("seq") // COPIES, lax.axis_index("seq") % COPIES
+def pack_kernel(per_device, q_hbm, new_hbm, out_ref, q_ref, new_ref, sem):
     moves = [
-        pltpu.make_async_copy(q_hbm, q_ref, sem.at[owners]),
-        pltpu.make_async_copy(new_hbm, new_ref, sem.at[owners + 1]),
-        pltpu.make_async_copy(len_hbm, len_ref, sem.at[owners + 2]),
-    ] + [
-        pltpu.make_async_copy(cache_hbm.at[chip ^ partner(k, core)], blocks[k], sem.at[k])
-        for k in range(owners)
+        pltpu.make_async_copy(q_hbm, q_ref, sem.at[0]),
+        pltpu.make_async_copy(new_hbm, new_ref, sem.at[1]),
     ]
     for move in moves:
         move.start()
-    moves[0].wait()
-    moves[1].wait()
+    for move in moves:
+        move.wait()
     heads, width = q_ref.shape[1:]
     fresh = new_ref[...].astype(jnp.float32)
     piece = SPEC * heads
@@ -69,10 +63,22 @@
             parts.append(jnp.zeros((spare, ROPE), jnp.float32))
         own = jnp.concatenate(parts, axis=0).astype(rows.dtype)
         out_ref[a * piece : (a + 1) * piece] = jnp.concatenate([rows, own], axis=1)
-    moves[2].wait()
+
+
+def pick_kernel(cache_hbm, len_hbm, *refs):
+    owners = cache_hbm.shape[0]
+    blocks, (limit_ref, len_ref, sem) = refs[:owners], refs[owners:]
+    chip, core = lax.axis_index("seq") // COPIES, lax.axis_index("seq") % COPIES
+    moves = [pltpu.make_async_copy(len_hbm, len_ref, sem.at[owners])] + [
+        pltpu.make_async_copy(cache_hbm.at[chip ^ partner(k, core)], blocks[k], sem.at[k])
+        for k in range(owners)
+    ]
+    for move in moves:
+        move.start()
+    moves[0].wait()
     length = len_ref[lax.axis_index("head") * owners + chip]
     limit_ref[...] = jnp.full(limit_ref.shape, length, limit_ref.dtype)
-    for move in moves[3:]:
+    for move in moves[1:]:
         move.wait()
 
 
@@ -242,25 +248,33 @@
     def in_plane(move):
         return [(g * COPIES + t, move(g, t)) for g in range(owners) for t in range(COPIES)]
 
-    *picked, packed, limit = pl.pallas_call(
-        functools.partial(pick_kernel, per_device),
-        out_shape=[jax.ShapeDtypeStruct((width, slots), cache.dtype)] * owners
-        + [
-            jax.ShapeDtypeStruct((all_rows, q_width + ROPE), queries.dtype),
-            jax.ShapeDtypeStruct((8, slots), jnp.int32),
-        ],
-        in_specs=[anywhere] * 4,
-        out_specs=[vmem] * (owners + 2),
+    packed = pl.pallas_call(
+        functools.partial(pack_kernel, per_device),
+        out_shape=jax.ShapeDtypeStruct((all_rows, q_width + ROPE), queries.dtype),
+        in_specs=[anywhere] * 2,
+        out_specs=vmem,
         scratch_shapes=[
             pltpu.VMEM(queries.shape, queries.dtype),
             pltpu.VMEM(new_latent.shape, new_latent.dtype),
+            pltpu.SemaphoreType.DMA((2,)),
+        ],
+        compiler_params=params,
+        cost_estimate=SHORT,
+    )(in_hbm(queries), in_hbm(new_latent))
+    moved = lax.ppermute(packed, both, [(flat(i, j), host(i, j)) for i, j in devices])
+    *picked, limit = pl.pallas_call(
+        pick_kernel,
+        out_shape=[jax.ShapeDtypeStruct((width, slots), cache.dtype)] * owners
+        + [jax.ShapeDtypeStruct((8, slots), jnp.int32)],
+        in_specs=[anywhere] * 2,
+        out_specs=[vmem] * (owners + 1),
+        scratch_shapes=[
             pltpu.SMEM(lengths.shape, lengths.dtype),
-            pltpu.SemaphoreType.DMA((owners + 3,)),
+            pltpu.SemaphoreType.DMA((owners + 1,)),
         ],
         compiler_params=params,
         cost_estimate=LONG,
-    )(*[in_hbm(x) for x in (jnp.swapaxes(cache, 1, 2), queries, new_latent, lengths)])
-    moved = lax.ppermute(packed, both, [(flat(i, j), host(i, j)) for i, j in devices])
+    )(in_hbm(jnp.swapaxes(cache, 1, 2)), in_hbm(lengths))
     own_keys = [picked[0]] + [
         lax.ppermute(picked[k], "seq", in_plane(lambda g, t: (g ^ partner(k, t)) * COPIES + t))
         for k in range(1, owners)

time: 26.5 us -> 27.3 us (1.030)
  Pallas kernels: 4.75 us -> 5.71 us
    ppermute x3, waiting for transfers between devices: 3.53 us -> 5.64 us  [whole_sequences(): lax.ppermute(picked[k], 'seq', in_plane(lambda g, t: (g ^ partner(k, t))...]
    ppermute x1, waiting for transfers between devices: 1.63 us -> 0.01 us  [whole_sequences(): lax.ppermute(packed, both, [(flat(i, j), host(i, j)) for i, j in devices])]
    ppermute x2, starting transfers between devices: 0.13 us -> 1.49 us  [whole_sequences(): lax.ppermute(pieces[k], both, [(host(i, j), owner(i, j, leaves_as(k, j)))...]
    ppermute x3, starting transfers between devices: 1.81 us -> 0.58 us  [whole_sequences(): lax.ppermute(keys, 'seq', other_core)]
    pallas_call x1 -> x2, Pallas kernels: 1.38 us -> 2.34 us  [the longest x1 1.33 us: whole_sequences(): pl.pallas_call(pick_kernel, out_shape=[jax.ShapeDtypeStruct((width, slots...]
    ppermute x2, waiting for transfers between devices: 0.74 us -> 0.01 us  [whole_sequences(): lax.ppermute(pieces[k], both, [(host(i, j), owner(i, j, leaves_as(k, j)))...]
    ppermute x2, starting transfers between devices: 3.85 us -> 3.51 us  [whole_sequences(): lax.ppermute(latent[k], both, [(owner(i, j, first_back(i // COPIES, j) ^...]
    ppermute x3, waiting for transfers between devices: 0.01 us -> 0.29 us  [whole_sequences(): lax.ppermute(keys, 'seq', other_core)]
  transfers between devices with their start and end apart: 11 -> 11, of which waited for: 7 -> 6; matrix products, arithmetic and copies ran while one was open for 0% -> 0% of each run, Pallas kernels for 6% -> 11%
where the time goes in v18:
time: 27.3 us; the launch traced here: 27 us
  waiting for transfers between devices  12 us (44%)
  starting transfers between devices  9.2 us (34%)
  Pallas kernels  5.71 us (21%)
    ppermute x2, waiting for transfers between devices, whole_sequences(): lax.ppermute(latent[k], both, [(owner(i, j, first_back(i // COPIES, j) ^...  6.02 us
    ppermute x3, waiting for transfers between devices, whole_sequences(): lax.ppermute(picked[k], 'seq', in_plane(lambda g, t: (g ^ partner(k, t))...  5.64 us
    ppermute x3, starting transfers between devices, whole_sequences(): lax.ppermute(picked[k], 'seq', in_plane(lambda g, t: (g ^ partner(k, t))...  3.55 us
    ppermute x2, starting transfers between devices, whole_sequences(): lax.ppermute(latent[k], both, [(owner(i, j, first_back(i // COPIES, j) ^...  3.51 us
    ppermute x2, starting transfers between devices, whole_sequences(): lax.ppermute(pieces[k], both, [(host(i, j), owner(i, j, leaves_as(k, j)))...  1.49 us
    pallas_call x1, Pallas kernels, whole_sequences(): pl.pallas_call(pick_kernel, out_shape=[jax.ShapeDtypeStruct((width, slots...  1.33 us
    pallas_call x1, Pallas kernels, whole_sequences(): pl.pallas_call(functools.partial(project_kernel, per_device), out_shape=j...  1.06 us
    pallas_call x1, Pallas kernels, whole_sequences(): pl.pallas_call(functools.partial(pack_kernel, per_device), out_shape=jax....  1 us
  transfers between devices with their start and end apart: 11, of which 6 were waited for; matrix products, arithmetic and copies ran while one was open for 0% of the time, Pallas kernels for 11%

profile of v18, /device:TPU:6, one launch (start us, length us, event | category | flops | bytes accessed | tf_op | source)
XLA Modules:
  0.0 27.0 jit_solution(4730425515126946689)
XLA Ops:
  0.0 1.0 %shard_map.65 = bf16[128,256]{1,0:T(8,128)(2,1)S(1)} custom-call(bf16[8,16,192]{2,1,0:T(8,128)(2,1)} %q_hbm.1, bf16[8,576]{1,0:T(8,128)(2,1)} %new_hbm.1), custom_call_target="tpu_custom_call" | custom-call | flops 100000000 | tf_op jit(solution)/shard_map/pallas_call | solution.py:251
  1.0 0.1 collective-permute-start
  1.1 0.0 copy-start.1
  1.1 1.3 %shard_map.64 = (bf16[576,128]{1,0:T(8,128)(2,1)S(1)}, bf16[576,128]{1,0:T(8,128)(2,1)S(1)}, bf16[576,128]{1,0:T(8,128)(2,1)S(1)}, bf16[576,128]{1,0:T(8,128)(2,1)S(1)}, s32[8,128]{1,0:T(8,128)S(1)}) custom-call(bf16[4,576,128]{2,1,0:T(8,128)(2,1)} %bitcast.1, s32[16]{0:T(128)} %len_hbm.1), custom_call_target="tpu_custom_call" | custom-call | flops 20000000000 | tf_op jit(solution)/shard_map/pallas_call | solution.py:265
  2.4 2.0 %collective-permute-start.3 = (bf16[576,128]{1,0:T(8,128)(2,1)S(1)}, bf16[576,128]{1,0:T(8,128)(2,1)S(1)}, u32[]{:S(2)}, u32[]{:S(2)}) collective-permute-start(bf16[576,128]{1,0:T(8,128)(2,1)S(1)} %get-tuple-element.22), channel_id=1, source_target_pairs={{0,24},{4,28},{8,16},{12,20},{16,8},{20,12},{24,0},{28,4},{1,25},{... | collective-permute-start | bytes 442376 | tf_op jit(solution)/shard_map/ppermute | solution.py:279
  4.4 0.0 collective-permute-start.4
  4.5 1.5 %collective-permute-start.5 = (bf16[576,128]{1,0:T(8,128)(2,1)S(1)}, bf16[576,128]{1,0:T(8,128)(2,1)S(1)}, u32[]{:S(2)}, u32[]{:S(2)}) collective-permute-start(bf16[576,128]{1,0:T(8,128)(2,1)S(1)} %get-tuple-element.24), channel_id=1, source_target_pairs={{0,16},{4,12},{8,24},{12,4},{16,0},{20,28},{24,8},{28,20},{1,17},{... | collective-permute-start | bytes 442376 | tf_op jit(solution)/shard_map/ppermute | solution.py:279
  6.0 0.5 %shard_map.66 = (bf16[64,640]{1,0:T(8,128)(2,1)S(1)}, bf16[64,640]{1,0:T(8,128)(2,1)S(1)}) custom-call(bf16[16,128,512]{2,1,0:T(8,128)(2,1)S(1)} %copy-done.1, bf16[128,256]{1,0:T(8,128)(2,1)S(1)} %collective-permute-done.packed_ref), custom_call_target="tpu_custom_call" | custom-call | flops 20000000000 | tf_op jit(solution)/shard_map/pallas_call | solution.py:293
  6.5 0.6 %collective-permute-start.1 = (bf16[64,640]{1,0:T(8,128)(2,1)S(1)}, bf16[64,640]{1,0:T(8,128)(2,1)S(1)}, u32[]{:S(2)}, u32[]{:S(2)}) collective-permute-start(bf16[64,640]{1,0:T(8,128)(2,1)S(1)} %get-tuple-element.19), channel_id=1, source_target_pairs={{8,4},{5,12},{6,0},{11,8},{24,20},{21,28},{22,16},{27,24},{12,5},{... | collective-permute-start | bytes 245768 | tf_op jit(solution)/shard_map/ppermute | solution.py:302
  7.1 0.8 %collective-permute-start.2 = (bf16[64,640]{1,0:T(8,128)(2,1)S(1)}, bf16[64,640]{1,0:T(8,128)(2,1)S(1)}, u32[]{:S(2)}, u32[]{:S(2)}) collective-permute-start(bf16[64,640]{1,0:T(8,128)(2,1)S(1)} %get-tuple-element.20), channel_id=1, source_target_pairs={{8,12},{5,4},{6,8},{11,0},{24,28},{21,20},{22,24},{27,16},{12,13},... | collective-permute-start | bytes 245768 | tf_op jit(solution)/shard_map/ppermute | solution.py:302
  8.0 2.0 %collective-permute-done.3.refs_3_.second_ref = bf16[576,128]{1,0:T(8,128)(2,1)S(1)} collective-permute-done((bf16[576,128]{1,0:T(8,128)(2,1)S(1)}, bf16[576,128]{1,0:T(8,128)(2,1)S(1)}, u32[]{:S(2)}, u32[]{:S(2)}) %collective-permute-start.3) | collective-permute-done | bytes 147488 | tf_op jit(solution)/shard_map/ppermute | solution.py:279
  10.0 0.4 %shard_map.68 = bf16[2,576,128]{2,1,0:T(8,128)(2,1)S(1)} custom-call(bf16[576,128]{1,0:T(8,128)(2,1)S(1)} %get-tuple-element.21.refs_2_.first_ref, bf16[576,128]{1,0:T(8,128)(2,1)S(1)} %collective-permute-done.3.refs_3_.second_ref), custom_call_target="tpu_custom_call" | custom-call | tf_op jit(solution)/shard_map/pallas_call | solution.py:282
  10.3 0.1 collective-permute-start.6
  10.4 3.6 %collective-permute-done.4.refs_4_ = bf16[576,128]{1,0:T(8,128)(2,1)S(1)} collective-permute-done((bf16[576,128]{1,0:T(8,128)(2,1)S(1)}, bf16[576,128]{1,0:T(8,128)(2,1)S(1)}, u32[]{:S(2)}, u32[]{:S(2)}) %collective-permute-start.4) | collective-permute-done | bytes 147488 | tf_op jit(solution)/shard_map/ppermute | solution.py:279
  14.1 0.5 %collective-permute-start.8 = (bf16[576,128]{1,0:T(8,128)(2,1)S(1)}, bf16[576,128]{1,0:T(8,128)(2,1)S(1)}, u32[]{:S(2)}, u32[]{:S(2)}) collective-permute-start(bf16[576,128]{1,0:T(8,128)(2,1)S(1)} %collective-permute-done.5.refs_5_), channel_id=1, source_target_pairs={{0,4},{4,0},{8,12},{12,8},{16,20},{20,16},{24,28},{28,24},{1,5},{5... | collective-permute-start | bytes 442376 | tf_op jit(solution)/shard_map/ppermute | solution.py:291
  14.6 0.8 %shard_map.67 = (bf16[128,576]{1,0:T(8,128)(2,1)S(1)}, f32[128,128]{1,0:T(8,128)S(1)}, f32[128,128]{1,0:T(8,128)S(1)}, f32[128,512]{1,0:T(8,128)S(1)}) custom-call(s32[8,128]{1,0:T(8,128)S(1)} %get-tuple-element.18.limit_ref, bf16[64,640]{1,0:T(8,128)(2,1)S(1)} %collective-permute-done.1.refs_0_, bf16[64,640]{1,0:T(8,128)(2,1)S(1)} %collective-permute-done.2.refs_1_, ...), custom_call_target="tpu_custom_call" | custom-call | flops 20000000000 | tf_op jit(solution)/shard_map/pallas_call | solution.py:310
  15.4 0.1 collective-permute-done.7.refs_0_
  15.4 0.2 collective-permute-done.8.refs_1_
  15.6 0.7 %shard_map.69 = (bf16[64,512]{1,0:T(8,128)(2,1)S(1)}, bf16[64,512]{1,0:T(8,128)(2,1)S(1)}) custom-call(s32[8,128]{1,0:T(8,128)S(1)} %get-tuple-element.18.limit_ref, bf16[128,576]{1,0:T(8,128)(2,1)S(1)} %get-tuple-element.25.q_ref, f32[128,128]{1,0:T(8,128)S(1)} %get-tuple-element.26.top_ref, f32[128,128]{1,0:T(8,128)S(1)} %get-tuple-element.27.total_ref, ...), custom_call_target="tpu_custom_call" | custom-call | tf_op jit(solution)/shard_map/pallas_call | solution.py:323
  16.4 3.1 %collective-permute-start.10 = (bf16[64,512]{1,0:T(8,128)(2,1)S(1)}, bf16[64,512]{1,0:T(8,128)(2,1)S(1)}, u32[]{:S(2)}, u32[]{:S(2)}) collective-permute-start(bf16[64,512]{1,0:T(8,128)(2,1)S(1)} %get-tuple-element.30), channel_id=1, source_target_pairs={{4,0},{12,1},{0,2},{8,3},{20,4},{28,5},{16,6},{24,7},{5,8},{13,9},... | collective-permute-start | bytes 196616 | tf_op jit(solution)/shard_map/ppermute | solution.py:332
  19.4 0.4 %collective-permute-start.9 = (bf16[64,512]{1,0:T(8,128)(2,1)S(1)}, bf16[64,512]{1,0:T(8,128)(2,1)S(1)}, u32[]{:S(2)}, u32[]{:S(2)}) collective-permute-start(bf16[64,512]{1,0:T(8,128)(2,1)S(1)} %get-tuple-element.29), channel_id=1, source_target_pairs={{12,0},{4,1},{8,2},{0,3},{28,4},{20,5},{24,6},{16,7},{13,8},{5,9},... | collective-permute-start | bytes 196616 | tf_op jit(solution)/shard_map/ppermute | solution.py:332
  19.9 3.8 %collective-permute-done.10.refs_1_ = bf16[64,512]{1,0:T(8,128)(2,1)S(1)} collective-permute-done((bf16[64,512]{1,0:T(8,128)(2,1)S(1)}, bf16[64,512]{1,0:T(8,128)(2,1)S(1)}, u32[]{:S(2)}, u32[]{:S(2)}) %collective-permute-start.10) | collective-permute-done | bytes 65568 | tf_op jit(solution)/shard_map/ppermute | solution.py:332
  23.7 2.2 %collective-permute-done.9.refs_0_ = bf16[64,512]{1,0:T(8,128)(2,1)S(1)} collective-permute-done((bf16[64,512]{1,0:T(8,128)(2,1)S(1)}, bf16[64,512]{1,0:T(8,128)(2,1)S(1)}, u32[]{:S(2)}, u32[]{:S(2)}) %collective-permute-start.9) | collective-permute-done | bytes 65568 | tf_op jit(solution)/shard_map/ppermute | solution.py:332
  25.9 1.1 %shard_map.70 = bf16[8,16,128]{2,1,0:T(8,128)(2,1)} custom-call(bf16[16,512,128]{2,1,0:T(8,128)(2,1)S(1)} %copy-done, bf16[64,512]{1,0:T(8,128)(2,1)S(1)} %collective-permute-done.9.refs_0_, bf16[64,512]{1,0:T(8,128)(2,1)S(1)} %collective-permute-done.10.refs_1_), custom_call_target="tpu_custom_call" | custom-call | tf_op jit(solution)/shard_map/pallas_call | solution.py:339
  (9 shorter events, 0.0 us)
Async XLA Ops:
  1.0 5.0 %collective-permute-start = (bf16[128,256]{1,0:T(8,128)(2,1)S(1)}, bf16[128,256]{1,0:T(8,128)(2,1)S(1)}, u32[]{:S(2)}, u32[]{:S(2)}) collective-permute-start(bf16[128,256]{1,0:T(8,128)(2,1)S(1)} %shard_map.65), channel_id=1, source_target_pairs={{0,8},{1,5},{2,6},{3,11},{4,24},{5,21},{6,22},{7,27},{8,12},{9,1},... | collective-permute-start | bytes 196616 | tf_op jit(solution)/shard_map/ppermute | solution.py:264
  1.1 4.9 %copy-start.1 = (bf16[16,128,512]{2,1,0:T(8,128)(2,1)S(1)}, bf16[16,128,512]{2,1,0:T(8,128)(2,1)}, u32[]{:S(2)}) copy-start(bf16[16,128,512]{2,1,0:T(8,128)(2,1)} %w_ref.2) | copy-start | bytes 6291460
  2.4 7.5 %collective-permute-start.3 = (bf16[576,128]{1,0:T(8,128)(2,1)S(1)}, bf16[576,128]{1,0:T(8,128)(2,1)S(1)}, u32[]{:S(2)}, u32[]{:S(2)}) collective-permute-start(bf16[576,128]{1,0:T(8,128)(2,1)S(1)} %get-tuple-element.22), channel_id=1, source_target_pairs={{0,24},{4,28},{8,16},{12,20},{16,8},{20,12},{24,0},{28,4},{1,25},{... | collective-permute-start | bytes 442376 | tf_op jit(solution)/shard_map/ppermute | solution.py:279
  4.4 9.6 %collective-permute-start.4 = (bf16[576,128]{1,0:T(8,128)(2,1)S(1)}, bf16[576,128]{1,0:T(8,128)(2,1)S(1)}, u32[]{:S(2)}, u32[]{:S(2)}) collective-permute-start(bf16[576,128]{1,0:T(8,128)(2,1)S(1)} %get-tuple-element.23), channel_id=1, source_target_pairs={{0,8},{4,20},{8,0},{12,28},{16,24},{20,4},{24,16},{28,12},{1,9},{5... | collective-permute-start | bytes 442376 | tf_op jit(solution)/shard_map/ppermute | solution.py:279
  4.5 9.6 %collective-permute-start.5 = (bf16[576,128]{1,0:T(8,128)(2,1)S(1)}, bf16[576,128]{1,0:T(8,128)(2,1)S(1)}, u32[]{:S(2)}, u32[]{:S(2)}) collective-permute-start(bf16[576,128]{1,0:T(8,128)(2,1)S(1)} %get-tuple-element.24), channel_id=1, source_target_pairs={{0,16},{4,12},{8,24},{12,4},{16,0},{20,28},{24,8},{28,20},{1,17},{... | collective-permute-start | bytes 442376 | tf_op jit(solution)/shard_map/ppermute | solution.py:279
  6.5 8.1 %collective-permute-start.1 = (bf16[64,640]{1,0:T(8,128)(2,1)S(1)}, bf16[64,640]{1,0:T(8,128)(2,1)S(1)}, u32[]{:S(2)}, u32[]{:S(2)}) collective-permute-start(bf16[64,640]{1,0:T(8,128)(2,1)S(1)} %get-tuple-element.19), channel_id=1, source_target_pairs={{8,4},{5,12},{6,0},{11,8},{24,20},{21,28},{22,16},{27,24},{12,5},{... | collective-permute-start | bytes 245768 | tf_op jit(solution)/shard_map/ppermute | solution.py:302
  7.1 7.5 %collective-permute-start.2 = (bf16[64,640]{1,0:T(8,128)(2,1)S(1)}, bf16[64,640]{1,0:T(8,128)(2,1)S(1)}, u32[]{:S(2)}, u32[]{:S(2)}) collective-permute-start(bf16[64,640]{1,0:T(8,128)(2,1)S(1)} %get-tuple-element.20), channel_id=1, source_target_pairs={{8,12},{5,4},{6,8},{11,0},{24,28},{21,20},{22,24},{27,16},{12,13},... | collective-permute-start | bytes 245768 | tf_op jit(solution)/shard_map/ppermute | solution.py:302
  10.3 5.3 %collective-permute-start.6 = (bf16[2,576,128]{2,1,0:T(8,128)(2,1)S(1)}, bf16[2,576,128]{2,1,0:T(8,128)(2,1)S(1)}, u32[]{:S(2)}, u32[]{:S(2)}) collective-permute-start(bf16[2,576,128]{2,1,0:T(8,128)(2,1)S(1)} %shard_map.68), channel_id=1, source_target_pairs={{0,4},{4,0},{8,12},{12,8},{16,20},{20,16},{24,28},{28,24},{1,5},{5... | collective-permute-start | bytes 884744 | tf_op jit(solution)/shard_map/ppermute | solution.py:291
  14.1 1.4 %collective-permute-start.7 = (bf16[576,128]{1,0:T(8,128)(2,1)S(1)}, bf16[576,128]{1,0:T(8,128)(2,1)S(1)}, u32[]{:S(2)}, u32[]{:S(2)}) collective-permute-start(bf16[576,128]{1,0:T(8,128)(2,1)S(1)} %collective-permute-done.4.refs_4_), channel_id=1, source_target_pairs={{0,4},{4,0},{8,12},{12,8},{16,20},{20,16},{24,28},{28,24},{1,5},{5... | collective-permute-start | bytes 442376 | tf_op jit(solution)/shard_map/ppermute | solution.py:291
  14.1 1.6 %collective-permute-start.8 = (bf16[576,128]{1,0:T(8,128)(2,1)S(1)}, bf16[576,128]{1,0:T(8,128)(2,1)S(1)}, u32[]{:S(2)}, u32[]{:S(2)}) collective-permute-start(bf16[576,128]{1,0:T(8,128)(2,1)S(1)} %collective-permute-done.5.refs_5_), channel_id=1, source_target_pairs={{0,4},{4,0},{8,12},{12,8},{16,20},{20,16},{24,28},{28,24},{1,5},{5... | collective-permute-start | bytes 442376 | tf_op jit(solution)/shard_map/ppermute | solution.py:291
  14.6 11.3 %copy-start = (bf16[16,512,128]{2,1,0:T(8,128)(2,1)S(1)}, bf16[16,512,128]{2,1,0:T(8,128)(2,1)}, u32[]{:S(2)}) copy-start(bf16[16,512,128]{2,1,0:T(8,128)(2,1)} %w_ref.3) | copy-start | bytes 6291460
  16.4 7.3 %collective-permute-start.10 = (bf16[64,512]{1,0:T(8,128)(2,1)S(1)}, bf16[64,512]{1,0:T(8,128)(2,1)S(1)}, u32[]{:S(2)}, u32[]{:S(2)}) collective-permute-start(bf16[64,512]{1,0:T(8,128)(2,1)S(1)} %get-tuple-element.30), channel_id=1, source_target_pairs={{4,0},{12,1},{0,2},{8,3},{20,4},{28,5},{16,6},{24,7},{5,8},{13,9},... | collective-permute-start | bytes 196616 | tf_op jit(solution)/shard_map/ppermute | solution.py:332
  19.4 6.5 %collective-permute-start.9 = (bf16[64,512]{1,0:T(8,128)(2,1)S(1)}, bf16[64,512]{1,0:T(8,128)(2,1)S(1)}, u32[]{:S(2)}, u32[]{:S(2)}) collective-permute-start(bf16[64,512]{1,0:T(8,128)(2,1)S(1)} %get-tuple-element.29), channel_id=1, source_target_pairs={{12,0},{4,1},{8,2},{0,3},{28,4},{20,5},{24,6},{16,7},{13,8},{5,9},... | collective-permute-start | bytes 196616 | tf_op jit(solution)/shard_map/ppermute | solution.py:332

commit v19 on v15

--- a/solution.py
+++ b/solution.py
@@ -38,7 +38,7 @@
 
 
 def partner(k, core):
-    return (0, 3, 1 ^ 3 * core, 2 ^ 3 * core)[k]
+    return (0, 1 ^ 3 * core, 3, 2 ^ 3 * core)[k]
 
 
 def pick_kernel(per_device, cache_hbm, q_hbm, new_hbm, len_hbm, *refs):

time: 26.5 us -> 27.3 us (1.030)
  waiting for transfers between devices: 12.1 us -> 14.7 us
  starting transfers between devices: 9.4 us -> 7.62 us
    ppermute x3, waiting for transfers between devices: 3.53 us -> 6.4 us  [whole_sequences(): lax.ppermute(picked[k], 'seq', in_plane(lambda g, t: (g ^ partner(k, t))...]
    ppermute x3, starting transfers between devices: 1.81 us -> 0.59 us  [whole_sequences(): lax.ppermute(keys, 'seq', other_core)]
    ppermute x2, waiting for transfers between devices: 0.74 us -> 0.01 us  [whole_sequences(): lax.ppermute(pieces[k], both, [(host(i, j), owner(i, j, leaves_as(k, j)))...]
    ppermute x2, starting transfers between devices: 3.85 us -> 3.28 us  [whole_sequences(): lax.ppermute(latent[k], both, [(owner(i, j, first_back(i // COPIES, j) ^...]
    ppermute x3, waiting for transfers between devices: 0.01 us -> 0.29 us  [whole_sequences(): lax.ppermute(keys, 'seq', other_core)]
where the time goes in v19:
time: 27.3 us; the launch traced here: 27.2 us
  waiting for transfers between devices  14.7 us (54%)
  starting transfers between devices  7.62 us (28%)
  Pallas kernels  4.75 us (17%)
    ppermute x3, waiting for transfers between devices, whole_sequences(): lax.ppermute(picked[k], 'seq', in_plane(lambda g, t: (g ^ partner(k, t))...  6.4 us
    ppermute x2, waiting for transfers between devices, whole_sequences(): lax.ppermute(latent[k], both, [(owner(i, j, first_back(i // COPIES, j) ^...  6.38 us
    ppermute x3, starting transfers between devices, whole_sequences(): lax.ppermute(picked[k], 'seq', in_plane(lambda g, t: (g ^ partner(k, t))...  3.55 us
    ppermute x2, starting transfers between devices, whole_sequences(): lax.ppermute(latent[k], both, [(owner(i, j, first_back(i // COPIES, j) ^...  3.28 us
    ppermute x1, waiting for transfers between devices, whole_sequences(): lax.ppermute(packed, both, [(flat(i, j), host(i, j)) for i, j in devices])  1.64 us
    pallas_call x1, Pallas kernels, whole_sequences(): pl.pallas_call(functools.partial(pick_kernel, per_device), out_shape=[jax...  1.38 us
    pallas_call x1, Pallas kernels, whole_sequences(): pl.pallas_call(functools.partial(project_kernel, per_device), out_shape=j...  1.06 us
    pallas_call x1, Pallas kernels, whole_sequences(): pl.pallas_call(functools.partial(begin_kernel, owners, per_device, heads)...  0.76 us
  transfers between devices with their start and end apart: 11, of which 7 were waited for; matrix products, arithmetic and copies ran while one was open for 0% of the time, Pallas kernels for 6%

profile of v19, /device:TPU:6, one launch (start us, length us, event | category | flops | bytes accessed | tf_op | source)
XLA Modules:
  0.0 27.2 jit_solution(10139067388011832375)
XLA Ops:
  0.0 1.4 %shard_map.64 = (bf16[576,128]{1,0:T(8,128)(2,1)S(1)}, bf16[576,128]{1,0:T(8,128)(2,1)S(1)}, bf16[576,128]{1,0:T(8,128)(2,1)S(1)}, bf16[576,128]{1,0:T(8,128)(2,...) custom-call(bf16[4,576,128]{2,1,0:T(8,128)(2,1)} %bitcast.1, bf16[8,16,192]{2,1,0:T(8,128)(2,1)} %q_hbm.1, ...), custom_call_target="tpu_custom_call" | custom-call | flops 20000000000 | tf_op jit(solution)/shard_map/pallas_call | solution.py:245
  1.4 0.1 collective-permute-start
  1.5 0.6 %collective-permute-start.3 = (bf16[576,128]{1,0:T(8,128)(2,1)S(1)}, bf16[576,128]{1,0:T(8,128)(2,1)S(1)}, u32[]{:S(2)}, u32[]{:S(2)}) collective-permute-start(bf16[576,128]{1,0:T(8,128)(2,1)S(1)} %get-tuple-element.24), channel_id=1, source_target_pairs={{0,8},{4,20},{8,0},{12,28},{16,24},{20,4},{24,16},{28,12},{1,9},{5... | collective-permute-start | bytes 442376 | tf_op jit(solution)/shard_map/ppermute | solution.py:265
  2.1 1.4 %collective-permute-start.4 = (bf16[576,128]{1,0:T(8,128)(2,1)S(1)}, bf16[576,128]{1,0:T(8,128)(2,1)S(1)}, u32[]{:S(2)}, u32[]{:S(2)}) collective-permute-start(bf16[576,128]{1,0:T(8,128)(2,1)S(1)} %get-tuple-element.25), channel_id=1, source_target_pairs={{0,24},{4,28},{8,16},{12,20},{16,8},{20,12},{24,0},{28,4},{1,25},{... | collective-permute-start | bytes 442376 | tf_op jit(solution)/shard_map/ppermute | solution.py:265
  3.5 1.5 %collective-permute-start.5 = (bf16[576,128]{1,0:T(8,128)(2,1)S(1)}, bf16[576,128]{1,0:T(8,128)(2,1)S(1)}, u32[]{:S(2)}, u32[]{:S(2)}) collective-permute-start(bf16[576,128]{1,0:T(8,128)(2,1)S(1)} %get-tuple-element.26), channel_id=1, source_target_pairs={{0,16},{4,12},{8,24},{12,4},{16,0},{20,28},{24,8},{28,20},{1,17},{... | collective-permute-start | bytes 442376 | tf_op jit(solution)/shard_map/ppermute | solution.py:265
  5.0 1.6 %collective-permute-done.packed_ref = bf16[128,256]{1,0:T(8,128)(2,1)S(1)} collective-permute-done((bf16[128,256]{1,0:T(8,128)(2,1)S(1)}, bf16[128,256]{1,0:T(8,128)(2,1)S(1)}, u32[]{:S(2)}, u32[]{:S(2)}) %collective-permute-start) | collective-permute-done | bytes 65568 | tf_op jit(solution)/shard_map/ppermute | solution.py:263
  6.7 0.5 %shard_map.65 = (bf16[64,640]{1,0:T(8,128)(2,1)S(1)}, bf16[64,640]{1,0:T(8,128)(2,1)S(1)}) custom-call(bf16[16,128,512]{2,1,0:T(8,128)(2,1)S(1)} %copy-done.1, bf16[128,256]{1,0:T(8,128)(2,1)S(1)} %collective-permute-done.packed_ref), custom_call_target="tpu_custom_call" | custom-call | flops 20000000000 | tf_op jit(solution)/shard_map/pallas_call | solution.py:279
  7.1 0.1 collective-permute-start.1
  7.2 0.1 collective-permute-start.2
  7.3 0.5 %collective-permute-done.3.refs_3_.second_ref = bf16[576,128]{1,0:T(8,128)(2,1)S(1)} collective-permute-done((bf16[576,128]{1,0:T(8,128)(2,1)S(1)}, bf16[576,128]{1,0:T(8,128)(2,1)S(1)}, u32[]{:S(2)}, u32[]{:S(2)}) %collective-permute-start.3) | collective-permute-done | bytes 147488 | tf_op jit(solution)/shard_map/ppermute | solution.py:265
  7.8 0.4 %shard_map.67 = bf16[2,576,128]{2,1,0:T(8,128)(2,1)S(1)} custom-call(bf16[576,128]{1,0:T(8,128)(2,1)S(1)} %get-tuple-element.23.refs_2_.first_ref, bf16[576,128]{1,0:T(8,128)(2,1)S(1)} %collective-permute-done.3.refs_3_.second_ref), custom_call_target="tpu_custom_call" | custom-call | tf_op jit(solution)/shard_map/pallas_call | solution.py:268
  8.2 0.1 collective-permute-start.6
  8.2 5.9 %collective-permute-done.4.refs_4_ = bf16[576,128]{1,0:T(8,128)(2,1)S(1)} collective-permute-done((bf16[576,128]{1,0:T(8,128)(2,1)S(1)}, bf16[576,128]{1,0:T(8,128)(2,1)S(1)}, u32[]{:S(2)}, u32[]{:S(2)}) %collective-permute-start.4) | collective-permute-done | bytes 147488 | tf_op jit(solution)/shard_map/ppermute | solution.py:265
  14.1 0.0 collective-permute-start.7
  14.1 0.0 collective-permute-done.5.refs_5_
  14.1 0.5 %collective-permute-start.8 = (bf16[576,128]{1,0:T(8,128)(2,1)S(1)}, bf16[576,128]{1,0:T(8,128)(2,1)S(1)}, u32[]{:S(2)}, u32[]{:S(2)}) collective-permute-start(bf16[576,128]{1,0:T(8,128)(2,1)S(1)} %collective-permute-done.5.refs_5_), channel_id=1, source_target_pairs={{0,4},{4,0},{8,12},{12,8},{16,20},{20,16},{24,28},{28,24},{1,5},{5... | collective-permute-start | bytes 442376 | tf_op jit(solution)/shard_map/ppermute | solution.py:277
  14.7 0.8 %shard_map.66 = (bf16[128,576]{1,0:T(8,128)(2,1)S(1)}, f32[128,128]{1,0:T(8,128)S(1)}, f32[128,128]{1,0:T(8,128)S(1)}, f32[128,512]{1,0:T(8,128)S(1)}) custom-call(s32[8,128]{1,0:T(8,128)S(1)} %get-tuple-element.19.limit_ref, bf16[64,640]{1,0:T(8,128)(2,1)S(1)} %collective-permute-done.1.refs_0_, bf16[64,640]{1,0:T(8,128)(2,1)S(1)} %collective-permute-done.2.refs_1_, ...), custom_call_target="tpu_custom_call" | custom-call | flops 20000000000 | tf_op jit(solution)/shard_map/pallas_call | solution.py:296
  15.4 0.1 collective-permute-done.7.refs_0_
  15.5 0.2 collective-permute-done.8.refs_1_
  15.7 0.7 %shard_map.68 = (bf16[64,512]{1,0:T(8,128)(2,1)S(1)}, bf16[64,512]{1,0:T(8,128)(2,1)S(1)}) custom-call(s32[8,128]{1,0:T(8,128)S(1)} %get-tuple-element.19.limit_ref, bf16[128,576]{1,0:T(8,128)(2,1)S(1)} %get-tuple-element.27.q_ref, f32[128,128]{1,0:T(8,128)S(1)} %get-tuple-element.28.top_ref, f32[128,128]{1,0:T(8,128)S(1)} %get-tuple-element.29.total_ref, ...), custom_call_target="tpu_custom_call" | custom-call | tf_op jit(solution)/shard_map/pallas_call | solution.py:309
  16.4 3.3 %collective-permute-start.10 = (bf16[64,512]{1,0:T(8,128)(2,1)S(1)}, bf16[64,512]{1,0:T(8,128)(2,1)S(1)}, u32[]{:S(2)}, u32[]{:S(2)}) collective-permute-start(bf16[64,512]{1,0:T(8,128)(2,1)S(1)} %get-tuple-element.32), channel_id=1, source_target_pairs={{4,0},{12,1},{0,2},{8,3},{20,4},{28,5},{16,6},{24,7},{5,8},{13,9},... | collective-permute-start | bytes 196616 | tf_op jit(solution)/shard_map/ppermute | solution.py:318
  19.7 4.1 %collective-permute-done.10.refs_1_ = bf16[64,512]{1,0:T(8,128)(2,1)S(1)} collective-permute-done((bf16[64,512]{1,0:T(8,128)(2,1)S(1)}, bf16[64,512]{1,0:T(8,128)(2,1)S(1)}, u32[]{:S(2)}, u32[]{:S(2)}) %collective-permute-start.10) | collective-permute-done | bytes 65568 | tf_op jit(solution)/shard_map/ppermute | solution.py:318
  23.8 2.3 %collective-permute-done.9.refs_0_ = bf16[64,512]{1,0:T(8,128)(2,1)S(1)} collective-permute-done((bf16[64,512]{1,0:T(8,128)(2,1)S(1)}, bf16[64,512]{1,0:T(8,128)(2,1)S(1)}, u32[]{:S(2)}, u32[]{:S(2)}) %collective-permute-start.9) | collective-permute-done | bytes 65568 | tf_op jit(solution)/shard_map/ppermute | solution.py:318
  26.1 1.1 %shard_map.69 = bf16[8,16,128]{2,1,0:T(8,128)(2,1)} custom-call(bf16[16,512,128]{2,1,0:T(8,128)(2,1)S(1)} %copy-done, bf16[64,512]{1,0:T(8,128)(2,1)S(1)} %collective-permute-done.9.refs_0_, bf16[64,512]{1,0:T(8,128)(2,1)S(1)} %collective-permute-done.10.refs_1_), custom_call_target="tpu_custom_call" | custom-call | tf_op jit(solution)/shard_map/pallas_call | solution.py:325
  (8 shorter events, 0.0 us)
Async XLA Ops:
  0.0 6.7 %copy-start.1 = (bf16[16,128,512]{2,1,0:T(8,128)(2,1)S(1)}, bf16[16,128,512]{2,1,0:T(8,128)(2,1)}, u32[]{:S(2)}) copy-start(bf16[16,128,512]{2,1,0:T(8,128)(2,1)} %w_ref.2) | copy-start | bytes 6291460
  1.4 5.3 %collective-permute-start = (bf16[128,256]{1,0:T(8,128)(2,1)S(1)}, bf16[128,256]{1,0:T(8,128)(2,1)S(1)}, u32[]{:S(2)}, u32[]{:S(2)}) collective-permute-start(bf16[128,256]{1,0:T(8,128)(2,1)S(1)} %get-tuple-element.20), channel_id=1, source_target_pairs={{0,8},{1,5},{2,6},{3,11},{4,24},{5,21},{6,22},{7,27},{8,12},{9,1},... | collective-permute-start | bytes 196616 | tf_op jit(solution)/shard_map/ppermute | solution.py:263
  1.5 6.3 %collective-permute-start.3 = (bf16[576,128]{1,0:T(8,128)(2,1)S(1)}, bf16[576,128]{1,0:T(8,128)(2,1)S(1)}, u32[]{:S(2)}, u32[]{:S(2)}) collective-permute-start(bf16[576,128]{1,0:T(8,128)(2,1)S(1)} %get-tuple-element.24), channel_id=1, source_target_pairs={{0,8},{4,20},{8,0},{12,28},{16,24},{20,4},{24,16},{28,12},{1,9},{5... | collective-permute-start | bytes 442376 | tf_op jit(solution)/shard_map/ppermute | solution.py:265
  2.1 12.1 %collective-permute-start.4 = (bf16[576,128]{1,0:T(8,128)(2,1)S(1)}, bf16[576,128]{1,0:T(8,128)(2,1)S(1)}, u32[]{:S(2)}, u32[]{:S(2)}) collective-permute-start(bf16[576,128]{1,0:T(8,128)(2,1)S(1)} %get-tuple-element.25), channel_id=1, source_target_pairs={{0,24},{4,28},{8,16},{12,20},{16,8},{20,12},{24,0},{28,4},{1,25},{... | collective-permute-start | bytes 442376 | tf_op jit(solution)/shard_map/ppermute | solution.py:265
  3.5 10.6 %collective-permute-start.5 = (bf16[576,128]{1,0:T(8,128)(2,1)S(1)}, bf16[576,128]{1,0:T(8,128)(2,1)S(1)}, u32[]{:S(2)}, u32[]{:S(2)}) collective-permute-start(bf16[576,128]{1,0:T(8,128)(2,1)S(1)} %get-tuple-element.26), channel_id=1, source_target_pairs={{0,16},{4,12},{8,24},{12,4},{16,0},{20,28},{24,8},{28,20},{1,17},{... | collective-permute-start | bytes 442376 | tf_op jit(solution)/shard_map/ppermute | solution.py:265
  7.1 7.5 %collective-permute-start.1 = (bf16[64,640]{1,0:T(8,128)(2,1)S(1)}, bf16[64,640]{1,0:T(8,128)(2,1)S(1)}, u32[]{:S(2)}, u32[]{:S(2)}) collective-permute-start(bf16[64,640]{1,0:T(8,128)(2,1)S(1)} %get-tuple-element.21), channel_id=1, source_target_pairs={{8,4},{5,12},{6,0},{11,8},{24,20},{21,28},{22,16},{27,24},{12,5},{... | collective-permute-start | bytes 245768 | tf_op jit(solution)/shard_map/ppermute | solution.py:288
  7.2 7.5 %collective-permute-start.2 = (bf16[64,640]{1,0:T(8,128)(2,1)S(1)}, bf16[64,640]{1,0:T(8,128)(2,1)S(1)}, u32[]{:S(2)}, u32[]{:S(2)}) collective-permute-start(bf16[64,640]{1,0:T(8,128)(2,1)S(1)} %get-tuple-element.22), channel_id=1, source_target_pairs={{8,12},{5,4},{6,8},{11,0},{24,28},{21,20},{22,24},{27,16},{12,13},... | collective-permute-start | bytes 245768 | tf_op jit(solution)/shard_map/ppermute | solution.py:288
  8.2 7.6 %collective-permute-start.6 = (bf16[2,576,128]{2,1,0:T(8,128)(2,1)S(1)}, bf16[2,576,128]{2,1,0:T(8,128)(2,1)S(1)}, u32[]{:S(2)}, u32[]{:S(2)}) collective-permute-start(bf16[2,576,128]{2,1,0:T(8,128)(2,1)S(1)} %shard_map.67), channel_id=1, source_target_pairs={{0,4},{4,0},{8,12},{12,8},{16,20},{20,16},{24,28},{28,24},{1,5},{5... | collective-permute-start | bytes 884744 | tf_op jit(solution)/shard_map/ppermute | solution.py:277
  14.1 1.4 %collective-permute-start.7 = (bf16[576,128]{1,0:T(8,128)(2,1)S(1)}, bf16[576,128]{1,0:T(8,128)(2,1)S(1)}, u32[]{:S(2)}, u32[]{:S(2)}) collective-permute-start(bf16[576,128]{1,0:T(8,128)(2,1)S(1)} %collective-permute-done.4.refs_4_), channel_id=1, source_target_pairs={{0,4},{4,0},{8,12},{12,8},{16,20},{20,16},{24,28},{28,24},{1,5},{5... | collective-permute-start | bytes 442376 | tf_op jit(solution)/shard_map/ppermute | solution.py:277
  14.1 1.6 %collective-permute-start.8 = (bf16[576,128]{1,0:T(8,128)(2,1)S(1)}, bf16[576,128]{1,0:T(8,128)(2,1)S(1)}, u32[]{:S(2)}, u32[]{:S(2)}) collective-permute-start(bf16[576,128]{1,0:T(8,128)(2,1)S(1)} %collective-permute-done.5.refs_5_), channel_id=1, source_target_pairs={{0,4},{4,0},{8,12},{12,8},{16,20},{20,16},{24,28},{28,24},{1,5},{5... | collective-permute-start | bytes 442376 | tf_op jit(solution)/shard_map/ppermute | solution.py:277
  14.7 11.5 %copy-start = (bf16[16,512,128]{2,1,0:T(8,128)(2,1)S(1)}, bf16[16,512,128]{2,1,0:T(8,128)(2,1)}, u32[]{:S(2)}) copy-start(bf16[16,512,128]{2,1,0:T(8,128)(2,1)} %w_ref.3) | copy-start | bytes 6291460
  16.4 7.4 %collective-permute-start.10 = (bf16[64,512]{1,0:T(8,128)(2,1)S(1)}, bf16[64,512]{1,0:T(8,128)(2,1)S(1)}, u32[]{:S(2)}, u32[]{:S(2)}) collective-permute-start(bf16[64,512]{1,0:T(8,128)(2,1)S(1)} %get-tuple-element.32), channel_id=1, source_target_pairs={{4,0},{12,1},{0,2},{8,3},{20,4},{28,5},{16,6},{24,7},{5,8},{13,9},... | collective-permute-start | bytes 196616 | tf_op jit(solution)/shard_map/ppermute | solution.py:318
  19.7 6.4 %collective-permute-start.9 = (bf16[64,512]{1,0:T(8,128)(2,1)S(1)}, bf16[64,512]{1,0:T(8,128)(2,1)S(1)}, u32[]{:S(2)}, u32[]{:S(2)}) collective-permute-start(bf16[64,512]{1,0:T(8,128)(2,1)S(1)} %get-tuple-element.31), channel_id=1, source_target_pairs={{12,0},{4,1},{8,2},{0,3},{28,4},{20,5},{24,6},{16,7},{13,8},{5,9},... | collective-permute-start | bytes 196616 | tf_op jit(solution)/shard_map/ppermute | solution.py:318

commit v20 on v15

--- a/solution.py
+++ b/solution.py
@@ -25,6 +25,10 @@
 
 def far_half(plane, pair):
     return 1 * (plane <= 2 * pair)
+
+
+def near_half(home_chip, head_shard):
+    return home_chip // 2 == head_shard // 2
 
 
 def first_back(home_chip, head_shard):
@@ -199,8 +203,13 @@
 def project_kernel(per_device, w_ref, *refs):
     lat_refs, out_ref = refs[:-1], refs[-1]
     rows, heads, width = out_ref.shape
-    first = first_back(lax.axis_index("seq") // COPIES, lax.axis_index("head"))
-    parts = [jnp.where(first == a, lat_refs[1][...], lat_refs[0][...]) for a in range(per_device)]
+    chip, head_shard = lax.axis_index("seq") // COPIES, lax.axis_index("head")
+    first, near = first_back(chip, head_shard), near_half(chip, head_shard)
+    came = [
+        jnp.where(near, lat_refs[1][...], lat_refs[3][...]),
+        jnp.where(near, lat_refs[2][...], lat_refs[0][...]),
+    ]
+    parts = [jnp.where(first == a, came[0], came[1]) for a in range(per_device)]
     latent = jnp.concatenate(parts, axis=0)
     out = jnp.zeros((rows * heads, width), jnp.float32)
     own_head = lax.broadcasted_iota(jnp.int32, out.shape, 0) % heads
@@ -318,17 +327,21 @@
         lax.ppermute(
             latent[k],
             both,
-            [(owner(i, j, first_back(i // COPIES, j) ^ k), flat(i, j)) for i, j in devices],
+            [
+                (owner(i, j, first_back(i // COPIES, j) ^ k), flat(i, j))
+                for i, j in devices
+                if near_half(i // COPIES, j) == near
+            ],
         )
-        for k in range(per_device)
+        for near, k in ((False, 1), (True, 0), (True, 1), (False, 0))
     ]
     return pl.pallas_call(
         functools.partial(project_kernel, per_device),
         out_shape=jax.ShapeDtypeStruct((rows, heads, w_uv.shape[2]), jnp.bfloat16),
-        in_specs=[vmem] * (1 + per_device),
+        in_specs=[vmem] * (1 + len(back)),
         out_specs=vmem,
         compiler_params=params,
-    )(w_uv, *back[::-1])
+    )(w_uv, *back)
 
 
 def local_partial(

time: 26.5 us -> 33.3 us (1.26)
  the two profiles are of different devices: /device:TPU:6 before, /device:TPU:18 now
where the time goes in v20:
time: 33.3 us; the launch traced here: 33.1 us
  starting transfers between devices  15.3 us (46%)
  waiting for transfers between devices  13 us (39%)
  Pallas kernels  4.75 us (14%)
    ppermute x4, starting transfers between devices, whole_sequences(): lax.ppermute(latent[k], both, [(owner(i, j, first_back(i // COPIES, j) ^...  9.31 us
    ppermute x4, waiting for transfers between devices, whole_sequences(): lax.ppermute(latent[k], both, [(owner(i, j, first_back(i // COPIES, j) ^...  7.83 us
    ppermute x3, starting transfers between devices, whole_sequences(): lax.ppermute(picked[k], 'seq', in_plane(lambda g, t: (g ^ partner(k, t))...  3.49 us
    ppermute x3, waiting for transfers between devices, whole_sequences(): lax.ppermute(picked[k], 'seq', in_plane(lambda g, t: (g ^ partner(k, t))...  3.16 us
    ppermute x1, waiting for transfers between devices, whole_sequences(): lax.ppermute(packed, both, [(flat(i, j), host(i, j)) for i, j in devices])  1.41 us
    pallas_call x1, Pallas kernels, whole_sequences(): pl.pallas_call(functools.partial(pick_kernel, per_device), out_shape=[jax...  1.38 us
    ppermute x2, starting transfers between devices, whole_sequences(): lax.ppermute(pieces[k], both, [(host(i, j), owner(i, j, leaves_as(k, j)))...  1.15 us
    pallas_call x1, Pallas kernels, whole_sequences(): pl.pallas_call(functools.partial(project_kernel, per_device), out_shape=j...  1.07 us
  transfers between devices with their start and end apart: 13, of which 7 were waited for; matrix products, arithmetic and copies ran while one was open for 0% of the time, Pallas kernels for 5%

profile of v20, /device:TPU:18, one launch (start us, length us, event | category | flops | bytes accessed | tf_op | source)
XLA Modules:
  0.0 33.1 jit_solution(14619246507401453460)
XLA Ops:
  0.0 1.4 %shard_map.64 = (bf16[576,128]{1,0:T(8,128)(2,1)S(1)}, bf16[576,128]{1,0:T(8,128)(2,1)S(1)}, bf16[576,128]{1,0:T(8,128)(2,1)S(1)}, bf16[576,128]{1,0:T(8,128)(2,...) custom-call(bf16[4,576,128]{2,1,0:T(8,128)(2,1)} %bitcast.1, bf16[8,16,192]{2,1,0:T(8,128)(2,1)} %q_hbm.1, ...), custom_call_target="tpu_custom_call" | custom-call | flops 20000000000 | tf_op jit(solution)/shard_map/pallas_call | solution.py:254
  1.4 0.6 %collective-permute-start = (bf16[128,256]{1,0:T(8,128)(2,1)S(1)}, bf16[128,256]{1,0:T(8,128)(2,1)S(1)}, u32[]{:S(2)}, u32[]{:S(2)}) collective-permute-start(bf16[128,256]{1,0:T(8,128)(2,1)S(1)} %get-tuple-element.20), channel_id=1, source_target_pairs={{0,8},{1,5},{2,6},{3,11},{4,24},{5,21},{6,22},{7,27},{8,12},{9,1},... | collective-permute-start | bytes 196616 | tf_op jit(solution)/shard_map/ppermute | solution.py:272
  2.0 1.8 %collective-permute-start.3 = (bf16[576,128]{1,0:T(8,128)(2,1)S(1)}, bf16[576,128]{1,0:T(8,128)(2,1)S(1)}, u32[]{:S(2)}, u32[]{:S(2)}) collective-permute-start(bf16[576,128]{1,0:T(8,128)(2,1)S(1)} %get-tuple-element.24), channel_id=1, source_target_pairs={{0,24},{4,28},{8,16},{12,20},{16,8},{20,12},{24,0},{28,4},{1,25},{... | collective-permute-start | bytes 442376 | tf_op jit(solution)/shard_map/ppermute | solution.py:274
  3.8 1.1 %collective-permute-start.4 = (bf16[576,128]{1,0:T(8,128)(2,1)S(1)}, bf16[576,128]{1,0:T(8,128)(2,1)S(1)}, u32[]{:S(2)}, u32[]{:S(2)}) collective-permute-start(bf16[576,128]{1,0:T(8,128)(2,1)S(1)} %get-tuple-element.25), channel_id=1, source_target_pairs={{0,8},{4,20},{8,0},{12,28},{16,24},{20,4},{24,16},{28,12},{1,9},{5... | collective-permute-start | bytes 442376 | tf_op jit(solution)/shard_map/ppermute | solution.py:274
  4.9 0.5 %collective-permute-start.5 = (bf16[576,128]{1,0:T(8,128)(2,1)S(1)}, bf16[576,128]{1,0:T(8,128)(2,1)S(1)}, u32[]{:S(2)}, u32[]{:S(2)}) collective-permute-start(bf16[576,128]{1,0:T(8,128)(2,1)S(1)} %get-tuple-element.26), channel_id=1, source_target_pairs={{0,16},{4,12},{8,24},{12,4},{16,0},{20,28},{24,8},{28,20},{1,17},{... | collective-permute-start | bytes 442376 | tf_op jit(solution)/shard_map/ppermute | solution.py:274
  5.5 1.4 %collective-permute-done.packed_ref = bf16[128,256]{1,0:T(8,128)(2,1)S(1)} collective-permute-done((bf16[128,256]{1,0:T(8,128)(2,1)S(1)}, bf16[128,256]{1,0:T(8,128)(2,1)S(1)}, u32[]{:S(2)}, u32[]{:S(2)}) %collective-permute-start) | collective-permute-done | bytes 65568 | tf_op jit(solution)/shard_map/ppermute | solution.py:272
  6.9 0.5 %shard_map.65 = (bf16[64,640]{1,0:T(8,128)(2,1)S(1)}, bf16[64,640]{1,0:T(8,128)(2,1)S(1)}) custom-call(bf16[16,128,512]{2,1,0:T(8,128)(2,1)S(1)} %copy-done.1, bf16[128,256]{1,0:T(8,128)(2,1)S(1)} %collective-permute-done.packed_ref), custom_call_target="tpu_custom_call" | custom-call | flops 20000000000 | tf_op jit(solution)/shard_map/pallas_call | solution.py:288
  7.4 1.1 %collective-permute-start.1 = (bf16[64,640]{1,0:T(8,128)(2,1)S(1)}, bf16[64,640]{1,0:T(8,128)(2,1)S(1)}, u32[]{:S(2)}, u32[]{:S(2)}) collective-permute-start(bf16[64,640]{1,0:T(8,128)(2,1)S(1)} %get-tuple-element.21), channel_id=1, source_target_pairs={{8,4},{5,12},{6,0},{11,8},{24,20},{21,28},{22,16},{27,24},{12,5},{... | collective-permute-start | bytes 245768 | tf_op jit(solution)/shard_map/ppermute | solution.py:297
  8.5 1.0 %collective-permute-done.3.refs_3_.second_ref = bf16[576,128]{1,0:T(8,128)(2,1)S(1)} collective-permute-done((bf16[576,128]{1,0:T(8,128)(2,1)S(1)}, bf16[576,128]{1,0:T(8,128)(2,1)S(1)}, u32[]{:S(2)}, u32[]{:S(2)}) %collective-permute-start.3) | collective-permute-done | bytes 147488 | tf_op jit(solution)/shard_map/ppermute | solution.py:274
  9.6 0.4 %shard_map.67 = bf16[2,576,128]{2,1,0:T(8,128)(2,1)S(1)} custom-call(bf16[576,128]{1,0:T(8,128)(2,1)S(1)} %get-tuple-element.23.refs_2_.first_ref, bf16[576,128]{1,0:T(8,128)(2,1)S(1)} %collective-permute-done.3.refs_3_.second_ref), custom_call_target="tpu_custom_call" | custom-call | tf_op jit(solution)/shard_map/pallas_call | solution.py:277
  9.9 0.1 collective-permute-start.6
  10.1 2.1 %collective-permute-done.4.refs_4_ = bf16[576,128]{1,0:T(8,128)(2,1)S(1)} collective-permute-done((bf16[576,128]{1,0:T(8,128)(2,1)S(1)}, bf16[576,128]{1,0:T(8,128)(2,1)S(1)}, u32[]{:S(2)}, u32[]{:S(2)}) %collective-permute-start.4) | collective-permute-done | bytes 147488 | tf_op jit(solution)/shard_map/ppermute | solution.py:274
  12.2 0.6 %collective-permute-start.7 = (bf16[576,128]{1,0:T(8,128)(2,1)S(1)}, bf16[576,128]{1,0:T(8,128)(2,1)S(1)}, u32[]{:S(2)}, u32[]{:S(2)}) collective-permute-start(bf16[576,128]{1,0:T(8,128)(2,1)S(1)} %collective-permute-done.4.refs_4_), channel_id=1, source_target_pairs={{0,4},{4,0},{8,12},{12,8},{16,20},{20,16},{24,28},{28,24},{1,5},{5... | collective-permute-start | bytes 442376 | tf_op jit(solution)/shard_map/ppermute | solution.py:286
  12.8 0.3 collective-permute-done.1.refs_0_
  13.1 0.8 %shard_map.66 = (bf16[128,576]{1,0:T(8,128)(2,1)S(1)}, f32[128,128]{1,0:T(8,128)S(1)}, f32[128,128]{1,0:T(8,128)S(1)}, f32[128,512]{1,0:T(8,128)S(1)}) custom-call(s32[8,128]{1,0:T(8,128)S(1)} %get-tuple-element.19.limit_ref, bf16[64,640]{1,0:T(8,128)(2,1)S(1)} %collective-permute-done.1.refs_0_, bf16[64,640]{1,0:T(8,128)(2,1)S(1)} %collective-permute-done.2.refs_1_, ...), custom_call_target="tpu_custom_call" | custom-call | flops 20000000000 | tf_op jit(solution)/shard_map/pallas_call | solution.py:305
  13.8 0.3 collective-permute-done.8.refs_1_
  14.1 0.7 %shard_map.68 = (bf16[64,512]{1,0:T(8,128)(2,1)S(1)}, bf16[64,512]{1,0:T(8,128)(2,1)S(1)}) custom-call(s32[8,128]{1,0:T(8,128)S(1)} %get-tuple-element.19.limit_ref, bf16[128,576]{1,0:T(8,128)(2,1)S(1)} %get-tuple-element.27.q_ref, f32[128,128]{1,0:T(8,128)S(1)} %get-tuple-element.28.top_ref, f32[128,128]{1,0:T(8,128)S(1)} %get-tuple-element.29.total_ref, ...), custom_call_target="tpu_custom_call" | custom-call | tf_op jit(solution)/shard_map/pallas_call | solution.py:318
  14.9 5.4 %collective-permute-start.10 = (bf16[64,512]{1,0:T(8,128)(2,1)S(1)}, bf16[64,512]{1,0:T(8,128)(2,1)S(1)}, u32[]{:S(2)}, u32[]{:S(2)}) collective-permute-start(bf16[64,512]{1,0:T(8,128)(2,1)S(1)} %get-tuple-element.32), channel_id=1, source_target_pairs={{4,0},{12,1},{20,4},{28,5},{5,8},{13,9},{21,12},{29,13},{2,18},{10... | collective-permute-start | bytes 196616 | tf_op jit(solution)/shard_map/ppermute | solution.py:327
  20.3 1.3 %collective-permute-start.11 = (bf16[64,512]{1,0:T(8,128)(2,1)S(1)}, bf16[64,512]{1,0:T(8,128)(2,1)S(1)}, u32[]{:S(2)}, u32[]{:S(2)}) collective-permute-start(bf16[64,512]{1,0:T(8,128)(2,1)S(1)} %get-tuple-element.31), channel_id=1, source_target_pairs={{12,0},{4,1},{28,4},{20,5},{13,8},{5,9},{29,12},{21,13},{10,18},{2... | collective-permute-start | bytes 196616 | tf_op jit(solution)/shard_map/ppermute | solution.py:327
  21.6 1.3 %collective-permute-start.12 = (bf16[64,512]{1,0:T(8,128)(2,1)S(1)}, bf16[64,512]{1,0:T(8,128)(2,1)S(1)}, u32[]{:S(2)}, u32[]{:S(2)}) collective-permute-start(bf16[64,512]{1,0:T(8,128)(2,1)S(1)} %get-tuple-element.32), channel_id=1, source_target_pairs={{0,2},{8,3},{16,6},{24,7},{9,10},{1,11},{25,14},{17,15},{14,16},{6... | collective-permute-start | bytes 196616 | tf_op jit(solution)/shard_map/ppermute | solution.py:327
  22.9 1.3 %collective-permute-start.9 = (bf16[64,512]{1,0:T(8,128)(2,1)S(1)}, bf16[64,512]{1,0:T(8,128)(2,1)S(1)}, u32[]{:S(2)}, u32[]{:S(2)}) collective-permute-start(bf16[64,512]{1,0:T(8,128)(2,1)S(1)} %get-tuple-element.31), channel_id=1, source_target_pairs={{8,2},{0,3},{24,6},{16,7},{1,10},{9,11},{17,14},{25,15},{6,16},{14... | collective-permute-start | bytes 196616 | tf_op jit(solution)/shard_map/ppermute | solution.py:327
  24.2 3.5 %collective-permute-done.12.refs_3_ = bf16[64,512]{1,0:T(8,128)(2,1)S(1)} collective-permute-done((bf16[64,512]{1,0:T(8,128)(2,1)S(1)}, bf16[64,512]{1,0:T(8,128)(2,1)S(1)}, u32[]{:S(2)}, u32[]{:S(2)}) %collective-permute-start.12) | collective-permute-done | bytes 65568 | tf_op jit(solution)/shard_map/ppermute | solution.py:327
  27.8 4.3 %collective-permute-done.9.refs_0_ = bf16[64,512]{1,0:T(8,128)(2,1)S(1)} collective-permute-done((bf16[64,512]{1,0:T(8,128)(2,1)S(1)}, bf16[64,512]{1,0:T(8,128)(2,1)S(1)}, u32[]{:S(2)}, u32[]{:S(2)}) %collective-permute-start.9) | collective-permute-done | bytes 65568 | tf_op jit(solution)/shard_map/ppermute | solution.py:327
  32.1 1.1 %shard_map.69 = bf16[8,16,128]{2,1,0:T(8,128)(2,1)} custom-call(bf16[16,512,128]{2,1,0:T(8,128)(2,1)S(1)} %copy-done, bf16[64,512]{1,0:T(8,128)(2,1)S(1)} %collective-permute-done.9.refs_0_, bf16[64,512]{1,0:T(8,128)(2,1)S(1)} %collective-permute-done.10.refs_1_, bf16[64,512]{1,0:T(8,128)(2,1)S(1)} %collective-permute-done.11.refs_2_, ...), custom_call_target="tpu_custom_call" | custom-call | tf_op jit(solution)/shard_map/pallas_call | solution.py:338
  (12 shorter events, 0.0 us)
Async XLA Ops:
  0.0 6.9 %copy-start.1 = (bf16[16,128,512]{2,1,0:T(8,128)(2,1)S(1)}, bf16[16,128,512]{2,1,0:T(8,128)(2,1)}, u32[]{:S(2)}) copy-start(bf16[16,128,512]{2,1,0:T(8,128)(2,1)} %w_ref.2) | copy-start | bytes 6291460
  1.4 5.5 %collective-permute-start = (bf16[128,256]{1,0:T(8,128)(2,1)S(1)}, bf16[128,256]{1,0:T(8,128)(2,1)S(1)}, u32[]{:S(2)}, u32[]{:S(2)}) collective-permute-start(bf16[128,256]{1,0:T(8,128)(2,1)S(1)} %get-tuple-element.20), channel_id=1, source_target_pairs={{0,8},{1,5},{2,6},{3,11},{4,24},{5,21},{6,22},{7,27},{8,12},{9,1},... | collective-permute-start | bytes 196616 | tf_op jit(solution)/shard_map/ppermute | solution.py:272
  2.0 7.6 %collective-permute-start.3 = (bf16[576,128]{1,0:T(8,128)(2,1)S(1)}, bf16[576,128]{1,0:T(8,128)(2,1)S(1)}, u32[]{:S(2)}, u32[]{:S(2)}) collective-permute-start(bf16[576,128]{1,0:T(8,128)(2,1)S(1)} %get-tuple-element.24), channel_id=1, source_target_pairs={{0,24},{4,28},{8,16},{12,20},{16,8},{20,12},{24,0},{28,4},{1,25},{... | collective-permute-start | bytes 442376 | tf_op jit(solution)/shard_map/ppermute | solution.py:274
  3.8 8.4 %collective-permute-start.4 = (bf16[576,128]{1,0:T(8,128)(2,1)S(1)}, bf16[576,128]{1,0:T(8,128)(2,1)S(1)}, u32[]{:S(2)}, u32[]{:S(2)}) collective-permute-start(bf16[576,128]{1,0:T(8,128)(2,1)S(1)} %get-tuple-element.25), channel_id=1, source_target_pairs={{0,8},{4,20},{8,0},{12,28},{16,24},{20,4},{24,16},{28,12},{1,9},{5... | collective-permute-start | bytes 442376 | tf_op jit(solution)/shard_map/ppermute | solution.py:274
  4.9 7.8 %collective-permute-start.5 = (bf16[576,128]{1,0:T(8,128)(2,1)S(1)}, bf16[576,128]{1,0:T(8,128)(2,1)S(1)}, u32[]{:S(2)}, u32[]{:S(2)}) collective-permute-start(bf16[576,128]{1,0:T(8,128)(2,1)S(1)} %get-tuple-element.26), channel_id=1, source_target_pairs={{0,16},{4,12},{8,24},{12,4},{16,0},{20,28},{24,8},{28,20},{1,17},{... | collective-permute-start | bytes 442376 | tf_op jit(solution)/shard_map/ppermute | solution.py:274
  7.4 5.7 %collective-permute-start.1 = (bf16[64,640]{1,0:T(8,128)(2,1)S(1)}, bf16[64,640]{1,0:T(8,128)(2,1)S(1)}, u32[]{:S(2)}, u32[]{:S(2)}) collective-permute-start(bf16[64,640]{1,0:T(8,128)(2,1)S(1)} %get-tuple-element.21), channel_id=1, source_target_pairs={{8,4},{5,12},{6,0},{11,8},{24,20},{21,28},{22,16},{27,24},{12,5},{... | collective-permute-start | bytes 245768 | tf_op jit(solution)/shard_map/ppermute | solution.py:297
  8.5 4.5 %collective-permute-start.2 = (bf16[64,640]{1,0:T(8,128)(2,1)S(1)}, bf16[64,640]{1,0:T(8,128)(2,1)S(1)}, u32[]{:S(2)}, u32[]{:S(2)}) collective-permute-start(bf16[64,640]{1,0:T(8,128)(2,1)S(1)} %get-tuple-element.22), channel_id=1, source_target_pairs={{8,12},{5,4},{6,8},{11,0},{24,28},{21,20},{22,24},{27,16},{12,13},... | collective-permute-start | bytes 245768 | tf_op jit(solution)/shard_map/ppermute | solution.py:297
  9.9 4.2 %collective-permute-start.6 = (bf16[2,576,128]{2,1,0:T(8,128)(2,1)S(1)}, bf16[2,576,128]{2,1,0:T(8,128)(2,1)S(1)}, u32[]{:S(2)}, u32[]{:S(2)}) collective-permute-start(bf16[2,576,128]{2,1,0:T(8,128)(2,1)S(1)} %shard_map.67), channel_id=1, source_target_pairs={{0,4},{4,0},{8,12},{12,8},{16,20},{20,16},{24,28},{28,24},{1,5},{5... | collective-permute-start | bytes 884744 | tf_op jit(solution)/shard_map/ppermute | solution.py:286
  12.2 1.6 %collective-permute-start.7 = (bf16[576,128]{1,0:T(8,128)(2,1)S(1)}, bf16[576,128]{1,0:T(8,128)(2,1)S(1)}, u32[]{:S(2)}, u32[]{:S(2)}) collective-permute-start(bf16[576,128]{1,0:T(8,128)(2,1)S(1)} %collective-permute-done.4.refs_4_), channel_id=1, source_target_pairs={{0,4},{4,0},{8,12},{12,8},{16,20},{20,16},{24,28},{28,24},{1,5},{5... | collective-permute-start | bytes 442376 | tf_op jit(solution)/shard_map/ppermute | solution.py:286
  12.8 1.4 %collective-permute-start.8 = (bf16[576,128]{1,0:T(8,128)(2,1)S(1)}, bf16[576,128]{1,0:T(8,128)(2,1)S(1)}, u32[]{:S(2)}, u32[]{:S(2)}) collective-permute-start(bf16[576,128]{1,0:T(8,128)(2,1)S(1)} %collective-permute-done.5.refs_5_), channel_id=1, source_target_pairs={{0,4},{4,0},{8,12},{12,8},{16,20},{20,16},{24,28},{28,24},{1,5},{5... | collective-permute-start | bytes 442376 | tf_op jit(solution)/shard_map/ppermute | solution.py:286
  13.1 19.0 %copy-start = (bf16[16,512,128]{2,1,0:T(8,128)(2,1)S(1)}, bf16[16,512,128]{2,1,0:T(8,128)(2,1)}, u32[]{:S(2)}) copy-start(bf16[16,512,128]{2,1,0:T(8,128)(2,1)} %w_ref.3) | copy-start | bytes 6291460
  14.9 9.3 %collective-permute-start.10 = (bf16[64,512]{1,0:T(8,128)(2,1)S(1)}, bf16[64,512]{1,0:T(8,128)(2,1)S(1)}, u32[]{:S(2)}, u32[]{:S(2)}) collective-permute-start(bf16[64,512]{1,0:T(8,128)(2,1)S(1)} %get-tuple-element.32), channel_id=1, source_target_pairs={{4,0},{12,1},{20,4},{28,5},{5,8},{13,9},{21,12},{29,13},{2,18},{10... | collective-permute-start | bytes 196616 | tf_op jit(solution)/shard_map/ppermute | solution.py:327
  20.3 3.9 %collective-permute-start.11 = (bf16[64,512]{1,0:T(8,128)(2,1)S(1)}, bf16[64,512]{1,0:T(8,128)(2,1)S(1)}, u32[]{:S(2)}, u32[]{:S(2)}) collective-permute-start(bf16[64,512]{1,0:T(8,128)(2,1)S(1)} %get-tuple-element.31), channel_id=1, source_target_pairs={{12,0},{4,1},{28,4},{20,5},{13,8},{5,9},{29,12},{21,13},{10,18},{2... | collective-permute-start | bytes 196616 | tf_op jit(solution)/shard_map/ppermute | solution.py:327
  21.6 6.2 %collective-permute-start.12 = (bf16[64,512]{1,0:T(8,128)(2,1)S(1)}, bf16[64,512]{1,0:T(8,128)(2,1)S(1)}, u32[]{:S(2)}, u32[]{:S(2)}) collective-permute-start(bf16[64,512]{1,0:T(8,128)(2,1)S(1)} %get-tuple-element.32), channel_id=1, source_target_pairs={{0,2},{8,3},{16,6},{24,7},{9,10},{1,11},{25,14},{17,15},{14,16},{6... | collective-permute-start | bytes 196616 | tf_op jit(solution)/shard_map/ppermute | solution.py:327
  22.9 9.2 %collective-permute-start.9 = (bf16[64,512]{1,0:T(8,128)(2,1)S(1)}, bf16[64,512]{1,0:T(8,128)(2,1)S(1)}, u32[]{:S(2)}, u32[]{:S(2)}) collective-permute-start(bf16[64,512]{1,0:T(8,128)(2,1)S(1)} %get-tuple-element.31), channel_id=1, source_target_pairs={{8,2},{0,3},{24,6},{16,7},{1,10},{9,11},{17,14},{25,15},{6,16},{14... | collective-permute-start | bytes 196616 | tf_op jit(solution)/shard_map/ppermute | solution.py:327

commit v21 on v15

--- a/solution.py
+++ b/solution.py
@@ -191,7 +191,7 @@
     for k in range(per_device):
         for n in range(per_device):
 
-            @pl.when(sent_first ^ k == n)
+            @pl.when(sent_first ^ k != n)
             def _():
                 outs[k][...] = out[n * piece : (n + 1) * piece]
 
@@ -200,7 +200,7 @@
     lat_refs, out_ref = refs[:-1], refs[-1]
     rows, heads, width = out_ref.shape
     first = first_back(lax.axis_index("seq") // COPIES, lax.axis_index("head"))
-    parts = [jnp.where(first == a, lat_refs[1][...], lat_refs[0][...]) for a in range(per_device)]
+    parts = [jnp.where(first == a, lat_refs[0][...], lat_refs[1][...]) for a in range(per_device)]
     latent = jnp.concatenate(parts, axis=0)
     out = jnp.zeros((rows * heads, width), jnp.float32)
     own_head = lax.broadcasted_iota(jnp.int32, out.shape, 0) % heads
@@ -318,7 +318,7 @@
         lax.ppermute(
             latent[k],
             both,
-            [(owner(i, j, first_back(i // COPIES, j) ^ k), flat(i, j)) for i, j in devices],
+            [(owner(i, j, first_back(i // COPIES, j) ^ k ^ 1), flat(i, j)) for i, j in devices],
         )
         for k in range(per_device)
     ]

time: 26.5 us -> 27.4 us (1.034)
  starting transfers between devices: 9.4 us -> 10.4 us
    ppermute x2, starting transfers between devices: 3.85 us -> 4.87 us  [whole_sequences(): lax.ppermute(latent[k], both, [(owner(i, j, first_back(i // COPIES, j) ^...]
where the time goes in v21:
time: 27.4 us; the launch traced here: 27.3 us
  waiting for transfers between devices  12 us (44%)
  starting transfers between devices  10.4 us (38%)
  Pallas kernels  4.75 us (17%)
    ppermute x2, waiting for transfers between devices, whole_sequences(): lax.ppermute(latent[k], both, [(owner(i, j, first_back(i // COPIES, j) ^...  6.07 us
    ppermute x2, starting transfers between devices, whole_sequences(): lax.ppermute(latent[k], both, [(owner(i, j, first_back(i // COPIES, j) ^...  4.87 us
    ppermute x3, starting transfers between devices, whole_sequences(): lax.ppermute(picked[k], 'seq', in_plane(lambda g, t: (g ^ partner(k, t))...  3.55 us
    ppermute x3, waiting for transfers between devices, whole_sequences(): lax.ppermute(picked[k], 'seq', in_plane(lambda g, t: (g ^ partner(k, t))...  3.53 us
    ppermute x3, starting transfers between devices, whole_sequences(): lax.ppermute(keys, 'seq', other_core)  1.81 us
    ppermute x1, waiting for transfers between devices, whole_sequences(): lax.ppermute(packed, both, [(flat(i, j), host(i, j)) for i, j in devices])  1.63 us
    pallas_call x1, Pallas kernels, whole_sequences(): pl.pallas_call(functools.partial(pick_kernel, per_device), out_shape=[jax...  1.38 us
    pallas_call x1, Pallas kernels, whole_sequences(): pl.pallas_call(functools.partial(project_kernel, per_device), out_shape=j...  1.06 us
  transfers between devices with their start and end apart: 11, of which 7 were waited for; matrix products, arithmetic and copies ran while one was open for 0% of the time, Pallas kernels for 6%

profile of v21, /device:TPU:6, one launch (start us, length us, event | category | flops | bytes accessed | tf_op | source)
XLA Modules:
  0.0 27.3 jit_solution(18217712745960668456)
XLA Ops:
  0.0 1.4 %shard_map.64 = (bf16[576,128]{1,0:T(8,128)(2,1)S(1)}, bf16[576,128]{1,0:T(8,128)(2,1)S(1)}, bf16[576,128]{1,0:T(8,128)(2,1)S(1)}, bf16[576,128]{1,0:T(8,128)(2,...) custom-call(bf16[4,576,128]{2,1,0:T(8,128)(2,1)} %bitcast.1, bf16[8,16,192]{2,1,0:T(8,128)(2,1)} %q_hbm.1, ...), custom_call_target="tpu_custom_call" | custom-call | flops 20000000000 | tf_op jit(solution)/shard_map/pallas_call | solution.py:245
  1.4 0.1 collective-permute-start
  1.5 2.0 %collective-permute-start.3 = (bf16[576,128]{1,0:T(8,128)(2,1)S(1)}, bf16[576,128]{1,0:T(8,128)(2,1)S(1)}, u32[]{:S(2)}, u32[]{:S(2)}) collective-permute-start(bf16[576,128]{1,0:T(8,128)(2,1)S(1)} %get-tuple-element.24), channel_id=1, source_target_pairs={{0,24},{4,28},{8,16},{12,20},{16,8},{20,12},{24,0},{28,4},{1,25},{... | collective-permute-start | bytes 442376 | tf_op jit(solution)/shard_map/ppermute | solution.py:265
  3.4 0.1 collective-permute-start.4
  3.5 1.5 %collective-permute-start.5 = (bf16[576,128]{1,0:T(8,128)(2,1)S(1)}, bf16[576,128]{1,0:T(8,128)(2,1)S(1)}, u32[]{:S(2)}, u32[]{:S(2)}) collective-permute-start(bf16[576,128]{1,0:T(8,128)(2,1)S(1)} %get-tuple-element.26), channel_id=1, source_target_pairs={{0,16},{4,12},{8,24},{12,4},{16,0},{20,28},{24,8},{28,20},{1,17},{... | collective-permute-start | bytes 442376 | tf_op jit(solution)/shard_map/ppermute | solution.py:265
  5.0 1.6 %collective-permute-done.packed_ref = bf16[128,256]{1,0:T(8,128)(2,1)S(1)} collective-permute-done((bf16[128,256]{1,0:T(8,128)(2,1)S(1)}, bf16[128,256]{1,0:T(8,128)(2,1)S(1)}, u32[]{:S(2)}, u32[]{:S(2)}) %collective-permute-start) | collective-permute-done | bytes 65568 | tf_op jit(solution)/shard_map/ppermute | solution.py:263
  6.7 0.5 %shard_map.65 = (bf16[64,640]{1,0:T(8,128)(2,1)S(1)}, bf16[64,640]{1,0:T(8,128)(2,1)S(1)}) custom-call(bf16[16,128,512]{2,1,0:T(8,128)(2,1)S(1)} %copy-done.1, bf16[128,256]{1,0:T(8,128)(2,1)S(1)} %collective-permute-done.packed_ref), custom_call_target="tpu_custom_call" | custom-call | flops 20000000000 | tf_op jit(solution)/shard_map/pallas_call | solution.py:279
  7.1 0.1 collective-permute-start.1
  7.2 0.1 collective-permute-start.2
  7.3 2.0 %collective-permute-done.3.refs_3_.second_ref = bf16[576,128]{1,0:T(8,128)(2,1)S(1)} collective-permute-done((bf16[576,128]{1,0:T(8,128)(2,1)S(1)}, bf16[576,128]{1,0:T(8,128)(2,1)S(1)}, u32[]{:S(2)}, u32[]{:S(2)}) %collective-permute-start.3) | collective-permute-done | bytes 147488 | tf_op jit(solution)/shard_map/ppermute | solution.py:265
  9.3 0.4 %shard_map.67 = bf16[2,576,128]{2,1,0:T(8,128)(2,1)S(1)} custom-call(bf16[576,128]{1,0:T(8,128)(2,1)S(1)} %get-tuple-element.23.refs_2_.first_ref, bf16[576,128]{1,0:T(8,128)(2,1)S(1)} %collective-permute-done.3.refs_3_.second_ref), custom_call_target="tpu_custom_call" | custom-call | tf_op jit(solution)/shard_map/pallas_call | solution.py:268
  9.7 1.3 %collective-permute-start.6 = (bf16[2,576,128]{2,1,0:T(8,128)(2,1)S(1)}, bf16[2,576,128]{2,1,0:T(8,128)(2,1)S(1)}, u32[]{:S(2)}, u32[]{:S(2)}) collective-permute-start(bf16[2,576,128]{2,1,0:T(8,128)(2,1)S(1)} %shard_map.67), channel_id=1, source_target_pairs={{0,4},{4,0},{8,12},{12,8},{16,20},{20,16},{24,28},{28,24},{1,5},{5... | collective-permute-start | bytes 884744 | tf_op jit(solution)/shard_map/ppermute | solution.py:277
  11.0 1.5 %collective-permute-done.4.refs_4_ = bf16[576,128]{1,0:T(8,128)(2,1)S(1)} collective-permute-done((bf16[576,128]{1,0:T(8,128)(2,1)S(1)}, bf16[576,128]{1,0:T(8,128)(2,1)S(1)}, u32[]{:S(2)}, u32[]{:S(2)}) %collective-permute-start.4) | collective-permute-done | bytes 147488 | tf_op jit(solution)/shard_map/ppermute | solution.py:265
  12.5 0.3 %collective-permute-start.7 = (bf16[576,128]{1,0:T(8,128)(2,1)S(1)}, bf16[576,128]{1,0:T(8,128)(2,1)S(1)}, u32[]{:S(2)}, u32[]{:S(2)}) collective-permute-start(bf16[576,128]{1,0:T(8,128)(2,1)S(1)} %collective-permute-done.4.refs_4_), channel_id=1, source_target_pairs={{0,4},{4,0},{8,12},{12,8},{16,20},{20,16},{24,28},{28,24},{1,5},{5... | collective-permute-start | bytes 442376 | tf_op jit(solution)/shard_map/ppermute | solution.py:277
  12.8 0.2 collective-permute-start.8
  13.0 0.6 %collective-permute-done.1.refs_0_ = bf16[64,640]{1,0:T(8,128)(2,1)S(1)} collective-permute-done((bf16[64,640]{1,0:T(8,128)(2,1)S(1)}, bf16[64,640]{1,0:T(8,128)(2,1)S(1)}, u32[]{:S(2)}, u32[]{:S(2)}) %collective-permute-start.1) | collective-permute-done | bytes 81952 | tf_op jit(solution)/shard_map/ppermute | solution.py:288
  13.6 0.1 collective-permute-done.2.refs_1_
  13.7 0.8 %shard_map.66 = (bf16[128,576]{1,0:T(8,128)(2,1)S(1)}, f32[128,128]{1,0:T(8,128)S(1)}, f32[128,128]{1,0:T(8,128)S(1)}, f32[128,512]{1,0:T(8,128)S(1)}) custom-call(s32[8,128]{1,0:T(8,128)S(1)} %get-tuple-element.19.limit_ref, bf16[64,640]{1,0:T(8,128)(2,1)S(1)} %collective-permute-done.1.refs_0_, bf16[64,640]{1,0:T(8,128)(2,1)S(1)} %collective-permute-done.2.refs_1_, ...), custom_call_target="tpu_custom_call" | custom-call | flops 20000000000 | tf_op jit(solution)/shard_map/pallas_call | solution.py:296
  14.5 0.7 %shard_map.68 = (bf16[64,512]{1,0:T(8,128)(2,1)S(1)}, bf16[64,512]{1,0:T(8,128)(2,1)S(1)}) custom-call(s32[8,128]{1,0:T(8,128)S(1)} %get-tuple-element.19.limit_ref, bf16[128,576]{1,0:T(8,128)(2,1)S(1)} %get-tuple-element.27.q_ref, f32[128,128]{1,0:T(8,128)S(1)} %get-tuple-element.28.top_ref, f32[128,128]{1,0:T(8,128)S(1)} %get-tuple-element.29.total_ref, ...), custom_call_target="tpu_custom_call" | custom-call | tf_op jit(solution)/shard_map/pallas_call | solution.py:309
  15.3 3.7 %collective-permute-start.10 = (bf16[64,512]{1,0:T(8,128)(2,1)S(1)}, bf16[64,512]{1,0:T(8,128)(2,1)S(1)}, u32[]{:S(2)}, u32[]{:S(2)}) collective-permute-start(bf16[64,512]{1,0:T(8,128)(2,1)S(1)} %get-tuple-element.32), channel_id=1, source_target_pairs={{12,0},{4,1},{8,2},{0,3},{28,4},{20,5},{24,6},{16,7},{13,8},{5,9},... | collective-permute-start | bytes 196616 | tf_op jit(solution)/shard_map/ppermute | solution.py:318
  18.9 1.2 %collective-permute-start.9 = (bf16[64,512]{1,0:T(8,128)(2,1)S(1)}, bf16[64,512]{1,0:T(8,128)(2,1)S(1)}, u32[]{:S(2)}, u32[]{:S(2)}) collective-permute-start(bf16[64,512]{1,0:T(8,128)(2,1)S(1)} %get-tuple-element.31), channel_id=1, source_target_pairs={{4,0},{12,1},{0,2},{8,3},{20,4},{28,5},{16,6},{24,7},{5,8},{13,9},... | collective-permute-start | bytes 196616 | tf_op jit(solution)/shard_map/ppermute | solution.py:318
  20.1 1.9 %collective-permute-done.10.refs_1_ = bf16[64,512]{1,0:T(8,128)(2,1)S(1)} collective-permute-done((bf16[64,512]{1,0:T(8,128)(2,1)S(1)}, bf16[64,512]{1,0:T(8,128)(2,1)S(1)}, u32[]{:S(2)}, u32[]{:S(2)}) %collective-permute-start.10) | collective-permute-done | bytes 65568 | tf_op jit(solution)/shard_map/ppermute | solution.py:318
  22.1 4.1 %collective-permute-done.9.refs_0_ = bf16[64,512]{1,0:T(8,128)(2,1)S(1)} collective-permute-done((bf16[64,512]{1,0:T(8,128)(2,1)S(1)}, bf16[64,512]{1,0:T(8,128)(2,1)S(1)}, u32[]{:S(2)}, u32[]{:S(2)}) %collective-permute-start.9) | collective-permute-done | bytes 65568 | tf_op jit(solution)/shard_map/ppermute | solution.py:318
  26.2 1.1 %shard_map.69 = bf16[8,16,128]{2,1,0:T(8,128)(2,1)} custom-call(bf16[16,512,128]{2,1,0:T(8,128)(2,1)S(1)} %copy-done, bf16[64,512]{1,0:T(8,128)(2,1)S(1)} %collective-permute-done.9.refs_0_, bf16[64,512]{1,0:T(8,128)(2,1)S(1)} %collective-permute-done.10.refs_1_), custom_call_target="tpu_custom_call" | custom-call | tf_op jit(solution)/shard_map/pallas_call | solution.py:325
  (8 shorter events, 0.0 us)
Async XLA Ops:
  0.0 6.7 %copy-start.1 = (bf16[16,128,512]{2,1,0:T(8,128)(2,1)S(1)}, bf16[16,128,512]{2,1,0:T(8,128)(2,1)}, u32[]{:S(2)}) copy-start(bf16[16,128,512]{2,1,0:T(8,128)(2,1)} %w_ref.2) | copy-start | bytes 6291460
  1.4 5.3 %collective-permute-start = (bf16[128,256]{1,0:T(8,128)(2,1)S(1)}, bf16[128,256]{1,0:T(8,128)(2,1)S(1)}, u32[]{:S(2)}, u32[]{:S(2)}) collective-permute-start(bf16[128,256]{1,0:T(8,128)(2,1)S(1)} %get-tuple-element.20), channel_id=1, source_target_pairs={{0,8},{1,5},{2,6},{3,11},{4,24},{5,21},{6,22},{7,27},{8,12},{9,1},... | collective-permute-start | bytes 196616 | tf_op jit(solution)/shard_map/ppermute | solution.py:263
  1.5 7.9 %collective-permute-start.3 = (bf16[576,128]{1,0:T(8,128)(2,1)S(1)}, bf16[576,128]{1,0:T(8,128)(2,1)S(1)}, u32[]{:S(2)}, u32[]{:S(2)}) collective-permute-start(bf16[576,128]{1,0:T(8,128)(2,1)S(1)} %get-tuple-element.24), channel_id=1, source_target_pairs={{0,24},{4,28},{8,16},{12,20},{16,8},{20,12},{24,0},{28,4},{1,25},{... | collective-permute-start | bytes 442376 | tf_op jit(solution)/shard_map/ppermute | solution.py:265
  3.4 9.1 %collective-permute-start.4 = (bf16[576,128]{1,0:T(8,128)(2,1)S(1)}, bf16[576,128]{1,0:T(8,128)(2,1)S(1)}, u32[]{:S(2)}, u32[]{:S(2)}) collective-permute-start(bf16[576,128]{1,0:T(8,128)(2,1)S(1)} %get-tuple-element.25), channel_id=1, source_target_pairs={{0,8},{4,20},{8,0},{12,28},{16,24},{20,4},{24,16},{28,12},{1,9},{5... | collective-permute-start | bytes 442376 | tf_op jit(solution)/shard_map/ppermute | solution.py:265
  3.5 9.3 %collective-permute-start.5 = (bf16[576,128]{1,0:T(8,128)(2,1)S(1)}, bf16[576,128]{1,0:T(8,128)(2,1)S(1)}, u32[]{:S(2)}, u32[]{:S(2)}) collective-permute-start(bf16[576,128]{1,0:T(8,128)(2,1)S(1)} %get-tuple-element.26), channel_id=1, source_target_pairs={{0,16},{4,12},{8,24},{12,4},{16,0},{20,28},{24,8},{28,20},{1,17},{... | collective-permute-start | bytes 442376 | tf_op jit(solution)/shard_map/ppermute | solution.py:265
  7.1 6.5 %collective-permute-start.1 = (bf16[64,640]{1,0:T(8,128)(2,1)S(1)}, bf16[64,640]{1,0:T(8,128)(2,1)S(1)}, u32[]{:S(2)}, u32[]{:S(2)}) collective-permute-start(bf16[64,640]{1,0:T(8,128)(2,1)S(1)} %get-tuple-element.21), channel_id=1, source_target_pairs={{8,4},{5,12},{6,0},{11,8},{24,20},{21,28},{22,16},{27,24},{12,5},{... | collective-permute-start | bytes 245768 | tf_op jit(solution)/shard_map/ppermute | solution.py:288
  7.2 6.5 %collective-permute-start.2 = (bf16[64,640]{1,0:T(8,128)(2,1)S(1)}, bf16[64,640]{1,0:T(8,128)(2,1)S(1)}, u32[]{:S(2)}, u32[]{:S(2)}) collective-permute-start(bf16[64,640]{1,0:T(8,128)(2,1)S(1)} %get-tuple-element.22), channel_id=1, source_target_pairs={{8,12},{5,4},{6,8},{11,0},{24,28},{21,20},{22,24},{27,16},{12,13},... | collective-permute-start | bytes 245768 | tf_op jit(solution)/shard_map/ppermute | solution.py:288
  9.7 4.8 %collective-permute-start.6 = (bf16[2,576,128]{2,1,0:T(8,128)(2,1)S(1)}, bf16[2,576,128]{2,1,0:T(8,128)(2,1)S(1)}, u32[]{:S(2)}, u32[]{:S(2)}) collective-permute-start(bf16[2,576,128]{2,1,0:T(8,128)(2,1)S(1)} %shard_map.67), channel_id=1, source_target_pairs={{0,4},{4,0},{8,12},{12,8},{16,20},{20,16},{24,28},{28,24},{1,5},{5... | collective-permute-start | bytes 884744 | tf_op jit(solution)/shard_map/ppermute | solution.py:277
  12.5 2.0 %collective-permute-start.7 = (bf16[576,128]{1,0:T(8,128)(2,1)S(1)}, bf16[576,128]{1,0:T(8,128)(2,1)S(1)}, u32[]{:S(2)}, u32[]{:S(2)}) collective-permute-start(bf16[576,128]{1,0:T(8,128)(2,1)S(1)} %collective-permute-done.4.refs_4_), channel_id=1, source_target_pairs={{0,4},{4,0},{8,12},{12,8},{16,20},{20,16},{24,28},{28,24},{1,5},{5... | collective-permute-start | bytes 442376 | tf_op jit(solution)/shard_map/ppermute | solution.py:277
  12.8 1.7 %collective-permute-start.8 = (bf16[576,128]{1,0:T(8,128)(2,1)S(1)}, bf16[576,128]{1,0:T(8,128)(2,1)S(1)}, u32[]{:S(2)}, u32[]{:S(2)}) collective-permute-start(bf16[576,128]{1,0:T(8,128)(2,1)S(1)} %collective-permute-done.5.refs_5_), channel_id=1, source_target_pairs={{0,4},{4,0},{8,12},{12,8},{16,20},{20,16},{24,28},{28,24},{1,5},{5... | collective-permute-start | bytes 442376 | tf_op jit(solution)/shard_map/ppermute | solution.py:277
  13.7 12.5 %copy-start = (bf16[16,512,128]{2,1,0:T(8,128)(2,1)S(1)}, bf16[16,512,128]{2,1,0:T(8,128)(2,1)}, u32[]{:S(2)}) copy-start(bf16[16,512,128]{2,1,0:T(8,128)(2,1)} %w_ref.3) | copy-start | bytes 6291460
  15.3 6.8 %collective-permute-start.10 = (bf16[64,512]{1,0:T(8,128)(2,1)S(1)}, bf16[64,512]{1,0:T(8,128)(2,1)S(1)}, u32[]{:S(2)}, u32[]{:S(2)}) collective-permute-start(bf16[64,512]{1,0:T(8,128)(2,1)S(1)} %get-tuple-element.32), channel_id=1, source_target_pairs={{12,0},{4,1},{8,2},{0,3},{28,4},{20,5},{24,6},{16,7},{13,8},{5,9},... | collective-permute-start | bytes 196616 | tf_op jit(solution)/shard_map/ppermute | solution.py:318
  18.9 7.3 %collective-permute-start.9 = (bf16[64,512]{1,0:T(8,128)(2,1)S(1)}, bf16[64,512]{1,0:T(8,128)(2,1)S(1)}, u32[]{:S(2)}, u32[]{:S(2)}) collective-permute-start(bf16[64,512]{1,0:T(8,128)(2,1)S(1)} %get-tuple-element.31), channel_id=1, source_target_pairs={{4,0},{12,1},{0,2},{8,3},{20,4},{28,5},{16,6},{24,7},{5,8},{13,9},... | collective-permute-start | bytes 196616 | tf_op jit(solution)/shard_map/ppermute | solution.py:318

commit v22 on v15

--- a/solution.py
+++ b/solution.py
@@ -41,22 +41,20 @@
     return (0, 3, 1 ^ 3 * core, 2 ^ 3 * core)[k]
 
 
-def pick_kernel(per_device, cache_hbm, q_hbm, new_hbm, len_hbm, *refs):
-    owners = cache_hbm.shape[0]
-    blocks, (out_ref, limit_ref, q_ref, new_ref, len_ref, sem) = refs[:owners], refs[owners:]
-    chip, core = lax.axis_index("seq") // COPIES, lax.axis_index("seq") % COPIES
+def pack_kernel(
+    per_device, owners, q_hbm, new_hbm, len_hbm, out_ref, limit_ref, q_ref, new_ref, len_ref, sem
+):
     moves = [
-        pltpu.make_async_copy(q_hbm, q_ref, sem.at[owners]),
-        pltpu.make_async_copy(new_hbm, new_ref, sem.at[owners + 1]),
-        pltpu.make_async_copy(len_hbm, len_ref, sem.at[owners + 2]),
-    ] + [
-        pltpu.make_async_copy(cache_hbm.at[chip ^ partner(k, core)], blocks[k], sem.at[k])
-        for k in range(owners)
+        pltpu.make_async_copy(q_hbm, q_ref, sem.at[0]),
+        pltpu.make_async_copy(new_hbm, new_ref, sem.at[1]),
+        pltpu.make_async_copy(len_hbm, len_ref, sem.at[2]),
     ]
     for move in moves:
         move.start()
-    moves[0].wait()
-    moves[1].wait()
+    for move in moves:
+        move.wait()
+    length = len_ref[lax.axis_index("head") * owners + lax.axis_index("seq") // COPIES]
+    limit_ref[...] = jnp.full(limit_ref.shape, length, limit_ref.dtype)
     heads, width = q_ref.shape[1:]
     fresh = new_ref[...].astype(jnp.float32)
     piece = SPEC * heads
@@ -69,10 +67,18 @@
             parts.append(jnp.zeros((spare, ROPE), jnp.float32))
         own = jnp.concatenate(parts, axis=0).astype(rows.dtype)
         out_ref[a * piece : (a + 1) * piece] = jnp.concatenate([rows, own], axis=1)
-    moves[2].wait()
-    length = len_ref[lax.axis_index("head") * owners + chip]
-    limit_ref[...] = jnp.full(limit_ref.shape, length, limit_ref.dtype)
-    for move in moves[3:]:
+
+
+def pick_kernel(cache_ref, *refs):
+    blocks, sem = refs[:-1], refs[-1]
+    chip, core = lax.axis_index("seq") // COPIES, lax.axis_index("seq") % COPIES
+    moves = [
+        pltpu.make_async_copy(cache_ref.at[chip ^ partner(k, core)], block, sem.at[k])
+        for k, block in enumerate(blocks)
+    ]
+    for move in moves:
+        move.start()
+    for move in moves:
         move.wait()
 
 
@@ -242,25 +248,33 @@
     def in_plane(move):
         return [(g * COPIES + t, move(g, t)) for g in range(owners) for t in range(COPIES)]
 
-    *picked, packed, limit = pl.pallas_call(
-        functools.partial(pick_kernel, per_device),
-        out_shape=[jax.ShapeDtypeStruct((width, slots), cache.dtype)] * owners
-        + [
+    packed, limit = pl.pallas_call(
+        functools.partial(pack_kernel, per_device, owners),
+        out_shape=[
             jax.ShapeDtypeStruct((all_rows, q_width + ROPE), queries.dtype),
             jax.ShapeDtypeStruct((8, slots), jnp.int32),
         ],
-        in_specs=[anywhere] * 4,
-        out_specs=[vmem] * (owners + 2),
+        in_specs=[anywhere] * 3,
+        out_specs=[vmem] * 2,
         scratch_shapes=[
             pltpu.VMEM(queries.shape, queries.dtype),
             pltpu.VMEM(new_latent.shape, new_latent.dtype),
             pltpu.SMEM(lengths.shape, lengths.dtype),
-            pltpu.SemaphoreType.DMA((owners + 3,)),
+            pltpu.SemaphoreType.DMA((3,)),
         ],
         compiler_params=params,
         cost_estimate=LONG,
-    )(*[in_hbm(x) for x in (jnp.swapaxes(cache, 1, 2), queries, new_latent, lengths)])
+    )(in_hbm(queries), in_hbm(new_latent), in_hbm(lengths))
     moved = lax.ppermute(packed, both, [(flat(i, j), host(i, j)) for i, j in devices])
+    picked = pl.pallas_call(
+        pick_kernel,
+        out_shape=[jax.ShapeDtypeStruct((width, slots), cache.dtype)] * owners,
+        in_specs=[anywhere],
+        out_specs=[vmem] * owners,
+        scratch_shapes=[pltpu.SemaphoreType.DMA((owners,))],
+        compiler_params=params,
+        cost_estimate=LONG,
+    )(jnp.swapaxes(cache, 1, 2))
     own_keys = [picked[0]] + [
         lax.ppermute(picked[k], "seq", in_plane(lambda g, t: (g ^ partner(k, t)) * COPIES + t))
         for k in range(1, owners)

time: 26.5 us -> 26.8 us (1.011)
  starting transfers between devices: 9.4 us -> 8.65 us
  Pallas kernels: 4.75 us -> 5.28 us
  waiting for transfers between devices: 12.1 us -> 12.5 us
    ppermute x3, waiting for transfers between devices: 3.53 us -> 5.68 us  [whole_sequences(): lax.ppermute(picked[k], 'seq', in_plane(lambda g, t: (g ^ partner(k, t))...]
    ppermute x3, starting transfers between devices: 1.81 us -> 0.58 us  [whole_sequences(): lax.ppermute(keys, 'seq', other_core)]
    ppermute x1, waiting for transfers between devices: 1.63 us -> 0.49 us  [whole_sequences(): lax.ppermute(packed, both, [(flat(i, j), host(i, j)) for i, j in devices])]
    ppermute x2, starting transfers between devices: 0.13 us -> 0.98 us  [whole_sequences(): lax.ppermute(pieces[k], both, [(host(i, j), owner(i, j, leaves_as(k, j)))...]
    ppermute x2, waiting for transfers between devices: 0.74 us -> 0.01 us  [whole_sequences(): lax.ppermute(pieces[k], both, [(host(i, j), owner(i, j, leaves_as(k, j)))...]
    pallas_call x1 -> x2, Pallas kernels: 1.38 us -> 1.91 us  [the longest x1 1.08 us: whole_sequences(): pl.pallas_call(functools.partial(pack_kernel, per_device, owners), out_sh...]
    ppermute x2, starting transfers between devices: 3.85 us -> 3.47 us  [whole_sequences(): lax.ppermute(latent[k], both, [(owner(i, j, first_back(i // COPIES, j) ^...]
    ppermute x3, waiting for transfers between devices: 0.01 us -> 0.29 us  [whole_sequences(): lax.ppermute(keys, 'seq', other_core)]
  transfers between devices with their start and end apart: 11 -> 11, of which waited for: 7 -> 7; matrix products, arithmetic and copies ran while one was open for 0% -> 0% of each run, Pallas kernels for 6% -> 9%
where the time goes in v22:
time: 26.8 us; the launch traced here: 26.5 us
  waiting for transfers between devices  12.5 us (47%)
  starting transfers between devices  8.65 us (32%)
  Pallas kernels  5.28 us (20%)
    ppermute x2, waiting for transfers between devices, whole_sequences(): lax.ppermute(latent[k], both, [(owner(i, j, first_back(i // COPIES, j) ^...  6.02 us
    ppermute x3, waiting for transfers between devices, whole_sequences(): lax.ppermute(picked[k], 'seq', in_plane(lambda g, t: (g ^ partner(k, t))...  5.68 us
    ppermute x3, starting transfers between devices, whole_sequences(): lax.ppermute(picked[k], 'seq', in_plane(lambda g, t: (g ^ partner(k, t))...  3.55 us
    ppermute x2, starting transfers between devices, whole_sequences(): lax.ppermute(latent[k], both, [(owner(i, j, first_back(i // COPIES, j) ^...  3.47 us
    pallas_call x1, Pallas kernels, whole_sequences(): pl.pallas_call(functools.partial(pack_kernel, per_device, owners), out_sh...  1.08 us
    pallas_call x1, Pallas kernels, whole_sequences(): pl.pallas_call(functools.partial(project_kernel, per_device), out_shape=j...  1.06 us
    ppermute x2, starting transfers between devices, whole_sequences(): lax.ppermute(pieces[k], both, [(host(i, j), owner(i, j, leaves_as(k, j)))...  0.98 us
    pallas_call x1, Pallas kernels, whole_sequences(): pl.pallas_call(pick_kernel, out_shape=[jax.ShapeDtypeStruct((width, slots...  0.82 us
  transfers between devices with their start and end apart: 11, of which 7 were waited for; matrix products, arithmetic and copies ran while one was open for 0% of the time, Pallas kernels for 9%

profile of v22, /device:TPU:6, one launch (start us, length us, event | category | flops | bytes accessed | tf_op | source)
XLA Modules:
  0.0 26.5 jit_solution(17048612510716153788)
XLA Ops:
  0.0 1.1 %shard_map.64 = (bf16[128,256]{1,0:T(8,128)(2,1)S(1)}, s32[8,128]{1,0:T(8,128)S(1)}) custom-call(bf16[8,16,192]{2,1,0:T(8,128)(2,1)} %q_hbm.1, bf16[8,576]{1,0:T(8,128)(2,1)} %new_hbm.1, s32[16]{0:T(128)} %len_hbm.1), custom_call_target="tpu_custom_call" | custom-call | flops 20000000000 | tf_op jit(solution)/shard_map/pallas_call | solution.py:251
  1.1 0.1 collective-permute-start
  1.2 0.8 %shard_map.66 = (bf16[576,128]{1,0:T(8,128)(2,1)S(1)}, bf16[576,128]{1,0:T(8,128)(2,1)S(1)}, bf16[576,128]{1,0:T(8,128)(2,1)S(1)}, bf16[576,128]{1,0:T(8,128)(2,1)S(1)}) custom-call(bf16[4,576,128]{2,1,0:T(8,128)(2,1)S(1)} %bitcast.1), custom_call_target="tpu_custom_call" | custom-call | flops 20000000000 | tf_op jit(solution)/shard_map/pallas_call | solution.py:269
  2.0 2.0 %collective-permute-start.3 = (bf16[576,128]{1,0:T(8,128)(2,1)S(1)}, bf16[576,128]{1,0:T(8,128)(2,1)S(1)}, u32[]{:S(2)}, u32[]{:S(2)}) collective-permute-start(bf16[576,128]{1,0:T(8,128)(2,1)S(1)} %get-tuple-element.24), channel_id=1, source_target_pairs={{0,24},{4,28},{8,16},{12,20},{16,8},{20,12},{24,0},{28,4},{1,25},{... | collective-permute-start | bytes 442376 | tf_op jit(solution)/shard_map/ppermute | solution.py:279
  4.0 0.1 collective-permute-start.4
  4.1 1.5 %collective-permute-start.5 = (bf16[576,128]{1,0:T(8,128)(2,1)S(1)}, bf16[576,128]{1,0:T(8,128)(2,1)S(1)}, u32[]{:S(2)}, u32[]{:S(2)}) collective-permute-start(bf16[576,128]{1,0:T(8,128)(2,1)S(1)} %get-tuple-element.26), channel_id=1, source_target_pairs={{0,16},{4,12},{8,24},{12,4},{16,0},{20,28},{24,8},{28,20},{1,17},{... | collective-permute-start | bytes 442376 | tf_op jit(solution)/shard_map/ppermute | solution.py:279
  5.6 0.5 %collective-permute-done.packed_ref = bf16[128,256]{1,0:T(8,128)(2,1)S(1)} collective-permute-done((bf16[128,256]{1,0:T(8,128)(2,1)S(1)}, bf16[128,256]{1,0:T(8,128)(2,1)S(1)}, u32[]{:S(2)}, u32[]{:S(2)}) %collective-permute-start) | collective-permute-done | bytes 65568 | tf_op jit(solution)/shard_map/ppermute | solution.py:268
  6.1 0.5 %shard_map.65 = (bf16[64,640]{1,0:T(8,128)(2,1)S(1)}, bf16[64,640]{1,0:T(8,128)(2,1)S(1)}) custom-call(bf16[16,128,512]{2,1,0:T(8,128)(2,1)S(1)} %copy-done.1, bf16[128,256]{1,0:T(8,128)(2,1)S(1)} %collective-permute-done.packed_ref), custom_call_target="tpu_custom_call" | custom-call | flops 20000000000 | tf_op jit(solution)/shard_map/pallas_call | solution.py:293
  6.5 0.1 collective-permute-start.1
  6.7 0.8 %collective-permute-start.2 = (bf16[64,640]{1,0:T(8,128)(2,1)S(1)}, bf16[64,640]{1,0:T(8,128)(2,1)S(1)}, u32[]{:S(2)}, u32[]{:S(2)}) collective-permute-start(bf16[64,640]{1,0:T(8,128)(2,1)S(1)} %get-tuple-element.22), channel_id=1, source_target_pairs={{8,12},{5,4},{6,8},{11,0},{24,28},{21,20},{22,24},{27,16},{12,13},... | collective-permute-start | bytes 245768 | tf_op jit(solution)/shard_map/ppermute | solution.py:302
  7.5 2.2 %collective-permute-done.3.refs_3_.second_ref = bf16[576,128]{1,0:T(8,128)(2,1)S(1)} collective-permute-done((bf16[576,128]{1,0:T(8,128)(2,1)S(1)}, bf16[576,128]{1,0:T(8,128)(2,1)S(1)}, u32[]{:S(2)}, u32[]{:S(2)}) %collective-permute-start.3) | collective-permute-done | bytes 147488 | tf_op jit(solution)/shard_map/ppermute | solution.py:279
  9.8 0.4 %shard_map.68 = bf16[2,576,128]{2,1,0:T(8,128)(2,1)S(1)} custom-call(bf16[576,128]{1,0:T(8,128)(2,1)S(1)} %get-tuple-element.23.refs_2_.first_ref, bf16[576,128]{1,0:T(8,128)(2,1)S(1)} %collective-permute-done.3.refs_3_.second_ref), custom_call_target="tpu_custom_call" | custom-call | tf_op jit(solution)/shard_map/pallas_call | solution.py:282
  10.1 0.1 collective-permute-start.6
  10.2 3.4 %collective-permute-done.4.refs_4_ = bf16[576,128]{1,0:T(8,128)(2,1)S(1)} collective-permute-done((bf16[576,128]{1,0:T(8,128)(2,1)S(1)}, bf16[576,128]{1,0:T(8,128)(2,1)S(1)}, u32[]{:S(2)}, u32[]{:S(2)}) %collective-permute-start.4) | collective-permute-done | bytes 147488 | tf_op jit(solution)/shard_map/ppermute | solution.py:279
  13.7 0.5 %collective-permute-start.8 = (bf16[576,128]{1,0:T(8,128)(2,1)S(1)}, bf16[576,128]{1,0:T(8,128)(2,1)S(1)}, u32[]{:S(2)}, u32[]{:S(2)}) collective-permute-start(bf16[576,128]{1,0:T(8,128)(2,1)S(1)} %collective-permute-done.5.refs_5_), channel_id=1, source_target_pairs={{0,4},{4,0},{8,12},{12,8},{16,20},{20,16},{24,28},{28,24},{1,5},{5... | collective-permute-start | bytes 442376 | tf_op jit(solution)/shard_map/ppermute | solution.py:291
  14.2 0.8 %shard_map.67 = (bf16[128,576]{1,0:T(8,128)(2,1)S(1)}, f32[128,128]{1,0:T(8,128)S(1)}, f32[128,128]{1,0:T(8,128)S(1)}, f32[128,512]{1,0:T(8,128)S(1)}) custom-call(s32[8,128]{1,0:T(8,128)S(1)} %get-tuple-element.19.limit_ref, bf16[64,640]{1,0:T(8,128)(2,1)S(1)} %collective-permute-done.1.refs_0_, bf16[64,640]{1,0:T(8,128)(2,1)S(1)} %collective-permute-done.2.refs_1_, ...), custom_call_target="tpu_custom_call" | custom-call | flops 20000000000 | tf_op jit(solution)/shard_map/pallas_call | solution.py:310
  15.0 0.1 collective-permute-done.7.refs_0_
  15.0 0.2 collective-permute-done.8.refs_1_
  15.3 0.7 %shard_map.69 = (bf16[64,512]{1,0:T(8,128)(2,1)S(1)}, bf16[64,512]{1,0:T(8,128)(2,1)S(1)}) custom-call(s32[8,128]{1,0:T(8,128)S(1)} %get-tuple-element.19.limit_ref, bf16[128,576]{1,0:T(8,128)(2,1)S(1)} %get-tuple-element.27.q_ref, f32[128,128]{1,0:T(8,128)S(1)} %get-tuple-element.28.top_ref, f32[128,128]{1,0:T(8,128)S(1)} %get-tuple-element.29.total_ref, ...), custom_call_target="tpu_custom_call" | custom-call | tf_op jit(solution)/shard_map/pallas_call | solution.py:323
  16.0 3.0 %collective-permute-start.10 = (bf16[64,512]{1,0:T(8,128)(2,1)S(1)}, bf16[64,512]{1,0:T(8,128)(2,1)S(1)}, u32[]{:S(2)}, u32[]{:S(2)}) collective-permute-start(bf16[64,512]{1,0:T(8,128)(2,1)S(1)} %get-tuple-element.32), channel_id=1, source_target_pairs={{4,0},{12,1},{0,2},{8,3},{20,4},{28,5},{16,6},{24,7},{5,8},{13,9},... | collective-permute-start | bytes 196616 | tf_op jit(solution)/shard_map/ppermute | solution.py:332
  19.0 0.4 %collective-permute-start.9 = (bf16[64,512]{1,0:T(8,128)(2,1)S(1)}, bf16[64,512]{1,0:T(8,128)(2,1)S(1)}, u32[]{:S(2)}, u32[]{:S(2)}) collective-permute-start(bf16[64,512]{1,0:T(8,128)(2,1)S(1)} %get-tuple-element.31), channel_id=1, source_target_pairs={{12,0},{4,1},{8,2},{0,3},{28,4},{20,5},{24,6},{16,7},{13,8},{5,9},... | collective-permute-start | bytes 196616 | tf_op jit(solution)/shard_map/ppermute | solution.py:332
  19.4 3.9 %collective-permute-done.10.refs_1_ = bf16[64,512]{1,0:T(8,128)(2,1)S(1)} collective-permute-done((bf16[64,512]{1,0:T(8,128)(2,1)S(1)}, bf16[64,512]{1,0:T(8,128)(2,1)S(1)}, u32[]{:S(2)}, u32[]{:S(2)}) %collective-permute-start.10) | collective-permute-done | bytes 65568 | tf_op jit(solution)/shard_map/ppermute | solution.py:332
  23.3 2.1 %collective-permute-done.9.refs_0_ = bf16[64,512]{1,0:T(8,128)(2,1)S(1)} collective-permute-done((bf16[64,512]{1,0:T(8,128)(2,1)S(1)}, bf16[64,512]{1,0:T(8,128)(2,1)S(1)}, u32[]{:S(2)}, u32[]{:S(2)}) %collective-permute-start.9) | collective-permute-done | bytes 65568 | tf_op jit(solution)/shard_map/ppermute | solution.py:332
  25.5 1.1 %shard_map.70 = bf16[8,16,128]{2,1,0:T(8,128)(2,1)} custom-call(bf16[16,512,128]{2,1,0:T(8,128)(2,1)S(1)} %copy-done, bf16[64,512]{1,0:T(8,128)(2,1)S(1)} %collective-permute-done.9.refs_0_, bf16[64,512]{1,0:T(8,128)(2,1)S(1)} %collective-permute-done.10.refs_1_), custom_call_target="tpu_custom_call" | custom-call | tf_op jit(solution)/shard_map/pallas_call | solution.py:339
  (11 shorter events, 0.0 us)
Async XLA Ops:
  0.0 1.2 %copy-start.2 = (bf16[4,128,576]{1,2,0:T(8,128)(2,1)S(1)}, bf16[4,128,576]{1,2,0:T(8,128)(2,1)}, u32[]{:S(2)}) copy-start(bf16[4,128,576]{1,2,0:T(8,128)(2,1)} %param.8) | copy-start | bytes 1769476
  1.1 5.0 %collective-permute-start = (bf16[128,256]{1,0:T(8,128)(2,1)S(1)}, bf16[128,256]{1,0:T(8,128)(2,1)S(1)}, u32[]{:S(2)}, u32[]{:S(2)}) collective-permute-start(bf16[128,256]{1,0:T(8,128)(2,1)S(1)} %get-tuple-element.20), channel_id=1, source_target_pairs={{0,8},{1,5},{2,6},{3,11},{4,24},{5,21},{6,22},{7,27},{8,12},{9,1},... | collective-permute-start | bytes 196616 | tf_op jit(solution)/shard_map/ppermute | solution.py:268
  1.2 4.9 %copy-start.1 = (bf16[16,128,512]{2,1,0:T(8,128)(2,1)S(1)}, bf16[16,128,512]{2,1,0:T(8,128)(2,1)}, u32[]{:S(2)}) copy-start(bf16[16,128,512]{2,1,0:T(8,128)(2,1)} %w_ref.2) | copy-start | bytes 6291460
  2.0 7.7 %collective-permute-start.3 = (bf16[576,128]{1,0:T(8,128)(2,1)S(1)}, bf16[576,128]{1,0:T(8,128)(2,1)S(1)}, u32[]{:S(2)}, u32[]{:S(2)}) collective-permute-start(bf16[576,128]{1,0:T(8,128)(2,1)S(1)} %get-tuple-element.24), channel_id=1, source_target_pairs={{0,24},{4,28},{8,16},{12,20},{16,8},{20,12},{24,0},{28,4},{1,25},{... | collective-permute-start | bytes 442376 | tf_op jit(solution)/shard_map/ppermute | solution.py:279
  4.0 9.7 %collective-permute-start.4 = (bf16[576,128]{1,0:T(8,128)(2,1)S(1)}, bf16[576,128]{1,0:T(8,128)(2,1)S(1)}, u32[]{:S(2)}, u32[]{:S(2)}) collective-permute-start(bf16[576,128]{1,0:T(8,128)(2,1)S(1)} %get-tuple-element.25), channel_id=1, source_target_pairs={{0,8},{4,20},{8,0},{12,28},{16,24},{20,4},{24,16},{28,12},{1,9},{5... | collective-permute-start | bytes 442376 | tf_op jit(solution)/shard_map/ppermute | solution.py:279
  4.1 9.6 %collective-permute-start.5 = (bf16[576,128]{1,0:T(8,128)(2,1)S(1)}, bf16[576,128]{1,0:T(8,128)(2,1)S(1)}, u32[]{:S(2)}, u32[]{:S(2)}) collective-permute-start(bf16[576,128]{1,0:T(8,128)(2,1)S(1)} %get-tuple-element.26), channel_id=1, source_target_pairs={{0,16},{4,12},{8,24},{12,4},{16,0},{20,28},{24,8},{28,20},{1,17},{... | collective-permute-start | bytes 442376 | tf_op jit(solution)/shard_map/ppermute | solution.py:279
  6.5 7.6 %collective-permute-start.1 = (bf16[64,640]{1,0:T(8,128)(2,1)S(1)}, bf16[64,640]{1,0:T(8,128)(2,1)S(1)}, u32[]{:S(2)}, u32[]{:S(2)}) collective-permute-start(bf16[64,640]{1,0:T(8,128)(2,1)S(1)} %get-tuple-element.21), channel_id=1, source_target_pairs={{8,4},{5,12},{6,0},{11,8},{24,20},{21,28},{22,16},{27,24},{12,5},{... | collective-permute-start | bytes 245768 | tf_op jit(solution)/shard_map/ppermute | solution.py:302
  6.7 7.5 %collective-permute-start.2 = (bf16[64,640]{1,0:T(8,128)(2,1)S(1)}, bf16[64,640]{1,0:T(8,128)(2,1)S(1)}, u32[]{:S(2)}, u32[]{:S(2)}) collective-permute-start(bf16[64,640]{1,0:T(8,128)(2,1)S(1)} %get-tuple-element.22), channel_id=1, source_target_pairs={{8,12},{5,4},{6,8},{11,0},{24,28},{21,20},{22,24},{27,16},{12,13},... | collective-permute-start | bytes 245768 | tf_op jit(solution)/shard_map/ppermute | solution.py:302
  10.1 5.1 %collective-permute-start.6 = (bf16[2,576,128]{2,1,0:T(8,128)(2,1)S(1)}, bf16[2,576,128]{2,1,0:T(8,128)(2,1)S(1)}, u32[]{:S(2)}, u32[]{:S(2)}) collective-permute-start(bf16[2,576,128]{2,1,0:T(8,128)(2,1)S(1)} %shard_map.68), channel_id=1, source_target_pairs={{0,4},{4,0},{8,12},{12,8},{16,20},{20,16},{24,28},{28,24},{1,5},{5... | collective-permute-start | bytes 884744 | tf_op jit(solution)/shard_map/ppermute | solution.py:291
  13.7 1.4 %collective-permute-start.7 = (bf16[576,128]{1,0:T(8,128)(2,1)S(1)}, bf16[576,128]{1,0:T(8,128)(2,1)S(1)}, u32[]{:S(2)}, u32[]{:S(2)}) collective-permute-start(bf16[576,128]{1,0:T(8,128)(2,1)S(1)} %collective-permute-done.4.refs_4_), channel_id=1, source_target_pairs={{0,4},{4,0},{8,12},{12,8},{16,20},{20,16},{24,28},{28,24},{1,5},{5... | collective-permute-start | bytes 442376 | tf_op jit(solution)/shard_map/ppermute | solution.py:291
  13.7 1.6 %collective-permute-start.8 = (bf16[576,128]{1,0:T(8,128)(2,1)S(1)}, bf16[576,128]{1,0:T(8,128)(2,1)S(1)}, u32[]{:S(2)}, u32[]{:S(2)}) collective-permute-start(bf16[576,128]{1,0:T(8,128)(2,1)S(1)} %collective-permute-done.5.refs_5_), channel_id=1, source_target_pairs={{0,4},{4,0},{8,12},{12,8},{16,20},{20,16},{24,28},{28,24},{1,5},{5... | collective-permute-start | bytes 442376 | tf_op jit(solution)/shard_map/ppermute | solution.py:291
  14.2 11.3 %copy-start = (bf16[16,512,128]{2,1,0:T(8,128)(2,1)S(1)}, bf16[16,512,128]{2,1,0:T(8,128)(2,1)}, u32[]{:S(2)}) copy-start(bf16[16,512,128]{2,1,0:T(8,128)(2,1)} %w_ref.3) | copy-start | bytes 6291460
  16.0 7.3 %collective-permute-start.10 = (bf16[64,512]{1,0:T(8,128)(2,1)S(1)}, bf16[64,512]{1,0:T(8,128)(2,1)S(1)}, u32[]{:S(2)}, u32[]{:S(2)}) collective-permute-start(bf16[64,512]{1,0:T(8,128)(2,1)S(1)} %get-tuple-element.32), channel_id=1, source_target_pairs={{4,0},{12,1},{0,2},{8,3},{20,4},{28,5},{16,6},{24,7},{5,8},{13,9},... | collective-permute-start | bytes 196616 | tf_op jit(solution)/shard_map/ppermute | solution.py:332
  19.0 6.5 %collective-permute-start.9 = (bf16[64,512]{1,0:T(8,128)(2,1)S(1)}, bf16[64,512]{1,0:T(8,128)(2,1)S(1)}, u32[]{:S(2)}, u32[]{:S(2)}) collective-permute-start(bf16[64,512]{1,0:T(8,128)(2,1)S(1)} %get-tuple-element.31), channel_id=1, source_target_pairs={{12,0},{4,1},{8,2},{0,3},{28,4},{20,5},{24,6},{16,7},{13,8},{5,9},... | collective-permute-start | bytes 196616 | tf_op jit(solution)/shard_map/ppermute | solution.py:332

commit v23 on v15

--- a/solution.py
+++ b/solution.py
@@ -20,7 +20,11 @@
 
 
 def leaves_as(k, head_shard):
-    return (k + head_shard) % 2
+    return head_shard % 2 == k
+
+
+def stays(home_chip, core, half):
+    return home_chip % 2 ^ half & (home_chip // 2 ^ core)
 
 
 def far_half(plane, pair):
@@ -33,8 +37,8 @@
 
 
 def first_block(plane, chip, core):
-    near = 1 * (chip % 2 == plane % 2)
-    return far_half(plane, 1 - core) ^ near ^ chip % 2
+    first = far_half(plane, 1 - core) ^ 1 * (chip % 2 == plane % 2)
+    return first ^ 1 * (stays(plane, chip // 2, 1 - core) != chip % 2)
 
 
 def partner(k, core):
@@ -43,7 +47,8 @@
 
 def pick_kernel(per_device, cache_hbm, q_hbm, new_hbm, len_hbm, *refs):
     owners = cache_hbm.shape[0]
-    blocks, (out_ref, limit_ref, q_ref, new_ref, len_ref, sem) = refs[:owners], refs[owners:]
+    blocks, outs = refs[:owners], refs[owners : owners + per_device]
+    limit_ref, q_ref, new_ref, len_ref, sem = refs[owners + per_device :]
     chip, core = lax.axis_index("seq") // COPIES, lax.axis_index("seq") % COPIES
     moves = [
         pltpu.make_async_copy(q_hbm, q_ref, sem.at[owners]),
@@ -68,7 +73,13 @@
         if spare:
             parts.append(jnp.zeros((spare, ROPE), jnp.float32))
         own = jnp.concatenate(parts, axis=0).astype(rows.dtype)
-        out_ref[a * piece : (a + 1) * piece] = jnp.concatenate([rows, own], axis=1)
+        packed = jnp.concatenate([rows, own], axis=1)
+        for n, out in enumerate(outs):
+
+            @pl.when(stays(chip, core, lax.axis_index("head") // 2) ^ n == a)
+            def _():
+                out[...] = packed
+
     moves[2].wait()
     length = len_ref[lax.axis_index("head") * owners + chip]
     limit_ref[...] = jnp.full(limit_ref.shape, length, limit_ref.dtype)
@@ -87,10 +98,11 @@
         move.wait()
 
 
-def absorb_kernel(per_device, w_ref, packed_ref, *outs):
+def absorb_kernel(per_device, w_ref, *refs):
+    packed, outs = refs[:per_device], refs[per_device:]
     heads = w_ref.shape[0]
     piece = SPEC * heads
-    nope = packed_ref[:, :NOPE]
+    nope = jnp.concatenate([ref[:, :NOPE] for ref in packed], axis=0)
     own_head = lax.broadcasted_iota(jnp.int32, nope.shape, 0) % heads
     spread = jnp.concatenate(
         [jnp.where(own_head == h, nope, jnp.zeros_like(nope)) for h in range(heads)], axis=1
@@ -99,14 +111,13 @@
         spread, w_ref[...].reshape(heads * NOPE, LATENT), preferred_element_type=jnp.float32
     ).astype(jnp.bfloat16)
     for k in range(per_device):
-        which = leaves_as(k, lax.axis_index("head"))
-        for a in range(per_device):
-
-            @pl.when(which == a)
+        home_made = leaves_as(k, lax.axis_index("head"))
+        for n in range(per_device):
+
+            @pl.when(home_made == (n == 0))
             def _():
-                rows = slice(a * piece, (a + 1) * piece)
-                outs[k][:, :LATENT] = absorbed[rows]
-                outs[k][:, LATENT:] = packed_ref[rows, NOPE:]
+                outs[k][:, :LATENT] = absorbed[n * piece : (n + 1) * piece]
+                outs[k][:, LATENT:] = packed[n][:, NOPE:]
 
 
 def block_scores(q, refs, starts, limit_ref):
@@ -231,9 +242,12 @@
     def in_hbm(x):
         return pltpu.with_memory_space_constraint(x, pltpu.HBM)
 
-    def host(i, j):
-        other = (i // COPIES) ^ (2 - ((j ^ (j >> 1)) & 1))
-        return flat(((i % COPIES) * 2 + other // 2) * COPIES + other % 2, j)
+    def maker(i, j, k):
+        home, row = i // COPIES, i % COPIES
+        a = stays(home, row, j // 2)
+        if leaves_as(k, j):
+            return flat(i, j), a
+        return flat((row * per_device + 1 - a) * COPIES + home // 2, j), 1 - a
 
     def owner(i, j, a):
         plane, chip = i // COPIES, i % COPIES * per_device + a
@@ -242,15 +256,13 @@
     def in_plane(move):
         return [(g * COPIES + t, move(g, t)) for g in range(owners) for t in range(COPIES)]
 
-    *picked, packed, limit = pl.pallas_call(
+    *picked, kept, left, limit = pl.pallas_call(
         functools.partial(pick_kernel, per_device),
         out_shape=[jax.ShapeDtypeStruct((width, slots), cache.dtype)] * owners
-        + [
-            jax.ShapeDtypeStruct((all_rows, q_width + ROPE), queries.dtype),
-            jax.ShapeDtypeStruct((8, slots), jnp.int32),
-        ],
+        + [jax.ShapeDtypeStruct((piece, q_width + ROPE), queries.dtype)] * per_device
+        + [jax.ShapeDtypeStruct((8, slots), jnp.int32)],
         in_specs=[anywhere] * 4,
-        out_specs=[vmem] * (owners + 2),
+        out_specs=[vmem] * (owners + per_device + 1),
         scratch_shapes=[
             pltpu.VMEM(queries.shape, queries.dtype),
             pltpu.VMEM(new_latent.shape, new_latent.dtype),
@@ -260,7 +272,9 @@
         compiler_params=params,
         cost_estimate=LONG,
     )(*[in_hbm(x) for x in (jnp.swapaxes(cache, 1, 2), queries, new_latent, lengths)])
-    moved = lax.ppermute(packed, both, [(flat(i, j), host(i, j)) for i, j in devices])
+    moved = lax.ppermute(
+        left, both, [(flat(i, j), maker(i, j, 1 - j % 2)[0]) for i, j in devices]
+    )
     own_keys = [picked[0]] + [
         lax.ppermute(picked[k], "seq", in_plane(lambda g, t: (g ^ partner(k, t)) * COPIES + t))
         for k in range(1, owners)
@@ -279,16 +293,20 @@
     pieces = pl.pallas_call(
         functools.partial(absorb_kernel, per_device),
         out_shape=[jax.ShapeDtypeStruct((piece, width + ROPE), cache.dtype)] * per_device,
-        in_specs=[vmem] * 2,
+        in_specs=[vmem] * (1 + per_device),
         out_specs=[vmem] * per_device,
         compiler_params=params,
         cost_estimate=LONG,
-    )(w_uk, moved)
+    )(w_uk, kept, moved)
     arrived = [
         lax.ppermute(
             pieces[k],
             both,
-            [(host(i, j), owner(i, j, leaves_as(k, j))) for i, j in devices],
+            [
+                (source, owner(i, j, a))
+                for i, j in devices
+                for source, a in [maker(i, j, k)]
+            ],
         )
         for k in range(per_device)
     ]

time: 26.5 us -> 28.5 us (1.075)
  the two profiles are of different devices: /device:TPU:6 before, /device:TPU:25 now
where the time goes in v23:
time: 28.5 us; the launch traced here: 28.3 us
  starting transfers between devices  15.3 us (54%)
  waiting for transfers between devices  8.16 us (29%)
  Pallas kernels  4.77 us (17%)
    ppermute x2, waiting for transfers between devices, whole_sequences(): lax.ppermute(latent[k], both, [(owner(i, j, first_back(i // COPIES, j) ^...  6.38 us
    ppermute x2, starting transfers between devices, whole_sequences(): lax.ppermute(pieces[k], both, [(source, owner(i, j, a)) for i, j in devic...  5.43 us
    ppermute x2, starting transfers between devices, whole_sequences(): lax.ppermute(latent[k], both, [(owner(i, j, first_back(i // COPIES, j) ^...  4.71 us
    ppermute x3, starting transfers between devices, whole_sequences(): lax.ppermute(picked[k], 'seq', in_plane(lambda g, t: (g ^ partner(k, t))...  2.65 us
    ppermute x1, starting transfers between devices, whole_sequences(): lax.ppermute(left, both, [(flat(i, j), maker(i, j, 1 - j % 2)[0]) for i,...  1.86 us
    ppermute x3, waiting for transfers between devices, whole_sequences(): lax.ppermute(picked[k], 'seq', in_plane(lambda g, t: (g ^ partner(k, t))...  1.54 us
    pallas_call x1, Pallas kernels, whole_sequences(): pl.pallas_call(functools.partial(pick_kernel, per_device), out_shape=[jax...  1.38 us
    pallas_call x1, Pallas kernels, whole_sequences(): pl.pallas_call(functools.partial(project_kernel, per_device), out_shape=j...  1.07 us
  transfers between devices with their start and end apart: 11, of which 4 were waited for; matrix products, arithmetic and copies ran while one was open for 0% of the time, Pallas kernels for 6%

profile of v23, /device:TPU:25, one launch (start us, length us, event | category | flops | bytes accessed | tf_op | source)
XLA Modules:
  0.0 28.3 jit_solution(14099593791363334424)
XLA Ops:
  0.0 1.4 %shard_map.64 = (bf16[576,128]{1,0:T(8,128)(2,1)S(1)}, bf16[576,128]{1,0:T(8,128)(2,1)S(1)}, bf16[576,128]{1,0:T(8,128)(2,1)S(1)}, bf16[576,128]{1,0:T(8,128)(2,...) custom-call(bf16[4,576,128]{2,1,0:T(8,128)(2,1)} %bitcast.1, ...), custom_call_target="tpu_custom_call" | custom-call | flops 20000000000 | tf_op jit(solution)/shard_map/pallas_call | solution.py:259
  1.4 1.9 %collective-permute-start = (bf16[64,256]{1,0:T(8,128)(2,1)S(1)}, bf16[64,256]{1,0:T(8,128)(2,1)S(1)}, u32[]{:S(2)}, u32[]{:S(2)}) collective-permute-start(bf16[64,256]{1,0:T(8,128)(2,1)S(1)} %get-tuple-element.22), channel_id=1, source_target_pairs={{0,8},{1,9},{2,10},{3,11},{4,24},{5,25},{6,18},{7,19},{8,0},{9,1},... | collective-permute-start | bytes 98312 | tf_op jit(solution)/shard_map/ppermute | solution.py:275
  3.3 0.6 %collective-permute-start.3 = (bf16[576,128]{1,0:T(8,128)(2,1)S(1)}, bf16[576,128]{1,0:T(8,128)(2,1)S(1)}, u32[]{:S(2)}, u32[]{:S(2)}) collective-permute-start(bf16[576,128]{1,0:T(8,128)(2,1)S(1)} %get-tuple-element.26), channel_id=1, source_target_pairs={{0,24},{4,28},{8,16},{12,20},{16,8},{20,12},{24,0},{28,4},{1,25},{... | collective-permute-start | bytes 442376 | tf_op jit(solution)/shard_map/ppermute | solution.py:279
  3.9 1.8 %collective-permute-start.4 = (bf16[576,128]{1,0:T(8,128)(2,1)S(1)}, bf16[576,128]{1,0:T(8,128)(2,1)S(1)}, u32[]{:S(2)}, u32[]{:S(2)}) collective-permute-start(bf16[576,128]{1,0:T(8,128)(2,1)S(1)} %get-tuple-element.27), channel_id=1, source_target_pairs={{0,8},{4,20},{8,0},{12,28},{16,24},{20,4},{24,16},{28,12},{1,9},{5... | collective-permute-start | bytes 442376 | tf_op jit(solution)/shard_map/ppermute | solution.py:279
  5.6 0.3 collective-permute-start.5
  5.9 0.5 %shard_map.65 = (bf16[64,640]{1,0:T(8,128)(2,1)S(1)}, bf16[64,640]{1,0:T(8,128)(2,1)S(1)}) custom-call(bf16[16,128,512]{2,1,0:T(8,128)(2,1)S(1)} %copy-done.1, bf16[64,256]{1,0:T(8,128)(2,1)S(1)} %get-tuple-element.21.refs_0_, bf16[64,256]{1,0:T(8,128)(2,1)S(1)} %collective-permute-done.refs_1_), custom_call_target="tpu_custom_call" | custom-call | flops 20000000000 | tf_op jit(solution)/shard_map/pallas_call | solution.py:293
  6.4 1.3 %collective-permute-start.1 = (bf16[64,640]{1,0:T(8,128)(2,1)S(1)}, bf16[64,640]{1,0:T(8,128)(2,1)S(1)}, u32[]{:S(2)}, u32[]{:S(2)}) collective-permute-start(bf16[64,640]{1,0:T(8,128)(2,1)S(1)} %get-tuple-element.23), channel_id=1, source_target_pairs={{0,4},{9,12},{2,0},{11,8},{4,20},{25,28},{6,24},{19,16},{8,13},{1,... | collective-permute-start | bytes 245768 | tf_op jit(solution)/shard_map/ppermute | solution.py:302
  7.7 4.1 %collective-permute-start.2 = (bf16[64,640]{1,0:T(8,128)(2,1)S(1)}, bf16[64,640]{1,0:T(8,128)(2,1)S(1)}, u32[]{:S(2)}, u32[]{:S(2)}) collective-permute-start(bf16[64,640]{1,0:T(8,128)(2,1)S(1)} %get-tuple-element.24), channel_id=1, source_target_pairs={{8,12},{1,4},{10,8},{3,0},{24,28},{5,20},{18,16},{7,24},{0,5},{9,1... | collective-permute-start | bytes 245768 | tf_op jit(solution)/shard_map/ppermute | solution.py:302
  11.8 0.4 %shard_map.67 = bf16[2,576,128]{2,1,0:T(8,128)(2,1)S(1)} custom-call(bf16[576,128]{1,0:T(8,128)(2,1)S(1)} %get-tuple-element.25.refs_2_.first_ref, bf16[576,128]{1,0:T(8,128)(2,1)S(1)} %collective-permute-done.3.refs_3_.second_ref), custom_call_target="tpu_custom_call" | custom-call | tf_op jit(solution)/shard_map/pallas_call | solution.py:282
  12.2 0.1 collective-permute-start.6
  12.3 1.5 %collective-permute-done.4.refs_4_ = bf16[576,128]{1,0:T(8,128)(2,1)S(1)} collective-permute-done((bf16[576,128]{1,0:T(8,128)(2,1)S(1)}, bf16[576,128]{1,0:T(8,128)(2,1)S(1)}, u32[]{:S(2)}, u32[]{:S(2)}) %collective-permute-start.4) | collective-permute-done | bytes 147488 | tf_op jit(solution)/shard_map/ppermute | solution.py:279
  13.8 0.6 %collective-permute-start.8 = (bf16[576,128]{1,0:T(8,128)(2,1)S(1)}, bf16[576,128]{1,0:T(8,128)(2,1)S(1)}, u32[]{:S(2)}, u32[]{:S(2)}) collective-permute-start(bf16[576,128]{1,0:T(8,128)(2,1)S(1)} %collective-permute-done.5.refs_5_), channel_id=1, source_target_pairs={{0,4},{4,0},{8,12},{12,8},{16,20},{20,16},{24,28},{28,24},{1,5},{5... | collective-permute-start | bytes 442376 | tf_op jit(solution)/shard_map/ppermute | solution.py:291
  14.4 0.0 collective-permute-done.1.refs_0_
  14.4 0.0 collective-permute-done.2.refs_1_
  14.4 0.8 %shard_map.66 = (bf16[128,576]{1,0:T(8,128)(2,1)S(1)}, f32[128,128]{1,0:T(8,128)S(1)}, f32[128,128]{1,0:T(8,128)S(1)}, f32[128,512]{1,0:T(8,128)S(1)}) custom-call(s32[8,128]{1,0:T(8,128)S(1)} %get-tuple-element.20.limit_ref, bf16[64,640]{1,0:T(8,128)(2,1)S(1)} %collective-permute-done.1.refs_0_, bf16[64,640]{1,0:T(8,128)(2,1)S(1)} %collective-permute-done.2.refs_1_, ...), custom_call_target="tpu_custom_call" | custom-call | flops 20000000000 | tf_op jit(solution)/shard_map/pallas_call | solution.py:314
  15.2 0.0 collective-permute-done.7.refs_0_
  15.2 0.2 collective-permute-done.8.refs_1_
  15.4 0.0 collective-permute-done.6.pair_ref
  15.4 0.7 %shard_map.68 = (bf16[64,512]{1,0:T(8,128)(2,1)S(1)}, bf16[64,512]{1,0:T(8,128)(2,1)S(1)}) custom-call(s32[8,128]{1,0:T(8,128)S(1)} %get-tuple-element.20.limit_ref, bf16[128,576]{1,0:T(8,128)(2,1)S(1)} %get-tuple-element.29.q_ref, f32[128,128]{1,0:T(8,128)S(1)} %get-tuple-element.30.top_ref, f32[128,128]{1,0:T(8,128)S(1)} %get-tuple-element.31.total_ref, ...), custom_call_target="tpu_custom_call" | custom-call | tf_op jit(solution)/shard_map/pallas_call | solution.py:327
  16.1 4.7 %collective-permute-start.10 = (bf16[64,512]{1,0:T(8,128)(2,1)S(1)}, bf16[64,512]{1,0:T(8,128)(2,1)S(1)}, u32[]{:S(2)}, u32[]{:S(2)}) collective-permute-start(bf16[64,512]{1,0:T(8,128)(2,1)S(1)} %get-tuple-element.34), channel_id=1, source_target_pairs={{4,0},{12,1},{0,2},{8,3},{20,4},{28,5},{16,6},{24,7},{5,8},{13,9},... | collective-permute-start | bytes 196616 | tf_op jit(solution)/shard_map/ppermute | solution.py:336
  20.9 0.0 collective-permute-start.9
  20.9 2.7 %collective-permute-done.10.refs_1_ = bf16[64,512]{1,0:T(8,128)(2,1)S(1)} collective-permute-done((bf16[64,512]{1,0:T(8,128)(2,1)S(1)}, bf16[64,512]{1,0:T(8,128)(2,1)S(1)}, u32[]{:S(2)}, u32[]{:S(2)}) %collective-permute-start.10) | collective-permute-done | bytes 65568 | tf_op jit(solution)/shard_map/ppermute | solution.py:336
  23.6 3.7 %collective-permute-done.9.refs_0_ = bf16[64,512]{1,0:T(8,128)(2,1)S(1)} collective-permute-done((bf16[64,512]{1,0:T(8,128)(2,1)S(1)}, bf16[64,512]{1,0:T(8,128)(2,1)S(1)}, u32[]{:S(2)}, u32[]{:S(2)}) %collective-permute-start.9) | collective-permute-done | bytes 65568 | tf_op jit(solution)/shard_map/ppermute | solution.py:336
  27.2 1.1 %shard_map.69 = bf16[8,16,128]{2,1,0:T(8,128)(2,1)} custom-call(bf16[16,512,128]{2,1,0:T(8,128)(2,1)S(1)} %copy-done, bf16[64,512]{1,0:T(8,128)(2,1)S(1)} %collective-permute-done.9.refs_0_, bf16[64,512]{1,0:T(8,128)(2,1)S(1)} %collective-permute-done.10.refs_1_), custom_call_target="tpu_custom_call" | custom-call | tf_op jit(solution)/shard_map/pallas_call | solution.py:343
  (8 shorter events, 0.0 us)
Async XLA Ops:
  0.0 5.9 %copy-start.1 = (bf16[16,128,512]{2,1,0:T(8,128)(2,1)S(1)}, bf16[16,128,512]{2,1,0:T(8,128)(2,1)}, u32[]{:S(2)}) copy-start(bf16[16,128,512]{2,1,0:T(8,128)(2,1)} %w_ref.2) | copy-start | bytes 6291460
  1.4 4.5 %collective-permute-start = (bf16[64,256]{1,0:T(8,128)(2,1)S(1)}, bf16[64,256]{1,0:T(8,128)(2,1)S(1)}, u32[]{:S(2)}, u32[]{:S(2)}) collective-permute-start(bf16[64,256]{1,0:T(8,128)(2,1)S(1)} %get-tuple-element.22), channel_id=1, source_target_pairs={{0,8},{1,9},{2,10},{3,11},{4,24},{5,25},{6,18},{7,19},{8,0},{9,1},... | collective-permute-start | bytes 98312 | tf_op jit(solution)/shard_map/ppermute | solution.py:275
  3.3 8.6 %collective-permute-start.3 = (bf16[576,128]{1,0:T(8,128)(2,1)S(1)}, bf16[576,128]{1,0:T(8,128)(2,1)S(1)}, u32[]{:S(2)}, u32[]{:S(2)}) collective-permute-start(bf16[576,128]{1,0:T(8,128)(2,1)S(1)} %get-tuple-element.26), channel_id=1, source_target_pairs={{0,24},{4,28},{8,16},{12,20},{16,8},{20,12},{24,0},{28,4},{1,25},{... | collective-permute-start | bytes 442376 | tf_op jit(solution)/shard_map/ppermute | solution.py:279
  3.9 9.9 %collective-permute-start.4 = (bf16[576,128]{1,0:T(8,128)(2,1)S(1)}, bf16[576,128]{1,0:T(8,128)(2,1)S(1)}, u32[]{:S(2)}, u32[]{:S(2)}) collective-permute-start(bf16[576,128]{1,0:T(8,128)(2,1)S(1)} %get-tuple-element.27), channel_id=1, source_target_pairs={{0,8},{4,20},{8,0},{12,28},{16,24},{20,4},{24,16},{28,12},{1,9},{5... | collective-permute-start | bytes 442376 | tf_op jit(solution)/shard_map/ppermute | solution.py:279
  5.6 8.2 %collective-permute-start.5 = (bf16[576,128]{1,0:T(8,128)(2,1)S(1)}, bf16[576,128]{1,0:T(8,128)(2,1)S(1)}, u32[]{:S(2)}, u32[]{:S(2)}) collective-permute-start(bf16[576,128]{1,0:T(8,128)(2,1)S(1)} %get-tuple-element.28), channel_id=1, source_target_pairs={{0,16},{4,12},{8,24},{12,4},{16,0},{20,28},{24,8},{28,20},{1,17},{... | collective-permute-start | bytes 442376 | tf_op jit(solution)/shard_map/ppermute | solution.py:279
  6.4 8.0 %collective-permute-start.1 = (bf16[64,640]{1,0:T(8,128)(2,1)S(1)}, bf16[64,640]{1,0:T(8,128)(2,1)S(1)}, u32[]{:S(2)}, u32[]{:S(2)}) collective-permute-start(bf16[64,640]{1,0:T(8,128)(2,1)S(1)} %get-tuple-element.23), channel_id=1, source_target_pairs={{0,4},{9,12},{2,0},{11,8},{4,20},{25,28},{6,24},{19,16},{8,13},{1,... | collective-permute-start | bytes 245768 | tf_op jit(solution)/shard_map/ppermute | solution.py:302
  7.7 6.7 %collective-permute-start.2 = (bf16[64,640]{1,0:T(8,128)(2,1)S(1)}, bf16[64,640]{1,0:T(8,128)(2,1)S(1)}, u32[]{:S(2)}, u32[]{:S(2)}) collective-permute-start(bf16[64,640]{1,0:T(8,128)(2,1)S(1)} %get-tuple-element.24), channel_id=1, source_target_pairs={{8,12},{1,4},{10,8},{3,0},{24,28},{5,20},{18,16},{7,24},{0,5},{9,1... | collective-permute-start | bytes 245768 | tf_op jit(solution)/shard_map/ppermute | solution.py:302
  12.2 3.2 %collective-permute-start.6 = (bf16[2,576,128]{2,1,0:T(8,128)(2,1)S(1)}, bf16[2,576,128]{2,1,0:T(8,128)(2,1)S(1)}, u32[]{:S(2)}, u32[]{:S(2)}) collective-permute-start(bf16[2,576,128]{2,1,0:T(8,128)(2,1)S(1)} %shard_map.67), channel_id=1, source_target_pairs={{0,4},{4,0},{8,12},{12,8},{16,20},{20,16},{24,28},{28,24},{1,5},{5... | collective-permute-start | bytes 884744 | tf_op jit(solution)/shard_map/ppermute | solution.py:291
  13.8 1.4 %collective-permute-start.7 = (bf16[576,128]{1,0:T(8,128)(2,1)S(1)}, bf16[576,128]{1,0:T(8,128)(2,1)S(1)}, u32[]{:S(2)}, u32[]{:S(2)}) collective-permute-start(bf16[576,128]{1,0:T(8,128)(2,1)S(1)} %collective-permute-done.4.refs_4_), channel_id=1, source_target_pairs={{0,4},{4,0},{8,12},{12,8},{16,20},{20,16},{24,28},{28,24},{1,5},{5... | collective-permute-start | bytes 442376 | tf_op jit(solution)/shard_map/ppermute | solution.py:291
  13.8 1.6 %collective-permute-start.8 = (bf16[576,128]{1,0:T(8,128)(2,1)S(1)}, bf16[576,128]{1,0:T(8,128)(2,1)S(1)}, u32[]{:S(2)}, u32[]{:S(2)}) collective-permute-start(bf16[576,128]{1,0:T(8,128)(2,1)S(1)} %collective-permute-done.5.refs_5_), channel_id=1, source_target_pairs={{0,4},{4,0},{8,12},{12,8},{16,20},{20,16},{24,28},{28,24},{1,5},{5... | collective-permute-start | bytes 442376 | tf_op jit(solution)/shard_map/ppermute | solution.py:291
  14.4 12.8 %copy-start = (bf16[16,512,128]{2,1,0:T(8,128)(2,1)S(1)}, bf16[16,512,128]{2,1,0:T(8,128)(2,1)}, u32[]{:S(2)}) copy-start(bf16[16,512,128]{2,1,0:T(8,128)(2,1)} %w_ref.3) | copy-start | bytes 6291460
  16.1 7.4 %collective-permute-start.10 = (bf16[64,512]{1,0:T(8,128)(2,1)S(1)}, bf16[64,512]{1,0:T(8,128)(2,1)S(1)}, u32[]{:S(2)}, u32[]{:S(2)}) collective-permute-start(bf16[64,512]{1,0:T(8,128)(2,1)S(1)} %get-tuple-element.34), channel_id=1, source_target_pairs={{4,0},{12,1},{0,2},{8,3},{20,4},{28,5},{16,6},{24,7},{5,8},{13,9},... | collective-permute-start | bytes 196616 | tf_op jit(solution)/shard_map/ppermute | solution.py:336
  20.9 6.4 %collective-permute-start.9 = (bf16[64,512]{1,0:T(8,128)(2,1)S(1)}, bf16[64,512]{1,0:T(8,128)(2,1)S(1)}, u32[]{:S(2)}, u32[]{:S(2)}) collective-permute-start(bf16[64,512]{1,0:T(8,128)(2,1)S(1)} %get-tuple-element.33), channel_id=1, source_target_pairs={{12,0},{4,1},{8,2},{0,3},{28,4},{20,5},{24,6},{16,7},{13,8},{5,9},... | collective-permute-start | bytes 196616 | tf_op jit(solution)/shard_map/ppermute | solution.py:336

commit v24 on v23

--- a/solution.py
+++ b/solution.py
@@ -24,7 +24,8 @@
 
 
 def stays(home_chip, core, half):
-    return home_chip % 2 ^ half & (home_chip // 2 ^ core)
+    row = home_chip // 2
+    return home_chip % 2 ^ (1 ^ half ^ row) & (row ^ core)
 
 
 def far_half(plane, pair):

time: 28.5 us -> 26.9 us (0.944)
  the two profiles are of different devices: /device:TPU:25 before, /device:TPU:16 now
where the time goes in v24:
time: 26.9 us; the launch traced here: 26.8 us
  waiting for transfers between devices  13.5 us (50%)
  starting transfers between devices  8.45 us (31%)
  Pallas kernels  4.75 us (18%)
    ppermute x2, waiting for transfers between devices, whole_sequences(): lax.ppermute(latent[k], both, [(owner(i, j, first_back(i // COPIES, j) ^...  6.91 us
    ppermute x3, waiting for transfers between devices, whole_sequences(): lax.ppermute(picked[k], 'seq', in_plane(lambda g, t: (g ^ partner(k, t))...  6 us
    ppermute x3, starting transfers between devices, whole_sequences(): lax.ppermute(picked[k], 'seq', in_plane(lambda g, t: (g ^ partner(k, t))...  3.49 us
    ppermute x2, starting transfers between devices, whole_sequences(): lax.ppermute(latent[k], both, [(owner(i, j, first_back(i // COPIES, j) ^...  2.71 us
    ppermute x1, starting transfers between devices, whole_sequences(): lax.ppermute(left, both, [(flat(i, j), maker(i, j, 1 - j % 2)[0]) for i,...  1.54 us
    pallas_call x1, Pallas kernels, whole_sequences(): pl.pallas_call(functools.partial(pick_kernel, per_device), out_shape=[jax...  1.38 us
    pallas_call x1, Pallas kernels, whole_sequences(): pl.pallas_call(functools.partial(project_kernel, per_device), out_shape=j...  1.06 us
    pallas_call x1, Pallas kernels, whole_sequences(): pl.pallas_call(functools.partial(begin_kernel, owners, per_device, heads)...  0.76 us
  transfers between devices with their start and end apart: 11, of which 6 were waited for; matrix products, arithmetic and copies ran while one was open for 0% of the time, Pallas kernels for 6%

profile of v24, /device:TPU:16, one launch (start us, length us, event | category | flops | bytes accessed | tf_op | source)
XLA Modules:
  0.0 26.8 jit_solution(16754685304194692864)
XLA Ops:
  0.0 1.4 %shard_map.64 = (bf16[576,128]{1,0:T(8,128)(2,1)S(1)}, bf16[576,128]{1,0:T(8,128)(2,1)S(1)}, bf16[576,128]{1,0:T(8,128)(2,1)S(1)}, bf16[576,128]{1,0:T(8,128)(2,...) custom-call(bf16[4,576,128]{2,1,0:T(8,128)(2,1)} %bitcast.1, ...), custom_call_target="tpu_custom_call" | custom-call | flops 20000000000 | tf_op jit(solution)/shard_map/pallas_call | solution.py:260
  1.4 1.5 %collective-permute-start = (bf16[64,256]{1,0:T(8,128)(2,1)S(1)}, bf16[64,256]{1,0:T(8,128)(2,1)S(1)}, u32[]{:S(2)}, u32[]{:S(2)}) collective-permute-start(bf16[64,256]{1,0:T(8,128)(2,1)S(1)} %get-tuple-element.22), channel_id=1, source_target_pairs={{0,8},{1,9},{2,10},{3,11},{4,16},{5,17},{6,26},{7,27},{8,0},{9,1},... | collective-permute-start | bytes 98312 | tf_op jit(solution)/shard_map/ppermute | solution.py:276
  2.9 1.0 %collective-permute-start.3 = (bf16[576,128]{1,0:T(8,128)(2,1)S(1)}, bf16[576,128]{1,0:T(8,128)(2,1)S(1)}, u32[]{:S(2)}, u32[]{:S(2)}) collective-permute-start(bf16[576,128]{1,0:T(8,128)(2,1)S(1)} %get-tuple-element.26), channel_id=1, source_target_pairs={{0,24},{4,28},{8,16},{12,20},{16,8},{20,12},{24,0},{28,4},{1,25},{... | collective-permute-start | bytes 442376 | tf_op jit(solution)/shard_map/ppermute | solution.py:280
  4.0 0.5 %collective-permute-start.4 = (bf16[576,128]{1,0:T(8,128)(2,1)S(1)}, bf16[576,128]{1,0:T(8,128)(2,1)S(1)}, u32[]{:S(2)}, u32[]{:S(2)}) collective-permute-start(bf16[576,128]{1,0:T(8,128)(2,1)S(1)} %get-tuple-element.27), channel_id=1, source_target_pairs={{0,8},{4,20},{8,0},{12,28},{16,24},{20,4},{24,16},{28,12},{1,9},{5... | collective-permute-start | bytes 442376 | tf_op jit(solution)/shard_map/ppermute | solution.py:280
  4.5 1.9 %collective-permute-start.5 = (bf16[576,128]{1,0:T(8,128)(2,1)S(1)}, bf16[576,128]{1,0:T(8,128)(2,1)S(1)}, u32[]{:S(2)}, u32[]{:S(2)}) collective-permute-start(bf16[576,128]{1,0:T(8,128)(2,1)S(1)} %get-tuple-element.28), channel_id=1, source_target_pairs={{0,16},{4,12},{8,24},{12,4},{16,0},{20,28},{24,8},{28,20},{1,17},{... | collective-permute-start | bytes 442376 | tf_op jit(solution)/shard_map/ppermute | solution.py:280
  6.4 0.0 collective-permute-done.refs_1_
  6.4 0.5 %shard_map.65 = (bf16[64,640]{1,0:T(8,128)(2,1)S(1)}, bf16[64,640]{1,0:T(8,128)(2,1)S(1)}) custom-call(bf16[16,128,512]{2,1,0:T(8,128)(2,1)S(1)} %copy-done.1, bf16[64,256]{1,0:T(8,128)(2,1)S(1)} %get-tuple-element.21.refs_0_, bf16[64,256]{1,0:T(8,128)(2,1)S(1)} %collective-permute-done.refs_1_), custom_call_target="tpu_custom_call" | custom-call | flops 20000000000 | tf_op jit(solution)/shard_map/pallas_call | solution.py:294
  6.9 0.4 %collective-permute-start.1 = (bf16[64,640]{1,0:T(8,128)(2,1)S(1)}, bf16[64,640]{1,0:T(8,128)(2,1)S(1)}, u32[]{:S(2)}, u32[]{:S(2)}) collective-permute-start(bf16[64,640]{1,0:T(8,128)(2,1)S(1)} %get-tuple-element.23), channel_id=1, source_target_pairs={{0,4},{9,12},{2,0},{11,8},{4,28},{17,20},{6,16},{27,24},{8,13},{1,... | collective-permute-start | bytes 245768 | tf_op jit(solution)/shard_map/ppermute | solution.py:303
  7.3 0.2 collective-permute-start.2
  7.5 3.1 %collective-permute-done.3.refs_3_.second_ref = bf16[576,128]{1,0:T(8,128)(2,1)S(1)} collective-permute-done((bf16[576,128]{1,0:T(8,128)(2,1)S(1)}, bf16[576,128]{1,0:T(8,128)(2,1)S(1)}, u32[]{:S(2)}, u32[]{:S(2)}) %collective-permute-start.3) | collective-permute-done | bytes 147488 | tf_op jit(solution)/shard_map/ppermute | solution.py:280
  10.6 0.4 %shard_map.67 = bf16[2,576,128]{2,1,0:T(8,128)(2,1)S(1)} custom-call(bf16[576,128]{1,0:T(8,128)(2,1)S(1)} %get-tuple-element.25.refs_2_.first_ref, bf16[576,128]{1,0:T(8,128)(2,1)S(1)} %collective-permute-done.3.refs_3_.second_ref), custom_call_target="tpu_custom_call" | custom-call | tf_op jit(solution)/shard_map/pallas_call | solution.py:283
  10.9 0.1 collective-permute-start.6
  11.1 1.3 %collective-permute-done.4.refs_4_ = bf16[576,128]{1,0:T(8,128)(2,1)S(1)} collective-permute-done((bf16[576,128]{1,0:T(8,128)(2,1)S(1)}, bf16[576,128]{1,0:T(8,128)(2,1)S(1)}, u32[]{:S(2)}, u32[]{:S(2)}) %collective-permute-start.4) | collective-permute-done | bytes 147488 | tf_op jit(solution)/shard_map/ppermute | solution.py:280
  12.4 1.6 %collective-permute-done.5.refs_5_ = bf16[576,128]{1,0:T(8,128)(2,1)S(1)} collective-permute-done((bf16[576,128]{1,0:T(8,128)(2,1)S(1)}, bf16[576,128]{1,0:T(8,128)(2,1)S(1)}, u32[]{:S(2)}, u32[]{:S(2)}) %collective-permute-start.5) | collective-permute-done | bytes 147488 | tf_op jit(solution)/shard_map/ppermute | solution.py:280
  14.0 0.0 collective-permute-start.8
  14.0 0.0 copy-start
  14.0 0.8 %shard_map.66 = (bf16[128,576]{1,0:T(8,128)(2,1)S(1)}, f32[128,128]{1,0:T(8,128)S(1)}, f32[128,128]{1,0:T(8,128)S(1)}, f32[128,512]{1,0:T(8,128)S(1)}) custom-call(s32[8,128]{1,0:T(8,128)S(1)} %get-tuple-element.20.limit_ref, bf16[64,640]{1,0:T(8,128)(2,1)S(1)} %collective-permute-done.1.refs_0_, bf16[64,640]{1,0:T(8,128)(2,1)S(1)} %collective-permute-done.2.refs_1_, ...), custom_call_target="tpu_custom_call" | custom-call | flops 20000000000 | tf_op jit(solution)/shard_map/pallas_call | solution.py:315
  14.8 0.6 %collective-permute-done.8.refs_1_ = bf16[576,128]{1,0:T(8,128)(2,1)S(1)} collective-permute-done((bf16[576,128]{1,0:T(8,128)(2,1)S(1)}, bf16[576,128]{1,0:T(8,128)(2,1)S(1)}, u32[]{:S(2)}, u32[]{:S(2)}) %collective-permute-start.8) | collective-permute-done | bytes 147488 | tf_op jit(solution)/shard_map/ppermute | solution.py:292
  15.4 0.7 %shard_map.68 = (bf16[64,512]{1,0:T(8,128)(2,1)S(1)}, bf16[64,512]{1,0:T(8,128)(2,1)S(1)}) custom-call(s32[8,128]{1,0:T(8,128)S(1)} %get-tuple-element.20.limit_ref, bf16[128,576]{1,0:T(8,128)(2,1)S(1)} %get-tuple-element.29.q_ref, f32[128,128]{1,0:T(8,128)S(1)} %get-tuple-element.30.top_ref, f32[128,128]{1,0:T(8,128)S(1)} %get-tuple-element.31.total_ref, ...), custom_call_target="tpu_custom_call" | custom-call | tf_op jit(solution)/shard_map/pallas_call | solution.py:328
  16.1 0.5 %collective-permute-start.10 = (bf16[64,512]{1,0:T(8,128)(2,1)S(1)}, bf16[64,512]{1,0:T(8,128)(2,1)S(1)}, u32[]{:S(2)}, u32[]{:S(2)}) collective-permute-start(bf16[64,512]{1,0:T(8,128)(2,1)S(1)} %get-tuple-element.34), channel_id=1, source_target_pairs={{4,0},{12,1},{0,2},{8,3},{20,4},{28,5},{16,6},{24,7},{5,8},{13,9},... | collective-permute-start | bytes 196616 | tf_op jit(solution)/shard_map/ppermute | solution.py:337
  16.6 2.2 %collective-permute-start.9 = (bf16[64,512]{1,0:T(8,128)(2,1)S(1)}, bf16[64,512]{1,0:T(8,128)(2,1)S(1)}, u32[]{:S(2)}, u32[]{:S(2)}) collective-permute-start(bf16[64,512]{1,0:T(8,128)(2,1)S(1)} %get-tuple-element.33), channel_id=1, source_target_pairs={{12,0},{4,1},{8,2},{0,3},{28,4},{20,5},{24,6},{16,7},{13,8},{5,9},... | collective-permute-start | bytes 196616 | tf_op jit(solution)/shard_map/ppermute | solution.py:337
  18.8 2.5 %collective-permute-done.10.refs_1_ = bf16[64,512]{1,0:T(8,128)(2,1)S(1)} collective-permute-done((bf16[64,512]{1,0:T(8,128)(2,1)S(1)}, bf16[64,512]{1,0:T(8,128)(2,1)S(1)}, u32[]{:S(2)}, u32[]{:S(2)}) %collective-permute-start.10) | collective-permute-done | bytes 65568 | tf_op jit(solution)/shard_map/ppermute | solution.py:337
  21.3 4.4 %collective-permute-done.9.refs_0_ = bf16[64,512]{1,0:T(8,128)(2,1)S(1)} collective-permute-done((bf16[64,512]{1,0:T(8,128)(2,1)S(1)}, bf16[64,512]{1,0:T(8,128)(2,1)S(1)}, u32[]{:S(2)}, u32[]{:S(2)}) %collective-permute-start.9) | collective-permute-done | bytes 65568 | tf_op jit(solution)/shard_map/ppermute | solution.py:337
  25.7 1.1 %shard_map.69 = bf16[8,16,128]{2,1,0:T(8,128)(2,1)} custom-call(bf16[16,512,128]{2,1,0:T(8,128)(2,1)S(1)} %copy-done, bf16[64,512]{1,0:T(8,128)(2,1)S(1)} %collective-permute-done.9.refs_0_, bf16[64,512]{1,0:T(8,128)(2,1)S(1)} %collective-permute-done.10.refs_1_), custom_call_target="tpu_custom_call" | custom-call | tf_op jit(solution)/shard_map/pallas_call | solution.py:344
  (8 shorter events, 0.0 us)
Async XLA Ops:
  0.0 6.4 %copy-start.1 = (bf16[16,128,512]{2,1,0:T(8,128)(2,1)S(1)}, bf16[16,128,512]{2,1,0:T(8,128)(2,1)}, u32[]{:S(2)}) copy-start(bf16[16,128,512]{2,1,0:T(8,128)(2,1)} %w_ref.2) | copy-start | bytes 6291460
  1.4 5.0 %collective-permute-start = (bf16[64,256]{1,0:T(8,128)(2,1)S(1)}, bf16[64,256]{1,0:T(8,128)(2,1)S(1)}, u32[]{:S(2)}, u32[]{:S(2)}) collective-permute-start(bf16[64,256]{1,0:T(8,128)(2,1)S(1)} %get-tuple-element.22), channel_id=1, source_target_pairs={{0,8},{1,9},{2,10},{3,11},{4,16},{5,17},{6,26},{7,27},{8,0},{9,1},... | collective-permute-start | bytes 98312 | tf_op jit(solution)/shard_map/ppermute | solution.py:276
  2.9 7.6 %collective-permute-start.3 = (bf16[576,128]{1,0:T(8,128)(2,1)S(1)}, bf16[576,128]{1,0:T(8,128)(2,1)S(1)}, u32[]{:S(2)}, u32[]{:S(2)}) collective-permute-start(bf16[576,128]{1,0:T(8,128)(2,1)S(1)} %get-tuple-element.26), channel_id=1, source_target_pairs={{0,24},{4,28},{8,16},{12,20},{16,8},{20,12},{24,0},{28,4},{1,25},{... | collective-permute-start | bytes 442376 | tf_op jit(solution)/shard_map/ppermute | solution.py:280
  4.0 8.4 %collective-permute-start.4 = (bf16[576,128]{1,0:T(8,128)(2,1)S(1)}, bf16[576,128]{1,0:T(8,128)(2,1)S(1)}, u32[]{:S(2)}, u32[]{:S(2)}) collective-permute-start(bf16[576,128]{1,0:T(8,128)(2,1)S(1)} %get-tuple-element.27), channel_id=1, source_target_pairs={{0,8},{4,20},{8,0},{12,28},{16,24},{20,4},{24,16},{28,12},{1,9},{5... | collective-permute-start | bytes 442376 | tf_op jit(solution)/shard_map/ppermute | solution.py:280
  4.5 9.5 %collective-permute-start.5 = (bf16[576,128]{1,0:T(8,128)(2,1)S(1)}, bf16[576,128]{1,0:T(8,128)(2,1)S(1)}, u32[]{:S(2)}, u32[]{:S(2)}) collective-permute-start(bf16[576,128]{1,0:T(8,128)(2,1)S(1)} %get-tuple-element.28), channel_id=1, source_target_pairs={{0,16},{4,12},{8,24},{12,4},{16,0},{20,28},{24,8},{28,20},{1,17},{... | collective-permute-start | bytes 442376 | tf_op jit(solution)/shard_map/ppermute | solution.py:280
  6.9 7.1 %collective-permute-start.1 = (bf16[64,640]{1,0:T(8,128)(2,1)S(1)}, bf16[64,640]{1,0:T(8,128)(2,1)S(1)}, u32[]{:S(2)}, u32[]{:S(2)}) collective-permute-start(bf16[64,640]{1,0:T(8,128)(2,1)S(1)} %get-tuple-element.23), channel_id=1, source_target_pairs={{0,4},{9,12},{2,0},{11,8},{4,28},{17,20},{6,16},{27,24},{8,13},{1,... | collective-permute-start | bytes 245768 | tf_op jit(solution)/shard_map/ppermute | solution.py:303
  7.3 6.7 %collective-permute-start.2 = (bf16[64,640]{1,0:T(8,128)(2,1)S(1)}, bf16[64,640]{1,0:T(8,128)(2,1)S(1)}, u32[]{:S(2)}, u32[]{:S(2)}) collective-permute-start(bf16[64,640]{1,0:T(8,128)(2,1)S(1)} %get-tuple-element.24), channel_id=1, source_target_pairs={{8,12},{1,4},{10,8},{3,0},{16,20},{5,28},{26,24},{7,16},{0,5},{9,1... | collective-permute-start | bytes 245768 | tf_op jit(solution)/shard_map/ppermute | solution.py:303
  10.9 4.4 %collective-permute-start.6 = (bf16[2,576,128]{2,1,0:T(8,128)(2,1)S(1)}, bf16[2,576,128]{2,1,0:T(8,128)(2,1)S(1)}, u32[]{:S(2)}, u32[]{:S(2)}) collective-permute-start(bf16[2,576,128]{2,1,0:T(8,128)(2,1)S(1)} %shard_map.67), channel_id=1, source_target_pairs={{0,4},{4,0},{8,12},{12,8},{16,20},{20,16},{24,28},{28,24},{1,5},{5... | collective-permute-start | bytes 884744 | tf_op jit(solution)/shard_map/ppermute | solution.py:292
  12.4 2.4 %collective-permute-start.7 = (bf16[576,128]{1,0:T(8,128)(2,1)S(1)}, bf16[576,128]{1,0:T(8,128)(2,1)S(1)}, u32[]{:S(2)}, u32[]{:S(2)}) collective-permute-start(bf16[576,128]{1,0:T(8,128)(2,1)S(1)} %collective-permute-done.4.refs_4_), channel_id=1, source_target_pairs={{0,4},{4,0},{8,12},{12,8},{16,20},{20,16},{24,28},{28,24},{1,5},{5... | collective-permute-start | bytes 442376 | tf_op jit(solution)/shard_map/ppermute | solution.py:292
  14.0 1.4 %collective-permute-start.8 = (bf16[576,128]{1,0:T(8,128)(2,1)S(1)}, bf16[576,128]{1,0:T(8,128)(2,1)S(1)}, u32[]{:S(2)}, u32[]{:S(2)}) collective-permute-start(bf16[576,128]{1,0:T(8,128)(2,1)S(1)} %collective-permute-done.5.refs_5_), channel_id=1, source_target_pairs={{0,4},{4,0},{8,12},{12,8},{16,20},{20,16},{24,28},{28,24},{1,5},{5... | collective-permute-start | bytes 442376 | tf_op jit(solution)/shard_map/ppermute | solution.py:292
  14.0 11.7 %copy-start = (bf16[16,512,128]{2,1,0:T(8,128)(2,1)S(1)}, bf16[16,512,128]{2,1,0:T(8,128)(2,1)}, u32[]{:S(2)}) copy-start(bf16[16,512,128]{2,1,0:T(8,128)(2,1)} %w_ref.3) | copy-start | bytes 6291460
  16.1 5.2 %collective-permute-start.10 = (bf16[64,512]{1,0:T(8,128)(2,1)S(1)}, bf16[64,512]{1,0:T(8,128)(2,1)S(1)}, u32[]{:S(2)}, u32[]{:S(2)}) collective-permute-start(bf16[64,512]{1,0:T(8,128)(2,1)S(1)} %get-tuple-element.34), channel_id=1, source_target_pairs={{4,0},{12,1},{0,2},{8,3},{20,4},{28,5},{16,6},{24,7},{5,8},{13,9},... | collective-permute-start | bytes 196616 | tf_op jit(solution)/shard_map/ppermute | solution.py:337
  16.6 9.1 %collective-permute-start.9 = (bf16[64,512]{1,0:T(8,128)(2,1)S(1)}, bf16[64,512]{1,0:T(8,128)(2,1)S(1)}, u32[]{:S(2)}, u32[]{:S(2)}) collective-permute-start(bf16[64,512]{1,0:T(8,128)(2,1)S(1)} %get-tuple-element.33), channel_id=1, source_target_pairs={{12,0},{4,1},{8,2},{0,3},{28,4},{20,5},{24,6},{16,7},{13,8},{5,9},... | collective-permute-start | bytes 196616 | tf_op jit(solution)/shard_map/ppermute | solution.py:337

commit v25 on v24

--- a/solution.py
+++ b/solution.py
@@ -20,7 +20,7 @@
 
 
 def leaves_as(k, head_shard):
-    return head_shard % 2 == k
+    return head_shard % 2 != k
 
 
 def stays(home_chip, core, half):
@@ -39,7 +39,7 @@
 
 def first_block(plane, chip, core):
     first = far_half(plane, 1 - core) ^ 1 * (chip % 2 == plane % 2)
-    return first ^ 1 * (stays(plane, chip // 2, 1 - core) != chip % 2)
+    return first ^ 1 * (stays(plane, chip // 2, 1 - core) == chip % 2)
 
 
 def partner(k, core):
@@ -274,7 +274,7 @@
         cost_estimate=LONG,
     )(*[in_hbm(x) for x in (jnp.swapaxes(cache, 1, 2), queries, new_latent, lengths)])
     moved = lax.ppermute(
-        left, both, [(flat(i, j), maker(i, j, 1 - j % 2)[0]) for i, j in devices]
+        left, both, [(flat(i, j), maker(i, j, j % 2)[0]) for i, j in devices]
     )
     own_keys = [picked[0]] + [
         lax.ppermute(picked[k], "seq", in_plane(lambda g, t: (g ^ partner(k, t)) * COPIES + t))

time: 26.9 us -> 27.2 us (1.011)
  starting transfers between devices: 8.45 us -> 9.21 us
  waiting for transfers between devices: 13.5 us -> 13 us
    ppermute x3, waiting for transfers between devices: 6 us -> 5.39 us  [whole_sequences(): lax.ppermute(picked[k], 'seq', in_plane(lambda g, t: (g ^ partner(k, t))...]
    ppermute x2, starting transfers between devices: 2.71 us -> 3.17 us  [whole_sequences(): lax.ppermute(latent[k], both, [(owner(i, j, first_back(i // COPIES, j) ^...]
    ppermute x2, starting transfers between devices: 0.58 us -> 0.87 us  [whole_sequences(): lax.ppermute(pieces[k], both, [(source, owner(i, j, a)) for i, j in devic...]
where the time goes in v25:
time: 27.2 us; the launch traced here: 27.1 us
  waiting for transfers between devices  13 us (48%)
  starting transfers between devices  9.21 us (34%)
  Pallas kernels  4.76 us (18%)
    ppermute x2, waiting for transfers between devices, whole_sequences(): lax.ppermute(latent[k], both, [(owner(i, j, first_back(i // COPIES, j) ^...  7.05 us
    ppermute x3, waiting for transfers between devices, whole_sequences(): lax.ppermute(picked[k], 'seq', in_plane(lambda g, t: (g ^ partner(k, t))...  5.39 us
    ppermute x3, starting transfers between devices, whole_sequences(): lax.ppermute(picked[k], 'seq', in_plane(lambda g, t: (g ^ partner(k, t))...  3.49 us
    ppermute x2, starting transfers between devices, whole_sequences(): lax.ppermute(latent[k], both, [(owner(i, j, first_back(i // COPIES, j) ^...  3.17 us
    ppermute x1, starting transfers between devices, whole_sequences(): lax.ppermute(left, both, [(flat(i, j), maker(i, j, j % 2)[0]) for i, j in...  1.54 us
    pallas_call x1, Pallas kernels, whole_sequences(): pl.pallas_call(functools.partial(pick_kernel, per_device), out_shape=[jax...  1.38 us
    pallas_call x1, Pallas kernels, whole_sequences(): pl.pallas_call(functools.partial(project_kernel, per_device), out_shape=j...  1.06 us
    ppermute x2, starting transfers between devices, whole_sequences(): lax.ppermute(pieces[k], both, [(source, owner(i, j, a)) for i, j in devic...  0.87 us
  transfers between devices with their start and end apart: 11, of which 6 were waited for; matrix products, arithmetic and copies ran while one was open for 0% of the time, Pallas kernels for 6%

profile of v25, /device:TPU:16, one launch (start us, length us, event | category | flops | bytes accessed | tf_op | source)
XLA Modules:
  0.0 27.1 jit_solution(11288603262143584100)
XLA Ops:
  0.0 1.4 %shard_map.64 = (bf16[576,128]{1,0:T(8,128)(2,1)S(1)}, bf16[576,128]{1,0:T(8,128)(2,1)S(1)}, bf16[576,128]{1,0:T(8,128)(2,1)S(1)}, bf16[576,128]{1,0:T(8,128)(2,...) custom-call(bf16[4,576,128]{2,1,0:T(8,128)(2,1)} %bitcast.1, ...), custom_call_target="tpu_custom_call" | custom-call | flops 20000000000 | tf_op jit(solution)/shard_map/pallas_call | solution.py:260
  1.4 1.5 %collective-permute-start = (bf16[64,256]{1,0:T(8,128)(2,1)S(1)}, bf16[64,256]{1,0:T(8,128)(2,1)S(1)}, u32[]{:S(2)}, u32[]{:S(2)}) collective-permute-start(bf16[64,256]{1,0:T(8,128)(2,1)S(1)} %get-tuple-element.22), channel_id=1, source_target_pairs={{0,8},{1,9},{2,10},{3,11},{4,16},{5,17},{6,26},{7,27},{8,0},{9,1},... | collective-permute-start | bytes 98312 | tf_op jit(solution)/shard_map/ppermute | solution.py:276
  2.9 1.0 %collective-permute-start.3 = (bf16[576,128]{1,0:T(8,128)(2,1)S(1)}, bf16[576,128]{1,0:T(8,128)(2,1)S(1)}, u32[]{:S(2)}, u32[]{:S(2)}) collective-permute-start(bf16[576,128]{1,0:T(8,128)(2,1)S(1)} %get-tuple-element.26), channel_id=1, source_target_pairs={{0,24},{4,28},{8,16},{12,20},{16,8},{20,12},{24,0},{28,4},{1,25},{... | collective-permute-start | bytes 442376 | tf_op jit(solution)/shard_map/ppermute | solution.py:280
  4.0 0.5 %collective-permute-start.4 = (bf16[576,128]{1,0:T(8,128)(2,1)S(1)}, bf16[576,128]{1,0:T(8,128)(2,1)S(1)}, u32[]{:S(2)}, u32[]{:S(2)}) collective-permute-start(bf16[576,128]{1,0:T(8,128)(2,1)S(1)} %get-tuple-element.27), channel_id=1, source_target_pairs={{0,8},{4,20},{8,0},{12,28},{16,24},{20,4},{24,16},{28,12},{1,9},{5... | collective-permute-start | bytes 442376 | tf_op jit(solution)/shard_map/ppermute | solution.py:280
  4.5 1.9 %collective-permute-start.5 = (bf16[576,128]{1,0:T(8,128)(2,1)S(1)}, bf16[576,128]{1,0:T(8,128)(2,1)S(1)}, u32[]{:S(2)}, u32[]{:S(2)}) collective-permute-start(bf16[576,128]{1,0:T(8,128)(2,1)S(1)} %get-tuple-element.28), channel_id=1, source_target_pairs={{0,16},{4,12},{8,24},{12,4},{16,0},{20,28},{24,8},{28,20},{1,17},{... | collective-permute-start | bytes 442376 | tf_op jit(solution)/shard_map/ppermute | solution.py:280
  6.4 0.0 collective-permute-done.refs_1_
  6.4 0.5 %shard_map.65 = (bf16[64,640]{1,0:T(8,128)(2,1)S(1)}, bf16[64,640]{1,0:T(8,128)(2,1)S(1)}) custom-call(bf16[16,128,512]{2,1,0:T(8,128)(2,1)S(1)} %copy-done.1, bf16[64,256]{1,0:T(8,128)(2,1)S(1)} %get-tuple-element.21.refs_0_, bf16[64,256]{1,0:T(8,128)(2,1)S(1)} %collective-permute-done.refs_1_), custom_call_target="tpu_custom_call" | custom-call | flops 20000000000 | tf_op jit(solution)/shard_map/pallas_call | solution.py:294
  6.9 0.5 %collective-permute-start.1 = (bf16[64,640]{1,0:T(8,128)(2,1)S(1)}, bf16[64,640]{1,0:T(8,128)(2,1)S(1)}, u32[]{:S(2)}, u32[]{:S(2)}) collective-permute-start(bf16[64,640]{1,0:T(8,128)(2,1)S(1)} %get-tuple-element.23), channel_id=1, source_target_pairs={{8,12},{1,4},{10,8},{3,0},{16,20},{5,28},{26,24},{7,16},{0,5},{9,1... | collective-permute-start | bytes 245768 | tf_op jit(solution)/shard_map/ppermute | solution.py:303
  7.4 0.4 %collective-permute-start.2 = (bf16[64,640]{1,0:T(8,128)(2,1)S(1)}, bf16[64,640]{1,0:T(8,128)(2,1)S(1)}, u32[]{:S(2)}, u32[]{:S(2)}) collective-permute-start(bf16[64,640]{1,0:T(8,128)(2,1)S(1)} %get-tuple-element.24), channel_id=1, source_target_pairs={{0,4},{9,12},{2,0},{11,8},{4,28},{17,20},{6,16},{27,24},{8,13},{1,... | collective-permute-start | bytes 245768 | tf_op jit(solution)/shard_map/ppermute | solution.py:303
  7.8 2.8 %collective-permute-done.3.refs_3_.second_ref = bf16[576,128]{1,0:T(8,128)(2,1)S(1)} collective-permute-done((bf16[576,128]{1,0:T(8,128)(2,1)S(1)}, bf16[576,128]{1,0:T(8,128)(2,1)S(1)}, u32[]{:S(2)}, u32[]{:S(2)}) %collective-permute-start.3) | collective-permute-done | bytes 147488 | tf_op jit(solution)/shard_map/ppermute | solution.py:280
  10.6 0.4 %shard_map.67 = bf16[2,576,128]{2,1,0:T(8,128)(2,1)S(1)} custom-call(bf16[576,128]{1,0:T(8,128)(2,1)S(1)} %get-tuple-element.25.refs_2_.first_ref, bf16[576,128]{1,0:T(8,128)(2,1)S(1)} %collective-permute-done.3.refs_3_.second_ref), custom_call_target="tpu_custom_call" | custom-call | tf_op jit(solution)/shard_map/pallas_call | solution.py:283
  10.9 0.1 collective-permute-start.6
  11.1 1.3 %collective-permute-done.4.refs_4_ = bf16[576,128]{1,0:T(8,128)(2,1)S(1)} collective-permute-done((bf16[576,128]{1,0:T(8,128)(2,1)S(1)}, bf16[576,128]{1,0:T(8,128)(2,1)S(1)}, u32[]{:S(2)}, u32[]{:S(2)}) %collective-permute-start.4) | collective-permute-done | bytes 147488 | tf_op jit(solution)/shard_map/ppermute | solution.py:280
  12.4 1.3 %collective-permute-done.5.refs_5_ = bf16[576,128]{1,0:T(8,128)(2,1)S(1)} collective-permute-done((bf16[576,128]{1,0:T(8,128)(2,1)S(1)}, bf16[576,128]{1,0:T(8,128)(2,1)S(1)}, u32[]{:S(2)}, u32[]{:S(2)}) %collective-permute-start.5) | collective-permute-done | bytes 147488 | tf_op jit(solution)/shard_map/ppermute | solution.py:280
  13.7 0.0 collective-permute-start.8
  13.7 0.0 copy-start
  13.7 0.8 %shard_map.66 = (bf16[128,576]{1,0:T(8,128)(2,1)S(1)}, f32[128,128]{1,0:T(8,128)S(1)}, f32[128,128]{1,0:T(8,128)S(1)}, f32[128,512]{1,0:T(8,128)S(1)}) custom-call(s32[8,128]{1,0:T(8,128)S(1)} %get-tuple-element.20.limit_ref, bf16[64,640]{1,0:T(8,128)(2,1)S(1)} %collective-permute-done.1.refs_0_, bf16[64,640]{1,0:T(8,128)(2,1)S(1)} %collective-permute-done.2.refs_1_, ...), custom_call_target="tpu_custom_call" | custom-call | flops 20000000000 | tf_op jit(solution)/shard_map/pallas_call | solution.py:315
  14.5 0.6 %collective-permute-done.8.refs_1_ = bf16[576,128]{1,0:T(8,128)(2,1)S(1)} collective-permute-done((bf16[576,128]{1,0:T(8,128)(2,1)S(1)}, bf16[576,128]{1,0:T(8,128)(2,1)S(1)}, u32[]{:S(2)}, u32[]{:S(2)}) %collective-permute-start.8) | collective-permute-done | bytes 147488 | tf_op jit(solution)/shard_map/ppermute | solution.py:292
  15.1 0.7 %shard_map.68 = (bf16[64,512]{1,0:T(8,128)(2,1)S(1)}, bf16[64,512]{1,0:T(8,128)(2,1)S(1)}) custom-call(s32[8,128]{1,0:T(8,128)S(1)} %get-tuple-element.20.limit_ref, bf16[128,576]{1,0:T(8,128)(2,1)S(1)} %get-tuple-element.29.q_ref, f32[128,128]{1,0:T(8,128)S(1)} %get-tuple-element.30.top_ref, f32[128,128]{1,0:T(8,128)S(1)} %get-tuple-element.31.total_ref, ...), custom_call_target="tpu_custom_call" | custom-call | tf_op jit(solution)/shard_map/pallas_call | solution.py:328
  15.8 0.8 %collective-permute-start.10 = (bf16[64,512]{1,0:T(8,128)(2,1)S(1)}, bf16[64,512]{1,0:T(8,128)(2,1)S(1)}, u32[]{:S(2)}, u32[]{:S(2)}) collective-permute-start(bf16[64,512]{1,0:T(8,128)(2,1)S(1)} %get-tuple-element.34), channel_id=1, source_target_pairs={{4,0},{12,1},{0,2},{8,3},{20,4},{28,5},{16,6},{24,7},{5,8},{13,9},... | collective-permute-start | bytes 196616 | tf_op jit(solution)/shard_map/ppermute | solution.py:337
  16.6 2.4 %collective-permute-start.9 = (bf16[64,512]{1,0:T(8,128)(2,1)S(1)}, bf16[64,512]{1,0:T(8,128)(2,1)S(1)}, u32[]{:S(2)}, u32[]{:S(2)}) collective-permute-start(bf16[64,512]{1,0:T(8,128)(2,1)S(1)} %get-tuple-element.33), channel_id=1, source_target_pairs={{12,0},{4,1},{8,2},{0,3},{28,4},{20,5},{24,6},{16,7},{13,8},{5,9},... | collective-permute-start | bytes 196616 | tf_op jit(solution)/shard_map/ppermute | solution.py:337
  18.9 2.1 %collective-permute-done.10.refs_1_ = bf16[64,512]{1,0:T(8,128)(2,1)S(1)} collective-permute-done((bf16[64,512]{1,0:T(8,128)(2,1)S(1)}, bf16[64,512]{1,0:T(8,128)(2,1)S(1)}, u32[]{:S(2)}, u32[]{:S(2)}) %collective-permute-start.10) | collective-permute-done | bytes 65568 | tf_op jit(solution)/shard_map/ppermute | solution.py:337
  21.0 5.0 %collective-permute-done.9.refs_0_ = bf16[64,512]{1,0:T(8,128)(2,1)S(1)} collective-permute-done((bf16[64,512]{1,0:T(8,128)(2,1)S(1)}, bf16[64,512]{1,0:T(8,128)(2,1)S(1)}, u32[]{:S(2)}, u32[]{:S(2)}) %collective-permute-start.9) | collective-permute-done | bytes 65568 | tf_op jit(solution)/shard_map/ppermute | solution.py:337
  26.0 1.1 %shard_map.69 = bf16[8,16,128]{2,1,0:T(8,128)(2,1)} custom-call(bf16[16,512,128]{2,1,0:T(8,128)(2,1)S(1)} %copy-done, bf16[64,512]{1,0:T(8,128)(2,1)S(1)} %collective-permute-done.9.refs_0_, bf16[64,512]{1,0:T(8,128)(2,1)S(1)} %collective-permute-done.10.refs_1_), custom_call_target="tpu_custom_call" | custom-call | tf_op jit(solution)/shard_map/pallas_call | solution.py:344
  (8 shorter events, 0.0 us)
Async XLA Ops:
  0.0 6.4 %copy-start.1 = (bf16[16,128,512]{2,1,0:T(8,128)(2,1)S(1)}, bf16[16,128,512]{2,1,0:T(8,128)(2,1)}, u32[]{:S(2)}) copy-start(bf16[16,128,512]{2,1,0:T(8,128)(2,1)} %w_ref.2) | copy-start | bytes 6291460
  1.4 5.0 %collective-permute-start = (bf16[64,256]{1,0:T(8,128)(2,1)S(1)}, bf16[64,256]{1,0:T(8,128)(2,1)S(1)}, u32[]{:S(2)}, u32[]{:S(2)}) collective-permute-start(bf16[64,256]{1,0:T(8,128)(2,1)S(1)} %get-tuple-element.22), channel_id=1, source_target_pairs={{0,8},{1,9},{2,10},{3,11},{4,16},{5,17},{6,26},{7,27},{8,0},{9,1},... | collective-permute-start | bytes 98312 | tf_op jit(solution)/shard_map/ppermute | solution.py:276
  2.9 7.6 %collective-permute-start.3 = (bf16[576,128]{1,0:T(8,128)(2,1)S(1)}, bf16[576,128]{1,0:T(8,128)(2,1)S(1)}, u32[]{:S(2)}, u32[]{:S(2)}) collective-permute-start(bf16[576,128]{1,0:T(8,128)(2,1)S(1)} %get-tuple-element.26), channel_id=1, source_target_pairs={{0,24},{4,28},{8,16},{12,20},{16,8},{20,12},{24,0},{28,4},{1,25},{... | collective-permute-start | bytes 442376 | tf_op jit(solution)/shard_map/ppermute | solution.py:280
  4.0 8.4 %collective-permute-start.4 = (bf16[576,128]{1,0:T(8,128)(2,1)S(1)}, bf16[576,128]{1,0:T(8,128)(2,1)S(1)}, u32[]{:S(2)}, u32[]{:S(2)}) collective-permute-start(bf16[576,128]{1,0:T(8,128)(2,1)S(1)} %get-tuple-element.27), channel_id=1, source_target_pairs={{0,8},{4,20},{8,0},{12,28},{16,24},{20,4},{24,16},{28,12},{1,9},{5... | collective-permute-start | bytes 442376 | tf_op jit(solution)/shard_map/ppermute | solution.py:280
  4.5 9.2 %collective-permute-start.5 = (bf16[576,128]{1,0:T(8,128)(2,1)S(1)}, bf16[576,128]{1,0:T(8,128)(2,1)S(1)}, u32[]{:S(2)}, u32[]{:S(2)}) collective-permute-start(bf16[576,128]{1,0:T(8,128)(2,1)S(1)} %get-tuple-element.28), channel_id=1, source_target_pairs={{0,16},{4,12},{8,24},{12,4},{16,0},{20,28},{24,8},{28,20},{1,17},{... | collective-permute-start | bytes 442376 | tf_op jit(solution)/shard_map/ppermute | solution.py:280
  6.9 6.8 %collective-permute-start.1 = (bf16[64,640]{1,0:T(8,128)(2,1)S(1)}, bf16[64,640]{1,0:T(8,128)(2,1)S(1)}, u32[]{:S(2)}, u32[]{:S(2)}) collective-permute-start(bf16[64,640]{1,0:T(8,128)(2,1)S(1)} %get-tuple-element.23), channel_id=1, source_target_pairs={{8,12},{1,4},{10,8},{3,0},{16,20},{5,28},{26,24},{7,16},{0,5},{9,1... | collective-permute-start | bytes 245768 | tf_op jit(solution)/shard_map/ppermute | solution.py:303
  7.4 6.3 %collective-permute-start.2 = (bf16[64,640]{1,0:T(8,128)(2,1)S(1)}, bf16[64,640]{1,0:T(8,128)(2,1)S(1)}, u32[]{:S(2)}, u32[]{:S(2)}) collective-permute-start(bf16[64,640]{1,0:T(8,128)(2,1)S(1)} %get-tuple-element.24), channel_id=1, source_target_pairs={{0,4},{9,12},{2,0},{11,8},{4,28},{17,20},{6,16},{27,24},{8,13},{1,... | collective-permute-start | bytes 245768 | tf_op jit(solution)/shard_map/ppermute | solution.py:303
  10.9 4.1 %collective-permute-start.6 = (bf16[2,576,128]{2,1,0:T(8,128)(2,1)S(1)}, bf16[2,576,128]{2,1,0:T(8,128)(2,1)S(1)}, u32[]{:S(2)}, u32[]{:S(2)}) collective-permute-start(bf16[2,576,128]{2,1,0:T(8,128)(2,1)S(1)} %shard_map.67), channel_id=1, source_target_pairs={{0,4},{4,0},{8,12},{12,8},{16,20},{20,16},{24,28},{28,24},{1,5},{5... | collective-permute-start | bytes 884744 | tf_op jit(solution)/shard_map/ppermute | solution.py:292
  12.4 2.1 %collective-permute-start.7 = (bf16[576,128]{1,0:T(8,128)(2,1)S(1)}, bf16[576,128]{1,0:T(8,128)(2,1)S(1)}, u32[]{:S(2)}, u32[]{:S(2)}) collective-permute-start(bf16[576,128]{1,0:T(8,128)(2,1)S(1)} %collective-permute-done.4.refs_4_), channel_id=1, source_target_pairs={{0,4},{4,0},{8,12},{12,8},{16,20},{20,16},{24,28},{28,24},{1,5},{5... | collective-permute-start | bytes 442376 | tf_op jit(solution)/shard_map/ppermute | solution.py:292
  13.7 1.4 %collective-permute-start.8 = (bf16[576,128]{1,0:T(8,128)(2,1)S(1)}, bf16[576,128]{1,0:T(8,128)(2,1)S(1)}, u32[]{:S(2)}, u32[]{:S(2)}) collective-permute-start(bf16[576,128]{1,0:T(8,128)(2,1)S(1)} %collective-permute-done.5.refs_5_), channel_id=1, source_target_pairs={{0,4},{4,0},{8,12},{12,8},{16,20},{20,16},{24,28},{28,24},{1,5},{5... | collective-permute-start | bytes 442376 | tf_op jit(solution)/shard_map/ppermute | solution.py:292
  13.7 12.3 %copy-start = (bf16[16,512,128]{2,1,0:T(8,128)(2,1)S(1)}, bf16[16,512,128]{2,1,0:T(8,128)(2,1)}, u32[]{:S(2)}) copy-start(bf16[16,512,128]{2,1,0:T(8,128)(2,1)} %w_ref.3) | copy-start | bytes 6291460
  15.8 5.2 %collective-permute-start.10 = (bf16[64,512]{1,0:T(8,128)(2,1)S(1)}, bf16[64,512]{1,0:T(8,128)(2,1)S(1)}, u32[]{:S(2)}, u32[]{:S(2)}) collective-permute-start(bf16[64,512]{1,0:T(8,128)(2,1)S(1)} %get-tuple-element.34), channel_id=1, source_target_pairs={{4,0},{12,1},{0,2},{8,3},{20,4},{28,5},{16,6},{24,7},{5,8},{13,9},... | collective-permute-start | bytes 196616 | tf_op jit(solution)/shard_map/ppermute | solution.py:337
  16.6 9.4 %collective-permute-start.9 = (bf16[64,512]{1,0:T(8,128)(2,1)S(1)}, bf16[64,512]{1,0:T(8,128)(2,1)S(1)}, u32[]{:S(2)}, u32[]{:S(2)}) collective-permute-start(bf16[64,512]{1,0:T(8,128)(2,1)S(1)} %get-tuple-element.33), channel_id=1, source_target_pairs={{12,0},{4,1},{8,2},{0,3},{28,4},{20,5},{24,6},{16,7},{13,8},{5,9},... | collective-permute-start | bytes 196616 | tf_op jit(solution)/shard_map/ppermute | solution.py:337

commit v26 on v19

--- a/solution.py
+++ b/solution.py
@@ -38,7 +38,7 @@
 
 
 def partner(k, core):
-    return (0, 1 ^ 3 * core, 3, 2 ^ 3 * core)[k]
+    return (0, 3, 2 ^ 3 * core, 1 ^ 3 * core)[k]
 
 
 def pick_kernel(per_device, cache_hbm, q_hbm, new_hbm, len_hbm, *refs):

time: 27.3 us -> 27.1 us (level)
  waiting for transfers between devices: 14.7 us -> 12.3 us
  starting transfers between devices: 7.62 us -> 9.79 us
    ppermute x3, waiting for transfers between devices: 6.4 us -> 3.73 us  [whole_sequences(): lax.ppermute(picked[k], 'seq', in_plane(lambda g, t: (g ^ partner(k, t))...]
    ppermute x3, starting transfers between devices: 0.59 us -> 1.81 us  [whole_sequences(): lax.ppermute(keys, 'seq', other_core)]
    ppermute x2, starting transfers between devices: 3.28 us -> 4.23 us  [whole_sequences(): lax.ppermute(latent[k], both, [(owner(i, j, first_back(i // COPIES, j) ^...]
    ppermute x2, waiting for transfers between devices: 0.01 us -> 0.55 us  [whole_sequences(): lax.ppermute(pieces[k], both, [(host(i, j), owner(i, j, leaves_as(k, j)))...]
    ppermute x3, waiting for transfers between devices: 0.29 us -> 0.01 us  [whole_sequences(): lax.ppermute(keys, 'seq', other_core)]
where the time goes in v26:
time: 27.1 us; the launch traced here: 26.9 us
  waiting for transfers between devices  12.3 us (45%)
  starting transfers between devices  9.79 us (36%)
  Pallas kernels  4.75 us (18%)
    ppermute x2, waiting for transfers between devices, whole_sequences(): lax.ppermute(latent[k], both, [(owner(i, j, first_back(i // COPIES, j) ^...  6.38 us
    ppermute x2, starting transfers between devices, whole_sequences(): lax.ppermute(latent[k], both, [(owner(i, j, first_back(i // COPIES, j) ^...  4.23 us
    ppermute x3, waiting for transfers between devices, whole_sequences(): lax.ppermute(picked[k], 'seq', in_plane(lambda g, t: (g ^ partner(k, t))...  3.73 us
    ppermute x3, starting transfers between devices, whole_sequences(): lax.ppermute(picked[k], 'seq', in_plane(lambda g, t: (g ^ partner(k, t))...  3.55 us
    ppermute x3, starting transfers between devices, whole_sequences(): lax.ppermute(keys, 'seq', other_core)  1.81 us
    ppermute x1, waiting for transfers between devices, whole_sequences(): lax.ppermute(packed, both, [(flat(i, j), host(i, j)) for i, j in devices])  1.63 us
    pallas_call x1, Pallas kernels, whole_sequences(): pl.pallas_call(functools.partial(pick_kernel, per_device), out_shape=[jax...  1.38 us
    pallas_call x1, Pallas kernels, whole_sequences(): pl.pallas_call(functools.partial(project_kernel, per_device), out_shape=j...  1.06 us
  transfers between devices with their start and end apart: 11, of which 7 were waited for; matrix products, arithmetic and copies ran while one was open for 0% of the time, Pallas kernels for 6%

profile of v26, /device:TPU:6, one launch (start us, length us, event | category | flops | bytes accessed | tf_op | source)
XLA Modules:
  0.0 26.9 jit_solution(2972146015665282539)
XLA Ops:
  0.0 1.4 %shard_map.64 = (bf16[576,128]{1,0:T(8,128)(2,1)S(1)}, bf16[576,128]{1,0:T(8,128)(2,1)S(1)}, bf16[576,128]{1,0:T(8,128)(2,1)S(1)}, bf16[576,128]{1,0:T(8,128)(2,...) custom-call(bf16[4,576,128]{2,1,0:T(8,128)(2,1)} %bitcast.1, bf16[8,16,192]{2,1,0:T(8,128)(2,1)} %q_hbm.1, ...), custom_call_target="tpu_custom_call" | custom-call | flops 20000000000 | tf_op jit(solution)/shard_map/pallas_call | solution.py:245
  1.4 0.1 collective-permute-start
  1.5 2.0 %collective-permute-start.3 = (bf16[576,128]{1,0:T(8,128)(2,1)S(1)}, bf16[576,128]{1,0:T(8,128)(2,1)S(1)}, u32[]{:S(2)}, u32[]{:S(2)}) collective-permute-start(bf16[576,128]{1,0:T(8,128)(2,1)S(1)} %get-tuple-element.24), channel_id=1, source_target_pairs={{0,24},{4,28},{8,16},{12,20},{16,8},{20,12},{24,0},{28,4},{1,25},{... | collective-permute-start | bytes 442376 | tf_op jit(solution)/shard_map/ppermute | solution.py:265
  3.4 0.1 collective-permute-start.4
  3.5 1.5 %collective-permute-start.5 = (bf16[576,128]{1,0:T(8,128)(2,1)S(1)}, bf16[576,128]{1,0:T(8,128)(2,1)S(1)}, u32[]{:S(2)}, u32[]{:S(2)}) collective-permute-start(bf16[576,128]{1,0:T(8,128)(2,1)S(1)} %get-tuple-element.26), channel_id=1, source_target_pairs={{0,8},{4,20},{8,0},{12,28},{16,24},{20,4},{24,16},{28,12},{1,9},{5... | collective-permute-start | bytes 442376 | tf_op jit(solution)/shard_map/ppermute | solution.py:265
  5.0 1.6 %collective-permute-done.packed_ref = bf16[128,256]{1,0:T(8,128)(2,1)S(1)} collective-permute-done((bf16[128,256]{1,0:T(8,128)(2,1)S(1)}, bf16[128,256]{1,0:T(8,128)(2,1)S(1)}, u32[]{:S(2)}, u32[]{:S(2)}) %collective-permute-start) | collective-permute-done | bytes 65568 | tf_op jit(solution)/shard_map/ppermute | solution.py:263
  6.7 0.5 %shard_map.65 = (bf16[64,640]{1,0:T(8,128)(2,1)S(1)}, bf16[64,640]{1,0:T(8,128)(2,1)S(1)}) custom-call(bf16[16,128,512]{2,1,0:T(8,128)(2,1)S(1)} %copy-done.1, bf16[128,256]{1,0:T(8,128)(2,1)S(1)} %collective-permute-done.packed_ref), custom_call_target="tpu_custom_call" | custom-call | flops 20000000000 | tf_op jit(solution)/shard_map/pallas_call | solution.py:279
  7.1 0.1 collective-permute-start.1
  7.2 0.1 collective-permute-start.2
  7.3 2.0 %collective-permute-done.3.refs_3_.second_ref = bf16[576,128]{1,0:T(8,128)(2,1)S(1)} collective-permute-done((bf16[576,128]{1,0:T(8,128)(2,1)S(1)}, bf16[576,128]{1,0:T(8,128)(2,1)S(1)}, u32[]{:S(2)}, u32[]{:S(2)}) %collective-permute-start.3) | collective-permute-done | bytes 147488 | tf_op jit(solution)/shard_map/ppermute | solution.py:265
  9.3 0.4 %shard_map.67 = bf16[2,576,128]{2,1,0:T(8,128)(2,1)S(1)} custom-call(bf16[576,128]{1,0:T(8,128)(2,1)S(1)} %get-tuple-element.23.refs_2_.first_ref, bf16[576,128]{1,0:T(8,128)(2,1)S(1)} %collective-permute-done.3.refs_3_.second_ref), custom_call_target="tpu_custom_call" | custom-call | tf_op jit(solution)/shard_map/pallas_call | solution.py:268
  9.7 1.3 %collective-permute-start.6 = (bf16[2,576,128]{2,1,0:T(8,128)(2,1)S(1)}, bf16[2,576,128]{2,1,0:T(8,128)(2,1)S(1)}, u32[]{:S(2)}, u32[]{:S(2)}) collective-permute-start(bf16[2,576,128]{2,1,0:T(8,128)(2,1)S(1)} %shard_map.67), channel_id=1, source_target_pairs={{0,4},{4,0},{8,12},{12,8},{16,20},{20,16},{24,28},{28,24},{1,5},{5... | collective-permute-start | bytes 884744 | tf_op jit(solution)/shard_map/ppermute | solution.py:277
  11.0 1.7 %collective-permute-done.4.refs_4_ = bf16[576,128]{1,0:T(8,128)(2,1)S(1)} collective-permute-done((bf16[576,128]{1,0:T(8,128)(2,1)S(1)}, bf16[576,128]{1,0:T(8,128)(2,1)S(1)}, u32[]{:S(2)}, u32[]{:S(2)}) %collective-permute-start.4) | collective-permute-done | bytes 147488 | tf_op jit(solution)/shard_map/ppermute | solution.py:265
  12.7 0.5 %collective-permute-start.8 = (bf16[576,128]{1,0:T(8,128)(2,1)S(1)}, bf16[576,128]{1,0:T(8,128)(2,1)S(1)}, u32[]{:S(2)}, u32[]{:S(2)}) collective-permute-start(bf16[576,128]{1,0:T(8,128)(2,1)S(1)} %collective-permute-done.5.refs_5_), channel_id=1, source_target_pairs={{0,4},{4,0},{8,12},{12,8},{16,20},{20,16},{24,28},{28,24},{1,5},{5... | collective-permute-start | bytes 442376 | tf_op jit(solution)/shard_map/ppermute | solution.py:277
  13.2 0.4 %collective-permute-done.1.refs_0_ = bf16[64,640]{1,0:T(8,128)(2,1)S(1)} collective-permute-done((bf16[64,640]{1,0:T(8,128)(2,1)S(1)}, bf16[64,640]{1,0:T(8,128)(2,1)S(1)}, u32[]{:S(2)}, u32[]{:S(2)}) %collective-permute-start.1) | collective-permute-done | bytes 81952 | tf_op jit(solution)/shard_map/ppermute | solution.py:288
  13.6 0.1 collective-permute-done.2.refs_1_
  13.7 0.8 %shard_map.66 = (bf16[128,576]{1,0:T(8,128)(2,1)S(1)}, f32[128,128]{1,0:T(8,128)S(1)}, f32[128,128]{1,0:T(8,128)S(1)}, f32[128,512]{1,0:T(8,128)S(1)}) custom-call(s32[8,128]{1,0:T(8,128)S(1)} %get-tuple-element.19.limit_ref, bf16[64,640]{1,0:T(8,128)(2,1)S(1)} %collective-permute-done.1.refs_0_, bf16[64,640]{1,0:T(8,128)(2,1)S(1)} %collective-permute-done.2.refs_1_, ...), custom_call_target="tpu_custom_call" | custom-call | flops 20000000000 | tf_op jit(solution)/shard_map/pallas_call | solution.py:296
  14.5 0.0 collective-permute-done.8.refs_1_
  14.5 0.0 collective-permute-done.6.pair_ref
  14.5 0.7 %shard_map.68 = (bf16[64,512]{1,0:T(8,128)(2,1)S(1)}, bf16[64,512]{1,0:T(8,128)(2,1)S(1)}) custom-call(s32[8,128]{1,0:T(8,128)S(1)} %get-tuple-element.19.limit_ref, bf16[128,576]{1,0:T(8,128)(2,1)S(1)} %get-tuple-element.27.q_ref, f32[128,128]{1,0:T(8,128)S(1)} %get-tuple-element.28.top_ref, f32[128,128]{1,0:T(8,128)S(1)} %get-tuple-element.29.total_ref, ...), custom_call_target="tpu_custom_call" | custom-call | tf_op jit(solution)/shard_map/pallas_call | solution.py:309
  15.3 4.2 %collective-permute-start.10 = (bf16[64,512]{1,0:T(8,128)(2,1)S(1)}, bf16[64,512]{1,0:T(8,128)(2,1)S(1)}, u32[]{:S(2)}, u32[]{:S(2)}) collective-permute-start(bf16[64,512]{1,0:T(8,128)(2,1)S(1)} %get-tuple-element.32), channel_id=1, source_target_pairs={{4,0},{12,1},{0,2},{8,3},{20,4},{28,5},{16,6},{24,7},{5,8},{13,9},... | collective-permute-start | bytes 196616 | tf_op jit(solution)/shard_map/ppermute | solution.py:318
  19.5 3.6 %collective-permute-done.10.refs_1_ = bf16[64,512]{1,0:T(8,128)(2,1)S(1)} collective-permute-done((bf16[64,512]{1,0:T(8,128)(2,1)S(1)}, bf16[64,512]{1,0:T(8,128)(2,1)S(1)}, u32[]{:S(2)}, u32[]{:S(2)}) %collective-permute-start.10) | collective-permute-done | bytes 65568 | tf_op jit(solution)/shard_map/ppermute | solution.py:318
  23.1 2.8 %collective-permute-done.9.refs_0_ = bf16[64,512]{1,0:T(8,128)(2,1)S(1)} collective-permute-done((bf16[64,512]{1,0:T(8,128)(2,1)S(1)}, bf16[64,512]{1,0:T(8,128)(2,1)S(1)}, u32[]{:S(2)}, u32[]{:S(2)}) %collective-permute-start.9) | collective-permute-done | bytes 65568 | tf_op jit(solution)/shard_map/ppermute | solution.py:318
  25.9 1.1 %shard_map.69 = bf16[8,16,128]{2,1,0:T(8,128)(2,1)} custom-call(bf16[16,512,128]{2,1,0:T(8,128)(2,1)S(1)} %copy-done, bf16[64,512]{1,0:T(8,128)(2,1)S(1)} %collective-permute-done.9.refs_0_, bf16[64,512]{1,0:T(8,128)(2,1)S(1)} %collective-permute-done.10.refs_1_), custom_call_target="tpu_custom_call" | custom-call | tf_op jit(solution)/shard_map/pallas_call | solution.py:325
  (8 shorter events, 0.0 us)
Async XLA Ops:
  0.0 6.7 %copy-start.1 = (bf16[16,128,512]{2,1,0:T(8,128)(2,1)S(1)}, bf16[16,128,512]{2,1,0:T(8,128)(2,1)}, u32[]{:S(2)}) copy-start(bf16[16,128,512]{2,1,0:T(8,128)(2,1)} %w_ref.2) | copy-start | bytes 6291460
  1.4 5.3 %collective-permute-start = (bf16[128,256]{1,0:T(8,128)(2,1)S(1)}, bf16[128,256]{1,0:T(8,128)(2,1)S(1)}, u32[]{:S(2)}, u32[]{:S(2)}) collective-permute-start(bf16[128,256]{1,0:T(8,128)(2,1)S(1)} %get-tuple-element.20), channel_id=1, source_target_pairs={{0,8},{1,5},{2,6},{3,11},{4,24},{5,21},{6,22},{7,27},{8,12},{9,1},... | collective-permute-start | bytes 196616 | tf_op jit(solution)/shard_map/ppermute | solution.py:263
  1.5 7.9 %collective-permute-start.3 = (bf16[576,128]{1,0:T(8,128)(2,1)S(1)}, bf16[576,128]{1,0:T(8,128)(2,1)S(1)}, u32[]{:S(2)}, u32[]{:S(2)}) collective-permute-start(bf16[576,128]{1,0:T(8,128)(2,1)S(1)} %get-tuple-element.24), channel_id=1, source_target_pairs={{0,24},{4,28},{8,16},{12,20},{16,8},{20,12},{24,0},{28,4},{1,25},{... | collective-permute-start | bytes 442376 | tf_op jit(solution)/shard_map/ppermute | solution.py:265
  3.4 9.3 %collective-permute-start.4 = (bf16[576,128]{1,0:T(8,128)(2,1)S(1)}, bf16[576,128]{1,0:T(8,128)(2,1)S(1)}, u32[]{:S(2)}, u32[]{:S(2)}) collective-permute-start(bf16[576,128]{1,0:T(8,128)(2,1)S(1)} %get-tuple-element.25), channel_id=1, source_target_pairs={{0,16},{4,12},{8,24},{12,4},{16,0},{20,28},{24,8},{28,20},{1,17},{... | collective-permute-start | bytes 442376 | tf_op jit(solution)/shard_map/ppermute | solution.py:265
  3.5 9.2 %collective-permute-start.5 = (bf16[576,128]{1,0:T(8,128)(2,1)S(1)}, bf16[576,128]{1,0:T(8,128)(2,1)S(1)}, u32[]{:S(2)}, u32[]{:S(2)}) collective-permute-start(bf16[576,128]{1,0:T(8,128)(2,1)S(1)} %get-tuple-element.26), channel_id=1, source_target_pairs={{0,8},{4,20},{8,0},{12,28},{16,24},{20,4},{24,16},{28,12},{1,9},{5... | collective-permute-start | bytes 442376 | tf_op jit(solution)/shard_map/ppermute | solution.py:265
  7.1 6.5 %collective-permute-start.1 = (bf16[64,640]{1,0:T(8,128)(2,1)S(1)}, bf16[64,640]{1,0:T(8,128)(2,1)S(1)}, u32[]{:S(2)}, u32[]{:S(2)}) collective-permute-start(bf16[64,640]{1,0:T(8,128)(2,1)S(1)} %get-tuple-element.21), channel_id=1, source_target_pairs={{8,4},{5,12},{6,0},{11,8},{24,20},{21,28},{22,16},{27,24},{12,5},{... | collective-permute-start | bytes 245768 | tf_op jit(solution)/shard_map/ppermute | solution.py:288
  7.2 6.5 %collective-permute-start.2 = (bf16[64,640]{1,0:T(8,128)(2,1)S(1)}, bf16[64,640]{1,0:T(8,128)(2,1)S(1)}, u32[]{:S(2)}, u32[]{:S(2)}) collective-permute-start(bf16[64,640]{1,0:T(8,128)(2,1)S(1)} %get-tuple-element.22), channel_id=1, source_target_pairs={{8,12},{5,4},{6,8},{11,0},{24,28},{21,20},{22,24},{27,16},{12,13},... | collective-permute-start | bytes 245768 | tf_op jit(solution)/shard_map/ppermute | solution.py:288
  9.7 4.8 %collective-permute-start.6 = (bf16[2,576,128]{2,1,0:T(8,128)(2,1)S(1)}, bf16[2,576,128]{2,1,0:T(8,128)(2,1)S(1)}, u32[]{:S(2)}, u32[]{:S(2)}) collective-permute-start(bf16[2,576,128]{2,1,0:T(8,128)(2,1)S(1)} %shard_map.67), channel_id=1, source_target_pairs={{0,4},{4,0},{8,12},{12,8},{16,20},{20,16},{24,28},{28,24},{1,5},{5... | collective-permute-start | bytes 884744 | tf_op jit(solution)/shard_map/ppermute | solution.py:277
  12.7 1.8 %collective-permute-start.7 = (bf16[576,128]{1,0:T(8,128)(2,1)S(1)}, bf16[576,128]{1,0:T(8,128)(2,1)S(1)}, u32[]{:S(2)}, u32[]{:S(2)}) collective-permute-start(bf16[576,128]{1,0:T(8,128)(2,1)S(1)} %collective-permute-done.4.refs_4_), channel_id=1, source_target_pairs={{0,4},{4,0},{8,12},{12,8},{16,20},{20,16},{24,28},{28,24},{1,5},{5... | collective-permute-start | bytes 442376 | tf_op jit(solution)/shard_map/ppermute | solution.py:277
  12.7 1.8 %collective-permute-start.8 = (bf16[576,128]{1,0:T(8,128)(2,1)S(1)}, bf16[576,128]{1,0:T(8,128)(2,1)S(1)}, u32[]{:S(2)}, u32[]{:S(2)}) collective-permute-start(bf16[576,128]{1,0:T(8,128)(2,1)S(1)} %collective-permute-done.5.refs_5_), channel_id=1, source_target_pairs={{0,4},{4,0},{8,12},{12,8},{16,20},{20,16},{24,28},{28,24},{1,5},{5... | collective-permute-start | bytes 442376 | tf_op jit(solution)/shard_map/ppermute | solution.py:277
  13.7 12.1 %copy-start = (bf16[16,512,128]{2,1,0:T(8,128)(2,1)S(1)}, bf16[16,512,128]{2,1,0:T(8,128)(2,1)}, u32[]{:S(2)}) copy-start(bf16[16,512,128]{2,1,0:T(8,128)(2,1)} %w_ref.3) | copy-start | bytes 6291460
  15.3 7.8 %collective-permute-start.10 = (bf16[64,512]{1,0:T(8,128)(2,1)S(1)}, bf16[64,512]{1,0:T(8,128)(2,1)S(1)}, u32[]{:S(2)}, u32[]{:S(2)}) collective-permute-start(bf16[64,512]{1,0:T(8,128)(2,1)S(1)} %get-tuple-element.32), channel_id=1, source_target_pairs={{4,0},{12,1},{0,2},{8,3},{20,4},{28,5},{16,6},{24,7},{5,8},{13,9},... | collective-permute-start | bytes 196616 | tf_op jit(solution)/shard_map/ppermute | solution.py:318
  19.5 6.4 %collective-permute-start.9 = (bf16[64,512]{1,0:T(8,128)(2,1)S(1)}, bf16[64,512]{1,0:T(8,128)(2,1)S(1)}, u32[]{:S(2)}, u32[]{:S(2)}) collective-permute-start(bf16[64,512]{1,0:T(8,128)(2,1)S(1)} %get-tuple-element.31), channel_id=1, source_target_pairs={{12,0},{4,1},{8,2},{0,3},{28,4},{20,5},{24,6},{16,7},{13,8},{5,9},... | collective-permute-start | bytes 196616 | tf_op jit(solution)/shard_map/ppermute | solution.py:318

commit v27 on v15

--- a/solution.py
+++ b/solution.py
@@ -20,7 +20,7 @@
 
 
 def leaves_as(k, head_shard):
-    return (k + head_shard) % 2
+    return (k + head_shard + 1) % 2
 
 
 def far_half(plane, pair):
@@ -34,7 +34,7 @@
 
 def first_block(plane, chip, core):
     near = 1 * (chip % 2 == plane % 2)
-    return far_half(plane, 1 - core) ^ near ^ chip % 2
+    return far_half(plane, 1 - core) ^ near ^ 1 - chip % 2
 
 
 def partner(k, core):

time: 26.5 us -> 27 us (1.019)
  waiting for transfers between devices: 12.1 us -> 12.9 us
  starting transfers between devices: 9.4 us -> 9.05 us
    ppermute x2, starting transfers between devices: 0.13 us -> 2.29 us  [whole_sequences(): lax.ppermute(pieces[k], both, [(host(i, j), owner(i, j, leaves_as(k, j)))...]
    ppermute x2, starting transfers between devices: 3.85 us -> 2.33 us  [whole_sequences(): lax.ppermute(latent[k], both, [(owner(i, j, first_back(i // COPIES, j) ^...]
    ppermute x2, waiting for transfers between devices: 0.74 us -> 2.19 us  [whole_sequences(): lax.ppermute(pieces[k], both, [(host(i, j), owner(i, j, leaves_as(k, j)))...]
    ppermute x3, waiting for transfers between devices: 3.53 us -> 2.47 us  [whole_sequences(): lax.ppermute(picked[k], 'seq', in_plane(lambda g, t: (g ^ partner(k, t))...]
    ppermute x3, starting transfers between devices: 1.81 us -> 0.81 us  [whole_sequences(): lax.ppermute(keys, 'seq', other_core)]
    ppermute x2, waiting for transfers between devices: 6.18 us -> 6.62 us  [whole_sequences(): lax.ppermute(latent[k], both, [(owner(i, j, first_back(i // COPIES, j) ^...]
  transfers between devices with their start and end apart: 11 -> 11, of which waited for: 7 -> 6; matrix products, arithmetic and copies ran while one was open for 0% -> 0% of each run, Pallas kernels for 6% -> 6%
where the time goes in v27:
time: 27 us; the launch traced here: 26.8 us
  waiting for transfers between devices  12.9 us (48%)
  starting transfers between devices  9.05 us (34%)
  Pallas kernels  4.75 us (18%)
    ppermute x2, waiting for transfers between devices, whole_sequences(): lax.ppermute(latent[k], both, [(owner(i, j, first_back(i // COPIES, j) ^...  6.62 us
    ppermute x3, starting transfers between devices, whole_sequences(): lax.ppermute(picked[k], 'seq', in_plane(lambda g, t: (g ^ partner(k, t))...  3.55 us
    ppermute x3, waiting for transfers between devices, whole_sequences(): lax.ppermute(picked[k], 'seq', in_plane(lambda g, t: (g ^ partner(k, t))...  2.47 us
    ppermute x2, starting transfers between devices, whole_sequences(): lax.ppermute(latent[k], both, [(owner(i, j, first_back(i // COPIES, j) ^...  2.33 us
    ppermute x2, starting transfers between devices, whole_sequences(): lax.ppermute(pieces[k], both, [(host(i, j), owner(i, j, leaves_as(k, j)))...  2.29 us
    ppermute x2, waiting for transfers between devices, whole_sequences(): lax.ppermute(pieces[k], both, [(host(i, j), owner(i, j, leaves_as(k, j)))...  2.19 us
    ppermute x1, waiting for transfers between devices, whole_sequences(): lax.ppermute(packed, both, [(flat(i, j), host(i, j)) for i, j in devices])  1.63 us
    pallas_call x1, Pallas kernels, whole_sequences(): pl.pallas_call(functools.partial(pick_kernel, per_device), out_shape=[jax...  1.38 us
  transfers between devices with their start and end apart: 11, of which 6 were waited for; matrix products, arithmetic and copies ran while one was open for 0% of the time, Pallas kernels for 6%

profile of v27, /device:TPU:6, one launch (start us, length us, event | category | flops | bytes accessed | tf_op | source)
XLA Modules:
  0.0 26.8 jit_solution(16657564064470848057)
XLA Ops:
  0.0 1.4 %shard_map.64 = (bf16[576,128]{1,0:T(8,128)(2,1)S(1)}, bf16[576,128]{1,0:T(8,128)(2,1)S(1)}, bf16[576,128]{1,0:T(8,128)(2,1)S(1)}, bf16[576,128]{1,0:T(8,128)(2,...) custom-call(bf16[4,576,128]{2,1,0:T(8,128)(2,1)} %bitcast.1, bf16[8,16,192]{2,1,0:T(8,128)(2,1)} %q_hbm.1, ...), custom_call_target="tpu_custom_call" | custom-call | flops 20000000000 | tf_op jit(solution)/shard_map/pallas_call | solution.py:245
  1.4 0.1 collective-permute-start
  1.5 2.0 %collective-permute-start.3 = (bf16[576,128]{1,0:T(8,128)(2,1)S(1)}, bf16[576,128]{1,0:T(8,128)(2,1)S(1)}, u32[]{:S(2)}, u32[]{:S(2)}) collective-permute-start(bf16[576,128]{1,0:T(8,128)(2,1)S(1)} %get-tuple-element.24), channel_id=1, source_target_pairs={{0,24},{4,28},{8,16},{12,20},{16,8},{20,12},{24,0},{28,4},{1,25},{... | collective-permute-start | bytes 442376 | tf_op jit(solution)/shard_map/ppermute | solution.py:265
  3.4 0.1 collective-permute-start.4
  3.5 1.5 %collective-permute-start.5 = (bf16[576,128]{1,0:T(8,128)(2,1)S(1)}, bf16[576,128]{1,0:T(8,128)(2,1)S(1)}, u32[]{:S(2)}, u32[]{:S(2)}) collective-permute-start(bf16[576,128]{1,0:T(8,128)(2,1)S(1)} %get-tuple-element.26), channel_id=1, source_target_pairs={{0,16},{4,12},{8,24},{12,4},{16,0},{20,28},{24,8},{28,20},{1,17},{... | collective-permute-start | bytes 442376 | tf_op jit(solution)/shard_map/ppermute | solution.py:265
  5.0 1.6 %collective-permute-done.packed_ref = bf16[128,256]{1,0:T(8,128)(2,1)S(1)} collective-permute-done((bf16[128,256]{1,0:T(8,128)(2,1)S(1)}, bf16[128,256]{1,0:T(8,128)(2,1)S(1)}, u32[]{:S(2)}, u32[]{:S(2)}) %collective-permute-start) | collective-permute-done | bytes 65568 | tf_op jit(solution)/shard_map/ppermute | solution.py:263
  6.7 0.5 %shard_map.65 = (bf16[64,640]{1,0:T(8,128)(2,1)S(1)}, bf16[64,640]{1,0:T(8,128)(2,1)S(1)}) custom-call(bf16[16,128,512]{2,1,0:T(8,128)(2,1)S(1)} %copy-done.1, bf16[128,256]{1,0:T(8,128)(2,1)S(1)} %collective-permute-done.packed_ref), custom_call_target="tpu_custom_call" | custom-call | flops 20000000000 | tf_op jit(solution)/shard_map/pallas_call | solution.py:279
  7.1 0.1 collective-permute-start.1
  7.2 2.2 %collective-permute-start.2 = (bf16[64,640]{1,0:T(8,128)(2,1)S(1)}, bf16[64,640]{1,0:T(8,128)(2,1)S(1)}, u32[]{:S(2)}, u32[]{:S(2)}) collective-permute-start(bf16[64,640]{1,0:T(8,128)(2,1)S(1)} %get-tuple-element.22), channel_id=1, source_target_pairs={{8,4},{5,12},{6,0},{11,8},{24,20},{21,28},{22,16},{27,24},{12,5},{... | collective-permute-start | bytes 245768 | tf_op jit(solution)/shard_map/ppermute | solution.py:288
  9.4 0.0 collective-permute-done.3.refs_3_.second_ref
  9.4 0.4 %shard_map.67 = bf16[2,576,128]{2,1,0:T(8,128)(2,1)S(1)} custom-call(bf16[576,128]{1,0:T(8,128)(2,1)S(1)} %get-tuple-element.23.refs_2_.first_ref, bf16[576,128]{1,0:T(8,128)(2,1)S(1)} %collective-permute-done.3.refs_3_.second_ref), custom_call_target="tpu_custom_call" | custom-call | tf_op jit(solution)/shard_map/pallas_call | solution.py:268
  9.8 0.3 %collective-permute-start.6 = (bf16[2,576,128]{2,1,0:T(8,128)(2,1)S(1)}, bf16[2,576,128]{2,1,0:T(8,128)(2,1)S(1)}, u32[]{:S(2)}, u32[]{:S(2)}) collective-permute-start(bf16[2,576,128]{2,1,0:T(8,128)(2,1)S(1)} %shard_map.67), channel_id=1, source_target_pairs={{0,4},{4,0},{8,12},{12,8},{16,20},{20,16},{24,28},{28,24},{1,5},{5... | collective-permute-start | bytes 884744 | tf_op jit(solution)/shard_map/ppermute | solution.py:277
  10.1 2.5 %collective-permute-done.4.refs_4_ = bf16[576,128]{1,0:T(8,128)(2,1)S(1)} collective-permute-done((bf16[576,128]{1,0:T(8,128)(2,1)S(1)}, bf16[576,128]{1,0:T(8,128)(2,1)S(1)}, u32[]{:S(2)}, u32[]{:S(2)}) %collective-permute-start.4) | collective-permute-done | bytes 147488 | tf_op jit(solution)/shard_map/ppermute | solution.py:265
  12.6 0.2 collective-permute-start.7
  12.8 0.0 collective-permute-done.5.refs_5_
  12.8 0.3 %collective-permute-start.8 = (bf16[576,128]{1,0:T(8,128)(2,1)S(1)}, bf16[576,128]{1,0:T(8,128)(2,1)S(1)}, u32[]{:S(2)}, u32[]{:S(2)}) collective-permute-start(bf16[576,128]{1,0:T(8,128)(2,1)S(1)} %collective-permute-done.5.refs_5_), channel_id=1, source_target_pairs={{0,4},{4,0},{8,12},{12,8},{16,20},{20,16},{24,28},{28,24},{1,5},{5... | collective-permute-start | bytes 442376 | tf_op jit(solution)/shard_map/ppermute | solution.py:277
  13.1 0.6 %collective-permute-done.1.refs_0_ = bf16[64,640]{1,0:T(8,128)(2,1)S(1)} collective-permute-done((bf16[64,640]{1,0:T(8,128)(2,1)S(1)}, bf16[64,640]{1,0:T(8,128)(2,1)S(1)}, u32[]{:S(2)}, u32[]{:S(2)}) %collective-permute-start.1) | collective-permute-done | bytes 81952 | tf_op jit(solution)/shard_map/ppermute | solution.py:288
  13.7 1.6 %collective-permute-done.2.refs_1_ = bf16[64,640]{1,0:T(8,128)(2,1)S(1)} collective-permute-done((bf16[64,640]{1,0:T(8,128)(2,1)S(1)}, bf16[64,640]{1,0:T(8,128)(2,1)S(1)}, u32[]{:S(2)}, u32[]{:S(2)}) %collective-permute-start.2) | collective-permute-done | bytes 81952 | tf_op jit(solution)/shard_map/ppermute | solution.py:288
  15.3 0.8 %shard_map.66 = (bf16[128,576]{1,0:T(8,128)(2,1)S(1)}, f32[128,128]{1,0:T(8,128)S(1)}, f32[128,128]{1,0:T(8,128)S(1)}, f32[128,512]{1,0:T(8,128)S(1)}) custom-call(s32[8,128]{1,0:T(8,128)S(1)} %get-tuple-element.19.limit_ref, bf16[64,640]{1,0:T(8,128)(2,1)S(1)} %collective-permute-done.1.refs_0_, bf16[64,640]{1,0:T(8,128)(2,1)S(1)} %collective-permute-done.2.refs_1_, ...), custom_call_target="tpu_custom_call" | custom-call | flops 20000000000 | tf_op jit(solution)/shard_map/pallas_call | solution.py:296
  16.1 0.7 %shard_map.68 = (bf16[64,512]{1,0:T(8,128)(2,1)S(1)}, bf16[64,512]{1,0:T(8,128)(2,1)S(1)}) custom-call(s32[8,128]{1,0:T(8,128)S(1)} %get-tuple-element.19.limit_ref, bf16[128,576]{1,0:T(8,128)(2,1)S(1)} %get-tuple-element.27.q_ref, f32[128,128]{1,0:T(8,128)S(1)} %get-tuple-element.28.top_ref, f32[128,128]{1,0:T(8,128)S(1)} %get-tuple-element.29.total_ref, ...), custom_call_target="tpu_custom_call" | custom-call | tf_op jit(solution)/shard_map/pallas_call | solution.py:309
  16.8 2.3 %collective-permute-start.10 = (bf16[64,512]{1,0:T(8,128)(2,1)S(1)}, bf16[64,512]{1,0:T(8,128)(2,1)S(1)}, u32[]{:S(2)}, u32[]{:S(2)}) collective-permute-start(bf16[64,512]{1,0:T(8,128)(2,1)S(1)} %get-tuple-element.32), channel_id=1, source_target_pairs={{4,0},{12,1},{0,2},{8,3},{20,4},{28,5},{16,6},{24,7},{5,8},{13,9},... | collective-permute-start | bytes 196616 | tf_op jit(solution)/shard_map/ppermute | solution.py:318
  19.1 5.4 %collective-permute-done.10.refs_1_ = bf16[64,512]{1,0:T(8,128)(2,1)S(1)} collective-permute-done((bf16[64,512]{1,0:T(8,128)(2,1)S(1)}, bf16[64,512]{1,0:T(8,128)(2,1)S(1)}, u32[]{:S(2)}, u32[]{:S(2)}) %collective-permute-start.10) | collective-permute-done | bytes 65568 | tf_op jit(solution)/shard_map/ppermute | solution.py:318
  24.6 1.2 %collective-permute-done.9.refs_0_ = bf16[64,512]{1,0:T(8,128)(2,1)S(1)} collective-permute-done((bf16[64,512]{1,0:T(8,128)(2,1)S(1)}, bf16[64,512]{1,0:T(8,128)(2,1)S(1)}, u32[]{:S(2)}, u32[]{:S(2)}) %collective-permute-start.9) | collective-permute-done | bytes 65568 | tf_op jit(solution)/shard_map/ppermute | solution.py:318
  25.8 1.1 %shard_map.69 = bf16[8,16,128]{2,1,0:T(8,128)(2,1)} custom-call(bf16[16,512,128]{2,1,0:T(8,128)(2,1)S(1)} %copy-done, bf16[64,512]{1,0:T(8,128)(2,1)S(1)} %collective-permute-done.9.refs_0_, bf16[64,512]{1,0:T(8,128)(2,1)S(1)} %collective-permute-done.10.refs_1_), custom_call_target="tpu_custom_call" | custom-call | tf_op jit(solution)/shard_map/pallas_call | solution.py:325
  (8 shorter events, 0.0 us)
Async XLA Ops:
  0.0 6.7 %copy-start.1 = (bf16[16,128,512]{2,1,0:T(8,128)(2,1)S(1)}, bf16[16,128,512]{2,1,0:T(8,128)(2,1)}, u32[]{:S(2)}) copy-start(bf16[16,128,512]{2,1,0:T(8,128)(2,1)} %w_ref.2) | copy-start | bytes 6291460
  1.4 5.3 %collective-permute-start = (bf16[128,256]{1,0:T(8,128)(2,1)S(1)}, bf16[128,256]{1,0:T(8,128)(2,1)S(1)}, u32[]{:S(2)}, u32[]{:S(2)}) collective-permute-start(bf16[128,256]{1,0:T(8,128)(2,1)S(1)} %get-tuple-element.20), channel_id=1, source_target_pairs={{0,8},{1,5},{2,6},{3,11},{4,24},{5,21},{6,22},{7,27},{8,12},{9,1},... | collective-permute-start | bytes 196616 | tf_op jit(solution)/shard_map/ppermute | solution.py:263
  1.5 8.0 %collective-permute-start.3 = (bf16[576,128]{1,0:T(8,128)(2,1)S(1)}, bf16[576,128]{1,0:T(8,128)(2,1)S(1)}, u32[]{:S(2)}, u32[]{:S(2)}) collective-permute-start(bf16[576,128]{1,0:T(8,128)(2,1)S(1)} %get-tuple-element.24), channel_id=1, source_target_pairs={{0,24},{4,28},{8,16},{12,20},{16,8},{20,12},{24,0},{28,4},{1,25},{... | collective-permute-start | bytes 442376 | tf_op jit(solution)/shard_map/ppermute | solution.py:265
  3.4 9.2 %collective-permute-start.4 = (bf16[576,128]{1,0:T(8,128)(2,1)S(1)}, bf16[576,128]{1,0:T(8,128)(2,1)S(1)}, u32[]{:S(2)}, u32[]{:S(2)}) collective-permute-start(bf16[576,128]{1,0:T(8,128)(2,1)S(1)} %get-tuple-element.25), channel_id=1, source_target_pairs={{0,8},{4,20},{8,0},{12,28},{16,24},{20,4},{24,16},{28,12},{1,9},{5... | collective-permute-start | bytes 442376 | tf_op jit(solution)/shard_map/ppermute | solution.py:265
  3.5 9.3 %collective-permute-start.5 = (bf16[576,128]{1,0:T(8,128)(2,1)S(1)}, bf16[576,128]{1,0:T(8,128)(2,1)S(1)}, u32[]{:S(2)}, u32[]{:S(2)}) collective-permute-start(bf16[576,128]{1,0:T(8,128)(2,1)S(1)} %get-tuple-element.26), channel_id=1, source_target_pairs={{0,16},{4,12},{8,24},{12,4},{16,0},{20,28},{24,8},{28,20},{1,17},{... | collective-permute-start | bytes 442376 | tf_op jit(solution)/shard_map/ppermute | solution.py:265
  7.1 6.5 %collective-permute-start.1 = (bf16[64,640]{1,0:T(8,128)(2,1)S(1)}, bf16[64,640]{1,0:T(8,128)(2,1)S(1)}, u32[]{:S(2)}, u32[]{:S(2)}) collective-permute-start(bf16[64,640]{1,0:T(8,128)(2,1)S(1)} %get-tuple-element.21), channel_id=1, source_target_pairs={{8,12},{5,4},{6,8},{11,0},{24,28},{21,20},{22,24},{27,16},{12,13},... | collective-permute-start | bytes 245768 | tf_op jit(solution)/shard_map/ppermute | solution.py:288
  7.2 8.1 %collective-permute-start.2 = (bf16[64,640]{1,0:T(8,128)(2,1)S(1)}, bf16[64,640]{1,0:T(8,128)(2,1)S(1)}, u32[]{:S(2)}, u32[]{:S(2)}) collective-permute-start(bf16[64,640]{1,0:T(8,128)(2,1)S(1)} %get-tuple-element.22), channel_id=1, source_target_pairs={{8,4},{5,12},{6,0},{11,8},{24,20},{21,28},{22,16},{27,24},{12,5},{... | collective-permute-start | bytes 245768 | tf_op jit(solution)/shard_map/ppermute | solution.py:288
  9.8 6.3 %collective-permute-start.6 = (bf16[2,576,128]{2,1,0:T(8,128)(2,1)S(1)}, bf16[2,576,128]{2,1,0:T(8,128)(2,1)S(1)}, u32[]{:S(2)}, u32[]{:S(2)}) collective-permute-start(bf16[2,576,128]{2,1,0:T(8,128)(2,1)S(1)} %shard_map.67), channel_id=1, source_target_pairs={{0,4},{4,0},{8,12},{12,8},{16,20},{20,16},{24,28},{28,24},{1,5},{5... | collective-permute-start | bytes 884744 | tf_op jit(solution)/shard_map/ppermute | solution.py:277
  12.6 3.5 %collective-permute-start.7 = (bf16[576,128]{1,0:T(8,128)(2,1)S(1)}, bf16[576,128]{1,0:T(8,128)(2,1)S(1)}, u32[]{:S(2)}, u32[]{:S(2)}) collective-permute-start(bf16[576,128]{1,0:T(8,128)(2,1)S(1)} %collective-permute-done.4.refs_4_), channel_id=1, source_target_pairs={{0,4},{4,0},{8,12},{12,8},{16,20},{20,16},{24,28},{28,24},{1,5},{5... | collective-permute-start | bytes 442376 | tf_op jit(solution)/shard_map/ppermute | solution.py:277
  12.8 3.3 %collective-permute-start.8 = (bf16[576,128]{1,0:T(8,128)(2,1)S(1)}, bf16[576,128]{1,0:T(8,128)(2,1)S(1)}, u32[]{:S(2)}, u32[]{:S(2)}) collective-permute-start(bf16[576,128]{1,0:T(8,128)(2,1)S(1)} %collective-permute-done.5.refs_5_), channel_id=1, source_target_pairs={{0,4},{4,0},{8,12},{12,8},{16,20},{20,16},{24,28},{28,24},{1,5},{5... | collective-permute-start | bytes 442376 | tf_op jit(solution)/shard_map/ppermute | solution.py:277
  15.3 10.5 %copy-start = (bf16[16,512,128]{2,1,0:T(8,128)(2,1)S(1)}, bf16[16,512,128]{2,1,0:T(8,128)(2,1)}, u32[]{:S(2)}) copy-start(bf16[16,512,128]{2,1,0:T(8,128)(2,1)} %w_ref.3) | copy-start | bytes 6291460
  16.8 7.8 %collective-permute-start.10 = (bf16[64,512]{1,0:T(8,128)(2,1)S(1)}, bf16[64,512]{1,0:T(8,128)(2,1)S(1)}, u32[]{:S(2)}, u32[]{:S(2)}) collective-permute-start(bf16[64,512]{1,0:T(8,128)(2,1)S(1)} %get-tuple-element.32), channel_id=1, source_target_pairs={{4,0},{12,1},{0,2},{8,3},{20,4},{28,5},{16,6},{24,7},{5,8},{13,9},... | collective-permute-start | bytes 196616 | tf_op jit(solution)/shard_map/ppermute | solution.py:318
  19.1 6.6 %collective-permute-start.9 = (bf16[64,512]{1,0:T(8,128)(2,1)S(1)}, bf16[64,512]{1,0:T(8,128)(2,1)S(1)}, u32[]{:S(2)}, u32[]{:S(2)}) collective-permute-start(bf16[64,512]{1,0:T(8,128)(2,1)S(1)} %get-tuple-element.31), channel_id=1, source_target_pairs={{12,0},{4,1},{8,2},{0,3},{28,4},{20,5},{24,6},{16,7},{13,8},{5,9},... | collective-permute-start | bytes 196616 | tf_op jit(solution)/shard_map/ppermute | solution.py:318

commit v28 on v15

--- a/solution.py
+++ b/solution.py
@@ -46,17 +46,19 @@
     blocks, (out_ref, limit_ref, q_ref, new_ref, len_ref, sem) = refs[:owners], refs[owners:]
     chip, core = lax.axis_index("seq") // COPIES, lax.axis_index("seq") % COPIES
     moves = [
-        pltpu.make_async_copy(q_hbm, q_ref, sem.at[owners]),
-        pltpu.make_async_copy(new_hbm, new_ref, sem.at[owners + 1]),
-        pltpu.make_async_copy(len_hbm, len_ref, sem.at[owners + 2]),
-    ] + [
         pltpu.make_async_copy(cache_hbm.at[chip ^ partner(k, core)], blocks[k], sem.at[k])
         for k in range(owners)
     ]
-    for move in moves:
+    small = [
+        pltpu.make_async_copy(source, target, sem.at[owners + n])
+        for n, (source, target) in enumerate(
+            ((q_hbm, q_ref), (new_hbm, new_ref), (len_hbm, len_ref))
+        )
+    ]
+    for move in moves + small:
         move.start()
-    moves[0].wait()
-    moves[1].wait()
+    small[0].wait()
+    small[1].wait()
     heads, width = q_ref.shape[1:]
     fresh = new_ref[...].astype(jnp.float32)
     piece = SPEC * heads
@@ -69,10 +71,10 @@
             parts.append(jnp.zeros((spare, ROPE), jnp.float32))
         own = jnp.concatenate(parts, axis=0).astype(rows.dtype)
         out_ref[a * piece : (a + 1) * piece] = jnp.concatenate([rows, own], axis=1)
-    moves[2].wait()
+    small[2].wait()
     length = len_ref[lax.axis_index("head") * owners + chip]
     limit_ref[...] = jnp.full(limit_ref.shape, length, limit_ref.dtype)
-    for move in moves[3:]:
+    for move in moves:
         move.wait()
 
 

time: 26.5 us -> 26.6 us (level)
  no operation moved by 1% of the time
where the time goes in v28:
time: 26.6 us; the launch traced here: 26.5 us
  waiting for transfers between devices  12.1 us (45%)
  starting transfers between devices  9.41 us (35%)
  Pallas kernels  4.88 us (18%)
    ppermute x2, waiting for transfers between devices, whole_sequences(): lax.ppermute(latent[k], both, [(owner(i, j, first_back(i // COPIES, j) ^...  6.18 us
    ppermute x2, starting transfers between devices, whole_sequences(): lax.ppermute(latent[k], both, [(owner(i, j, first_back(i // COPIES, j) ^...  3.86 us
    ppermute x3, starting transfers between devices, whole_sequences(): lax.ppermute(picked[k], 'seq', in_plane(lambda g, t: (g ^ partner(k, t))...  3.55 us
    ppermute x3, waiting for transfers between devices, whole_sequences(): lax.ppermute(picked[k], 'seq', in_plane(lambda g, t: (g ^ partner(k, t))...  3.53 us
    ppermute x3, starting transfers between devices, whole_sequences(): lax.ppermute(keys, 'seq', other_core)  1.81 us
    ppermute x1, waiting for transfers between devices, whole_sequences(): lax.ppermute(packed, both, [(flat(i, j), host(i, j)) for i, j in devices])  1.63 us
    pallas_call x1, Pallas kernels, whole_sequences(): pl.pallas_call(functools.partial(pick_kernel, per_device), out_shape=[jax...  1.5 us
    pallas_call x1, Pallas kernels, whole_sequences(): pl.pallas_call(functools.partial(project_kernel, per_device), out_shape=j...  1.07 us
  transfers between devices with their start and end apart: 11, of which 7 were waited for; matrix products, arithmetic and copies ran while one was open for 0% of the time, Pallas kernels for 6%

profile of v28, /device:TPU:6, one launch (start us, length us, event | category | flops | bytes accessed | tf_op | source)
XLA Modules:
  0.0 26.5 jit_solution(15646639392135962399)
XLA Ops:
  0.0 1.5 %shard_map.64 = (bf16[576,128]{1,0:T(8,128)(2,1)S(1)}, bf16[576,128]{1,0:T(8,128)(2,1)S(1)}, bf16[576,128]{1,0:T(8,128)(2,1)S(1)}, bf16[576,128]{1,0:T(8,128)(2,...) custom-call(bf16[4,576,128]{2,1,0:T(8,128)(2,1)} %bitcast.1, bf16[8,16,192]{2,1,0:T(8,128)(2,1)} %q_hbm.1, ...), custom_call_target="tpu_custom_call" | custom-call | flops 20000000000 | tf_op jit(solution)/shard_map/pallas_call | solution.py:247
  1.5 0.1 collective-permute-start
  1.6 2.0 %collective-permute-start.3 = (bf16[576,128]{1,0:T(8,128)(2,1)S(1)}, bf16[576,128]{1,0:T(8,128)(2,1)S(1)}, u32[]{:S(2)}, u32[]{:S(2)}) collective-permute-start(bf16[576,128]{1,0:T(8,128)(2,1)S(1)} %get-tuple-element.24), channel_id=1, source_target_pairs={{0,24},{4,28},{8,16},{12,20},{16,8},{20,12},{24,0},{28,4},{1,25},{... | collective-permute-start | bytes 442376 | tf_op jit(solution)/shard_map/ppermute | solution.py:267
  3.5 0.1 collective-permute-start.4
  3.6 1.5 %collective-permute-start.5 = (bf16[576,128]{1,0:T(8,128)(2,1)S(1)}, bf16[576,128]{1,0:T(8,128)(2,1)S(1)}, u32[]{:S(2)}, u32[]{:S(2)}) collective-permute-start(bf16[576,128]{1,0:T(8,128)(2,1)S(1)} %get-tuple-element.26), channel_id=1, source_target_pairs={{0,16},{4,12},{8,24},{12,4},{16,0},{20,28},{24,8},{28,20},{1,17},{... | collective-permute-start | bytes 442376 | tf_op jit(solution)/shard_map/ppermute | solution.py:267
  5.1 1.6 %collective-permute-done.packed_ref = bf16[128,256]{1,0:T(8,128)(2,1)S(1)} collective-permute-done((bf16[128,256]{1,0:T(8,128)(2,1)S(1)}, bf16[128,256]{1,0:T(8,128)(2,1)S(1)}, u32[]{:S(2)}, u32[]{:S(2)}) %collective-permute-start) | collective-permute-done | bytes 65568 | tf_op jit(solution)/shard_map/ppermute | solution.py:265
  6.8 0.5 %shard_map.65 = (bf16[64,640]{1,0:T(8,128)(2,1)S(1)}, bf16[64,640]{1,0:T(8,128)(2,1)S(1)}) custom-call(bf16[16,128,512]{2,1,0:T(8,128)(2,1)S(1)} %copy-done.1, bf16[128,256]{1,0:T(8,128)(2,1)S(1)} %collective-permute-done.packed_ref), custom_call_target="tpu_custom_call" | custom-call | flops 20000000000 | tf_op jit(solution)/shard_map/pallas_call | solution.py:281
  7.3 0.1 collective-permute-start.1
  7.3 0.1 collective-permute-start.2
  7.4 2.0 %collective-permute-done.3.refs_3_.second_ref = bf16[576,128]{1,0:T(8,128)(2,1)S(1)} collective-permute-done((bf16[576,128]{1,0:T(8,128)(2,1)S(1)}, bf16[576,128]{1,0:T(8,128)(2,1)S(1)}, u32[]{:S(2)}, u32[]{:S(2)}) %collective-permute-start.3) | collective-permute-done | bytes 147488 | tf_op jit(solution)/shard_map/ppermute | solution.py:267
  9.4 0.4 %shard_map.67 = bf16[2,576,128]{2,1,0:T(8,128)(2,1)S(1)} custom-call(bf16[576,128]{1,0:T(8,128)(2,1)S(1)} %get-tuple-element.23.refs_2_.first_ref, bf16[576,128]{1,0:T(8,128)(2,1)S(1)} %collective-permute-done.3.refs_3_.second_ref), custom_call_target="tpu_custom_call" | custom-call | tf_op jit(solution)/shard_map/pallas_call | solution.py:270
  9.8 1.3 %collective-permute-start.6 = (bf16[2,576,128]{2,1,0:T(8,128)(2,1)S(1)}, bf16[2,576,128]{2,1,0:T(8,128)(2,1)S(1)}, u32[]{:S(2)}, u32[]{:S(2)}) collective-permute-start(bf16[2,576,128]{2,1,0:T(8,128)(2,1)S(1)} %shard_map.67), channel_id=1, source_target_pairs={{0,4},{4,0},{8,12},{12,8},{16,20},{20,16},{24,28},{28,24},{1,5},{5... | collective-permute-start | bytes 884744 | tf_op jit(solution)/shard_map/ppermute | solution.py:279
  11.1 1.5 %collective-permute-done.4.refs_4_ = bf16[576,128]{1,0:T(8,128)(2,1)S(1)} collective-permute-done((bf16[576,128]{1,0:T(8,128)(2,1)S(1)}, bf16[576,128]{1,0:T(8,128)(2,1)S(1)}, u32[]{:S(2)}, u32[]{:S(2)}) %collective-permute-start.4) | collective-permute-done | bytes 147488 | tf_op jit(solution)/shard_map/ppermute | solution.py:267
  12.6 0.3 %collective-permute-start.7 = (bf16[576,128]{1,0:T(8,128)(2,1)S(1)}, bf16[576,128]{1,0:T(8,128)(2,1)S(1)}, u32[]{:S(2)}, u32[]{:S(2)}) collective-permute-start(bf16[576,128]{1,0:T(8,128)(2,1)S(1)} %collective-permute-done.4.refs_4_), channel_id=1, source_target_pairs={{0,4},{4,0},{8,12},{12,8},{16,20},{20,16},{24,28},{28,24},{1,5},{5... | collective-permute-start | bytes 442376 | tf_op jit(solution)/shard_map/ppermute | solution.py:279
  12.9 0.2 collective-permute-start.8
  13.1 0.6 %collective-permute-done.1.refs_0_ = bf16[64,640]{1,0:T(8,128)(2,1)S(1)} collective-permute-done((bf16[64,640]{1,0:T(8,128)(2,1)S(1)}, bf16[64,640]{1,0:T(8,128)(2,1)S(1)}, u32[]{:S(2)}, u32[]{:S(2)}) %collective-permute-start.1) | collective-permute-done | bytes 81952 | tf_op jit(solution)/shard_map/ppermute | solution.py:290
  13.7 0.1 collective-permute-done.2.refs_1_
  13.9 0.8 %shard_map.66 = (bf16[128,576]{1,0:T(8,128)(2,1)S(1)}, f32[128,128]{1,0:T(8,128)S(1)}, f32[128,128]{1,0:T(8,128)S(1)}, f32[128,512]{1,0:T(8,128)S(1)}) custom-call(s32[8,128]{1,0:T(8,128)S(1)} %get-tuple-element.19.limit_ref, bf16[64,640]{1,0:T(8,128)(2,1)S(1)} %collective-permute-done.1.refs_0_, bf16[64,640]{1,0:T(8,128)(2,1)S(1)} %collective-permute-done.2.refs_1_, ...), custom_call_target="tpu_custom_call" | custom-call | flops 20000000000 | tf_op jit(solution)/shard_map/pallas_call | solution.py:298
  14.7 0.7 %shard_map.68 = (bf16[64,512]{1,0:T(8,128)(2,1)S(1)}, bf16[64,512]{1,0:T(8,128)(2,1)S(1)}) custom-call(s32[8,128]{1,0:T(8,128)S(1)} %get-tuple-element.19.limit_ref, bf16[128,576]{1,0:T(8,128)(2,1)S(1)} %get-tuple-element.27.q_ref, f32[128,128]{1,0:T(8,128)S(1)} %get-tuple-element.28.top_ref, f32[128,128]{1,0:T(8,128)S(1)} %get-tuple-element.29.total_ref, ...), custom_call_target="tpu_custom_call" | custom-call | tf_op jit(solution)/shard_map/pallas_call | solution.py:311
  15.4 3.4 %collective-permute-start.10 = (bf16[64,512]{1,0:T(8,128)(2,1)S(1)}, bf16[64,512]{1,0:T(8,128)(2,1)S(1)}, u32[]{:S(2)}, u32[]{:S(2)}) collective-permute-start(bf16[64,512]{1,0:T(8,128)(2,1)S(1)} %get-tuple-element.32), channel_id=1, source_target_pairs={{4,0},{12,1},{0,2},{8,3},{20,4},{28,5},{16,6},{24,7},{5,8},{13,9},... | collective-permute-start | bytes 196616 | tf_op jit(solution)/shard_map/ppermute | solution.py:320
  18.8 0.4 %collective-permute-start.9 = (bf16[64,512]{1,0:T(8,128)(2,1)S(1)}, bf16[64,512]{1,0:T(8,128)(2,1)S(1)}, u32[]{:S(2)}, u32[]{:S(2)}) collective-permute-start(bf16[64,512]{1,0:T(8,128)(2,1)S(1)} %get-tuple-element.31), channel_id=1, source_target_pairs={{12,0},{4,1},{8,2},{0,3},{28,4},{20,5},{24,6},{16,7},{13,8},{5,9},... | collective-permute-start | bytes 196616 | tf_op jit(solution)/shard_map/ppermute | solution.py:320
  19.2 3.8 %collective-permute-done.10.refs_1_ = bf16[64,512]{1,0:T(8,128)(2,1)S(1)} collective-permute-done((bf16[64,512]{1,0:T(8,128)(2,1)S(1)}, bf16[64,512]{1,0:T(8,128)(2,1)S(1)}, u32[]{:S(2)}, u32[]{:S(2)}) %collective-permute-start.10) | collective-permute-done | bytes 65568 | tf_op jit(solution)/shard_map/ppermute | solution.py:320
  23.1 2.4 %collective-permute-done.9.refs_0_ = bf16[64,512]{1,0:T(8,128)(2,1)S(1)} collective-permute-done((bf16[64,512]{1,0:T(8,128)(2,1)S(1)}, bf16[64,512]{1,0:T(8,128)(2,1)S(1)}, u32[]{:S(2)}, u32[]{:S(2)}) %collective-permute-start.9) | collective-permute-done | bytes 65568 | tf_op jit(solution)/shard_map/ppermute | solution.py:320
  25.4 1.1 %shard_map.69 = bf16[8,16,128]{2,1,0:T(8,128)(2,1)} custom-call(bf16[16,512,128]{2,1,0:T(8,128)(2,1)S(1)} %copy-done, bf16[64,512]{1,0:T(8,128)(2,1)S(1)} %collective-permute-done.9.refs_0_, bf16[64,512]{1,0:T(8,128)(2,1)S(1)} %collective-permute-done.10.refs_1_), custom_call_target="tpu_custom_call" | custom-call | tf_op jit(solution)/shard_map/pallas_call | solution.py:327
  (8 shorter events, 0.0 us)
Async XLA Ops:
  0.0 6.8 %copy-start.1 = (bf16[16,128,512]{2,1,0:T(8,128)(2,1)S(1)}, bf16[16,128,512]{2,1,0:T(8,128)(2,1)}, u32[]{:S(2)}) copy-start(bf16[16,128,512]{2,1,0:T(8,128)(2,1)} %w_ref.2) | copy-start | bytes 6291460
  1.5 5.3 %collective-permute-start = (bf16[128,256]{1,0:T(8,128)(2,1)S(1)}, bf16[128,256]{1,0:T(8,128)(2,1)S(1)}, u32[]{:S(2)}, u32[]{:S(2)}) collective-permute-start(bf16[128,256]{1,0:T(8,128)(2,1)S(1)} %get-tuple-element.20), channel_id=1, source_target_pairs={{0,8},{1,5},{2,6},{3,11},{4,24},{5,21},{6,22},{7,27},{8,12},{9,1},... | collective-permute-start | bytes 196616 | tf_op jit(solution)/shard_map/ppermute | solution.py:265
  1.6 7.9 %collective-permute-start.3 = (bf16[576,128]{1,0:T(8,128)(2,1)S(1)}, bf16[576,128]{1,0:T(8,128)(2,1)S(1)}, u32[]{:S(2)}, u32[]{:S(2)}) collective-permute-start(bf16[576,128]{1,0:T(8,128)(2,1)S(1)} %get-tuple-element.24), channel_id=1, source_target_pairs={{0,24},{4,28},{8,16},{12,20},{16,8},{20,12},{24,0},{28,4},{1,25},{... | collective-permute-start | bytes 442376 | tf_op jit(solution)/shard_map/ppermute | solution.py:267
  3.5 9.1 %collective-permute-start.4 = (bf16[576,128]{1,0:T(8,128)(2,1)S(1)}, bf16[576,128]{1,0:T(8,128)(2,1)S(1)}, u32[]{:S(2)}, u32[]{:S(2)}) collective-permute-start(bf16[576,128]{1,0:T(8,128)(2,1)S(1)} %get-tuple-element.25), channel_id=1, source_target_pairs={{0,8},{4,20},{8,0},{12,28},{16,24},{20,4},{24,16},{28,12},{1,9},{5... | collective-permute-start | bytes 442376 | tf_op jit(solution)/shard_map/ppermute | solution.py:267
  3.6 9.3 %collective-permute-start.5 = (bf16[576,128]{1,0:T(8,128)(2,1)S(1)}, bf16[576,128]{1,0:T(8,128)(2,1)S(1)}, u32[]{:S(2)}, u32[]{:S(2)}) collective-permute-start(bf16[576,128]{1,0:T(8,128)(2,1)S(1)} %get-tuple-element.26), channel_id=1, source_target_pairs={{0,16},{4,12},{8,24},{12,4},{16,0},{20,28},{24,8},{28,20},{1,17},{... | collective-permute-start | bytes 442376 | tf_op jit(solution)/shard_map/ppermute | solution.py:267
  7.3 6.5 %collective-permute-start.1 = (bf16[64,640]{1,0:T(8,128)(2,1)S(1)}, bf16[64,640]{1,0:T(8,128)(2,1)S(1)}, u32[]{:S(2)}, u32[]{:S(2)}) collective-permute-start(bf16[64,640]{1,0:T(8,128)(2,1)S(1)} %get-tuple-element.21), channel_id=1, source_target_pairs={{8,4},{5,12},{6,0},{11,8},{24,20},{21,28},{22,16},{27,24},{12,5},{... | collective-permute-start | bytes 245768 | tf_op jit(solution)/shard_map/ppermute | solution.py:290
  7.3 6.5 %collective-permute-start.2 = (bf16[64,640]{1,0:T(8,128)(2,1)S(1)}, bf16[64,640]{1,0:T(8,128)(2,1)S(1)}, u32[]{:S(2)}, u32[]{:S(2)}) collective-permute-start(bf16[64,640]{1,0:T(8,128)(2,1)S(1)} %get-tuple-element.22), channel_id=1, source_target_pairs={{8,12},{5,4},{6,8},{11,0},{24,28},{21,20},{22,24},{27,16},{12,13},... | collective-permute-start | bytes 245768 | tf_op jit(solution)/shard_map/ppermute | solution.py:290
  9.8 4.8 %collective-permute-start.6 = (bf16[2,576,128]{2,1,0:T(8,128)(2,1)S(1)}, bf16[2,576,128]{2,1,0:T(8,128)(2,1)S(1)}, u32[]{:S(2)}, u32[]{:S(2)}) collective-permute-start(bf16[2,576,128]{2,1,0:T(8,128)(2,1)S(1)} %shard_map.67), channel_id=1, source_target_pairs={{0,4},{4,0},{8,12},{12,8},{16,20},{20,16},{24,28},{28,24},{1,5},{5... | collective-permute-start | bytes 884744 | tf_op jit(solution)/shard_map/ppermute | solution.py:279
  12.6 2.0 %collective-permute-start.7 = (bf16[576,128]{1,0:T(8,128)(2,1)S(1)}, bf16[576,128]{1,0:T(8,128)(2,1)S(1)}, u32[]{:S(2)}, u32[]{:S(2)}) collective-permute-start(bf16[576,128]{1,0:T(8,128)(2,1)S(1)} %collective-permute-done.4.refs_4_), channel_id=1, source_target_pairs={{0,4},{4,0},{8,12},{12,8},{16,20},{20,16},{24,28},{28,24},{1,5},{5... | collective-permute-start | bytes 442376 | tf_op jit(solution)/shard_map/ppermute | solution.py:279
  12.9 1.7 %collective-permute-start.8 = (bf16[576,128]{1,0:T(8,128)(2,1)S(1)}, bf16[576,128]{1,0:T(8,128)(2,1)S(1)}, u32[]{:S(2)}, u32[]{:S(2)}) collective-permute-start(bf16[576,128]{1,0:T(8,128)(2,1)S(1)} %collective-permute-done.5.refs_5_), channel_id=1, source_target_pairs={{0,4},{4,0},{8,12},{12,8},{16,20},{20,16},{24,28},{28,24},{1,5},{5... | collective-permute-start | bytes 442376 | tf_op jit(solution)/shard_map/ppermute | solution.py:279
  13.9 11.6 %copy-start = (bf16[16,512,128]{2,1,0:T(8,128)(2,1)S(1)}, bf16[16,512,128]{2,1,0:T(8,128)(2,1)}, u32[]{:S(2)}) copy-start(bf16[16,512,128]{2,1,0:T(8,128)(2,1)} %w_ref.3) | copy-start | bytes 6291460
  15.4 7.7 %collective-permute-start.10 = (bf16[64,512]{1,0:T(8,128)(2,1)S(1)}, bf16[64,512]{1,0:T(8,128)(2,1)S(1)}, u32[]{:S(2)}, u32[]{:S(2)}) collective-permute-start(bf16[64,512]{1,0:T(8,128)(2,1)S(1)} %get-tuple-element.32), channel_id=1, source_target_pairs={{4,0},{12,1},{0,2},{8,3},{20,4},{28,5},{16,6},{24,7},{5,8},{13,9},... | collective-permute-start | bytes 196616 | tf_op jit(solution)/shard_map/ppermute | solution.py:320
  18.8 6.6 %collective-permute-start.9 = (bf16[64,512]{1,0:T(8,128)(2,1)S(1)}, bf16[64,512]{1,0:T(8,128)(2,1)S(1)}, u32[]{:S(2)}, u32[]{:S(2)}) collective-permute-start(bf16[64,512]{1,0:T(8,128)(2,1)S(1)} %get-tuple-element.31), channel_id=1, source_target_pairs={{12,0},{4,1},{8,2},{0,3},{28,4},{20,5},{24,6},{16,7},{13,8},{5,9},... | collective-permute-start | bytes 196616 | tf_op jit(solution)/shard_map/ppermute | solution.py:320

commit v29 on v15

--- a/solution.py
+++ b/solution.py
@@ -13,6 +13,7 @@
 SPEC = 4
 SCORE_SCALE = (NOPE + ROPE) ** (-0.5)
 COPIES = 2
+COPY_PARTS = 3
 VMEM_LIMIT = 16 * 1024 * 1024
 LONG = pl.CostEstimate(flops=2 * 10**10, bytes_accessed=0, transcendentals=0)
 
@@ -46,13 +47,21 @@
     blocks, (out_ref, limit_ref, q_ref, new_ref, len_ref, sem) = refs[:owners], refs[owners:]
     chip, core = lax.axis_index("seq") // COPIES, lax.axis_index("seq") % COPIES
     moves = [
-        pltpu.make_async_copy(q_hbm, q_ref, sem.at[owners]),
-        pltpu.make_async_copy(new_hbm, new_ref, sem.at[owners + 1]),
-        pltpu.make_async_copy(len_hbm, len_ref, sem.at[owners + 2]),
-    ] + [
-        pltpu.make_async_copy(cache_hbm.at[chip ^ partner(k, core)], blocks[k], sem.at[k])
-        for k in range(owners)
+        pltpu.make_async_copy(q_hbm, q_ref, sem.at[0]),
+        pltpu.make_async_copy(new_hbm, new_ref, sem.at[1]),
+        pltpu.make_async_copy(len_hbm, len_ref, sem.at[2]),
     ]
+    part = cache_hbm.shape[1] // COPY_PARTS
+    for k in range(owners):
+        for n in range(COPY_PARTS):
+            rows = pl.ds(n * part, part)
+            moves.append(
+                pltpu.make_async_copy(
+                    cache_hbm.at[chip ^ partner(k, core), rows],
+                    blocks[k].at[rows],
+                    sem.at[3 + k * COPY_PARTS + n],
+                )
+            )
     for move in moves:
         move.start()
     moves[0].wait()
@@ -255,7 +264,7 @@
             pltpu.VMEM(queries.shape, queries.dtype),
             pltpu.VMEM(new_latent.shape, new_latent.dtype),
             pltpu.SMEM(lengths.shape, lengths.dtype),
-            pltpu.SemaphoreType.DMA((owners + 3,)),
+            pltpu.SemaphoreType.DMA((3 + owners * COPY_PARTS,)),
         ],
         compiler_params=params,
         cost_estimate=LONG,
@@ -438,6 +447,7 @@
         and rows % SPEC == 0
         and seq_size == COPIES * owners
         and head_size == owners == 4
+        and cache.shape[2] % (16 * COPY_PARTS) == 0
     ):
         return whole_sequences(
             seq_size, head_size, queries, new_latent, cache, lengths, w_uk, w_uv

time: 26.5 us -> 26.5 us (level)
  no operation moved by 1% of the time
where the time goes in v29:
time: 26.5 us; the launch traced here: 26.4 us
  waiting for transfers between devices  12.1 us (46%)
  starting transfers between devices  9.42 us (36%)
  Pallas kernels  4.74 us (18%)
    ppermute x2, waiting for transfers between devices, whole_sequences(): lax.ppermute(latent[k], both, [(owner(i, j, first_back(i // COPIES, j) ^...  6.18 us
    ppermute x2, starting transfers between devices, whole_sequences(): lax.ppermute(latent[k], both, [(owner(i, j, first_back(i // COPIES, j) ^...  3.86 us
    ppermute x3, starting transfers between devices, whole_sequences(): lax.ppermute(picked[k], 'seq', in_plane(lambda g, t: (g ^ partner(k, t))...  3.55 us
    ppermute x3, waiting for transfers between devices, whole_sequences(): lax.ppermute(picked[k], 'seq', in_plane(lambda g, t: (g ^ partner(k, t))...  3.54 us
    ppermute x3, starting transfers between devices, whole_sequences(): lax.ppermute(keys, 'seq', other_core)  1.81 us
    ppermute x1, waiting for transfers between devices, whole_sequences(): lax.ppermute(packed, both, [(flat(i, j), host(i, j)) for i, j in devices])  1.63 us
    pallas_call x1, Pallas kernels, whole_sequences(): pl.pallas_call(functools.partial(pick_kernel, per_device), out_shape=[jax...  1.37 us
    pallas_call x1, Pallas kernels, whole_sequences(): pl.pallas_call(functools.partial(project_kernel, per_device), out_shape=j...  1.06 us
  transfers between devices with their start and end apart: 11, of which 7 were waited for; matrix products, arithmetic and copies ran while one was open for 0% of the time, Pallas kernels for 6%

profile of v29, /device:TPU:6, one launch (start us, length us, event | category | flops | bytes accessed | tf_op | source)
XLA Modules:
  0.0 26.4 jit_solution(18172883074837377250)
XLA Ops:
  0.0 1.4 %shard_map.64 = (bf16[576,128]{1,0:T(8,128)(2,1)S(1)}, bf16[576,128]{1,0:T(8,128)(2,1)S(1)}, bf16[576,128]{1,0:T(8,128)(2,1)S(1)}, bf16[576,128]{1,0:T(8,128)(2,...) custom-call(bf16[4,576,128]{2,1,0:T(8,128)(2,1)} %bitcast.1, bf16[8,16,192]{2,1,0:T(8,128)(2,1)} %q_hbm.1, ...), custom_call_target="tpu_custom_call" | custom-call | flops 20000000000 | tf_op jit(solution)/shard_map/pallas_call | solution.py:254
  1.4 0.1 collective-permute-start
  1.5 2.0 %collective-permute-start.3 = (bf16[576,128]{1,0:T(8,128)(2,1)S(1)}, bf16[576,128]{1,0:T(8,128)(2,1)S(1)}, u32[]{:S(2)}, u32[]{:S(2)}) collective-permute-start(bf16[576,128]{1,0:T(8,128)(2,1)S(1)} %get-tuple-element.24), channel_id=1, source_target_pairs={{0,24},{4,28},{8,16},{12,20},{16,8},{20,12},{24,0},{28,4},{1,25},{... | collective-permute-start | bytes 442376 | tf_op jit(solution)/shard_map/ppermute | solution.py:274
  3.4 0.1 collective-permute-start.4
  3.5 1.5 %collective-permute-start.5 = (bf16[576,128]{1,0:T(8,128)(2,1)S(1)}, bf16[576,128]{1,0:T(8,128)(2,1)S(1)}, u32[]{:S(2)}, u32[]{:S(2)}) collective-permute-start(bf16[576,128]{1,0:T(8,128)(2,1)S(1)} %get-tuple-element.26), channel_id=1, source_target_pairs={{0,16},{4,12},{8,24},{12,4},{16,0},{20,28},{24,8},{28,20},{1,17},{... | collective-permute-start | bytes 442376 | tf_op jit(solution)/shard_map/ppermute | solution.py:274
  5.0 1.6 %collective-permute-done.packed_ref = bf16[128,256]{1,0:T(8,128)(2,1)S(1)} collective-permute-done((bf16[128,256]{1,0:T(8,128)(2,1)S(1)}, bf16[128,256]{1,0:T(8,128)(2,1)S(1)}, u32[]{:S(2)}, u32[]{:S(2)}) %collective-permute-start) | collective-permute-done | bytes 65568 | tf_op jit(solution)/shard_map/ppermute | solution.py:272
  6.6 0.5 %shard_map.65 = (bf16[64,640]{1,0:T(8,128)(2,1)S(1)}, bf16[64,640]{1,0:T(8,128)(2,1)S(1)}) custom-call(bf16[16,128,512]{2,1,0:T(8,128)(2,1)S(1)} %copy-done.1, bf16[128,256]{1,0:T(8,128)(2,1)S(1)} %collective-permute-done.packed_ref), custom_call_target="tpu_custom_call" | custom-call | flops 20000000000 | tf_op jit(solution)/shard_map/pallas_call | solution.py:288
  7.1 0.1 collective-permute-start.1
  7.2 0.1 collective-permute-start.2
  7.3 2.0 %collective-permute-done.3.refs_3_.second_ref = bf16[576,128]{1,0:T(8,128)(2,1)S(1)} collective-permute-done((bf16[576,128]{1,0:T(8,128)(2,1)S(1)}, bf16[576,128]{1,0:T(8,128)(2,1)S(1)}, u32[]{:S(2)}, u32[]{:S(2)}) %collective-permute-start.3) | collective-permute-done | bytes 147488 | tf_op jit(solution)/shard_map/ppermute | solution.py:274
  9.3 0.4 %shard_map.67 = bf16[2,576,128]{2,1,0:T(8,128)(2,1)S(1)} custom-call(bf16[576,128]{1,0:T(8,128)(2,1)S(1)} %get-tuple-element.23.refs_2_.first_ref, bf16[576,128]{1,0:T(8,128)(2,1)S(1)} %collective-permute-done.3.refs_3_.second_ref), custom_call_target="tpu_custom_call" | custom-call | tf_op jit(solution)/shard_map/pallas_call | solution.py:277
  9.7 1.3 %collective-permute-start.6 = (bf16[2,576,128]{2,1,0:T(8,128)(2,1)S(1)}, bf16[2,576,128]{2,1,0:T(8,128)(2,1)S(1)}, u32[]{:S(2)}, u32[]{:S(2)}) collective-permute-start(bf16[2,576,128]{2,1,0:T(8,128)(2,1)S(1)} %shard_map.67), channel_id=1, source_target_pairs={{0,4},{4,0},{8,12},{12,8},{16,20},{20,16},{24,28},{28,24},{1,5},{5... | collective-permute-start | bytes 884744 | tf_op jit(solution)/shard_map/ppermute | solution.py:286
  11.0 1.5 %collective-permute-done.4.refs_4_ = bf16[576,128]{1,0:T(8,128)(2,1)S(1)} collective-permute-done((bf16[576,128]{1,0:T(8,128)(2,1)S(1)}, bf16[576,128]{1,0:T(8,128)(2,1)S(1)}, u32[]{:S(2)}, u32[]{:S(2)}) %collective-permute-start.4) | collective-permute-done | bytes 147488 | tf_op jit(solution)/shard_map/ppermute | solution.py:274
  12.5 0.3 %collective-permute-start.7 = (bf16[576,128]{1,0:T(8,128)(2,1)S(1)}, bf16[576,128]{1,0:T(8,128)(2,1)S(1)}, u32[]{:S(2)}, u32[]{:S(2)}) collective-permute-start(bf16[576,128]{1,0:T(8,128)(2,1)S(1)} %collective-permute-done.4.refs_4_), channel_id=1, source_target_pairs={{0,4},{4,0},{8,12},{12,8},{16,20},{20,16},{24,28},{28,24},{1,5},{5... | collective-permute-start | bytes 442376 | tf_op jit(solution)/shard_map/ppermute | solution.py:286
  12.8 0.2 collective-permute-start.8
  13.0 0.6 %collective-permute-done.1.refs_0_ = bf16[64,640]{1,0:T(8,128)(2,1)S(1)} collective-permute-done((bf16[64,640]{1,0:T(8,128)(2,1)S(1)}, bf16[64,640]{1,0:T(8,128)(2,1)S(1)}, u32[]{:S(2)}, u32[]{:S(2)}) %collective-permute-start.1) | collective-permute-done | bytes 81952 | tf_op jit(solution)/shard_map/ppermute | solution.py:297
  13.6 0.1 collective-permute-done.2.refs_1_
  13.7 0.8 %shard_map.66 = (bf16[128,576]{1,0:T(8,128)(2,1)S(1)}, f32[128,128]{1,0:T(8,128)S(1)}, f32[128,128]{1,0:T(8,128)S(1)}, f32[128,512]{1,0:T(8,128)S(1)}) custom-call(s32[8,128]{1,0:T(8,128)S(1)} %get-tuple-element.19.limit_ref, bf16[64,640]{1,0:T(8,128)(2,1)S(1)} %collective-permute-done.1.refs_0_, bf16[64,640]{1,0:T(8,128)(2,1)S(1)} %collective-permute-done.2.refs_1_, ...), custom_call_target="tpu_custom_call" | custom-call | flops 20000000000 | tf_op jit(solution)/shard_map/pallas_call | solution.py:305
  14.5 0.7 %shard_map.68 = (bf16[64,512]{1,0:T(8,128)(2,1)S(1)}, bf16[64,512]{1,0:T(8,128)(2,1)S(1)}) custom-call(s32[8,128]{1,0:T(8,128)S(1)} %get-tuple-element.19.limit_ref, bf16[128,576]{1,0:T(8,128)(2,1)S(1)} %get-tuple-element.27.q_ref, f32[128,128]{1,0:T(8,128)S(1)} %get-tuple-element.28.top_ref, f32[128,128]{1,0:T(8,128)S(1)} %get-tuple-element.29.total_ref, ...), custom_call_target="tpu_custom_call" | custom-call | tf_op jit(solution)/shard_map/pallas_call | solution.py:318
  15.2 3.4 %collective-permute-start.10 = (bf16[64,512]{1,0:T(8,128)(2,1)S(1)}, bf16[64,512]{1,0:T(8,128)(2,1)S(1)}, u32[]{:S(2)}, u32[]{:S(2)}) collective-permute-start(bf16[64,512]{1,0:T(8,128)(2,1)S(1)} %get-tuple-element.32), channel_id=1, source_target_pairs={{4,0},{12,1},{0,2},{8,3},{20,4},{28,5},{16,6},{24,7},{5,8},{13,9},... | collective-permute-start | bytes 196616 | tf_op jit(solution)/shard_map/ppermute | solution.py:327
  18.7 0.4 %collective-permute-start.9 = (bf16[64,512]{1,0:T(8,128)(2,1)S(1)}, bf16[64,512]{1,0:T(8,128)(2,1)S(1)}, u32[]{:S(2)}, u32[]{:S(2)}) collective-permute-start(bf16[64,512]{1,0:T(8,128)(2,1)S(1)} %get-tuple-element.31), channel_id=1, source_target_pairs={{12,0},{4,1},{8,2},{0,3},{28,4},{20,5},{24,6},{16,7},{13,8},{5,9},... | collective-permute-start | bytes 196616 | tf_op jit(solution)/shard_map/ppermute | solution.py:327
  19.1 3.8 %collective-permute-done.10.refs_1_ = bf16[64,512]{1,0:T(8,128)(2,1)S(1)} collective-permute-done((bf16[64,512]{1,0:T(8,128)(2,1)S(1)}, bf16[64,512]{1,0:T(8,128)(2,1)S(1)}, u32[]{:S(2)}, u32[]{:S(2)}) %collective-permute-start.10) | collective-permute-done | bytes 65568 | tf_op jit(solution)/shard_map/ppermute | solution.py:327
  22.9 2.4 %collective-permute-done.9.refs_0_ = bf16[64,512]{1,0:T(8,128)(2,1)S(1)} collective-permute-done((bf16[64,512]{1,0:T(8,128)(2,1)S(1)}, bf16[64,512]{1,0:T(8,128)(2,1)S(1)}, u32[]{:S(2)}, u32[]{:S(2)}) %collective-permute-start.9) | collective-permute-done | bytes 65568 | tf_op jit(solution)/shard_map/ppermute | solution.py:327
  25.3 1.1 %shard_map.69 = bf16[8,16,128]{2,1,0:T(8,128)(2,1)} custom-call(bf16[16,512,128]{2,1,0:T(8,128)(2,1)S(1)} %copy-done, bf16[64,512]{1,0:T(8,128)(2,1)S(1)} %collective-permute-done.9.refs_0_, bf16[64,512]{1,0:T(8,128)(2,1)S(1)} %collective-permute-done.10.refs_1_), custom_call_target="tpu_custom_call" | custom-call | tf_op jit(solution)/shard_map/pallas_call | solution.py:334
  (8 shorter events, 0.0 us)
Async XLA Ops:
  0.0 6.6 %copy-start.1 = (bf16[16,128,512]{2,1,0:T(8,128)(2,1)S(1)}, bf16[16,128,512]{2,1,0:T(8,128)(2,1)}, u32[]{:S(2)}) copy-start(bf16[16,128,512]{2,1,0:T(8,128)(2,1)} %w_ref.2) | copy-start | bytes 6291460
  1.4 5.3 %collective-permute-start = (bf16[128,256]{1,0:T(8,128)(2,1)S(1)}, bf16[128,256]{1,0:T(8,128)(2,1)S(1)}, u32[]{:S(2)}, u32[]{:S(2)}) collective-permute-start(bf16[128,256]{1,0:T(8,128)(2,1)S(1)} %get-tuple-element.20), channel_id=1, source_target_pairs={{0,8},{1,5},{2,6},{3,11},{4,24},{5,21},{6,22},{7,27},{8,12},{9,1},... | collective-permute-start | bytes 196616 | tf_op jit(solution)/shard_map/ppermute | solution.py:272
  1.5 7.9 %collective-permute-start.3 = (bf16[576,128]{1,0:T(8,128)(2,1)S(1)}, bf16[576,128]{1,0:T(8,128)(2,1)S(1)}, u32[]{:S(2)}, u32[]{:S(2)}) collective-permute-start(bf16[576,128]{1,0:T(8,128)(2,1)S(1)} %get-tuple-element.24), channel_id=1, source_target_pairs={{0,24},{4,28},{8,16},{12,20},{16,8},{20,12},{24,0},{28,4},{1,25},{... | collective-permute-start | bytes 442376 | tf_op jit(solution)/shard_map/ppermute | solution.py:274
  3.4 9.1 %collective-permute-start.4 = (bf16[576,128]{1,0:T(8,128)(2,1)S(1)}, bf16[576,128]{1,0:T(8,128)(2,1)S(1)}, u32[]{:S(2)}, u32[]{:S(2)}) collective-permute-start(bf16[576,128]{1,0:T(8,128)(2,1)S(1)} %get-tuple-element.25), channel_id=1, source_target_pairs={{0,8},{4,20},{8,0},{12,28},{16,24},{20,4},{24,16},{28,12},{1,9},{5... | collective-permute-start | bytes 442376 | tf_op jit(solution)/shard_map/ppermute | solution.py:274
  3.5 9.3 %collective-permute-start.5 = (bf16[576,128]{1,0:T(8,128)(2,1)S(1)}, bf16[576,128]{1,0:T(8,128)(2,1)S(1)}, u32[]{:S(2)}, u32[]{:S(2)}) collective-permute-start(bf16[576,128]{1,0:T(8,128)(2,1)S(1)} %get-tuple-element.26), channel_id=1, source_target_pairs={{0,16},{4,12},{8,24},{12,4},{16,0},{20,28},{24,8},{28,20},{1,17},{... | collective-permute-start | bytes 442376 | tf_op jit(solution)/shard_map/ppermute | solution.py:274
  7.1 6.5 %collective-permute-start.1 = (bf16[64,640]{1,0:T(8,128)(2,1)S(1)}, bf16[64,640]{1,0:T(8,128)(2,1)S(1)}, u32[]{:S(2)}, u32[]{:S(2)}) collective-permute-start(bf16[64,640]{1,0:T(8,128)(2,1)S(1)} %get-tuple-element.21), channel_id=1, source_target_pairs={{8,4},{5,12},{6,0},{11,8},{24,20},{21,28},{22,16},{27,24},{12,5},{... | collective-permute-start | bytes 245768 | tf_op jit(solution)/shard_map/ppermute | solution.py:297
  7.2 6.5 %collective-permute-start.2 = (bf16[64,640]{1,0:T(8,128)(2,1)S(1)}, bf16[64,640]{1,0:T(8,128)(2,1)S(1)}, u32[]{:S(2)}, u32[]{:S(2)}) collective-permute-start(bf16[64,640]{1,0:T(8,128)(2,1)S(1)} %get-tuple-element.22), channel_id=1, source_target_pairs={{8,12},{5,4},{6,8},{11,0},{24,28},{21,20},{22,24},{27,16},{12,13},... | collective-permute-start | bytes 245768 | tf_op jit(solution)/shard_map/ppermute | solution.py:297
  9.7 4.8 %collective-permute-start.6 = (bf16[2,576,128]{2,1,0:T(8,128)(2,1)S(1)}, bf16[2,576,128]{2,1,0:T(8,128)(2,1)S(1)}, u32[]{:S(2)}, u32[]{:S(2)}) collective-permute-start(bf16[2,576,128]{2,1,0:T(8,128)(2,1)S(1)} %shard_map.67), channel_id=1, source_target_pairs={{0,4},{4,0},{8,12},{12,8},{16,20},{20,16},{24,28},{28,24},{1,5},{5... | collective-permute-start | bytes 884744 | tf_op jit(solution)/shard_map/ppermute | solution.py:286
  12.5 2.0 %collective-permute-start.7 = (bf16[576,128]{1,0:T(8,128)(2,1)S(1)}, bf16[576,128]{1,0:T(8,128)(2,1)S(1)}, u32[]{:S(2)}, u32[]{:S(2)}) collective-permute-start(bf16[576,128]{1,0:T(8,128)(2,1)S(1)} %collective-permute-done.4.refs_4_), channel_id=1, source_target_pairs={{0,4},{4,0},{8,12},{12,8},{16,20},{20,16},{24,28},{28,24},{1,5},{5... | collective-permute-start | bytes 442376 | tf_op jit(solution)/shard_map/ppermute | solution.py:286
  12.8 1.7 %collective-permute-start.8 = (bf16[576,128]{1,0:T(8,128)(2,1)S(1)}, bf16[576,128]{1,0:T(8,128)(2,1)S(1)}, u32[]{:S(2)}, u32[]{:S(2)}) collective-permute-start(bf16[576,128]{1,0:T(8,128)(2,1)S(1)} %collective-permute-done.5.refs_5_), channel_id=1, source_target_pairs={{0,4},{4,0},{8,12},{12,8},{16,20},{20,16},{24,28},{28,24},{1,5},{5... | collective-permute-start | bytes 442376 | tf_op jit(solution)/shard_map/ppermute | solution.py:286
  13.7 11.6 %copy-start = (bf16[16,512,128]{2,1,0:T(8,128)(2,1)S(1)}, bf16[16,512,128]{2,1,0:T(8,128)(2,1)}, u32[]{:S(2)}) copy-start(bf16[16,512,128]{2,1,0:T(8,128)(2,1)} %w_ref.3) | copy-start | bytes 6291460
  15.2 7.7 %collective-permute-start.10 = (bf16[64,512]{1,0:T(8,128)(2,1)S(1)}, bf16[64,512]{1,0:T(8,128)(2,1)S(1)}, u32[]{:S(2)}, u32[]{:S(2)}) collective-permute-start(bf16[64,512]{1,0:T(8,128)(2,1)S(1)} %get-tuple-element.32), channel_id=1, source_target_pairs={{4,0},{12,1},{0,2},{8,3},{20,4},{28,5},{16,6},{24,7},{5,8},{13,9},... | collective-permute-start | bytes 196616 | tf_op jit(solution)/shard_map/ppermute | solution.py:327
  18.7 6.6 %collective-permute-start.9 = (bf16[64,512]{1,0:T(8,128)(2,1)S(1)}, bf16[64,512]{1,0:T(8,128)(2,1)S(1)}, u32[]{:S(2)}, u32[]{:S(2)}) collective-permute-start(bf16[64,512]{1,0:T(8,128)(2,1)S(1)} %get-tuple-element.31), channel_id=1, source_target_pairs={{12,0},{4,1},{8,2},{0,3},{28,4},{20,5},{24,6},{16,7},{13,8},{5,9},... | collective-permute-start | bytes 196616 | tf_op jit(solution)/shard_map/ppermute | solution.py:327

commit v30 on v29

--- a/solution.py
+++ b/solution.py
@@ -34,8 +34,8 @@
 
 
 def first_block(plane, chip, core):
-    near = 1 * (chip % 2 == plane % 2)
-    return far_half(plane, 1 - core) ^ near ^ chip % 2
+    a = 1 - chip % 2
+    return far_half(plane, 1 - core) ^ 1 * (a == plane % 2) ^ a
 
 
 def partner(k, core):
@@ -57,7 +57,7 @@
             rows = pl.ds(n * part, part)
             moves.append(
                 pltpu.make_async_copy(
-                    cache_hbm.at[chip ^ partner(k, core), rows],
+                    cache_hbm.at[chip ^ partner(k, core) ^ 1, rows],
                     blocks[k].at[rows],
                     sem.at[3 + k * COPY_PARTS + n],
                 )
@@ -79,7 +79,7 @@
         own = jnp.concatenate(parts, axis=0).astype(rows.dtype)
         out_ref[a * piece : (a + 1) * piece] = jnp.concatenate([rows, own], axis=1)
     moves[2].wait()
-    length = len_ref[lax.axis_index("head") * owners + chip]
+    length = len_ref[lax.axis_index("head") * owners + (chip ^ 1)]
     limit_ref[...] = jnp.full(limit_ref.shape, length, limit_ref.dtype)
     for move in moves[3:]:
         move.wait()
@@ -245,7 +245,7 @@
         return flat(((i % COPIES) * 2 + other // 2) * COPIES + other % 2, j)
 
     def owner(i, j, a):
-        plane, chip = i // COPIES, i % COPIES * per_device + a
+        plane, chip = i // COPIES, (i % COPIES * per_device + a) ^ 1
         return flat(chip * COPIES + 1 - j // 2, plane)
 
     def in_plane(move):

time: 26.5 us -> 27.5 us (1.038)
  starting transfers between devices: 9.42 us -> 10.7 us
  waiting for transfers between devices: 12.1 us -> 11.7 us
    ppermute x2, starting transfers between devices: 0.13 us -> 2.29 us  [whole_sequences(): lax.ppermute(pieces[k], both, [(host(i, j), owner(i, j, leaves_as(k, j)))...]
    ppermute x2, waiting for transfers between devices: 0.73 us -> 2.18 us  [whole_sequences(): lax.ppermute(pieces[k], both, [(host(i, j), owner(i, j, leaves_as(k, j)))...]
    ppermute x3, waiting for transfers between devices: 3.54 us -> 2.47 us  [whole_sequences(): lax.ppermute(picked[k], 'seq', in_plane(lambda g, t: (g ^ partner(k, t))...]
    ppermute x3, starting transfers between devices: 1.81 us -> 0.81 us  [whole_sequences(): lax.ppermute(keys, 'seq', other_core)]
    ppermute x2, waiting for transfers between devices: 6.18 us -> 5.43 us  [whole_sequences(): lax.ppermute(latent[k], both, [(owner(i, j, first_back(i // COPIES, j) ^...]
  transfers between devices with their start and end apart: 11 -> 11, of which waited for: 7 -> 6; matrix products, arithmetic and copies ran while one was open for 0% -> 0% of each run, Pallas kernels for 6% -> 6%
where the time goes in v30:
time: 27.5 us; the launch traced here: 27.3 us
  waiting for transfers between devices  11.7 us (43%)
  starting transfers between devices  10.7 us (39%)
  Pallas kernels  4.75 us (17%)
    ppermute x2, waiting for transfers between devices, whole_sequences(): lax.ppermute(latent[k], both, [(owner(i, j, first_back(i // COPIES, j) ^...  5.43 us
    ppermute x2, starting transfers between devices, whole_sequences(): lax.ppermute(latent[k], both, [(owner(i, j, first_back(i // COPIES, j) ^...  3.97 us
    ppermute x3, starting transfers between devices, whole_sequences(): lax.ppermute(picked[k], 'seq', in_plane(lambda g, t: (g ^ partner(k, t))...  3.55 us
    ppermute x3, waiting for transfers between devices, whole_sequences(): lax.ppermute(picked[k], 'seq', in_plane(lambda g, t: (g ^ partner(k, t))...  2.47 us
    ppermute x2, starting transfers between devices, whole_sequences(): lax.ppermute(pieces[k], both, [(host(i, j), owner(i, j, leaves_as(k, j)))...  2.29 us
    ppermute x2, waiting for transfers between devices, whole_sequences(): lax.ppermute(pieces[k], both, [(host(i, j), owner(i, j, leaves_as(k, j)))...  2.18 us
    ppermute x1, waiting for transfers between devices, whole_sequences(): lax.ppermute(packed, both, [(flat(i, j), host(i, j)) for i, j in devices])  1.63 us
    pallas_call x1, Pallas kernels, whole_sequences(): pl.pallas_call(functools.partial(pick_kernel, per_device), out_shape=[jax...  1.37 us
  transfers between devices with their start and end apart: 11, of which 6 were waited for; matrix products, arithmetic and copies ran while one was open for 0% of the time, Pallas kernels for 6%

profile of v30, /device:TPU:6, one launch (start us, length us, event | category | flops | bytes accessed | tf_op | source)
XLA Modules:
  0.0 27.3 jit_solution(49464082977919746)
XLA Ops:
  0.0 1.4 %shard_map.64 = (bf16[576,128]{1,0:T(8,128)(2,1)S(1)}, bf16[576,128]{1,0:T(8,128)(2,1)S(1)}, bf16[576,128]{1,0:T(8,128)(2,1)S(1)}, bf16[576,128]{1,0:T(8,128)(2,...) custom-call(bf16[4,576,128]{2,1,0:T(8,128)(2,1)} %bitcast.1, bf16[8,16,192]{2,1,0:T(8,128)(2,1)} %q_hbm.1, ...), custom_call_target="tpu_custom_call" | custom-call | flops 20000000000 | tf_op jit(solution)/shard_map/pallas_call | solution.py:254
  1.4 0.1 collective-permute-start
  1.5 2.0 %collective-permute-start.3 = (bf16[576,128]{1,0:T(8,128)(2,1)S(1)}, bf16[576,128]{1,0:T(8,128)(2,1)S(1)}, u32[]{:S(2)}, u32[]{:S(2)}) collective-permute-start(bf16[576,128]{1,0:T(8,128)(2,1)S(1)} %get-tuple-element.24), channel_id=1, source_target_pairs={{0,24},{4,28},{8,16},{12,20},{16,8},{20,12},{24,0},{28,4},{1,25},{... | collective-permute-start | bytes 442376 | tf_op jit(solution)/shard_map/ppermute | solution.py:274
  3.4 0.1 collective-permute-start.4
  3.5 1.5 %collective-permute-start.5 = (bf16[576,128]{1,0:T(8,128)(2,1)S(1)}, bf16[576,128]{1,0:T(8,128)(2,1)S(1)}, u32[]{:S(2)}, u32[]{:S(2)}) collective-permute-start(bf16[576,128]{1,0:T(8,128)(2,1)S(1)} %get-tuple-element.26), channel_id=1, source_target_pairs={{0,16},{4,12},{8,24},{12,4},{16,0},{20,28},{24,8},{28,20},{1,17},{... | collective-permute-start | bytes 442376 | tf_op jit(solution)/shard_map/ppermute | solution.py:274
  5.0 1.6 %collective-permute-done.packed_ref = bf16[128,256]{1,0:T(8,128)(2,1)S(1)} collective-permute-done((bf16[128,256]{1,0:T(8,128)(2,1)S(1)}, bf16[128,256]{1,0:T(8,128)(2,1)S(1)}, u32[]{:S(2)}, u32[]{:S(2)}) %collective-permute-start) | collective-permute-done | bytes 65568 | tf_op jit(solution)/shard_map/ppermute | solution.py:272
  6.6 0.5 %shard_map.65 = (bf16[64,640]{1,0:T(8,128)(2,1)S(1)}, bf16[64,640]{1,0:T(8,128)(2,1)S(1)}) custom-call(bf16[16,128,512]{2,1,0:T(8,128)(2,1)S(1)} %copy-done.1, bf16[128,256]{1,0:T(8,128)(2,1)S(1)} %collective-permute-done.packed_ref), custom_call_target="tpu_custom_call" | custom-call | flops 20000000000 | tf_op jit(solution)/shard_map/pallas_call | solution.py:288
  7.1 0.1 collective-permute-start.1
  7.2 2.2 %collective-permute-start.2 = (bf16[64,640]{1,0:T(8,128)(2,1)S(1)}, bf16[64,640]{1,0:T(8,128)(2,1)S(1)}, u32[]{:S(2)}, u32[]{:S(2)}) collective-permute-start(bf16[64,640]{1,0:T(8,128)(2,1)S(1)} %get-tuple-element.22), channel_id=1, source_target_pairs={{8,4},{5,12},{6,0},{11,8},{24,20},{21,28},{22,16},{27,24},{12,5},{... | collective-permute-start | bytes 245768 | tf_op jit(solution)/shard_map/ppermute | solution.py:297
  9.4 0.4 %shard_map.67 = bf16[2,576,128]{2,1,0:T(8,128)(2,1)S(1)} custom-call(bf16[576,128]{1,0:T(8,128)(2,1)S(1)} %get-tuple-element.23.refs_2_.first_ref, bf16[576,128]{1,0:T(8,128)(2,1)S(1)} %collective-permute-done.3.refs_3_.second_ref), custom_call_target="tpu_custom_call" | custom-call | tf_op jit(solution)/shard_map/pallas_call | solution.py:277
  9.8 0.3 %collective-permute-start.6 = (bf16[2,576,128]{2,1,0:T(8,128)(2,1)S(1)}, bf16[2,576,128]{2,1,0:T(8,128)(2,1)S(1)}, u32[]{:S(2)}, u32[]{:S(2)}) collective-permute-start(bf16[2,576,128]{2,1,0:T(8,128)(2,1)S(1)} %shard_map.67), channel_id=1, source_target_pairs={{0,4},{4,0},{8,12},{12,8},{16,20},{20,16},{24,28},{28,24},{1,5},{5... | collective-permute-start | bytes 884744 | tf_op jit(solution)/shard_map/ppermute | solution.py:286
  10.1 2.5 %collective-permute-done.4.refs_4_ = bf16[576,128]{1,0:T(8,128)(2,1)S(1)} collective-permute-done((bf16[576,128]{1,0:T(8,128)(2,1)S(1)}, bf16[576,128]{1,0:T(8,128)(2,1)S(1)}, u32[]{:S(2)}, u32[]{:S(2)}) %collective-permute-start.4) | collective-permute-done | bytes 147488 | tf_op jit(solution)/shard_map/ppermute | solution.py:274
  12.6 0.2 collective-permute-start.7
  12.8 0.3 %collective-permute-start.8 = (bf16[576,128]{1,0:T(8,128)(2,1)S(1)}, bf16[576,128]{1,0:T(8,128)(2,1)S(1)}, u32[]{:S(2)}, u32[]{:S(2)}) collective-permute-start(bf16[576,128]{1,0:T(8,128)(2,1)S(1)} %collective-permute-done.5.refs_5_), channel_id=1, source_target_pairs={{0,4},{4,0},{8,12},{12,8},{16,20},{20,16},{24,28},{28,24},{1,5},{5... | collective-permute-start | bytes 442376 | tf_op jit(solution)/shard_map/ppermute | solution.py:286
  13.1 0.6 %collective-permute-done.1.refs_0_ = bf16[64,640]{1,0:T(8,128)(2,1)S(1)} collective-permute-done((bf16[64,640]{1,0:T(8,128)(2,1)S(1)}, bf16[64,640]{1,0:T(8,128)(2,1)S(1)}, u32[]{:S(2)}, u32[]{:S(2)}) %collective-permute-start.1) | collective-permute-done | bytes 81952 | tf_op jit(solution)/shard_map/ppermute | solution.py:297
  13.7 1.6 %collective-permute-done.2.refs_1_ = bf16[64,640]{1,0:T(8,128)(2,1)S(1)} collective-permute-done((bf16[64,640]{1,0:T(8,128)(2,1)S(1)}, bf16[64,640]{1,0:T(8,128)(2,1)S(1)}, u32[]{:S(2)}, u32[]{:S(2)}) %collective-permute-start.2) | collective-permute-done | bytes 81952 | tf_op jit(solution)/shard_map/ppermute | solution.py:297
  15.3 0.8 %shard_map.66 = (bf16[128,576]{1,0:T(8,128)(2,1)S(1)}, f32[128,128]{1,0:T(8,128)S(1)}, f32[128,128]{1,0:T(8,128)S(1)}, f32[128,512]{1,0:T(8,128)S(1)}) custom-call(s32[8,128]{1,0:T(8,128)S(1)} %get-tuple-element.19.limit_ref, bf16[64,640]{1,0:T(8,128)(2,1)S(1)} %collective-permute-done.1.refs_0_, bf16[64,640]{1,0:T(8,128)(2,1)S(1)} %collective-permute-done.2.refs_1_, ...), custom_call_target="tpu_custom_call" | custom-call | flops 20000000000 | tf_op jit(solution)/shard_map/pallas_call | solution.py:305
  16.0 0.0 collective-permute-done.7.refs_0_
  16.1 0.7 %shard_map.68 = (bf16[64,512]{1,0:T(8,128)(2,1)S(1)}, bf16[64,512]{1,0:T(8,128)(2,1)S(1)}) custom-call(s32[8,128]{1,0:T(8,128)S(1)} %get-tuple-element.19.limit_ref, bf16[128,576]{1,0:T(8,128)(2,1)S(1)} %get-tuple-element.27.q_ref, f32[128,128]{1,0:T(8,128)S(1)} %get-tuple-element.28.top_ref, f32[128,128]{1,0:T(8,128)S(1)} %get-tuple-element.29.total_ref, ...), custom_call_target="tpu_custom_call" | custom-call | tf_op jit(solution)/shard_map/pallas_call | solution.py:318
  16.8 2.1 %collective-permute-start.10 = (bf16[64,512]{1,0:T(8,128)(2,1)S(1)}, bf16[64,512]{1,0:T(8,128)(2,1)S(1)}, u32[]{:S(2)}, u32[]{:S(2)}) collective-permute-start(bf16[64,512]{1,0:T(8,128)(2,1)S(1)} %get-tuple-element.32), channel_id=1, source_target_pairs={{12,0},{4,1},{8,2},{0,3},{28,4},{20,5},{24,6},{16,7},{13,8},{5,9},... | collective-permute-start | bytes 196616 | tf_op jit(solution)/shard_map/ppermute | solution.py:327
  18.9 1.9 %collective-permute-start.9 = (bf16[64,512]{1,0:T(8,128)(2,1)S(1)}, bf16[64,512]{1,0:T(8,128)(2,1)S(1)}, u32[]{:S(2)}, u32[]{:S(2)}) collective-permute-start(bf16[64,512]{1,0:T(8,128)(2,1)S(1)} %get-tuple-element.31), channel_id=1, source_target_pairs={{4,0},{12,1},{0,2},{8,3},{20,4},{28,5},{16,6},{24,7},{5,8},{13,9},... | collective-permute-start | bytes 196616 | tf_op jit(solution)/shard_map/ppermute | solution.py:327
  20.8 2.8 %collective-permute-done.10.refs_1_ = bf16[64,512]{1,0:T(8,128)(2,1)S(1)} collective-permute-done((bf16[64,512]{1,0:T(8,128)(2,1)S(1)}, bf16[64,512]{1,0:T(8,128)(2,1)S(1)}, u32[]{:S(2)}, u32[]{:S(2)}) %collective-permute-start.10) | collective-permute-done | bytes 65568 | tf_op jit(solution)/shard_map/ppermute | solution.py:327
  23.6 2.6 %collective-permute-done.9.refs_0_ = bf16[64,512]{1,0:T(8,128)(2,1)S(1)} collective-permute-done((bf16[64,512]{1,0:T(8,128)(2,1)S(1)}, bf16[64,512]{1,0:T(8,128)(2,1)S(1)}, u32[]{:S(2)}, u32[]{:S(2)}) %collective-permute-start.9) | collective-permute-done | bytes 65568 | tf_op jit(solution)/shard_map/ppermute | solution.py:327
  26.2 1.1 %shard_map.69 = bf16[8,16,128]{2,1,0:T(8,128)(2,1)} custom-call(bf16[16,512,128]{2,1,0:T(8,128)(2,1)S(1)} %copy-done, bf16[64,512]{1,0:T(8,128)(2,1)S(1)} %collective-permute-done.9.refs_0_, bf16[64,512]{1,0:T(8,128)(2,1)S(1)} %collective-permute-done.10.refs_1_), custom_call_target="tpu_custom_call" | custom-call | tf_op jit(solution)/shard_map/pallas_call | solution.py:334
  (8 shorter events, 0.0 us)
Async XLA Ops:
  0.0 6.6 %copy-start.1 = (bf16[16,128,512]{2,1,0:T(8,128)(2,1)S(1)}, bf16[16,128,512]{2,1,0:T(8,128)(2,1)}, u32[]{:S(2)}) copy-start(bf16[16,128,512]{2,1,0:T(8,128)(2,1)} %w_ref.2) | copy-start | bytes 6291460
  1.4 5.3 %collective-permute-start = (bf16[128,256]{1,0:T(8,128)(2,1)S(1)}, bf16[128,256]{1,0:T(8,128)(2,1)S(1)}, u32[]{:S(2)}, u32[]{:S(2)}) collective-permute-start(bf16[128,256]{1,0:T(8,128)(2,1)S(1)} %get-tuple-element.20), channel_id=1, source_target_pairs={{0,8},{1,5},{2,6},{3,11},{4,24},{5,21},{6,22},{7,27},{8,12},{9,1},... | collective-permute-start | bytes 196616 | tf_op jit(solution)/shard_map/ppermute | solution.py:272
  1.5 8.0 %collective-permute-start.3 = (bf16[576,128]{1,0:T(8,128)(2,1)S(1)}, bf16[576,128]{1,0:T(8,128)(2,1)S(1)}, u32[]{:S(2)}, u32[]{:S(2)}) collective-permute-start(bf16[576,128]{1,0:T(8,128)(2,1)S(1)} %get-tuple-element.24), channel_id=1, source_target_pairs={{0,24},{4,28},{8,16},{12,20},{16,8},{20,12},{24,0},{28,4},{1,25},{... | collective-permute-start | bytes 442376 | tf_op jit(solution)/shard_map/ppermute | solution.py:274
  3.4 9.2 %collective-permute-start.4 = (bf16[576,128]{1,0:T(8,128)(2,1)S(1)}, bf16[576,128]{1,0:T(8,128)(2,1)S(1)}, u32[]{:S(2)}, u32[]{:S(2)}) collective-permute-start(bf16[576,128]{1,0:T(8,128)(2,1)S(1)} %get-tuple-element.25), channel_id=1, source_target_pairs={{0,8},{4,20},{8,0},{12,28},{16,24},{20,4},{24,16},{28,12},{1,9},{5... | collective-permute-start | bytes 442376 | tf_op jit(solution)/shard_map/ppermute | solution.py:274
  3.5 9.3 %collective-permute-start.5 = (bf16[576,128]{1,0:T(8,128)(2,1)S(1)}, bf16[576,128]{1,0:T(8,128)(2,1)S(1)}, u32[]{:S(2)}, u32[]{:S(2)}) collective-permute-start(bf16[576,128]{1,0:T(8,128)(2,1)S(1)} %get-tuple-element.26), channel_id=1, source_target_pairs={{0,16},{4,12},{8,24},{12,4},{16,0},{20,28},{24,8},{28,20},{1,17},{... | collective-permute-start | bytes 442376 | tf_op jit(solution)/shard_map/ppermute | solution.py:274
  7.1 6.5 %collective-permute-start.1 = (bf16[64,640]{1,0:T(8,128)(2,1)S(1)}, bf16[64,640]{1,0:T(8,128)(2,1)S(1)}, u32[]{:S(2)}, u32[]{:S(2)}) collective-permute-start(bf16[64,640]{1,0:T(8,128)(2,1)S(1)} %get-tuple-element.21), channel_id=1, source_target_pairs={{8,12},{5,4},{6,8},{11,0},{24,28},{21,20},{22,24},{27,16},{12,13},... | collective-permute-start | bytes 245768 | tf_op jit(solution)/shard_map/ppermute | solution.py:297
  7.2 8.1 %collective-permute-start.2 = (bf16[64,640]{1,0:T(8,128)(2,1)S(1)}, bf16[64,640]{1,0:T(8,128)(2,1)S(1)}, u32[]{:S(2)}, u32[]{:S(2)}) collective-permute-start(bf16[64,640]{1,0:T(8,128)(2,1)S(1)} %get-tuple-element.22), channel_id=1, source_target_pairs={{8,4},{5,12},{6,0},{11,8},{24,20},{21,28},{22,16},{27,24},{12,5},{... | collective-permute-start | bytes 245768 | tf_op jit(solution)/shard_map/ppermute | solution.py:297
  9.8 6.2 %collective-permute-start.6 = (bf16[2,576,128]{2,1,0:T(8,128)(2,1)S(1)}, bf16[2,576,128]{2,1,0:T(8,128)(2,1)S(1)}, u32[]{:S(2)}, u32[]{:S(2)}) collective-permute-start(bf16[2,576,128]{2,1,0:T(8,128)(2,1)S(1)} %shard_map.67), channel_id=1, source_target_pairs={{0,4},{4,0},{8,12},{12,8},{16,20},{20,16},{24,28},{28,24},{1,5},{5... | collective-permute-start | bytes 884744 | tf_op jit(solution)/shard_map/ppermute | solution.py:286
  12.6 3.5 %collective-permute-start.7 = (bf16[576,128]{1,0:T(8,128)(2,1)S(1)}, bf16[576,128]{1,0:T(8,128)(2,1)S(1)}, u32[]{:S(2)}, u32[]{:S(2)}) collective-permute-start(bf16[576,128]{1,0:T(8,128)(2,1)S(1)} %collective-permute-done.4.refs_4_), channel_id=1, source_target_pairs={{0,4},{4,0},{8,12},{12,8},{16,20},{20,16},{24,28},{28,24},{1,5},{5... | collective-permute-start | bytes 442376 | tf_op jit(solution)/shard_map/ppermute | solution.py:286
  12.8 3.3 %collective-permute-start.8 = (bf16[576,128]{1,0:T(8,128)(2,1)S(1)}, bf16[576,128]{1,0:T(8,128)(2,1)S(1)}, u32[]{:S(2)}, u32[]{:S(2)}) collective-permute-start(bf16[576,128]{1,0:T(8,128)(2,1)S(1)} %collective-permute-done.5.refs_5_), channel_id=1, source_target_pairs={{0,4},{4,0},{8,12},{12,8},{16,20},{20,16},{24,28},{28,24},{1,5},{5... | collective-permute-start | bytes 442376 | tf_op jit(solution)/shard_map/ppermute | solution.py:286
  15.3 10.9 %copy-start = (bf16[16,512,128]{2,1,0:T(8,128)(2,1)S(1)}, bf16[16,512,128]{2,1,0:T(8,128)(2,1)}, u32[]{:S(2)}) copy-start(bf16[16,512,128]{2,1,0:T(8,128)(2,1)} %w_ref.3) | copy-start | bytes 6291460
  16.8 6.8 %collective-permute-start.10 = (bf16[64,512]{1,0:T(8,128)(2,1)S(1)}, bf16[64,512]{1,0:T(8,128)(2,1)S(1)}, u32[]{:S(2)}, u32[]{:S(2)}) collective-permute-start(bf16[64,512]{1,0:T(8,128)(2,1)S(1)} %get-tuple-element.32), channel_id=1, source_target_pairs={{12,0},{4,1},{8,2},{0,3},{28,4},{20,5},{24,6},{16,7},{13,8},{5,9},... | collective-permute-start | bytes 196616 | tf_op jit(solution)/shard_map/ppermute | solution.py:327
  18.9 7.3 %collective-permute-start.9 = (bf16[64,512]{1,0:T(8,128)(2,1)S(1)}, bf16[64,512]{1,0:T(8,128)(2,1)S(1)}, u32[]{:S(2)}, u32[]{:S(2)}) collective-permute-start(bf16[64,512]{1,0:T(8,128)(2,1)S(1)} %get-tuple-element.31), channel_id=1, source_target_pairs={{4,0},{12,1},{0,2},{8,3},{20,4},{28,5},{16,6},{24,7},{5,8},{13,9},... | collective-permute-start | bytes 196616 | tf_op jit(solution)/shard_map/ppermute | solution.py:327

commit v31 on v29

--- a/solution.py
+++ b/solution.py
@@ -208,9 +208,7 @@
 def project_kernel(per_device, w_ref, *refs):
     lat_refs, out_ref = refs[:-1], refs[-1]
     rows, heads, width = out_ref.shape
-    first = first_back(lax.axis_index("seq") // COPIES, lax.axis_index("head"))
-    parts = [jnp.where(first == a, lat_refs[1][...], lat_refs[0][...]) for a in range(per_device)]
-    latent = jnp.concatenate(parts, axis=0)
+    latent = jnp.concatenate([ref[...] for ref in lat_refs], axis=0)
     out = jnp.zeros((rows * heads, width), jnp.float32)
     own_head = lax.broadcasted_iota(jnp.int32, out.shape, 0) % heads
     step = 2 if heads % 2 == 0 else 1
@@ -219,7 +217,16 @@
         product = jnp.dot(latent, group, preferred_element_type=jnp.float32)
         for n in range(step):
             out = jnp.where(own_head == h + n, product[:, n * width : (n + 1) * width], out)
-    out_ref[...] = out.astype(out_ref.dtype).reshape(out_ref.shape)
+    out = out.astype(out_ref.dtype)
+    first = first_back(lax.axis_index("seq") // COPIES, lax.axis_index("head"))
+    piece = SPEC * heads
+    for n in range(per_device):
+        for a in range(per_device):
+
+            @pl.when(first ^ n != a)
+            def _():
+                block = out[n * piece : (n + 1) * piece]
+                out_ref[a * SPEC : (a + 1) * SPEC] = block.reshape(SPEC, heads, width)
 
 
 def whole_sequences(seq_size, head_size, queries, new_latent, cache, lengths, w_uk, w_uv):

time: 26.5 us -> 26.5 us (level)
  no operation moved by 1% of the time
where the time goes in v31:
time: 26.5 us; the launch traced here: 26.4 us
  waiting for transfers between devices  12.1 us (46%)
  starting transfers between devices  9.42 us (36%)
  Pallas kernels  4.75 us (18%)
    ppermute x2, waiting for transfers between devices, whole_sequences(): lax.ppermute(latent[k], both, [(owner(i, j, first_back(i // COPIES, j) ^...  6.18 us
    ppermute x2, starting transfers between devices, whole_sequences(): lax.ppermute(latent[k], both, [(owner(i, j, first_back(i // COPIES, j) ^...  3.86 us
    ppermute x3, starting transfers between devices, whole_sequences(): lax.ppermute(picked[k], 'seq', in_plane(lambda g, t: (g ^ partner(k, t))...  3.55 us
    ppermute x3, waiting for transfers between devices, whole_sequences(): lax.ppermute(picked[k], 'seq', in_plane(lambda g, t: (g ^ partner(k, t))...  3.54 us
    ppermute x3, starting transfers between devices, whole_sequences(): lax.ppermute(keys, 'seq', other_core)  1.81 us
    ppermute x1, waiting for transfers between devices, whole_sequences(): lax.ppermute(packed, both, [(flat(i, j), host(i, j)) for i, j in devices])  1.63 us
    pallas_call x1, Pallas kernels, whole_sequences(): pl.pallas_call(functools.partial(pick_kernel, per_device), out_shape=[jax...  1.37 us
    pallas_call x1, Pallas kernels, whole_sequences(): pl.pallas_call(functools.partial(project_kernel, per_device), out_shape=j...  1.07 us
  transfers between devices with their start and end apart: 11, of which 7 were waited for; matrix products, arithmetic and copies ran while one was open for 0% of the time, Pallas kernels for 6%

profile of v31, /device:TPU:6, one launch (start us, length us, event | category | flops | bytes accessed | tf_op | source)
XLA Modules:
  0.0 26.4 jit_solution(17351994292066614789)
XLA Ops:
  0.0 1.4 %shard_map.64 = (bf16[576,128]{1,0:T(8,128)(2,1)S(1)}, bf16[576,128]{1,0:T(8,128)(2,1)S(1)}, bf16[576,128]{1,0:T(8,128)(2,1)S(1)}, bf16[576,128]{1,0:T(8,128)(2,...) custom-call(bf16[4,576,128]{2,1,0:T(8,128)(2,1)} %bitcast.1, bf16[8,16,192]{2,1,0:T(8,128)(2,1)} %q_hbm.1, ...), custom_call_target="tpu_custom_call" | custom-call | flops 20000000000 | tf_op jit(solution)/shard_map/pallas_call | solution.py:261
  1.4 0.1 collective-permute-start
  1.5 2.0 %collective-permute-start.3 = (bf16[576,128]{1,0:T(8,128)(2,1)S(1)}, bf16[576,128]{1,0:T(8,128)(2,1)S(1)}, u32[]{:S(2)}, u32[]{:S(2)}) collective-permute-start(bf16[576,128]{1,0:T(8,128)(2,1)S(1)} %get-tuple-element.24), channel_id=1, source_target_pairs={{0,24},{4,28},{8,16},{12,20},{16,8},{20,12},{24,0},{28,4},{1,25},{... | collective-permute-start | bytes 442376 | tf_op jit(solution)/shard_map/ppermute | solution.py:281
  3.4 0.1 collective-permute-start.4
  3.5 1.5 %collective-permute-start.5 = (bf16[576,128]{1,0:T(8,128)(2,1)S(1)}, bf16[576,128]{1,0:T(8,128)(2,1)S(1)}, u32[]{:S(2)}, u32[]{:S(2)}) collective-permute-start(bf16[576,128]{1,0:T(8,128)(2,1)S(1)} %get-tuple-element.26), channel_id=1, source_target_pairs={{0,16},{4,12},{8,24},{12,4},{16,0},{20,28},{24,8},{28,20},{1,17},{... | collective-permute-start | bytes 442376 | tf_op jit(solution)/shard_map/ppermute | solution.py:281
  5.0 1.6 %collective-permute-done.packed_ref = bf16[128,256]{1,0:T(8,128)(2,1)S(1)} collective-permute-done((bf16[128,256]{1,0:T(8,128)(2,1)S(1)}, bf16[128,256]{1,0:T(8,128)(2,1)S(1)}, u32[]{:S(2)}, u32[]{:S(2)}) %collective-permute-start) | collective-permute-done | bytes 65568 | tf_op jit(solution)/shard_map/ppermute | solution.py:279
  6.6 0.5 %shard_map.65 = (bf16[64,640]{1,0:T(8,128)(2,1)S(1)}, bf16[64,640]{1,0:T(8,128)(2,1)S(1)}) custom-call(bf16[16,128,512]{2,1,0:T(8,128)(2,1)S(1)} %copy-done.1, bf16[128,256]{1,0:T(8,128)(2,1)S(1)} %collective-permute-done.packed_ref), custom_call_target="tpu_custom_call" | custom-call | flops 20000000000 | tf_op jit(solution)/shard_map/pallas_call | solution.py:295
  7.1 0.1 collective-permute-start.1
  7.2 0.1 collective-permute-start.2
  7.3 2.0 %collective-permute-done.3.refs_3_.second_ref = bf16[576,128]{1,0:T(8,128)(2,1)S(1)} collective-permute-done((bf16[576,128]{1,0:T(8,128)(2,1)S(1)}, bf16[576,128]{1,0:T(8,128)(2,1)S(1)}, u32[]{:S(2)}, u32[]{:S(2)}) %collective-permute-start.3) | collective-permute-done | bytes 147488 | tf_op jit(solution)/shard_map/ppermute | solution.py:281
  9.3 0.4 %shard_map.67 = bf16[2,576,128]{2,1,0:T(8,128)(2,1)S(1)} custom-call(bf16[576,128]{1,0:T(8,128)(2,1)S(1)} %get-tuple-element.23.refs_2_.first_ref, bf16[576,128]{1,0:T(8,128)(2,1)S(1)} %collective-permute-done.3.refs_3_.second_ref), custom_call_target="tpu_custom_call" | custom-call | tf_op jit(solution)/shard_map/pallas_call | solution.py:284
  9.7 1.3 %collective-permute-start.6 = (bf16[2,576,128]{2,1,0:T(8,128)(2,1)S(1)}, bf16[2,576,128]{2,1,0:T(8,128)(2,1)S(1)}, u32[]{:S(2)}, u32[]{:S(2)}) collective-permute-start(bf16[2,576,128]{2,1,0:T(8,128)(2,1)S(1)} %shard_map.67), channel_id=1, source_target_pairs={{0,4},{4,0},{8,12},{12,8},{16,20},{20,16},{24,28},{28,24},{1,5},{5... | collective-permute-start | bytes 884744 | tf_op jit(solution)/shard_map/ppermute | solution.py:293
  11.0 1.5 %collective-permute-done.4.refs_4_ = bf16[576,128]{1,0:T(8,128)(2,1)S(1)} collective-permute-done((bf16[576,128]{1,0:T(8,128)(2,1)S(1)}, bf16[576,128]{1,0:T(8,128)(2,1)S(1)}, u32[]{:S(2)}, u32[]{:S(2)}) %collective-permute-start.4) | collective-permute-done | bytes 147488 | tf_op jit(solution)/shard_map/ppermute | solution.py:281
  12.5 0.3 %collective-permute-start.7 = (bf16[576,128]{1,0:T(8,128)(2,1)S(1)}, bf16[576,128]{1,0:T(8,128)(2,1)S(1)}, u32[]{:S(2)}, u32[]{:S(2)}) collective-permute-start(bf16[576,128]{1,0:T(8,128)(2,1)S(1)} %collective-permute-done.4.refs_4_), channel_id=1, source_target_pairs={{0,4},{4,0},{8,12},{12,8},{16,20},{20,16},{24,28},{28,24},{1,5},{5... | collective-permute-start | bytes 442376 | tf_op jit(solution)/shard_map/ppermute | solution.py:293
  12.8 0.2 collective-permute-start.8
  13.0 0.6 %collective-permute-done.1.refs_0_ = bf16[64,640]{1,0:T(8,128)(2,1)S(1)} collective-permute-done((bf16[64,640]{1,0:T(8,128)(2,1)S(1)}, bf16[64,640]{1,0:T(8,128)(2,1)S(1)}, u32[]{:S(2)}, u32[]{:S(2)}) %collective-permute-start.1) | collective-permute-done | bytes 81952 | tf_op jit(solution)/shard_map/ppermute | solution.py:304
  13.6 0.1 collective-permute-done.2.refs_1_
  13.7 0.8 %shard_map.66 = (bf16[128,576]{1,0:T(8,128)(2,1)S(1)}, f32[128,128]{1,0:T(8,128)S(1)}, f32[128,128]{1,0:T(8,128)S(1)}, f32[128,512]{1,0:T(8,128)S(1)}) custom-call(s32[8,128]{1,0:T(8,128)S(1)} %get-tuple-element.19.limit_ref, bf16[64,640]{1,0:T(8,128)(2,1)S(1)} %collective-permute-done.1.refs_0_, bf16[64,640]{1,0:T(8,128)(2,1)S(1)} %collective-permute-done.2.refs_1_, ...), custom_call_target="tpu_custom_call" | custom-call | flops 20000000000 | tf_op jit(solution)/shard_map/pallas_call | solution.py:312
  14.5 0.7 %shard_map.68 = (bf16[64,512]{1,0:T(8,128)(2,1)S(1)}, bf16[64,512]{1,0:T(8,128)(2,1)S(1)}) custom-call(s32[8,128]{1,0:T(8,128)S(1)} %get-tuple-element.19.limit_ref, bf16[128,576]{1,0:T(8,128)(2,1)S(1)} %get-tuple-element.27.q_ref, f32[128,128]{1,0:T(8,128)S(1)} %get-tuple-element.28.top_ref, f32[128,128]{1,0:T(8,128)S(1)} %get-tuple-element.29.total_ref, ...), custom_call_target="tpu_custom_call" | custom-call | tf_op jit(solution)/shard_map/pallas_call | solution.py:325
  15.2 3.4 %collective-permute-start.10 = (bf16[64,512]{1,0:T(8,128)(2,1)S(1)}, bf16[64,512]{1,0:T(8,128)(2,1)S(1)}, u32[]{:S(2)}, u32[]{:S(2)}) collective-permute-start(bf16[64,512]{1,0:T(8,128)(2,1)S(1)} %get-tuple-element.32), channel_id=1, source_target_pairs={{4,0},{12,1},{0,2},{8,3},{20,4},{28,5},{16,6},{24,7},{5,8},{13,9},... | collective-permute-start | bytes 196616 | tf_op jit(solution)/shard_map/ppermute | solution.py:334
  18.7 0.4 %collective-permute-start.9 = (bf16[64,512]{1,0:T(8,128)(2,1)S(1)}, bf16[64,512]{1,0:T(8,128)(2,1)S(1)}, u32[]{:S(2)}, u32[]{:S(2)}) collective-permute-start(bf16[64,512]{1,0:T(8,128)(2,1)S(1)} %get-tuple-element.31), channel_id=1, source_target_pairs={{12,0},{4,1},{8,2},{0,3},{28,4},{20,5},{24,6},{16,7},{13,8},{5,9},... | collective-permute-start | bytes 196616 | tf_op jit(solution)/shard_map/ppermute | solution.py:334
  19.1 3.8 %collective-permute-done.10.refs_1_ = bf16[64,512]{1,0:T(8,128)(2,1)S(1)} collective-permute-done((bf16[64,512]{1,0:T(8,128)(2,1)S(1)}, bf16[64,512]{1,0:T(8,128)(2,1)S(1)}, u32[]{:S(2)}, u32[]{:S(2)}) %collective-permute-start.10) | collective-permute-done | bytes 65568 | tf_op jit(solution)/shard_map/ppermute | solution.py:334
  22.9 2.4 %collective-permute-done.9.refs_0_ = bf16[64,512]{1,0:T(8,128)(2,1)S(1)} collective-permute-done((bf16[64,512]{1,0:T(8,128)(2,1)S(1)}, bf16[64,512]{1,0:T(8,128)(2,1)S(1)}, u32[]{:S(2)}, u32[]{:S(2)}) %collective-permute-start.9) | collective-permute-done | bytes 65568 | tf_op jit(solution)/shard_map/ppermute | solution.py:334
  25.3 1.1 %shard_map.69 = bf16[8,16,128]{2,1,0:T(8,128)(2,1)} custom-call(bf16[16,512,128]{2,1,0:T(8,128)(2,1)S(1)} %copy-done, bf16[64,512]{1,0:T(8,128)(2,1)S(1)} %collective-permute-done.9.refs_0_, bf16[64,512]{1,0:T(8,128)(2,1)S(1)} %collective-permute-done.10.refs_1_), custom_call_target="tpu_custom_call" | custom-call | tf_op jit(solution)/shard_map/pallas_call | solution.py:341
  (8 shorter events, 0.0 us)
Async XLA Ops:
  0.0 6.6 %copy-start.1 = (bf16[16,128,512]{2,1,0:T(8,128)(2,1)S(1)}, bf16[16,128,512]{2,1,0:T(8,128)(2,1)}, u32[]{:S(2)}) copy-start(bf16[16,128,512]{2,1,0:T(8,128)(2,1)} %w_ref.2) | copy-start | bytes 6291460
  1.4 5.3 %collective-permute-start = (bf16[128,256]{1,0:T(8,128)(2,1)S(1)}, bf16[128,256]{1,0:T(8,128)(2,1)S(1)}, u32[]{:S(2)}, u32[]{:S(2)}) collective-permute-start(bf16[128,256]{1,0:T(8,128)(2,1)S(1)} %get-tuple-element.20), channel_id=1, source_target_pairs={{0,8},{1,5},{2,6},{3,11},{4,24},{5,21},{6,22},{7,27},{8,12},{9,1},... | collective-permute-start | bytes 196616 | tf_op jit(solution)/shard_map/ppermute | solution.py:279
  1.5 7.9 %collective-permute-start.3 = (bf16[576,128]{1,0:T(8,128)(2,1)S(1)}, bf16[576,128]{1,0:T(8,128)(2,1)S(1)}, u32[]{:S(2)}, u32[]{:S(2)}) collective-permute-start(bf16[576,128]{1,0:T(8,128)(2,1)S(1)} %get-tuple-element.24), channel_id=1, source_target_pairs={{0,24},{4,28},{8,16},{12,20},{16,8},{20,12},{24,0},{28,4},{1,25},{... | collective-permute-start | bytes 442376 | tf_op jit(solution)/shard_map/ppermute | solution.py:281
  3.4 9.1 %collective-permute-start.4 = (bf16[576,128]{1,0:T(8,128)(2,1)S(1)}, bf16[576,128]{1,0:T(8,128)(2,1)S(1)}, u32[]{:S(2)}, u32[]{:S(2)}) collective-permute-start(bf16[576,128]{1,0:T(8,128)(2,1)S(1)} %get-tuple-element.25), channel_id=1, source_target_pairs={{0,8},{4,20},{8,0},{12,28},{16,24},{20,4},{24,16},{28,12},{1,9},{5... | collective-permute-start | bytes 442376 | tf_op jit(solution)/shard_map/ppermute | solution.py:281
  3.5 9.3 %collective-permute-start.5 = (bf16[576,128]{1,0:T(8,128)(2,1)S(1)}, bf16[576,128]{1,0:T(8,128)(2,1)S(1)}, u32[]{:S(2)}, u32[]{:S(2)}) collective-permute-start(bf16[576,128]{1,0:T(8,128)(2,1)S(1)} %get-tuple-element.26), channel_id=1, source_target_pairs={{0,16},{4,12},{8,24},{12,4},{16,0},{20,28},{24,8},{28,20},{1,17},{... | collective-permute-start | bytes 442376 | tf_op jit(solution)/shard_map/ppermute | solution.py:281
  7.1 6.5 %collective-permute-start.1 = (bf16[64,640]{1,0:T(8,128)(2,1)S(1)}, bf16[64,640]{1,0:T(8,128)(2,1)S(1)}, u32[]{:S(2)}, u32[]{:S(2)}) collective-permute-start(bf16[64,640]{1,0:T(8,128)(2,1)S(1)} %get-tuple-element.21), channel_id=1, source_target_pairs={{8,4},{5,12},{6,0},{11,8},{24,20},{21,28},{22,16},{27,24},{12,5},{... | collective-permute-start | bytes 245768 | tf_op jit(solution)/shard_map/ppermute | solution.py:304
  7.2 6.5 %collective-permute-start.2 = (bf16[64,640]{1,0:T(8,128)(2,1)S(1)}, bf16[64,640]{1,0:T(8,128)(2,1)S(1)}, u32[]{:S(2)}, u32[]{:S(2)}) collective-permute-start(bf16[64,640]{1,0:T(8,128)(2,1)S(1)} %get-tuple-element.22), channel_id=1, source_target_pairs={{8,12},{5,4},{6,8},{11,0},{24,28},{21,20},{22,24},{27,16},{12,13},... | collective-permute-start | bytes 245768 | tf_op jit(solution)/shard_map/ppermute | solution.py:304
  9.7 4.8 %collective-permute-start.6 = (bf16[2,576,128]{2,1,0:T(8,128)(2,1)S(1)}, bf16[2,576,128]{2,1,0:T(8,128)(2,1)S(1)}, u32[]{:S(2)}, u32[]{:S(2)}) collective-permute-start(bf16[2,576,128]{2,1,0:T(8,128)(2,1)S(1)} %shard_map.67), channel_id=1, source_target_pairs={{0,4},{4,0},{8,12},{12,8},{16,20},{20,16},{24,28},{28,24},{1,5},{5... | collective-permute-start | bytes 884744 | tf_op jit(solution)/shard_map/ppermute | solution.py:293
  12.5 2.0 %collective-permute-start.7 = (bf16[576,128]{1,0:T(8,128)(2,1)S(1)}, bf16[576,128]{1,0:T(8,128)(2,1)S(1)}, u32[]{:S(2)}, u32[]{:S(2)}) collective-permute-start(bf16[576,128]{1,0:T(8,128)(2,1)S(1)} %collective-permute-done.4.refs_4_), channel_id=1, source_target_pairs={{0,4},{4,0},{8,12},{12,8},{16,20},{20,16},{24,28},{28,24},{1,5},{5... | collective-permute-start | bytes 442376 | tf_op jit(solution)/shard_map/ppermute | solution.py:293
  12.8 1.7 %collective-permute-start.8 = (bf16[576,128]{1,0:T(8,128)(2,1)S(1)}, bf16[576,128]{1,0:T(8,128)(2,1)S(1)}, u32[]{:S(2)}, u32[]{:S(2)}) collective-permute-start(bf16[576,128]{1,0:T(8,128)(2,1)S(1)} %collective-permute-done.5.refs_5_), channel_id=1, source_target_pairs={{0,4},{4,0},{8,12},{12,8},{16,20},{20,16},{24,28},{28,24},{1,5},{5... | collective-permute-start | bytes 442376 | tf_op jit(solution)/shard_map/ppermute | solution.py:293
  13.7 11.6 %copy-start = (bf16[16,512,128]{2,1,0:T(8,128)(2,1)S(1)}, bf16[16,512,128]{2,1,0:T(8,128)(2,1)}, u32[]{:S(2)}) copy-start(bf16[16,512,128]{2,1,0:T(8,128)(2,1)} %w_ref.3) | copy-start | bytes 6291460
  15.2 7.7 %collective-permute-start.10 = (bf16[64,512]{1,0:T(8,128)(2,1)S(1)}, bf16[64,512]{1,0:T(8,128)(2,1)S(1)}, u32[]{:S(2)}, u32[]{:S(2)}) collective-permute-start(bf16[64,512]{1,0:T(8,128)(2,1)S(1)} %get-tuple-element.32), channel_id=1, source_target_pairs={{4,0},{12,1},{0,2},{8,3},{20,4},{28,5},{16,6},{24,7},{5,8},{13,9},... | collective-permute-start | bytes 196616 | tf_op jit(solution)/shard_map/ppermute | solution.py:334
  18.7 6.6 %collective-permute-start.9 = (bf16[64,512]{1,0:T(8,128)(2,1)S(1)}, bf16[64,512]{1,0:T(8,128)(2,1)S(1)}, u32[]{:S(2)}, u32[]{:S(2)}) collective-permute-start(bf16[64,512]{1,0:T(8,128)(2,1)S(1)} %get-tuple-element.31), channel_id=1, source_target_pairs={{12,0},{4,1},{8,2},{0,3},{28,4},{20,5},{24,6},{16,7},{13,8},{5,9},... | collective-permute-start | bytes 196616 | tf_op jit(solution)/shard_map/ppermute | solution.py:334

commit v32 on v29

--- a/solution.py
+++ b/solution.py
@@ -96,7 +96,8 @@
         move.wait()
 
 
-def absorb_kernel(per_device, w_ref, packed_ref, *outs):
+def absorb_kernel(per_device, w_ref, packed_ref, block_ref, *outs):
+    del block_ref
     heads = w_ref.shape[0]
     piece = SPEC * heads
     nope = packed_ref[:, :NOPE]
@@ -270,6 +271,16 @@
         cost_estimate=LONG,
     )(*[in_hbm(x) for x in (jnp.swapaxes(cache, 1, 2), queries, new_latent, lengths)])
     moved = lax.ppermute(packed, both, [(flat(i, j), host(i, j)) for i, j in devices])
+    *pieces, picked[-1] = pl.pallas_call(
+        functools.partial(absorb_kernel, per_device),
+        out_shape=[jax.ShapeDtypeStruct((piece, width + ROPE), cache.dtype)] * per_device
+        + [jax.ShapeDtypeStruct((width, slots), cache.dtype)],
+        in_specs=[vmem] * 2 + [anywhere],
+        out_specs=[vmem] * per_device + [anywhere],
+        input_output_aliases={2: per_device},
+        compiler_params=params,
+        cost_estimate=LONG,
+    )(w_uk, moved, picked[-1])
     own_keys = [picked[0]] + [
         lax.ppermute(picked[k], "seq", in_plane(lambda g, t: (g ^ partner(k, t)) * COPIES + t))
         for k in range(1, owners)
@@ -285,14 +296,6 @@
     other_core = in_plane(lambda g, t: g * COPIES + 1 - t)
     far_keys = [lax.ppermute(keys, "seq", other_core) for keys in [pair] + own_keys[2:]]
 
-    pieces = pl.pallas_call(
-        functools.partial(absorb_kernel, per_device),
-        out_shape=[jax.ShapeDtypeStruct((piece, width + ROPE), cache.dtype)] * per_device,
-        in_specs=[vmem] * 2,
-        out_specs=[vmem] * per_device,
-        compiler_params=params,
-        cost_estimate=LONG,
-    )(w_uk, moved)
     arrived = [
         lax.ppermute(
             pieces[k],

time: 26.5 us -> 28.3 us (1.068)
  waiting for transfers between devices: 12.1 us -> 14.6 us
  starting transfers between devices: 9.42 us -> 8.69 us
    ppermute x2, starting transfers between devices: 3.86 us -> 5.55 us  [whole_sequences(): lax.ppermute(latent[k], both, [(owner(i, j, first_back(i // COPIES, j) ^...]
    ppermute x1, waiting for transfers between devices: 1.63 us -> 3.15 us  [whole_sequences(): lax.ppermute(packed, both, [(flat(i, j), host(i, j)) for i, j in devices])]
    ppermute x3, starting transfers between devices: 3.55 us -> 2.1 us  [whole_sequences(): lax.ppermute(picked[k], 'seq', in_plane(lambda g, t: (g ^ partner(k, t))...]
    ppermute x3, starting transfers between devices: 1.81 us -> 0.51 us  [whole_sequences(): lax.ppermute(keys, 'seq', other_core)]
    ppermute x2, waiting for transfers between devices: 0.73 us -> 1.42 us  [whole_sequences(): lax.ppermute(pieces[k], both, [(host(i, j), owner(i, j, leaves_as(k, j)))...]
    ppermute x3, waiting for transfers between devices: 3.54 us -> 4.19 us  [whole_sequences(): lax.ppermute(picked[k], 'seq', in_plane(lambda g, t: (g ^ partner(k, t))...]
    ppermute x2, waiting for transfers between devices: 6.18 us -> 5.81 us  [whole_sequences(): lax.ppermute(latent[k], both, [(owner(i, j, first_back(i // COPIES, j) ^...]
    ppermute x2, starting transfers between devices: 0.13 us -> 0.46 us  [whole_sequences(): lax.ppermute(pieces[k], both, [(host(i, j), owner(i, j, leaves_as(k, j)))...]
where the time goes in v32:
time: 28.3 us; the launch traced here: 28.1 us
  waiting for transfers between devices  14.6 us (52%)
  starting transfers between devices  8.69 us (31%)
  Pallas kernels  4.76 us (17%)
    ppermute x2, waiting for transfers between devices, whole_sequences(): lax.ppermute(latent[k], both, [(owner(i, j, first_back(i // COPIES, j) ^...  5.81 us
    ppermute x2, starting transfers between devices, whole_sequences(): lax.ppermute(latent[k], both, [(owner(i, j, first_back(i // COPIES, j) ^...  5.55 us
    ppermute x3, waiting for transfers between devices, whole_sequences(): lax.ppermute(picked[k], 'seq', in_plane(lambda g, t: (g ^ partner(k, t))...  4.19 us
    ppermute x1, waiting for transfers between devices, whole_sequences(): lax.ppermute(packed, both, [(flat(i, j), host(i, j)) for i, j in devices])  3.15 us
    ppermute x3, starting transfers between devices, whole_sequences(): lax.ppermute(picked[k], 'seq', in_plane(lambda g, t: (g ^ partner(k, t))...  2.1 us
    ppermute x2, waiting for transfers between devices, whole_sequences(): lax.ppermute(pieces[k], both, [(host(i, j), owner(i, j, leaves_as(k, j)))...  1.42 us
    pallas_call x1, Pallas kernels, whole_sequences(): pl.pallas_call(functools.partial(pick_kernel, per_device), out_shape=[jax...  1.37 us
    pallas_call x1, Pallas kernels, whole_sequences(): pl.pallas_call(functools.partial(project_kernel, per_device), out_shape=j...  1.06 us
  transfers between devices with their start and end apart: 11, of which 7 were waited for; matrix products, arithmetic and copies ran while one was open for 0% of the time, Pallas kernels for 6%

profile of v32, /device:TPU:6, one launch (start us, length us, event | category | flops | bytes accessed | tf_op | source)
XLA Modules:
  0.0 28.1 jit_solution(2490784443200456975)
XLA Ops:
  0.0 1.4 %shard_map.64 = (bf16[576,128]{1,0:T(8,128)(2,1)S(1)}, bf16[576,128]{1,0:T(8,128)(2,1)S(1)}, bf16[576,128]{1,0:T(8,128)(2,1)S(1)}, bf16[576,128]{1,0:T(8,128)(2,...) custom-call(bf16[4,576,128]{2,1,0:T(8,128)(2,1)} %bitcast.1, bf16[8,16,192]{2,1,0:T(8,128)(2,1)} %q_hbm.1, ...), custom_call_target="tpu_custom_call" | custom-call | flops 20000000000 | tf_op jit(solution)/shard_map/pallas_call | solution.py:255
  1.4 0.1 collective-permute-start
  1.5 2.0 %collective-permute-start.3 = (bf16[576,128]{1,0:T(8,128)(2,1)S(1)}, bf16[576,128]{1,0:T(8,128)(2,1)S(1)}, u32[]{:S(2)}, u32[]{:S(2)}) collective-permute-start(bf16[576,128]{1,0:T(8,128)(2,1)S(1)} %get-tuple-element.26), channel_id=1, source_target_pairs={{0,24},{4,28},{8,16},{12,20},{16,8},{20,12},{24,0},{28,4},{1,25},{... | collective-permute-start | bytes 442376 | tf_op jit(solution)/shard_map/ppermute | solution.py:285
  3.4 0.1 collective-permute-start.4
  3.5 3.2 %collective-permute-done.packed_ref = bf16[128,256]{1,0:T(8,128)(2,1)S(1)} collective-permute-done((bf16[128,256]{1,0:T(8,128)(2,1)S(1)}, bf16[128,256]{1,0:T(8,128)(2,1)S(1)}, u32[]{:S(2)}, u32[]{:S(2)}) %collective-permute-start) | collective-permute-done | bytes 65568 | tf_op jit(solution)/shard_map/ppermute | solution.py:273
  6.6 0.5 %shard_map.65 = (bf16[64,640]{1,0:T(8,128)(2,1)S(1)}, bf16[64,640]{1,0:T(8,128)(2,1)S(1)}, bf16[576,128]{1,0:T(8,128)(2,1)S(1)}) custom-call(bf16[16,128,512]{2,1,0:T(8,128)(2,1)S(1)} %copy-done.1, bf16[128,256]{1,0:T(8,128)(2,1)S(1)} %collective-permute-done.packed_ref, ...), custom_call_target="tpu_custom_call", output_to_operand_aliasing={{2}: (2, {})} | custom-call | flops 20000000000 | tf_op jit(solution)/shard_map/pallas_call | solution.py:274
  7.1 0.1 collective-permute-start.5
  7.2 0.1 collective-permute-start.1
  7.3 0.4 %collective-permute-start.2 = (bf16[64,640]{1,0:T(8,128)(2,1)S(1)}, bf16[64,640]{1,0:T(8,128)(2,1)S(1)}, u32[]{:S(2)}, u32[]{:S(2)}) collective-permute-start(bf16[64,640]{1,0:T(8,128)(2,1)S(1)} %get-tuple-element.24), channel_id=1, source_target_pairs={{8,12},{5,4},{6,8},{11,0},{24,28},{21,20},{22,24},{27,16},{12,13},... | collective-permute-start | bytes 245768 | tf_op jit(solution)/shard_map/ppermute | solution.py:300
  7.7 1.6 %collective-permute-done.3.refs_3_.second_ref = bf16[576,128]{1,0:T(8,128)(2,1)S(1)} collective-permute-done((bf16[576,128]{1,0:T(8,128)(2,1)S(1)}, bf16[576,128]{1,0:T(8,128)(2,1)S(1)}, u32[]{:S(2)}, u32[]{:S(2)}) %collective-permute-start.3) | collective-permute-done | bytes 147488 | tf_op jit(solution)/shard_map/ppermute | solution.py:285
  9.3 0.4 %shard_map.67 = bf16[2,576,128]{2,1,0:T(8,128)(2,1)S(1)} custom-call(bf16[576,128]{1,0:T(8,128)(2,1)S(1)} %get-tuple-element.25.refs_2_.first_ref, bf16[576,128]{1,0:T(8,128)(2,1)S(1)} %collective-permute-done.3.refs_3_.second_ref), custom_call_target="tpu_custom_call" | custom-call | tf_op jit(solution)/shard_map/pallas_call | solution.py:288
  9.7 0.4 %collective-permute-start.6 = (bf16[2,576,128]{2,1,0:T(8,128)(2,1)S(1)}, bf16[2,576,128]{2,1,0:T(8,128)(2,1)S(1)}, u32[]{:S(2)}, u32[]{:S(2)}) collective-permute-start(bf16[2,576,128]{2,1,0:T(8,128)(2,1)S(1)} %shard_map.67), channel_id=1, source_target_pairs={{0,4},{4,0},{8,12},{12,8},{16,20},{20,16},{24,28},{28,24},{1,5},{5... | collective-permute-start | bytes 884744 | tf_op jit(solution)/shard_map/ppermute | solution.py:297
  10.1 2.1 %collective-permute-done.4.refs_4_ = bf16[576,128]{1,0:T(8,128)(2,1)S(1)} collective-permute-done((bf16[576,128]{1,0:T(8,128)(2,1)S(1)}, bf16[576,128]{1,0:T(8,128)(2,1)S(1)}, u32[]{:S(2)}, u32[]{:S(2)}) %collective-permute-start.4) | collective-permute-done | bytes 147488 | tf_op jit(solution)/shard_map/ppermute | solution.py:285
  12.3 0.4 %collective-permute-done.5.refs_5_ = bf16[576,128]{1,0:T(8,128)(2,1)S(1)} collective-permute-done((bf16[576,128]{1,0:T(8,128)(2,1)S(1)}, bf16[576,128]{1,0:T(8,128)(2,1)S(1)}, u32[]{:S(2)}, u32[]{:S(2)}) %collective-permute-start.5) | collective-permute-done | bytes 147488 | tf_op jit(solution)/shard_map/ppermute | solution.py:285
  12.7 0.1 collective-permute-start.8
  12.8 1.4 %collective-permute-done.1.refs_0_ = bf16[64,640]{1,0:T(8,128)(2,1)S(1)} collective-permute-done((bf16[64,640]{1,0:T(8,128)(2,1)S(1)}, bf16[64,640]{1,0:T(8,128)(2,1)S(1)}, u32[]{:S(2)}, u32[]{:S(2)}) %collective-permute-start.1) | collective-permute-done | bytes 81952 | tf_op jit(solution)/shard_map/ppermute | solution.py:300
  14.2 0.0 collective-permute-done.2.refs_1_
  14.2 0.8 %shard_map.66 = (bf16[128,576]{1,0:T(8,128)(2,1)S(1)}, f32[128,128]{1,0:T(8,128)S(1)}, f32[128,128]{1,0:T(8,128)S(1)}, f32[128,512]{1,0:T(8,128)S(1)}) custom-call(s32[8,128]{1,0:T(8,128)S(1)} %get-tuple-element.20.limit_ref, bf16[64,640]{1,0:T(8,128)(2,1)S(1)} %collective-permute-done.1.refs_0_, bf16[64,640]{1,0:T(8,128)(2,1)S(1)} %collective-permute-done.2.refs_1_, ...), custom_call_target="tpu_custom_call" | custom-call | flops 20000000000 | tf_op jit(solution)/shard_map/pallas_call | solution.py:308
  15.0 0.7 %shard_map.68 = (bf16[64,512]{1,0:T(8,128)(2,1)S(1)}, bf16[64,512]{1,0:T(8,128)(2,1)S(1)}) custom-call(s32[8,128]{1,0:T(8,128)S(1)} %get-tuple-element.20.limit_ref, bf16[128,576]{1,0:T(8,128)(2,1)S(1)} %get-tuple-element.29.q_ref, f32[128,128]{1,0:T(8,128)S(1)} %get-tuple-element.30.top_ref, f32[128,128]{1,0:T(8,128)S(1)} %get-tuple-element.31.total_ref, ...), custom_call_target="tpu_custom_call" | custom-call | tf_op jit(solution)/shard_map/pallas_call | solution.py:321
  15.7 5.0 %collective-permute-start.10 = (bf16[64,512]{1,0:T(8,128)(2,1)S(1)}, bf16[64,512]{1,0:T(8,128)(2,1)S(1)}, u32[]{:S(2)}, u32[]{:S(2)}) collective-permute-start(bf16[64,512]{1,0:T(8,128)(2,1)S(1)} %get-tuple-element.34), channel_id=1, source_target_pairs={{4,0},{12,1},{0,2},{8,3},{20,4},{28,5},{16,6},{24,7},{5,8},{13,9},... | collective-permute-start | bytes 196616 | tf_op jit(solution)/shard_map/ppermute | solution.py:330
  20.7 0.6 %collective-permute-start.9 = (bf16[64,512]{1,0:T(8,128)(2,1)S(1)}, bf16[64,512]{1,0:T(8,128)(2,1)S(1)}, u32[]{:S(2)}, u32[]{:S(2)}) collective-permute-start(bf16[64,512]{1,0:T(8,128)(2,1)S(1)} %get-tuple-element.33), channel_id=1, source_target_pairs={{12,0},{4,1},{8,2},{0,3},{28,4},{20,5},{24,6},{16,7},{13,8},{5,9},... | collective-permute-start | bytes 196616 | tf_op jit(solution)/shard_map/ppermute | solution.py:330
  21.3 2.2 %collective-permute-done.10.refs_1_ = bf16[64,512]{1,0:T(8,128)(2,1)S(1)} collective-permute-done((bf16[64,512]{1,0:T(8,128)(2,1)S(1)}, bf16[64,512]{1,0:T(8,128)(2,1)S(1)}, u32[]{:S(2)}, u32[]{:S(2)}) %collective-permute-start.10) | collective-permute-done | bytes 65568 | tf_op jit(solution)/shard_map/ppermute | solution.py:330
  23.5 3.6 %collective-permute-done.9.refs_0_ = bf16[64,512]{1,0:T(8,128)(2,1)S(1)} collective-permute-done((bf16[64,512]{1,0:T(8,128)(2,1)S(1)}, bf16[64,512]{1,0:T(8,128)(2,1)S(1)}, u32[]{:S(2)}, u32[]{:S(2)}) %collective-permute-start.9) | collective-permute-done | bytes 65568 | tf_op jit(solution)/shard_map/ppermute | solution.py:330
  27.1 1.1 %shard_map.69 = bf16[8,16,128]{2,1,0:T(8,128)(2,1)} custom-call(bf16[16,512,128]{2,1,0:T(8,128)(2,1)S(1)} %copy-done, bf16[64,512]{1,0:T(8,128)(2,1)S(1)} %collective-permute-done.9.refs_0_, bf16[64,512]{1,0:T(8,128)(2,1)S(1)} %collective-permute-done.10.refs_1_), custom_call_target="tpu_custom_call" | custom-call | tf_op jit(solution)/shard_map/pallas_call | solution.py:337
  (8 shorter events, 0.0 us)
Async XLA Ops:
  0.0 6.6 %copy-start.1 = (bf16[16,128,512]{2,1,0:T(8,128)(2,1)S(1)}, bf16[16,128,512]{2,1,0:T(8,128)(2,1)}, u32[]{:S(2)}) copy-start(bf16[16,128,512]{2,1,0:T(8,128)(2,1)} %w_ref.2) | copy-start | bytes 6291460
  1.4 5.3 %collective-permute-start = (bf16[128,256]{1,0:T(8,128)(2,1)S(1)}, bf16[128,256]{1,0:T(8,128)(2,1)S(1)}, u32[]{:S(2)}, u32[]{:S(2)}) collective-permute-start(bf16[128,256]{1,0:T(8,128)(2,1)S(1)} %get-tuple-element.21), channel_id=1, source_target_pairs={{0,8},{1,5},{2,6},{3,11},{4,24},{5,21},{6,22},{7,27},{8,12},{9,1},... | collective-permute-start | bytes 196616 | tf_op jit(solution)/shard_map/ppermute | solution.py:273
  1.5 7.9 %collective-permute-start.3 = (bf16[576,128]{1,0:T(8,128)(2,1)S(1)}, bf16[576,128]{1,0:T(8,128)(2,1)S(1)}, u32[]{:S(2)}, u32[]{:S(2)}) collective-permute-start(bf16[576,128]{1,0:T(8,128)(2,1)S(1)} %get-tuple-element.26), channel_id=1, source_target_pairs={{0,24},{4,28},{8,16},{12,20},{16,8},{20,12},{24,0},{28,4},{1,25},{... | collective-permute-start | bytes 442376 | tf_op jit(solution)/shard_map/ppermute | solution.py:285
  3.4 8.8 %collective-permute-start.4 = (bf16[576,128]{1,0:T(8,128)(2,1)S(1)}, bf16[576,128]{1,0:T(8,128)(2,1)S(1)}, u32[]{:S(2)}, u32[]{:S(2)}) collective-permute-start(bf16[576,128]{1,0:T(8,128)(2,1)S(1)} %get-tuple-element.27), channel_id=1, source_target_pairs={{0,8},{4,20},{8,0},{12,28},{16,24},{20,4},{24,16},{28,12},{1,9},{5... | collective-permute-start | bytes 442376 | tf_op jit(solution)/shard_map/ppermute | solution.py:285
  7.1 5.5 %collective-permute-start.5 = (bf16[576,128]{1,0:T(8,128)(2,1)S(1)}, bf16[576,128]{1,0:T(8,128)(2,1)S(1)}, u32[]{:S(2)}, u32[]{:S(2)}) collective-permute-start(bf16[576,128]{1,0:T(8,128)(2,1)S(1)} %get-tuple-element.28), channel_id=1, source_target_pairs={{0,16},{4,12},{8,24},{12,4},{16,0},{20,28},{24,8},{28,20},{1,17},{... | collective-permute-start | bytes 442376 | tf_op jit(solution)/shard_map/ppermute | solution.py:285
  7.2 7.0 %collective-permute-start.1 = (bf16[64,640]{1,0:T(8,128)(2,1)S(1)}, bf16[64,640]{1,0:T(8,128)(2,1)S(1)}, u32[]{:S(2)}, u32[]{:S(2)}) collective-permute-start(bf16[64,640]{1,0:T(8,128)(2,1)S(1)} %get-tuple-element.23), channel_id=1, source_target_pairs={{8,4},{5,12},{6,0},{11,8},{24,20},{21,28},{22,16},{27,24},{12,5},{... | collective-permute-start | bytes 245768 | tf_op jit(solution)/shard_map/ppermute | solution.py:300
  7.3 6.9 %collective-permute-start.2 = (bf16[64,640]{1,0:T(8,128)(2,1)S(1)}, bf16[64,640]{1,0:T(8,128)(2,1)S(1)}, u32[]{:S(2)}, u32[]{:S(2)}) collective-permute-start(bf16[64,640]{1,0:T(8,128)(2,1)S(1)} %get-tuple-element.24), channel_id=1, source_target_pairs={{8,12},{5,4},{6,8},{11,0},{24,28},{21,20},{22,24},{27,16},{12,13},... | collective-permute-start | bytes 245768 | tf_op jit(solution)/shard_map/ppermute | solution.py:300
  9.7 5.3 %collective-permute-start.6 = (bf16[2,576,128]{2,1,0:T(8,128)(2,1)S(1)}, bf16[2,576,128]{2,1,0:T(8,128)(2,1)S(1)}, u32[]{:S(2)}, u32[]{:S(2)}) collective-permute-start(bf16[2,576,128]{2,1,0:T(8,128)(2,1)S(1)} %shard_map.67), channel_id=1, source_target_pairs={{0,4},{4,0},{8,12},{12,8},{16,20},{20,16},{24,28},{28,24},{1,5},{5... | collective-permute-start | bytes 884744 | tf_op jit(solution)/shard_map/ppermute | solution.py:297
  12.3 2.7 %collective-permute-start.7 = (bf16[576,128]{1,0:T(8,128)(2,1)S(1)}, bf16[576,128]{1,0:T(8,128)(2,1)S(1)}, u32[]{:S(2)}, u32[]{:S(2)}) collective-permute-start(bf16[576,128]{1,0:T(8,128)(2,1)S(1)} %collective-permute-done.4.refs_4_), channel_id=1, source_target_pairs={{0,4},{4,0},{8,12},{12,8},{16,20},{20,16},{24,28},{28,24},{1,5},{5... | collective-permute-start | bytes 442376 | tf_op jit(solution)/shard_map/ppermute | solution.py:297
  12.7 2.3 %collective-permute-start.8 = (bf16[576,128]{1,0:T(8,128)(2,1)S(1)}, bf16[576,128]{1,0:T(8,128)(2,1)S(1)}, u32[]{:S(2)}, u32[]{:S(2)}) collective-permute-start(bf16[576,128]{1,0:T(8,128)(2,1)S(1)} %collective-permute-done.5.refs_5_), channel_id=1, source_target_pairs={{0,4},{4,0},{8,12},{12,8},{16,20},{20,16},{24,28},{28,24},{1,5},{5... | collective-permute-start | bytes 442376 | tf_op jit(solution)/shard_map/ppermute | solution.py:297
  14.2 12.9 %copy-start = (bf16[16,512,128]{2,1,0:T(8,128)(2,1)S(1)}, bf16[16,512,128]{2,1,0:T(8,128)(2,1)}, u32[]{:S(2)}) copy-start(bf16[16,512,128]{2,1,0:T(8,128)(2,1)} %w_ref.3) | copy-start | bytes 6291460
  15.7 7.7 %collective-permute-start.10 = (bf16[64,512]{1,0:T(8,128)(2,1)S(1)}, bf16[64,512]{1,0:T(8,128)(2,1)S(1)}, u32[]{:S(2)}, u32[]{:S(2)}) collective-permute-start(bf16[64,512]{1,0:T(8,128)(2,1)S(1)} %get-tuple-element.34), channel_id=1, source_target_pairs={{4,0},{12,1},{0,2},{8,3},{20,4},{28,5},{16,6},{24,7},{5,8},{13,9},... | collective-permute-start | bytes 196616 | tf_op jit(solution)/shard_map/ppermute | solution.py:330
  20.7 6.4 %collective-permute-start.9 = (bf16[64,512]{1,0:T(8,128)(2,1)S(1)}, bf16[64,512]{1,0:T(8,128)(2,1)S(1)}, u32[]{:S(2)}, u32[]{:S(2)}) collective-permute-start(bf16[64,512]{1,0:T(8,128)(2,1)S(1)} %get-tuple-element.33), channel_id=1, source_target_pairs={{12,0},{4,1},{8,2},{0,3},{28,4},{20,5},{24,6},{16,7},{13,8},{5,9},... | collective-permute-start | bytes 196616 | tf_op jit(solution)/shard_map/ppermute | solution.py:330

commit v33 on v29

--- a/solution.py
+++ b/solution.py
@@ -178,31 +178,25 @@
 
 
 def finish_kernel(
-    owners, per_device, limit_ref, q_ref, top_ref, total_ref, part_ref, pair_ref, *refs
+    owners, place, limit_ref, q_ref, top_ref, total_ref, part_ref, pair_ref, *refs
 ):
     key_refs = [pair_ref.at[0], pair_ref.at[1], *refs[: owners - 2]]
-    outs = refs[owners - 2 :]
+    out_ref = refs[owners - 2]
     seq_index = lax.axis_index("seq")
     chip, core = seq_index // COPIES, seq_index % COPIES
     plane = lax.axis_index("head")
     slots = key_refs[0].shape[1]
+    piece = out_ref.shape[0]
+    rows = pl.ds(pl.multiple_of((first_block(plane, chip, core) ^ place) * piece, piece), piece)
     starts = [((chip ^ partner(k, 1 - core)) * COPIES + 1 - core) * slots for k in range(owners)]
-    s = block_scores(q_ref[...], key_refs, starts, limit_ref)
-    first = top_ref[:, :1]
+    s = block_scores(q_ref[rows, :], key_refs, starts, limit_ref)
+    first = top_ref[rows, :][:, :1]
     top = jnp.maximum(first, jnp.max(s, axis=1, keepdims=True))
     total, out = weigh(s, key_refs, top)
     scale = jnp.exp(first - top)
-    total += total_ref[:, :1] * scale
-    out += part_ref[...] * scale
-    out = (out * (1.0 / total)).astype(jnp.bfloat16)
-    piece = out.shape[0] // per_device
-    sent_first = first_block(plane, chip, core)
-    for k in range(per_device):
-        for n in range(per_device):
-
-            @pl.when(sent_first ^ k == n)
-            def _():
-                outs[k][...] = out[n * piece : (n + 1) * piece]
+    total += total_ref[rows, :][:, :1] * scale
+    out += part_ref[rows, :] * scale
+    out_ref[...] = (out * (1.0 / total)).astype(out_ref.dtype)
 
 
 def project_kernel(per_device, w_ref, *refs):
@@ -315,13 +309,17 @@
         compiler_params=params,
         cost_estimate=LONG,
     )(limit, *arrived, *own_keys)
-    latent = pl.pallas_call(
-        functools.partial(finish_kernel, owners, per_device),
-        out_shape=[jax.ShapeDtypeStruct((piece, LATENT), jnp.bfloat16)] * per_device,
-        in_specs=[vmem] * (1 + len(state) + len(far_keys)),
-        out_specs=[vmem] * per_device,
-        compiler_params=params,
-    )(limit, *state, *far_keys)
+    latent = [
+        pl.pallas_call(
+            functools.partial(finish_kernel, owners, k),
+            out_shape=jax.ShapeDtypeStruct((piece, LATENT), jnp.bfloat16),
+            in_specs=[vmem] * (1 + len(state) + len(far_keys)),
+            out_specs=vmem,
+            compiler_params=params,
+            cost_estimate=LONG if k else None,
+        )(limit, *state, *far_keys)
+        for k in range(per_device)
+    ]
 
     back = [
         lax.ppermute(

time: 26.5 us -> 27.1 us (1.023)
  Pallas kernels: 4.74 us -> 5.33 us
    pallas_call x1 -> x2, Pallas kernels: 0.71 us -> 1.29 us  [whole_sequences(): pl.pallas_call(functools.partial(finish_kernel, owners, k), out_shape=jax...]
  transfers between devices with their start and end apart: 11 -> 11, of which waited for: 7 -> 7; matrix products, arithmetic and copies ran while one was open for 0% -> 0% of each run, Pallas kernels for 6% -> 8%
where the time goes in v33:
time: 27.1 us; the launch traced here: 27 us
  waiting for transfers between devices  12.1 us (45%)
  starting transfers between devices  9.47 us (35%)
  Pallas kernels  5.33 us (20%)
    ppermute x2, waiting for transfers between devices, whole_sequences(): lax.ppermute(latent[k], both, [(owner(i, j, first_back(i // COPIES, j) ^...  6.18 us
    ppermute x2, starting transfers between devices, whole_sequences(): lax.ppermute(latent[k], both, [(owner(i, j, first_back(i // COPIES, j) ^...  3.91 us
    ppermute x3, starting transfers between devices, whole_sequences(): lax.ppermute(picked[k], 'seq', in_plane(lambda g, t: (g ^ partner(k, t))...  3.55 us
    ppermute x3, waiting for transfers between devices, whole_sequences(): lax.ppermute(picked[k], 'seq', in_plane(lambda g, t: (g ^ partner(k, t))...  3.52 us
    ppermute x3, starting transfers between devices, whole_sequences(): lax.ppermute(keys, 'seq', other_core)  1.81 us
    ppermute x1, waiting for transfers between devices, whole_sequences(): lax.ppermute(packed, both, [(flat(i, j), host(i, j)) for i, j in devices])  1.63 us
    pallas_call x1, Pallas kernels, whole_sequences(): pl.pallas_call(functools.partial(pick_kernel, per_device), out_shape=[jax...  1.37 us
    pallas_call x2, Pallas kernels, whole_sequences(): pl.pallas_call(functools.partial(finish_kernel, owners, k), out_shape=jax...  1.29 us
  transfers between devices with their start and end apart: 11, of which 7 were waited for; matrix products, arithmetic and copies ran while one was open for 0% of the time, Pallas kernels for 8%

profile of v33, /device:TPU:6, one launch (start us, length us, event | category | flops | bytes accessed | tf_op | source)
XLA Modules:
  0.0 27.0 jit_solution(11266826971398429280)
XLA Ops:
  0.0 1.4 %shard_map.64 = (bf16[576,128]{1,0:T(8,128)(2,1)S(1)}, bf16[576,128]{1,0:T(8,128)(2,1)S(1)}, bf16[576,128]{1,0:T(8,128)(2,1)S(1)}, bf16[576,128]{1,0:T(8,128)(2,...) custom-call(bf16[4,576,128]{2,1,0:T(8,128)(2,1)} %bitcast.1, bf16[8,16,192]{2,1,0:T(8,128)(2,1)} %q_hbm.1, ...), custom_call_target="tpu_custom_call" | custom-call | flops 20000000000 | tf_op jit(solution)/shard_map/pallas_call | solution.py:248
  1.5 2.0 %collective-permute-start.3 = (bf16[576,128]{1,0:T(8,128)(2,1)S(1)}, bf16[576,128]{1,0:T(8,128)(2,1)S(1)}, u32[]{:S(2)}, u32[]{:S(2)}) collective-permute-start(bf16[576,128]{1,0:T(8,128)(2,1)S(1)} %get-tuple-element.22), channel_id=1, source_target_pairs={{0,24},{4,28},{8,16},{12,20},{16,8},{20,12},{24,0},{28,4},{1,25},{... | collective-permute-start | bytes 442376 | tf_op jit(solution)/shard_map/ppermute | solution.py:268
  3.4 0.1 collective-permute-start.4
  3.5 1.5 %collective-permute-start.5 = (bf16[576,128]{1,0:T(8,128)(2,1)S(1)}, bf16[576,128]{1,0:T(8,128)(2,1)S(1)}, u32[]{:S(2)}, u32[]{:S(2)}) collective-permute-start(bf16[576,128]{1,0:T(8,128)(2,1)S(1)} %get-tuple-element.24), channel_id=1, source_target_pairs={{0,16},{4,12},{8,24},{12,4},{16,0},{20,28},{24,8},{28,20},{1,17},{... | collective-permute-start | bytes 442376 | tf_op jit(solution)/shard_map/ppermute | solution.py:268
  5.0 1.6 %collective-permute-done.packed_ref = bf16[128,256]{1,0:T(8,128)(2,1)S(1)} collective-permute-done((bf16[128,256]{1,0:T(8,128)(2,1)S(1)}, bf16[128,256]{1,0:T(8,128)(2,1)S(1)}, u32[]{:S(2)}, u32[]{:S(2)}) %collective-permute-start) | collective-permute-done | bytes 65568 | tf_op jit(solution)/shard_map/ppermute | solution.py:266
  6.6 0.5 %shard_map.65 = (bf16[64,640]{1,0:T(8,128)(2,1)S(1)}, bf16[64,640]{1,0:T(8,128)(2,1)S(1)}) custom-call(bf16[16,128,512]{2,1,0:T(8,128)(2,1)S(1)} %copy-done.1, bf16[128,256]{1,0:T(8,128)(2,1)S(1)} %collective-permute-done.packed_ref), custom_call_target="tpu_custom_call" | custom-call | flops 20000000000 | tf_op jit(solution)/shard_map/pallas_call | solution.py:282
  7.1 0.1 collective-permute-start.1
  7.2 0.1 collective-permute-start.2
  7.3 2.0 %collective-permute-done.3.refs_3_.second_ref = bf16[576,128]{1,0:T(8,128)(2,1)S(1)} collective-permute-done((bf16[576,128]{1,0:T(8,128)(2,1)S(1)}, bf16[576,128]{1,0:T(8,128)(2,1)S(1)}, u32[]{:S(2)}, u32[]{:S(2)}) %collective-permute-start.3) | collective-permute-done | bytes 147488 | tf_op jit(solution)/shard_map/ppermute | solution.py:268
  9.3 0.4 %shard_map.67 = bf16[2,576,128]{2,1,0:T(8,128)(2,1)S(1)} custom-call(bf16[576,128]{1,0:T(8,128)(2,1)S(1)} %get-tuple-element.21.refs_2_.first_ref, bf16[576,128]{1,0:T(8,128)(2,1)S(1)} %collective-permute-done.3.refs_3_.second_ref), custom_call_target="tpu_custom_call" | custom-call | tf_op jit(solution)/shard_map/pallas_call | solution.py:271
  9.7 1.3 %collective-permute-start.6 = (bf16[2,576,128]{2,1,0:T(8,128)(2,1)S(1)}, bf16[2,576,128]{2,1,0:T(8,128)(2,1)S(1)}, u32[]{:S(2)}, u32[]{:S(2)}) collective-permute-start(bf16[2,576,128]{2,1,0:T(8,128)(2,1)S(1)} %shard_map.67), channel_id=1, source_target_pairs={{0,4},{4,0},{8,12},{12,8},{16,20},{20,16},{24,28},{28,24},{1,5},{5... | collective-permute-start | bytes 884744 | tf_op jit(solution)/shard_map/ppermute | solution.py:280
  11.0 1.5 %collective-permute-done.4.refs_4_ = bf16[576,128]{1,0:T(8,128)(2,1)S(1)} collective-permute-done((bf16[576,128]{1,0:T(8,128)(2,1)S(1)}, bf16[576,128]{1,0:T(8,128)(2,1)S(1)}, u32[]{:S(2)}, u32[]{:S(2)}) %collective-permute-start.4) | collective-permute-done | bytes 147488 | tf_op jit(solution)/shard_map/ppermute | solution.py:268
  12.5 0.3 %collective-permute-start.7 = (bf16[576,128]{1,0:T(8,128)(2,1)S(1)}, bf16[576,128]{1,0:T(8,128)(2,1)S(1)}, u32[]{:S(2)}, u32[]{:S(2)}) collective-permute-start(bf16[576,128]{1,0:T(8,128)(2,1)S(1)} %collective-permute-done.4.refs_4_), channel_id=1, source_target_pairs={{0,4},{4,0},{8,12},{12,8},{16,20},{20,16},{24,28},{28,24},{1,5},{5... | collective-permute-start | bytes 442376 | tf_op jit(solution)/shard_map/ppermute | solution.py:280
  12.8 0.2 collective-permute-start.8
  13.0 0.6 %collective-permute-done.1.refs_0_ = bf16[64,640]{1,0:T(8,128)(2,1)S(1)} collective-permute-done((bf16[64,640]{1,0:T(8,128)(2,1)S(1)}, bf16[64,640]{1,0:T(8,128)(2,1)S(1)}, u32[]{:S(2)}, u32[]{:S(2)}) %collective-permute-start.1) | collective-permute-done | bytes 81952 | tf_op jit(solution)/shard_map/ppermute | solution.py:291
  13.6 0.1 collective-permute-done.2.refs_1_
  13.7 0.8 %shard_map.66 = (bf16[128,576]{1,0:T(8,128)(2,1)S(1)}, f32[128,128]{1,0:T(8,128)S(1)}, f32[128,128]{1,0:T(8,128)S(1)}, f32[128,512]{1,0:T(8,128)S(1)}) custom-call(s32[8,128]{1,0:T(8,128)S(1)} %get-tuple-element.17.limit_ref, bf16[64,640]{1,0:T(8,128)(2,1)S(1)} %collective-permute-done.1.refs_0_, bf16[64,640]{1,0:T(8,128)(2,1)S(1)} %collective-permute-done.2.refs_1_, ...), custom_call_target="tpu_custom_call" | custom-call | flops 20000000000 | tf_op jit(solution)/shard_map/pallas_call | solution.py:299
  14.5 0.6 %shard_map.69 = bf16[64,512]{1,0:T(8,128)(2,1)S(1)} custom-call(s32[8,128]{1,0:T(8,128)S(1)} %get-tuple-element.17.limit_ref, bf16[128,576]{1,0:T(8,128)(2,1)S(1)} %get-tuple-element.25.q_ref, f32[128,128]{1,0:T(8,128)S(1)} %get-tuple-element.26.top_ref, f32[128,128]{1,0:T(8,128)S(1)} %get-tuple-element.27.total_ref, ...), custom_call_target="tpu_custom_call" | custom-call | tf_op jit(solution)/shard_map/pallas_call | solution.py:313
  15.2 3.4 %collective-permute-start.10 = (bf16[64,512]{1,0:T(8,128)(2,1)S(1)}, bf16[64,512]{1,0:T(8,128)(2,1)S(1)}, u32[]{:S(2)}, u32[]{:S(2)}) collective-permute-start(bf16[64,512]{1,0:T(8,128)(2,1)S(1)} %shard_map.69), channel_id=1, source_target_pairs={{4,0},{12,1},{0,2},{8,3},{20,4},{28,5},{16,6},{24,7},{5,8},{13,9},... | collective-permute-start | bytes 196616 | tf_op jit(solution)/shard_map/ppermute | solution.py:325
  18.6 0.6 %shard_map.68 = bf16[64,512]{1,0:T(8,128)(2,1)S(1)} custom-call(s32[8,128]{1,0:T(8,128)S(1)} %get-tuple-element.17.limit_ref, bf16[128,576]{1,0:T(8,128)(2,1)S(1)} %get-tuple-element.25.q_ref, f32[128,128]{1,0:T(8,128)S(1)} %get-tuple-element.26.top_ref, f32[128,128]{1,0:T(8,128)S(1)} %get-tuple-element.27.total_ref, ...), custom_call_target="tpu_custom_call" | custom-call | flops 20000000000 | tf_op jit(solution)/shard_map/pallas_call | solution.py:313
  19.3 0.5 %collective-permute-start.9 = (bf16[64,512]{1,0:T(8,128)(2,1)S(1)}, bf16[64,512]{1,0:T(8,128)(2,1)S(1)}, u32[]{:S(2)}, u32[]{:S(2)}) collective-permute-start(bf16[64,512]{1,0:T(8,128)(2,1)S(1)} %shard_map.68), channel_id=1, source_target_pairs={{12,0},{4,1},{8,2},{0,3},{28,4},{20,5},{24,6},{16,7},{13,8},{5,9},... | collective-permute-start | bytes 196616 | tf_op jit(solution)/shard_map/ppermute | solution.py:325
  19.8 3.1 %collective-permute-done.10.refs_1_ = bf16[64,512]{1,0:T(8,128)(2,1)S(1)} collective-permute-done((bf16[64,512]{1,0:T(8,128)(2,1)S(1)}, bf16[64,512]{1,0:T(8,128)(2,1)S(1)}, u32[]{:S(2)}, u32[]{:S(2)}) %collective-permute-start.10) | collective-permute-done | bytes 65568 | tf_op jit(solution)/shard_map/ppermute | solution.py:325
  22.9 3.0 %collective-permute-done.9.refs_0_ = bf16[64,512]{1,0:T(8,128)(2,1)S(1)} collective-permute-done((bf16[64,512]{1,0:T(8,128)(2,1)S(1)}, bf16[64,512]{1,0:T(8,128)(2,1)S(1)}, u32[]{:S(2)}, u32[]{:S(2)}) %collective-permute-start.9) | collective-permute-done | bytes 65568 | tf_op jit(solution)/shard_map/ppermute | solution.py:325
  25.9 1.1 %shard_map.70 = bf16[8,16,128]{2,1,0:T(8,128)(2,1)} custom-call(bf16[16,512,128]{2,1,0:T(8,128)(2,1)S(1)} %copy-done, bf16[64,512]{1,0:T(8,128)(2,1)S(1)} %collective-permute-done.9.refs_0_, bf16[64,512]{1,0:T(8,128)(2,1)S(1)} %collective-permute-done.10.refs_1_), custom_call_target="tpu_custom_call" | custom-call | tf_op jit(solution)/shard_map/pallas_call | solution.py:332
  (9 shorter events, 0.1 us)
Async XLA Ops:
  0.0 6.6 %copy-start.1 = (bf16[16,128,512]{2,1,0:T(8,128)(2,1)S(1)}, bf16[16,128,512]{2,1,0:T(8,128)(2,1)}, u32[]{:S(2)}) copy-start(bf16[16,128,512]{2,1,0:T(8,128)(2,1)} %w_ref.2) | copy-start | bytes 6291460
  1.4 5.3 %collective-permute-start = (bf16[128,256]{1,0:T(8,128)(2,1)S(1)}, bf16[128,256]{1,0:T(8,128)(2,1)S(1)}, u32[]{:S(2)}, u32[]{:S(2)}) collective-permute-start(bf16[128,256]{1,0:T(8,128)(2,1)S(1)} %get-tuple-element.18), channel_id=1, source_target_pairs={{0,8},{1,5},{2,6},{3,11},{4,24},{5,21},{6,22},{7,27},{8,12},{9,1},... | collective-permute-start | bytes 196616 | tf_op jit(solution)/shard_map/ppermute | solution.py:266
  1.5 7.9 %collective-permute-start.3 = (bf16[576,128]{1,0:T(8,128)(2,1)S(1)}, bf16[576,128]{1,0:T(8,128)(2,1)S(1)}, u32[]{:S(2)}, u32[]{:S(2)}) collective-permute-start(bf16[576,128]{1,0:T(8,128)(2,1)S(1)} %get-tuple-element.22), channel_id=1, source_target_pairs={{0,24},{4,28},{8,16},{12,20},{16,8},{20,12},{24,0},{28,4},{1,25},{... | collective-permute-start | bytes 442376 | tf_op jit(solution)/shard_map/ppermute | solution.py:268
  3.4 9.1 %collective-permute-start.4 = (bf16[576,128]{1,0:T(8,128)(2,1)S(1)}, bf16[576,128]{1,0:T(8,128)(2,1)S(1)}, u32[]{:S(2)}, u32[]{:S(2)}) collective-permute-start(bf16[576,128]{1,0:T(8,128)(2,1)S(1)} %get-tuple-element.23), channel_id=1, source_target_pairs={{0,8},{4,20},{8,0},{12,28},{16,24},{20,4},{24,16},{28,12},{1,9},{5... | collective-permute-start | bytes 442376 | tf_op jit(solution)/shard_map/ppermute | solution.py:268
  3.5 9.3 %collective-permute-start.5 = (bf16[576,128]{1,0:T(8,128)(2,1)S(1)}, bf16[576,128]{1,0:T(8,128)(2,1)S(1)}, u32[]{:S(2)}, u32[]{:S(2)}) collective-permute-start(bf16[576,128]{1,0:T(8,128)(2,1)S(1)} %get-tuple-element.24), channel_id=1, source_target_pairs={{0,16},{4,12},{8,24},{12,4},{16,0},{20,28},{24,8},{28,20},{1,17},{... | collective-permute-start | bytes 442376 | tf_op jit(solution)/shard_map/ppermute | solution.py:268
  7.1 6.5 %collective-permute-start.1 = (bf16[64,640]{1,0:T(8,128)(2,1)S(1)}, bf16[64,640]{1,0:T(8,128)(2,1)S(1)}, u32[]{:S(2)}, u32[]{:S(2)}) collective-permute-start(bf16[64,640]{1,0:T(8,128)(2,1)S(1)} %get-tuple-element.19), channel_id=1, source_target_pairs={{8,4},{5,12},{6,0},{11,8},{24,20},{21,28},{22,16},{27,24},{12,5},{... | collective-permute-start | bytes 245768 | tf_op jit(solution)/shard_map/ppermute | solution.py:291
  7.2 6.5 %collective-permute-start.2 = (bf16[64,640]{1,0:T(8,128)(2,1)S(1)}, bf16[64,640]{1,0:T(8,128)(2,1)S(1)}, u32[]{:S(2)}, u32[]{:S(2)}) collective-permute-start(bf16[64,640]{1,0:T(8,128)(2,1)S(1)} %get-tuple-element.20), channel_id=1, source_target_pairs={{8,12},{5,4},{6,8},{11,0},{24,28},{21,20},{22,24},{27,16},{12,13},... | collective-permute-start | bytes 245768 | tf_op jit(solution)/shard_map/ppermute | solution.py:291
  9.7 4.8 %collective-permute-start.6 = (bf16[2,576,128]{2,1,0:T(8,128)(2,1)S(1)}, bf16[2,576,128]{2,1,0:T(8,128)(2,1)S(1)}, u32[]{:S(2)}, u32[]{:S(2)}) collective-permute-start(bf16[2,576,128]{2,1,0:T(8,128)(2,1)S(1)} %shard_map.67), channel_id=1, source_target_pairs={{0,4},{4,0},{8,12},{12,8},{16,20},{20,16},{24,28},{28,24},{1,5},{5... | collective-permute-start | bytes 884744 | tf_op jit(solution)/shard_map/ppermute | solution.py:280
  12.5 2.0 %collective-permute-start.7 = (bf16[576,128]{1,0:T(8,128)(2,1)S(1)}, bf16[576,128]{1,0:T(8,128)(2,1)S(1)}, u32[]{:S(2)}, u32[]{:S(2)}) collective-permute-start(bf16[576,128]{1,0:T(8,128)(2,1)S(1)} %collective-permute-done.4.refs_4_), channel_id=1, source_target_pairs={{0,4},{4,0},{8,12},{12,8},{16,20},{20,16},{24,28},{28,24},{1,5},{5... | collective-permute-start | bytes 442376 | tf_op jit(solution)/shard_map/ppermute | solution.py:280
  12.8 1.7 %collective-permute-start.8 = (bf16[576,128]{1,0:T(8,128)(2,1)S(1)}, bf16[576,128]{1,0:T(8,128)(2,1)S(1)}, u32[]{:S(2)}, u32[]{:S(2)}) collective-permute-start(bf16[576,128]{1,0:T(8,128)(2,1)S(1)} %collective-permute-done.5.refs_5_), channel_id=1, source_target_pairs={{0,4},{4,0},{8,12},{12,8},{16,20},{20,16},{24,28},{28,24},{1,5},{5... | collective-permute-start | bytes 442376 | tf_op jit(solution)/shard_map/ppermute | solution.py:280
  15.2 10.7 %copy-start = (bf16[16,512,128]{2,1,0:T(8,128)(2,1)S(1)}, bf16[16,512,128]{2,1,0:T(8,128)(2,1)}, u32[]{:S(2)}) copy-start(bf16[16,512,128]{2,1,0:T(8,128)(2,1)} %w_ref.3) | copy-start | bytes 6291460
  15.2 7.7 %collective-permute-start.10 = (bf16[64,512]{1,0:T(8,128)(2,1)S(1)}, bf16[64,512]{1,0:T(8,128)(2,1)S(1)}, u32[]{:S(2)}, u32[]{:S(2)}) collective-permute-start(bf16[64,512]{1,0:T(8,128)(2,1)S(1)} %shard_map.69), channel_id=1, source_target_pairs={{4,0},{12,1},{0,2},{8,3},{20,4},{28,5},{16,6},{24,7},{5,8},{13,9},... | collective-permute-start | bytes 196616 | tf_op jit(solution)/shard_map/ppermute | solution.py:325
  19.3 6.7 %collective-permute-start.9 = (bf16[64,512]{1,0:T(8,128)(2,1)S(1)}, bf16[64,512]{1,0:T(8,128)(2,1)S(1)}, u32[]{:S(2)}, u32[]{:S(2)}) collective-permute-start(bf16[64,512]{1,0:T(8,128)(2,1)S(1)} %shard_map.68), channel_id=1, source_target_pairs={{12,0},{4,1},{8,2},{0,3},{28,4},{20,5},{24,6},{16,7},{13,8},{5,9},... | collective-permute-start | bytes 196616 | tf_op jit(solution)/shard_map/ppermute | solution.py:325

commit v34 on v29

--- a/solution.py
+++ b/solution.py
@@ -21,7 +21,7 @@
 
 
 def leaves_as(k, head_shard):
-    return (k + head_shard) % 2
+    return (k + head_shard + 1) % 2
 
 
 def far_half(plane, pair):
@@ -35,11 +35,11 @@
 
 def first_block(plane, chip, core):
     near = 1 * (chip % 2 == plane % 2)
-    return far_half(plane, 1 - core) ^ near ^ chip % 2
+    return far_half(plane, 1 - core) ^ near ^ 1 - chip % 2
 
 
 def partner(k, core):
-    return (0, 3, 1 ^ 3 * core, 2 ^ 3 * core)[k]
+    return (0, 3, 2 ^ 3 * core, 1 ^ 3 * core)[k]
 
 
 def pick_kernel(per_device, cache_hbm, q_hbm, new_hbm, len_hbm, *refs):

time: 26.5 us -> 27.2 us (1.026)
  waiting for transfers between devices: 12.1 us -> 12.8 us
    ppermute x2, starting transfers between devices: 0.13 us -> 2.3 us  [whole_sequences(): lax.ppermute(pieces[k], both, [(host(i, j), owner(i, j, leaves_as(k, j)))...]
    ppermute x2, waiting for transfers between devices: 0.73 us -> 2.09 us  [whole_sequences(): lax.ppermute(pieces[k], both, [(host(i, j), owner(i, j, leaves_as(k, j)))...]
    ppermute x2, starting transfers between devices: 3.86 us -> 2.69 us  [whole_sequences(): lax.ppermute(latent[k], both, [(owner(i, j, first_back(i // COPIES, j) ^...]
    ppermute x3, starting transfers between devices: 1.81 us -> 0.81 us  [whole_sequences(): lax.ppermute(keys, 'seq', other_core)]
    ppermute x3, waiting for transfers between devices: 3.54 us -> 2.57 us  [whole_sequences(): lax.ppermute(picked[k], 'seq', in_plane(lambda g, t: (g ^ partner(k, t))...]
    ppermute x2, waiting for transfers between devices: 6.18 us -> 6.48 us  [whole_sequences(): lax.ppermute(latent[k], both, [(owner(i, j, first_back(i // COPIES, j) ^...]
  transfers between devices with their start and end apart: 11 -> 11, of which waited for: 7 -> 6; matrix products, arithmetic and copies ran while one was open for 0% -> 0% of each run, Pallas kernels for 6% -> 6%
where the time goes in v34:
time: 27.2 us; the launch traced here: 27 us
  waiting for transfers between devices  12.8 us (47%)
  starting transfers between devices  9.41 us (35%)
  Pallas kernels  4.75 us (17%)
    ppermute x2, waiting for transfers between devices, whole_sequences(): lax.ppermute(latent[k], both, [(owner(i, j, first_back(i // COPIES, j) ^...  6.48 us
    ppermute x3, starting transfers between devices, whole_sequences(): lax.ppermute(picked[k], 'seq', in_plane(lambda g, t: (g ^ partner(k, t))...  3.55 us
    ppermute x2, starting transfers between devices, whole_sequences(): lax.ppermute(latent[k], both, [(owner(i, j, first_back(i // COPIES, j) ^...  2.69 us
    ppermute x3, waiting for transfers between devices, whole_sequences(): lax.ppermute(picked[k], 'seq', in_plane(lambda g, t: (g ^ partner(k, t))...  2.57 us
    ppermute x2, starting transfers between devices, whole_sequences(): lax.ppermute(pieces[k], both, [(host(i, j), owner(i, j, leaves_as(k, j)))...  2.3 us
    ppermute x2, waiting for transfers between devices, whole_sequences(): lax.ppermute(pieces[k], both, [(host(i, j), owner(i, j, leaves_as(k, j)))...  2.09 us
    ppermute x1, waiting for transfers between devices, whole_sequences(): lax.ppermute(packed, both, [(flat(i, j), host(i, j)) for i, j in devices])  1.63 us
    pallas_call x1, Pallas kernels, whole_sequences(): pl.pallas_call(functools.partial(pick_kernel, per_device), out_shape=[jax...  1.37 us
  transfers between devices with their start and end apart: 11, of which 6 were waited for; matrix products, arithmetic and copies ran while one was open for 0% of the time, Pallas kernels for 6%

profile of v34, /device:TPU:6, one launch (start us, length us, event | category | flops | bytes accessed | tf_op | source)
XLA Modules:
  0.0 27.0 jit_solution(4383020197191627000)
XLA Ops:
  0.0 1.4 %shard_map.64 = (bf16[576,128]{1,0:T(8,128)(2,1)S(1)}, bf16[576,128]{1,0:T(8,128)(2,1)S(1)}, bf16[576,128]{1,0:T(8,128)(2,1)S(1)}, bf16[576,128]{1,0:T(8,128)(2,...) custom-call(bf16[4,576,128]{2,1,0:T(8,128)(2,1)} %bitcast.1, bf16[8,16,192]{2,1,0:T(8,128)(2,1)} %q_hbm.1, ...), custom_call_target="tpu_custom_call" | custom-call | flops 20000000000 | tf_op jit(solution)/shard_map/pallas_call | solution.py:254
  1.4 0.1 collective-permute-start
  1.5 2.0 %collective-permute-start.3 = (bf16[576,128]{1,0:T(8,128)(2,1)S(1)}, bf16[576,128]{1,0:T(8,128)(2,1)S(1)}, u32[]{:S(2)}, u32[]{:S(2)}) collective-permute-start(bf16[576,128]{1,0:T(8,128)(2,1)S(1)} %get-tuple-element.24), channel_id=1, source_target_pairs={{0,24},{4,28},{8,16},{12,20},{16,8},{20,12},{24,0},{28,4},{1,25},{... | collective-permute-start | bytes 442376 | tf_op jit(solution)/shard_map/ppermute | solution.py:274
  3.4 0.1 collective-permute-start.4
  3.5 1.5 %collective-permute-start.5 = (bf16[576,128]{1,0:T(8,128)(2,1)S(1)}, bf16[576,128]{1,0:T(8,128)(2,1)S(1)}, u32[]{:S(2)}, u32[]{:S(2)}) collective-permute-start(bf16[576,128]{1,0:T(8,128)(2,1)S(1)} %get-tuple-element.26), channel_id=1, source_target_pairs={{0,8},{4,20},{8,0},{12,28},{16,24},{20,4},{24,16},{28,12},{1,9},{5... | collective-permute-start | bytes 442376 | tf_op jit(solution)/shard_map/ppermute | solution.py:274
  5.0 1.6 %collective-permute-done.packed_ref = bf16[128,256]{1,0:T(8,128)(2,1)S(1)} collective-permute-done((bf16[128,256]{1,0:T(8,128)(2,1)S(1)}, bf16[128,256]{1,0:T(8,128)(2,1)S(1)}, u32[]{:S(2)}, u32[]{:S(2)}) %collective-permute-start) | collective-permute-done | bytes 65568 | tf_op jit(solution)/shard_map/ppermute | solution.py:272
  6.6 0.5 %shard_map.65 = (bf16[64,640]{1,0:T(8,128)(2,1)S(1)}, bf16[64,640]{1,0:T(8,128)(2,1)S(1)}) custom-call(bf16[16,128,512]{2,1,0:T(8,128)(2,1)S(1)} %copy-done.1, bf16[128,256]{1,0:T(8,128)(2,1)S(1)} %collective-permute-done.packed_ref), custom_call_target="tpu_custom_call" | custom-call | flops 20000000000 | tf_op jit(solution)/shard_map/pallas_call | solution.py:288
  7.1 0.1 collective-permute-start.1
  7.2 2.2 %collective-permute-start.2 = (bf16[64,640]{1,0:T(8,128)(2,1)S(1)}, bf16[64,640]{1,0:T(8,128)(2,1)S(1)}, u32[]{:S(2)}, u32[]{:S(2)}) collective-permute-start(bf16[64,640]{1,0:T(8,128)(2,1)S(1)} %get-tuple-element.22), channel_id=1, source_target_pairs={{8,4},{5,12},{6,0},{11,8},{24,20},{21,28},{22,16},{27,24},{12,5},{... | collective-permute-start | bytes 245768 | tf_op jit(solution)/shard_map/ppermute | solution.py:297
  9.4 0.4 %shard_map.67 = bf16[2,576,128]{2,1,0:T(8,128)(2,1)S(1)} custom-call(bf16[576,128]{1,0:T(8,128)(2,1)S(1)} %get-tuple-element.23.refs_2_.first_ref, bf16[576,128]{1,0:T(8,128)(2,1)S(1)} %collective-permute-done.3.refs_3_.second_ref), custom_call_target="tpu_custom_call" | custom-call | tf_op jit(solution)/shard_map/pallas_call | solution.py:277
  9.8 0.3 %collective-permute-start.6 = (bf16[2,576,128]{2,1,0:T(8,128)(2,1)S(1)}, bf16[2,576,128]{2,1,0:T(8,128)(2,1)S(1)}, u32[]{:S(2)}, u32[]{:S(2)}) collective-permute-start(bf16[2,576,128]{2,1,0:T(8,128)(2,1)S(1)} %shard_map.67), channel_id=1, source_target_pairs={{0,4},{4,0},{8,12},{12,8},{16,20},{20,16},{24,28},{28,24},{1,5},{5... | collective-permute-start | bytes 884744 | tf_op jit(solution)/shard_map/ppermute | solution.py:286
  10.1 2.6 %collective-permute-done.4.refs_4_ = bf16[576,128]{1,0:T(8,128)(2,1)S(1)} collective-permute-done((bf16[576,128]{1,0:T(8,128)(2,1)S(1)}, bf16[576,128]{1,0:T(8,128)(2,1)S(1)}, u32[]{:S(2)}, u32[]{:S(2)}) %collective-permute-start.4) | collective-permute-done | bytes 147488 | tf_op jit(solution)/shard_map/ppermute | solution.py:274
  12.7 0.1 collective-permute-start.7
  12.7 0.0 collective-permute-done.5.refs_5_
  12.8 0.4 %collective-permute-start.8 = (bf16[576,128]{1,0:T(8,128)(2,1)S(1)}, bf16[576,128]{1,0:T(8,128)(2,1)S(1)}, u32[]{:S(2)}, u32[]{:S(2)}) collective-permute-start(bf16[576,128]{1,0:T(8,128)(2,1)S(1)} %collective-permute-done.5.refs_5_), channel_id=1, source_target_pairs={{0,4},{4,0},{8,12},{12,8},{16,20},{20,16},{24,28},{28,24},{1,5},{5... | collective-permute-start | bytes 442376 | tf_op jit(solution)/shard_map/ppermute | solution.py:286
  13.2 0.5 %collective-permute-done.1.refs_0_ = bf16[64,640]{1,0:T(8,128)(2,1)S(1)} collective-permute-done((bf16[64,640]{1,0:T(8,128)(2,1)S(1)}, bf16[64,640]{1,0:T(8,128)(2,1)S(1)}, u32[]{:S(2)}, u32[]{:S(2)}) %collective-permute-start.1) | collective-permute-done | bytes 81952 | tf_op jit(solution)/shard_map/ppermute | solution.py:297
  13.7 1.6 %collective-permute-done.2.refs_1_ = bf16[64,640]{1,0:T(8,128)(2,1)S(1)} collective-permute-done((bf16[64,640]{1,0:T(8,128)(2,1)S(1)}, bf16[64,640]{1,0:T(8,128)(2,1)S(1)}, u32[]{:S(2)}, u32[]{:S(2)}) %collective-permute-start.2) | collective-permute-done | bytes 81952 | tf_op jit(solution)/shard_map/ppermute | solution.py:297
  15.3 0.8 %shard_map.66 = (bf16[128,576]{1,0:T(8,128)(2,1)S(1)}, f32[128,128]{1,0:T(8,128)S(1)}, f32[128,128]{1,0:T(8,128)S(1)}, f32[128,512]{1,0:T(8,128)S(1)}) custom-call(s32[8,128]{1,0:T(8,128)S(1)} %get-tuple-element.19.limit_ref, bf16[64,640]{1,0:T(8,128)(2,1)S(1)} %collective-permute-done.1.refs_0_, bf16[64,640]{1,0:T(8,128)(2,1)S(1)} %collective-permute-done.2.refs_1_, ...), custom_call_target="tpu_custom_call" | custom-call | flops 20000000000 | tf_op jit(solution)/shard_map/pallas_call | solution.py:305
  16.0 0.0 collective-permute-done.7.refs_0_
  16.1 0.7 %shard_map.68 = (bf16[64,512]{1,0:T(8,128)(2,1)S(1)}, bf16[64,512]{1,0:T(8,128)(2,1)S(1)}) custom-call(s32[8,128]{1,0:T(8,128)S(1)} %get-tuple-element.19.limit_ref, bf16[128,576]{1,0:T(8,128)(2,1)S(1)} %get-tuple-element.27.q_ref, f32[128,128]{1,0:T(8,128)S(1)} %get-tuple-element.28.top_ref, f32[128,128]{1,0:T(8,128)S(1)} %get-tuple-element.29.total_ref, ...), custom_call_target="tpu_custom_call" | custom-call | tf_op jit(solution)/shard_map/pallas_call | solution.py:318
  16.8 2.7 %collective-permute-start.10 = (bf16[64,512]{1,0:T(8,128)(2,1)S(1)}, bf16[64,512]{1,0:T(8,128)(2,1)S(1)}, u32[]{:S(2)}, u32[]{:S(2)}) collective-permute-start(bf16[64,512]{1,0:T(8,128)(2,1)S(1)} %get-tuple-element.32), channel_id=1, source_target_pairs={{4,0},{12,1},{0,2},{8,3},{20,4},{28,5},{16,6},{24,7},{5,8},{13,9},... | collective-permute-start | bytes 196616 | tf_op jit(solution)/shard_map/ppermute | solution.py:327
  19.5 5.0 %collective-permute-done.10.refs_1_ = bf16[64,512]{1,0:T(8,128)(2,1)S(1)} collective-permute-done((bf16[64,512]{1,0:T(8,128)(2,1)S(1)}, bf16[64,512]{1,0:T(8,128)(2,1)S(1)}, u32[]{:S(2)}, u32[]{:S(2)}) %collective-permute-start.10) | collective-permute-done | bytes 65568 | tf_op jit(solution)/shard_map/ppermute | solution.py:327
  24.5 1.5 %collective-permute-done.9.refs_0_ = bf16[64,512]{1,0:T(8,128)(2,1)S(1)} collective-permute-done((bf16[64,512]{1,0:T(8,128)(2,1)S(1)}, bf16[64,512]{1,0:T(8,128)(2,1)S(1)}, u32[]{:S(2)}, u32[]{:S(2)}) %collective-permute-start.9) | collective-permute-done | bytes 65568 | tf_op jit(solution)/shard_map/ppermute | solution.py:327
  26.0 1.1 %shard_map.69 = bf16[8,16,128]{2,1,0:T(8,128)(2,1)} custom-call(bf16[16,512,128]{2,1,0:T(8,128)(2,1)S(1)} %copy-done, bf16[64,512]{1,0:T(8,128)(2,1)S(1)} %collective-permute-done.9.refs_0_, bf16[64,512]{1,0:T(8,128)(2,1)S(1)} %collective-permute-done.10.refs_1_), custom_call_target="tpu_custom_call" | custom-call | tf_op jit(solution)/shard_map/pallas_call | solution.py:334
  (8 shorter events, 0.0 us)
Async XLA Ops:
  0.0 6.6 %copy-start.1 = (bf16[16,128,512]{2,1,0:T(8,128)(2,1)S(1)}, bf16[16,128,512]{2,1,0:T(8,128)(2,1)}, u32[]{:S(2)}) copy-start(bf16[16,128,512]{2,1,0:T(8,128)(2,1)} %w_ref.2) | copy-start | bytes 6291460
  1.4 5.3 %collective-permute-start = (bf16[128,256]{1,0:T(8,128)(2,1)S(1)}, bf16[128,256]{1,0:T(8,128)(2,1)S(1)}, u32[]{:S(2)}, u32[]{:S(2)}) collective-permute-start(bf16[128,256]{1,0:T(8,128)(2,1)S(1)} %get-tuple-element.20), channel_id=1, source_target_pairs={{0,8},{1,5},{2,6},{3,11},{4,24},{5,21},{6,22},{7,27},{8,12},{9,1},... | collective-permute-start | bytes 196616 | tf_op jit(solution)/shard_map/ppermute | solution.py:272
  1.5 8.0 %collective-permute-start.3 = (bf16[576,128]{1,0:T(8,128)(2,1)S(1)}, bf16[576,128]{1,0:T(8,128)(2,1)S(1)}, u32[]{:S(2)}, u32[]{:S(2)}) collective-permute-start(bf16[576,128]{1,0:T(8,128)(2,1)S(1)} %get-tuple-element.24), channel_id=1, source_target_pairs={{0,24},{4,28},{8,16},{12,20},{16,8},{20,12},{24,0},{28,4},{1,25},{... | collective-permute-start | bytes 442376 | tf_op jit(solution)/shard_map/ppermute | solution.py:274
  3.4 9.3 %collective-permute-start.4 = (bf16[576,128]{1,0:T(8,128)(2,1)S(1)}, bf16[576,128]{1,0:T(8,128)(2,1)S(1)}, u32[]{:S(2)}, u32[]{:S(2)}) collective-permute-start(bf16[576,128]{1,0:T(8,128)(2,1)S(1)} %get-tuple-element.25), channel_id=1, source_target_pairs={{0,16},{4,12},{8,24},{12,4},{16,0},{20,28},{24,8},{28,20},{1,17},{... | collective-permute-start | bytes 442376 | tf_op jit(solution)/shard_map/ppermute | solution.py:274
  3.5 9.2 %collective-permute-start.5 = (bf16[576,128]{1,0:T(8,128)(2,1)S(1)}, bf16[576,128]{1,0:T(8,128)(2,1)S(1)}, u32[]{:S(2)}, u32[]{:S(2)}) collective-permute-start(bf16[576,128]{1,0:T(8,128)(2,1)S(1)} %get-tuple-element.26), channel_id=1, source_target_pairs={{0,8},{4,20},{8,0},{12,28},{16,24},{20,4},{24,16},{28,12},{1,9},{5... | collective-permute-start | bytes 442376 | tf_op jit(solution)/shard_map/ppermute | solution.py:274
  7.1 6.5 %collective-permute-start.1 = (bf16[64,640]{1,0:T(8,128)(2,1)S(1)}, bf16[64,640]{1,0:T(8,128)(2,1)S(1)}, u32[]{:S(2)}, u32[]{:S(2)}) collective-permute-start(bf16[64,640]{1,0:T(8,128)(2,1)S(1)} %get-tuple-element.21), channel_id=1, source_target_pairs={{8,12},{5,4},{6,8},{11,0},{24,28},{21,20},{22,24},{27,16},{12,13},... | collective-permute-start | bytes 245768 | tf_op jit(solution)/shard_map/ppermute | solution.py:297
  7.2 8.1 %collective-permute-start.2 = (bf16[64,640]{1,0:T(8,128)(2,1)S(1)}, bf16[64,640]{1,0:T(8,128)(2,1)S(1)}, u32[]{:S(2)}, u32[]{:S(2)}) collective-permute-start(bf16[64,640]{1,0:T(8,128)(2,1)S(1)} %get-tuple-element.22), channel_id=1, source_target_pairs={{8,4},{5,12},{6,0},{11,8},{24,20},{21,28},{22,16},{27,24},{12,5},{... | collective-permute-start | bytes 245768 | tf_op jit(solution)/shard_map/ppermute | solution.py:297
  9.8 6.3 %collective-permute-start.6 = (bf16[2,576,128]{2,1,0:T(8,128)(2,1)S(1)}, bf16[2,576,128]{2,1,0:T(8,128)(2,1)S(1)}, u32[]{:S(2)}, u32[]{:S(2)}) collective-permute-start(bf16[2,576,128]{2,1,0:T(8,128)(2,1)S(1)} %shard_map.67), channel_id=1, source_target_pairs={{0,4},{4,0},{8,12},{12,8},{16,20},{20,16},{24,28},{28,24},{1,5},{5... | collective-permute-start | bytes 884744 | tf_op jit(solution)/shard_map/ppermute | solution.py:286
  12.7 3.4 %collective-permute-start.7 = (bf16[576,128]{1,0:T(8,128)(2,1)S(1)}, bf16[576,128]{1,0:T(8,128)(2,1)S(1)}, u32[]{:S(2)}, u32[]{:S(2)}) collective-permute-start(bf16[576,128]{1,0:T(8,128)(2,1)S(1)} %collective-permute-done.4.refs_4_), channel_id=1, source_target_pairs={{0,4},{4,0},{8,12},{12,8},{16,20},{20,16},{24,28},{28,24},{1,5},{5... | collective-permute-start | bytes 442376 | tf_op jit(solution)/shard_map/ppermute | solution.py:286
  12.8 3.3 %collective-permute-start.8 = (bf16[576,128]{1,0:T(8,128)(2,1)S(1)}, bf16[576,128]{1,0:T(8,128)(2,1)S(1)}, u32[]{:S(2)}, u32[]{:S(2)}) collective-permute-start(bf16[576,128]{1,0:T(8,128)(2,1)S(1)} %collective-permute-done.5.refs_5_), channel_id=1, source_target_pairs={{0,4},{4,0},{8,12},{12,8},{16,20},{20,16},{24,28},{28,24},{1,5},{5... | collective-permute-start | bytes 442376 | tf_op jit(solution)/shard_map/ppermute | solution.py:286
  15.3 10.7 %copy-start = (bf16[16,512,128]{2,1,0:T(8,128)(2,1)S(1)}, bf16[16,512,128]{2,1,0:T(8,128)(2,1)}, u32[]{:S(2)}) copy-start(bf16[16,512,128]{2,1,0:T(8,128)(2,1)} %w_ref.3) | copy-start | bytes 6291460
  16.8 7.7 %collective-permute-start.10 = (bf16[64,512]{1,0:T(8,128)(2,1)S(1)}, bf16[64,512]{1,0:T(8,128)(2,1)S(1)}, u32[]{:S(2)}, u32[]{:S(2)}) collective-permute-start(bf16[64,512]{1,0:T(8,128)(2,1)S(1)} %get-tuple-element.32), channel_id=1, source_target_pairs={{4,0},{12,1},{0,2},{8,3},{20,4},{28,5},{16,6},{24,7},{5,8},{13,9},... | collective-permute-start | bytes 196616 | tf_op jit(solution)/shard_map/ppermute | solution.py:327
  19.5 6.5 %collective-permute-start.9 = (bf16[64,512]{1,0:T(8,128)(2,1)S(1)}, bf16[64,512]{1,0:T(8,128)(2,1)S(1)}, u32[]{:S(2)}, u32[]{:S(2)}) collective-permute-start(bf16[64,512]{1,0:T(8,128)(2,1)S(1)} %get-tuple-element.31), channel_id=1, source_target_pairs={{12,0},{4,1},{8,2},{0,3},{28,4},{20,5},{24,6},{16,7},{13,8},{5,9},... | collective-permute-start | bytes 196616 | tf_op jit(solution)/shard_map/ppermute | solution.py:327

commit v35 on v34

--- a/solution.py
+++ b/solution.py
@@ -39,7 +39,7 @@
 
 
 def partner(k, core):
-    return (0, 3, 2 ^ 3 * core, 1 ^ 3 * core)[k]
+    return (0, 1 ^ 3 * core, 3, 2 ^ 3 * core)[k]
 
 
 def pick_kernel(per_device, cache_hbm, q_hbm, new_hbm, len_hbm, *refs):

time: 27.2 us -> 27.1 us (level)
  waiting for transfers between devices: 12.8 us -> 12.4 us
    ppermute x3, waiting for transfers between devices: 2.57 us -> 4.24 us  [whole_sequences(): lax.ppermute(picked[k], 'seq', in_plane(lambda g, t: (g ^ partner(k, t))...]
    ppermute x2, waiting for transfers between devices: 2.09 us -> 0.92 us  [whole_sequences(): lax.ppermute(pieces[k], both, [(host(i, j), owner(i, j, leaves_as(k, j)))...]
    ppermute x2, waiting for transfers between devices: 6.48 us -> 5.63 us  [whole_sequences(): lax.ppermute(latent[k], both, [(owner(i, j, first_back(i // COPIES, j) ^...]
    ppermute x2, starting transfers between devices: 2.69 us -> 3.03 us  [whole_sequences(): lax.ppermute(latent[k], both, [(owner(i, j, first_back(i // COPIES, j) ^...]
  transfers between devices with their start and end apart: 11 -> 11, of which waited for: 6 -> 5; matrix products, arithmetic and copies ran while one was open for 0% -> 0% of each run, Pallas kernels for 6% -> 6%
where the time goes in v35:
time: 27.1 us; the launch traced here: 26.8 us
  waiting for transfers between devices  12.4 us (46%)
  starting transfers between devices  9.53 us (35%)
  Pallas kernels  4.76 us (18%)
    ppermute x2, waiting for transfers between devices, whole_sequences(): lax.ppermute(latent[k], both, [(owner(i, j, first_back(i // COPIES, j) ^...  5.63 us
    ppermute x3, waiting for transfers between devices, whole_sequences(): lax.ppermute(picked[k], 'seq', in_plane(lambda g, t: (g ^ partner(k, t))...  4.24 us
    ppermute x3, starting transfers between devices, whole_sequences(): lax.ppermute(picked[k], 'seq', in_plane(lambda g, t: (g ^ partner(k, t))...  3.55 us
    ppermute x2, starting transfers between devices, whole_sequences(): lax.ppermute(latent[k], both, [(owner(i, j, first_back(i // COPIES, j) ^...  3.03 us
    ppermute x2, starting transfers between devices, whole_sequences(): lax.ppermute(pieces[k], both, [(host(i, j), owner(i, j, leaves_as(k, j)))...  2.29 us
    ppermute x1, waiting for transfers between devices, whole_sequences(): lax.ppermute(packed, both, [(flat(i, j), host(i, j)) for i, j in devices])  1.64 us
    pallas_call x1, Pallas kernels, whole_sequences(): pl.pallas_call(functools.partial(pick_kernel, per_device), out_shape=[jax...  1.37 us
    pallas_call x1, Pallas kernels, whole_sequences(): pl.pallas_call(functools.partial(project_kernel, per_device), out_shape=j...  1.06 us
  transfers between devices with their start and end apart: 11, of which 5 were waited for; matrix products, arithmetic and copies ran while one was open for 0% of the time, Pallas kernels for 6%

profile of v35, /device:TPU:6, one launch (start us, length us, event | category | flops | bytes accessed | tf_op | source)
XLA Modules:
  0.0 26.8 jit_solution(7043931085210569692)
XLA Ops:
  0.0 1.4 %shard_map.64 = (bf16[576,128]{1,0:T(8,128)(2,1)S(1)}, bf16[576,128]{1,0:T(8,128)(2,1)S(1)}, bf16[576,128]{1,0:T(8,128)(2,1)S(1)}, bf16[576,128]{1,0:T(8,128)(2,...) custom-call(bf16[4,576,128]{2,1,0:T(8,128)(2,1)} %bitcast.1, bf16[8,16,192]{2,1,0:T(8,128)(2,1)} %q_hbm.1, ...), custom_call_target="tpu_custom_call" | custom-call | flops 20000000000 | tf_op jit(solution)/shard_map/pallas_call | solution.py:254
  1.4 0.1 collective-permute-start
  1.5 0.6 %collective-permute-start.3 = (bf16[576,128]{1,0:T(8,128)(2,1)S(1)}, bf16[576,128]{1,0:T(8,128)(2,1)S(1)}, u32[]{:S(2)}, u32[]{:S(2)}) collective-permute-start(bf16[576,128]{1,0:T(8,128)(2,1)S(1)} %get-tuple-element.24), channel_id=1, source_target_pairs={{0,8},{4,20},{8,0},{12,28},{16,24},{20,4},{24,16},{28,12},{1,9},{5... | collective-permute-start | bytes 442376 | tf_op jit(solution)/shard_map/ppermute | solution.py:274
  2.1 1.4 %collective-permute-start.4 = (bf16[576,128]{1,0:T(8,128)(2,1)S(1)}, bf16[576,128]{1,0:T(8,128)(2,1)S(1)}, u32[]{:S(2)}, u32[]{:S(2)}) collective-permute-start(bf16[576,128]{1,0:T(8,128)(2,1)S(1)} %get-tuple-element.25), channel_id=1, source_target_pairs={{0,24},{4,28},{8,16},{12,20},{16,8},{20,12},{24,0},{28,4},{1,25},{... | collective-permute-start | bytes 442376 | tf_op jit(solution)/shard_map/ppermute | solution.py:274
  3.5 1.5 %collective-permute-start.5 = (bf16[576,128]{1,0:T(8,128)(2,1)S(1)}, bf16[576,128]{1,0:T(8,128)(2,1)S(1)}, u32[]{:S(2)}, u32[]{:S(2)}) collective-permute-start(bf16[576,128]{1,0:T(8,128)(2,1)S(1)} %get-tuple-element.26), channel_id=1, source_target_pairs={{0,16},{4,12},{8,24},{12,4},{16,0},{20,28},{24,8},{28,20},{1,17},{... | collective-permute-start | bytes 442376 | tf_op jit(solution)/shard_map/ppermute | solution.py:274
  5.0 1.6 %collective-permute-done.packed_ref = bf16[128,256]{1,0:T(8,128)(2,1)S(1)} collective-permute-done((bf16[128,256]{1,0:T(8,128)(2,1)S(1)}, bf16[128,256]{1,0:T(8,128)(2,1)S(1)}, u32[]{:S(2)}, u32[]{:S(2)}) %collective-permute-start) | collective-permute-done | bytes 65568 | tf_op jit(solution)/shard_map/ppermute | solution.py:272
  6.7 0.5 %shard_map.65 = (bf16[64,640]{1,0:T(8,128)(2,1)S(1)}, bf16[64,640]{1,0:T(8,128)(2,1)S(1)}) custom-call(bf16[16,128,512]{2,1,0:T(8,128)(2,1)S(1)} %copy-done.1, bf16[128,256]{1,0:T(8,128)(2,1)S(1)} %collective-permute-done.packed_ref), custom_call_target="tpu_custom_call" | custom-call | flops 20000000000 | tf_op jit(solution)/shard_map/pallas_call | solution.py:288
  7.1 0.1 collective-permute-start.1
  7.2 2.2 %collective-permute-start.2 = (bf16[64,640]{1,0:T(8,128)(2,1)S(1)}, bf16[64,640]{1,0:T(8,128)(2,1)S(1)}, u32[]{:S(2)}, u32[]{:S(2)}) collective-permute-start(bf16[64,640]{1,0:T(8,128)(2,1)S(1)} %get-tuple-element.22), channel_id=1, source_target_pairs={{8,4},{5,12},{6,0},{11,8},{24,20},{21,28},{22,16},{27,24},{12,5},{... | collective-permute-start | bytes 245768 | tf_op jit(solution)/shard_map/ppermute | solution.py:297
  9.4 0.4 %shard_map.67 = bf16[2,576,128]{2,1,0:T(8,128)(2,1)S(1)} custom-call(bf16[576,128]{1,0:T(8,128)(2,1)S(1)} %get-tuple-element.23.refs_2_.first_ref, bf16[576,128]{1,0:T(8,128)(2,1)S(1)} %collective-permute-done.3.refs_3_.second_ref), custom_call_target="tpu_custom_call" | custom-call | tf_op jit(solution)/shard_map/pallas_call | solution.py:277
  9.8 0.1 collective-permute-start.6
  9.9 4.2 %collective-permute-done.4.refs_4_ = bf16[576,128]{1,0:T(8,128)(2,1)S(1)} collective-permute-done((bf16[576,128]{1,0:T(8,128)(2,1)S(1)}, bf16[576,128]{1,0:T(8,128)(2,1)S(1)}, u32[]{:S(2)}, u32[]{:S(2)}) %collective-permute-start.4) | collective-permute-done | bytes 147488 | tf_op jit(solution)/shard_map/ppermute | solution.py:274
  14.1 0.0 collective-permute-start.7
  14.1 0.5 %collective-permute-start.8 = (bf16[576,128]{1,0:T(8,128)(2,1)S(1)}, bf16[576,128]{1,0:T(8,128)(2,1)S(1)}, u32[]{:S(2)}, u32[]{:S(2)}) collective-permute-start(bf16[576,128]{1,0:T(8,128)(2,1)S(1)} %collective-permute-done.5.refs_5_), channel_id=1, source_target_pairs={{0,4},{4,0},{8,12},{12,8},{16,20},{20,16},{24,28},{28,24},{1,5},{5... | collective-permute-start | bytes 442376 | tf_op jit(solution)/shard_map/ppermute | solution.py:286
  14.7 0.9 %collective-permute-done.2.refs_1_ = bf16[64,640]{1,0:T(8,128)(2,1)S(1)} collective-permute-done((bf16[64,640]{1,0:T(8,128)(2,1)S(1)}, bf16[64,640]{1,0:T(8,128)(2,1)S(1)}, u32[]{:S(2)}, u32[]{:S(2)}) %collective-permute-start.2) | collective-permute-done | bytes 81952 | tf_op jit(solution)/shard_map/ppermute | solution.py:297
  15.6 0.8 %shard_map.66 = (bf16[128,576]{1,0:T(8,128)(2,1)S(1)}, f32[128,128]{1,0:T(8,128)S(1)}, f32[128,128]{1,0:T(8,128)S(1)}, f32[128,512]{1,0:T(8,128)S(1)}) custom-call(s32[8,128]{1,0:T(8,128)S(1)} %get-tuple-element.19.limit_ref, bf16[64,640]{1,0:T(8,128)(2,1)S(1)} %collective-permute-done.1.refs_0_, bf16[64,640]{1,0:T(8,128)(2,1)S(1)} %collective-permute-done.2.refs_1_, ...), custom_call_target="tpu_custom_call" | custom-call | flops 20000000000 | tf_op jit(solution)/shard_map/pallas_call | solution.py:305
  16.3 0.0 collective-permute-done.7.refs_0_
  16.4 0.0 collective-permute-done.8.refs_1_
  16.4 0.7 %shard_map.68 = (bf16[64,512]{1,0:T(8,128)(2,1)S(1)}, bf16[64,512]{1,0:T(8,128)(2,1)S(1)}) custom-call(s32[8,128]{1,0:T(8,128)S(1)} %get-tuple-element.19.limit_ref, bf16[128,576]{1,0:T(8,128)(2,1)S(1)} %get-tuple-element.27.q_ref, f32[128,128]{1,0:T(8,128)S(1)} %get-tuple-element.28.top_ref, f32[128,128]{1,0:T(8,128)S(1)} %get-tuple-element.29.total_ref, ...), custom_call_target="tpu_custom_call" | custom-call | tf_op jit(solution)/shard_map/pallas_call | solution.py:318
  17.1 2.3 %collective-permute-start.10 = (bf16[64,512]{1,0:T(8,128)(2,1)S(1)}, bf16[64,512]{1,0:T(8,128)(2,1)S(1)}, u32[]{:S(2)}, u32[]{:S(2)}) collective-permute-start(bf16[64,512]{1,0:T(8,128)(2,1)S(1)} %get-tuple-element.32), channel_id=1, source_target_pairs={{4,0},{12,1},{0,2},{8,3},{20,4},{28,5},{16,6},{24,7},{5,8},{13,9},... | collective-permute-start | bytes 196616 | tf_op jit(solution)/shard_map/ppermute | solution.py:327
  19.4 0.8 %collective-permute-start.9 = (bf16[64,512]{1,0:T(8,128)(2,1)S(1)}, bf16[64,512]{1,0:T(8,128)(2,1)S(1)}, u32[]{:S(2)}, u32[]{:S(2)}) collective-permute-start(bf16[64,512]{1,0:T(8,128)(2,1)S(1)} %get-tuple-element.31), channel_id=1, source_target_pairs={{12,0},{4,1},{8,2},{0,3},{28,4},{20,5},{24,6},{16,7},{13,8},{5,9},... | collective-permute-start | bytes 196616 | tf_op jit(solution)/shard_map/ppermute | solution.py:327
  20.1 4.4 %collective-permute-done.10.refs_1_ = bf16[64,512]{1,0:T(8,128)(2,1)S(1)} collective-permute-done((bf16[64,512]{1,0:T(8,128)(2,1)S(1)}, bf16[64,512]{1,0:T(8,128)(2,1)S(1)}, u32[]{:S(2)}, u32[]{:S(2)}) %collective-permute-start.10) | collective-permute-done | bytes 65568 | tf_op jit(solution)/shard_map/ppermute | solution.py:327
  24.5 1.2 %collective-permute-done.9.refs_0_ = bf16[64,512]{1,0:T(8,128)(2,1)S(1)} collective-permute-done((bf16[64,512]{1,0:T(8,128)(2,1)S(1)}, bf16[64,512]{1,0:T(8,128)(2,1)S(1)}, u32[]{:S(2)}, u32[]{:S(2)}) %collective-permute-start.9) | collective-permute-done | bytes 65568 | tf_op jit(solution)/shard_map/ppermute | solution.py:327
  25.8 1.1 %shard_map.69 = bf16[8,16,128]{2,1,0:T(8,128)(2,1)} custom-call(bf16[16,512,128]{2,1,0:T(8,128)(2,1)S(1)} %copy-done, bf16[64,512]{1,0:T(8,128)(2,1)S(1)} %collective-permute-done.9.refs_0_, bf16[64,512]{1,0:T(8,128)(2,1)S(1)} %collective-permute-done.10.refs_1_), custom_call_target="tpu_custom_call" | custom-call | tf_op jit(solution)/shard_map/pallas_call | solution.py:334
  (8 shorter events, 0.0 us)
Async XLA Ops:
  0.0 6.6 %copy-start.1 = (bf16[16,128,512]{2,1,0:T(8,128)(2,1)S(1)}, bf16[16,128,512]{2,1,0:T(8,128)(2,1)}, u32[]{:S(2)}) copy-start(bf16[16,128,512]{2,1,0:T(8,128)(2,1)} %w_ref.2) | copy-start | bytes 6291460
  1.4 5.3 %collective-permute-start = (bf16[128,256]{1,0:T(8,128)(2,1)S(1)}, bf16[128,256]{1,0:T(8,128)(2,1)S(1)}, u32[]{:S(2)}, u32[]{:S(2)}) collective-permute-start(bf16[128,256]{1,0:T(8,128)(2,1)S(1)} %get-tuple-element.20), channel_id=1, source_target_pairs={{0,8},{1,5},{2,6},{3,11},{4,24},{5,21},{6,22},{7,27},{8,12},{9,1},... | collective-permute-start | bytes 196616 | tf_op jit(solution)/shard_map/ppermute | solution.py:272
  1.5 8.0 %collective-permute-start.3 = (bf16[576,128]{1,0:T(8,128)(2,1)S(1)}, bf16[576,128]{1,0:T(8,128)(2,1)S(1)}, u32[]{:S(2)}, u32[]{:S(2)}) collective-permute-start(bf16[576,128]{1,0:T(8,128)(2,1)S(1)} %get-tuple-element.24), channel_id=1, source_target_pairs={{0,8},{4,20},{8,0},{12,28},{16,24},{20,4},{24,16},{28,12},{1,9},{5... | collective-permute-start | bytes 442376 | tf_op jit(solution)/shard_map/ppermute | solution.py:274
  2.1 12.1 %collective-permute-start.4 = (bf16[576,128]{1,0:T(8,128)(2,1)S(1)}, bf16[576,128]{1,0:T(8,128)(2,1)S(1)}, u32[]{:S(2)}, u32[]{:S(2)}) collective-permute-start(bf16[576,128]{1,0:T(8,128)(2,1)S(1)} %get-tuple-element.25), channel_id=1, source_target_pairs={{0,24},{4,28},{8,16},{12,20},{16,8},{20,12},{24,0},{28,4},{1,25},{... | collective-permute-start | bytes 442376 | tf_op jit(solution)/shard_map/ppermute | solution.py:274
  3.5 10.6 %collective-permute-start.5 = (bf16[576,128]{1,0:T(8,128)(2,1)S(1)}, bf16[576,128]{1,0:T(8,128)(2,1)S(1)}, u32[]{:S(2)}, u32[]{:S(2)}) collective-permute-start(bf16[576,128]{1,0:T(8,128)(2,1)S(1)} %get-tuple-element.26), channel_id=1, source_target_pairs={{0,16},{4,12},{8,24},{12,4},{16,0},{20,28},{24,8},{28,20},{1,17},{... | collective-permute-start | bytes 442376 | tf_op jit(solution)/shard_map/ppermute | solution.py:274
  7.1 7.5 %collective-permute-start.1 = (bf16[64,640]{1,0:T(8,128)(2,1)S(1)}, bf16[64,640]{1,0:T(8,128)(2,1)S(1)}, u32[]{:S(2)}, u32[]{:S(2)}) collective-permute-start(bf16[64,640]{1,0:T(8,128)(2,1)S(1)} %get-tuple-element.21), channel_id=1, source_target_pairs={{8,12},{5,4},{6,8},{11,0},{24,28},{21,20},{22,24},{27,16},{12,13},... | collective-permute-start | bytes 245768 | tf_op jit(solution)/shard_map/ppermute | solution.py:297
  7.2 8.4 %collective-permute-start.2 = (bf16[64,640]{1,0:T(8,128)(2,1)S(1)}, bf16[64,640]{1,0:T(8,128)(2,1)S(1)}, u32[]{:S(2)}, u32[]{:S(2)}) collective-permute-start(bf16[64,640]{1,0:T(8,128)(2,1)S(1)} %get-tuple-element.22), channel_id=1, source_target_pairs={{8,4},{5,12},{6,0},{11,8},{24,20},{21,28},{22,16},{27,24},{12,5},{... | collective-permute-start | bytes 245768 | tf_op jit(solution)/shard_map/ppermute | solution.py:297
  9.8 6.5 %collective-permute-start.6 = (bf16[2,576,128]{2,1,0:T(8,128)(2,1)S(1)}, bf16[2,576,128]{2,1,0:T(8,128)(2,1)S(1)}, u32[]{:S(2)}, u32[]{:S(2)}) collective-permute-start(bf16[2,576,128]{2,1,0:T(8,128)(2,1)S(1)} %shard_map.67), channel_id=1, source_target_pairs={{0,4},{4,0},{8,12},{12,8},{16,20},{20,16},{24,28},{28,24},{1,5},{5... | collective-permute-start | bytes 884744 | tf_op jit(solution)/shard_map/ppermute | solution.py:286
  14.1 2.2 %collective-permute-start.7 = (bf16[576,128]{1,0:T(8,128)(2,1)S(1)}, bf16[576,128]{1,0:T(8,128)(2,1)S(1)}, u32[]{:S(2)}, u32[]{:S(2)}) collective-permute-start(bf16[576,128]{1,0:T(8,128)(2,1)S(1)} %collective-permute-done.4.refs_4_), channel_id=1, source_target_pairs={{0,4},{4,0},{8,12},{12,8},{16,20},{20,16},{24,28},{28,24},{1,5},{5... | collective-permute-start | bytes 442376 | tf_op jit(solution)/shard_map/ppermute | solution.py:286
  14.1 2.2 %collective-permute-start.8 = (bf16[576,128]{1,0:T(8,128)(2,1)S(1)}, bf16[576,128]{1,0:T(8,128)(2,1)S(1)}, u32[]{:S(2)}, u32[]{:S(2)}) collective-permute-start(bf16[576,128]{1,0:T(8,128)(2,1)S(1)} %collective-permute-done.5.refs_5_), channel_id=1, source_target_pairs={{0,4},{4,0},{8,12},{12,8},{16,20},{20,16},{24,28},{28,24},{1,5},{5... | collective-permute-start | bytes 442376 | tf_op jit(solution)/shard_map/ppermute | solution.py:286
  15.6 10.2 %copy-start = (bf16[16,512,128]{2,1,0:T(8,128)(2,1)S(1)}, bf16[16,512,128]{2,1,0:T(8,128)(2,1)}, u32[]{:S(2)}) copy-start(bf16[16,512,128]{2,1,0:T(8,128)(2,1)} %w_ref.3) | copy-start | bytes 6291460
  17.1 7.4 %collective-permute-start.10 = (bf16[64,512]{1,0:T(8,128)(2,1)S(1)}, bf16[64,512]{1,0:T(8,128)(2,1)S(1)}, u32[]{:S(2)}, u32[]{:S(2)}) collective-permute-start(bf16[64,512]{1,0:T(8,128)(2,1)S(1)} %get-tuple-element.32), channel_id=1, source_target_pairs={{4,0},{12,1},{0,2},{8,3},{20,4},{28,5},{16,6},{24,7},{5,8},{13,9},... | collective-permute-start | bytes 196616 | tf_op jit(solution)/shard_map/ppermute | solution.py:327
  19.4 6.4 %collective-permute-start.9 = (bf16[64,512]{1,0:T(8,128)(2,1)S(1)}, bf16[64,512]{1,0:T(8,128)(2,1)S(1)}, u32[]{:S(2)}, u32[]{:S(2)}) collective-permute-start(bf16[64,512]{1,0:T(8,128)(2,1)S(1)} %get-tuple-element.31), channel_id=1, source_target_pairs={{12,0},{4,1},{8,2},{0,3},{28,4},{20,5},{24,6},{16,7},{13,8},{5,9},... | collective-permute-start | bytes 196616 | tf_op jit(solution)/shard_map/ppermute | solution.py:327

commit v36 on v29

--- a/solution.py
+++ b/solution.py
@@ -62,7 +62,7 @@
                     sem.at[3 + k * COPY_PARTS + n],
                 )
             )
-    for move in moves:
+    for move in moves[:2] + moves[3:] + moves[2:3]:
         move.start()
     moves[0].wait()
     moves[1].wait()

time: 26.5 us -> 26.5 us (level)
  no operation moved by 1% of the time
where the time goes in v36:
time: 26.5 us; the launch traced here: 26.4 us
  waiting for transfers between devices  12.1 us (46%)
  starting transfers between devices  9.42 us (36%)
  Pallas kernels  4.74 us (18%)
    ppermute x2, waiting for transfers between devices, whole_sequences(): lax.ppermute(latent[k], both, [(owner(i, j, first_back(i // COPIES, j) ^...  6.18 us
    ppermute x2, starting transfers between devices, whole_sequences(): lax.ppermute(latent[k], both, [(owner(i, j, first_back(i // COPIES, j) ^...  3.86 us
    ppermute x3, starting transfers between devices, whole_sequences(): lax.ppermute(picked[k], 'seq', in_plane(lambda g, t: (g ^ partner(k, t))...  3.55 us
    ppermute x3, waiting for transfers between devices, whole_sequences(): lax.ppermute(picked[k], 'seq', in_plane(lambda g, t: (g ^ partner(k, t))...  3.54 us
    ppermute x3, starting transfers between devices, whole_sequences(): lax.ppermute(keys, 'seq', other_core)  1.81 us
    ppermute x1, waiting for transfers between devices, whole_sequences(): lax.ppermute(packed, both, [(flat(i, j), host(i, j)) for i, j in devices])  1.63 us
    pallas_call x1, Pallas kernels, whole_sequences(): pl.pallas_call(functools.partial(pick_kernel, per_device), out_shape=[jax...  1.37 us
    pallas_call x1, Pallas kernels, whole_sequences(): pl.pallas_call(functools.partial(project_kernel, per_device), out_shape=j...  1.06 us
  transfers between devices with their start and end apart: 11, of which 7 were waited for; matrix products, arithmetic and copies ran while one was open for 0% of the time, Pallas kernels for 6%

profile of v36, /device:TPU:6, one launch (start us, length us, event | category | flops | bytes accessed | tf_op | source)
XLA Modules:
  0.0 26.4 jit_solution(16113651422102297350)
XLA Ops:
  0.0 1.4 %shard_map.64 = (bf16[576,128]{1,0:T(8,128)(2,1)S(1)}, bf16[576,128]{1,0:T(8,128)(2,1)S(1)}, bf16[576,128]{1,0:T(8,128)(2,1)S(1)}, bf16[576,128]{1,0:T(8,128)(2,...) custom-call(bf16[4,576,128]{2,1,0:T(8,128)(2,1)} %bitcast.1, bf16[8,16,192]{2,1,0:T(8,128)(2,1)} %q_hbm.1, ...), custom_call_target="tpu_custom_call" | custom-call | flops 20000000000 | tf_op jit(solution)/shard_map/pallas_call | solution.py:254
  1.4 0.1 collective-permute-start
  1.5 2.0 %collective-permute-start.3 = (bf16[576,128]{1,0:T(8,128)(2,1)S(1)}, bf16[576,128]{1,0:T(8,128)(2,1)S(1)}, u32[]{:S(2)}, u32[]{:S(2)}) collective-permute-start(bf16[576,128]{1,0:T(8,128)(2,1)S(1)} %get-tuple-element.24), channel_id=1, source_target_pairs={{0,24},{4,28},{8,16},{12,20},{16,8},{20,12},{24,0},{28,4},{1,25},{... | collective-permute-start | bytes 442376 | tf_op jit(solution)/shard_map/ppermute | solution.py:274
  3.4 0.1 collective-permute-start.4
  3.5 1.5 %collective-permute-start.5 = (bf16[576,128]{1,0:T(8,128)(2,1)S(1)}, bf16[576,128]{1,0:T(8,128)(2,1)S(1)}, u32[]{:S(2)}, u32[]{:S(2)}) collective-permute-start(bf16[576,128]{1,0:T(8,128)(2,1)S(1)} %get-tuple-element.26), channel_id=1, source_target_pairs={{0,16},{4,12},{8,24},{12,4},{16,0},{20,28},{24,8},{28,20},{1,17},{... | collective-permute-start | bytes 442376 | tf_op jit(solution)/shard_map/ppermute | solution.py:274
  5.0 1.6 %collective-permute-done.packed_ref = bf16[128,256]{1,0:T(8,128)(2,1)S(1)} collective-permute-done((bf16[128,256]{1,0:T(8,128)(2,1)S(1)}, bf16[128,256]{1,0:T(8,128)(2,1)S(1)}, u32[]{:S(2)}, u32[]{:S(2)}) %collective-permute-start) | collective-permute-done | bytes 65568 | tf_op jit(solution)/shard_map/ppermute | solution.py:272
  6.6 0.5 %shard_map.65 = (bf16[64,640]{1,0:T(8,128)(2,1)S(1)}, bf16[64,640]{1,0:T(8,128)(2,1)S(1)}) custom-call(bf16[16,128,512]{2,1,0:T(8,128)(2,1)S(1)} %copy-done.1, bf16[128,256]{1,0:T(8,128)(2,1)S(1)} %collective-permute-done.packed_ref), custom_call_target="tpu_custom_call" | custom-call | flops 20000000000 | tf_op jit(solution)/shard_map/pallas_call | solution.py:288
  7.1 0.1 collective-permute-start.1
  7.2 0.1 collective-permute-start.2
  7.3 2.0 %collective-permute-done.3.refs_3_.second_ref = bf16[576,128]{1,0:T(8,128)(2,1)S(1)} collective-permute-done((bf16[576,128]{1,0:T(8,128)(2,1)S(1)}, bf16[576,128]{1,0:T(8,128)(2,1)S(1)}, u32[]{:S(2)}, u32[]{:S(2)}) %collective-permute-start.3) | collective-permute-done | bytes 147488 | tf_op jit(solution)/shard_map/ppermute | solution.py:274
  9.3 0.4 %shard_map.67 = bf16[2,576,128]{2,1,0:T(8,128)(2,1)S(1)} custom-call(bf16[576,128]{1,0:T(8,128)(2,1)S(1)} %get-tuple-element.23.refs_2_.first_ref, bf16[576,128]{1,0:T(8,128)(2,1)S(1)} %collective-permute-done.3.refs_3_.second_ref), custom_call_target="tpu_custom_call" | custom-call | tf_op jit(solution)/shard_map/pallas_call | solution.py:277
  9.7 1.3 %collective-permute-start.6 = (bf16[2,576,128]{2,1,0:T(8,128)(2,1)S(1)}, bf16[2,576,128]{2,1,0:T(8,128)(2,1)S(1)}, u32[]{:S(2)}, u32[]{:S(2)}) collective-permute-start(bf16[2,576,128]{2,1,0:T(8,128)(2,1)S(1)} %shard_map.67), channel_id=1, source_target_pairs={{0,4},{4,0},{8,12},{12,8},{16,20},{20,16},{24,28},{28,24},{1,5},{5... | collective-permute-start | bytes 884744 | tf_op jit(solution)/shard_map/ppermute | solution.py:286
  11.0 1.5 %collective-permute-done.4.refs_4_ = bf16[576,128]{1,0:T(8,128)(2,1)S(1)} collective-permute-done((bf16[576,128]{1,0:T(8,128)(2,1)S(1)}, bf16[576,128]{1,0:T(8,128)(2,1)S(1)}, u32[]{:S(2)}, u32[]{:S(2)}) %collective-permute-start.4) | collective-permute-done | bytes 147488 | tf_op jit(solution)/shard_map/ppermute | solution.py:274
  12.5 0.3 %collective-permute-start.7 = (bf16[576,128]{1,0:T(8,128)(2,1)S(1)}, bf16[576,128]{1,0:T(8,128)(2,1)S(1)}, u32[]{:S(2)}, u32[]{:S(2)}) collective-permute-start(bf16[576,128]{1,0:T(8,128)(2,1)S(1)} %collective-permute-done.4.refs_4_), channel_id=1, source_target_pairs={{0,4},{4,0},{8,12},{12,8},{16,20},{20,16},{24,28},{28,24},{1,5},{5... | collective-permute-start | bytes 442376 | tf_op jit(solution)/shard_map/ppermute | solution.py:286
  12.8 0.2 collective-permute-start.8
  13.0 0.6 %collective-permute-done.1.refs_0_ = bf16[64,640]{1,0:T(8,128)(2,1)S(1)} collective-permute-done((bf16[64,640]{1,0:T(8,128)(2,1)S(1)}, bf16[64,640]{1,0:T(8,128)(2,1)S(1)}, u32[]{:S(2)}, u32[]{:S(2)}) %collective-permute-start.1) | collective-permute-done | bytes 81952 | tf_op jit(solution)/shard_map/ppermute | solution.py:297
  13.6 0.1 collective-permute-done.2.refs_1_
  13.7 0.8 %shard_map.66 = (bf16[128,576]{1,0:T(8,128)(2,1)S(1)}, f32[128,128]{1,0:T(8,128)S(1)}, f32[128,128]{1,0:T(8,128)S(1)}, f32[128,512]{1,0:T(8,128)S(1)}) custom-call(s32[8,128]{1,0:T(8,128)S(1)} %get-tuple-element.19.limit_ref, bf16[64,640]{1,0:T(8,128)(2,1)S(1)} %collective-permute-done.1.refs_0_, bf16[64,640]{1,0:T(8,128)(2,1)S(1)} %collective-permute-done.2.refs_1_, ...), custom_call_target="tpu_custom_call" | custom-call | flops 20000000000 | tf_op jit(solution)/shard_map/pallas_call | solution.py:305
  14.5 0.7 %shard_map.68 = (bf16[64,512]{1,0:T(8,128)(2,1)S(1)}, bf16[64,512]{1,0:T(8,128)(2,1)S(1)}) custom-call(s32[8,128]{1,0:T(8,128)S(1)} %get-tuple-element.19.limit_ref, bf16[128,576]{1,0:T(8,128)(2,1)S(1)} %get-tuple-element.27.q_ref, f32[128,128]{1,0:T(8,128)S(1)} %get-tuple-element.28.top_ref, f32[128,128]{1,0:T(8,128)S(1)} %get-tuple-element.29.total_ref, ...), custom_call_target="tpu_custom_call" | custom-call | tf_op jit(solution)/shard_map/pallas_call | solution.py:318
  15.2 3.4 %collective-permute-start.10 = (bf16[64,512]{1,0:T(8,128)(2,1)S(1)}, bf16[64,512]{1,0:T(8,128)(2,1)S(1)}, u32[]{:S(2)}, u32[]{:S(2)}) collective-permute-start(bf16[64,512]{1,0:T(8,128)(2,1)S(1)} %get-tuple-element.32), channel_id=1, source_target_pairs={{4,0},{12,1},{0,2},{8,3},{20,4},{28,5},{16,6},{24,7},{5,8},{13,9},... | collective-permute-start | bytes 196616 | tf_op jit(solution)/shard_map/ppermute | solution.py:327
  18.7 0.4 %collective-permute-start.9 = (bf16[64,512]{1,0:T(8,128)(2,1)S(1)}, bf16[64,512]{1,0:T(8,128)(2,1)S(1)}, u32[]{:S(2)}, u32[]{:S(2)}) collective-permute-start(bf16[64,512]{1,0:T(8,128)(2,1)S(1)} %get-tuple-element.31), channel_id=1, source_target_pairs={{12,0},{4,1},{8,2},{0,3},{28,4},{20,5},{24,6},{16,7},{13,8},{5,9},... | collective-permute-start | bytes 196616 | tf_op jit(solution)/shard_map/ppermute | solution.py:327
  19.1 3.8 %collective-permute-done.10.refs_1_ = bf16[64,512]{1,0:T(8,128)(2,1)S(1)} collective-permute-done((bf16[64,512]{1,0:T(8,128)(2,1)S(1)}, bf16[64,512]{1,0:T(8,128)(2,1)S(1)}, u32[]{:S(2)}, u32[]{:S(2)}) %collective-permute-start.10) | collective-permute-done | bytes 65568 | tf_op jit(solution)/shard_map/ppermute | solution.py:327
  22.9 2.4 %collective-permute-done.9.refs_0_ = bf16[64,512]{1,0:T(8,128)(2,1)S(1)} collective-permute-done((bf16[64,512]{1,0:T(8,128)(2,1)S(1)}, bf16[64,512]{1,0:T(8,128)(2,1)S(1)}, u32[]{:S(2)}, u32[]{:S(2)}) %collective-permute-start.9) | collective-permute-done | bytes 65568 | tf_op jit(solution)/shard_map/ppermute | solution.py:327
  25.3 1.1 %shard_map.69 = bf16[8,16,128]{2,1,0:T(8,128)(2,1)} custom-call(bf16[16,512,128]{2,1,0:T(8,128)(2,1)S(1)} %copy-done, bf16[64,512]{1,0:T(8,128)(2,1)S(1)} %collective-permute-done.9.refs_0_, bf16[64,512]{1,0:T(8,128)(2,1)S(1)} %collective-permute-done.10.refs_1_), custom_call_target="tpu_custom_call" | custom-call | tf_op jit(solution)/shard_map/pallas_call | solution.py:334
  (8 shorter events, 0.0 us)
Async XLA Ops:
  0.0 6.6 %copy-start.1 = (bf16[16,128,512]{2,1,0:T(8,128)(2,1)S(1)}, bf16[16,128,512]{2,1,0:T(8,128)(2,1)}, u32[]{:S(2)}) copy-start(bf16[16,128,512]{2,1,0:T(8,128)(2,1)} %w_ref.2) | copy-start | bytes 6291460
  1.4 5.3 %collective-permute-start = (bf16[128,256]{1,0:T(8,128)(2,1)S(1)}, bf16[128,256]{1,0:T(8,128)(2,1)S(1)}, u32[]{:S(2)}, u32[]{:S(2)}) collective-permute-start(bf16[128,256]{1,0:T(8,128)(2,1)S(1)} %get-tuple-element.20), channel_id=1, source_target_pairs={{0,8},{1,5},{2,6},{3,11},{4,24},{5,21},{6,22},{7,27},{8,12},{9,1},... | collective-permute-start | bytes 196616 | tf_op jit(solution)/shard_map/ppermute | solution.py:272
  1.5 7.9 %collective-permute-start.3 = (bf16[576,128]{1,0:T(8,128)(2,1)S(1)}, bf16[576,128]{1,0:T(8,128)(2,1)S(1)}, u32[]{:S(2)}, u32[]{:S(2)}) collective-permute-start(bf16[576,128]{1,0:T(8,128)(2,1)S(1)} %get-tuple-element.24), channel_id=1, source_target_pairs={{0,24},{4,28},{8,16},{12,20},{16,8},{20,12},{24,0},{28,4},{1,25},{... | collective-permute-start | bytes 442376 | tf_op jit(solution)/shard_map/ppermute | solution.py:274
  3.4 9.1 %collective-permute-start.4 = (bf16[576,128]{1,0:T(8,128)(2,1)S(1)}, bf16[576,128]{1,0:T(8,128)(2,1)S(1)}, u32[]{:S(2)}, u32[]{:S(2)}) collective-permute-start(bf16[576,128]{1,0:T(8,128)(2,1)S(1)} %get-tuple-element.25), channel_id=1, source_target_pairs={{0,8},{4,20},{8,0},{12,28},{16,24},{20,4},{24,16},{28,12},{1,9},{5... | collective-permute-start | bytes 442376 | tf_op jit(solution)/shard_map/ppermute | solution.py:274
  3.5 9.3 %collective-permute-start.5 = (bf16[576,128]{1,0:T(8,128)(2,1)S(1)}, bf16[576,128]{1,0:T(8,128)(2,1)S(1)}, u32[]{:S(2)}, u32[]{:S(2)}) collective-permute-start(bf16[576,128]{1,0:T(8,128)(2,1)S(1)} %get-tuple-element.26), channel_id=1, source_target_pairs={{0,16},{4,12},{8,24},{12,4},{16,0},{20,28},{24,8},{28,20},{1,17},{... | collective-permute-start | bytes 442376 | tf_op jit(solution)/shard_map/ppermute | solution.py:274
  7.1 6.5 %collective-permute-start.1 = (bf16[64,640]{1,0:T(8,128)(2,1)S(1)}, bf16[64,640]{1,0:T(8,128)(2,1)S(1)}, u32[]{:S(2)}, u32[]{:S(2)}) collective-permute-start(bf16[64,640]{1,0:T(8,128)(2,1)S(1)} %get-tuple-element.21), channel_id=1, source_target_pairs={{8,4},{5,12},{6,0},{11,8},{24,20},{21,28},{22,16},{27,24},{12,5},{... | collective-permute-start | bytes 245768 | tf_op jit(solution)/shard_map/ppermute | solution.py:297
  7.2 6.5 %collective-permute-start.2 = (bf16[64,640]{1,0:T(8,128)(2,1)S(1)}, bf16[64,640]{1,0:T(8,128)(2,1)S(1)}, u32[]{:S(2)}, u32[]{:S(2)}) collective-permute-start(bf16[64,640]{1,0:T(8,128)(2,1)S(1)} %get-tuple-element.22), channel_id=1, source_target_pairs={{8,12},{5,4},{6,8},{11,0},{24,28},{21,20},{22,24},{27,16},{12,13},... | collective-permute-start | bytes 245768 | tf_op jit(solution)/shard_map/ppermute | solution.py:297
  9.7 4.8 %collective-permute-start.6 = (bf16[2,576,128]{2,1,0:T(8,128)(2,1)S(1)}, bf16[2,576,128]{2,1,0:T(8,128)(2,1)S(1)}, u32[]{:S(2)}, u32[]{:S(2)}) collective-permute-start(bf16[2,576,128]{2,1,0:T(8,128)(2,1)S(1)} %shard_map.67), channel_id=1, source_target_pairs={{0,4},{4,0},{8,12},{12,8},{16,20},{20,16},{24,28},{28,24},{1,5},{5... | collective-permute-start | bytes 884744 | tf_op jit(solution)/shard_map/ppermute | solution.py:286
  12.5 2.0 %collective-permute-start.7 = (bf16[576,128]{1,0:T(8,128)(2,1)S(1)}, bf16[576,128]{1,0:T(8,128)(2,1)S(1)}, u32[]{:S(2)}, u32[]{:S(2)}) collective-permute-start(bf16[576,128]{1,0:T(8,128)(2,1)S(1)} %collective-permute-done.4.refs_4_), channel_id=1, source_target_pairs={{0,4},{4,0},{8,12},{12,8},{16,20},{20,16},{24,28},{28,24},{1,5},{5... | collective-permute-start | bytes 442376 | tf_op jit(solution)/shard_map/ppermute | solution.py:286
  12.8 1.7 %collective-permute-start.8 = (bf16[576,128]{1,0:T(8,128)(2,1)S(1)}, bf16[576,128]{1,0:T(8,128)(2,1)S(1)}, u32[]{:S(2)}, u32[]{:S(2)}) collective-permute-start(bf16[576,128]{1,0:T(8,128)(2,1)S(1)} %collective-permute-done.5.refs_5_), channel_id=1, source_target_pairs={{0,4},{4,0},{8,12},{12,8},{16,20},{20,16},{24,28},{28,24},{1,5},{5... | collective-permute-start | bytes 442376 | tf_op jit(solution)/shard_map/ppermute | solution.py:286
  13.7 11.6 %copy-start = (bf16[16,512,128]{2,1,0:T(8,128)(2,1)S(1)}, bf16[16,512,128]{2,1,0:T(8,128)(2,1)}, u32[]{:S(2)}) copy-start(bf16[16,512,128]{2,1,0:T(8,128)(2,1)} %w_ref.3) | copy-start | bytes 6291460
  15.2 7.7 %collective-permute-start.10 = (bf16[64,512]{1,0:T(8,128)(2,1)S(1)}, bf16[64,512]{1,0:T(8,128)(2,1)S(1)}, u32[]{:S(2)}, u32[]{:S(2)}) collective-permute-start(bf16[64,512]{1,0:T(8,128)(2,1)S(1)} %get-tuple-element.32), channel_id=1, source_target_pairs={{4,0},{12,1},{0,2},{8,3},{20,4},{28,5},{16,6},{24,7},{5,8},{13,9},... | collective-permute-start | bytes 196616 | tf_op jit(solution)/shard_map/ppermute | solution.py:327
  18.7 6.6 %collective-permute-start.9 = (bf16[64,512]{1,0:T(8,128)(2,1)S(1)}, bf16[64,512]{1,0:T(8,128)(2,1)S(1)}, u32[]{:S(2)}, u32[]{:S(2)}) collective-permute-start(bf16[64,512]{1,0:T(8,128)(2,1)S(1)} %get-tuple-element.31), channel_id=1, source_target_pairs={{12,0},{4,1},{8,2},{0,3},{28,4},{20,5},{24,6},{16,7},{13,8},{5,9},... | collective-permute-start | bytes 196616 | tf_op jit(solution)/shard_map/ppermute | solution.py:327
